TPU v7x, 32 devices: a whole 2x2x4 slice. The times are simulated.
32 devices in a mesh: dp: 8 (over z, x), tensor: 4 (over y, core).
Axes of the slice: x: 2, y: 2, z: 4, core: 2. Of those that a mesh axis runs over, the one named last changes fastest.
Arguments:
- inputs: bfloat16 [1024, 8192], P('dp', 'tensor')
- cotangent: bfloat16 [1024, 8192], P('dp', 'tensor'), may hold values from -6 to 6
- norm_gain: bfloat16 [8192], P('tensor'), may hold values from 0.5 to 12
- w_query: bfloat16 [8192, 512], P(None, 'tensor')
- w_key: bfloat16 [8192, 512], P(None, 'tensor')
- w_value: bfloat16 [8192, 512], P(None, 'tensor'), may hold values from -0.0625 to 0.0625
- w_output: bfloat16 [512, 8192], P('tensor'), may hold values from -0.25 to 0.25
- send_rows: int32 [8, 128], P('dp'), may hold values from 0 to 128, as said below
- receive_slots: int32 [1024], P('dp'), may hold values from 0 to 127, as said below
- owner_segments: int32 [1024], P('dp'), may hold values from 0 to 1, as said below
Outputs:
- layer_out: bfloat16 [1024, 8192], P('dp', 'tensor')
- input_grad: bfloat16 [1024, 8192], P('dp', 'tensor')
Inputs may be any that keep to these rules, and one draw needn't show every extreme that they name: `send_rows`: entry o * 16 + c of device p's list is the local row that p sends to device o in slot c, or 128 for an empty slot; every local row is sent exactly once, and a device sends either 16 rows or none to each device. `receive_slots`: entry i of device o is the slot p * 16 + c received from device p in slot c; the entries of one device are distinct and match send_rows, so each device ends with 128 rows. `owner_segments`: starts at 0 on each device, never falls along its rows and rises by at most one from row to row; a device holds at most 2 stays.
All inputs are finite; a program needn't handle non-finite values.
Results may differ from a plain program's by a relative error of at most 0.017.
The roundings to bfloat16 on the way count: a program that leaves them out, or rounds other values in their place, can miss the bound.
Values may be sent and summed in bfloat16 or wider, within the bound.
No kernel may reach another device: no remote copies, remote signals or barrier semaphores. Data moves between devices by JAX's collectives and lax.ppermute only.
A program may use at most 64 MiB of HBM per device.

v0:
```python
import math

import jax
import jax.numpy as jnp
from jax import lax
from jax.sharding import PartitionSpec as P

D = 8192
HEAD_DIM = 128


EPSILON = 1e-05
CONTRACT_LAST = (((1,), (1,)), ((), ()))


def to_buckets(rows_in, send_rows):
    padded = jnp.concatenate([rows_in, jnp.zeros((1, rows_in.shape[1]), rows_in.dtype)], axis=0)
    return padded[send_rows[0]]


def into_buckets(rows_in, receive_slots, slot_count):
    return jnp.zeros((slot_count, rows_in.shape[1]), rows_in.dtype).at[receive_slots].set(rows_in)


def sent_positions(send_rows, row_count):
    slot_numbers = jnp.arange(send_rows.shape[1], dtype=jnp.int32)
    return jnp.zeros((row_count,), jnp.int32).at[send_rows[0]].set(slot_numbers, mode="drop")


def gather_normed(inputs, cotangent, norm_gain):
    wide_in = inputs.astype(jnp.float32)
    squares = jnp.sum(wide_in * wide_in, axis=-1, keepdims=True)
    total = lax.psum(squares, "tensor")
    inverse_rms = lax.rsqrt(total / D + EPSILON)
    scaled = wide_in * inverse_rms
    normed_part = (scaled * norm_gain.astype(jnp.float32)).astype(jnp.bfloat16)
    normed, grad_rows = (
        lax.all_gather(normed_part, "tensor", axis=1, tiled=True),
        lax.all_gather(cotangent, "tensor", axis=1, tiled=True),
    )
    return (normed, grad_rows, scaled, inverse_rms)


def project(normed, grad_rows, w_query, w_key, w_value, w_output):
    queries = jnp.dot(normed, w_query, preferred_element_type=jnp.float32).astype(jnp.bfloat16)
    key_rows = jnp.dot(normed, w_key, preferred_element_type=jnp.float32).astype(jnp.bfloat16)
    value_rows = jnp.dot(normed, w_value, preferred_element_type=jnp.float32).astype(jnp.bfloat16)
    head_grad = lax.dot_general(
        grad_rows, w_output, CONTRACT_LAST, preferred_element_type=jnp.float32
    ).astype(jnp.bfloat16)
    return (queries, key_rows, value_rows, head_grad)


def attend(queries, key_rows, value_rows, head_grad, segments):
    row_count = queries.shape[0]
    head_shape = (row_count, queries.shape[1] // HEAD_DIM, HEAD_DIM)
    flat_shape = (row_count, queries.shape[1])
    query_heads = queries.reshape(head_shape)
    key_heads = key_rows.reshape(head_shape)
    value_heads = value_rows.reshape(head_shape)
    grad_heads = head_grad.reshape(head_shape)
    scaling = 1.0 / math.sqrt(HEAD_DIM)
    scores = (
        jnp.einsum("qhe,khe->hqk", query_heads, key_heads, preferred_element_type=jnp.float32)
        * scaling
    )
    position = jnp.arange(row_count, dtype=jnp.int32)
    allowed = (segments[:, None] == segments[None, :]) & (position[None, :] <= position[:, None])
    scores = jnp.where(allowed[None], scores, -1e30)
    largest = jnp.max(scores, axis=-1, keepdims=True)
    raised = jnp.exp(scores - largest)
    softmax_out = raised / jnp.sum(raised, axis=-1, keepdims=True)
    low_weights = softmax_out.astype(jnp.bfloat16)
    attended = jnp.einsum(
        "hqk,khe->qhe", low_weights, value_heads, preferred_element_type=jnp.float32
    ).astype(jnp.bfloat16)
    grad_value = jnp.einsum(
        "hqk,qhe->khe", low_weights, grad_heads, preferred_element_type=jnp.float32
    ).astype(jnp.bfloat16)
    grad_probs = jnp.einsum(
        "qhe,khe->hqk", grad_heads, value_heads, preferred_element_type=jnp.float32
    )
    grad_scores = (
        softmax_out
        * (grad_probs - jnp.sum(softmax_out * grad_probs, axis=-1, keepdims=True))
        * scaling
    )
    grad_scores = grad_scores.astype(jnp.bfloat16)
    grad_query = jnp.einsum(
        "hqk,khe->qhe", grad_scores, key_heads, preferred_element_type=jnp.float32
    ).astype(jnp.bfloat16)
    grad_key = jnp.einsum(
        "hqk,qhe->khe", grad_scores, query_heads, preferred_element_type=jnp.float32
    ).astype(jnp.bfloat16)
    return (
        attended.reshape(flat_shape),
        grad_query.reshape(flat_shape),
        grad_key.reshape(flat_shape),
        grad_value.reshape(flat_shape),
    )


def finish(
    inputs,
    cotangent,
    attended,
    grad_query,
    grad_key,
    grad_value,
    scaled,
    inverse_rms,
    norm_gain,
    w_query,
    w_key,
    w_value,
    w_output,
):
    partial_out = jnp.dot(attended, w_output, preferred_element_type=jnp.float32)
    summed = lax.psum_scatter(
        partial_out.astype(jnp.bfloat16), "tensor", scatter_dimension=1, tiled=True
    ).astype(jnp.float32)
    layer_out = (inputs.astype(jnp.float32) + summed).astype(jnp.bfloat16)
    grad_part = lax.dot_general(
        grad_query, w_query, CONTRACT_LAST, preferred_element_type=jnp.float32
    )
    grad_part = grad_part + lax.dot_general(
        grad_key, w_key, CONTRACT_LAST, preferred_element_type=jnp.float32
    )
    grad_part = grad_part + lax.dot_general(
        grad_value, w_value, CONTRACT_LAST, preferred_element_type=jnp.float32
    )
    grad_normed = lax.psum_scatter(
        grad_part.astype(jnp.bfloat16), "tensor", scatter_dimension=1, tiled=True
    ).astype(jnp.float32)
    grad_hat = grad_normed * norm_gain.astype(jnp.float32)
    row_dot = jnp.sum(grad_hat * scaled, axis=-1, keepdims=True)
    total_dot = lax.psum(row_dot, "tensor")
    input_grad = (
        cotangent.astype(jnp.float32) + inverse_rms * (grad_hat - scaled * (total_dot / D))
    ).astype(jnp.bfloat16)
    return (layer_out, input_grad)


def on_device(
    inputs,
    cotangent,
    norm_gain,
    w_query,
    w_key,
    w_value,
    w_output,
    send_rows,
    receive_slots,
    owner_segments,
):
    row_count = inputs.shape[0]
    slot_count = send_rows.shape[1]
    positions = sent_positions(send_rows, row_count)
    moved_in, moved_grad = (
        lax.all_to_all(
            to_buckets(inputs, send_rows), "dp", split_axis=0, concat_axis=0, tiled=True
        ),
        lax.all_to_all(
            to_buckets(cotangent, send_rows), "dp", split_axis=0, concat_axis=0, tiled=True
        ),
    )
    owned_in = moved_in[receive_slots]
    owned_grad = moved_grad[receive_slots]
    normed, grad_rows, scaled, inverse_rms = gather_normed(owned_in, owned_grad, norm_gain)
    queries, key_rows, value_rows, head_grad = project(
        normed, grad_rows, w_query, w_key, w_value, w_output
    )
    attended, grad_query, grad_key, grad_value = attend(
        queries, key_rows, value_rows, head_grad, owner_segments
    )
    owned_out, owned_input_grad = finish(
        owned_in,
        owned_grad,
        attended,
        grad_query,
        grad_key,
        grad_value,
        scaled,
        inverse_rms,
        norm_gain,
        w_query,
        w_key,
        w_value,
        w_output,
    )
    back_out, back_grad = (
        lax.all_to_all(
            into_buckets(owned_out, receive_slots, slot_count),
            "dp",
            split_axis=0,
            concat_axis=0,
            tiled=True,
        ),
        lax.all_to_all(
            into_buckets(owned_input_grad, receive_slots, slot_count),
            "dp",
            split_axis=0,
            concat_axis=0,
            tiled=True,
        ),
    )
    layer_out = back_out[positions]
    input_grad = back_grad[positions]
    return (layer_out, input_grad)


def solution(mesh):
    return jax.shard_map(
        on_device,
        mesh=mesh,
        in_specs=(
            P("dp", "tensor"),
            P("dp", "tensor"),
            P("tensor"),
            P(None, "tensor"),
            P(None, "tensor"),
            P(None, "tensor"),
            P("tensor", None),
            P("dp", None),
            P("dp"),
            P("dp"),
        ),
        out_specs=(P("dp", "tensor"), P("dp", "tensor")),
        check_vma=False,
    )
```

profile of v0, /device:TPU:0, one launch (start us, length us, event | category | flops | bytes accessed | tf_op | source)
XLA Modules:
  0.0 200.5 jit_solution(4729550072413186758)
XLA Ops:
  9.1 1.7 gather_fusion
  10.8 7.3 %all-to-all-start = ((bf16[8,16,2048]{2,1,0:T(8,128)(2,1)}), bf16[8,16,2048]{2,1,0:T(8,128)(2,1)S(1)}, u32[]{:S(2)}, u32[]{:S(2)}) async-start(bf16[8,16,2048]{2,1,0:T(8,128)(2,1)} %bitcast.2), calls=%async_computation | async-start | bytes 1048576 | tf_op jit(solution)/shard_map/all_to_all | solution.py:160
  18.2 14.4 %all-to-all-done = bf16[8,16,2048]{2,1,0:T(8,128)(2,1)S(1)} async-done(((bf16[8,16,2048]{2,1,0:T(8,128)(2,1)}), bf16[8,16,2048]{2,1,0:T(8,128)(2,1)S(1)}, u32[]{:S(2)}, u32[]{:S(2)}) %all-to-all-start) | async-done | bytes 524320 | tf_op jit(solution)/shard_map/all_to_all | solution.py:160
  33.7 5.7 %psum.14 = f32[128,1]{0,1:T(1,128)S(1)} all-reduce(f32[128,1]{0,1:T(1,128)S(1)} %bitcast.83), channel_id=1, replica_groups=mesh['dp'=8,'tensor'=4] {'tensor'}, use_global_device_ids=true, to_apply=%region_1.0 | all-reduce | flops 128 | bytes 1024 | tf_op jit(solution)/shard_map/psum | solution.py:33
  41.5 1.7 gather_fusion.3
  43.2 18.2 %all_to_all.48 = bf16[8,16,2048]{2,1,0:T(8,128)(2,1)S(1)} all-to-all(bf16[8,16,2048]{2,1,0:T(8,128)(2,1)} %bitcast.79), channel_id=1, replica_groups=mesh['dp'=8,'tensor'=4] {'dp'}, dimensions={0} | all-to-all | bytes 1048576 | tf_op jit(solution)/shard_map/all_to_all | solution.py:163
  61.4 1.7 gather_fusion.4
  63.3 3.1 %convolution_convert_fusion.6 = bf16[128,128]{1,0:T(8,128)(2,1)S(1)} fusion(bf16[128,8192]{1,0:T(8,128)(2,1)} %all-gather.4.cloned.1.call-done, bf16[8192,128]{1,0:T(8,128)(2,1)} %param.14), kind=kOutput, calls=%fused_computation.26 | convolution fusion | flops 268451840 | bytes 4227072 | tf_op jit(solution)/shard_map/dot_general | solution.py:46
  68.7 18.6 %all-gather.6.cloned.1.call-done = bf16[128,8192]{1,0:T(8,128)(2,1)} async-done(((bf16[128,2048]{1,0:T(8,128)(2,1)}), bf16[128,8192]{1,0:T(8,128)(2,1)}) %all-gather.6.cloned.1.call-update) | async-done | bytes 2097168 | tf_op jit(solution)/shard_map/all_gather | solution.py:39
  87.2 2.9 %convolution_convert_fusion.4 = bf16[128,128]{1,0:T(8,128)(2,1)S(1)} fusion(bf16[128,8192]{1,0:T(8,128)(2,1)} %all-gather.6.cloned.1.call-done, bf16[128,8192]{1,0:T(8,128)(2,1)} %param.16), kind=kOutput, calls=%fused_computation.24 | convolution fusion | flops 268451840 | bytes 4227072 | tf_op jit(solution)/shard_map/dot_general | solution.py:48
  90.4 2.8 %fusion.7 = f32[128,8192]{1,0:T(8,128)} fusion(bf16[8192,128]{1,0:T(8,128)(2,1)S(1)} %copy-done, bf16[128,128]{1,0:T(8,128)(2,1)S(1)} %convolution_convert_fusion.6, bf16[128,128]{0,1:T(8,128)(2,1)S(1)} %multiply_convert_fusion), kind=kOutput, calls=%fused_computation.31 | convolution fusion | flops 272646144 | bytes 6356992 | tf_op jit(solution)/shard_map/dot_general | solution.py:123
  93.2 5.7 %convolution_add_fusion.1 = f32[128,8192]{1,0:T(8,128)} fusion(f32[128,8192]{1,0:T(8,128)} %fusion.7, bf16[8192,128]{1,0:T(8,128)(2,1)} %param.14, bf16[128,128]{1,0:T(8,128)(2,1)S(1)} %convolution_convert_fusion.7, bf16[128,128]{0,1:T(8,128)(2,1)S(1)} %multiply_convert_fusion), kind=kOutput, calls=%fused_computation.10 | convolution fusion | flops 273694720 | bytes 10551296 | tf_op jit(solution)/shard_map/dot_general | solution.py:126
  98.9 5.1 %fusion = bf16[128,8192]{1,0:T(8,128)(2,1)} fusion(f32[128,8192]{1,0:T(8,128)} %convolution_add_fusion.1, bf16[8192,128]{1,0:T(8,128)(2,1)} %param.15, bf16[128,128]{1,0:T(8,128)(2,1)S(1)} %convolution_convert_fusion.4, f32[128,128]{0,1:T(8,128)S(1)} %get-tuple-element.5, f32[128]{0:T(128)S(1)} %fusion.29, f32[128]{0:T(128)S(1)} %get-tuple-element.4), kind=kOutput, calls=%fused_computation.11 | convolution fusion | flops 274792448 | bytes 8487936 | tf_op jit(solution)/shard_map/dot_general | solution.py:129
  104.1 3.9 %convolution_convert_fusion = bf16[128,8192]{1,0:T(8,128)(2,1)} fusion(bf16[128,8192]{1,0:T(8,128)(2,1)} %param.16, bf16[128,128]{1,0:T(8,128)(2,1)S(1)} %convolution_convert_fusion.8, f32[128,128]{0,1:T(8,128)S(1)} %get-tuple-element.5, f32[128]{0:T(128)S(1)} %fusion.29, f32[128]{0:T(128)S(1)} %get-tuple-element.4), kind=kOutput, calls=%fused_computation.12 | convolution fusion | flops 273743872 | bytes 4293632 | tf_op jit(solution)/shard_map/dot_general | solution.py:118
  107.9 27.6 %reduce-scatter.5.cloned.1.call-done = bf16[128,2048]{1,0:T(8,128)(2,1)} async-done(((bf16[128,8192]{1,0:T(8,128)(2,1)}), bf16[128,2048]{1,0:T(8,128)(2,1)}) %reduce-scatter.5.cloned.1.call-update) | async-done | bytes 524304 | tf_op jit(solution)/shard_map/reduce_scatter | solution.py:132
  137.0 5.8 %psum.15 = f32[128,1]{0,1:T(1,128)S(1)} all-reduce(f32[128,1]{0,1:T(1,128)S(1)} %bitcast.82), channel_id=1, replica_groups=mesh['dp'=8,'tensor'=4] {'tensor'}, use_global_device_ids=true, to_apply=%region_10.11 | all-reduce | flops 128 | bytes 1024 | tf_op jit(solution)/shard_map/psum | solution.py:137
  142.7 3.1 %scatter_custom_fusion.2 = bf16[128,2048]{1,0:T(8,128)(2,1)} fusion(s32[128]{0:T(128)S(1)} %compare_select_fusion.3, bf16[128,2048]{1,0:T(8,128)(2,1)S(1)} %gather_fusion.1, bf16[128,2048]{1,0:T(8,128)(2,1)} %reduce-scatter.5.cloned.1.call-done, bf16[128,2048]{1,0:T(8,128)(2,1)S(1)} %copy-done.3, f32[128]{0:T(128)S(1)} %multiply_bitcast_fusion, ...), kind=kCustom, calls=%fused_computation.44 | custom fusion | flops 2621440 | bytes 2106370 | tf_op jit(solution)/shard_map/scatter | solution.py:22
  145.8 5.7 %all-to-all-start.3 = ((bf16[8,16,2048]{2,1,0:T(8,128)(2,1)}), bf16[8,16,2048]{2,1,0:T(8,128)(2,1)S(1)}, u32[]{:S(2)}, u32[]{:S(2)}) async-start(bf16[8,16,2048]{2,1,0:T(8,128)(2,1)} %bitcast.81), calls=%async_computation.5 | async-start | bytes 1048576 | tf_op jit(solution)/shard_map/all_to_all | solution.py:199
  151.5 18.1 %reduce-scatter.3.cloned.1.call-done = bf16[128,2048]{1,0:T(8,128)(2,1)} async-done(((bf16[128,8192]{1,0:T(8,128)(2,1)}), bf16[128,2048]{1,0:T(8,128)(2,1)}) %reduce-scatter.3.cloned.1.call-update) | async-done | bytes 524304 | tf_op jit(solution)/shard_map/reduce_scatter | solution.py:119
  169.6 2.7 %scatter_custom_fusion = bf16[128,2048]{1,0:T(8,128)(2,1)} fusion(s32[128]{0:T(128)S(1)} %compare_select_fusion.3, bf16[128,2048]{1,0:T(8,128)(2,1)S(1)} %gather_fusion.1, bf16[128,2048]{1,0:T(8,128)(2,1)} %reduce-scatter.3.cloned.1.call-done, bf16[]{:T(256)} %constant.10.clone.1), kind=kCustom, calls=%fused_computation.43 | custom fusion | flops 1048576 | bytes 1572866 | tf_op jit(solution)/shard_map/scatter | solution.py:22
  172.3 5.5 %all-to-all-start.1 = ((bf16[8,16,2048]{2,1,0:T(8,128)(2,1)}), bf16[8,16,2048]{2,1,0:T(8,128)(2,1)S(1)}, u32[]{:S(2)}, u32[]{:S(2)}) async-start(bf16[8,16,2048]{2,1,0:T(8,128)(2,1)} %bitcast.80), calls=%async_computation.2 | async-start | bytes 1048576 | tf_op jit(solution)/shard_map/all_to_all | solution.py:192
  178.8 1.7 gather_fusion.5
  180.5 11.8 %all-to-all-done.1 = bf16[8,16,2048]{2,1,0:T(8,128)(2,1)S(1)} async-done(((bf16[8,16,2048]{2,1,0:T(8,128)(2,1)}), bf16[8,16,2048]{2,1,0:T(8,128)(2,1)S(1)}, u32[]{:S(2)}, u32[]{:S(2)}) %all-to-all-start.1) | async-done | bytes 524320 | tf_op jit(solution)/shard_map/all_to_all | solution.py:192
  192.3 1.7 gather_fusion.2
  (47 shorter events, 10.2 us)
Async XLA Ops:
  7.2 59.2 %copy-start = (bf16[8192,128]{1,0:T(8,128)(2,1)S(1)}, bf16[8192,128]{1,0:T(8,128)(2,1)}, u32[]{:S(2)}) copy-start(bf16[8192,128]{1,0:T(8,128)(2,1)} %param.13) | copy-start | bytes 6291460
  9.1 9.1 %copy-start.4 = (bf16[2048]{0:T(1024)(128)(2,1)S(1)}, bf16[2048]{0:T(1024)(128)(2,1)}, u32[]{:S(2)}) copy-start(bf16[2048]{0:T(1024)(128)(2,1)} %param.12) | copy-start | bytes 12292
  9.1 9.1 %copy-start.5 = (s32[128]{0:T(128)S(1)}, s32[128]{0:T(128)}, u32[]{:S(2)}) copy-start(s32[128]{0:T(128)} %param.18) | copy-start | bytes 1540
  10.8 21.7 %all-to-all-start = ((bf16[8,16,2048]{2,1,0:T(8,128)(2,1)}), bf16[8,16,2048]{2,1,0:T(8,128)(2,1)S(1)}, u32[]{:S(2)}, u32[]{:S(2)}) async-start(bf16[8,16,2048]{2,1,0:T(8,128)(2,1)} %bitcast.2), calls=%async_computation | async-start | bytes 1048576 | tf_op jit(solution)/shard_map/all_to_all | solution.py:160
  18.1 45.2 %all-gather.4.cloned.1.call-start = ((), (), s32[]{:S(2)}) async-start(), calls=%async_computation.6 | async-start | bytes 2621440 | tf_op jit(solution)/shard_map/all_gather | solution.py:38
  40.4 46.9 %all-gather.6.cloned.1.call-start = ((), (), s32[]{:S(2)}) async-start(), calls=%async_computation.9 | async-start | bytes 2621440 | tf_op jit(solution)/shard_map/all_gather | solution.py:39
  63.2 72.4 %reduce-scatter.5.cloned.1.call-start = ((), (), s32[]{:S(2)}) async-start(), calls=%async_computation.8 | async-start | bytes 2621440 | tf_op jit(solution)/shard_map/reduce_scatter | solution.py:132
  63.3 3.1 %copy-start.1 = (bf16[128,8192]{1,0:T(8,128)(2,1)S(1)}, bf16[128,8192]{1,0:T(8,128)(2,1)}, u32[]{:S(2)}) copy-start(bf16[128,8192]{1,0:T(8,128)(2,1)} %all-gather.4.cloned.1.call-done) | copy-start | bytes 6291460
  66.4 0.7 copy-start.6
  66.4 1.6 copy-start.2
  104.0 65.6 %reduce-scatter.3.cloned.1.call-start = ((), (), s32[]{:S(2)}) async-start(), calls=%async_computation.7 | async-start | bytes 2621440 | tf_op jit(solution)/shard_map/reduce_scatter | solution.py:119
  107.9 34.8 %copy-start.3 = (bf16[128,2048]{1,0:T(8,128)(2,1)S(1)}, bf16[128,2048]{1,0:T(8,128)(2,1)}, u32[]{:S(2)}) copy-start(bf16[128,2048]{1,0:T(8,128)(2,1)} %gather_fusion.4) | copy-start | bytes 1572868
  145.8 26.5 %all-to-all-start.3 = ((bf16[8,16,2048]{2,1,0:T(8,128)(2,1)}), bf16[8,16,2048]{2,1,0:T(8,128)(2,1)S(1)}, u32[]{:S(2)}, u32[]{:S(2)}) async-start(bf16[8,16,2048]{2,1,0:T(8,128)(2,1)} %bitcast.81), calls=%async_computation.5 | async-start | bytes 1048576 | tf_op jit(solution)/shard_map/all_to_all | solution.py:199
  172.3 20.0 %all-to-all-start.1 = ((bf16[8,16,2048]{2,1,0:T(8,128)(2,1)}), bf16[8,16,2048]{2,1,0:T(8,128)(2,1)S(1)}, u32[]{:S(2)}, u32[]{:S(2)}) async-start(bf16[8,16,2048]{2,1,0:T(8,128)(2,1)} %bitcast.80), calls=%async_computation.2 | async-start | bytes 1048576 | tf_op jit(solution)/shard_map/all_to_all | solution.py:192
Sparse Core Ops, SparseCore 0:
  40.5 21.9 all-gather.3
  64.6 22.5 all-gather.5
  104.1 31.4 reduce-scatter.4
  138.1 31.4 reduce-scatter.2
where the time goes:
time: 201 us
  waiting for transfers between devices  90.5 us (45%)
  blocking collectives  29.6 us (15%)
  matrix products  25.2 us (13%)
  starting transfers between devices  18.6 us (9%)
  between operations  14 us (7%)
  local copies, waits for them, and re-layouts  13.4 us (7%)
  other arithmetic  9.27 us (5%)
    reduce_scatter x1, waiting for transfers between devices, finish(): lax.psum_scatter(grad_part.astype(jnp.bfloat16), 'tensor', scatter_dimens...  27.6 us
    all_gather x1, waiting for transfers between devices, gather_normed(): lax.all_gather(cotangent, 'tensor', axis=1, tiled=True)  18.6 us
    all_to_all x1, blocking collectives, on_device(): lax.all_to_all(to_buckets(cotangent, send_rows), 'dp', split_axis=0, conc...  18.2 us
    reduce_scatter x1, waiting for transfers between devices, finish(): lax.psum_scatter(partial_out.astype(jnp.bfloat16), 'tensor', scatter_dime...  18.1 us
    all_to_all x1, waiting for transfers between devices, on_device(): lax.all_to_all(to_buckets(inputs, send_rows), 'dp', split_axis=0, concat_...  14.4 us
    all_to_all x1, waiting for transfers between devices, on_device(): lax.all_to_all(into_buckets(owned_out, receive_slots, slot_count), 'dp',...  11.8 us
    all_to_all x1, starting transfers between devices, on_device(): lax.all_to_all(to_buckets(inputs, send_rows), 'dp', split_axis=0, concat_...  7.25 us
    scatter x2, other arithmetic, into_buckets(): jnp.zeros((slot_count, rows_in.shape[1]), rows_in.dtype).at[receive_slots]  5.8 us
  transfers between devices with their start and end apart: 7, of which 5 were waited for; matrix products, arithmetic and copies ran while one was open for 11% of the time, Pallas kernels for 0%

commit v1 on v0

v1 whole, which is shorter than its diff:
```python
import functools
import math

import jax
import jax.numpy as jnp
from jax import lax
from jax.experimental import pallas as pl
from jax.experimental.pallas import tpu as pltpu
from jax.sharding import PartitionSpec as P

HEAD_DIM = 128
EPSILON = 1e-05
SCALING = 1.0 / math.sqrt(HEAD_DIM)
CONTRACT_LAST = (((1,), (1,)), ((), ()))
CONTRACT_FIRST = (((0,), (0,)), ((), ()))
VMEM_LIMIT = 48 * 1024 * 1024


def dot(left, right, dims=(((1,), (0,)), ((), ()))):
    return lax.dot_general(left, right, dims, preferred_element_type=jnp.float32)


def params():
    return pltpu.CompilerParams(vmem_limit_bytes=VMEM_LIMIT)


def whole(array):
    zeros = (0,) * array.ndim
    return pl.BlockSpec(array.shape, lambda *_: zeros)


def swap(array, mask, count):
    return lax.ppermute(array, "tensor", [(i, i ^ mask) for i in range(count)])


def project_rows_kernel(
    order, x0, x1, x2, x3, gain, w_query, w_key, w_value, send, home, bucket, inverse, total
):
    step = pl.program_id(0)
    blocks = (x0, x1, x2, x3)
    features = sum(block.shape[1] for block in blocks)

    @pl.when(step == 0)
    def _():
        squares = 0.0
        for block in blocks:
            wide = block[...].astype(jnp.float32)
            squares = squares + jnp.sum(wide * wide, axis=-1, keepdims=True)
        inverse[...] = lax.rsqrt(squares / features + EPSILON)
        total[...] = jnp.zeros_like(total)

    for index, block in enumerate(blocks):

        @pl.when(step == index)
        def _():
            scaled = block[...].astype(jnp.float32) * inverse[...]
            normed = (scaled * gain[index : index + 1, :].astype(jnp.float32)).astype(jnp.bfloat16)
            for place, weight in enumerate((w_query, w_key, w_value)):
                part = slice(place * HEAD_DIM, (place + 1) * HEAD_DIM)
                total[:, part] += dot(normed, weight[...])

    @pl.when(step == len(blocks) - 1)
    def _():
        rounded = total[...].astype(jnp.bfloat16)
        home[...] = rounded
        rows = lax.broadcasted_iota(jnp.int32, (send.shape[0], rounded.shape[0]), 1)
        chosen = jnp.where(send[...] == rows, 1.0, 0.0).astype(jnp.bfloat16)
        bucket[...] = dot(chosen, rounded).astype(jnp.bfloat16)


def project_rows(order, blocks, gain, w_query, w_key, w_value, send):
    rows, width = blocks[0].shape
    slots = send.shape[0]
    weight_spec = pl.BlockSpec((width, HEAD_DIM), lambda s, order: (order[s], 0))
    return pl.pallas_call(
        project_rows_kernel,
        out_shape=(
            jax.ShapeDtypeStruct((rows, 3 * HEAD_DIM), jnp.bfloat16),
            jax.ShapeDtypeStruct((slots, 3 * HEAD_DIM), jnp.bfloat16),
            jax.ShapeDtypeStruct((rows, 1), jnp.float32),
        ),
        grid_spec=pltpu.PrefetchScalarGridSpec(
            num_scalar_prefetch=1,
            grid=(4,),
            in_specs=[whole(b) for b in blocks] + [whole(gain)] + [weight_spec] * 3 + [whole(send)],
            out_specs=[
                pl.BlockSpec((rows, 3 * HEAD_DIM), lambda *_: (0, 0)),
                pl.BlockSpec((slots, 3 * HEAD_DIM), lambda *_: (0, 0)),
                pl.BlockSpec((rows, 1), lambda *_: (0, 0)),
            ],
            scratch_shapes=[pltpu.VMEM((rows, 3 * HEAD_DIM), jnp.float32)],
        ),
        compiler_params=params(),
        name="project_rows",
    )(order, *blocks, gain, w_query, w_key, w_value, send)


def project_grad_kernel(order, c0, c1, c2, c3, w_output, send, home, bucket, total):
    step = pl.program_id(0)
    blocks = (c0, c1, c2, c3)

    @pl.when(step == 0)
    def _():
        total[...] = jnp.zeros_like(total)

    for index, block in enumerate(blocks):

        @pl.when(step == index)
        def _():
            total[...] += dot(block[...], w_output[...], CONTRACT_LAST)

    @pl.when(step == len(blocks) - 1)
    def _():
        rounded = total[...].astype(jnp.bfloat16)
        home[...] = rounded
        rows = lax.broadcasted_iota(jnp.int32, (send.shape[0], rounded.shape[0]), 1)
        chosen = jnp.where(send[...] == rows, 1.0, 0.0).astype(jnp.bfloat16)
        bucket[...] = dot(chosen, rounded).astype(jnp.bfloat16)


def project_grad(order, blocks, w_output, send):
    rows, width = blocks[0].shape
    slots = send.shape[0]
    return pl.pallas_call(
        project_grad_kernel,
        out_shape=(
            jax.ShapeDtypeStruct((rows, HEAD_DIM), jnp.bfloat16),
            jax.ShapeDtypeStruct((slots, HEAD_DIM), jnp.bfloat16),
        ),
        grid_spec=pltpu.PrefetchScalarGridSpec(
            num_scalar_prefetch=1,
            grid=(4,),
            in_specs=[whole(b) for b in blocks]
            + [pl.BlockSpec((HEAD_DIM, width), lambda s, order: (0, order[s])), whole(send)],
            out_specs=[
                pl.BlockSpec((rows, HEAD_DIM), lambda *_: (0, 0)),
                pl.BlockSpec((slots, HEAD_DIM), lambda *_: (0, 0)),
            ],
            scratch_shapes=[pltpu.VMEM((rows, HEAD_DIM), jnp.float32)],
        ),
        compiler_params=params(),
        name="project_grad",
    )(order, *blocks, w_output, send)


def one_owner(queries, key_rows, value_rows, head_grad, allowed):
    scores = jnp.where(allowed, dot(queries, key_rows, CONTRACT_LAST) * SCALING, -1e30)
    raised = jnp.exp(scores - jnp.max(scores, axis=-1, keepdims=True))
    softmax_out = raised / jnp.sum(raised, axis=-1, keepdims=True)
    low_weights = softmax_out.astype(jnp.bfloat16)
    attended = dot(low_weights, value_rows).astype(jnp.bfloat16)
    grad_value = dot(low_weights, head_grad, CONTRACT_FIRST).astype(jnp.bfloat16)
    grad_probs = dot(head_grad, value_rows, CONTRACT_LAST)
    inner = jnp.sum(softmax_out * grad_probs, axis=-1, keepdims=True)
    grad_scores = (softmax_out * (grad_probs - inner) * SCALING).astype(jnp.bfloat16)
    grad_query = dot(grad_scores, key_rows).astype(jnp.bfloat16)
    grad_key = dot(grad_scores, queries, CONTRACT_FIRST).astype(jnp.bfloat16)
    return attended, grad_query, grad_key, grad_value


def attend_kernel(me, qkv, grad, code_down, code_across, send, out, held, picked):
    devices, owners, cap, _ = qkv.shape
    slots = devices * cap
    mine = pl.ds(pl.multiple_of(me[0] * cap, cap), cap)
    for owner in range(owners):
        rows = qkv[:, owner].reshape(slots, 3 * HEAD_DIM)
        head_grad = grad[:, owner].reshape(slots, HEAD_DIM)
        down = code_down[:, owner : owner + 1]
        across = code_across[owner : owner + 1, :]
        allowed = (across <= down) & (across >= (down // slots) * slots)
        results = one_owner(
            rows[:, :HEAD_DIM],
            rows[:, HEAD_DIM : 2 * HEAD_DIM],
            rows[:, 2 * HEAD_DIM :],
            head_grad,
            allowed,
        )
        for place, result in enumerate(results):
            held[owner, :, place * HEAD_DIM : (place + 1) * HEAD_DIM] = result
    for owner in range(owners):
        picked[owner * cap : (owner + 1) * cap, :] = held[owner, mine, :]
    rows = lax.broadcasted_iota(jnp.int32, (out.shape[0], slots), 0)
    chosen = jnp.where(send[...] == rows, 1.0, 0.0).astype(jnp.bfloat16)
    out[...] = dot(chosen, picked[...]).astype(jnp.bfloat16)


def attend_all(me, qkv, grad, code_down, code_across, send, rows):
    devices, owners, cap, _ = qkv.shape
    slots = devices * cap
    vmem = pl.BlockSpec(memory_space=pltpu.VMEM)
    return pl.pallas_call(
        attend_kernel,
        out_shape=jax.ShapeDtypeStruct((rows, 4 * HEAD_DIM), jnp.bfloat16),
        in_specs=[pl.BlockSpec(memory_space=pltpu.SMEM)] + [vmem] * 5,
        out_specs=vmem,
        scratch_shapes=[
            pltpu.VMEM((owners, slots, 4 * HEAD_DIM), jnp.bfloat16),
            pltpu.VMEM((slots, 4 * HEAD_DIM), jnp.bfloat16),
        ],
        compiler_params=params(),
        name="attend_all",
    )(me, qkv, grad, code_down, code_across, send)


def spread_kernel(order, own, near, wq, wk, wv, wo, nq, nk, nv, no, grad_part, out_part):
    grad = 0.0
    for place, weight in ((1, wq), (2, wk), (3, wv)):
        grad += dot(own[:, place * HEAD_DIM : (place + 1) * HEAD_DIM], weight[...], CONTRACT_LAST)
    for place, weight in ((1, nq), (2, nk), (3, nv)):
        grad += dot(near[:, place * HEAD_DIM : (place + 1) * HEAD_DIM], weight[...], CONTRACT_LAST)
    grad_part[...] = grad.astype(grad_part.dtype)
    out = dot(own[:, :HEAD_DIM], wo[...]) + dot(near[:, :HEAD_DIM], no[...])
    out_part[...] = out.astype(out_part.dtype)


def spread(order, slot, own, near, own_weights, near_weights, width, dtype, tile=512):
    rows = own.shape[0]
    steps = width // tile
    here = lambda j, order: (order[slot] * steps + j, 0)
    here_across = lambda j, order: (0, order[slot] * steps + j)
    flat = lambda j, order: (j, 0)
    flat_across = lambda j, order: (0, j)
    return pl.pallas_call(
        spread_kernel,
        out_shape=(
            jax.ShapeDtypeStruct((rows, width), dtype),
            jax.ShapeDtypeStruct((rows, width), dtype),
        ),
        grid_spec=pltpu.PrefetchScalarGridSpec(
            num_scalar_prefetch=1,
            grid=(steps,),
            in_specs=[whole(own), whole(near)]
            + [pl.BlockSpec((tile, HEAD_DIM), here)] * 3
            + [pl.BlockSpec((HEAD_DIM, tile), here_across)]
            + [pl.BlockSpec((tile, HEAD_DIM), flat)] * 3
            + [pl.BlockSpec((HEAD_DIM, tile), flat_across)],
            out_specs=[pl.BlockSpec((rows, tile), flat_across)] * 2,
        ),
        compiler_params=params(),
        name="spread",
    )(order, own, near, *own_weights, *near_weights)


def balanced_codes(receive_slots, owner_segments, slots):
    rows = receive_slots.shape[0]
    taken = receive_slots[:, None] == jnp.arange(slots, dtype=jnp.int32)[None, :]
    code = owner_segments * slots + jnp.arange(rows, dtype=jnp.int32)
    return jnp.sum(jnp.where(taken, code[:, None], 0), axis=0)


def attend_gathered(bucket_qkv, bucket_grad, send_rows, receive_slots, owner_segments, rows):
    devices = lax.axis_size("dp")
    slots = send_rows.shape[1]
    cap = slots // devices
    code = balanced_codes(receive_slots, owner_segments, slots)
    codes = lax.all_gather(code, "dp")
    qkv = lax.all_gather(bucket_qkv, "dp").reshape(devices, devices, cap, 3 * HEAD_DIM)
    grad = lax.all_gather(bucket_grad, "dp").reshape(devices, devices, cap, HEAD_DIM)
    me = lax.axis_index("dp").astype(jnp.int32).reshape(1)
    return attend_all(me, qkv, grad, codes.T, codes, send_rows, rows)


def attend_exchanged(bucket_qkv, bucket_grad, send_rows, receive_slots, owner_segments, rows):
    slots = send_rows.shape[1]
    bucket = jnp.concatenate([bucket_qkv, bucket_grad], axis=1)
    moved = lax.all_to_all(bucket, "dp", split_axis=0, concat_axis=0, tiled=True)
    parts = jnp.split(moved[receive_slots], 4, axis=1)
    position = jnp.arange(rows, dtype=jnp.int32)
    same = owner_segments[:, None] == owner_segments[None, :]
    allowed = same & (position[None, :] <= position[:, None])
    results = jnp.concatenate(one_owner(*parts, allowed), axis=1)
    back = jnp.zeros((slots, 4 * HEAD_DIM), jnp.bfloat16).at[receive_slots].set(results)
    back = lax.all_to_all(back, "dp", split_axis=0, concat_axis=0, tiled=True)
    return jnp.zeros((rows, 4 * HEAD_DIM), jnp.bfloat16).at[send_rows[0]].set(back, mode="drop")


def on_device(
    inputs,
    cotangent,
    norm_gain,
    w_query,
    w_key,
    w_value,
    w_output,
    send_rows,
    receive_slots,
    owner_segments,
):
    rows, width = inputs.shape
    slots = send_rows.shape[1]
    tensor = lax.axis_size("tensor")
    features = width * tensor
    order = lax.axis_index("tensor").astype(jnp.int32) ^ jnp.arange(4, dtype=jnp.int32)
    send_down = send_rows.reshape(slots, 1)

    x2 = swap(inputs, 2, tensor)
    c2 = swap(cotangent, 2, tensor)
    x1 = swap(inputs, 1, tensor)
    c1 = swap(cotangent, 1, tensor)
    x3 = swap(x2, 1, tensor)
    c3 = swap(c2, 1, tensor)
    gain_row = norm_gain.reshape(1, width)
    gain2 = jnp.concatenate([gain_row, swap(gain_row, 1, tensor)], axis=0)
    gain = jnp.concatenate([gain2, swap(gain2, 2, tensor)], axis=0)

    near = []
    for weight in (w_query, w_key, w_value):
        pieces = [
            lax.dynamic_slice_in_dim(weight, order[slot] * width, width, axis=0) for slot in (1, 3)
        ]
        near.append(swap(jnp.concatenate(pieces, axis=0), 1, tensor))
    pieces = [
        lax.dynamic_slice_in_dim(w_output, order[slot] * width, width, axis=1) for slot in (1, 3)
    ]
    near.append(swap(jnp.concatenate(pieces, axis=1), 1, tensor))

    home, bucket_qkv, inverse_rms = project_rows(
        order, (inputs, x1, x2, x3), gain, w_query, w_key, w_value, send_down
    )
    _, bucket_grad = project_grad(order, (cotangent, c1, c2, c3), w_output, send_down)
    dense = slots == rows
    attend = attend_gathered if dense else attend_exchanged
    results = attend(bucket_qkv, bucket_grad, send_rows, receive_slots, owner_segments, rows)
    results_near = swap(results, 1, tensor)

    own_weights = (w_query, w_key, w_value, w_output)
    far_near = [n[width:] for n in near[:3]] + [near[3][:, width:]]
    grad_far, out_far = spread(
        order, 2, results, results_near, own_weights, far_near, width, jnp.bfloat16
    )
    grad_got = swap(grad_far, 2, tensor)
    out_got = swap(out_far, 2, tensor)
    grad_own, out_own = spread(
        order, 0, results, results_near, own_weights, near, width, jnp.float32
    )
    row_dot = jnp.sum(
        results[:, HEAD_DIM:].astype(jnp.float32) * home.astype(jnp.float32),
        axis=-1,
        keepdims=True,
    )
    row_dot = row_dot + swap(row_dot, 1, tensor)
    row_dot = row_dot + swap(row_dot, 2, tensor)

    wide_in = inputs.astype(jnp.float32)
    layer_out = (wide_in + out_own + out_got.astype(jnp.float32)).astype(jnp.bfloat16)
    scaled = wide_in * inverse_rms
    grad_hat = (grad_own + grad_got.astype(jnp.float32)) * norm_gain.astype(jnp.float32)
    input_grad = (
        cotangent.astype(jnp.float32) + inverse_rms * (grad_hat - scaled * (row_dot / features))
    ).astype(jnp.bfloat16)
    return (layer_out, input_grad)


def solution(mesh):
    return jax.shard_map(
        on_device,
        mesh=mesh,
        in_specs=(
            P("dp", "tensor"),
            P("dp", "tensor"),
            P("tensor"),
            P(None, "tensor"),
            P(None, "tensor"),
            P(None, "tensor"),
            P("tensor", None),
            P("dp", None),
            P("dp"),
            P("dp"),
        ),
        out_specs=(P("dp", "tensor"), P("dp", "tensor")),
        check_vma=False,
    )
```

time: 201 us -> 171 us (0.85)
  blocking collectives: 29.6 us -> 83.5 us
  waiting for transfers between devices: 90.5 us -> 38.7 us
  matrix products: 25.2 us -> 0 us
  Pallas kernels: 0 us -> 21.9 us
  between operations: 14 us -> 2.18 us
  starting transfers between devices: 18.6 us -> 10.2 us
  local copies, waits for them, and re-layouts: 13.4 us -> 7.61 us
  other arithmetic: 9.27 us -> 6.21 us
    all_gather x0 -> x3, blocking collectives: none -> 83.5 us  [the longest x1 31.9 us: attend_gathered(): lax.all_gather(bucket_qkv, 'dp')]
    reduce_scatter x2 -> x0, waiting for transfers between devices: 45.7 us -> none  [the longest x1 27.6 us: finish(): lax.psum_scatter(grad_part.astype(jnp.bfloat16), 'tensor', scatter_dimens...]
    ppermute x0 -> x17, waiting for transfers between devices: none -> 38.7 us  [swap(): return lax.ppermute(array, 'tensor', [(i, i ^ mask) for i in range(count)])]
    all_to_all x3 -> x0, waiting for transfers between devices: 26.1 us -> none  [the longest x1 14.4 us: on_device(): lax.all_to_all(to_buckets(inputs, send_rows), 'dp', split_axis=0, concat_...]
    dot_general x10 -> x0, matrix products: 25.2 us -> none  [the longest x1 5.68 us: finish(): lax.dot_general(grad_key, w_key, CONTRACT_LAST, preferred_element_type=jn...]
    pallas_call x0 -> x5, Pallas kernels: none -> 21.9 us  [the longest x2 9.29 us: spread(): pl.pallas_call(spread_kernel, out_shape=(jax.ShapeDtypeStruct((rows, widt...]
    all_gather x2 -> x0, waiting for transfers between devices: 18.6 us -> none  [the longest x1 18.6 us: gather_normed(): lax.all_gather(cotangent, 'tensor', axis=1, tiled=True)]
    all_to_all x3 -> x0, starting transfers between devices: 18.4 us -> none  [the longest x1 7.25 us: on_device(): lax.all_to_all(to_buckets(inputs, send_rows), 'dp', split_axis=0, concat_...]
  transfers between devices with their start and end apart: 7 -> 17, of which waited for: 5 -> 4; matrix products, arithmetic and copies ran while one was open for 11% -> 6% of each run, Pallas kernels for 0% -> 10%
where the time goes in v1:
time: 171 us; the launch traced here: 170 us
  blocking collectives  83.5 us (49%)
  waiting for transfers between devices  38.7 us (23%)
  Pallas kernels  21.9 us (13%)
  starting transfers between devices  10.2 us (6%)
  local copies, waits for them, and re-layouts  7.61 us (4%)
  other arithmetic  6.21 us (4%)
  between operations  2.18 us (1%)
    ppermute x17, waiting for transfers between devices, swap(): return lax.ppermute(array, 'tensor', [(i, i ^ mask) for i in range(count)])  38.7 us
    all_gather x1, blocking collectives, attend_gathered(): lax.all_gather(bucket_qkv, 'dp')  31.9 us
    all_gather x1, blocking collectives, attend_gathered(): lax.all_gather(bucket_grad, 'dp').reshape(devices, devices, cap, HEAD_DIM)  30.7 us
    all_gather x1, blocking collectives, attend_gathered(): codes = lax.all_gather(code, 'dp')  20.9 us
    ppermute x17, starting transfers between devices, swap(): return lax.ppermute(array, 'tensor', [(i, i ^ mask) for i in range(count)])  10.2 us
    pallas_call x2, Pallas kernels, spread(): pl.pallas_call(spread_kernel, out_shape=(jax.ShapeDtypeStruct((rows, widt...  9.29 us
    pallas_call x1, Pallas kernels, project_rows(): pl.pallas_call(project_rows_kernel, out_shape=(jax.ShapeDtypeStruct((rows...  6.21 us
    pallas_call x1, Pallas kernels, project_grad(): pl.pallas_call(project_grad_kernel, out_shape=(jax.ShapeDtypeStruct((rows...  4.27 us
  transfers between devices with their start and end apart: 17, of which 4 were waited for; matrix products, arithmetic and copies ran while one was open for 6% of the time, Pallas kernels for 10%

profile of v1, /device:TPU:0, one launch (start us, length us, event | category | flops | bytes accessed | tf_op | source)
XLA Modules:
  0.0 170.3 jit_solution(1213461058418368704)
XLA Ops:
  1.1 2.6 %collective-permute-start.1 = (bf16[128,2048]{1,0:T(8,128)(2,1)}, bf16[128,2048]{1,0:T(8,128)(2,1)}, u32[]{:S(2)}, u32[]{:S(2)}) collective-permute-start(bf16[128,2048]{1,0:T(8,128)(2,1)} %x0.1), channel_id=1, source_target_pairs={{0,2},{1,3},{2,0},{3,1},{4,6},{5,7},{6,4},{7,5},{8,10},{9,11},{10,... | collective-permute-start | bytes 1572872 | tf_op jit(solution)/shard_map/ppermute | solution.py:33
  6.9 1.4 constant_dynamic-slice_fusion.6
  8.3 1.1 pad_maximum_fusion
  10.7 1.1 pad_maximum_fusion.2
  11.8 16.0 %collective-permute-done.6.c2 = bf16[128,2048]{1,0:T(8,128)(2,1)} collective-permute-done((bf16[128,2048]{1,0:T(8,128)(2,1)}, bf16[128,2048]{1,0:T(8,128)(2,1)}, u32[]{:S(2)}, u32[]{:S(2)}) %collective-permute-start.6) | collective-permute-done | bytes 524320 | tf_op jit(solution)/shard_map/ppermute | solution.py:33
  27.8 1.8 %collective-permute-start.4 = (bf16[2,2048]{1,0:T(2,128)(2,1)S(1)}, bf16[2,2048]{1,0:T(2,128)(2,1)S(1)}, u32[]{:S(2)}, u32[]{:S(2)}) collective-permute-start(bf16[2,2048]{1,0:T(2,128)(2,1)S(1)} %pad_maximum_fusion.5), channel_id=1, source_target_pairs={{0,2},{1,3},{2,0},{3,1},{4,6},{5,7},{6,4},{7,5},{8,10},{9,11},{10,... | collective-permute-start | bytes 24584 | tf_op jit(solution)/shard_map/ppermute | solution.py:33
  29.7 1.1 pad_maximum_fusion.3
  32.8 20.9 %all-gather.3 = s32[8,1,128]{2,1,0:T(1,128)S(1)} all-gather(s32[1,1,128]{2,1,0:T(1,128)S(1)} %bitcast.20), channel_id=4, replica_groups=mesh['dp'=8,'tensor'=4] {'dp'}, dimensions={0}, use_global_device_ids=true | all-gather | bytes 4608 | tf_op jit(solution)/shard_map/all_gather | solution.py:256
  53.9 1.0 copy-done.4
  54.9 4.3 %project_grad.1 = (bf16[128,128]{1,0:T(8,128)(2,1)}, bf16[128,128]{1,0:T(8,128)(2,1)S(1)}) custom-call(s32[4]{0:T(128)S(1)} %iota_xor_fusion.order, bf16[128,2048]{1,0:T(8,128)(2,1)S(1)} %copy-done.4, bf16[128,2048]{1,0:T(8,128)(2,1)} %collective-permute-done.5.c1, bf16[128,2048]{1,0:T(8,128)(2,1)} %collective-permute-done.6.c2, ...), custom_call_target="tpu_custom_call" | custom-call | tf_op jit(solution)/shard_map/project_grad/pallas_call | solution.py:124
  59.2 6.2 %project_rows.1 = (bf16[128,384]{1,0:T(8,128)(2,1)S(1)}, bf16[128,384]{1,0:T(8,128)(2,1)S(1)}, f32[128,1]{1,0:T(8,128)S(1)}) custom-call(s32[4]{0:T(128)S(1)} %iota_xor_fusion.order, bf16[128,2048]{1,0:T(8,128)(2,1)S(1)} %copy-done.2, bf16[128,2048]{1,0:T(8,128)(2,1)} %collective-permute-done.x1, bf16[128,2048]{1,0:T(8,128)(2,1)} %collective-permute-done.1.x2, ...), custom_call_target="tpu_custom_call" | custom-call | tf_op jit(solution)/shard_map/project_rows/pallas_call | solution.py:75
  65.4 30.7 %all-gather.1 = bf16[1024,128]{1,0:T(8,128)(2,1)S(1)} all-gather(bf16[128,128]{1,0:T(8,128)(2,1)S(1)} %get-tuple-element.11), channel_id=3, replica_groups=mesh['dp'=8,'tensor'=4] {'dp'}, dimensions={0}, use_global_device_ids=true | all-gather | bytes 294912 | tf_op jit(solution)/shard_map/all_gather | solution.py:258
  96.1 31.9 %all-gather = bf16[1024,384]{1,0:T(8,128)(2,1)S(1)} all-gather(bf16[128,384]{1,0:T(8,128)(2,1)S(1)} %get-tuple-element.10), channel_id=2, replica_groups=mesh['dp'=8,'tensor'=4] {'dp'}, dimensions={0}, use_global_device_ids=true | all-gather | bytes 884736 | tf_op jit(solution)/shard_map/all_gather | solution.py:257
  128.0 2.1 %attend_all.1.own = bf16[128,512]{1,0:T(8,128)(2,1)S(1)} custom-call(s32[1]{0:T(128)} %bitcast.me, bf16[8,8,16,384]{3,2,1,0:T(8,128)(2,1)S(1)} %bitcast.14, bf16[8,8,16,128]{3,2,1,0:T(8,128)(2,1)S(1)} %bitcast.15, s32[128,8]{1,0:T(8,128)S(1)} %copy.25.code_down, s32[8,128]{1,0:T(8,128)S(1)} %bitcast.17, s32[1,128]{1,0:T(1,128)S(1)} %copy-done.6), custom_call_target="tpu_custom_call" | custom-call | tf_op jit(solution)/shard_map/attend_all/pallas_call | solution.py:191
  130.2 1.1 slice.35.nk
  131.3 1.1 slice.36.nv
  132.4 1.1 slice.37.no
  133.5 4.7 %spread.3 = (bf16[128,2048]{1,0:T(8,128)(2,1)}, bf16[128,2048]{1,0:T(8,128)(2,1)S(1)}) custom-call(s32[4]{0:T(128)S(1)} %iota_xor_fusion.order, bf16[128,512]{1,0:T(8,128)(2,1)S(1)} %attend_all.1.own, bf16[128,512]{1,0:T(8,128)(2,1)S(1)} %collective-permute-done.8.near, bf16[8192,128]{1,0:T(8,128)(2,1)S(1)} %copy-done.1, bf16[8192,128]{1,0:T(8,128)(2,1)} %wk.3, ...), custom_call_target="tpu_custom_call" | custom-call | tf_op jit(solution)/shard_map/spread/pallas_call | solution.py:223
  138.2 1.5 collective-permute-start.14
  140.4 1.1 collective-permute-done.15
  141.6 1.5 collective-permute-start.16
  143.2 20.9 %collective-permute-done.16 = f32[128,1]{0,1:T(1,128)S(1)} collective-permute-done((f32[128,1]{0,1:T(1,128)S(1)}, f32[128,1]{0,1:T(1,128)S(1)}, u32[]{:S(2)}, u32[]{:S(2)}) %collective-permute-start.16) | collective-permute-done | bytes 544 | tf_op jit(solution)/shard_map/ppermute | solution.py:33
  164.1 4.6 %spread.2 = (f32[128,2048]{1,0:T(8,128)S(1)}, f32[128,2048]{1,0:T(8,128)S(1)}) custom-call(s32[4]{0:T(128)S(1)} %iota_xor_fusion.order, bf16[128,512]{1,0:T(8,128)(2,1)S(1)} %attend_all.1.own, bf16[128,512]{1,0:T(8,128)(2,1)S(1)} %collective-permute-done.8.near, bf16[8192,128]{1,0:T(8,128)(2,1)} %wq.3, bf16[8192,128]{1,0:T(8,128)(2,1)} %wk.3, ...), custom_call_target="tpu_custom_call" | custom-call | tf_op jit(solution)/shard_map/spread/pallas_call | solution.py:223
  168.7 1.6 fusion.6
  (68 shorter events, 6.9 us)
Async XLA Ops:
  0.6 30.9 %collective-permute-start = (bf16[128,2048]{1,0:T(8,128)(2,1)}, bf16[128,2048]{1,0:T(8,128)(2,1)}, u32[]{:S(2)}, u32[]{:S(2)}) collective-permute-start(bf16[128,2048]{1,0:T(8,128)(2,1)} %x0.1), channel_id=1, source_target_pairs={{0,1},{1,0},{2,3},{3,2},{4,5},{5,4},{6,7},{7,6},{8,9},{9,8},{10,11... | collective-permute-start | bytes 1572872 | tf_op jit(solution)/shard_map/ppermute | solution.py:33
  1.1 30.9 %collective-permute-start.1 = (bf16[128,2048]{1,0:T(8,128)(2,1)}, bf16[128,2048]{1,0:T(8,128)(2,1)}, u32[]{:S(2)}, u32[]{:S(2)}) collective-permute-start(bf16[128,2048]{1,0:T(8,128)(2,1)} %x0.1), channel_id=1, source_target_pairs={{0,2},{1,3},{2,0},{3,1},{4,6},{5,7},{6,4},{7,5},{8,10},{9,11},{10,... | collective-permute-start | bytes 1572872 | tf_op jit(solution)/shard_map/ppermute | solution.py:33
  3.7 28.4 %collective-permute-start.5 = (bf16[128,2048]{1,0:T(8,128)(2,1)}, bf16[128,2048]{1,0:T(8,128)(2,1)}, u32[]{:S(2)}, u32[]{:S(2)}) collective-permute-start(bf16[128,2048]{1,0:T(8,128)(2,1)} %c0.1), channel_id=1, source_target_pairs={{0,1},{1,0},{2,3},{3,2},{4,5},{5,4},{6,7},{7,6},{8,9},{9,8},{10,11... | collective-permute-start | bytes 1572872 | tf_op jit(solution)/shard_map/ppermute | solution.py:33
  3.9 23.9 %collective-permute-start.6 = (bf16[128,2048]{1,0:T(8,128)(2,1)}, bf16[128,2048]{1,0:T(8,128)(2,1)}, u32[]{:S(2)}, u32[]{:S(2)}) collective-permute-start(bf16[128,2048]{1,0:T(8,128)(2,1)} %c0.1), channel_id=1, source_target_pairs={{0,2},{1,3},{2,0},{3,1},{4,6},{5,7},{6,4},{7,5},{8,10},{9,11},{10,... | collective-permute-start | bytes 1572872 | tf_op jit(solution)/shard_map/ppermute | solution.py:33
  4.9 22.9 %collective-permute-start.3 = (bf16[1,2048]{1,0:T(2,128)(2,1)S(1)}, bf16[1,2048]{1,0:T(2,128)(2,1)S(1)}, u32[]{:S(2)}, u32[]{:S(2)}) collective-permute-start(bf16[1,2048]{1,0:T(2,128)(2,1)S(1)} %reshape.27), channel_id=1, source_target_pairs={{0,1},{1,0},{2,3},{3,2},{4,5},{5,4},{6,7},{7,6},{8,9},{9,8},{10,11... | collective-permute-start | bytes 12296 | tf_op jit(solution)/shard_map/ppermute | solution.py:33
  11.7 19.0 %copy-start.6 = (s32[1,128]{1,0:T(1,128)S(1)}, s32[1,128]{1,0:T(1,128)}, u32[]{:S(2)}) copy-start(s32[1,128]{1,0:T(1,128)} %send.1) | copy-start | bytes 1540
  11.7 20.9 %copy-start.10 = (s32[128]{0:T(128)S(1)}, s32[128]{0:T(128)}, u32[]{:S(2)}) copy-start(s32[128]{0:T(128)} %param.19) | copy-start | bytes 1540
  11.7 21.0 %copy-start.11 = (s32[128]{0:T(128)S(1)}, s32[128]{0:T(128)}, u32[]{:S(2)}) copy-start(s32[128]{0:T(128)} %param.18) | copy-start | bytes 1540
  27.8 4.8 %collective-permute-start.7 = (bf16[128,2048]{1,0:T(8,128)(2,1)}, bf16[128,2048]{1,0:T(8,128)(2,1)}, u32[]{:S(2)}, u32[]{:S(2)}) collective-permute-start(bf16[128,2048]{1,0:T(8,128)(2,1)} %collective-permute-done.6.c2), channel_id=1, source_target_pairs={{0,1},{1,0},{2,3},{3,2},{4,5},{5,4},{6,7},{7,6},{8,9},{9,8},{10,11... | collective-permute-start | bytes 1572872 | tf_op jit(solution)/shard_map/ppermute | solution.py:33
  27.8 3.7 %collective-permute-start.4 = (bf16[2,2048]{1,0:T(2,128)(2,1)S(1)}, bf16[2,2048]{1,0:T(2,128)(2,1)S(1)}, u32[]{:S(2)}, u32[]{:S(2)}) collective-permute-start(bf16[2,2048]{1,0:T(2,128)(2,1)S(1)} %pad_maximum_fusion.5), channel_id=1, source_target_pairs={{0,2},{1,3},{2,0},{3,1},{4,6},{5,7},{6,4},{7,5},{8,10},{9,11},{10,... | collective-permute-start | bytes 24584 | tf_op jit(solution)/shard_map/ppermute | solution.py:33
  31.6 98.6 %collective-permute-start.9 = (bf16[4096,128]{1,0:T(8,128)(2,1)}, bf16[4096,128]{1,0:T(8,128)(2,1)S(1)}, u32[]{:S(2)}, u32[]{:S(2)}) collective-permute-start(bf16[4096,128]{1,0:T(8,128)(2,1)} %pad_maximum_fusion), channel_id=1, source_target_pairs={{0,1},{1,0},{2,3},{3,2},{4,5},{5,4},{6,7},{7,6},{8,9},{9,8},{10,11... | collective-permute-start | bytes 3145736 | tf_op jit(solution)/shard_map/ppermute | solution.py:33
  31.6 98.7 %collective-permute-start.10 = (bf16[4096,128]{1,0:T(8,128)(2,1)}, bf16[4096,128]{1,0:T(8,128)(2,1)}, u32[]{:S(2)}, u32[]{:S(2)}) collective-permute-start(bf16[4096,128]{1,0:T(8,128)(2,1)} %pad_maximum_fusion.1), channel_id=1, source_target_pairs={{0,1},{1,0},{2,3},{3,2},{4,5},{5,4},{6,7},{7,6},{8,9},{9,8},{10,11... | collective-permute-start | bytes 3145736 | tf_op jit(solution)/shard_map/ppermute | solution.py:33
  32.1 99.2 %collective-permute-start.11 = (bf16[4096,128]{1,0:T(8,128)(2,1)}, bf16[4096,128]{1,0:T(8,128)(2,1)}, u32[]{:S(2)}, u32[]{:S(2)}) collective-permute-start(bf16[4096,128]{1,0:T(8,128)(2,1)} %pad_maximum_fusion.2), channel_id=1, source_target_pairs={{0,1},{1,0},{2,3},{3,2},{4,5},{5,4},{6,7},{7,6},{8,9},{9,8},{10,11... | collective-permute-start | bytes 3145736 | tf_op jit(solution)/shard_map/ppermute | solution.py:33
  32.2 100.2 %collective-permute-start.12 = (bf16[128,4096]{1,0:T(8,128)(2,1)}, bf16[128,4096]{1,0:T(8,128)(2,1)}, u32[]{:S(2)}, u32[]{:S(2)}) collective-permute-start(bf16[128,4096]{1,0:T(8,128)(2,1)} %pad_maximum_fusion.3), channel_id=1, source_target_pairs={{0,1},{1,0},{2,3},{3,2},{4,5},{5,4},{6,7},{7,6},{8,9},{9,8},{10,11... | collective-permute-start | bytes 3145736 | tf_op jit(solution)/shard_map/ppermute | solution.py:33
  32.6 26.6 %collective-permute-start.2 = (bf16[128,2048]{1,0:T(8,128)(2,1)}, bf16[128,2048]{1,0:T(8,128)(2,1)}, u32[]{:S(2)}, u32[]{:S(2)}) collective-permute-start(bf16[128,2048]{1,0:T(8,128)(2,1)} %collective-permute-done.1.x2), channel_id=1, source_target_pairs={{0,1},{1,0},{2,3},{3,2},{4,5},{5,4},{6,7},{7,6},{8,9},{9,8},{10,11... | collective-permute-start | bytes 1572872 | tf_op jit(solution)/shard_map/ppermute | solution.py:33
  54.9 4.3 %copy-start.2 = (bf16[128,2048]{1,0:T(8,128)(2,1)S(1)}, bf16[128,2048]{1,0:T(8,128)(2,1)}, u32[]{:S(2)}) copy-start(bf16[128,2048]{1,0:T(8,128)(2,1)} %x0.1) | copy-start | bytes 1572868
  130.1 3.4 %collective-permute-start.8 = (bf16[128,512]{1,0:T(8,128)(2,1)S(1)}, bf16[128,512]{1,0:T(8,128)(2,1)S(1)}, u32[]{:S(2)}, u32[]{:S(2)}) collective-permute-start(bf16[128,512]{1,0:T(8,128)(2,1)S(1)} %attend_all.1.own), channel_id=1, source_target_pairs={{0,1},{1,0},{2,3},{3,2},{4,5},{5,4},{6,7},{7,6},{8,9},{9,8},{10,11... | collective-permute-start | bytes 393224 | tf_op jit(solution)/shard_map/ppermute | solution.py:33
  133.5 9.6 %copy-start.9 = (bf16[2048]{0:T(1024)(128)(2,1)S(1)}, bf16[2048]{0:T(1024)(128)(2,1)}, u32[]{:S(2)}) copy-start(bf16[2048]{0:T(1024)(128)(2,1)} %param.12) | copy-start | bytes 12292
  138.2 30.4 %collective-permute-start.14 = (bf16[128,2048]{1,0:T(8,128)(2,1)}, bf16[128,2048]{1,0:T(8,128)(2,1)S(1)}, u32[]{:S(2)}, u32[]{:S(2)}) collective-permute-start(bf16[128,2048]{1,0:T(8,128)(2,1)} %get-tuple-element.16), channel_id=1, source_target_pairs={{0,2},{1,3},{2,0},{3,1},{4,6},{5,7},{6,4},{7,5},{8,10},{9,11},{10,... | collective-permute-start | bytes 1572872 | tf_op jit(solution)/shard_map/ppermute | solution.py:33
  139.7 28.9 %collective-permute-start.13 = (bf16[128,2048]{1,0:T(8,128)(2,1)S(1)}, bf16[128,2048]{1,0:T(8,128)(2,1)S(1)}, u32[]{:S(2)}, u32[]{:S(2)}) collective-permute-start(bf16[128,2048]{1,0:T(8,128)(2,1)S(1)} %get-tuple-element.13), channel_id=1, source_target_pairs={{0,2},{1,3},{2,0},{3,1},{4,6},{5,7},{6,4},{7,5},{8,10},{9,11},{10,... | collective-permute-start | bytes 1572872 | tf_op jit(solution)/shard_map/ppermute | solution.py:33
  140.4 1.2 collective-permute-start.15
  141.6 22.5 %collective-permute-start.16 = (f32[128,1]{0,1:T(1,128)S(1)}, f32[128,1]{0,1:T(1,128)S(1)}, u32[]{:S(2)}, u32[]{:S(2)}) collective-permute-start(f32[128,1]{0,1:T(1,128)S(1)} %bitcast_add_fusion), channel_id=1, source_target_pairs={{0,2},{1,3},{2,0},{3,1},{4,6},{5,7},{6,4},{7,5},{8,10},{9,11},{10,... | collective-permute-start | bytes 1544 | tf_op jit(solution)/shard_map/ppermute | solution.py:33
  164.1 4.6 %copy-start.3 = (bf16[128,2048]{1,0:T(8,128)(2,1)S(1)}, bf16[128,2048]{1,0:T(8,128)(2,1)}, u32[]{:S(2)}) copy-start(bf16[128,2048]{1,0:T(8,128)(2,1)} %x0.1) | copy-start | bytes 1572868
  164.1 4.6 %copy-start.5 = (bf16[128,2048]{1,0:T(8,128)(2,1)S(1)}, bf16[128,2048]{1,0:T(8,128)(2,1)}, u32[]{:S(2)}) copy-start(bf16[128,2048]{1,0:T(8,128)(2,1)} %c0.1) | copy-start | bytes 1572868
  (5 other events, 12.6 us)

commit v2 on v1

v2 whole, which is shorter than its diff:
```python
import functools
import math

import jax
import jax.numpy as jnp
from jax import lax
from jax.experimental import pallas as pl
from jax.experimental.pallas import tpu as pltpu
from jax.sharding import PartitionSpec as P

HEAD_DIM = 128
EPSILON = 1e-05
SCALING = 1.0 / math.sqrt(HEAD_DIM)
CONTRACT_LAST = (((1,), (1,)), ((), ()))
CONTRACT_FIRST = (((0,), (0,)), ((), ()))
VMEM_LIMIT = 24 * 1024 * 1024


def dot(left, right, dims=(((1,), (0,)), ((), ()))):
    return lax.dot_general(left, right, dims, preferred_element_type=jnp.float32)


def params():
    return pltpu.CompilerParams(vmem_limit_bytes=VMEM_LIMIT)


def whole(array):
    zeros = (0,) * len(array.shape)
    return pl.BlockSpec(array.shape, lambda *_: zeros)


def swap(array, mask, count):
    return lax.ppermute(array, "tensor", [(i, i ^ mask) for i in range(count)])


def one_hot(places, shape, dimension):
    rows = lax.broadcasted_iota(jnp.int32, shape, dimension)
    return jnp.where(places == rows, 1.0, 0.0).astype(jnp.bfloat16)


def write_buckets(rounded, send, buckets):
    chosen = one_hot(send[...], (send.shape[0], rounded.shape[0]), 1)
    sorted_rows = dot(chosen, rounded).astype(jnp.bfloat16)
    cap = buckets[0].shape[0]
    for index, bucket in enumerate(buckets):
        bucket[...] = sorted_rows[index * cap : (index + 1) * cap, :]


def bucket_shapes(count, slots, width):
    return [jax.ShapeDtypeStruct((slots // max(count, 1), width), jnp.bfloat16)] * count


def project_rows_kernel(
    order, x0, x1, x2, x3, g0, g1, g2, g3, weights, send, home, inverse, *rest
):
    *buckets, total = rest
    step = pl.program_id(0)
    blocks = (x0, x1, x2, x3)
    features = sum(block.shape[1] for block in blocks)

    @pl.when(step == 0)
    def _():
        squares = 0.0
        for block in blocks:
            wide = block[...].astype(jnp.float32)
            squares = squares + jnp.sum(wide * wide, axis=-1, keepdims=True)
        inverse[...] = lax.rsqrt(squares / features + EPSILON)
        total[...] = jnp.zeros_like(total)

    for index, (block, gain) in enumerate(zip(blocks, (g0, g1, g2, g3))):

        @pl.when(step == index)
        def _():
            scaled = block[...].astype(jnp.float32) * inverse[...]
            normed = (scaled * gain[...].astype(jnp.float32)).astype(jnp.bfloat16)
            total[...] += dot(normed, weights[...])

    @pl.when(step == len(blocks) - 1)
    def _():
        rounded = total[...].astype(jnp.bfloat16)
        home[...] = rounded
        if buckets:
            write_buckets(rounded, send, buckets)


def project_rows(order, blocks, gains, weights, send, count):
    rows, width = blocks[0].shape
    columns = weights.shape[1]
    shapes = [
        jax.ShapeDtypeStruct((rows, columns), jnp.bfloat16),
        jax.ShapeDtypeStruct((rows, 1), jnp.float32),
    ] + bucket_shapes(count, send.shape[0], columns)
    return pl.pallas_call(
        project_rows_kernel,
        out_shape=shapes,
        grid_spec=pltpu.PrefetchScalarGridSpec(
            num_scalar_prefetch=1,
            grid=(4,),
            in_specs=[whole(b) for b in blocks + gains]
            + [pl.BlockSpec((width, columns), lambda s, order: (order[s], 0)), whole(send)],
            out_specs=[whole(shape) for shape in shapes],
            scratch_shapes=[pltpu.VMEM((rows, columns), jnp.float32)],
        ),
        compiler_params=params(),
        name="project_rows",
    )(order, *blocks, *gains, weights, send)


def grad_part_kernel(order, block, own, near, *rest):
    *before, total, other = rest
    weights = jnp.concatenate([own[...], near[...]], axis=0)
    part = dot(block[...], weights, CONTRACT_LAST)
    heads = own.shape[0]
    for place, out in enumerate((total, other)):
        value = part[:, place * heads : (place + 1) * heads]
        out[...] = value + before[place][...] if before else value


def grad_part(order, slot, half, block, w_output, near, before):
    rows, width = block.shape
    heads = w_output.shape[0]
    shapes = [jax.ShapeDtypeStruct((rows, heads), jnp.float32)] * 2
    return pl.pallas_call(
        grad_part_kernel,
        out_shape=shapes,
        grid_spec=pltpu.PrefetchScalarGridSpec(
            num_scalar_prefetch=1,
            grid=(1,),
            in_specs=[
                whole(block),
                pl.BlockSpec((heads, width), lambda s, order: (0, order[slot])),
                pl.BlockSpec((heads, width), lambda s, order: (0, half)),
            ]
            + [whole(b) for b in before],
            out_specs=[whole(shape) for shape in shapes],
        ),
        compiler_params=params(),
        name="grad_part",
    )(order, block, w_output, near, *before)


def grad_buckets_kernel(total, other, send, *buckets):
    write_buckets((total[...] + other[...]).astype(jnp.bfloat16), send, buckets)


def grad_buckets(total, other, send, count):
    return pl.pallas_call(
        grad_buckets_kernel,
        out_shape=bucket_shapes(count, send.shape[0], total.shape[1]),
        compiler_params=params(),
        name="grad_buckets",
    )(total, other, send)


def softmax_rows(queries, key_rows, allowed):
    scores = jnp.where(allowed, dot(queries, key_rows, CONTRACT_LAST) * SCALING, -1e30)
    raised = jnp.exp(scores - jnp.max(scores, axis=-1, keepdims=True))
    return raised / jnp.sum(raised, axis=-1, keepdims=True)


def attended_rows(softmax_out, value_rows):
    return dot(softmax_out.astype(jnp.bfloat16), value_rows).astype(jnp.bfloat16)


def attention_grads(softmax_out, queries, key_rows, value_rows, head_grad):
    low_weights = softmax_out.astype(jnp.bfloat16)
    grad_value = dot(low_weights, head_grad, CONTRACT_FIRST).astype(jnp.bfloat16)
    grad_probs = dot(head_grad, value_rows, CONTRACT_LAST)
    inner = jnp.sum(softmax_out * grad_probs, axis=-1, keepdims=True)
    grad_scores = (softmax_out * (grad_probs - inner) * SCALING).astype(jnp.bfloat16)
    grad_query = dot(grad_scores, key_rows).astype(jnp.bfloat16)
    grad_key = dot(grad_scores, queries, CONTRACT_FIRST).astype(jnp.bfloat16)
    return jnp.concatenate([grad_query, grad_key, grad_value], axis=1)


def thirds(rows):
    return (rows[:, :HEAD_DIM], rows[:, HEAD_DIM : 2 * HEAD_DIM], rows[:, 2 * HEAD_DIM :])


def attend_kernel(count, code_down, code_across, *refs):
    pieces, (softmax, qkv), backs = refs[:count], refs[count : count + 2], refs[count + 2 :]
    rows = jnp.concatenate([piece[...] for piece in pieces], axis=0)
    qkv[...] = rows
    queries, key_rows, value_rows = thirds(rows)
    slots = rows.shape[0]
    down, across = code_down[...], code_across[...]
    allowed = (across <= down) & (across >= (down // slots) * slots)
    softmax_out = softmax_rows(queries, key_rows, allowed)
    softmax[...] = softmax_out
    attended = attended_rows(softmax_out, value_rows)
    cap = pieces[0].shape[0]
    for index, back in enumerate(backs):
        back[...] = attended[index * cap : (index + 1) * cap, :]


def attend(code, pieces):
    count = len(pieces)
    cap, columns = pieces[0].shape
    slots = count * cap
    return pl.pallas_call(
        functools.partial(attend_kernel, count),
        out_shape=[
            jax.ShapeDtypeStruct((slots, slots), jnp.float32),
            jax.ShapeDtypeStruct((slots, columns), jnp.bfloat16),
        ]
        + bucket_shapes(count, slots, HEAD_DIM),
        compiler_params=params(),
        name="attend",
    )(code.reshape(slots, 1), code.reshape(1, slots), *pieces)


def attend_back_kernel(softmax, qkv, *refs):
    count = len(refs) // 2
    pieces, backs = refs[:count], refs[count:]
    head_grad = jnp.concatenate([piece[...] for piece in pieces], axis=0)
    grads = attention_grads(softmax[...], *thirds(qkv[...]), head_grad)
    cap = pieces[0].shape[0]
    for index, back in enumerate(backs):
        back[...] = grads[index * cap : (index + 1) * cap, :]


def attend_back(softmax, qkv, pieces):
    return pl.pallas_call(
        attend_back_kernel,
        out_shape=bucket_shapes(len(pieces), qkv.shape[0], qkv.shape[1]),
        compiler_params=params(),
        name="attend_back",
    )(softmax, qkv, *pieces)


def bring_home_kernel(send, *refs):
    *pieces, out = refs
    rows = jnp.concatenate([piece[...] for piece in pieces], axis=0)
    chosen = one_hot(send[...], (out.shape[0], rows.shape[0]), 0)
    out[...] = dot(chosen, rows).astype(jnp.bfloat16)


def bring_home(send, pieces, rows):
    return pl.pallas_call(
        bring_home_kernel,
        out_shape=jax.ShapeDtypeStruct((rows, pieces[0].shape[1]), jnp.bfloat16),
        compiler_params=params(),
        name="bring_home",
    )(send, *pieces)


def spread_kernel(dims, order, own, near, own_weights, near_weights, out):
    total = dot(own[...], own_weights[...], dims) + dot(near[...], near_weights[...], dims)
    out[...] = total.astype(out.dtype)


def spread_grad(order, slot, half, own, near, weights, near_weights, start, span, dtype, tile=512):
    rows, columns = own.shape
    width = near_weights.shape[0] // 2
    steps, first = width // tile, start // tile
    return pl.pallas_call(
        functools.partial(spread_kernel, CONTRACT_LAST),
        out_shape=jax.ShapeDtypeStruct((rows, span), dtype),
        grid_spec=pltpu.PrefetchScalarGridSpec(
            num_scalar_prefetch=1,
            grid=(span // tile,),
            in_specs=[
                whole(own),
                whole(near),
                pl.BlockSpec((tile, columns), lambda j, order: (order[slot] * steps + first + j, 0)),
                pl.BlockSpec((tile, columns), lambda j, order: (half * steps + first + j, 0)),
            ],
            out_specs=pl.BlockSpec((rows, tile), lambda j, order: (0, j)),
        ),
        compiler_params=params(),
        name="spread_grad",
    )(order, own, near, weights, near_weights)


def spread_out(order, slot, half, own, near, weights, near_weights, dtype, tile=1024):
    rows, heads = own.shape
    width = near_weights.shape[1] // 2
    steps = width // tile
    return pl.pallas_call(
        functools.partial(spread_kernel, (((1,), (0,)), ((), ()))),
        out_shape=jax.ShapeDtypeStruct((rows, width), dtype),
        grid_spec=pltpu.PrefetchScalarGridSpec(
            num_scalar_prefetch=1,
            grid=(steps,),
            in_specs=[
                whole(own),
                whole(near),
                pl.BlockSpec((heads, tile), lambda j, order: (0, order[slot] * steps + j)),
                pl.BlockSpec((heads, tile), lambda j, order: (0, half * steps + j)),
            ],
            out_specs=pl.BlockSpec((rows, tile), lambda j, order: (0, j)),
        ),
        compiler_params=params(),
        name="spread_out",
    )(order, own, near, weights, near_weights)


def exchange(pieces):
    count = len(pieces)
    return [pieces[0]] + [
        lax.ppermute(piece, "dp", [(i, i ^ k) for i in range(count)])
        for k, piece in enumerate(pieces)
        if k
    ]


def balanced_codes(receive_slots, owner_segments, slots):
    rows = receive_slots.shape[0]
    taken = receive_slots[:, None] == jnp.arange(slots, dtype=jnp.int32)[None, :]
    code = owner_segments * slots + jnp.arange(rows, dtype=jnp.int32)
    return jnp.sum(jnp.where(taken, code[:, None], 0), axis=0)


def attend_sparse(qkv, head_grad, send_rows, receive_slots, owner_segments):
    rows = qkv.shape[0]
    slots = send_rows.shape[1]
    both = jnp.concatenate([qkv, head_grad], axis=1)
    padded = jnp.concatenate([both, jnp.zeros((1, 4 * HEAD_DIM), both.dtype)], axis=0)
    moved = lax.all_to_all(padded[send_rows[0]], "dp", split_axis=0, concat_axis=0, tiled=True)
    queries, key_rows, value_rows, grads = jnp.split(moved[receive_slots], 4, axis=1)
    position = jnp.arange(rows, dtype=jnp.int32)
    same = owner_segments[:, None] == owner_segments[None, :]
    allowed = same & (position[None, :] <= position[:, None])
    softmax_out = softmax_rows(queries, key_rows, allowed)
    attended = attended_rows(softmax_out, value_rows)
    grads = attention_grads(softmax_out, queries, key_rows, value_rows, grads)
    results = jnp.concatenate([attended, grads], axis=1)
    back = jnp.zeros((slots, 4 * HEAD_DIM), jnp.bfloat16).at[receive_slots].set(results)
    back = lax.all_to_all(back, "dp", split_axis=0, concat_axis=0, tiled=True)
    home = jnp.zeros((rows, 4 * HEAD_DIM), jnp.bfloat16).at[send_rows[0]].set(back, mode="drop")
    return home[:, :HEAD_DIM], home[:, HEAD_DIM:]


def on_device(
    inputs,
    cotangent,
    norm_gain,
    w_query,
    w_key,
    w_value,
    w_output,
    send_rows,
    receive_slots,
    owner_segments,
):
    rows, width = inputs.shape
    slots = send_rows.shape[1]
    tensor = lax.axis_size("tensor")
    owners = lax.axis_size("dp")
    features = width * tensor
    order = lax.axis_index("tensor").astype(jnp.int32) ^ jnp.arange(4, dtype=jnp.int32)
    dense = slots == rows and owners & (owners - 1) == 0
    count = owners if dense else 0
    gain_row = norm_gain.reshape(1, width)

    gain2 = swap(gain_row, 2, tensor)
    gain1 = swap(gain_row, 1, tensor)
    x2 = swap(inputs, 2, tensor)
    x1 = swap(inputs, 1, tensor)
    later, x2 = lax.optimization_barrier((cotangent, x2))
    c2 = swap(later, 2, tensor)
    x3 = swap(x2, 1, tensor)
    gain3 = swap(gain2, 1, tensor)

    weights = jnp.concatenate([w_query, w_key, w_value], axis=1)
    near_weights = swap(
        jnp.concatenate(
            [lax.dynamic_slice_in_dim(weights, order[s] * width, width, axis=0) for s in (1, 3)],
            axis=0,
        ),
        1,
        tensor,
    )
    near_output = swap(
        jnp.concatenate(
            [lax.dynamic_slice_in_dim(w_output, order[s] * width, width, axis=1) for s in (1, 3)],
            axis=1,
        ),
        1,
        tensor,
    )
    if dense:
        turned = lax.axis_index("dp").astype(jnp.int32) ^ jnp.arange(owners, dtype=jnp.int32)
        code = balanced_codes(receive_slots, owner_segments, slots)
        code = code.reshape(owners, -1)[turned].reshape(-1)
        send = send_rows.reshape(owners, -1)[turned].reshape(-1)
    else:
        send = send_rows.reshape(-1)
    send_down = send.reshape(slots, 1)
    send_across = send.reshape(1, slots)

    first = grad_part(order, 0, 0, cotangent, w_output, near_output, ())
    home, inverse_rms, *buckets = project_rows(
        order, [inputs, x1, x2, x3], [gain_row, gain1, gain2, gain3], weights, send_down, count
    )
    if dense:
        softmax, qkv, *backs = attend(code, exchange(buckets))
        attended = bring_home(send_across, exchange(backs), rows)
    own_grad, near_grad = grad_part(order, 2, 1, c2, w_output, near_output, first)
    got_grad = swap(near_grad, 1, tensor)
    if dense:
        grad_pieces = exchange(grad_buckets(own_grad, got_grad, send_down, count))
        backs = attend_back(softmax, qkv, grad_pieces)
        grads = bring_home(send_across, exchange(backs), rows)
    else:
        head_grad = (own_grad + got_grad).astype(jnp.bfloat16)
        attended, grads = attend_sparse(home, head_grad, send_rows, receive_slots, owner_segments)

    attended_near = swap(attended, 1, tensor)
    out_far = spread_out(
        order, 2, 1, attended, attended_near, w_output, near_output, jnp.bfloat16
    )
    out_got = swap(out_far, 2, tensor)
    out_own = spread_out(
        order, 0, 0, attended, attended_near, w_output, near_output, jnp.float32
    )

    grads_near = swap(grads, 1, tensor)
    span = width // 2
    grad_got = []
    for start in (0, span):
        part = spread_grad(
            order, 2, 1, grads, grads_near, weights, near_weights, start, span, jnp.bfloat16
        )
        grad_got.append(swap(part, 2, tensor))
    grad_own = spread_grad(
        order, 0, 0, grads, grads_near, weights, near_weights, 0, width, jnp.float32
    )
    row_dot = jnp.sum(
        grads.astype(jnp.float32) * home.astype(jnp.float32), axis=-1, keepdims=True
    )
    row_dot = row_dot + swap(row_dot, 1, tensor)
    row_dot, grad_own = lax.optimization_barrier((row_dot, grad_own))
    row_dot = row_dot + swap(row_dot, 2, tensor)

    wide_in = inputs.astype(jnp.float32)
    layer_out = (wide_in + out_own + out_got.astype(jnp.float32)).astype(jnp.bfloat16)
    scaled = wide_in * inverse_rms
    grad_sum = grad_own + jnp.concatenate(grad_got, axis=1).astype(jnp.float32)
    grad_hat = grad_sum * norm_gain.astype(jnp.float32)
    input_grad = (
        cotangent.astype(jnp.float32) + inverse_rms * (grad_hat - scaled * (row_dot / features))
    ).astype(jnp.bfloat16)
    return (layer_out, input_grad)


def solution(mesh):
    return jax.shard_map(
        on_device,
        mesh=mesh,
        in_specs=(
            P("dp", "tensor"),
            P("dp", "tensor"),
            P("tensor"),
            P(None, "tensor"),
            P(None, "tensor"),
            P(None, "tensor"),
            P("tensor", None),
            P("dp", None),
            P("dp"),
            P("dp"),
        ),
        out_specs=(P("dp", "tensor"), P("dp", "tensor")),
        check_vma=False,
    )
```

time: 171 us -> 142 us (0.83)
  blocking collectives: 83.5 us -> 0 us
  starting transfers between devices: 10.2 us -> 57.2 us
  waiting for transfers between devices: 38.7 us -> 25.7 us
  local copies, waits for them, and re-layouts: 7.61 us -> 20.4 us
  Pallas kernels: 21.9 us -> 26.9 us
  other arithmetic: 6.21 us -> 8.4 us
    all_gather x3 -> x0, blocking collectives: 83.5 us -> none  [the longest x1 31.9 us: attend_gathered(): lax.all_gather(bucket_qkv, 'dp')]
    ppermute x0 -> x28, starting transfers between devices: none -> 45.4 us  [exchange(): lax.ppermute(piece, 'dp', [(i, i ^ k) for i in range(count)])]
    ppermute x17, waiting for transfers between devices: 38.7 us -> 14.1 us  [swap(): return lax.ppermute(array, 'tensor', [(i, i ^ mask) for i in range(count)])]
    unnamed x24 -> x47, local copies, waits for them, and re-layouts: 1.21 us -> 13.2 us
    ppermute x0 -> x28, waiting for transfers between devices: none -> 11.6 us  [exchange(): lax.ppermute(piece, 'dp', [(i, i ^ k) for i in range(count)])]
    pallas_call x5 -> x13, Pallas kernels: 21.9 us -> 26.9 us  [the longest x3 9.74 us: spread_grad(): pl.pallas_call(functools.partial(spread_kernel, CONTRACT_LAST), out_shape...]
    slice x5 -> x1, local copies, waits for them, and re-layouts: 3.86 us -> 0.59 us  [on_device(): order[s] * width]
    concatenate x6 -> x2, other arithmetic: 4.27 us -> 3.1 us  [the longest x1 2.06 us: on_device(): jnp.concatenate([lax.dynamic_slice_in_dim(weights, order[s] * width, widt...]
  transfers between devices with their start and end apart: 17 -> 45, of which waited for: 4 -> 15; matrix products, arithmetic and copies ran while one was open for 6% -> 5% of each run, Pallas kernels for 10% -> 19%
where the time goes in v2:
time: 142 us; the launch traced here: 141 us
  starting transfers between devices  57.2 us (40%)
  Pallas kernels  26.9 us (19%)
  waiting for transfers between devices  25.7 us (18%)
  local copies, waits for them, and re-layouts  20.4 us (14%)
  other arithmetic  8.4 us (6%)
  between operations  2.3 us (2%)
    ppermute x28, starting transfers between devices, exchange(): lax.ppermute(piece, 'dp', [(i, i ^ k) for i in range(count)])  45.4 us
    ppermute x17, waiting for transfers between devices, swap(): return lax.ppermute(array, 'tensor', [(i, i ^ mask) for i in range(count)])  14.1 us
    unnamed x47, local copies, waits for them, and re-layouts  13.2 us
    ppermute x17, starting transfers between devices, swap(): return lax.ppermute(array, 'tensor', [(i, i ^ mask) for i in range(count)])  11.7 us
    ppermute x28, waiting for transfers between devices, exchange(): lax.ppermute(piece, 'dp', [(i, i ^ k) for i in range(count)])  11.6 us
    pallas_call x3, Pallas kernels, spread_grad(): pl.pallas_call(functools.partial(spread_kernel, CONTRACT_LAST), out_shape...  9.74 us
    pallas_call x1, Pallas kernels, project_rows(): pl.pallas_call(project_rows_kernel, out_shape=shapes, grid_spec=pltpu.Pre...  6.31 us
    pallas_call x2, Pallas kernels, grad_part(): pl.pallas_call(grad_part_kernel, out_shape=shapes, grid_spec=pltpu.Prefet...  4.74 us
  transfers between devices with their start and end apart: 45, of which 15 were waited for; matrix products, arithmetic and copies ran while one was open for 5% of the time, Pallas kernels for 19%

profile of v2, /device:TPU:0, one launch (start us, length us, event | category | flops | bytes accessed | tf_op | source)
XLA Modules:
  0.0 140.8 jit_solution(9396244256939247938)
XLA Ops:
  2.6 3.3 %constant_dynamic-update-slice_fusion.2 = bf16[8192,384]{1,0:T(8,128)(2,1)} fusion(bf16[8192,128]{1,0:T(8,128)(2,1)} %param.13), kind=kLoop, calls=%fused_computation.18 | loop fusion | bytes 4194304
  8.9 2.2 %constant_dynamic-slice_fusion.1 = (bf16[2048,384]{1,0:T(8,128)(2,1)S(1)}, bf16[2048,384]{1,0:T(8,128)(2,1)S(1)}) fusion(bf16[8192,384]{1,0:T(8,128)(2,1)} %constant_dynamic-update-slice_fusion.weights.own_weights, s32[]{:T(128)S(6)} %select_n.25, s32[]{:T(128)S(6)} %select_n.26), kind=kLoop, calls=%fused_computation.22 | loop fusion | bytes 6291464 | tf_op jit(solution)/shard_map/dynamic_slice | solution.py:368
  13.6 2.5 %collective-permute-start.1 = (bf16[128,2048]{1,0:T(8,128)(2,1)}, bf16[128,2048]{1,0:T(8,128)(2,1)}, u32[]{:S(2)}, u32[]{:S(2)}) collective-permute-start(bf16[128,2048]{1,0:T(8,128)(2,1)} %x0.1), channel_id=1, source_target_pairs={{0,2},{1,3},{2,0},{3,1},{4,6},{5,7},{6,4},{7,5},{8,10},{9,11},{10,... | collective-permute-start | bytes 1572872 | tf_op jit(solution)/shard_map/ppermute | solution.py:33
  18.0 11.2 %collective-permute-done.4.g2 = bf16[1,2048]{1,0:T(2,128)(2,1)S(1)} collective-permute-done((bf16[1,2048]{1,0:T(2,128)(2,1)S(1)}, bf16[1,2048]{1,0:T(2,128)(2,1)S(1)}, u32[]{:S(2)}, u32[]{:S(2)}) %collective-permute-start.4) | collective-permute-done | bytes 4128 | tf_op jit(solution)/shard_map/ppermute | solution.py:33
  34.0 6.3 %project_rows.1 = (bf16[128,384]{1,0:T(8,128)(2,1)S(1)}, f32[128,1]{1,0:T(8,128)S(1)}, bf16[16,384]{1,0:T(8,128)(2,1)S(1)}, bf16[16,384]{1,0:T(8,128)(2,1)S(1)},...) custom-call(s32[4]{0:T(128)S(1)} %iota_xor_fusion.order, ...), custom_call_target="tpu_custom_call" | custom-call | tf_op jit(solution)/shard_map/project_rows/pallas_call | solution.py:93
  44.6 2.7 %collective-permute-start.8 = (bf16[16,384]{1,0:T(8,128)(2,1)S(1)}, bf16[16,384]{1,0:T(8,128)(2,1)S(1)}, u32[]{:S(2)}, u32[]{:S(2)}) collective-permute-start(bf16[16,384]{1,0:T(8,128)(2,1)S(1)} %get-tuple-element.50), channel_id=1, source_target_pairs={{0,12},{4,8},{8,4},{12,0},{16,28},{20,24},{24,20},{28,16},{1,13},{... | collective-permute-start | bytes 36872 | tf_op jit(solution)/shard_map/ppermute | solution.py:301
  47.4 2.6 %collective-permute-start.9 = (bf16[16,384]{1,0:T(8,128)(2,1)S(1)}, bf16[16,384]{1,0:T(8,128)(2,1)S(1)}, u32[]{:S(2)}, u32[]{:S(2)}) collective-permute-start(bf16[16,384]{1,0:T(8,128)(2,1)S(1)} %get-tuple-element.51), channel_id=1, source_target_pairs={{0,16},{4,20},{8,24},{12,28},{16,0},{20,4},{24,8},{28,12},{1,17},{... | collective-permute-start | bytes 36872 | tf_op jit(solution)/shard_map/ppermute | solution.py:301
  52.0 2.7 %grad_part.3 = (f32[128,128]{1,0:T(8,128)S(1)}, f32[128,128]{1,0:T(8,128)}) custom-call(s32[4]{0:T(128)S(1)} %iota_xor_fusion.order, bf16[128,2048]{1,0:T(8,128)(2,1)} %collective-permute-done.23.block, bf16[128,8192]{1,0:T(8,128)(2,1)S(1)} %copy-done, bf16[128,4096]{1,0:T(8,128)(2,1)S(1)} %collective-permute-done.21.near_weights.near, ...), custom_call_target="tpu_custom_call" | custom-call | tf_op jit(solution)/shard_map/grad_part/pallas_call | solution.py:123
  55.7 2.5 %collective-permute-start.11 = (bf16[16,384]{1,0:T(8,128)(2,1)S(1)}, bf16[16,384]{1,0:T(8,128)(2,1)S(1)}, u32[]{:S(2)}, u32[]{:S(2)}) collective-permute-start(bf16[16,384]{1,0:T(8,128)(2,1)S(1)} %get-tuple-element.53), channel_id=1, source_target_pairs={{0,24},{4,28},{8,16},{12,20},{16,8},{20,12},{24,0},{28,4},{1,25},{... | collective-permute-start | bytes 36872 | tf_op jit(solution)/shard_map/ppermute | solution.py:301
  58.1 2.3 %collective-permute-start.12 = (bf16[16,384]{1,0:T(8,128)(2,1)S(1)}, bf16[16,384]{1,0:T(8,128)(2,1)S(1)}, u32[]{:S(2)}, u32[]{:S(2)}) collective-permute-start(bf16[16,384]{1,0:T(8,128)(2,1)S(1)} %get-tuple-element.54), channel_id=1, source_target_pairs={{0,28},{4,24},{8,20},{12,16},{16,12},{20,8},{24,4},{28,0},{1,29},{... | collective-permute-start | bytes 36872 | tf_op jit(solution)/shard_map/ppermute | solution.py:301
  74.0 2.4 %collective-permute-start.17 = (bf16[16,128]{1,0:T(8,128)(2,1)}, bf16[16,128]{1,0:T(8,128)(2,1)S(1)}, u32[]{:S(2)}, u32[]{:S(2)}) collective-permute-start(bf16[16,128]{1,0:T(8,128)(2,1)} %get-tuple-element.60), channel_id=1, source_target_pairs={{0,20},{4,16},{8,28},{12,24},{16,4},{20,0},{24,12},{28,8},{1,21},{... | collective-permute-start | bytes 12296 | tf_op jit(solution)/shard_map/ppermute | solution.py:301
  77.7 2.5 %collective-permute-start.19 = (bf16[16,128]{1,0:T(8,128)(2,1)}, bf16[16,128]{1,0:T(8,128)(2,1)S(1)}, u32[]{:S(2)}, u32[]{:S(2)}) collective-permute-start(bf16[16,128]{1,0:T(8,128)(2,1)} %get-tuple-element.62), channel_id=1, source_target_pairs={{0,28},{4,24},{8,20},{12,16},{16,12},{20,8},{24,4},{28,0},{1,29},{... | collective-permute-start | bytes 12296 | tf_op jit(solution)/shard_map/ppermute | solution.py:301
  82.0 2.2 %collective-permute-done.19.refs_7_ = bf16[16,128]{1,0:T(8,128)(2,1)S(1)} collective-permute-done((bf16[16,128]{1,0:T(8,128)(2,1)}, bf16[16,128]{1,0:T(8,128)(2,1)S(1)}, u32[]{:S(2)}, u32[]{:S(2)}) %collective-permute-start.19) | collective-permute-done | bytes 4128 | tf_op jit(solution)/shard_map/ppermute | solution.py:301
  87.1 2.7 %collective-permute-start.27 = (bf16[16,128]{1,0:T(8,128)(2,1)S(1)}, bf16[16,128]{1,0:T(8,128)(2,1)S(1)}, u32[]{:S(2)}, u32[]{:S(2)}) collective-permute-start(bf16[16,128]{1,0:T(8,128)(2,1)S(1)} %get-tuple-element.74), channel_id=1, source_target_pairs={{0,12},{4,8},{8,4},{12,0},{16,28},{20,24},{24,20},{28,16},{1,13},{... | collective-permute-start | bytes 12296 | tf_op jit(solution)/shard_map/ppermute | solution.py:301
  90.8 2.3 %collective-permute-start.29 = (bf16[16,128]{1,0:T(8,128)(2,1)S(1)}, bf16[16,128]{1,0:T(8,128)(2,1)S(1)}, u32[]{:S(2)}, u32[]{:S(2)}) collective-permute-start(bf16[16,128]{1,0:T(8,128)(2,1)S(1)} %get-tuple-element.76), channel_id=1, source_target_pairs={{0,20},{4,16},{8,28},{12,24},{16,4},{20,0},{24,12},{28,8},{1,21},{... | collective-permute-start | bytes 12296 | tf_op jit(solution)/shard_map/ppermute | solution.py:301
  93.1 2.2 %collective-permute-start.30 = (bf16[16,128]{1,0:T(8,128)(2,1)S(1)}, bf16[16,128]{1,0:T(8,128)(2,1)S(1)}, u32[]{:S(2)}, u32[]{:S(2)}) collective-permute-start(bf16[16,128]{1,0:T(8,128)(2,1)S(1)} %get-tuple-element.77), channel_id=1, source_target_pairs={{0,24},{4,28},{8,16},{12,20},{16,8},{20,12},{24,0},{28,4},{1,25},{... | collective-permute-start | bytes 12296 | tf_op jit(solution)/shard_map/ppermute | solution.py:301
  95.3 2.3 %collective-permute-start.31 = (bf16[16,128]{1,0:T(8,128)(2,1)S(1)}, bf16[16,128]{1,0:T(8,128)(2,1)S(1)}, u32[]{:S(2)}, u32[]{:S(2)}) collective-permute-start(bf16[16,128]{1,0:T(8,128)(2,1)S(1)} %get-tuple-element.78), channel_id=1, source_target_pairs={{0,28},{4,24},{8,20},{12,16},{16,12},{20,8},{24,4},{28,0},{1,29},{... | collective-permute-start | bytes 12296 | tf_op jit(solution)/shard_map/ppermute | solution.py:301
  98.5 3.1 %collective-permute-done.31.refs_7_ = bf16[16,128]{1,0:T(8,128)(2,1)S(1)} collective-permute-done((bf16[16,128]{1,0:T(8,128)(2,1)S(1)}, bf16[16,128]{1,0:T(8,128)(2,1)S(1)}, u32[]{:S(2)}, u32[]{:S(2)}) %collective-permute-start.31) | collective-permute-done | bytes 4128 | tf_op jit(solution)/shard_map/ppermute | solution.py:301
  106.6 3.7 %collective-permute-start.36 = (bf16[16,384]{1,0:T(8,128)(2,1)S(1)}, bf16[16,384]{1,0:T(8,128)(2,1)S(1)}, u32[]{:S(2)}, u32[]{:S(2)}) collective-permute-start(bf16[16,384]{1,0:T(8,128)(2,1)S(1)} %get-tuple-element.84), channel_id=1, source_target_pairs={{0,20},{4,16},{8,28},{12,24},{16,4},{20,0},{24,12},{28,8},{1,21},{... | collective-permute-start | bytes 36872 | tf_op jit(solution)/shard_map/ppermute | solution.py:301
  111.6 2.5 %collective-permute-start.38 = (bf16[16,384]{1,0:T(8,128)(2,1)S(1)}, bf16[16,384]{1,0:T(8,128)(2,1)S(1)}, u32[]{:S(2)}, u32[]{:S(2)}) collective-permute-start(bf16[16,384]{1,0:T(8,128)(2,1)S(1)} %get-tuple-element.86), channel_id=1, source_target_pairs={{0,28},{4,24},{8,20},{12,16},{16,12},{20,8},{24,4},{28,0},{1,29},{... | collective-permute-start | bytes 36872 | tf_op jit(solution)/shard_map/ppermute | solution.py:301
  119.6 2.5 %spread_grad.5 = bf16[128,1024]{1,0:T(8,128)(2,1)S(1)} custom-call(s32[4]{0:T(128)S(1)} %iota_xor_fusion.order, bf16[128,384]{1,0:T(8,128)(2,1)S(1)} %bring_home.3.own, bf16[128,384]{1,0:T(8,128)(2,1)S(1)} %collective-permute-done.40.near, bf16[8192,384]{1,0:T(8,128)(2,1)} %constant_dynamic-update-slice_fusion.weights.own_weights, ...), custom_call_target="tpu_custom_call" | custom-call | tf_op jit(solution)/shard_map/spread_grad/pallas_call | solution.py:256
  123.7 3.1 %spread_grad.4 = bf16[128,1024]{1,0:T(8,128)(2,1)} custom-call(s32[4]{0:T(128)S(1)} %iota_xor_fusion.order, bf16[128,384]{1,0:T(8,128)(2,1)S(1)} %bring_home.3.own, bf16[128,384]{1,0:T(8,128)(2,1)S(1)} %collective-permute-done.40.near, bf16[8192,384]{1,0:T(8,128)(2,1)} %constant_dynamic-update-slice_fusion.weights.own_weights, ...), custom_call_target="tpu_custom_call" | custom-call | tf_op jit(solution)/shard_map/spread_grad/pallas_call | solution.py:256
  127.8 4.1 %spread_grad.3 = f32[128,2048]{1,0:T(8,128)S(1)} custom-call(s32[4]{0:T(128)S(1)} %iota_xor_fusion.order, bf16[128,384]{1,0:T(8,128)(2,1)S(1)} %bring_home.3.own, bf16[128,384]{1,0:T(8,128)(2,1)S(1)} %collective-permute-done.40.near, bf16[8192,384]{1,0:T(8,128)(2,1)} %constant_dynamic-update-slice_fusion.weights.own_weights, ...), custom_call_target="tpu_custom_call" | custom-call | tf_op jit(solution)/shard_map/spread_grad/pallas_call | solution.py:256
  137.7 3.1 %fusion.6 = (bf16[128,2048]{1,0:T(8,128)(2,1)}, bf16[128,2048]{1,0:T(8,128)(2,1)}) fusion(bf16[128,2048]{1,0:T(8,128)(2,1)} %x0.1, f32[128,2048]{1,0:T(8,128)S(1)} %copy-done.2, bf16[128,2048]{1,0:T(8,128)(2,1)} %block.1, bf16[128,1024]{1,0:T(8,128)(2,1)} %collective-permute-done.43, bf16[128,1024]{1,0:T(8,128)(2,1)} %collective-permute-done.42, ...), kind=kLoop, calls=%fused_computation.11 | loop fusion | flops 4718592 | bytes 5252096 | tf_op jit(solution)/shard_map/convert_element_type | solution.py:443
  (153 shorter events, 61.8 us)
Async XLA Ops:
  13.2 106.4 %collective-permute-start.41 = (bf16[4096,384]{1,0:T(8,128)(2,1)}, bf16[4096,384]{1,0:T(8,128)(2,1)}, u32[]{:S(2)}, u32[]{:S(2)}) collective-permute-start(bf16[4096,384]{1,0:T(8,128)(2,1)} %pad_maximum_fusion), channel_id=1, source_target_pairs={{0,1},{1,0},{2,3},{3,2},{4,5},{5,4},{6,7},{7,6},{8,9},{9,8},{10,11... | collective-permute-start | bytes 9437192 | tf_op jit(solution)/shard_map/ppermute | solution.py:33
  13.6 15.5 %collective-permute-start.1 = (bf16[128,2048]{1,0:T(8,128)(2,1)}, bf16[128,2048]{1,0:T(8,128)(2,1)}, u32[]{:S(2)}, u32[]{:S(2)}) collective-permute-start(bf16[128,2048]{1,0:T(8,128)(2,1)} %x0.1), channel_id=1, source_target_pairs={{0,2},{1,3},{2,0},{3,1},{4,6},{5,7},{6,4},{7,5},{8,10},{9,11},{10,... | collective-permute-start | bytes 1572872 | tf_op jit(solution)/shard_map/ppermute | solution.py:33
  17.3 30.1 %collective-permute-start.21 = (bf16[128,4096]{1,0:T(8,128)(2,1)}, bf16[128,4096]{1,0:T(8,128)(2,1)S(1)}, u32[]{:S(2)}, u32[]{:S(2)}) collective-permute-start(bf16[128,4096]{1,0:T(8,128)(2,1)} %pad_maximum_fusion.1), channel_id=1, source_target_pairs={{0,1},{1,0},{2,3},{3,2},{4,5},{5,4},{6,7},{7,6},{8,9},{9,8},{10,11... | collective-permute-start | bytes 3145736 | tf_op jit(solution)/shard_map/ppermute | solution.py:33
  17.6 11.6 %collective-permute-start.4 = (bf16[1,2048]{1,0:T(2,128)(2,1)S(1)}, bf16[1,2048]{1,0:T(2,128)(2,1)S(1)}, u32[]{:S(2)}, u32[]{:S(2)}) collective-permute-start(bf16[1,2048]{1,0:T(2,128)(2,1)S(1)} %reshape.38.g0), channel_id=1, source_target_pairs={{0,2},{1,3},{2,0},{3,1},{4,6},{5,7},{6,4},{7,5},{8,10},{9,11},{10,... | collective-permute-start | bytes 12296 | tf_op jit(solution)/shard_map/ppermute | solution.py:33
  17.9 11.8 %collective-permute-start.3 = (bf16[1,2048]{1,0:T(2,128)(2,1)S(1)}, bf16[1,2048]{1,0:T(2,128)(2,1)S(1)}, u32[]{:S(2)}, u32[]{:S(2)}) collective-permute-start(bf16[1,2048]{1,0:T(2,128)(2,1)S(1)} %reshape.38.g0), channel_id=1, source_target_pairs={{0,1},{1,0},{2,3},{3,2},{4,5},{5,4},{6,7},{7,6},{8,9},{9,8},{10,11... | collective-permute-start | bytes 12296 | tf_op jit(solution)/shard_map/ppermute | solution.py:33
  30.3 14.3 %collective-permute-start.23 = (bf16[128,2048]{1,0:T(8,128)(2,1)}, bf16[128,2048]{1,0:T(8,128)(2,1)}, u32[]{:S(2)}, u32[]{:S(2)}) collective-permute-start(bf16[128,2048]{1,0:T(8,128)(2,1)} %block.1), channel_id=1, source_target_pairs={{0,2},{1,3},{2,0},{3,1},{4,6},{5,7},{6,4},{7,5},{8,10},{9,11},{10,... | collective-permute-start | bytes 1572872 | tf_op jit(solution)/shard_map/ppermute | solution.py:33
  41.0 14.4 %collective-permute-start.6 = (bf16[16,384]{1,0:T(8,128)(2,1)S(1)}, bf16[16,384]{1,0:T(8,128)(2,1)S(1)}, u32[]{:S(2)}, u32[]{:S(2)}) collective-permute-start(bf16[16,384]{1,0:T(8,128)(2,1)S(1)} %get-tuple-element.48), channel_id=1, source_target_pairs={{0,4},{4,0},{8,12},{12,8},{16,20},{20,16},{24,28},{28,24},{1,5},{5... | collective-permute-start | bytes 36872 | tf_op jit(solution)/shard_map/ppermute | solution.py:301
  42.5 13.2 %collective-permute-start.7 = (bf16[16,384]{1,0:T(8,128)(2,1)S(1)}, bf16[16,384]{1,0:T(8,128)(2,1)S(1)}, u32[]{:S(2)}, u32[]{:S(2)}) collective-permute-start(bf16[16,384]{1,0:T(8,128)(2,1)S(1)} %get-tuple-element.49), channel_id=1, source_target_pairs={{0,8},{4,12},{8,0},{12,4},{16,24},{20,28},{24,16},{28,20},{1,9},{5... | collective-permute-start | bytes 36872 | tf_op jit(solution)/shard_map/ppermute | solution.py:301
  44.6 13.5 %collective-permute-start.8 = (bf16[16,384]{1,0:T(8,128)(2,1)S(1)}, bf16[16,384]{1,0:T(8,128)(2,1)S(1)}, u32[]{:S(2)}, u32[]{:S(2)}) collective-permute-start(bf16[16,384]{1,0:T(8,128)(2,1)S(1)} %get-tuple-element.50), channel_id=1, source_target_pairs={{0,12},{4,8},{8,4},{12,0},{16,28},{20,24},{24,20},{28,16},{1,13},{... | collective-permute-start | bytes 36872 | tf_op jit(solution)/shard_map/ppermute | solution.py:301
  47.4 13.0 %collective-permute-start.9 = (bf16[16,384]{1,0:T(8,128)(2,1)S(1)}, bf16[16,384]{1,0:T(8,128)(2,1)S(1)}, u32[]{:S(2)}, u32[]{:S(2)}) collective-permute-start(bf16[16,384]{1,0:T(8,128)(2,1)S(1)} %get-tuple-element.51), channel_id=1, source_target_pairs={{0,16},{4,20},{8,24},{12,28},{16,0},{20,4},{24,8},{28,12},{1,17},{... | collective-permute-start | bytes 36872 | tf_op jit(solution)/shard_map/ppermute | solution.py:301
  55.4 6.5 %collective-permute-start.10 = (bf16[16,384]{1,0:T(8,128)(2,1)S(1)}, bf16[16,384]{1,0:T(8,128)(2,1)S(1)}, u32[]{:S(2)}, u32[]{:S(2)}) collective-permute-start(bf16[16,384]{1,0:T(8,128)(2,1)S(1)} %get-tuple-element.52), channel_id=1, source_target_pairs={{0,20},{4,16},{8,28},{12,24},{16,4},{20,0},{24,12},{28,8},{1,21},{... | collective-permute-start | bytes 36872 | tf_op jit(solution)/shard_map/ppermute | solution.py:301
  60.4 23.9 %collective-permute-start.24 = (f32[128,128]{1,0:T(8,128)}, f32[128,128]{1,0:T(8,128)}, u32[]{:S(2)}, u32[]{:S(2)}) collective-permute-start(f32[128,128]{1,0:T(8,128)} %get-tuple-element.70), channel_id=1, source_target_pairs={{0,1},{1,0},{2,3},{3,2},{4,5},{5,4},{6,7},{7,6},{8,9},{9,8},{10,11... | collective-permute-start | bytes 196616 | tf_op jit(solution)/shard_map/ppermute | solution.py:33
  74.0 6.9 %collective-permute-start.17 = (bf16[16,128]{1,0:T(8,128)(2,1)}, bf16[16,128]{1,0:T(8,128)(2,1)S(1)}, u32[]{:S(2)}, u32[]{:S(2)}) collective-permute-start(bf16[16,128]{1,0:T(8,128)(2,1)} %get-tuple-element.60), channel_id=1, source_target_pairs={{0,20},{4,16},{8,28},{12,24},{16,4},{20,0},{24,12},{28,8},{1,21},{... | collective-permute-start | bytes 12296 | tf_op jit(solution)/shard_map/ppermute | solution.py:301
  77.7 6.5 %collective-permute-start.19 = (bf16[16,128]{1,0:T(8,128)(2,1)}, bf16[16,128]{1,0:T(8,128)(2,1)S(1)}, u32[]{:S(2)}, u32[]{:S(2)}) collective-permute-start(bf16[16,128]{1,0:T(8,128)(2,1)} %get-tuple-element.62), channel_id=1, source_target_pairs={{0,28},{4,24},{8,20},{12,16},{16,12},{20,8},{24,4},{28,0},{1,29},{... | collective-permute-start | bytes 12296 | tf_op jit(solution)/shard_map/ppermute | solution.py:301
  84.3 22.1 %collective-permute-start.20 = (bf16[128,128]{1,0:T(8,128)(2,1)S(1)}, bf16[128,128]{1,0:T(8,128)(2,1)S(1)}, u32[]{:S(2)}, u32[]{:S(2)}) collective-permute-start(bf16[128,128]{1,0:T(8,128)(2,1)S(1)} %bring_home.2.own), channel_id=1, source_target_pairs={{0,1},{1,0},{2,3},{3,2},{4,5},{5,4},{6,7},{7,6},{8,9},{9,8},{10,11... | collective-permute-start | bytes 98312 | tf_op jit(solution)/shard_map/ppermute | solution.py:33
  90.8 6.7 %collective-permute-start.29 = (bf16[16,128]{1,0:T(8,128)(2,1)S(1)}, bf16[16,128]{1,0:T(8,128)(2,1)S(1)}, u32[]{:S(2)}, u32[]{:S(2)}) collective-permute-start(bf16[16,128]{1,0:T(8,128)(2,1)S(1)} %get-tuple-element.76), channel_id=1, source_target_pairs={{0,20},{4,16},{8,28},{12,24},{16,4},{20,0},{24,12},{28,8},{1,21},{... | collective-permute-start | bytes 12296 | tf_op jit(solution)/shard_map/ppermute | solution.py:301
  104.4 7.2 %collective-permute-start.34 = (bf16[16,384]{1,0:T(8,128)(2,1)S(1)}, bf16[16,384]{1,0:T(8,128)(2,1)S(1)}, u32[]{:S(2)}, u32[]{:S(2)}) collective-permute-start(bf16[16,384]{1,0:T(8,128)(2,1)S(1)} %get-tuple-element.82), channel_id=1, source_target_pairs={{0,12},{4,8},{8,4},{12,0},{16,28},{20,24},{24,20},{28,16},{1,13},{... | collective-permute-start | bytes 36872 | tf_op jit(solution)/shard_map/ppermute | solution.py:301
  106.4 9.6 %collective-permute-start.35 = (bf16[16,384]{1,0:T(8,128)(2,1)S(1)}, bf16[16,384]{1,0:T(8,128)(2,1)S(1)}, u32[]{:S(2)}, u32[]{:S(2)}) collective-permute-start(bf16[16,384]{1,0:T(8,128)(2,1)S(1)} %get-tuple-element.83), channel_id=1, source_target_pairs={{0,16},{4,20},{8,24},{12,28},{16,0},{20,4},{24,8},{28,12},{1,17},{... | collective-permute-start | bytes 36872 | tf_op jit(solution)/shard_map/ppermute | solution.py:301
  106.6 10.9 %collective-permute-start.36 = (bf16[16,384]{1,0:T(8,128)(2,1)S(1)}, bf16[16,384]{1,0:T(8,128)(2,1)S(1)}, u32[]{:S(2)}, u32[]{:S(2)}) collective-permute-start(bf16[16,384]{1,0:T(8,128)(2,1)S(1)} %get-tuple-element.84), channel_id=1, source_target_pairs={{0,20},{4,16},{8,28},{12,24},{16,4},{20,0},{24,12},{28,8},{1,21},{... | collective-permute-start | bytes 36872 | tf_op jit(solution)/shard_map/ppermute | solution.py:301
  110.3 7.3 %collective-permute-start.37 = (bf16[16,384]{1,0:T(8,128)(2,1)S(1)}, bf16[16,384]{1,0:T(8,128)(2,1)S(1)}, u32[]{:S(2)}, u32[]{:S(2)}) collective-permute-start(bf16[16,384]{1,0:T(8,128)(2,1)S(1)} %get-tuple-element.85), channel_id=1, source_target_pairs={{0,24},{4,28},{8,16},{12,20},{16,8},{20,12},{24,0},{28,4},{1,25},{... | collective-permute-start | bytes 36872 | tf_op jit(solution)/shard_map/ppermute | solution.py:301
  116.1 21.6 %collective-permute-start.22 = (bf16[128,2048]{1,0:T(8,128)(2,1)}, bf16[128,2048]{1,0:T(8,128)(2,1)}, u32[]{:S(2)}, u32[]{:S(2)}) collective-permute-start(bf16[128,2048]{1,0:T(8,128)(2,1)} %spread_out.3), channel_id=1, source_target_pairs={{0,2},{1,3},{2,0},{3,1},{4,6},{5,7},{6,4},{7,5},{8,10},{9,11},{10,... | collective-permute-start | bytes 1572872 | tf_op jit(solution)/shard_map/ppermute | solution.py:33
  118.4 8.9 %collective-permute-start.39 = (f32[128,1]{0,1:T(1,128)S(1)}, f32[128,1]{0,1:T(1,128)S(1)}, u32[]{:S(2)}, u32[]{:S(2)}) collective-permute-start(f32[128,1]{0,1:T(1,128)S(1)} %bitcast.8), channel_id=1, source_target_pairs={{0,1},{1,0},{2,3},{3,2},{4,5},{5,4},{6,7},{7,6},{8,9},{9,8},{10,11... | collective-permute-start | bytes 1544 | tf_op jit(solution)/shard_map/ppermute | solution.py:33
  122.1 15.6 %collective-permute-start.43 = (bf16[128,1024]{1,0:T(8,128)(2,1)S(1)}, bf16[128,1024]{1,0:T(8,128)(2,1)}, u32[]{:S(2)}, u32[]{:S(2)}) collective-permute-start(bf16[128,1024]{1,0:T(8,128)(2,1)S(1)} %spread_grad.5), channel_id=1, source_target_pairs={{0,2},{1,3},{2,0},{3,1},{4,6},{5,7},{6,4},{7,5},{8,10},{9,11},{10,... | collective-permute-start | bytes 786440 | tf_op jit(solution)/shard_map/ppermute | solution.py:33
  126.8 10.9 %collective-permute-start.42 = (bf16[128,1024]{1,0:T(8,128)(2,1)}, bf16[128,1024]{1,0:T(8,128)(2,1)}, u32[]{:S(2)}, u32[]{:S(2)}) collective-permute-start(bf16[128,1024]{1,0:T(8,128)(2,1)} %spread_grad.4), channel_id=1, source_target_pairs={{0,2},{1,3},{2,0},{3,1},{4,6},{5,7},{6,4},{7,5},{8,10},{9,11},{10,... | collective-permute-start | bytes 786440 | tf_op jit(solution)/shard_map/ppermute | solution.py:33
  (43 other events, 199.2 us)

commit v3 on v0

v3 whole, which is shorter than its diff:
```python
import math

import jax
import jax.numpy as jnp
from jax import lax
from jax.experimental import pallas as pl
from jax.experimental.pallas import tpu as pltpu
from jax.sharding import PartitionSpec as P

HEAD_DIM = 128
EPSILON = 1e-05
SCALING = 1.0 / math.sqrt(HEAD_DIM)
CONTRACT_LAST = (((1,), (1,)), ((), ()))
CONTRACT_FIRST = (((0,), (0,)), ((), ()))
VMEM_LIMIT = 24 * 1024 * 1024
VMEM = pl.BlockSpec(memory_space=pltpu.VMEM)
SMEM = pl.BlockSpec(memory_space=pltpu.SMEM)
ANY = pl.BlockSpec(memory_space=pl.ANY)
TILE = 512


def dot(left, right, dims=(((1,), (0,)), ((), ()))):
    return lax.dot_general(left, right, dims, preferred_element_type=jnp.float32)


def call(kernel, name, out_shape, operands, scratch=(), first=SMEM, rest=VMEM):
    single = not isinstance(out_shape, (list, tuple))
    shapes = [out_shape] if single else list(out_shape)
    results = pl.pallas_call(
        kernel,
        out_shape=shapes,
        in_specs=[first] + [rest] * (len(operands) - 1),
        out_specs=[VMEM] * len(shapes),
        scratch_shapes=list(scratch),
        compiler_params=pltpu.CompilerParams(vmem_limit_bytes=VMEM_LIMIT),
        cost_estimate=pl.CostEstimate(flops=1000, bytes_accessed=1000, transcendentals=0),
        name=name,
    )(*operands)
    return results[0] if single else results


def shape(dtype, *sizes):
    return jax.ShapeDtypeStruct(sizes, dtype)


def swap(array, mask, count):
    return lax.ppermute(array, "tensor", [(i, i ^ mask) for i in range(count)])


def block_start(order, slot, width):
    return pl.multiple_of(order[slot] * width, width)


def one_hot(places, rows):
    row = lax.broadcasted_iota(jnp.int32, (rows, places.shape[1]), 0)
    return jnp.where(places == row, 1.0, 0.0).astype(jnp.bfloat16)


def into_slots(send, values):
    chosen = one_hot(send, values.shape[0])
    return dot(chosen, values, CONTRACT_FIRST).astype(jnp.bfloat16)


def prepare_kernel(
    order, w_query, w_key, w_value, w_output, joined, near_joined, near_output, far_output, sems
):
    width = near_joined.shape[0] // 2
    copies = []

    def copy(source, target):
        copies.append(pltpu.make_async_copy(source, target, sems.at[len(copies)]))

    for place, weight in enumerate((w_query, w_key, w_value)):
        columns = pl.ds(place * HEAD_DIM, HEAD_DIM)
        copy(weight, joined.at[:, columns])
        for part, slot in enumerate((1, 3)):
            rows = pl.ds(block_start(order, slot, width), width)
            copy(weight.at[rows, :], near_joined.at[pl.ds(part * width, width), columns])
    for target, slots in ((near_output, (1, 3)), (far_output, (2, 3))):
        for part, slot in enumerate(slots):
            columns = pl.ds(block_start(order, slot, width), width)
            copy(w_output.at[:, columns], target.at[:, pl.ds(part * width, width)])
    for one in copies:
        one.start()
    for one in copies:
        one.wait()


def prepare(order, w_query, w_key, w_value, w_output, width):
    depth, heads = w_query.shape
    low = jnp.bfloat16
    return call(
        prepare_kernel,
        "prepare",
        [
            shape(low, depth, 3 * heads),
            shape(low, 2 * width, 3 * heads),
            shape(low, heads, 2 * width),
            shape(low, heads, 2 * width),
        ],
        (order, w_query, w_key, w_value, w_output),
        scratch=[pltpu.SemaphoreType.DMA((13,))],
        rest=ANY,
    )


def project_rows_kernel(
    order, x0, x1, x2, x3, gain_own, gain_near, weights, send, home, inverse, bucket, total
):
    blocks = (x0, x1, x2, x3)
    width = x0.shape[1]
    squares = 0.0
    for block in blocks:
        wide = block[...].astype(jnp.float32)
        squares = squares + jnp.sum(wide * wide, axis=-1, keepdims=True)
    inverse_rms = lax.rsqrt(squares / (width * len(blocks)) + EPSILON)
    inverse[...] = inverse_rms
    for index, block in enumerate(blocks):
        gain = (gain_own, gain_near)[index % 2][index // 2 : index // 2 + 1, :]
        scaled = block[...].astype(jnp.float32) * inverse_rms
        normed = (scaled * gain.astype(jnp.float32)).astype(jnp.bfloat16)
        part = dot(normed, weights[pl.ds(block_start(order, index, width), width), :])
        total[...] = total[...] + part if index else part
    rounded = total[...].astype(jnp.bfloat16)
    home[...] = rounded
    bucket[...] = into_slots(send[...], rounded)


def project_rows(order, blocks, gains, weights, send):
    rows = blocks[0].shape[0]
    columns = weights.shape[1]
    return call(
        project_rows_kernel,
        "project_rows",
        [
            shape(jnp.bfloat16, rows, columns),
            shape(jnp.float32, rows, 1),
            shape(jnp.bfloat16, send.shape[1], columns),
        ],
        (order, *blocks, *gains, weights, send),
        scratch=[pltpu.VMEM((rows, columns), jnp.float32)],
    )


def grad_part_kernel(slot, half):
    def kernel(order, block, own, near, *rest):
        *before, total, other = rest
        width = block.shape[1]
        here = own[:, pl.ds(block_start(order, slot, width), width)]
        weights = jnp.concatenate([here, near[:, half * width : (half + 1) * width]], axis=0)
        part = dot(block[...], weights, CONTRACT_LAST)
        heads = own.shape[0]
        for place, out in enumerate((total, other)):
            value = part[:, place * heads : (place + 1) * heads]
            out[...] = value + before[place][...] if before else value

    return kernel


def grad_part(order, slot, half, block, w_output, near, before):
    shapes = [shape(jnp.float32, block.shape[0], w_output.shape[0])] * 2
    return call(
        grad_part_kernel(slot, half), "grad_part", shapes, (order, block, w_output, near, *before)
    )


def grad_bucket_kernel(total, other, send, bucket):
    bucket[...] = into_slots(send[...], (total[...] + other[...]).astype(jnp.bfloat16))


def grad_bucket(total, other, send):
    out = shape(jnp.bfloat16, send.shape[1], total.shape[1])
    return call(grad_bucket_kernel, "grad_bucket", out, (total, other, send), first=VMEM)


def balanced(receive, moved):
    chosen = one_hot(receive, moved.shape[0])
    return dot(chosen, moved, CONTRACT_FIRST).astype(jnp.bfloat16)


def thirds(rows):
    return (rows[:, :HEAD_DIM], rows[:, HEAD_DIM : 2 * HEAD_DIM], rows[:, 2 * HEAD_DIM :])


def attend_kernel(moved, receive, segments, softmax, attended, qkv):
    rows = balanced(receive[...], moved[...])
    qkv[...] = rows
    queries, key_rows, value_rows = thirds(rows)
    count = rows.shape[0]
    down = lax.broadcasted_iota(jnp.int32, (count, count), 0)
    across = lax.broadcasted_iota(jnp.int32, (count, count), 1)
    stays = segments[...]
    own_stay = jnp.sum(jnp.where(down == across, stays, 0), axis=1, keepdims=True)
    allowed = (own_stay == stays) & (across <= down)
    scores = jnp.where(allowed, dot(queries, key_rows, CONTRACT_LAST) * SCALING, -1e30)
    raised = jnp.exp(scores - jnp.max(scores, axis=-1, keepdims=True))
    softmax_out = raised / jnp.sum(raised, axis=-1, keepdims=True)
    softmax[...] = softmax_out
    attended[...] = dot(softmax_out.astype(jnp.bfloat16), value_rows).astype(jnp.bfloat16)


def attend(moved, receive, segments):
    rows = receive.shape[1]
    return call(
        attend_kernel,
        "attend",
        [
            shape(jnp.float32, rows, rows),
            shape(jnp.bfloat16, rows, HEAD_DIM),
            shape(jnp.bfloat16, rows, moved.shape[1]),
        ],
        (moved, receive, segments),
        first=VMEM,
    )


def attend_back_kernel(softmax, attended, qkv, moved, receive, back):
    queries, key_rows, value_rows = thirds(qkv[...])
    head_grad = balanced(receive[...], moved[...])
    softmax_out = softmax[...]
    low_weights = softmax_out.astype(jnp.bfloat16)
    grad_value = dot(low_weights, head_grad, CONTRACT_FIRST).astype(jnp.bfloat16)
    grad_probs = dot(head_grad, value_rows, CONTRACT_LAST)
    inner = jnp.sum(softmax_out * grad_probs, axis=-1, keepdims=True)
    grad_scores = (softmax_out * (grad_probs - inner) * SCALING).astype(jnp.bfloat16)
    grad_query = dot(grad_scores, key_rows).astype(jnp.bfloat16)
    grad_key = dot(grad_scores, queries, CONTRACT_FIRST).astype(jnp.bfloat16)
    results = jnp.concatenate([grad_query, grad_key, grad_value, attended[...]], axis=1)
    chosen = one_hot(receive[...], back.shape[0])
    back[...] = dot(chosen, results).astype(jnp.bfloat16)


def attend_back(softmax, attended, qkv, moved, receive):
    out = shape(jnp.bfloat16, moved.shape[0], 4 * HEAD_DIM)
    operands = (softmax, attended, qkv, moved, receive)
    return call(attend_back_kernel, "attend_back", out, operands, first=VMEM)


def bring_home_kernel(moved, send, home, results, row_dot):
    chosen = one_hot(send[...], results.shape[0])
    rows = dot(chosen, moved[...])
    results[...] = rows.astype(jnp.bfloat16)
    product = rows[:, : 3 * HEAD_DIM] * home[...].astype(jnp.float32)
    row_dot[...] = jnp.sum(product, axis=-1, keepdims=True)


def bring_home(moved, send, home):
    rows = home.shape[0]
    shapes = [shape(jnp.bfloat16, rows, 4 * HEAD_DIM), shape(jnp.float32, rows, 1)]
    return call(bring_home_kernel, "bring_home", shapes, (moved, send, home), first=VMEM)


def spread_kernel(slot, half):
    def kernel(order, own, near, weights, near_weights, out):
        width = out.shape[1]
        first = block_start(order, slot, width)
        own_grads = own[:, : 3 * HEAD_DIM]
        near_grads = near[:, : 3 * HEAD_DIM]
        for start in range(0, width, TILE):
            total = dot(own_grads, weights[pl.ds(first + start, TILE), :], CONTRACT_LAST)
            here = near_weights[half * width + start : half * width + start + TILE, :]
            total = total + dot(near_grads, here, CONTRACT_LAST)
            out[:, start : start + TILE] = total.astype(out.dtype)

    return kernel


def spread(order, slot, half, own, near, weights, near_weights, dtype):
    out = shape(dtype, own.shape[0], near_weights.shape[0] // 2)
    operands = (order, own, near, weights, near_weights)
    return call(spread_kernel(slot, half), "spread", out, operands)


def finish_out_kernel(order, inputs, own, near, far, w_own, w_near, w_far, w_last, out):
    width = inputs.shape[1]
    first = block_start(order, 0, width)
    last = slice(3 * HEAD_DIM, None)
    rows = (own[:, last], near[:, last], far[:, :HEAD_DIM], far[:, HEAD_DIM:])
    for start in range(0, width, TILE):
        tile = slice(start, start + TILE)
        total = dot(rows[0], w_own[:, pl.ds(first + start, TILE)])
        for left, weight in zip(rows[1:], (w_near, w_far, w_last)):
            total = total + dot(left, weight[:, tile])
        out[:, tile] = (inputs[:, tile].astype(jnp.float32) + total).astype(jnp.bfloat16)


def finish_grad_kernel(
    inputs, cotangent, gain, inverse, own, got, dot_own, dot_far, out
):
    features = 4 * inputs.shape[1]
    mean_dot = (dot_own[...] + dot_far[...]) / features
    inverse_rms = inverse[...]
    for start in range(0, inputs.shape[1], TILE):
        tile = slice(start, start + TILE)
        grad_normed = own[:, tile] + got[:, tile].astype(jnp.float32)
        grad_hat = grad_normed * gain[:, tile].astype(jnp.float32)
        scaled = inputs[:, tile].astype(jnp.float32) * inverse_rms
        change = inverse_rms * (grad_hat - scaled * mean_dot)
        out[:, tile] = (cotangent[:, tile].astype(jnp.float32) + change).astype(jnp.bfloat16)


def move(bucket):
    return lax.all_to_all(bucket, "dp", split_axis=0, concat_axis=0, tiled=True)


def after(array, *others):
    return lax.optimization_barrier((array, *others))[0]


def on_device(
    inputs,
    cotangent,
    norm_gain,
    w_query,
    w_key,
    w_value,
    w_output,
    send_rows,
    receive_slots,
    owner_segments,
):
    rows, width = inputs.shape
    tensor = lax.axis_size("tensor")
    order = lax.axis_index("tensor").astype(jnp.int32) ^ jnp.arange(4, dtype=jnp.int32)
    receive = receive_slots.reshape(1, rows)
    segments = owner_segments.reshape(1, rows)
    gain = norm_gain.reshape(1, width)

    gain2 = swap(gain, 2, tensor)
    x2 = swap(inputs, 2, tensor)
    x1 = swap(inputs, 1, tensor)
    c2 = swap(after(cotangent, gain2), 2, tensor)
    gain_own = jnp.concatenate([gain, gain2], axis=0)
    gain_near = swap(gain_own, 1, tensor)
    joined, near_joined, near_output, far_output = prepare(
        order, w_query, w_key, w_value, w_output, width
    )
    x3 = swap(x2, 1, tensor)
    near_output = swap(after(near_output, x2), 1, tensor)
    near_joined = swap(after(near_joined, x2), 1, tensor)

    home, inverse_rms, bucket = project_rows(
        order, (inputs, x1, x2, x3), (gain_own, gain_near), joined, send_rows
    )
    far_output = swap(after(far_output, home), 2, tensor)
    softmax, attended, qkv = attend(move(bucket), receive, segments)

    first = grad_part(order, 0, 0, cotangent, w_output, near_output, ())
    own_grad, near_grad = grad_part(order, 2, 1, c2, w_output, near_output, first)
    got_grad = swap(near_grad, 1, tensor)
    bucket = grad_bucket(own_grad, got_grad, send_rows)
    back = attend_back(softmax, attended, qkv, move(bucket), receive)
    own, row_dot = bring_home(move(back), send_rows, home)

    near = swap(own, 1, tensor)
    far_part = spread(order, 2, 1, own, near, joined, near_joined, jnp.bfloat16)
    grad_got = swap(far_part, 2, tensor)
    grad_own = spread(order, 0, 0, own, near, joined, near_joined, jnp.float32)

    last = slice(3 * HEAD_DIM, None)
    far = swap(jnp.concatenate([own[:, last], near[:, last]], axis=1), 2, tensor)
    last_output = swap(far_output[:, width:], 1, tensor)
    layer_out = call(
        finish_out_kernel,
        "finish_out",
        shape(jnp.bfloat16, rows, width),
        (order, inputs, own, near, far, w_output, near_output, far_output, last_output),
    )
    row_dot = row_dot + swap(row_dot, 1, tensor)
    row_dot_far = swap(row_dot, 2, tensor)
    input_grad = call(
        finish_grad_kernel,
        "finish_grad",
        shape(jnp.bfloat16, rows, width),
        (inputs, cotangent, gain, inverse_rms, grad_own, grad_got, row_dot, row_dot_far),
        first=VMEM,
    )
    return (layer_out, input_grad)


def solution(mesh):
    return jax.shard_map(
        on_device,
        mesh=mesh,
        in_specs=(
            P("dp", "tensor"),
            P("dp", "tensor"),
            P("tensor"),
            P(None, "tensor"),
            P(None, "tensor"),
            P(None, "tensor"),
            P("tensor", None),
            P("dp", None),
            P("dp"),
            P("dp"),
        ),
        out_specs=(P("dp", "tensor"), P("dp", "tensor")),
        check_vma=False,
    )
```

time: 201 us -> 127 us (0.63)
  waiting for transfers between devices: 90.5 us -> 49.8 us
  matrix products: 25.2 us -> 0 us
  Pallas kernels: 0 us -> 24.3 us
  blocking collectives: 29.6 us -> 9.74 us
  between operations: 14 us -> 0.85 us
  other arithmetic: 9.27 us -> 0.05 us
  starting transfers between devices: 18.6 us -> 23.8 us
  local copies, waits for them, and re-layouts: 13.4 us -> 17.6 us
    ppermute x0 -> x16, waiting for transfers between devices: none -> 46.3 us  [swap(): return lax.ppermute(array, 'tensor', [(i, i ^ mask) for i in range(count)])]
    reduce_scatter x2 -> x0, waiting for transfers between devices: 45.7 us -> none  [the longest x1 27.6 us: finish(): lax.psum_scatter(grad_part.astype(jnp.bfloat16), 'tensor', scatter_dimens...]
    dot_general x10 -> x0, matrix products: 25.2 us -> none  [the longest x1 5.68 us: finish(): lax.dot_general(grad_key, w_key, CONTRACT_LAST, preferred_element_type=jn...]
    pallas_call x0 -> x12, Pallas kernels: none -> 24.3 us  [call(): pl.pallas_call(kernel, out_shape=shapes, in_specs=[first] + [rest] * (len...]
    all_to_all x3 -> x2, waiting for transfers between devices: 26.1 us -> 3.49 us  [move(): return lax.all_to_all(bucket, 'dp', split_axis=0, concat_axis=0, tiled=True)]
    all_gather x2 -> x0, waiting for transfers between devices: 18.6 us -> none  [the longest x1 18.6 us: gather_normed(): lax.all_gather(cotangent, 'tensor', axis=1, tiled=True)]
    unnamed x14 -> x42, local copies, waits for them, and re-layouts: 0.69 us -> 16.4 us
    ppermute x0 -> x16, starting transfers between devices: none -> 12 us  [swap(): return lax.ppermute(array, 'tensor', [(i, i ^ mask) for i in range(count)])]
  transfers between devices with their start and end apart: 7 -> 18, of which waited for: 5 -> 8; matrix products, arithmetic and copies ran while one was open for 11% -> 1% of each run, Pallas kernels for 0% -> 17%
where the time goes in v3:
time: 127 us; the launch traced here: 126 us
  waiting for transfers between devices  49.8 us (39%)
  Pallas kernels  24.3 us (19%)
  starting transfers between devices  23.8 us (19%)
  local copies, waits for them, and re-layouts  17.6 us (14%)
  blocking collectives  9.74 us (8%)
    ppermute x16, waiting for transfers between devices, swap(): return lax.ppermute(array, 'tensor', [(i, i ^ mask) for i in range(count)])  46.3 us
    pallas_call x12, Pallas kernels, call(): pl.pallas_call(kernel, out_shape=shapes, in_specs=[first] + [rest] * (len...  24.3 us
    unnamed x42, local copies, waits for them, and re-layouts  16.4 us
    ppermute x16, starting transfers between devices, swap(): return lax.ppermute(array, 'tensor', [(i, i ^ mask) for i in range(count)])  12 us
    all_to_all x2, starting transfers between devices, move(): return lax.all_to_all(bucket, 'dp', split_axis=0, concat_axis=0, tiled=True)  11.8 us
    all_to_all x1, blocking collectives, move(): return lax.all_to_all(bucket, 'dp', split_axis=0, concat_axis=0, tiled=True)  9.74 us
    all_to_all x2, waiting for transfers between devices, move(): return lax.all_to_all(bucket, 'dp', split_axis=0, concat_axis=0, tiled=True)  3.49 us
  transfers between devices with their start and end apart: 18, of which 8 were waited for; matrix products, arithmetic and copies ran while one was open for 1% of the time, Pallas kernels for 17%

profile of v3, /device:TPU:0, one launch (start us, length us, event | category | flops | bytes accessed | tf_op | source)
XLA Modules:
  0.0 126.2 jit_solution(4687559404655503244)
XLA Ops:
  0.6 3.0 %collective-permute-start.1 = (bf16[128,2048]{1,0:T(8,128)(2,1)}, bf16[128,2048]{1,0:T(8,128)(2,1)S(1)}, u32[]{:S(2)}, u32[]{:S(2)}) collective-permute-start(bf16[128,2048]{1,0:T(8,128)(2,1)} %inputs.3), channel_id=1, source_target_pairs={{0,2},{1,3},{2,0},{3,1},{4,6},{5,7},{6,4},{7,5},{8,10},{9,11},{10,... | collective-permute-start | bytes 1572872 | tf_op jit(solution)/shard_map/ppermute | solution.py:47
  3.7 1.6 %copy-done.3 = bf16[128,8192]{1,0:T(8,128)(2,1)S(1)} copy-done((bf16[128,8192]{1,0:T(8,128)(2,1)S(1)}, bf16[128,8192]{1,0:T(8,128)(2,1)}, u32[]{:S(2)}) %copy-start.3) | copy-done | bytes 2097176
  5.3 1.6 %copy-done.7 = bf16[8192,128]{1,0:T(8,128)(2,1)S(1)} copy-done((bf16[8192,128]{1,0:T(8,128)(2,1)S(1)}, bf16[8192,128]{1,0:T(8,128)(2,1)}, u32[]{:S(2)}) %copy-start.7) | copy-done | bytes 2097176
  6.8 1.6 %copy-done.8 = bf16[8192,128]{1,0:T(8,128)(2,1)S(1)} copy-done((bf16[8192,128]{1,0:T(8,128)(2,1)S(1)}, bf16[8192,128]{1,0:T(8,128)(2,1)}, u32[]{:S(2)}) %copy-start.8) | copy-done | bytes 2097176
  8.4 1.6 %copy-done.9 = bf16[8192,128]{1,0:T(8,128)(2,1)S(1)} copy-done((bf16[8192,128]{1,0:T(8,128)(2,1)S(1)}, bf16[8192,128]{1,0:T(8,128)(2,1)}, u32[]{:S(2)}) %copy-start.9) | copy-done | bytes 2097176
  10.0 4.8 %prepare.1 = (bf16[8192,384]{1,0:T(8,128)(2,1)S(1)}, bf16[4096,384]{1,0:T(8,128)(2,1)}, bf16[128,4096]{1,0:T(8,128)(2,1)}, bf16[128,4096]{1,0:T(8,128)(2,1)}) custom-call(s32[4]{0:T(128)S(1)} %iota_xor_fusion.order, bf16[8192,128]{1,0:T(8,128)(2,1)S(1)} %copy-done.7, bf16[8192,128]{1,0:T(8,128)(2,1)S(1)} %copy-done.8, bf16[8192,128]{1,0:T(8,128)(2,1)S(1)} %copy-done.9, ...), custom_call_target="tpu_custom_call" | custom-call | flops 1000 | bytes 1000 | tf_op jit(solution)/shard_map/prepare/pallas_call | solution.py:29
  17.7 1.7 %collective-permute-start.3 = (bf16[1,2048]{1,0:T(2,128)(2,1)S(1)}, bf16[1,2048]{1,0:T(2,128)(2,1)S(1)}, u32[]{:S(2)}, u32[]{:S(2)}) collective-permute-start(bf16[1,2048]{1,0:T(2,128)(2,1)S(1)} %reshape.19.gain), channel_id=1, source_target_pairs={{0,2},{1,3},{2,0},{3,1},{4,6},{5,7},{6,4},{7,5},{8,10},{9,11},{10,... | collective-permute-start | bytes 12296 | tf_op jit(solution)/shard_map/ppermute | solution.py:47
  19.4 2.0 %collective-permute-done.3 = bf16[1,2048]{1,0:T(2,128)(2,1)S(1)} collective-permute-done((bf16[1,2048]{1,0:T(2,128)(2,1)S(1)}, bf16[1,2048]{1,0:T(2,128)(2,1)S(1)}, u32[]{:S(2)}, u32[]{:S(2)}) %collective-permute-start.3) | collective-permute-done | bytes 4128 | tf_op jit(solution)/shard_map/ppermute | solution.py:47
  21.6 2.5 %collective-permute-done.4.gain_near = bf16[2,2048]{1,0:T(2,128)(2,1)S(1)} collective-permute-done((bf16[2,2048]{1,0:T(2,128)(2,1)S(1)}, bf16[2,2048]{1,0:T(2,128)(2,1)S(1)}, u32[]{:S(2)}, u32[]{:S(2)}) %collective-permute-start.4) | collective-permute-done | bytes 8224 | tf_op jit(solution)/shard_map/ppermute | solution.py:47
  25.2 3.1 %project_rows.1 = (bf16[128,384]{1,0:T(8,128)(2,1)S(1)}, f32[128,1]{1,0:T(8,128)S(1)}, bf16[128,384]{1,0:T(8,128)(2,1)}) custom-call(s32[4]{0:T(128)S(1)} %iota_xor_fusion.order, bf16[128,2048]{1,0:T(8,128)(2,1)S(1)} %copy-done.5, bf16[128,2048]{1,0:T(8,128)(2,1)S(1)} %collective-permute-done.x1, bf16[128,2048]{1,0:T(8,128)(2,1)S(1)} %copy-done.11, ...), custom_call_target="tpu_custom_call" | custom-call | flops 1000 | bytes 1000 | tf_op jit(solution)/shard_map/project_rows/pallas_call | solution.py:29
  28.2 2.1 %collective-permute-start.10 = (bf16[128,4096]{1,0:T(8,128)(2,1)}, bf16[128,4096]{1,0:T(8,128)(2,1)}, u32[]{:S(2)}, u32[]{:S(2)}) collective-permute-start(bf16[128,4096]{1,0:T(8,128)(2,1)} %get-tuple-element.37), channel_id=1, source_target_pairs={{0,2},{1,3},{2,0},{3,1},{4,6},{5,7},{6,4},{7,5},{8,10},{9,11},{10,... | collective-permute-start | bytes 3145736 | tf_op jit(solution)/shard_map/ppermute | solution.py:47
  30.4 5.9 %all-to-all-start = ((bf16[8,16,384]{2,1,0:T(8,128)(2,1)}), bf16[8,16,384]{2,1,0:T(8,128)(2,1)S(1)}, u32[]{:S(2)}, u32[]{:S(2)}) async-start(bf16[8,16,384]{2,1,0:T(8,128)(2,1)} %bitcast), calls=%async_computation | async-start | bytes 196608 | tf_op jit(solution)/shard_map/all_to_all | solution.py:303
  37.8 27.5 %collective-permute-done.5.block = bf16[128,2048]{1,0:T(8,128)(2,1)} collective-permute-done((bf16[128,2048]{1,0:T(8,128)(2,1)}, bf16[128,2048]{1,0:T(8,128)(2,1)}, u32[]{:S(2)}, u32[]{:S(2)}) %collective-permute-start.5) | collective-permute-done | bytes 524320 | tf_op jit(solution)/shard_map/ppermute | solution.py:47
  69.0 5.9 %all-to-all-start.1 = ((bf16[8,16,128]{2,1,0:T(8,128)(2,1)}), bf16[8,16,128]{2,1,0:T(8,128)(2,1)S(1)}, u32[]{:S(2)}, u32[]{:S(2)}) async-start(bf16[8,16,128]{2,1,0:T(8,128)(2,1)} %bitcast.4), calls=%async_computation.1 | async-start | bytes 65536 | tf_op jit(solution)/shard_map/all_to_all | solution.py:303
  78.1 3.5 %all-to-all-done.1 = bf16[8,16,128]{2,1,0:T(8,128)(2,1)S(1)} async-done(((bf16[8,16,128]{2,1,0:T(8,128)(2,1)}), bf16[8,16,128]{2,1,0:T(8,128)(2,1)S(1)}, u32[]{:S(2)}, u32[]{:S(2)}) %all-to-all-start.1) | async-done | bytes 32800 | tf_op jit(solution)/shard_map/all_to_all | solution.py:303
  84.6 9.7 %all_to_all.33 = bf16[8,16,512]{2,1,0:T(8,128)(2,1)S(1)} all-to-all(bf16[8,16,512]{2,1,0:T(8,128)(2,1)S(1)} %bitcast.9), channel_id=1, replica_groups=mesh['dp'=8,'tensor'=4] {'dp'}, dimensions={0} | all-to-all | bytes 262144 | tf_op jit(solution)/shard_map/all_to_all | solution.py:303
  96.3 2.8 %copy-done.1 = bf16[8192,384]{1,0:T(8,128)(2,1)S(1)} copy-done((bf16[8192,384]{1,0:T(8,128)(2,1)S(1)}, bf16[8192,384]{1,0:T(8,128)(2,1)}, u32[]{:S(2)}) %copy-start.1) | copy-done | bytes 6291480
  99.1 3.0 %spread.3 = bf16[128,2048]{1,0:T(8,128)(2,1)S(1)} custom-call(s32[4]{0:T(128)S(1)} %iota_xor_fusion.order, bf16[128,512]{1,0:T(8,128)(2,1)S(1)} %get-tuple-element.35.own, bf16[128,512]{1,0:T(8,128)(2,1)S(1)} %collective-permute-done.8.near, bf16[8192,384]{1,0:T(8,128)(2,1)S(1)} %copy-done.1, bf16[4096,384]{1,0:T(8,128)(2,1)} %collective-permute-done.12.near_weights), custom_call_target="tpu_custom_call" | custom-call | flops 1000 | bytes 1000 | tf_op jit(solution)/shard_map/spread/pallas_call | solution.py:29
  102.1 1.7 %collective-permute-start.13 = (bf16[128,2048]{1,0:T(8,128)(2,1)S(1)}, bf16[128,2048]{1,0:T(8,128)(2,1)S(1)}, u32[]{:S(2)}, u32[]{:S(2)}) collective-permute-start(bf16[128,2048]{1,0:T(8,128)(2,1)S(1)} %spread.3), channel_id=1, source_target_pairs={{0,2},{1,3},{2,0},{3,1},{4,6},{5,7},{6,4},{7,5},{8,10},{9,11},{10,... | collective-permute-start | bytes 1572872 | tf_op jit(solution)/shard_map/ppermute | solution.py:47
  105.6 1.7 %collective-permute-start.15 = (f32[128,1]{1,0:T(8,128)S(1)}, f32[128,1]{1,0:T(8,128)S(1)}, u32[]{:S(2)}, u32[]{:S(2)}) collective-permute-start(f32[128,1]{1,0:T(8,128)S(1)} %add.3.dot_own), channel_id=1, source_target_pairs={{0,2},{1,3},{2,0},{3,1},{4,6},{5,7},{6,4},{7,5},{8,10},{9,11},{10,... | collective-permute-start | bytes 1544 | tf_op jit(solution)/shard_map/ppermute | solution.py:47
  107.3 10.9 %collective-permute-done.9.far = bf16[128,256]{1,0:T(8,128)(2,1)S(1)} collective-permute-done((bf16[128,256]{1,0:T(8,128)(2,1)S(1)}, bf16[128,256]{1,0:T(8,128)(2,1)S(1)}, u32[]{:S(2)}, u32[]{:S(2)}) %collective-permute-start.9) | collective-permute-done | bytes 65568 | tf_op jit(solution)/shard_map/ppermute | solution.py:47
  118.2 2.8 %finish_out.1 = bf16[128,2048]{1,0:T(8,128)(2,1)} custom-call(s32[4]{0:T(128)S(1)} %iota_xor_fusion.order, bf16[128,2048]{1,0:T(8,128)(2,1)S(1)} %copy-done.6, bf16[128,512]{1,0:T(8,128)(2,1)S(1)} %get-tuple-element.35.own, bf16[128,512]{1,0:T(8,128)(2,1)S(1)} %collective-permute-done.8.near, bf16[128,256]{1,0:T(8,128)(2,1)S(1)} %collective-permute-done.9.far, ...), custom_call_target="tpu_custom_call" | custom-call | flops 1000 | bytes 1000 | tf_op jit(solution)/shard_map/finish_out/pallas_call | solution.py:29
  120.9 3.0 %spread.2.own = f32[128,2048]{1,0:T(8,128)S(1)} custom-call(s32[4]{0:T(128)S(1)} %iota_xor_fusion.order, bf16[128,512]{1,0:T(8,128)(2,1)S(1)} %get-tuple-element.35.own, bf16[128,512]{1,0:T(8,128)(2,1)S(1)} %collective-permute-done.8.near, bf16[8192,384]{1,0:T(8,128)(2,1)S(1)} %copy-done.2, bf16[4096,384]{1,0:T(8,128)(2,1)} %collective-permute-done.12.near_weights), custom_call_target="tpu_custom_call" | custom-call | flops 1000 | bytes 1000 | tf_op jit(solution)/shard_map/spread/pallas_call | solution.py:29
  123.9 2.3 %finish_grad.1 = bf16[128,2048]{1,0:T(8,128)(2,1)} custom-call(bf16[128,2048]{1,0:T(8,128)(2,1)S(1)} %copy-done.6, bf16[128,2048]{1,0:T(8,128)(2,1)} %cotangent.1, bf16[1,2048]{1,0:T(2,128)(2,1)S(1)} %reshape.19.gain, f32[128,1]{1,0:T(8,128)S(1)} %get-tuple-element.38.inverse, f32[128,2048]{1,0:T(8,128)S(1)} %spread.2.own, ...), custom_call_target="tpu_custom_call" | custom-call | flops 1000 | bytes 1000 | tf_op jit(solution)/shard_map/finish_grad/pallas_call | solution.py:29
  (75 shorter events, 19.1 us)
Async XLA Ops:
  0.6 15.2 %collective-permute-start.1 = (bf16[128,2048]{1,0:T(8,128)(2,1)}, bf16[128,2048]{1,0:T(8,128)(2,1)S(1)}, u32[]{:S(2)}, u32[]{:S(2)}) collective-permute-start(bf16[128,2048]{1,0:T(8,128)(2,1)} %inputs.3), channel_id=1, source_target_pairs={{0,2},{1,3},{2,0},{3,1},{4,6},{5,7},{6,4},{7,5},{8,10},{9,11},{10,... | collective-permute-start | bytes 1572872 | tf_op jit(solution)/shard_map/ppermute | solution.py:47
  10.0 7.7 %copy-start.20 = (bf16[2048]{0:T(1024)(128)(2,1)S(1)}, bf16[2048]{0:T(1024)(128)(2,1)}, u32[]{:S(2)}) copy-start(bf16[2048]{0:T(1024)(128)(2,1)} %param.12) | copy-start | bytes 12292
  10.0 14.1 %copy-start.16 = (s32[1,128]{1,0:T(1,128)S(1)}, s32[1,128]{1,0:T(1,128)}, u32[]{:S(2)}) copy-start(s32[1,128]{1,0:T(1,128)} %send.5) | copy-start | bytes 1540
  14.9 13.4 %copy-start = (bf16[8192,384]{1,0:T(8,128)(2,1)}, bf16[8192,384]{1,0:T(8,128)(2,1)S(1)}, u32[]{:S(2)}) copy-start(bf16[8192,384]{1,0:T(8,128)(2,1)S(1)} %get-tuple-element.22.weights) | copy-start | bytes 18874372
  15.8 80.5 %collective-permute-start.12 = (bf16[4096,384]{1,0:T(8,128)(2,1)}, bf16[4096,384]{1,0:T(8,128)(2,1)}, u32[]{:S(2)}, u32[]{:S(2)}) collective-permute-start(bf16[4096,384]{1,0:T(8,128)(2,1)} %get-tuple-element.40), channel_id=1, source_target_pairs={{0,1},{1,0},{2,3},{3,2},{4,5},{5,4},{6,7},{7,6},{8,9},{9,8},{10,11... | collective-permute-start | bytes 9437192 | tf_op jit(solution)/shard_map/ppermute | solution.py:47
  15.8 8.3 %collective-permute-start = (bf16[128,2048]{1,0:T(8,128)(2,1)S(1)}, bf16[128,2048]{1,0:T(8,128)(2,1)S(1)}, u32[]{:S(2)}, u32[]{:S(2)}) collective-permute-start(bf16[128,2048]{1,0:T(8,128)(2,1)S(1)} %copy-done.5), channel_id=1, source_target_pairs={{0,1},{1,0},{2,3},{3,2},{4,5},{5,4},{6,7},{7,6},{8,9},{9,8},{10,11... | collective-permute-start | bytes 1572872 | tf_op jit(solution)/shard_map/ppermute | solution.py:47
  16.3 7.8 %collective-permute-start.2 = (bf16[128,2048]{1,0:T(8,128)(2,1)S(1)}, bf16[128,2048]{1,0:T(8,128)(2,1)S(1)}, u32[]{:S(2)}, u32[]{:S(2)}) collective-permute-start(bf16[128,2048]{1,0:T(8,128)(2,1)S(1)} %collective-permute-done.1.x2), channel_id=1, source_target_pairs={{0,1},{1,0},{2,3},{3,2},{4,5},{5,4},{6,7},{7,6},{8,9},{9,8},{10,11... | collective-permute-start | bytes 1572872 | tf_op jit(solution)/shard_map/ppermute | solution.py:47
  17.7 18.6 %collective-permute-start.6 = (bf16[128,4096]{1,0:T(8,128)(2,1)}, bf16[128,4096]{1,0:T(8,128)(2,1)S(1)}, u32[]{:S(2)}, u32[]{:S(2)}) collective-permute-start(bf16[128,4096]{1,0:T(8,128)(2,1)} %get-tuple-element.29), channel_id=1, source_target_pairs={{0,1},{1,0},{2,3},{3,2},{4,5},{5,4},{6,7},{7,6},{8,9},{9,8},{10,11... | collective-permute-start | bytes 3145736 | tf_op jit(solution)/shard_map/ppermute | solution.py:47
  17.7 3.7 %collective-permute-start.3 = (bf16[1,2048]{1,0:T(2,128)(2,1)S(1)}, bf16[1,2048]{1,0:T(2,128)(2,1)S(1)}, u32[]{:S(2)}, u32[]{:S(2)}) collective-permute-start(bf16[1,2048]{1,0:T(2,128)(2,1)S(1)} %reshape.19.gain), channel_id=1, source_target_pairs={{0,2},{1,3},{2,0},{3,1},{4,6},{5,7},{6,4},{7,5},{8,10},{9,11},{10,... | collective-permute-start | bytes 12296 | tf_op jit(solution)/shard_map/ppermute | solution.py:47
  21.5 2.6 %collective-permute-start.4 = (bf16[2,2048]{1,0:T(2,128)(2,1)S(1)}, bf16[2,2048]{1,0:T(2,128)(2,1)S(1)}, u32[]{:S(2)}, u32[]{:S(2)}) collective-permute-start(bf16[2,2048]{1,0:T(2,128)(2,1)S(1)} %pad_maximum_fusion.1.gain_own), channel_id=1, source_target_pairs={{0,1},{1,0},{2,3},{3,2},{4,5},{5,4},{6,7},{7,6},{8,9},{9,8},{10,11... | collective-permute-start | bytes 24584 | tf_op jit(solution)/shard_map/ppermute | solution.py:47
  25.2 11.1 %copy-start.4 = (bf16[128,8192]{1,0:T(8,128)(2,1)S(1)}, bf16[128,8192]{1,0:T(8,128)(2,1)}, u32[]{:S(2)}) copy-start(bf16[128,8192]{1,0:T(8,128)(2,1)} %w_own.1) | copy-start | bytes 6291460
  28.2 66.4 %collective-permute-start.10 = (bf16[128,4096]{1,0:T(8,128)(2,1)}, bf16[128,4096]{1,0:T(8,128)(2,1)}, u32[]{:S(2)}, u32[]{:S(2)}) collective-permute-start(bf16[128,4096]{1,0:T(8,128)(2,1)} %get-tuple-element.37), channel_id=1, source_target_pairs={{0,2},{1,3},{2,0},{3,1},{4,6},{5,7},{6,4},{7,5},{8,10},{9,11},{10,... | collective-permute-start | bytes 3145736 | tf_op jit(solution)/shard_map/ppermute | solution.py:47
  30.3 35.0 %collective-permute-start.5 = (bf16[128,2048]{1,0:T(8,128)(2,1)}, bf16[128,2048]{1,0:T(8,128)(2,1)}, u32[]{:S(2)}, u32[]{:S(2)}) collective-permute-start(bf16[128,2048]{1,0:T(8,128)(2,1)} %cotangent.1), channel_id=1, source_target_pairs={{0,2},{1,3},{2,0},{3,1},{4,6},{5,7},{6,4},{7,5},{8,10},{9,11},{10,... | collective-permute-start | bytes 1572872 | tf_op jit(solution)/shard_map/ppermute | solution.py:47
  30.4 38.6 %all-to-all-start = ((bf16[8,16,384]{2,1,0:T(8,128)(2,1)}), bf16[8,16,384]{2,1,0:T(8,128)(2,1)S(1)}, u32[]{:S(2)}, u32[]{:S(2)}) async-start(bf16[8,16,384]{2,1,0:T(8,128)(2,1)} %bitcast), calls=%async_computation | async-start | bytes 196608 | tf_op jit(solution)/shard_map/all_to_all | solution.py:303
  66.9 1.3 %collective-permute-start.7 = (f32[128,128]{1,0:T(8,128)S(1)}, f32[128,128]{1,0:T(8,128)S(1)}, u32[]{:S(2)}, u32[]{:S(2)}) collective-permute-start(f32[128,128]{1,0:T(8,128)S(1)} %get-tuple-element.33), channel_id=1, source_target_pairs={{0,1},{1,0},{2,3},{3,2},{4,5},{5,4},{6,7},{7,6},{8,9},{9,8},{10,11... | collective-permute-start | bytes 196616 | tf_op jit(solution)/shard_map/ppermute | solution.py:47
  69.0 12.6 %all-to-all-start.1 = ((bf16[8,16,128]{2,1,0:T(8,128)(2,1)}), bf16[8,16,128]{2,1,0:T(8,128)(2,1)S(1)}, u32[]{:S(2)}, u32[]{:S(2)}) async-start(bf16[8,16,128]{2,1,0:T(8,128)(2,1)} %bitcast.4), calls=%async_computation.1 | async-start | bytes 65536 | tf_op jit(solution)/shard_map/all_to_all | solution.py:303
  94.6 1.8 %collective-permute-start.8 = (bf16[128,512]{1,0:T(8,128)(2,1)S(1)}, bf16[128,512]{1,0:T(8,128)(2,1)S(1)}, u32[]{:S(2)}, u32[]{:S(2)}) collective-permute-start(bf16[128,512]{1,0:T(8,128)(2,1)S(1)} %get-tuple-element.35.own), channel_id=1, source_target_pairs={{0,1},{1,0},{2,3},{3,2},{4,5},{5,4},{6,7},{7,6},{8,9},{9,8},{10,11... | collective-permute-start | bytes 393224 | tf_op jit(solution)/shard_map/ppermute | solution.py:47
  94.6 23.5 %copy-start.6 = (bf16[128,2048]{1,0:T(8,128)(2,1)S(1)}, bf16[128,2048]{1,0:T(8,128)(2,1)}, u32[]{:S(2)}) copy-start(bf16[128,2048]{1,0:T(8,128)(2,1)} %inputs.3) | copy-start | bytes 1572868
  95.8 22.4 %collective-permute-start.11 = (bf16[128,2048]{1,0:T(8,128)(2,1)S(1)}, bf16[128,2048]{1,0:T(8,128)(2,1)S(1)}, u32[]{:S(2)}, u32[]{:S(2)}) collective-permute-start(bf16[128,2048]{1,0:T(8,128)(2,1)S(1)} %slice.13), channel_id=1, source_target_pairs={{0,1},{1,0},{2,3},{3,2},{4,5},{5,4},{6,7},{7,6},{8,9},{9,8},{10,11... | collective-permute-start | bytes 1572872 | tf_op jit(solution)/shard_map/ppermute | solution.py:47
  102.1 21.8 %collective-permute-start.13 = (bf16[128,2048]{1,0:T(8,128)(2,1)S(1)}, bf16[128,2048]{1,0:T(8,128)(2,1)S(1)}, u32[]{:S(2)}, u32[]{:S(2)}) collective-permute-start(bf16[128,2048]{1,0:T(8,128)(2,1)S(1)} %spread.3), channel_id=1, source_target_pairs={{0,2},{1,3},{2,0},{3,1},{4,6},{5,7},{6,4},{7,5},{8,10},{9,11},{10,... | collective-permute-start | bytes 1572872 | tf_op jit(solution)/shard_map/ppermute | solution.py:47
  103.9 14.3 %collective-permute-start.9 = (bf16[128,256]{1,0:T(8,128)(2,1)S(1)}, bf16[128,256]{1,0:T(8,128)(2,1)S(1)}, u32[]{:S(2)}, u32[]{:S(2)}) collective-permute-start(bf16[128,256]{1,0:T(8,128)(2,1)S(1)} %pad_maximum_fusion), channel_id=1, source_target_pairs={{0,2},{1,3},{2,0},{3,1},{4,6},{5,7},{6,4},{7,5},{8,10},{9,11},{10,... | collective-permute-start | bytes 196616 | tf_op jit(solution)/shard_map/ppermute | solution.py:47
  104.3 1.3 collective-permute-start.14
  105.6 15.3 %copy-start.2 = (bf16[8192,384]{1,0:T(8,128)(2,1)S(1)}, bf16[8192,384]{1,0:T(8,128)(2,1)}, u32[]{:S(2)}) copy-start(bf16[8192,384]{1,0:T(8,128)(2,1)} %copy-done) | copy-start | bytes 18874372
  105.6 18.3 %collective-permute-start.15 = (f32[128,1]{1,0:T(8,128)S(1)}, f32[128,1]{1,0:T(8,128)S(1)}, u32[]{:S(2)}, u32[]{:S(2)}) collective-permute-start(f32[128,1]{1,0:T(8,128)S(1)} %add.3.dot_own), channel_id=1, source_target_pairs={{0,2},{1,3},{2,0},{3,1},{4,6},{5,7},{6,4},{7,5},{8,10},{9,11},{10,... | collective-permute-start | bytes 1544 | tf_op jit(solution)/shard_map/ppermute | solution.py:47
  (15 other events, 22.2 us)

commit v4 on v3

v4 whole, which is shorter than its diff:
```python
import math

import jax
import jax.numpy as jnp
from jax import lax
from jax.experimental import pallas as pl
from jax.experimental.pallas import tpu as pltpu
from jax.sharding import PartitionSpec as P

HEAD_DIM = 128
EPSILON = 1e-05
SCALING = 1.0 / math.sqrt(HEAD_DIM)
CONTRACT_LAST = (((1,), (1,)), ((), ()))
CONTRACT_FIRST = (((0,), (0,)), ((), ()))
VMEM_LIMIT = 12 * 1024 * 1024
VMEM = pl.BlockSpec(memory_space=pltpu.VMEM)
SMEM = pl.BlockSpec(memory_space=pltpu.SMEM)
TILE = 512


def dot(left, right, dims=(((1,), (0,)), ((), ()))):
    return lax.dot_general(left, right, dims, preferred_element_type=jnp.float32)


def call(kernel, name, out_shape, operands, scratch=(), first=SMEM, rest=VMEM):
    single = not isinstance(out_shape, (list, tuple))
    shapes = [out_shape] if single else list(out_shape)
    results = pl.pallas_call(
        kernel,
        out_shape=shapes,
        in_specs=[first] + [rest] * (len(operands) - 1),
        out_specs=[VMEM] * len(shapes),
        scratch_shapes=list(scratch),
        compiler_params=pltpu.CompilerParams(vmem_limit_bytes=VMEM_LIMIT),
        cost_estimate=pl.CostEstimate(flops=1000, bytes_accessed=1000, transcendentals=0),
        name=name,
    )(*operands)
    return results[0] if single else results


def shape(dtype, *sizes):
    return jax.ShapeDtypeStruct(sizes, dtype)


def swap(array, mask, count):
    return lax.ppermute(array, "tensor", [(i, i ^ mask) for i in range(count)])


def block_start(order, slot, width):
    return pl.multiple_of(order[slot] * width, width)


def one_hot(places, rows):
    row = lax.broadcasted_iota(jnp.int32, (rows, places.shape[1]), 0)
    return jnp.where(places == row, 1.0, 0.0).astype(jnp.bfloat16)


def prepare_kernel(
    order,
    w_query,
    w_key,
    w_value,
    w_output,
    send,
    receive,
    segments,
    own_turned,
    near_turned,
    output_turned,
    near_output,
    far_output,
    send_out,
    receive_out,
    segments_out,
):
    width = near_output.shape[1]
    for target, slots in ((near_output, (1,)), (far_output, (2, 3))):
        for part, slot in enumerate(slots):
            columns = pl.ds(block_start(order, slot, width), width)
            target[:, part * width : (part + 1) * width] = w_output[:, columns]
    for start in range(0, w_output.shape[1], TILE):
        output_turned[start : start + TILE, :] = w_output[:, start : start + TILE].T
    for source, target in ((send, send_out), (receive, receive_out), (segments, segments_out)):
        target[...] = source[...]
    for out, slots in ((own_turned, (0, 2)), (near_turned, (1, 3))):
        for part, slot in enumerate(slots):
            first = block_start(order, slot, width)
            for start in range(0, width, TILE):
                columns = slice(part * width + start, part * width + start + TILE)
                for place, weight in enumerate((w_query, w_key, w_value)):
                    rows = slice(place * HEAD_DIM, (place + 1) * HEAD_DIM)
                    out[rows, columns] = weight[pl.ds(first + start, TILE), :].T


def prepare(order, w_query, w_key, w_value, w_output, send, receive, segments, width):
    heads = w_query.shape[1]
    low = jnp.bfloat16
    return call(
        prepare_kernel,
        "prepare",
        [
            shape(low, 3 * heads, 2 * width),
            shape(low, 3 * heads, 2 * width),
            shape(low, w_output.shape[1], heads),
            shape(low, heads, width),
            shape(low, heads, 2 * width),
            shape(jnp.int32, *send.shape),
            shape(jnp.int32, *receive.shape),
            shape(jnp.int32, *segments.shape),
        ],
        (order, w_query, w_key, w_value, w_output, send, receive, segments),
    )


def sum_squares(block):
    wide = block[...].astype(jnp.float32)
    return jnp.sum(wide * wide, axis=-1, keepdims=True)


def begin_kernel(order, x0, x1, x2, c0, c1, c2, output_turned, squares, part):
    width = x0.shape[1]
    squares[...] = sum_squares(x0) + sum_squares(x1) + sum_squares(x2)
    total = 0.0
    for index, block in enumerate((c0, c1, c2)):
        here = pl.ds(block_start(order, index, width), width)
        total = total + dot(block[...], output_turned[here, :])
    part[...] = total


def begin(order, blocks, output_turned):
    rows = blocks[0].shape[0]
    shapes = [shape(jnp.float32, rows, 1), shape(jnp.float32, rows, HEAD_DIM)]
    return call(begin_kernel, "begin", shapes, (order, *blocks, output_turned))


def project_kernel(
    order,
    x0,
    x1,
    x2,
    x3,
    c3,
    gain_own,
    gain_near,
    w_query,
    w_key,
    w_value,
    output_turned,
    squares,
    part,
    send,
    home,
    inverse,
    bucket,
    total,
):
    blocks = (x0, x1, x2, x3)
    width = x0.shape[1]
    mean = (squares[...] + sum_squares(x3)) / (width * len(blocks))
    inverse_rms = lax.rsqrt(mean + EPSILON)
    inverse[...] = inverse_rms
    here = pl.ds(block_start(order, 3, width), width)
    head_grad = (part[...] + dot(c3[...], output_turned[here, :])).astype(jnp.bfloat16)
    for index, block in enumerate(blocks):
        gain = (gain_own, gain_near)[index % 2][index // 2 : index // 2 + 1, :]
        scaled = block[...].astype(jnp.float32) * inverse_rms
        normed = (scaled * gain.astype(jnp.float32)).astype(jnp.bfloat16)
        here = pl.ds(block_start(order, index, width), width)
        weights = jnp.concatenate([w_query[here, :], w_key[here, :], w_value[here, :]], axis=1)
        product = dot(normed, weights)
        total[...] = total[...] + product if index else product
    rounded = total[...].astype(jnp.bfloat16)
    home[...] = rounded
    chosen = one_hot(send[...], rounded.shape[0])
    split = rounded.shape[1]
    bucket[:, :split] = dot(chosen, rounded, CONTRACT_FIRST).astype(jnp.bfloat16)
    bucket[:, split:] = dot(chosen, head_grad, CONTRACT_FIRST).astype(jnp.bfloat16)


def project(order, blocks, gains, weights, squares, part, send):
    rows = blocks[0].shape[0]
    columns = 3 * HEAD_DIM
    return call(
        project_kernel,
        "project",
        [
            shape(jnp.bfloat16, rows, columns),
            shape(jnp.float32, rows, 1),
            shape(jnp.bfloat16, send.shape[1], columns + HEAD_DIM),
        ],
        (order, *blocks, *gains, *weights, squares, part, send),
        scratch=[pltpu.VMEM((rows, columns), jnp.float32)],
    )


def attend_kernel(moved, receive, segments, back):
    place = one_hot(receive[...], moved.shape[0])
    rows = dot(place, moved[...], CONTRACT_FIRST).astype(jnp.bfloat16)
    queries, key_rows, value_rows, head_grad = (
        rows[:, index * HEAD_DIM : (index + 1) * HEAD_DIM] for index in range(4)
    )
    count = rows.shape[0]
    down = lax.broadcasted_iota(jnp.int32, (count, count), 0)
    across = lax.broadcasted_iota(jnp.int32, (count, count), 1)
    stays = segments[...]
    own_stay = jnp.sum(jnp.where(down == across, stays, 0), axis=1, keepdims=True)
    allowed = (own_stay == stays) & (across <= down)
    scores = jnp.where(allowed, dot(queries, key_rows, CONTRACT_LAST) * SCALING, -1e30)
    raised = jnp.exp(scores - jnp.max(scores, axis=-1, keepdims=True))
    softmax_out = raised / jnp.sum(raised, axis=-1, keepdims=True)
    low_weights = softmax_out.astype(jnp.bfloat16)
    attended = dot(low_weights, value_rows).astype(jnp.bfloat16)
    grad_value = dot(low_weights, head_grad, CONTRACT_FIRST).astype(jnp.bfloat16)
    grad_probs = dot(head_grad, value_rows, CONTRACT_LAST)
    inner = jnp.sum(softmax_out * grad_probs, axis=-1, keepdims=True)
    grad_scores = (softmax_out * (grad_probs - inner) * SCALING).astype(jnp.bfloat16)
    grad_query = dot(grad_scores, key_rows).astype(jnp.bfloat16)
    grad_key = dot(grad_scores, queries, CONTRACT_FIRST).astype(jnp.bfloat16)
    results = jnp.concatenate([grad_query, grad_key, grad_value, attended], axis=1)
    back[...] = dot(place, results).astype(jnp.bfloat16)


def attend(moved, receive, segments):
    out = shape(jnp.bfloat16, *moved.shape)
    return call(attend_kernel, "attend", out, (moved, receive, segments), first=VMEM)


def write_parts(value, out):
    out[...] = jnp.zeros_like(out)
    for place in range(3):
        low = value.astype(jnp.bfloat16)
        out[:, place : place + 1] = low
        value = value - low.astype(jnp.float32)


def read_parts(parts):
    return sum(parts[:, place : place + 1].astype(jnp.float32) for place in (2, 1, 0))


def bring_home_kernel(moved, send, home, results):
    chosen = one_hot(send[...], results.shape[0])
    rows = dot(chosen, moved[...])
    results[:, : 4 * HEAD_DIM] = rows.astype(jnp.bfloat16)
    product = rows[:, : 3 * HEAD_DIM] * home[...].astype(jnp.float32)
    row_dot = jnp.sum(product, axis=-1, keepdims=True)
    write_parts(row_dot, results.at[:, 4 * HEAD_DIM :])


def bring_home(moved, send, home):
    out = shape(jnp.bfloat16, home.shape[0], 5 * HEAD_DIM)
    return call(bring_home_kernel, "bring_home", out, (moved, send, home), first=VMEM)


def spread_into(own, near, weights, near_weights, first, out, place):
    own_grads = own[:, : 3 * HEAD_DIM]
    near_grads = near[:, : 3 * HEAD_DIM]
    for start in range(0, out.shape[1] - place, TILE):
        columns = slice(first + start, first + start + TILE)
        total = dot(own_grads, weights[:, columns]) + dot(near_grads, near_weights[:, columns])
        out[:, place + start : place + start + TILE] = total.astype(out.dtype)


def spread_far_kernel(own, near, weights, near_weights, out):
    width = weights.shape[1] // 2
    write_parts(
        read_parts(own[:, 4 * HEAD_DIM :]) + read_parts(near[:, 4 * HEAD_DIM :]),
        out.at[:, :HEAD_DIM],
    )
    attended = slice(3 * HEAD_DIM, 4 * HEAD_DIM)
    out[:, HEAD_DIM : 2 * HEAD_DIM] = own[:, attended]
    out[:, 2 * HEAD_DIM : 3 * HEAD_DIM] = near[:, attended]
    spread_into(own, near, weights, near_weights, width, out, 3 * HEAD_DIM)


def spread_rest_kernel(own, near, weights, near_weights, out):
    width = weights.shape[1] // 2
    spread_into(own, near, weights, near_weights, width + width // 2, out, 0)


def spread_own_kernel(own, near, weights, near_weights, out):
    spread_into(own, near, weights, near_weights, 0, out, 0)


def finish_out_kernel(order, inputs, own, near, far, w_own, w_near, w_far, w_last, out):
    width = inputs.shape[1]
    first = block_start(order, 0, width)
    attended = slice(3 * HEAD_DIM, 4 * HEAD_DIM)
    rows = (
        own[:, attended],
        near[:, attended],
        far[:, HEAD_DIM : 2 * HEAD_DIM],
        far[:, 2 * HEAD_DIM : 3 * HEAD_DIM],
    )
    for start in range(0, width, TILE):
        tile = slice(start, start + TILE)
        total = dot(rows[0], w_own[:, pl.ds(first + start, TILE)])
        for left, weight in zip(rows[1:], (w_near, w_far, w_last)):
            total = total + dot(left, weight[:, tile])
        out[:, tile] = (inputs[:, tile].astype(jnp.float32) + total).astype(jnp.bfloat16)


def finish_grad_kernel(inputs, cotangent, gain, inverse, own, near, grad_own, far, rest, out):
    width = inputs.shape[1]
    row_dot = read_parts(own[:, 4 * HEAD_DIM :]) + read_parts(near[:, 4 * HEAD_DIM :])
    mean_dot = (row_dot + read_parts(far[:, :HEAD_DIM])) / (4 * width)
    inverse_rms = inverse[...]
    for start in range(0, width, TILE):
        tile = slice(start, start + TILE)
        if start < width // 2:
            got = far[:, 3 * HEAD_DIM + start : 3 * HEAD_DIM + start + TILE]
        else:
            got = rest[:, start - width // 2 : start - width // 2 + TILE]
        grad_normed = grad_own[:, tile] + got.astype(jnp.float32)
        grad_hat = grad_normed * gain[:, tile].astype(jnp.float32)
        scaled = inputs[:, tile].astype(jnp.float32) * inverse_rms
        change = inverse_rms * (grad_hat - scaled * mean_dot)
        out[:, tile] = (cotangent[:, tile].astype(jnp.float32) + change).astype(jnp.bfloat16)


def move(bucket):
    return lax.all_to_all(bucket, "dp", split_axis=0, concat_axis=0, tiled=True)


def after(array, *others):
    return lax.optimization_barrier((array, *others))[0]


def on_device(
    inputs,
    cotangent,
    norm_gain,
    w_query,
    w_key,
    w_value,
    w_output,
    send_rows,
    receive_slots,
    owner_segments,
):
    rows, width = inputs.shape
    tensor = lax.axis_size("tensor")
    low = jnp.bfloat16
    order = lax.axis_index("tensor").astype(jnp.int32) ^ jnp.arange(4, dtype=jnp.int32)
    gain = norm_gain.reshape(1, width)

    x2 = swap(inputs, 2, tensor)
    c2 = swap(cotangent, 2, tensor)
    gain2 = swap(gain, 2, tensor)
    x1 = swap(inputs, 1, tensor)
    c1 = swap(cotangent, 1, tensor)
    weights = (w_query, w_key, w_value)
    own_turned, near_turned, output_turned, near_output, far_output, send, receive, segments = (
        prepare(
            order,
            *weights,
            w_output,
            send_rows,
            receive_slots.reshape(1, rows),
            owner_segments.reshape(1, rows),
            width,
        )
    )
    x2, c2, gain2, segments = lax.optimization_barrier((x2, c2, gain2, segments))
    x3 = swap(x2, 1, tensor)
    c3 = swap(c2, 1, tensor)
    gain_own = jnp.concatenate([gain, gain2], axis=0)
    gain_near = swap(gain_own, 1, tensor)

    squares, part = begin(order, (inputs, x1, x2, cotangent, c1, c2), output_turned)
    home, inverse_rms, bucket = project(
        order,
        (inputs, x1, x2, x3, c3),
        (gain_own, gain_near),
        (*weights, output_turned),
        squares,
        part,
        send,
    )
    near_output = swap(after(near_output, home), 1, tensor)
    near_turned = swap(after(near_turned, home), 1, tensor)
    far_output = swap(after(far_output, home), 2, tensor)
    last_output = swap(far_output[:, width:], 1, tensor)
    own = bring_home(move(attend(move(bucket), receive, segments)), send, home)

    near = swap(own, 1, tensor)
    sides = (own, near, own_turned, near_turned)
    half = width // 2
    far = call(
        spread_far_kernel,
        "spread_far",
        shape(low, rows, 3 * HEAD_DIM + half),
        sides,
        first=VMEM,
    )
    far = swap(far, 2, tensor)
    rest = call(spread_rest_kernel, "spread_rest", shape(low, rows, half), sides, first=VMEM)
    rest = swap(rest, 2, tensor)
    grad_own = call(
        spread_own_kernel, "spread_own", shape(jnp.float32, rows, width), sides, first=VMEM
    )
    layer_out = call(
        finish_out_kernel,
        "finish_out",
        shape(low, rows, width),
        (order, inputs, own, near, far, w_output, near_output, far_output, last_output),
    )
    input_grad = call(
        finish_grad_kernel,
        "finish_grad",
        shape(low, rows, width),
        (inputs, cotangent, gain, inverse_rms, own, near, grad_own, far, rest),
        first=VMEM,
    )
    return (layer_out, input_grad)


def solution(mesh):
    return jax.shard_map(
        on_device,
        mesh=mesh,
        in_specs=(
            P("dp", "tensor"),
            P("dp", "tensor"),
            P("tensor"),
            P(None, "tensor"),
            P(None, "tensor"),
            P(None, "tensor"),
            P("tensor", None),
            P("dp", None),
            P("dp"),
            P("dp"),
        ),
        out_specs=(P("dp", "tensor"), P("dp", "tensor")),
        check_vma=False,
    )
```

time: 127 us -> 83.5 us (0.66)
  waiting for transfers between devices: 49.8 us -> 20.4 us
  starting transfers between devices: 23.8 us -> 14.7 us
  local copies, waits for them, and re-layouts: 17.6 us -> 10.5 us
  blocking collectives: 9.74 us -> 12.9 us
    ppermute x16 -> x15, waiting for transfers between devices: 46.3 us -> 13.2 us  [swap(): return lax.ppermute(array, 'tensor', [(i, i ^ mask) for i in range(count)])]
    all_to_all x2 -> x1, starting transfers between devices: 11.8 us -> 3.37 us  [move(): return lax.all_to_all(bucket, 'dp', split_axis=0, concat_axis=0, tiled=True)]
    unnamed x42 -> x32, local copies, waits for them, and re-layouts: 16.4 us -> 8.72 us
    all_to_all x2 -> x1, waiting for transfers between devices: 3.49 us -> 7.2 us  [move(): return lax.all_to_all(bucket, 'dp', split_axis=0, concat_axis=0, tiled=True)]
    all_to_all x1, blocking collectives: 9.74 us -> 12.9 us  [move(): return lax.all_to_all(bucket, 'dp', split_axis=0, concat_axis=0, tiled=True)]
    pallas_call x12 -> x10, Pallas kernels: 24.3 us -> 23.5 us  [call(): pl.pallas_call(kernel, out_shape=shapes, in_specs=[first] + [rest] * (len...]
    ppermute x16 -> x15, starting transfers between devices: 12 us -> 11.3 us  [swap(): return lax.ppermute(array, 'tensor', [(i, i ^ mask) for i in range(count)])]
  transfers between devices with their start and end apart: 18 -> 16, of which waited for: 8 -> 4; matrix products, arithmetic and copies ran while one was open for 1% -> 2% of each run, Pallas kernels for 17% -> 23%
where the time goes in v4:
time: 83.5 us; the launch traced here: 82.9 us
  Pallas kernels  23.5 us (28%)
  waiting for transfers between devices  20.4 us (24%)
  starting transfers between devices  14.7 us (18%)
  blocking collectives  12.9 us (15%)
  local copies, waits for them, and re-layouts  10.5 us (13%)
  between operations  0.84 us (1%)
    pallas_call x10, Pallas kernels, call(): pl.pallas_call(kernel, out_shape=shapes, in_specs=[first] + [rest] * (len...  23.5 us
    ppermute x15, waiting for transfers between devices, swap(): return lax.ppermute(array, 'tensor', [(i, i ^ mask) for i in range(count)])  13.2 us
    all_to_all x1, blocking collectives, move(): return lax.all_to_all(bucket, 'dp', split_axis=0, concat_axis=0, tiled=True)  12.9 us
    ppermute x15, starting transfers between devices, swap(): return lax.ppermute(array, 'tensor', [(i, i ^ mask) for i in range(count)])  11.3 us
    unnamed x32, local copies, waits for them, and re-layouts  8.72 us
    all_to_all x1, waiting for transfers between devices, move(): return lax.all_to_all(bucket, 'dp', split_axis=0, concat_axis=0, tiled=True)  7.2 us
    all_to_all x1, starting transfers between devices, move(): return lax.all_to_all(bucket, 'dp', split_axis=0, concat_axis=0, tiled=True)  3.37 us
  transfers between devices with their start and end apart: 16, of which 4 were waited for; matrix products, arithmetic and copies ran while one was open for 2% of the time, Pallas kernels for 23%

profile of v4, /device:TPU:0, one launch (start us, length us, event | category | flops | bytes accessed | tf_op | source)
XLA Modules:
  0.0 82.9 jit_solution(17730457711506162738)
XLA Ops:
  0.6 3.0 %collective-permute-start.2 = (bf16[128,2048]{1,0:T(8,128)(2,1)}, bf16[128,2048]{1,0:T(8,128)(2,1)}, u32[]{:S(2)}, u32[]{:S(2)}) collective-permute-start(bf16[128,2048]{1,0:T(8,128)(2,1)} %cotangent.1), channel_id=1, source_target_pairs={{0,2},{1,3},{2,0},{3,1},{4,6},{5,7},{6,4},{7,5},{8,10},{9,11},{10,... | collective-permute-start | bytes 1572872 | tf_op jit(solution)/shard_map/ppermute | solution.py:46
  4.9 1.9 %collective-permute-start.3 = (bf16[1,2048]{1,0:T(2,128)(2,1)S(1)}, bf16[1,2048]{1,0:T(2,128)(2,1)S(1)}, u32[]{:S(2)}, u32[]{:S(2)}) collective-permute-start(bf16[1,2048]{1,0:T(2,128)(2,1)S(1)} %reshape.17.gain), channel_id=1, source_target_pairs={{0,2},{1,3},{2,0},{3,1},{4,6},{5,7},{6,4},{7,5},{8,10},{9,11},{10,... | collective-permute-start | bytes 12296 | tf_op jit(solution)/shard_map/ppermute | solution.py:46
  6.9 1.6 %copy-done = bf16[128,8192]{1,0:T(8,128)(2,1)S(1)} copy-done((bf16[128,8192]{1,0:T(8,128)(2,1)S(1)}, bf16[128,8192]{1,0:T(8,128)(2,1)}, u32[]{:S(2)}) %copy-start) | copy-done | bytes 2097176
  8.5 1.6 %copy-done.2 = bf16[8192,128]{1,0:T(8,128)(2,1)S(1)} copy-done((bf16[8192,128]{1,0:T(8,128)(2,1)S(1)}, bf16[8192,128]{1,0:T(8,128)(2,1)}, u32[]{:S(2)}) %copy-start.2) | copy-done | bytes 2097176
  10.1 1.6 %copy-done.4 = bf16[8192,128]{1,0:T(8,128)(2,1)S(1)} copy-done((bf16[8192,128]{1,0:T(8,128)(2,1)S(1)}, bf16[8192,128]{1,0:T(8,128)(2,1)}, u32[]{:S(2)}) %copy-start.4) | copy-done | bytes 2097176
  11.7 1.6 %copy-done.6 = bf16[8192,128]{1,0:T(8,128)(2,1)S(1)} copy-done((bf16[8192,128]{1,0:T(8,128)(2,1)S(1)}, bf16[8192,128]{1,0:T(8,128)(2,1)}, u32[]{:S(2)}) %copy-start.6) | copy-done | bytes 2097176
  15.2 4.7 %prepare.1 = (bf16[384,4096]{1,0:T(8,128)(2,1)S(1)}, bf16[384,4096]{1,0:T(8,128)(2,1)}, bf16[8192,128]{1,0:T(8,128)(2,1)S(1)}, bf16[128,2048]{1,0:T(8,128)(2,1)S...) custom-call(s32[4]{0:T(128)S(1)} %iota_xor_fusion.order, ...), custom_call_target="tpu_custom_call" | custom-call | flops 1000 | bytes 1000 | tf_op jit(solution)/shard_map/prepare/pallas_call | solution.py:28
  20.0 7.3 %collective-permute-done.3 = bf16[1,2048]{1,0:T(2,128)(2,1)S(1)} collective-permute-done((bf16[1,2048]{1,0:T(2,128)(2,1)S(1)}, bf16[1,2048]{1,0:T(2,128)(2,1)S(1)}, u32[]{:S(2)}, u32[]{:S(2)}) %collective-permute-start.3) | collective-permute-done | bytes 4128 | tf_op jit(solution)/shard_map/ppermute | solution.py:46
  28.0 2.4 %begin.1 = (f32[128,1]{1,0:T(8,128)S(1)}, f32[128,128]{1,0:T(8,128)S(1)}) custom-call(s32[4]{0:T(128)S(1)} %iota_xor_fusion.order, bf16[128,2048]{1,0:T(8,128)(2,1)S(1)} %copy-done.8, bf16[128,2048]{1,0:T(8,128)(2,1)} %collective-permute-done.x1, bf16[128,2048]{1,0:T(8,128)(2,1)} %collective-permute-done.1.x2, bf16[128,2048]{1,0:T(8,128)(2,1)S(1)} %copy-done.10, ...), custom_call_target="tpu_custom_call" | custom-call | flops 1000 | bytes 1000 | tf_op jit(solution)/shard_map/begin/pallas_call | solution.py:28
  30.8 2.9 %project.1 = (bf16[128,384]{1,0:T(8,128)(2,1)S(1)}, f32[128,1]{1,0:T(8,128)S(1)}, bf16[128,512]{1,0:T(8,128)(2,1)S(1)}) custom-call(s32[4]{0:T(128)S(1)} %iota_xor_fusion.order, bf16[128,2048]{1,0:T(8,128)(2,1)S(1)} %copy-done.8, bf16[128,2048]{1,0:T(8,128)(2,1)} %collective-permute-done.x1, bf16[128,2048]{1,0:T(8,128)(2,1)} %collective-permute-done.1.x2, ...), custom_call_target="tpu_custom_call" | custom-call | flops 1000 | bytes 1000 | tf_op jit(solution)/shard_map/project/pallas_call | solution.py:28
  34.2 1.7 %collective-permute-start.12 = (bf16[128,4096]{1,0:T(8,128)(2,1)}, bf16[128,4096]{1,0:T(8,128)(2,1)}, u32[]{:S(2)}, u32[]{:S(2)}) collective-permute-start(bf16[128,4096]{1,0:T(8,128)(2,1)} %get-tuple-element.40), channel_id=1, source_target_pairs={{0,2},{1,3},{2,0},{3,1},{4,6},{5,7},{6,4},{7,5},{8,10},{9,11},{10,... | collective-permute-start | bytes 3145736 | tf_op jit(solution)/shard_map/ppermute | solution.py:46
  35.9 12.9 %all_to_all.22 = bf16[8,16,512]{2,1,0:T(8,128)(2,1)S(1)} all-to-all(bf16[8,16,512]{2,1,0:T(8,128)(2,1)S(1)} %bitcast.8), channel_id=1, replica_groups=mesh['dp'=8,'tensor'=4] {'dp'}, dimensions={0} | all-to-all | bytes 262144 | tf_op jit(solution)/shard_map/all_to_all | solution.py:321
  48.8 1.7 %attend.1 = bf16[128,512]{1,0:T(8,128)(2,1)} custom-call(bf16[128,512]{1,0:T(8,128)(2,1)S(1)} %bitcast.7, s32[1,128]{1,0:T(1,128)S(1)} %get-tuple-element.31.receive, s32[1,128]{1,0:T(1,128)S(1)} %get-tuple-element.32.segments), custom_call_target="tpu_custom_call" | custom-call | flops 1000 | bytes 1000 | tf_op jit(solution)/shard_map/attend/pallas_call | solution.py:28
  50.6 3.4 %all-to-all-start.1 = ((bf16[8,16,512]{2,1,0:T(8,128)(2,1)}), bf16[8,16,512]{2,1,0:T(8,128)(2,1)S(1)}, u32[]{:S(2)}, u32[]{:S(2)}) async-start(bf16[8,16,512]{2,1,0:T(8,128)(2,1)} %bitcast.4), calls=%async_computation.1 | async-start | bytes 262144 | tf_op jit(solution)/shard_map/all_to_all | solution.py:321
  54.0 7.2 %all-to-all-done.1 = bf16[8,16,512]{2,1,0:T(8,128)(2,1)S(1)} async-done(((bf16[8,16,512]{2,1,0:T(8,128)(2,1)}), bf16[8,16,512]{2,1,0:T(8,128)(2,1)S(1)}, u32[]{:S(2)}, u32[]{:S(2)}) %all-to-all-start.1) | async-done | bytes 131104 | tf_op jit(solution)/shard_map/all_to_all | solution.py:321
  61.6 1.1 %slice.4 = bf16[128,2048]{1,0:T(8,128)(2,1)S(1)} slice(bf16[128,4096]{1,0:T(8,128)(2,1)} %collective-permute-done.12.w_far), slice={[0:128], [2048:4096]} | slice | bytes 1048576 | tf_op jit(solution)/shard_map/slice | solution.py:382
  63.2 2.3 %spread_far.1 = bf16[128,1408]{1,0:T(8,128)(2,1)S(1)} custom-call(bf16[128,640]{1,0:T(8,128)(2,1)S(1)} %bring_home.1.own, bf16[128,640]{1,0:T(8,128)(2,1)S(1)} %collective-permute-done.8.near, bf16[384,4096]{1,0:T(8,128)(2,1)S(1)} %get-tuple-element.34.weights, bf16[384,4096]{1,0:T(8,128)(2,1)} %collective-permute-done.9.near_weights), custom_call_target="tpu_custom_call" | custom-call | flops 1000 | bytes 1000 | tf_op jit(solution)/shard_map/spread_far/pallas_call | solution.py:28
  66.2 2.3 %spread_rest.1 = bf16[128,1024]{1,0:T(8,128)(2,1)S(1)} custom-call(bf16[128,640]{1,0:T(8,128)(2,1)S(1)} %bring_home.1.own, bf16[128,640]{1,0:T(8,128)(2,1)S(1)} %collective-permute-done.8.near, bf16[384,4096]{1,0:T(8,128)(2,1)S(1)} %get-tuple-element.34.weights, bf16[384,4096]{1,0:T(8,128)(2,1)} %collective-permute-done.9.near_weights), custom_call_target="tpu_custom_call" | custom-call | flops 1000 | bytes 1000 | tf_op jit(solution)/shard_map/spread_rest/pallas_call | solution.py:28
  68.5 1.6 %collective-permute-start.14 = (bf16[128,1024]{1,0:T(8,128)(2,1)S(1)}, bf16[128,1024]{1,0:T(8,128)(2,1)S(1)}, u32[]{:S(2)}, u32[]{:S(2)}) collective-permute-start(bf16[128,1024]{1,0:T(8,128)(2,1)S(1)} %spread_rest.1), channel_id=1, source_target_pairs={{0,2},{1,3},{2,0},{3,1},{4,6},{5,7},{6,4},{7,5},{8,10},{9,11},{10,... | collective-permute-start | bytes 786440 | tf_op jit(solution)/shard_map/ppermute | solution.py:46
  70.1 2.6 %spread_own.1.grad_own = f32[128,2048]{1,0:T(8,128)S(1)} custom-call(bf16[128,640]{1,0:T(8,128)(2,1)S(1)} %bring_home.1.own, bf16[128,640]{1,0:T(8,128)(2,1)S(1)} %collective-permute-done.8.near, bf16[384,4096]{1,0:T(8,128)(2,1)S(1)} %get-tuple-element.34.weights, bf16[384,4096]{1,0:T(8,128)(2,1)} %collective-permute-done.9.near_weights), custom_call_target="tpu_custom_call" | custom-call | flops 1000 | bytes 1000 | tf_op jit(solution)/shard_map/spread_own/pallas_call | solution.py:28
  72.8 4.2 %collective-permute-done.10.far = bf16[128,1408]{1,0:T(8,128)(2,1)S(1)} collective-permute-done((bf16[128,1408]{1,0:T(8,128)(2,1)S(1)}, bf16[128,1408]{1,0:T(8,128)(2,1)S(1)}, u32[]{:S(2)}, u32[]{:S(2)}) %collective-permute-start.10) | collective-permute-done | bytes 360480 | tf_op jit(solution)/shard_map/ppermute | solution.py:46
  76.9 2.9 %finish_out.1 = bf16[128,2048]{1,0:T(8,128)(2,1)} custom-call(s32[4]{0:T(128)S(1)} %iota_xor_fusion.order, bf16[128,2048]{1,0:T(8,128)(2,1)S(1)} %copy-done.9, bf16[128,640]{1,0:T(8,128)(2,1)S(1)} %bring_home.1.own, bf16[128,640]{1,0:T(8,128)(2,1)S(1)} %collective-permute-done.8.near, bf16[128,1408]{1,0:T(8,128)(2,1)S(1)} %collective-permute-done.10.far, ...), custom_call_target="tpu_custom_call" | custom-call | flops 1000 | bytes 1000 | tf_op jit(solution)/shard_map/finish_out/pallas_call | solution.py:28
  79.8 1.8 %collective-permute-done.14.rest = bf16[128,1024]{1,0:T(8,128)(2,1)S(1)} collective-permute-done((bf16[128,1024]{1,0:T(8,128)(2,1)S(1)}, bf16[128,1024]{1,0:T(8,128)(2,1)S(1)}, u32[]{:S(2)}, u32[]{:S(2)}) %collective-permute-start.14) | collective-permute-done | bytes 262176 | tf_op jit(solution)/shard_map/ppermute | solution.py:46
  81.6 1.3 %finish_grad.1 = bf16[128,2048]{1,0:T(8,128)(2,1)} custom-call(bf16[128,2048]{1,0:T(8,128)(2,1)S(1)} %copy-done.9, bf16[128,2048]{1,0:T(8,128)(2,1)S(1)} %copy-done.11, bf16[1,2048]{1,0:T(2,128)(2,1)S(1)} %reshape.17.gain, f32[128,1]{1,0:T(8,128)S(1)} %get-tuple-element.41.inverse, bf16[128,640]{1,0:T(8,128)(2,1)S(1)} %bring_home.1.own, ...), custom_call_target="tpu_custom_call" | custom-call | flops 1000 | bytes 1000 | tf_op jit(solution)/shard_map/finish_grad/pallas_call | solution.py:28
  (55 shorter events, 6.4 us)
Async XLA Ops:
  0.6 26.6 %collective-permute-start.2 = (bf16[128,2048]{1,0:T(8,128)(2,1)}, bf16[128,2048]{1,0:T(8,128)(2,1)}, u32[]{:S(2)}, u32[]{:S(2)}) collective-permute-start(bf16[128,2048]{1,0:T(8,128)(2,1)} %cotangent.1), channel_id=1, source_target_pairs={{0,2},{1,3},{2,0},{3,1},{4,6},{5,7},{6,4},{7,5},{8,10},{9,11},{10,... | collective-permute-start | bytes 1572872 | tf_op jit(solution)/shard_map/ppermute | solution.py:46
  3.7 23.6 %collective-permute-start.1 = (bf16[128,2048]{1,0:T(8,128)(2,1)}, bf16[128,2048]{1,0:T(8,128)(2,1)}, u32[]{:S(2)}, u32[]{:S(2)}) collective-permute-start(bf16[128,2048]{1,0:T(8,128)(2,1)} %inputs.3), channel_id=1, source_target_pairs={{0,2},{1,3},{2,0},{3,1},{4,6},{5,7},{6,4},{7,5},{8,10},{9,11},{10,... | collective-permute-start | bytes 1572872 | tf_op jit(solution)/shard_map/ppermute | solution.py:46
  3.7 24.2 %collective-permute-start.7 = (bf16[128,2048]{1,0:T(8,128)(2,1)}, bf16[128,2048]{1,0:T(8,128)(2,1)}, u32[]{:S(2)}, u32[]{:S(2)}) collective-permute-start(bf16[128,2048]{1,0:T(8,128)(2,1)} %cotangent.1), channel_id=1, source_target_pairs={{0,1},{1,0},{2,3},{3,2},{4,5},{5,4},{6,7},{7,6},{8,9},{9,8},{10,11... | collective-permute-start | bytes 1572872 | tf_op jit(solution)/shard_map/ppermute | solution.py:46
  3.7 24.2 %collective-permute-start = (bf16[128,2048]{1,0:T(8,128)(2,1)}, bf16[128,2048]{1,0:T(8,128)(2,1)}, u32[]{:S(2)}, u32[]{:S(2)}) collective-permute-start(bf16[128,2048]{1,0:T(8,128)(2,1)} %inputs.3), channel_id=1, source_target_pairs={{0,1},{1,0},{2,3},{3,2},{4,5},{5,4},{6,7},{7,6},{8,9},{9,8},{10,11... | collective-permute-start | bytes 1572872 | tf_op jit(solution)/shard_map/ppermute | solution.py:46
  4.9 22.3 %collective-permute-start.3 = (bf16[1,2048]{1,0:T(2,128)(2,1)S(1)}, bf16[1,2048]{1,0:T(2,128)(2,1)S(1)}, u32[]{:S(2)}, u32[]{:S(2)}) collective-permute-start(bf16[1,2048]{1,0:T(2,128)(2,1)S(1)} %reshape.17.gain), channel_id=1, source_target_pairs={{0,2},{1,3},{2,0},{3,1},{4,6},{5,7},{6,4},{7,5},{8,10},{9,11},{10,... | collective-permute-start | bytes 12296 | tf_op jit(solution)/shard_map/ppermute | solution.py:46
  15.2 12.7 %copy-start.8 = (bf16[128,2048]{1,0:T(8,128)(2,1)S(1)}, bf16[128,2048]{1,0:T(8,128)(2,1)}, u32[]{:S(2)}) copy-start(bf16[128,2048]{1,0:T(8,128)(2,1)} %inputs.3) | copy-start | bytes 1572868
  15.2 12.7 %copy-start.10 = (bf16[128,2048]{1,0:T(8,128)(2,1)S(1)}, bf16[128,2048]{1,0:T(8,128)(2,1)}, u32[]{:S(2)}) copy-start(bf16[128,2048]{1,0:T(8,128)(2,1)} %cotangent.1) | copy-start | bytes 1572868
  15.2 15.2 %copy-start.7 = (bf16[8192,128]{1,0:T(8,128)(2,1)S(1)}, bf16[8192,128]{1,0:T(8,128)(2,1)}, u32[]{:S(2)}) copy-start(bf16[8192,128]{1,0:T(8,128)(2,1)} %w_value.3) | copy-start | bytes 6291460
  20.0 10.4 %copy-start.15 = (bf16[128,2048]{1,0:T(8,128)(2,1)}, bf16[128,2048]{1,0:T(8,128)(2,1)S(1)}, u32[]{:S(2)}) copy-start(bf16[128,2048]{1,0:T(8,128)(2,1)S(1)} %get-tuple-element.38) | copy-start | bytes 1572868
  27.2 3.2 %collective-permute-start.5 = (bf16[128,2048]{1,0:T(8,128)(2,1)}, bf16[128,2048]{1,0:T(8,128)(2,1)S(1)}, u32[]{:S(2)}, u32[]{:S(2)}) collective-permute-start(bf16[128,2048]{1,0:T(8,128)(2,1)} %collective-permute-done.2.c2), channel_id=1, source_target_pairs={{0,1},{1,0},{2,3},{3,2},{4,5},{5,4},{6,7},{7,6},{8,9},{9,8},{10,11... | collective-permute-start | bytes 1572872 | tf_op jit(solution)/shard_map/ppermute | solution.py:46
  27.2 3.2 %collective-permute-start.4 = (bf16[128,2048]{1,0:T(8,128)(2,1)}, bf16[128,2048]{1,0:T(8,128)(2,1)S(1)}, u32[]{:S(2)}, u32[]{:S(2)}) collective-permute-start(bf16[128,2048]{1,0:T(8,128)(2,1)} %collective-permute-done.1.x2), channel_id=1, source_target_pairs={{0,1},{1,0},{2,3},{3,2},{4,5},{5,4},{6,7},{7,6},{8,9},{9,8},{10,11... | collective-permute-start | bytes 1572872 | tf_op jit(solution)/shard_map/ppermute | solution.py:46
  27.8 2.6 %collective-permute-start.6 = (bf16[2,2048]{1,0:T(2,128)(2,1)S(1)}, bf16[2,2048]{1,0:T(2,128)(2,1)S(1)}, u32[]{:S(2)}, u32[]{:S(2)}) collective-permute-start(bf16[2,2048]{1,0:T(2,128)(2,1)S(1)} %pad_maximum_fusion.gain_own), channel_id=1, source_target_pairs={{0,1},{1,0},{2,3},{3,2},{4,5},{5,4},{6,7},{7,6},{8,9},{9,8},{10,11... | collective-permute-start | bytes 24584 | tf_op jit(solution)/shard_map/ppermute | solution.py:46
  27.9 2.8 %copy-start.5 = (bf16[8192,128]{1,0:T(8,128)(2,1)S(1)}, bf16[8192,128]{1,0:T(8,128)(2,1)}, u32[]{:S(2)}) copy-start(bf16[8192,128]{1,0:T(8,128)(2,1)} %w_key.3) | copy-start | bytes 6291460
  33.7 29.6 %collective-permute-start.9 = (bf16[384,4096]{1,0:T(8,128)(2,1)}, bf16[384,4096]{1,0:T(8,128)(2,1)}, u32[]{:S(2)}, u32[]{:S(2)}) collective-permute-start(bf16[384,4096]{1,0:T(8,128)(2,1)} %get-tuple-element.36), channel_id=1, source_target_pairs={{0,1},{1,0},{2,3},{3,2},{4,5},{5,4},{6,7},{7,6},{8,9},{9,8},{10,11... | collective-permute-start | bytes 9437192 | tf_op jit(solution)/shard_map/ppermute | solution.py:46
  34.2 27.4 %collective-permute-start.12 = (bf16[128,4096]{1,0:T(8,128)(2,1)}, bf16[128,4096]{1,0:T(8,128)(2,1)}, u32[]{:S(2)}, u32[]{:S(2)}) collective-permute-start(bf16[128,4096]{1,0:T(8,128)(2,1)} %get-tuple-element.40), channel_id=1, source_target_pairs={{0,2},{1,3},{2,0},{3,1},{4,6},{5,7},{6,4},{7,5},{8,10},{9,11},{10,... | collective-permute-start | bytes 3145736 | tf_op jit(solution)/shard_map/ppermute | solution.py:46
  50.6 10.7 %all-to-all-start.1 = ((bf16[8,16,512]{2,1,0:T(8,128)(2,1)}), bf16[8,16,512]{2,1,0:T(8,128)(2,1)S(1)}, u32[]{:S(2)}, u32[]{:S(2)}) async-start(bf16[8,16,512]{2,1,0:T(8,128)(2,1)} %bitcast.4), calls=%async_computation.1 | async-start | bytes 262144 | tf_op jit(solution)/shard_map/all_to_all | solution.py:321
  54.0 18.8 %collective-permute-start.11 = (bf16[128,2048]{1,0:T(8,128)(2,1)}, bf16[128,2048]{1,0:T(8,128)(2,1)}, u32[]{:S(2)}, u32[]{:S(2)}) collective-permute-start(bf16[128,2048]{1,0:T(8,128)(2,1)} %copy-done.15), channel_id=1, source_target_pairs={{0,1},{1,0},{2,3},{3,2},{4,5},{5,4},{6,7},{7,6},{8,9},{9,8},{10,11... | collective-permute-start | bytes 1572872 | tf_op jit(solution)/shard_map/ppermute | solution.py:46
  61.5 1.7 %collective-permute-start.8 = (bf16[128,640]{1,0:T(8,128)(2,1)S(1)}, bf16[128,640]{1,0:T(8,128)(2,1)S(1)}, u32[]{:S(2)}, u32[]{:S(2)}) collective-permute-start(bf16[128,640]{1,0:T(8,128)(2,1)S(1)} %bring_home.1.own), channel_id=1, source_target_pairs={{0,1},{1,0},{2,3},{3,2},{4,5},{5,4},{6,7},{7,6},{8,9},{9,8},{10,11... | collective-permute-start | bytes 491528 | tf_op jit(solution)/shard_map/ppermute | solution.py:46
  62.7 10.1 %collective-permute-start.13 = (bf16[128,2048]{1,0:T(8,128)(2,1)S(1)}, bf16[128,2048]{1,0:T(8,128)(2,1)S(1)}, u32[]{:S(2)}, u32[]{:S(2)}) collective-permute-start(bf16[128,2048]{1,0:T(8,128)(2,1)S(1)} %slice.4), channel_id=1, source_target_pairs={{0,1},{1,0},{2,3},{3,2},{4,5},{5,4},{6,7},{7,6},{8,9},{9,8},{10,11... | collective-permute-start | bytes 1572872 | tf_op jit(solution)/shard_map/ppermute | solution.py:46
  65.6 11.3 %collective-permute-start.10 = (bf16[128,1408]{1,0:T(8,128)(2,1)S(1)}, bf16[128,1408]{1,0:T(8,128)(2,1)S(1)}, u32[]{:S(2)}, u32[]{:S(2)}) collective-permute-start(bf16[128,1408]{1,0:T(8,128)(2,1)S(1)} %spread_far.1), channel_id=1, source_target_pairs={{0,2},{1,3},{2,0},{3,1},{4,6},{5,7},{6,4},{7,5},{8,10},{9,11},{10,... | collective-permute-start | bytes 1081352 | tf_op jit(solution)/shard_map/ppermute | solution.py:46
  68.5 8.4 %copy-start.1 = (bf16[128,8192]{1,0:T(8,128)(2,1)S(1)}, bf16[128,8192]{1,0:T(8,128)(2,1)}, u32[]{:S(2)}) copy-start(bf16[128,8192]{1,0:T(8,128)(2,1)} %w_own.1) | copy-start | bytes 6291460
  68.5 8.4 %copy-start.9 = (bf16[128,2048]{1,0:T(8,128)(2,1)S(1)}, bf16[128,2048]{1,0:T(8,128)(2,1)}, u32[]{:S(2)}) copy-start(bf16[128,2048]{1,0:T(8,128)(2,1)} %inputs.3) | copy-start | bytes 1572868
  68.5 13.1 %collective-permute-start.14 = (bf16[128,1024]{1,0:T(8,128)(2,1)S(1)}, bf16[128,1024]{1,0:T(8,128)(2,1)S(1)}, u32[]{:S(2)}, u32[]{:S(2)}) collective-permute-start(bf16[128,1024]{1,0:T(8,128)(2,1)S(1)} %spread_rest.1), channel_id=1, source_target_pairs={{0,2},{1,3},{2,0},{3,1},{4,6},{5,7},{6,4},{7,5},{8,10},{9,11},{10,... | collective-permute-start | bytes 786440 | tf_op jit(solution)/shard_map/ppermute | solution.py:46
  72.7 8.9 %copy-start.11 = (bf16[128,2048]{1,0:T(8,128)(2,1)S(1)}, bf16[128,2048]{1,0:T(8,128)(2,1)}, u32[]{:S(2)}) copy-start(bf16[128,2048]{1,0:T(8,128)(2,1)} %cotangent.1) | copy-start | bytes 1572868
  (8 other events, 10.8 us)

commit v5 on v4

--- a/solution.py
+++ b/solution.py
@@ -67,17 +67,17 @@
     own_turned,
     near_turned,
     output_turned,
-    near_output,
+    own_here,
+    near_here,
     far_output,
     send_out,
     receive_out,
     segments_out,
 ):
-    width = near_output.shape[1]
-    for target, slots in ((near_output, (1,)), (far_output, (2, 3))):
-        for part, slot in enumerate(slots):
-            columns = pl.ds(block_start(order, slot, width), width)
-            target[:, part * width : (part + 1) * width] = w_output[:, columns]
+    width = near_here.shape[1]
+    far_left, far_right = far_output.at[:, :width], far_output.at[:, width:]
+    for slot, target in enumerate((own_here, near_here, far_left, far_right)):
+        target[...] = w_output[:, pl.ds(block_start(order, slot, width), width)]
     for start in range(0, w_output.shape[1], TILE):
         output_turned[start : start + TILE, :] = w_output[:, start : start + TILE].T
     for source, target in ((send, send_out), (receive, receive_out), (segments, segments_out)):
@@ -103,6 +103,7 @@
             shape(low, 3 * heads, 2 * width),
             shape(low, w_output.shape[1], heads),
             shape(low, heads, width),
+            shape(low, heads, width),
             shape(low, heads, 2 * width),
             shape(jnp.int32, *send.shape),
             shape(jnp.int32, *receive.shape),
@@ -117,20 +118,27 @@
     return jnp.sum(wide * wide, axis=-1, keepdims=True)
 
 
-def begin_kernel(order, x0, x1, x2, c0, c1, c2, output_turned, squares, part):
+def begin_kernel(order, x0, x1, c0, c1, output_turned, squares, part):
     width = x0.shape[1]
-    squares[...] = sum_squares(x0) + sum_squares(x1) + sum_squares(x2)
+    squares[...] = sum_squares(x0) + sum_squares(x1)
     total = 0.0
-    for index, block in enumerate((c0, c1, c2)):
+    for index, block in enumerate((c0, c1)):
         here = pl.ds(block_start(order, index, width), width)
         total = total + dot(block[...], output_turned[here, :])
     part[...] = total
 
 
-def begin(order, blocks, output_turned):
-    rows = blocks[0].shape[0]
+def go_on_kernel(order, x2, c2, output_turned, squares_in, part_in, squares, part):
+    width = x2.shape[1]
+    here = pl.ds(block_start(order, 2, width), width)
+    part[...] = part_in[...] + dot(c2[...], output_turned[here, :])
+    squares[...] = squares_in[...] + sum_squares(x2)
+
+
+def begin(kernel, name, *operands):
+    rows = operands[1].shape[0]
     shapes = [shape(jnp.float32, rows, 1), shape(jnp.float32, rows, HEAD_DIM)]
-    return call(begin_kernel, "begin", shapes, (order, *blocks, output_turned))
+    return call(kernel, name, shapes, operands)
 
 
 def project_kernel(
@@ -251,16 +259,23 @@
     return call(bring_home_kernel, "bring_home", out, (moved, send, home), first=VMEM)
 
 
-def spread_into(own, near, weights, near_weights, first, out, place):
+def spread_into(own, near, weights, near_weights, first, out, place, held, total, sem):
+    span = held.shape[1]
+    copy = pltpu.make_async_copy(near_weights.at[:, pl.ds(first, span)], held, sem)
+    copy.start()
     own_grads = own[:, : 3 * HEAD_DIM]
     near_grads = near[:, : 3 * HEAD_DIM]
-    for start in range(0, out.shape[1] - place, TILE):
+    for start in range(0, span, TILE):
         columns = slice(first + start, first + start + TILE)
-        total = dot(own_grads, weights[:, columns]) + dot(near_grads, near_weights[:, columns])
-        out[:, place + start : place + start + TILE] = total.astype(out.dtype)
-
-
-def spread_far_kernel(own, near, weights, near_weights, out):
+        total[:, start : start + TILE] = dot(own_grads, weights[:, columns])
+    copy.wait()
+    for start in range(0, span, TILE):
+        tile = slice(start, start + TILE)
+        result = total[:, tile] + dot(near_grads, held[:, tile])
+        out[:, place + start : place + start + TILE] = result.astype(out.dtype)
+
+
+def spread_far_kernel(own, near, weights, near_weights, out, *scratch):
     width = weights.shape[1] // 2
     write_parts(
         read_parts(own[:, 4 * HEAD_DIM :]) + read_parts(near[:, 4 * HEAD_DIM :]),
@@ -269,33 +284,47 @@
     attended = slice(3 * HEAD_DIM, 4 * HEAD_DIM)
     out[:, HEAD_DIM : 2 * HEAD_DIM] = own[:, attended]
     out[:, 2 * HEAD_DIM : 3 * HEAD_DIM] = near[:, attended]
-    spread_into(own, near, weights, near_weights, width, out, 3 * HEAD_DIM)
-
-
-def spread_rest_kernel(own, near, weights, near_weights, out):
+    spread_into(own, near, weights, near_weights, width, out, 3 * HEAD_DIM, *scratch)
+
+
+def spread_rest_kernel(own, near, weights, near_weights, out, *scratch):
     width = weights.shape[1] // 2
-    spread_into(own, near, weights, near_weights, width + width // 2, out, 0)
-
-
-def spread_own_kernel(own, near, weights, near_weights, out):
-    spread_into(own, near, weights, near_weights, 0, out, 0)
-
-
-def finish_out_kernel(order, inputs, own, near, far, w_own, w_near, w_far, w_last, out):
+    spread_into(own, near, weights, near_weights, width + width // 2, out, 0, *scratch)
+
+
+def spread_own_kernel(own, near, weights, near_weights, out, *scratch):
+    spread_into(own, near, weights, near_weights, 0, out, 0, *scratch)
+
+
+def spread(kernel, name, out, span, operands):
+    rows, depth = operands[0].shape[0], operands[2].shape[0]
+    return pl.pallas_call(
+        kernel,
+        out_shape=out,
+        in_specs=[VMEM] * 3 + [pl.BlockSpec(memory_space=pl.ANY)],
+        out_specs=VMEM,
+        scratch_shapes=[
+            pltpu.VMEM((depth, span), jnp.bfloat16),
+            pltpu.VMEM((rows, span), jnp.float32),
+            pltpu.SemaphoreType.DMA,
+        ],
+        compiler_params=pltpu.CompilerParams(vmem_limit_bytes=VMEM_LIMIT),
+        cost_estimate=pl.CostEstimate(flops=1000, bytes_accessed=1000, transcendentals=0),
+        name=name,
+    )(*operands)
+
+
+def finish_out_kernel(inputs, own, near, far, w_own, w_near, w_far, w_last, out):
     width = inputs.shape[1]
-    first = block_start(order, 0, width)
     attended = slice(3 * HEAD_DIM, 4 * HEAD_DIM)
-    rows = (
-        own[:, attended],
-        near[:, attended],
-        far[:, HEAD_DIM : 2 * HEAD_DIM],
-        far[:, 2 * HEAD_DIM : 3 * HEAD_DIM],
+    rows = jnp.concatenate(
+        [own[:, attended], near[:, attended], far[:, HEAD_DIM : 3 * HEAD_DIM]], axis=1
     )
     for start in range(0, width, TILE):
         tile = slice(start, start + TILE)
-        total = dot(rows[0], w_own[:, pl.ds(first + start, TILE)])
-        for left, weight in zip(rows[1:], (w_near, w_far, w_last)):
-            total = total + dot(left, weight[:, tile])
+        second = slice(width + start, width + start + TILE)
+        stacked = [w_own[:, tile], w_near[:, tile], w_far[:, tile], w_last[:, second]]
+        total = dot(rows, jnp.concatenate(stacked, axis=0))
         out[:, tile] = (inputs[:, tile].astype(jnp.float32) + total).astype(jnp.bfloat16)
 
 
@@ -349,24 +378,25 @@
     x1 = swap(inputs, 1, tensor)
     c1 = swap(cotangent, 1, tensor)
     weights = (w_query, w_key, w_value)
-    own_turned, near_turned, output_turned, near_output, far_output, send, receive, segments = (
-        prepare(
-            order,
-            *weights,
-            w_output,
-            send_rows,
-            receive_slots.reshape(1, rows),
-            owner_segments.reshape(1, rows),
-            width,
-        )
-    )
-    x2, c2, gain2, segments = lax.optimization_barrier((x2, c2, gain2, segments))
+    (own_turned, near_turned, output_turned, own_here, near_here, far_output, *indices) = prepare(
+        order,
+        *weights,
+        w_output,
+        send_rows,
+        receive_slots.reshape(1, rows),
+        owner_segments.reshape(1, rows),
+        width,
+    )
+    send, receive, segments = indices
+    squares, part = begin(
+        begin_kernel, "begin", order, inputs, x1, cotangent, c1, output_turned
+    )
+    x2, c2, gain2, squares, part = lax.optimization_barrier((x2, c2, gain2, squares, part))
     x3 = swap(x2, 1, tensor)
     c3 = swap(c2, 1, tensor)
     gain_own = jnp.concatenate([gain, gain2], axis=0)
     gain_near = swap(gain_own, 1, tensor)
-
-    squares, part = begin(order, (inputs, x1, x2, cotangent, c1, c2), output_turned)
+    squares, part = begin(go_on_kernel, "go_on", order, x2, c2, output_turned, squares, part)
     home, inverse_rms, bucket = project(
         order,
         (inputs, x1, x2, x3, c3),
@@ -376,34 +406,33 @@
         part,
         send,
     )
-    near_output = swap(after(near_output, home), 1, tensor)
     near_turned = swap(after(near_turned, home), 1, tensor)
     far_output = swap(after(far_output, home), 2, tensor)
-    last_output = swap(far_output[:, width:], 1, tensor)
-    own = bring_home(move(attend(move(bucket), receive, segments)), send, home)
+    back = attend(move(bucket), receive, segments)
+    own = bring_home(move(back), send, home)
 
     near = swap(own, 1, tensor)
     sides = (own, near, own_turned, near_turned)
     half = width // 2
-    far = call(
-        spread_far_kernel,
-        "spread_far",
-        shape(low, rows, 3 * HEAD_DIM + half),
-        sides,
-        first=VMEM,
-    )
-    far = swap(far, 2, tensor)
-    rest = call(spread_rest_kernel, "spread_rest", shape(low, rows, half), sides, first=VMEM)
-    rest = swap(rest, 2, tensor)
-    grad_own = call(
-        spread_own_kernel, "spread_own", shape(jnp.float32, rows, width), sides, first=VMEM
-    )
+    far_shape = shape(low, rows, 3 * HEAD_DIM + half)
+    far_part = spread(spread_far_kernel, "spread_far", far_shape, half, sides)
+    far = swap(far_part, 2, tensor)
+    sides = (after(own, far_part), *sides[1:])
+    rest_part = spread(spread_rest_kernel, "spread_rest", shape(low, rows, half), half, sides)
+    rest = swap(rest_part, 2, tensor)
+    sides = (after(own, rest_part), *sides[1:])
+    own_shape = shape(jnp.float32, rows, width)
+    grad_own = spread(spread_own_kernel, "spread_own", own_shape, width, sides)
+    near_here = swap(after(near_here, home), 1, tensor)
+    last_output = swap(after(far_output, near), 1, tensor)
     layer_out = call(
         finish_out_kernel,
         "finish_out",
         shape(low, rows, width),
-        (order, inputs, own, near, far, w_output, near_output, far_output, last_output),
-    )
+        (inputs, own, near, far, own_here, near_here, far_output, last_output),
+        first=VMEM,
+    )
+    rest = after(rest, layer_out)
     input_grad = call(
         finish_grad_kernel,
         "finish_grad",

time: 83.5 us -> 79.5 us (0.952)
  Pallas kernels: 23.5 us -> 13.3 us
  blocking collectives: 12.9 us -> 22.7 us
  starting transfers between devices: 14.7 us -> 10.9 us
  waiting for transfers between devices: 20.4 us -> 22.4 us
  local copies, waits for them, and re-layouts: 10.5 us -> 9.04 us
    pallas_call x10 -> x8, Pallas kernels: 23.5 us -> 10.9 us  [call(): pl.pallas_call(kernel, out_shape=shapes, in_specs=[first] + [rest] * (len...]
    all_to_all x1 -> x2, blocking collectives: 12.9 us -> 22.7 us  [move(): return lax.all_to_all(bucket, 'dp', split_axis=0, concat_axis=0, tiled=True)]
    ppermute x15, waiting for transfers between devices: 13.2 us -> 22.4 us  [swap(): return lax.ppermute(array, 'tensor', [(i, i ^ mask) for i in range(count)])]
    all_to_all x1 -> x0, waiting for transfers between devices: 7.2 us -> none  [move(): return lax.all_to_all(bucket, 'dp', split_axis=0, concat_axis=0, tiled=True)]
    all_to_all x1 -> x0, starting transfers between devices: 3.37 us -> none  [move(): return lax.all_to_all(bucket, 'dp', split_axis=0, concat_axis=0, tiled=True)]
    pallas_call x0 -> x3, Pallas kernels: none -> 2.35 us  [spread(): pl.pallas_call(kernel, out_shape=out, in_specs=[VMEM] * 3 + [pl.BlockSpec...]
    slice x1 -> x0, local copies, waits for them, and re-layouts: 1.08 us -> none  [on_device(): last_output = swap(far_output[:, width:], 1, tensor)]
    unnamed x32 -> x22, local copies, waits for them, and re-layouts: 8.72 us -> 8.34 us
  transfers between devices with their start and end apart: 16 -> 15, of which waited for: 4 -> 5; matrix products, arithmetic and copies ran while one was open for 2% -> 1% of each run, Pallas kernels for 23% -> 12%
where the time goes in v5:
time: 79.5 us; the launch traced here: 79.1 us
  blocking collectives  22.7 us (29%)
  waiting for transfers between devices  22.4 us (28%)
  Pallas kernels  13.3 us (17%)
  starting transfers between devices  10.9 us (14%)
  local copies, waits for them, and re-layouts  9.04 us (11%)
    all_to_all x2, blocking collectives, move(): return lax.all_to_all(bucket, 'dp', split_axis=0, concat_axis=0, tiled=True)  22.7 us
    ppermute x15, waiting for transfers between devices, swap(): return lax.ppermute(array, 'tensor', [(i, i ^ mask) for i in range(count)])  22.4 us
    pallas_call x8, Pallas kernels, call(): pl.pallas_call(kernel, out_shape=shapes, in_specs=[first] + [rest] * (len...  10.9 us
    ppermute x15, starting transfers between devices, swap(): return lax.ppermute(array, 'tensor', [(i, i ^ mask) for i in range(count)])  10.9 us
    unnamed x22, local copies, waits for them, and re-layouts  8.34 us
    pallas_call x3, Pallas kernels, spread(): pl.pallas_call(kernel, out_shape=out, in_specs=[VMEM] * 3 + [pl.BlockSpec...  2.35 us
  transfers between devices with their start and end apart: 15, of which 5 were waited for; matrix products, arithmetic and copies ran while one was open for 1% of the time, Pallas kernels for 12%

profile of v5, /device:TPU:0, one launch (start us, length us, event | category | flops | bytes accessed | tf_op | source)
XLA Modules:
  0.0 79.1 jit_solution(16547590034808469542)
XLA Ops:
  1.2 2.9 %collective-permute-start.2 = (bf16[128,2048]{1,0:T(8,128)(2,1)}, bf16[128,2048]{1,0:T(8,128)(2,1)S(1)}, u32[]{:S(2)}, u32[]{:S(2)}) collective-permute-start(bf16[128,2048]{1,0:T(8,128)(2,1)} %cotangent.1), channel_id=1, source_target_pairs={{0,2},{1,3},{2,0},{3,1},{4,6},{5,7},{6,4},{7,5},{8,10},{9,11},{10,... | collective-permute-start | bytes 1572872 | tf_op jit(solution)/shard_map/ppermute | solution.py:46
  4.9 2.0 %collective-permute-start.3 = (bf16[1,2048]{1,0:T(2,128)(2,1)S(1)}, bf16[1,2048]{1,0:T(2,128)(2,1)S(1)}, u32[]{:S(2)}, u32[]{:S(2)}) collective-permute-start(bf16[1,2048]{1,0:T(2,128)(2,1)S(1)} %reshape.17.gain), channel_id=1, source_target_pairs={{0,2},{1,3},{2,0},{3,1},{4,6},{5,7},{6,4},{7,5},{8,10},{9,11},{10,... | collective-permute-start | bytes 12296 | tf_op jit(solution)/shard_map/ppermute | solution.py:46
  6.9 1.6 %copy-done.1 = bf16[8192,128]{1,0:T(8,128)(2,1)S(1)} copy-done((bf16[8192,128]{1,0:T(8,128)(2,1)S(1)}, bf16[8192,128]{1,0:T(8,128)(2,1)}, u32[]{:S(2)}) %copy-start.1) | copy-done | bytes 2097176
  8.5 1.6 %copy-done.2 = bf16[8192,128]{1,0:T(8,128)(2,1)S(1)} copy-done((bf16[8192,128]{1,0:T(8,128)(2,1)S(1)}, bf16[8192,128]{1,0:T(8,128)(2,1)}, u32[]{:S(2)}) %copy-start.2) | copy-done | bytes 2097176
  10.1 1.6 %copy-done.4 = bf16[8192,128]{1,0:T(8,128)(2,1)S(1)} copy-done((bf16[8192,128]{1,0:T(8,128)(2,1)S(1)}, bf16[8192,128]{1,0:T(8,128)(2,1)}, u32[]{:S(2)}) %copy-start.4) | copy-done | bytes 2097176
  11.7 1.6 %copy-done.6 = bf16[128,8192]{1,0:T(8,128)(2,1)S(1)} copy-done((bf16[128,8192]{1,0:T(8,128)(2,1)S(1)}, bf16[128,8192]{1,0:T(8,128)(2,1)}, u32[]{:S(2)}) %copy-start.6) | copy-done | bytes 2097176
  15.2 2.8 %prepare.1 = (bf16[384,4096]{1,0:T(8,128)(2,1)S(1)}, bf16[384,4096]{1,0:T(8,128)(2,1)S(1)}, bf16[8192,128]{1,0:T(8,128)(2,1)S(1)}, bf16[128,2048]{1,0:T(8,128)(2...) custom-call(s32[4]{0:T(128)S(1)} %iota_xor_fusion.order, ...), custom_call_target="tpu_custom_call" | custom-call | flops 1000 | bytes 1000 | tf_op jit(solution)/shard_map/prepare/pallas_call | solution.py:28
  18.1 1.1 %begin.1 = (f32[128,1]{1,0:T(8,128)S(1)}, f32[128,128]{1,0:T(8,128)S(1)}) custom-call(s32[4]{0:T(128)S(1)} %iota_xor_fusion.order, bf16[128,2048]{1,0:T(8,128)(2,1)S(1)} %copy-done, bf16[128,2048]{1,0:T(8,128)(2,1)S(1)} %collective-permute-done.x1, bf16[128,2048]{1,0:T(8,128)(2,1)S(1)} %copy-done.7, bf16[128,2048]{1,0:T(8,128)(2,1)S(1)} %collective-permute-done.4.c1, ...), custom_call_target="tpu_custom_call" | custom-call | flops 1000 | bytes 1000 | tf_op jit(solution)/shard_map/begin/pallas_call | solution.py:28
  19.2 8.7 %collective-permute-done.3 = bf16[1,2048]{1,0:T(2,128)(2,1)S(1)} collective-permute-done((bf16[1,2048]{1,0:T(2,128)(2,1)S(1)}, bf16[1,2048]{1,0:T(2,128)(2,1)S(1)}, u32[]{:S(2)}, u32[]{:S(2)}) %collective-permute-start.3) | collective-permute-done | bytes 4128 | tf_op jit(solution)/shard_map/ppermute | solution.py:46
  28.6 0.9 %go_on.1 = (f32[128,1]{1,0:T(8,128)S(1)}, f32[128,128]{1,0:T(8,128)S(1)}) custom-call(s32[4]{0:T(128)S(1)} %iota_xor_fusion.order, bf16[128,2048]{1,0:T(8,128)(2,1)S(1)} %collective-permute-done.1.x2, bf16[128,2048]{1,0:T(8,128)(2,1)S(1)} %collective-permute-done.2.c2, bf16[8192,128]{1,0:T(8,128)(2,1)S(1)} %get-tuple-element.30.output_turned, ...), custom_call_target="tpu_custom_call" | custom-call | flops 1000 | bytes 1000 | tf_op jit(solution)/shard_map/go_on/pallas_call | solution.py:28
  29.5 1.1 %collective-permute-done.7.gain_near = bf16[2,2048]{1,0:T(2,128)(2,1)S(1)} collective-permute-done((bf16[2,2048]{1,0:T(2,128)(2,1)S(1)}, bf16[2,2048]{1,0:T(2,128)(2,1)S(1)}, u32[]{:S(2)}, u32[]{:S(2)}) %collective-permute-start.7) | collective-permute-done | bytes 8224 | tf_op jit(solution)/shard_map/ppermute | solution.py:46
  30.7 2.3 %project.1 = (bf16[128,384]{1,0:T(8,128)(2,1)S(1)}, f32[128,1]{1,0:T(8,128)S(1)}, bf16[128,512]{1,0:T(8,128)(2,1)S(1)}) custom-call(s32[4]{0:T(128)S(1)} %iota_xor_fusion.order, bf16[128,2048]{1,0:T(8,128)(2,1)S(1)} %copy-done, bf16[128,2048]{1,0:T(8,128)(2,1)S(1)} %collective-permute-done.x1, bf16[128,2048]{1,0:T(8,128)(2,1)S(1)} %collective-permute-done.1.x2, ...), custom_call_target="tpu_custom_call" | custom-call | flops 1000 | bytes 1000 | tf_op jit(solution)/shard_map/project/pallas_call | solution.py:28
  33.1 1.8 %collective-permute-start.12 = (bf16[128,4096]{1,0:T(8,128)(2,1)S(1)}, bf16[128,4096]{1,0:T(8,128)(2,1)S(1)}, u32[]{:S(2)}, u32[]{:S(2)}) collective-permute-start(bf16[128,4096]{1,0:T(8,128)(2,1)S(1)} %get-tuple-element.52), channel_id=1, source_target_pairs={{0,2},{1,3},{2,0},{3,1},{4,6},{5,7},{6,4},{7,5},{8,10},{9,11},{10,... | collective-permute-start | bytes 3145736 | tf_op jit(solution)/shard_map/ppermute | solution.py:46
  34.9 12.9 %all_to_all.22 = bf16[8,16,512]{2,1,0:T(8,128)(2,1)S(1)} all-to-all(bf16[8,16,512]{2,1,0:T(8,128)(2,1)S(1)} %bitcast.9), channel_id=1, replica_groups=mesh['dp'=8,'tensor'=4] {'dp'}, dimensions={0} | all-to-all | bytes 262144 | tf_op jit(solution)/shard_map/all_to_all | solution.py:350
  47.8 1.1 %attend.1 = bf16[128,512]{1,0:T(8,128)(2,1)S(1)} custom-call(bf16[128,512]{1,0:T(8,128)(2,1)S(1)} %bitcast.6, s32[1,128]{1,0:T(1,128)S(1)} %get-tuple-element.42.receive, s32[1,128]{1,0:T(1,128)S(1)} %get-tuple-element.43.segments), custom_call_target="tpu_custom_call" | custom-call | flops 1000 | bytes 1000 | tf_op jit(solution)/shard_map/attend/pallas_call | solution.py:28
  48.9 9.7 %all_to_all.23 = bf16[8,16,512]{2,1,0:T(8,128)(2,1)S(1)} all-to-all(bf16[8,16,512]{2,1,0:T(8,128)(2,1)S(1)} %bitcast.7), channel_id=1, replica_groups=mesh['dp'=8,'tensor'=4] {'dp'}, dimensions={0} | all-to-all | bytes 262144 | tf_op jit(solution)/shard_map/all_to_all | solution.py:350
  59.0 1.4 %collective-permute-done.8.near = bf16[128,640]{1,0:T(8,128)(2,1)S(1)} collective-permute-done((bf16[128,640]{1,0:T(8,128)(2,1)S(1)}, bf16[128,640]{1,0:T(8,128)(2,1)S(1)}, u32[]{:S(2)}, u32[]{:S(2)}) %collective-permute-start.8) | collective-permute-done | bytes 163872 | tf_op jit(solution)/shard_map/ppermute | solution.py:46
  60.9 0.8 %spread_far.1 = bf16[128,1408]{1,0:T(8,128)(2,1)S(1)} custom-call(bf16[128,640]{1,0:T(8,128)(2,1)S(1)} %bring_home.1.own, bf16[128,640]{1,0:T(8,128)(2,1)S(1)} %collective-permute-done.8.near, bf16[384,4096]{1,0:T(8,128)(2,1)S(1)} %get-tuple-element.45.weights, bf16[384,4096]{1,0:T(8,128)(2,1)S(1)} %collective-permute-done.9.near_weights), custom_call_target="tpu_custom_call" | custom-call | flops 1000 | bytes 1000 | tf_op jit(solution)/shard_map/spread_far/pallas_call | solution.py:301
  62.9 1.6 %collective-permute-start.14 = (bf16[128,1024]{1,0:T(8,128)(2,1)S(1)}, bf16[128,1024]{1,0:T(8,128)(2,1)S(1)}, u32[]{:S(2)}, u32[]{:S(2)}) collective-permute-start(bf16[128,1024]{1,0:T(8,128)(2,1)S(1)} %spread_rest.1), channel_id=1, source_target_pairs={{0,2},{1,3},{2,0},{3,1},{4,6},{5,7},{6,4},{7,5},{8,10},{9,11},{10,... | collective-permute-start | bytes 786440 | tf_op jit(solution)/shard_map/ppermute | solution.py:46
  64.4 1.0 %spread_own.1.grad_own = f32[128,2048]{1,0:T(8,128)S(1)} custom-call(bf16[128,640]{1,0:T(8,128)(2,1)S(1)} %bring_home.1.own, bf16[128,640]{1,0:T(8,128)(2,1)S(1)} %collective-permute-done.8.near, bf16[384,4096]{1,0:T(8,128)(2,1)S(1)} %get-tuple-element.45.weights, bf16[384,4096]{1,0:T(8,128)(2,1)S(1)} %collective-permute-done.9.near_weights), custom_call_target="tpu_custom_call" | custom-call | flops 1000 | bytes 1000 | tf_op jit(solution)/shard_map/spread_own/pallas_call | solution.py:301
  65.4 7.6 %collective-permute-done.10.far = bf16[128,1408]{1,0:T(8,128)(2,1)S(1)} collective-permute-done((bf16[128,1408]{1,0:T(8,128)(2,1)S(1)}, bf16[128,1408]{1,0:T(8,128)(2,1)S(1)}, u32[]{:S(2)}, u32[]{:S(2)}) %collective-permute-start.10) | collective-permute-done | bytes 360480 | tf_op jit(solution)/shard_map/ppermute | solution.py:46
  73.0 1.3 %finish_out.1 = bf16[128,2048]{1,0:T(8,128)(2,1)} custom-call(bf16[128,2048]{1,0:T(8,128)(2,1)S(1)} %copy-done, bf16[128,640]{1,0:T(8,128)(2,1)S(1)} %bring_home.1.own, bf16[128,640]{1,0:T(8,128)(2,1)S(1)} %collective-permute-done.8.near, bf16[128,1408]{1,0:T(8,128)(2,1)S(1)} %collective-permute-done.10.far, bf16[128,2048]{1,0:T(8,128)(2,1)S(1)} %get-tuple-element.48.w_own, ...), custom_call_target="tpu_custom_call" | custom-call | flops 1000 | bytes 1000 | tf_op jit(solution)/shard_map/finish_out/pallas_call | solution.py:28
  74.3 3.6 %collective-permute-done.14.rest = bf16[128,1024]{1,0:T(8,128)(2,1)S(1)} collective-permute-done((bf16[128,1024]{1,0:T(8,128)(2,1)S(1)}, bf16[128,1024]{1,0:T(8,128)(2,1)S(1)}, u32[]{:S(2)}, u32[]{:S(2)}) %collective-permute-start.14) | collective-permute-done | bytes 262176 | tf_op jit(solution)/shard_map/ppermute | solution.py:46
  77.8 1.3 %finish_grad.1 = bf16[128,2048]{1,0:T(8,128)(2,1)} custom-call(bf16[128,2048]{1,0:T(8,128)(2,1)S(1)} %copy-done, bf16[128,2048]{1,0:T(8,128)(2,1)S(1)} %copy-done.7, bf16[1,2048]{1,0:T(2,128)(2,1)S(1)} %reshape.17.gain, f32[128,1]{1,0:T(8,128)S(1)} %get-tuple-element.54.inverse, bf16[128,640]{1,0:T(8,128)(2,1)S(1)} %bring_home.1.own, ...), custom_call_target="tpu_custom_call" | custom-call | flops 1000 | bytes 1000 | tf_op jit(solution)/shard_map/finish_grad/pallas_call | solution.py:28
  (44 shorter events, 6.2 us)
Async XLA Ops:
  0.6 17.4 %collective-permute-start.4 = (bf16[128,2048]{1,0:T(8,128)(2,1)}, bf16[128,2048]{1,0:T(8,128)(2,1)S(1)}, u32[]{:S(2)}, u32[]{:S(2)}) collective-permute-start(bf16[128,2048]{1,0:T(8,128)(2,1)} %cotangent.1), channel_id=1, source_target_pairs={{0,1},{1,0},{2,3},{3,2},{4,5},{5,4},{6,7},{7,6},{8,9},{9,8},{10,11... | collective-permute-start | bytes 1572872 | tf_op jit(solution)/shard_map/ppermute | solution.py:46
  1.1 16.9 %collective-permute-start = (bf16[128,2048]{1,0:T(8,128)(2,1)}, bf16[128,2048]{1,0:T(8,128)(2,1)S(1)}, u32[]{:S(2)}, u32[]{:S(2)}) collective-permute-start(bf16[128,2048]{1,0:T(8,128)(2,1)} %inputs.3), channel_id=1, source_target_pairs={{0,1},{1,0},{2,3},{3,2},{4,5},{5,4},{6,7},{7,6},{8,9},{9,8},{10,11... | collective-permute-start | bytes 1572872 | tf_op jit(solution)/shard_map/ppermute | solution.py:46
  1.2 26.7 %collective-permute-start.2 = (bf16[128,2048]{1,0:T(8,128)(2,1)}, bf16[128,2048]{1,0:T(8,128)(2,1)S(1)}, u32[]{:S(2)}, u32[]{:S(2)}) collective-permute-start(bf16[128,2048]{1,0:T(8,128)(2,1)} %cotangent.1), channel_id=1, source_target_pairs={{0,2},{1,3},{2,0},{3,1},{4,6},{5,7},{6,4},{7,5},{8,10},{9,11},{10,... | collective-permute-start | bytes 1572872 | tf_op jit(solution)/shard_map/ppermute | solution.py:46
  4.2 23.8 %collective-permute-start.1 = (bf16[128,2048]{1,0:T(8,128)(2,1)}, bf16[128,2048]{1,0:T(8,128)(2,1)S(1)}, u32[]{:S(2)}, u32[]{:S(2)}) collective-permute-start(bf16[128,2048]{1,0:T(8,128)(2,1)} %inputs.3), channel_id=1, source_target_pairs={{0,2},{1,3},{2,0},{3,1},{4,6},{5,7},{6,4},{7,5},{8,10},{9,11},{10,... | collective-permute-start | bytes 1572872 | tf_op jit(solution)/shard_map/ppermute | solution.py:46
  4.9 23.1 %collective-permute-start.3 = (bf16[1,2048]{1,0:T(2,128)(2,1)S(1)}, bf16[1,2048]{1,0:T(2,128)(2,1)S(1)}, u32[]{:S(2)}, u32[]{:S(2)}) collective-permute-start(bf16[1,2048]{1,0:T(2,128)(2,1)S(1)} %reshape.17.gain), channel_id=1, source_target_pairs={{0,2},{1,3},{2,0},{3,1},{4,6},{5,7},{6,4},{7,5},{8,10},{9,11},{10,... | collective-permute-start | bytes 12296 | tf_op jit(solution)/shard_map/ppermute | solution.py:46
  6.9 1.6 %copy-start.1 = (bf16[8192,128]{1,0:T(8,128)(2,1)S(1)}, bf16[8192,128]{1,0:T(8,128)(2,1)}, u32[]{:S(2)}) copy-start(bf16[8192,128]{1,0:T(8,128)(2,1)} %w_query.3) | copy-start | bytes 6291460
  8.5 1.6 %copy-start.2 = (bf16[8192,128]{1,0:T(8,128)(2,1)S(1)}, bf16[8192,128]{1,0:T(8,128)(2,1)}, u32[]{:S(2)}) copy-start(bf16[8192,128]{1,0:T(8,128)(2,1)} %w_key.3) | copy-start | bytes 6291460
  10.1 1.6 %copy-start.4 = (bf16[8192,128]{1,0:T(8,128)(2,1)S(1)}, bf16[8192,128]{1,0:T(8,128)(2,1)}, u32[]{:S(2)}) copy-start(bf16[8192,128]{1,0:T(8,128)(2,1)} %w_value.3) | copy-start | bytes 6291460
  11.7 1.6 %copy-start.6 = (bf16[128,8192]{1,0:T(8,128)(2,1)S(1)}, bf16[128,8192]{1,0:T(8,128)(2,1)}, u32[]{:S(2)}) copy-start(bf16[128,8192]{1,0:T(8,128)(2,1)} %w_output.1) | copy-start | bytes 6291460
  13.3 0.7 copy-start.8
  15.2 2.9 %copy-start = (bf16[128,2048]{1,0:T(8,128)(2,1)S(1)}, bf16[128,2048]{1,0:T(8,128)(2,1)}, u32[]{:S(2)}) copy-start(bf16[128,2048]{1,0:T(8,128)(2,1)} %inputs.3) | copy-start | bytes 1572868
  15.2 2.9 %copy-start.7 = (bf16[128,2048]{1,0:T(8,128)(2,1)S(1)}, bf16[128,2048]{1,0:T(8,128)(2,1)}, u32[]{:S(2)}) copy-start(bf16[128,2048]{1,0:T(8,128)(2,1)} %cotangent.1) | copy-start | bytes 1572868
  18.1 12.5 %copy-start.5 = (bf16[8192,128]{1,0:T(8,128)(2,1)S(1)}, bf16[8192,128]{1,0:T(8,128)(2,1)}, u32[]{:S(2)}) copy-start(bf16[8192,128]{1,0:T(8,128)(2,1)} %w_value.3) | copy-start | bytes 6291460
  19.2 11.4 %copy-start.3 = (bf16[8192,128]{1,0:T(8,128)(2,1)S(1)}, bf16[8192,128]{1,0:T(8,128)(2,1)}, u32[]{:S(2)}) copy-start(bf16[8192,128]{1,0:T(8,128)(2,1)} %w_key.3) | copy-start | bytes 6291460
  28.0 2.7 %collective-permute-start.6 = (bf16[128,2048]{1,0:T(8,128)(2,1)S(1)}, bf16[128,2048]{1,0:T(8,128)(2,1)S(1)}, u32[]{:S(2)}, u32[]{:S(2)}) collective-permute-start(bf16[128,2048]{1,0:T(8,128)(2,1)S(1)} %collective-permute-done.2.c2), channel_id=1, source_target_pairs={{0,1},{1,0},{2,3},{3,2},{4,5},{5,4},{6,7},{7,6},{8,9},{9,8},{10,11... | collective-permute-start | bytes 1572872 | tf_op jit(solution)/shard_map/ppermute | solution.py:46
  28.0 2.7 %collective-permute-start.5 = (bf16[128,2048]{1,0:T(8,128)(2,1)S(1)}, bf16[128,2048]{1,0:T(8,128)(2,1)S(1)}, u32[]{:S(2)}, u32[]{:S(2)}) collective-permute-start(bf16[128,2048]{1,0:T(8,128)(2,1)S(1)} %collective-permute-done.1.x2), channel_id=1, source_target_pairs={{0,1},{1,0},{2,3},{3,2},{4,5},{5,4},{6,7},{7,6},{8,9},{9,8},{10,11... | collective-permute-start | bytes 1572872 | tf_op jit(solution)/shard_map/ppermute | solution.py:46
  28.5 2.1 %collective-permute-start.7 = (bf16[2,2048]{1,0:T(2,128)(2,1)S(1)}, bf16[2,2048]{1,0:T(2,128)(2,1)S(1)}, u32[]{:S(2)}, u32[]{:S(2)}) collective-permute-start(bf16[2,2048]{1,0:T(2,128)(2,1)S(1)} %pad_maximum_fusion.gain_own), channel_id=1, source_target_pairs={{0,1},{1,0},{2,3},{3,2},{4,5},{5,4},{6,7},{7,6},{8,9},{9,8},{10,11... | collective-permute-start | bytes 24584 | tf_op jit(solution)/shard_map/ppermute | solution.py:46
  32.9 28.0 %collective-permute-start.9 = (bf16[384,4096]{1,0:T(8,128)(2,1)S(1)}, bf16[384,4096]{1,0:T(8,128)(2,1)S(1)}, u32[]{:S(2)}, u32[]{:S(2)}) collective-permute-start(bf16[384,4096]{1,0:T(8,128)(2,1)S(1)} %get-tuple-element.47), channel_id=1, source_target_pairs={{0,1},{1,0},{2,3},{3,2},{4,5},{5,4},{6,7},{7,6},{8,9},{9,8},{10,11... | collective-permute-start | bytes 9437192 | tf_op jit(solution)/shard_map/ppermute | solution.py:46
  33.1 27.2 %collective-permute-start.12 = (bf16[128,4096]{1,0:T(8,128)(2,1)S(1)}, bf16[128,4096]{1,0:T(8,128)(2,1)S(1)}, u32[]{:S(2)}, u32[]{:S(2)}) collective-permute-start(bf16[128,4096]{1,0:T(8,128)(2,1)S(1)} %get-tuple-element.52), channel_id=1, source_target_pairs={{0,2},{1,3},{2,0},{3,1},{4,6},{5,7},{6,4},{7,5},{8,10},{9,11},{10,... | collective-permute-start | bytes 3145736 | tf_op jit(solution)/shard_map/ppermute | solution.py:46
  58.9 1.5 %collective-permute-start.8 = (bf16[128,640]{1,0:T(8,128)(2,1)S(1)}, bf16[128,640]{1,0:T(8,128)(2,1)S(1)}, u32[]{:S(2)}, u32[]{:S(2)}) collective-permute-start(bf16[128,640]{1,0:T(8,128)(2,1)S(1)} %bring_home.1.own), channel_id=1, source_target_pairs={{0,1},{1,0},{2,3},{3,2},{4,5},{5,4},{6,7},{7,6},{8,9},{9,8},{10,11... | collective-permute-start | bytes 491528 | tf_op jit(solution)/shard_map/ppermute | solution.py:46
  60.4 5.1 %collective-permute-start.13 = (bf16[128,4096]{1,0:T(8,128)(2,1)S(1)}, bf16[128,4096]{1,0:T(8,128)(2,1)S(1)}, u32[]{:S(2)}, u32[]{:S(2)}) collective-permute-start(bf16[128,4096]{1,0:T(8,128)(2,1)S(1)} %collective-permute-done.12.w_far), channel_id=1, source_target_pairs={{0,1},{1,0},{2,3},{3,2},{4,5},{5,4},{6,7},{7,6},{8,9},{9,8},{10,11... | collective-permute-start | bytes 3145736 | tf_op jit(solution)/shard_map/ppermute | solution.py:46
  60.5 4.9 %collective-permute-start.11 = (bf16[128,2048]{1,0:T(8,128)(2,1)S(1)}, bf16[128,2048]{1,0:T(8,128)(2,1)S(1)}, u32[]{:S(2)}, u32[]{:S(2)}) collective-permute-start(bf16[128,2048]{1,0:T(8,128)(2,1)S(1)} %get-tuple-element.50), channel_id=1, source_target_pairs={{0,1},{1,0},{2,3},{3,2},{4,5},{5,4},{6,7},{7,6},{8,9},{9,8},{10,11... | collective-permute-start | bytes 1572872 | tf_op jit(solution)/shard_map/ppermute | solution.py:46
  61.7 11.3 %collective-permute-start.10 = (bf16[128,1408]{1,0:T(8,128)(2,1)S(1)}, bf16[128,1408]{1,0:T(8,128)(2,1)S(1)}, u32[]{:S(2)}, u32[]{:S(2)}) collective-permute-start(bf16[128,1408]{1,0:T(8,128)(2,1)S(1)} %spread_far.1), channel_id=1, source_target_pairs={{0,2},{1,3},{2,0},{3,1},{4,6},{5,7},{6,4},{7,5},{8,10},{9,11},{10,... | collective-permute-start | bytes 1081352 | tf_op jit(solution)/shard_map/ppermute | solution.py:46
  62.9 15.0 %collective-permute-start.14 = (bf16[128,1024]{1,0:T(8,128)(2,1)S(1)}, bf16[128,1024]{1,0:T(8,128)(2,1)S(1)}, u32[]{:S(2)}, u32[]{:S(2)}) collective-permute-start(bf16[128,1024]{1,0:T(8,128)(2,1)S(1)} %spread_rest.1), channel_id=1, source_target_pairs={{0,2},{1,3},{2,0},{3,1},{4,6},{5,7},{6,4},{7,5},{8,10},{9,11},{10,... | collective-permute-start | bytes 786440 | tf_op jit(solution)/shard_map/ppermute | solution.py:46
  (2 other events, 1.3 us)

commit v6 on v5

v6 whole, which is shorter than its diff:
```python
import math

import jax
import jax.numpy as jnp
from jax import lax
from jax.experimental import pallas as pl
from jax.experimental.pallas import tpu as pltpu
from jax.sharding import PartitionSpec as P

HEAD_DIM = 128
EPSILON = 1e-05
SCALING = 1.0 / math.sqrt(HEAD_DIM)
CONTRACT_LAST = (((1,), (1,)), ((), ()))
CONTRACT_FIRST = (((0,), (0,)), ((), ()))
VMEM_LIMIT = 12 * 1024 * 1024
VMEM = pl.BlockSpec(memory_space=pltpu.VMEM)
SMEM = pl.BlockSpec(memory_space=pltpu.SMEM)
TILE = 512
GAIN_ROWS = 16


def dot(left, right, dims=(((1,), (0,)), ((), ()))):
    return lax.dot_general(left, right, dims, preferred_element_type=jnp.float32)


def call(kernel, name, out_shape, operands, scratch=(), first=SMEM, rest=VMEM):
    single = not isinstance(out_shape, (list, tuple))
    shapes = [out_shape] if single else list(out_shape)
    results = pl.pallas_call(
        kernel,
        out_shape=shapes,
        in_specs=[first] + [rest] * (len(operands) - 1),
        out_specs=[VMEM] * len(shapes),
        scratch_shapes=list(scratch),
        compiler_params=pltpu.CompilerParams(vmem_limit_bytes=VMEM_LIMIT),
        cost_estimate=pl.CostEstimate(flops=1000, bytes_accessed=1000, transcendentals=0),
        name=name,
    )(*operands)
    return results[0] if single else results


def shape(dtype, *sizes):
    return jax.ShapeDtypeStruct(sizes, dtype)


def swap(array, mask, count):
    return lax.ppermute(array, "tensor", [(i, i ^ mask) for i in range(count)])


def block_start(order, slot, width):
    return pl.multiple_of(order[slot] * width, width)


def one_hot(places, rows):
    row = lax.broadcasted_iota(jnp.int32, (rows, places.shape[1]), 0)
    return jnp.where(places == row, 1.0, 0.0).astype(jnp.bfloat16)


def prepare_kernel(
    order,
    w_query,
    w_key,
    w_value,
    w_output,
    send,
    receive,
    segments,
    own_turned,
    near_first,
    near_second,
    near_third,
    near_last,
    output_turned,
    own_here,
    far_output,
    send_out,
    receive_out,
    segments_out,
):
    width = own_here.shape[1]
    far_left, far_right = far_output.at[:, :width], far_output.at[:, width:]
    for slot, target in ((0, own_here), (2, far_left), (3, far_right)):
        target[...] = w_output[:, pl.ds(block_start(order, slot, width), width)]
    for index, target in enumerate((near_first, near_second)):
        first = order[1] * width + index * (width // 2)
        columns = pl.ds(pl.multiple_of(first, width // 2), width // 2)
        target[3 * HEAD_DIM :, :] = w_output[:, columns]
    for start in range(0, w_output.shape[1], TILE):
        output_turned[start : start + TILE, :] = w_output[:, start : start + TILE].T
    for source, target in ((send, send_out), (receive, receive_out), (segments, segments_out)):
        target[...] = source[...]
    half = width // 2
    near_parts = ((near_first, near_second), (near_third, near_last))
    for part in range(2):
        own_first = block_start(order, 2 * part, width)
        near_start = block_start(order, 2 * part + 1, width)
        for start in range(0, width, TILE):
            there = near_parts[part][start // half]
            columns = slice(start % half, start % half + TILE)
            for place, weight in enumerate((w_query, w_key, w_value)):
                rows = slice(place * HEAD_DIM, (place + 1) * HEAD_DIM)
                own_columns = slice(part * width + start, part * width + start + TILE)
                own_turned[rows, own_columns] = weight[pl.ds(own_first + start, TILE), :].T
                there[rows, columns] = weight[pl.ds(near_start + start, TILE), :].T


def prepare(order, w_query, w_key, w_value, w_output, send, receive, segments, width):
    heads = w_query.shape[1]
    low = jnp.bfloat16
    return call(
        prepare_kernel,
        "prepare",
        [
            shape(low, 3 * heads, 2 * width),
            *[shape(low, 4 * heads, width // 2)] * 2,
            *[shape(low, 3 * heads, width // 2)] * 2,
            shape(low, w_output.shape[1], heads),
            shape(low, heads, width),
            shape(low, heads, 2 * width),
            shape(jnp.int32, *send.shape),
            shape(jnp.int32, *receive.shape),
            shape(jnp.int32, *segments.shape),
        ],
        (order, w_query, w_key, w_value, w_output, send, receive, segments),
    )


def sum_squares(block):
    wide = block.astype(jnp.float32)
    return jnp.sum(wide * wide, axis=-1, keepdims=True)


def pack_kernel(gain, inputs, out, sem):
    rows = inputs.shape[0]
    copy = pltpu.make_async_copy(inputs, out.at[pl.ds(0, rows), :], sem)
    copy.start()
    out[rows:, :] = jnp.broadcast_to(gain[...], (out.shape[0] - rows, out.shape[1]))
    copy.wait()


def pack(gain, inputs):
    rows, width = inputs.shape
    return call(
        pack_kernel,
        "pack",
        shape(jnp.bfloat16, rows + GAIN_ROWS, width),
        (gain, inputs),
        scratch=[pltpu.SemaphoreType.DMA],
        first=VMEM,
        rest=pl.BlockSpec(memory_space=pl.ANY),
    )


def begin_kernel(order, x0, x1, c0, c1, output_turned, squares, part):
    rows, width = c0.shape
    squares[...] = sum_squares(x0[:rows, :]) + sum_squares(x1[:rows, :])
    total = 0.0
    for index, block in enumerate((c0, c1)):
        here = pl.ds(block_start(order, index, width), width)
        total = total + dot(block[...], output_turned[here, :])
    part[...] = total


def begin(order, x0, x1, c0, c1, output_turned):
    rows = c0.shape[0]
    shapes = [shape(jnp.float32, rows, 1), shape(jnp.float32, rows, HEAD_DIM)]
    operands = (order, x0, x1, c0, c1, output_turned)
    return call(begin_kernel, "begin", shapes, operands)


def go_on_kernel(x2, squares_in, squares, upper, lower):
    rows = squares.shape[0]
    half = upper.shape[0]
    squares[...] = squares_in[...] + sum_squares(x2[:rows, :])
    upper[...] = x2[:half, :]
    lower[...] = x2[half:, :]


def go_on(x2, squares):
    rows, width = squares.shape[0], x2.shape[1]
    shapes = [
        shape(jnp.float32, rows, 1),
        shape(jnp.bfloat16, rows // 2, width),
        shape(jnp.bfloat16, rows // 2 + GAIN_ROWS, width),
    ]
    return call(go_on_kernel, "go_on", shapes, (x2, squares), first=VMEM)


def project_kernel(
    order,
    x0,
    x1,
    x2,
    upper,
    lower,
    w_query,
    w_key,
    w_value,
    squares,
    send,
    home,
    inverse,
    bucket,
    total,
):
    rows, width = home.shape[0], x0.shape[1]
    x3 = jnp.concatenate([upper[...], lower[...]], axis=0)
    mean = (squares[...] + sum_squares(x3[:rows, :])) / (4 * width)
    inverse_rms = lax.rsqrt(mean + EPSILON)
    inverse[...] = inverse_rms
    for index, block in enumerate((x0[...], x1[...], x2[...], x3)):
        scaled = block[:rows, :].astype(jnp.float32) * inverse_rms
        gain = block[rows : rows + 1, :].astype(jnp.float32)
        normed = (scaled * gain).astype(jnp.bfloat16)
        here = pl.ds(block_start(order, index, width), width)
        weights = jnp.concatenate([w_query[here, :], w_key[here, :], w_value[here, :]], axis=1)
        product = dot(normed, weights)
        total[...] = total[...] + product if index else product
    rounded = total[...].astype(jnp.bfloat16)
    home[...] = rounded
    bucket[...] = dot(one_hot(send[...], rows), rounded, CONTRACT_FIRST).astype(jnp.bfloat16)


def project(order, blocks, weights, squares, send):
    rows = squares.shape[0]
    columns = 3 * HEAD_DIM
    return call(
        project_kernel,
        "project",
        [
            shape(jnp.bfloat16, rows, columns),
            shape(jnp.float32, rows, 1),
            shape(jnp.bfloat16, send.shape[1], columns),
        ],
        (order, *blocks, *weights, squares, send),
        scratch=[pltpu.VMEM((rows, columns), jnp.float32)],
    )


def add_grad_kernel(order, c2, output_turned, part_in, part):
    width = c2.shape[1]
    here = pl.ds(block_start(order, 2, width), width)
    part[...] = part_in[...] + dot(c2[...], output_turned[here, :])


def add_grad(order, c2, output_turned, part):
    out = shape(jnp.float32, *part.shape)
    return call(add_grad_kernel, "add_grad", out, (order, c2, output_turned, part))


def fill_kernel(order, c3, output_turned, part, send, attended, bucket):
    rows, width = c3.shape
    here = pl.ds(block_start(order, 3, width), width)
    head_grad = (part[...] + dot(c3[...], output_turned[here, :])).astype(jnp.bfloat16)
    sorted_grad = dot(one_hot(send[...], rows), head_grad, CONTRACT_FIRST)
    bucket[:, :HEAD_DIM] = sorted_grad.astype(jnp.bfloat16)
    bucket[:, HEAD_DIM:] = attended[...]


def fill(order, c3, output_turned, part, send, attended):
    out = shape(jnp.bfloat16, send.shape[1], 2 * HEAD_DIM)
    return call(fill_kernel, "fill", out, (order, c3, output_turned, part, send, attended))


def attend_kernel(moved, receive, segments, softmax, qkv, back):
    place = one_hot(receive[...], moved.shape[0])
    rows = dot(place, moved[...], CONTRACT_FIRST).astype(jnp.bfloat16)
    qkv[...] = rows
    queries, key_rows, value_rows = (
        rows[:, index * HEAD_DIM : (index + 1) * HEAD_DIM] for index in range(3)
    )
    count = rows.shape[0]
    down = lax.broadcasted_iota(jnp.int32, (count, count), 0)
    across = lax.broadcasted_iota(jnp.int32, (count, count), 1)
    stays = segments[...]
    own_stay = jnp.sum(jnp.where(down == across, stays, 0), axis=1, keepdims=True)
    allowed = (own_stay == stays) & (across <= down)
    scores = jnp.where(allowed, dot(queries, key_rows, CONTRACT_LAST) * SCALING, -1e30)
    raised = jnp.exp(scores - jnp.max(scores, axis=-1, keepdims=True))
    softmax_out = raised / jnp.sum(raised, axis=-1, keepdims=True)
    softmax[...] = softmax_out
    attended = dot(softmax_out.astype(jnp.bfloat16), value_rows).astype(jnp.bfloat16)
    back[...] = dot(place, attended).astype(jnp.bfloat16)


def attend(moved, receive, segments):
    rows = receive.shape[1]
    shapes = [
        shape(jnp.float32, rows, rows),
        shape(jnp.bfloat16, rows, moved.shape[1]),
        shape(jnp.bfloat16, moved.shape[0], HEAD_DIM),
    ]
    return call(attend_kernel, "attend", shapes, (moved, receive, segments), first=VMEM)


def attend_back_kernel(softmax, qkv, moved, receive, back):
    place = one_hot(receive[...], moved.shape[0])
    head_grad = dot(place, moved[:, :HEAD_DIM], CONTRACT_FIRST).astype(jnp.bfloat16)
    queries, key_rows, value_rows = (
        qkv[:, index * HEAD_DIM : (index + 1) * HEAD_DIM] for index in range(3)
    )
    softmax_out = softmax[...]
    low_weights = softmax_out.astype(jnp.bfloat16)
    grad_value = dot(low_weights, head_grad, CONTRACT_FIRST).astype(jnp.bfloat16)
    grad_probs = dot(head_grad, value_rows, CONTRACT_LAST)
    inner = jnp.sum(softmax_out * grad_probs, axis=-1, keepdims=True)
    grad_scores = (softmax_out * (grad_probs - inner) * SCALING).astype(jnp.bfloat16)
    grad_query = dot(grad_scores, key_rows).astype(jnp.bfloat16)
    grad_key = dot(grad_scores, queries, CONTRACT_FIRST).astype(jnp.bfloat16)
    results = jnp.concatenate([grad_query, grad_key, grad_value], axis=1)
    back[...] = dot(place, results).astype(jnp.bfloat16)


def attend_back(softmax, qkv, moved, receive):
    out = shape(jnp.bfloat16, moved.shape[0], qkv.shape[1])
    return call(attend_back_kernel, "attend_back", out, (softmax, qkv, moved, receive), first=VMEM)


def write_parts(value, out):
    out[...] = jnp.zeros_like(out)
    for place in range(3):
        low = value.astype(jnp.bfloat16)
        out[:, place : place + 1] = low
        value = value - low.astype(jnp.float32)


def read_parts(parts):
    return sum(parts[:, place : place + 1].astype(jnp.float32) for place in (2, 1, 0))


def bring_home_kernel(moved, moved_attended, send, home, results):
    chosen = one_hot(send[...], results.shape[0])
    grads = dot(chosen, moved[...])
    attended = dot(chosen, moved_attended[:, HEAD_DIM:])
    results[:, : 3 * HEAD_DIM] = grads.astype(jnp.bfloat16)
    results[:, 3 * HEAD_DIM : 4 * HEAD_DIM] = attended.astype(jnp.bfloat16)
    product = grads * home[...].astype(jnp.float32)
    row_dot = jnp.sum(product, axis=-1, keepdims=True)
    write_parts(row_dot, results.at[:, 4 * HEAD_DIM :])


def bring_home(moved, moved_attended, send, home):
    out = shape(jnp.bfloat16, home.shape[0], 5 * HEAD_DIM)
    operands = (moved, moved_attended, send, home)
    return call(bring_home_kernel, "bring_home", out, operands, first=VMEM)


def spread_into(own, near, weights, near_weights, first, out, place, held, total, sems):
    half = near_weights[0].shape[1]
    copies = [
        pltpu.make_async_copy(
            part.at[pl.ds(0, held.shape[0]), :],
            held.at[:, pl.ds(index * half, half)],
            sems.at[index],
        )
        for index, part in enumerate(near_weights)
    ]
    for copy in copies:
        copy.start()
    span = half * len(copies)
    own_grads = own[:, : 3 * HEAD_DIM]
    near_grads = near[:, : 3 * HEAD_DIM]
    for start in range(0, span, TILE):
        columns = slice(first + start, first + start + TILE)
        total[:, start : start + TILE] = dot(own_grads, weights[:, columns])
    for start in range(0, span, TILE):
        if start % half == 0:
            copies[start // half].wait()
        tile = slice(start, start + TILE)
        result = total[:, tile] + dot(near_grads, held[:, tile])
        out[:, place + start : place + start + TILE] = result.astype(out.dtype)


def spread_far_kernel(own, near, weights, near_weights, out, *scratch):
    width = weights.shape[1] // 2
    write_parts(
        read_parts(own[:, 4 * HEAD_DIM :]) + read_parts(near[:, 4 * HEAD_DIM :]),
        out.at[:, :HEAD_DIM],
    )
    attended = slice(3 * HEAD_DIM, 4 * HEAD_DIM)
    out[:, HEAD_DIM : 2 * HEAD_DIM] = own[:, attended]
    out[:, 2 * HEAD_DIM : 3 * HEAD_DIM] = near[:, attended]
    spread_into(own, near, weights, (near_weights,), width, out, 3 * HEAD_DIM, *scratch)


def spread_rest_kernel(own, near, weights, near_weights, out, *scratch):
    width = weights.shape[1] // 2
    first = width + width // 2
    spread_into(own, near, weights, (near_weights,), first, out, 0, *scratch)


def spread_own_kernel(own, near, weights, near_left, near_right, out, *scratch):
    spread_into(own, near, weights, (near_left, near_right), 0, out, 0, *scratch)


def spread(kernel, name, out, operands):
    rows, depth = operands[0].shape[0], operands[2].shape[0]
    parts = len(operands) - 3
    span = parts * operands[3].shape[1]
    return pl.pallas_call(
        kernel,
        out_shape=out,
        in_specs=[VMEM] * 3 + [pl.BlockSpec(memory_space=pl.ANY)] * parts,
        out_specs=VMEM,
        scratch_shapes=[
            pltpu.VMEM((depth, span), jnp.bfloat16),
            pltpu.VMEM((rows, span), jnp.float32),
            pltpu.SemaphoreType.DMA((parts,)),
        ],
        compiler_params=pltpu.CompilerParams(vmem_limit_bytes=VMEM_LIMIT),
        cost_estimate=pl.CostEstimate(flops=1000, bytes_accessed=1000, transcendentals=0),
        name=name,
    )(*operands)


def split_kernel(far_output, *pieces):
    width = far_output.shape[1] // 2
    span = width // len(pieces)
    for index, piece in enumerate(pieces):
        piece[...] = far_output[:, width + index * span : width + (index + 1) * span]


def split(far_output):
    heads, width = far_output.shape
    pieces = [shape(jnp.bfloat16, heads, width // 8)] * 4
    return call(split_kernel, "split", pieces, (far_output,), first=VMEM)


def finish_out_kernel(inputs, own, near, far, w_own, w_left, w_right, w_far, *rest):
    *w_last, out = rest
    width = inputs.shape[1]
    half = width // 2
    attended = slice(3 * HEAD_DIM, 4 * HEAD_DIM)
    rows = jnp.concatenate(
        [own[:, attended], near[:, attended], far[:, HEAD_DIM : 3 * HEAD_DIM]], axis=1
    )
    for start in range(0, width, TILE):
        tile = slice(start, start + TILE)
        w_near = (w_left, w_right)[start // half]
        w_near = w_near[3 * HEAD_DIM :, start % half : start % half + TILE]
        stacked = [w_own[:, tile], w_near, w_far[:, tile], w_last[start // TILE][...]]
        total = dot(rows, jnp.concatenate(stacked, axis=0))
        out[:, tile] = (inputs[:, tile].astype(jnp.float32) + total).astype(jnp.bfloat16)


def finish_grad_kernel(inputs, cotangent, gain, inverse, own, near, grad_own, far, rest, out):
    width = inputs.shape[1]
    row_dot = read_parts(own[:, 4 * HEAD_DIM :]) + read_parts(near[:, 4 * HEAD_DIM :])
    mean_dot = (row_dot + read_parts(far[:, :HEAD_DIM])) / (4 * width)
    inverse_rms = inverse[...]
    for start in range(0, width, TILE):
        tile = slice(start, start + TILE)
        if start < width // 2:
            got = far[:, 3 * HEAD_DIM + start : 3 * HEAD_DIM + start + TILE]
        else:
            got = rest[:, start - width // 2 : start - width // 2 + TILE]
        grad_normed = grad_own[:, tile] + got.astype(jnp.float32)
        grad_hat = grad_normed * gain[:, tile].astype(jnp.float32)
        scaled = inputs[:, tile].astype(jnp.float32) * inverse_rms
        change = inverse_rms * (grad_hat - scaled * mean_dot)
        out[:, tile] = (cotangent[:, tile].astype(jnp.float32) + change).astype(jnp.bfloat16)


def move(bucket):
    return lax.all_to_all(bucket, "dp", split_axis=0, concat_axis=0, tiled=True)


def after(array, *others):
    return lax.optimization_barrier((array, *others))[0]


def on_device(
    inputs,
    cotangent,
    norm_gain,
    w_query,
    w_key,
    w_value,
    w_output,
    send_rows,
    receive_slots,
    owner_segments,
):
    rows, width = inputs.shape
    tensor = lax.axis_size("tensor")
    low = jnp.bfloat16
    order = lax.axis_index("tensor").astype(jnp.int32) ^ jnp.arange(4, dtype=jnp.int32)
    gain = norm_gain.reshape(1, width)

    packed = pack(gain, inputs)
    x2 = swap(packed, 2, tensor)
    c2 = swap(cotangent, 2, tensor)
    x1 = swap(packed, 1, tensor)
    c1 = swap(cotangent, 1, tensor)
    weights = (w_query, w_key, w_value)
    own_turned, *prepared = prepare(
        order,
        *weights,
        w_output,
        send_rows,
        receive_slots.reshape(1, rows),
        owner_segments.reshape(1, rows),
        width,
    )
    near_turned, prepared = prepared[:4], prepared[4:]
    output_turned, own_here, far_output, send, receive, segments = prepared
    squares, part = begin(order, packed, x1, cotangent, c1, output_turned)

    x2, squares, part = lax.optimization_barrier((x2, squares, part))
    squares, upper, lower = go_on(x2, squares)
    home, inverse_rms, bucket = project(
        order,
        (packed, x1, x2, swap(upper, 1, tensor), swap(lower, 1, tensor)),
        weights,
        squares,
        send,
    )
    softmax, qkv, attended = attend(move(bucket), receive, segments)

    c2 = after(c2, softmax)
    c3 = swap(c2, 1, tensor)
    part = add_grad(order, c2, output_turned, part)
    c3, part = lax.optimization_barrier((c3, part))
    moved = move(fill(order, c3, output_turned, part, send, attended))
    far_output = swap(after(far_output, c3), 2, tensor)
    near_turned = [swap(after(piece, c3), 1, tensor) for piece in near_turned]
    back = attend_back(softmax, qkv, moved, receive)
    back, *near_turned = lax.optimization_barrier((back, *near_turned))
    own = bring_home(move(back), moved, send, home)

    near = swap(own, 1, tensor)
    half = width // 2
    far_shape = shape(low, rows, 3 * HEAD_DIM + half)
    rest_shape = shape(low, rows, half)
    own_shape = shape(jnp.float32, rows, width)
    sides = (own, near, own_turned, near_turned[2])
    far_part = spread(spread_far_kernel, "spread_far", far_shape, sides)
    far = swap(far_part, 2, tensor)
    sides = (after(own, far_part), near, own_turned, near_turned[3])
    rest_part = spread(spread_rest_kernel, "spread_rest", rest_shape, sides)
    rest = swap(rest_part, 2, tensor)
    sides = (after(own, rest_part), near, own_turned, *near_turned[:2])
    grad_own = spread(spread_own_kernel, "spread_own", own_shape, sides)
    last = [swap(piece, 1, tensor) for piece in split(after(far_output, grad_own))]
    layer_out = call(
        finish_out_kernel,
        "finish_out",
        shape(low, rows, width),
        (inputs, own, near, far, own_here, *near_turned[:2], far_output, *last),
        first=VMEM,
    )
    rest = after(rest, layer_out)
    input_grad = call(
        finish_grad_kernel,
        "finish_grad",
        shape(low, rows, width),
        (inputs, cotangent, gain, inverse_rms, own, near, grad_own, far, rest),
        first=VMEM,
    )
    return (layer_out, input_grad)


def solution(mesh):
    return jax.shard_map(
        on_device,
        mesh=mesh,
        in_specs=(
            P("dp", "tensor"),
            P("dp", "tensor"),
            P("tensor"),
            P(None, "tensor"),
            P(None, "tensor"),
            P(None, "tensor"),
            P("tensor", None),
            P("dp", None),
            P("dp"),
            P("dp"),
        ),
        out_specs=(P("dp", "tensor"), P("dp", "tensor")),
        check_vma=False,
    )
```

time: 79.5 us -> 83.6 us (1.052)
  blocking collectives: 22.7 us -> 31.9 us
  waiting for transfers between devices: 22.4 us -> 15.6 us
  Pallas kernels: 13.3 us -> 14.9 us
  starting transfers between devices: 10.9 us -> 9.7 us
  local copies, waits for them, and re-layouts: 9.04 us -> 10.1 us
    all_to_all x2 -> x3, blocking collectives: 22.7 us -> 31.9 us  [move(): return lax.all_to_all(bucket, 'dp', split_axis=0, concat_axis=0, tiled=True)]
    ppermute x15 -> x19, waiting for transfers between devices: 22.4 us -> 15.6 us  [swap(): return lax.ppermute(array, 'tensor', [(i, i ^ mask) for i in range(count)])]
    pallas_call x8 -> x13, Pallas kernels: 10.9 us -> 12.5 us  [call(): pl.pallas_call(kernel, out_shape=shapes, in_specs=[first] + [rest] * (len...]
    ppermute x15 -> x19, starting transfers between devices: 10.9 us -> 9.7 us  [swap(): return lax.ppermute(array, 'tensor', [(i, i ^ mask) for i in range(count)])]
    unnamed x22 -> x26, local copies, waits for them, and re-layouts: 8.34 us -> 9.39 us
  transfers between devices with their start and end apart: 15 -> 19, of which waited for: 5 -> 9; matrix products, arithmetic and copies ran while one was open for 1% -> 0% of each run, Pallas kernels for 12% -> 16%
where the time goes in v6:
time: 83.6 us; the launch traced here: 83.1 us
  blocking collectives  31.9 us (38%)
  waiting for transfers between devices  15.6 us (19%)
  Pallas kernels  14.9 us (18%)
  local copies, waits for them, and re-layouts  10.1 us (12%)
  starting transfers between devices  9.7 us (12%)
  between operations  0.87 us (1%)
    all_to_all x3, blocking collectives, move(): return lax.all_to_all(bucket, 'dp', split_axis=0, concat_axis=0, tiled=True)  31.9 us
    ppermute x19, waiting for transfers between devices, swap(): return lax.ppermute(array, 'tensor', [(i, i ^ mask) for i in range(count)])  15.6 us
    pallas_call x13, Pallas kernels, call(): pl.pallas_call(kernel, out_shape=shapes, in_specs=[first] + [rest] * (len...  12.5 us
    ppermute x19, starting transfers between devices, swap(): return lax.ppermute(array, 'tensor', [(i, i ^ mask) for i in range(count)])  9.7 us
    unnamed x26, local copies, waits for them, and re-layouts  9.39 us
    pallas_call x3, Pallas kernels, spread(): pl.pallas_call(kernel, out_shape=out, in_specs=[VMEM] * 3 + [pl.BlockSpec...  2.45 us
  transfers between devices with their start and end apart: 19, of which 9 were waited for; matrix products, arithmetic and copies ran while one was open for 0% of the time, Pallas kernels for 16%

profile of v6, /device:TPU:0, one launch (start us, length us, event | category | flops | bytes accessed | tf_op | source)
XLA Modules:
  0.0 83.1 jit_solution(3677172635993733839)
XLA Ops:
  1.3 1.0 %copy-done.6 = bf16[128,2048]{1,0:T(8,128)(2,1)S(1)} copy-done((bf16[128,2048]{1,0:T(8,128)(2,1)S(1)}, bf16[128,2048]{1,0:T(8,128)(2,1)}, u32[]{:S(2)}) %copy-start.6) | copy-done | bytes 524312
  3.0 2.6 %collective-permute-start.1 = (bf16[144,2048]{1,0:T(8,128)(2,1)S(1)}, bf16[144,2048]{1,0:T(8,128)(2,1)S(1)}, u32[]{:S(2)}, u32[]{:S(2)}) collective-permute-start(bf16[144,2048]{1,0:T(8,128)(2,1)S(1)} %pack.1.x0), channel_id=1, source_target_pairs={{0,2},{1,3},{2,0},{3,1},{4,6},{5,7},{6,4},{7,5},{8,10},{9,11},{10,... | collective-permute-start | bytes 1769480 | tf_op jit(solution)/shard_map/ppermute | solution.py:47
  6.0 1.6 %copy-done = bf16[8192,128]{1,0:T(8,128)(2,1)S(1)} copy-done((bf16[8192,128]{1,0:T(8,128)(2,1)S(1)}, bf16[8192,128]{1,0:T(8,128)(2,1)}, u32[]{:S(2)}) %copy-start) | copy-done | bytes 2097176
  7.6 1.6 %copy-done.2 = bf16[8192,128]{1,0:T(8,128)(2,1)S(1)} copy-done((bf16[8192,128]{1,0:T(8,128)(2,1)S(1)}, bf16[8192,128]{1,0:T(8,128)(2,1)}, u32[]{:S(2)}) %copy-start.2) | copy-done | bytes 2097176
  9.2 1.6 %copy-done.4 = bf16[8192,128]{1,0:T(8,128)(2,1)S(1)} copy-done((bf16[8192,128]{1,0:T(8,128)(2,1)S(1)}, bf16[8192,128]{1,0:T(8,128)(2,1)}, u32[]{:S(2)}) %copy-start.4) | copy-done | bytes 2097176
  10.8 1.6 %copy-done.8 = bf16[128,8192]{1,0:T(8,128)(2,1)S(1)} copy-done((bf16[128,8192]{1,0:T(8,128)(2,1)S(1)}, bf16[128,8192]{1,0:T(8,128)(2,1)}, u32[]{:S(2)}) %copy-start.8) | copy-done | bytes 2097176
  14.3 2.8 %prepare.1 = (bf16[384,4096]{1,0:T(8,128)(2,1)S(1)}, bf16[512,1024]{1,0:T(8,128)(2,1)S(1)}, bf16[512,1024]{1,0:T(8,128)(2,1)S(1)}, bf16[384,1024]{1,0:T(8,128)(2...) custom-call(s32[4]{0:T(128)S(1)} %iota_xor_fusion.order, ...), custom_call_target="tpu_custom_call" | custom-call | flops 1000 | bytes 1000 | tf_op jit(solution)/shard_map/prepare/pallas_call | solution.py:29
  17.2 1.1 %begin.1 = (f32[128,1]{1,0:T(8,128)S(1)}, f32[128,128]{1,0:T(8,128)S(1)}) custom-call(s32[4]{0:T(128)S(1)} %iota_xor_fusion.order, bf16[144,2048]{1,0:T(8,128)(2,1)S(1)} %pack.1.x0, bf16[144,2048]{1,0:T(8,128)(2,1)S(1)} %collective-permute-done.x1, bf16[128,2048]{1,0:T(8,128)(2,1)S(1)} %copy-done.9, bf16[128,2048]{1,0:T(8,128)(2,1)S(1)} %collective-permute-done.2.c1, ...), custom_call_target="tpu_custom_call" | custom-call | flops 1000 | bytes 1000 | tf_op jit(solution)/shard_map/begin/pallas_call | solution.py:29
  18.3 1.4 %collective-permute-done.1.x2 = bf16[144,2048]{1,0:T(8,128)(2,1)S(1)} collective-permute-done((bf16[144,2048]{1,0:T(8,128)(2,1)S(1)}, bf16[144,2048]{1,0:T(8,128)(2,1)S(1)}, u32[]{:S(2)}, u32[]{:S(2)}) %collective-permute-start.1) | collective-permute-done | bytes 589856 | tf_op jit(solution)/shard_map/ppermute | solution.py:47
  20.5 1.5 %collective-permute-done.3.upper = bf16[64,2048]{1,0:T(8,128)(2,1)S(1)} collective-permute-done((bf16[64,2048]{1,0:T(8,128)(2,1)S(1)}, bf16[64,2048]{1,0:T(8,128)(2,1)S(1)}, u32[]{:S(2)}, u32[]{:S(2)}) %collective-permute-start.3) | collective-permute-done | bytes 262176 | tf_op jit(solution)/shard_map/ppermute | solution.py:47
  22.0 2.2 %project.1 = (bf16[128,384]{1,0:T(8,128)(2,1)S(1)}, f32[128,1]{1,0:T(8,128)S(1)}, bf16[128,384]{1,0:T(8,128)(2,1)S(1)}) custom-call(s32[4]{0:T(128)S(1)} %iota_xor_fusion.order, bf16[144,2048]{1,0:T(8,128)(2,1)S(1)} %pack.1.x0, bf16[144,2048]{1,0:T(8,128)(2,1)S(1)} %collective-permute-done.x1, bf16[144,2048]{1,0:T(8,128)(2,1)S(1)} %collective-permute-done.1.x2, ...), custom_call_target="tpu_custom_call" | custom-call | flops 1000 | bytes 1000 | tf_op jit(solution)/shard_map/project/pallas_call | solution.py:29
  24.2 13.1 %all_to_all.33 = bf16[8,16,384]{2,1,0:T(8,128)(2,1)S(1)} all-to-all(bf16[8,16,384]{2,1,0:T(8,128)(2,1)S(1)} %bitcast.14), channel_id=1, replica_groups=mesh['dp'=8,'tensor'=4] {'dp'}, dimensions={0} | all-to-all | bytes 196608 | tf_op jit(solution)/shard_map/all_to_all | solution.py:465
  39.1 1.1 %collective-permute-done.6.c3 = bf16[128,2048]{1,0:T(8,128)(2,1)S(1)} collective-permute-done((bf16[128,2048]{1,0:T(8,128)(2,1)S(1)}, bf16[128,2048]{1,0:T(8,128)(2,1)S(1)}, u32[]{:S(2)}, u32[]{:S(2)}) %collective-permute-start.6) | collective-permute-done | bytes 524320 | tf_op jit(solution)/shard_map/ppermute | solution.py:47
  41.2 1.5 %collective-permute-start.13 = (bf16[128,4096]{1,0:T(8,128)(2,1)S(1)}, bf16[128,4096]{1,0:T(8,128)(2,1)S(1)}, u32[]{:S(2)}, u32[]{:S(2)}) collective-permute-start(bf16[128,4096]{1,0:T(8,128)(2,1)S(1)} %get-tuple-element.83), channel_id=1, source_target_pairs={{0,2},{1,3},{2,0},{3,1},{4,6},{5,7},{6,4},{7,5},{8,10},{9,11},{10,... | collective-permute-start | bytes 3145736 | tf_op jit(solution)/shard_map/ppermute | solution.py:47
  42.7 1.0 %fill.1 = bf16[128,256]{1,0:T(8,128)(2,1)S(1)} custom-call(s32[4]{0:T(128)S(1)} %iota_xor_fusion.order, bf16[128,2048]{1,0:T(8,128)(2,1)S(1)} %collective-permute-done.6.c3, bf16[8192,128]{1,0:T(8,128)(2,1)S(1)} %get-tuple-element.48.output_turned, f32[128,128]{1,0:T(8,128)S(1)} %add_grad.1.part, s32[1,128]{1,0:T(1,128)S(1)} %get-tuple-element.56.send, ...), custom_call_target="tpu_custom_call" | custom-call | flops 1000 | bytes 1000 | tf_op jit(solution)/shard_map/fill/pallas_call | solution.py:29
  43.6 9.3 %all_to_all.34 = bf16[8,16,256]{2,1,0:T(8,128)(2,1)S(1)} all-to-all(bf16[8,16,256]{2,1,0:T(8,128)(2,1)S(1)} %bitcast.13), channel_id=1, replica_groups=mesh['dp'=8,'tensor'=4] {'dp'}, dimensions={0} | all-to-all | bytes 131072 | tf_op jit(solution)/shard_map/all_to_all | solution.py:465
  53.7 9.5 %all_to_all.35 = bf16[8,16,384]{2,1,0:T(8,128)(2,1)S(1)} all-to-all(bf16[8,16,384]{2,1,0:T(8,128)(2,1)S(1)} %bitcast.11), channel_id=1, replica_groups=mesh['dp'=8,'tensor'=4] {'dp'}, dimensions={0} | all-to-all | bytes 196608 | tf_op jit(solution)/shard_map/all_to_all | solution.py:465
  63.5 1.4 %collective-permute-done.11.near = bf16[128,640]{1,0:T(8,128)(2,1)S(1)} collective-permute-done((bf16[128,640]{1,0:T(8,128)(2,1)S(1)}, bf16[128,640]{1,0:T(8,128)(2,1)S(1)}, u32[]{:S(2)}, u32[]{:S(2)}) %collective-permute-start.11) | collective-permute-done | bytes 163872 | tf_op jit(solution)/shard_map/ppermute | solution.py:47
  66.9 1.1 %spread_own.1.grad_own = f32[128,2048]{1,0:T(8,128)S(1)} custom-call(bf16[128,640]{1,0:T(8,128)(2,1)S(1)} %bring_home.1.own, bf16[128,640]{1,0:T(8,128)(2,1)S(1)} %collective-permute-done.11.near, bf16[384,4096]{1,0:T(8,128)(2,1)S(1)} %get-tuple-element.77.weights, bf16[512,1024]{1,0:T(8,128)(2,1)S(1)} %collective-permute-done.7.near_left.w_left, ...), custom_call_target="tpu_custom_call" | custom-call | flops 1000 | bytes 1000 | tf_op jit(solution)/shard_map/spread_own/pallas_call | solution.py:400
  68.1 1.6 %collective-permute-start.18 = (bf16[128,1024]{1,0:T(8,128)(2,1)S(1)}, bf16[128,1024]{1,0:T(8,128)(2,1)S(1)}, u32[]{:S(2)}, u32[]{:S(2)}) collective-permute-start(bf16[128,1024]{1,0:T(8,128)(2,1)S(1)} %spread_rest.1), channel_id=1, source_target_pairs={{0,2},{1,3},{2,0},{3,1},{4,6},{5,7},{6,4},{7,5},{8,10},{9,11},{10,... | collective-permute-start | bytes 786440 | tf_op jit(solution)/shard_map/ppermute | solution.py:47
  71.6 5.4 %collective-permute-done.12.far = bf16[128,1408]{1,0:T(8,128)(2,1)S(1)} collective-permute-done((bf16[128,1408]{1,0:T(8,128)(2,1)S(1)}, bf16[128,1408]{1,0:T(8,128)(2,1)S(1)}, u32[]{:S(2)}, u32[]{:S(2)}) %collective-permute-start.12) | collective-permute-done | bytes 360480 | tf_op jit(solution)/shard_map/ppermute | solution.py:47
  77.0 1.2 %finish_out.1 = bf16[128,2048]{1,0:T(8,128)(2,1)} custom-call(bf16[128,2048]{1,0:T(8,128)(2,1)S(1)} %copy-done.7, bf16[128,640]{1,0:T(8,128)(2,1)S(1)} %bring_home.1.own, bf16[128,640]{1,0:T(8,128)(2,1)S(1)} %collective-permute-done.11.near, bf16[128,1408]{1,0:T(8,128)(2,1)S(1)} %collective-permute-done.12.far, ...), custom_call_target="tpu_custom_call" | custom-call | flops 1000 | bytes 1000 | tf_op jit(solution)/shard_map/finish_out/pallas_call | solution.py:29
  78.3 3.6 %collective-permute-done.18.rest = bf16[128,1024]{1,0:T(8,128)(2,1)S(1)} collective-permute-done((bf16[128,1024]{1,0:T(8,128)(2,1)S(1)}, bf16[128,1024]{1,0:T(8,128)(2,1)S(1)}, u32[]{:S(2)}, u32[]{:S(2)}) %collective-permute-start.18) | collective-permute-done | bytes 262176 | tf_op jit(solution)/shard_map/ppermute | solution.py:47
  81.8 1.3 %finish_grad.1 = bf16[128,2048]{1,0:T(8,128)(2,1)} custom-call(bf16[128,2048]{1,0:T(8,128)(2,1)S(1)} %copy-done.7, bf16[128,2048]{1,0:T(8,128)(2,1)S(1)} %copy-done.9, bf16[1,2048]{1,0:T(2,128)(2,1)S(1)} %reshape.19.gain, f32[128,1]{1,0:T(8,128)S(1)} %get-tuple-element.92.inverse, bf16[128,640]{1,0:T(8,128)(2,1)S(1)} %bring_home.1.own, ...), custom_call_target="tpu_custom_call" | custom-call | flops 1000 | bytes 1000 | tf_op jit(solution)/shard_map/finish_grad/pallas_call | solution.py:29
  (61 shorter events, 12.1 us)
Async XLA Ops:
  2.4 14.7 %collective-permute-start = (bf16[144,2048]{1,0:T(8,128)(2,1)S(1)}, bf16[144,2048]{1,0:T(8,128)(2,1)S(1)}, u32[]{:S(2)}, u32[]{:S(2)}) collective-permute-start(bf16[144,2048]{1,0:T(8,128)(2,1)S(1)} %pack.1.x0), channel_id=1, source_target_pairs={{0,1},{1,0},{2,3},{3,2},{4,5},{5,4},{6,7},{7,6},{8,9},{9,8},{10,11... | collective-permute-start | bytes 1769480 | tf_op jit(solution)/shard_map/ppermute | solution.py:47
  3.0 16.8 %collective-permute-start.1 = (bf16[144,2048]{1,0:T(8,128)(2,1)S(1)}, bf16[144,2048]{1,0:T(8,128)(2,1)S(1)}, u32[]{:S(2)}, u32[]{:S(2)}) collective-permute-start(bf16[144,2048]{1,0:T(8,128)(2,1)S(1)} %pack.1.x0), channel_id=1, source_target_pairs={{0,2},{1,3},{2,0},{3,1},{4,6},{5,7},{6,4},{7,5},{8,10},{9,11},{10,... | collective-permute-start | bytes 1769480 | tf_op jit(solution)/shard_map/ppermute | solution.py:47
  5.5 11.6 %collective-permute-start.2 = (bf16[128,2048]{1,0:T(8,128)(2,1)}, bf16[128,2048]{1,0:T(8,128)(2,1)S(1)}, u32[]{:S(2)}, u32[]{:S(2)}) collective-permute-start(bf16[128,2048]{1,0:T(8,128)(2,1)} %cotangent.1), channel_id=1, source_target_pairs={{0,1},{1,0},{2,3},{3,2},{4,5},{5,4},{6,7},{7,6},{8,9},{9,8},{10,11... | collective-permute-start | bytes 1572872 | tf_op jit(solution)/shard_map/ppermute | solution.py:47
  5.7 32.4 %collective-permute-start.5 = (bf16[128,2048]{1,0:T(8,128)(2,1)}, bf16[128,2048]{1,0:T(8,128)(2,1)S(1)}, u32[]{:S(2)}, u32[]{:S(2)}) collective-permute-start(bf16[128,2048]{1,0:T(8,128)(2,1)} %cotangent.1), channel_id=1, source_target_pairs={{0,2},{1,3},{2,0},{3,1},{4,6},{5,7},{6,4},{7,5},{8,10},{9,11},{10,... | collective-permute-start | bytes 1572872 | tf_op jit(solution)/shard_map/ppermute | solution.py:47
  14.3 2.9 %copy-start.9 = (bf16[128,2048]{1,0:T(8,128)(2,1)S(1)}, bf16[128,2048]{1,0:T(8,128)(2,1)}, u32[]{:S(2)}) copy-start(bf16[128,2048]{1,0:T(8,128)(2,1)} %cotangent.1) | copy-start | bytes 1572868
  14.3 7.6 %copy-start.5 = (bf16[8192,128]{1,0:T(8,128)(2,1)S(1)}, bf16[8192,128]{1,0:T(8,128)(2,1)}, u32[]{:S(2)}) copy-start(bf16[8192,128]{1,0:T(8,128)(2,1)} %w_value.3) | copy-start | bytes 6291460
  17.2 4.8 %copy-start.1 = (bf16[8192,128]{1,0:T(8,128)(2,1)S(1)}, bf16[8192,128]{1,0:T(8,128)(2,1)}, u32[]{:S(2)}) copy-start(bf16[8192,128]{1,0:T(8,128)(2,1)} %w_query.3) | copy-start | bytes 6291460
  17.2 4.8 %copy-start.3 = (bf16[8192,128]{1,0:T(8,128)(2,1)S(1)}, bf16[8192,128]{1,0:T(8,128)(2,1)}, u32[]{:S(2)}) copy-start(bf16[8192,128]{1,0:T(8,128)(2,1)} %w_key.3) | copy-start | bytes 6291460
  19.9 2.0 %collective-permute-start.4 = (bf16[80,2048]{1,0:T(8,128)(2,1)S(1)}, bf16[80,2048]{1,0:T(8,128)(2,1)S(1)}, u32[]{:S(2)}, u32[]{:S(2)}) collective-permute-start(bf16[80,2048]{1,0:T(8,128)(2,1)S(1)} %get-tuple-element.54), channel_id=1, source_target_pairs={{0,1},{1,0},{2,3},{3,2},{4,5},{5,4},{6,7},{7,6},{8,9},{9,8},{10,11... | collective-permute-start | bytes 983048 | tf_op jit(solution)/shard_map/ppermute | solution.py:47
  20.0 2.0 %collective-permute-start.3 = (bf16[64,2048]{1,0:T(8,128)(2,1)S(1)}, bf16[64,2048]{1,0:T(8,128)(2,1)S(1)}, u32[]{:S(2)}, u32[]{:S(2)}) collective-permute-start(bf16[64,2048]{1,0:T(8,128)(2,1)S(1)} %get-tuple-element.53), channel_id=1, source_target_pairs={{0,1},{1,0},{2,3},{3,2},{4,5},{5,4},{6,7},{7,6},{8,9},{9,8},{10,11... | collective-permute-start | bytes 786440 | tf_op jit(solution)/shard_map/ppermute | solution.py:47
  38.2 2.0 %collective-permute-start.6 = (bf16[128,2048]{1,0:T(8,128)(2,1)S(1)}, bf16[128,2048]{1,0:T(8,128)(2,1)S(1)}, u32[]{:S(2)}, u32[]{:S(2)}) collective-permute-start(bf16[128,2048]{1,0:T(8,128)(2,1)S(1)} %collective-permute-done.5.c2), channel_id=1, source_target_pairs={{0,1},{1,0},{2,3},{3,2},{4,5},{5,4},{6,7},{7,6},{8,9},{9,8},{10,11... | collective-permute-start | bytes 1572872 | tf_op jit(solution)/shard_map/ppermute | solution.py:47
  40.1 13.5 %collective-permute-start.8 = (bf16[512,1024]{1,0:T(8,128)(2,1)S(1)}, bf16[512,1024]{1,0:T(8,128)(2,1)S(1)}, u32[]{:S(2)}, u32[]{:S(2)}) collective-permute-start(bf16[512,1024]{1,0:T(8,128)(2,1)S(1)} %get-tuple-element.70), channel_id=1, source_target_pairs={{0,1},{1,0},{2,3},{3,2},{4,5},{5,4},{6,7},{7,6},{8,9},{9,8},{10,11... | collective-permute-start | bytes 3145736 | tf_op jit(solution)/shard_map/ppermute | solution.py:47
  40.3 13.4 %collective-permute-start.7 = (bf16[512,1024]{1,0:T(8,128)(2,1)S(1)}, bf16[512,1024]{1,0:T(8,128)(2,1)S(1)}, u32[]{:S(2)}, u32[]{:S(2)}) collective-permute-start(bf16[512,1024]{1,0:T(8,128)(2,1)S(1)} %get-tuple-element.68), channel_id=1, source_target_pairs={{0,1},{1,0},{2,3},{3,2},{4,5},{5,4},{6,7},{7,6},{8,9},{9,8},{10,11... | collective-permute-start | bytes 3145736 | tf_op jit(solution)/shard_map/ppermute | solution.py:47
  40.6 13.0 %collective-permute-start.10 = (bf16[384,1024]{1,0:T(8,128)(2,1)S(1)}, bf16[384,1024]{1,0:T(8,128)(2,1)S(1)}, u32[]{:S(2)}, u32[]{:S(2)}) collective-permute-start(bf16[384,1024]{1,0:T(8,128)(2,1)S(1)} %get-tuple-element.74), channel_id=1, source_target_pairs={{0,1},{1,0},{2,3},{3,2},{4,5},{5,4},{6,7},{7,6},{8,9},{9,8},{10,11... | collective-permute-start | bytes 2359304 | tf_op jit(solution)/shard_map/ppermute | solution.py:47
  40.8 12.9 %collective-permute-start.9 = (bf16[384,1024]{1,0:T(8,128)(2,1)S(1)}, bf16[384,1024]{1,0:T(8,128)(2,1)S(1)}, u32[]{:S(2)}, u32[]{:S(2)}) collective-permute-start(bf16[384,1024]{1,0:T(8,128)(2,1)S(1)} %get-tuple-element.72), channel_id=1, source_target_pairs={{0,1},{1,0},{2,3},{3,2},{4,5},{5,4},{6,7},{7,6},{8,9},{9,8},{10,11... | collective-permute-start | bytes 2359304 | tf_op jit(solution)/shard_map/ppermute | solution.py:47
  41.2 26.8 %collective-permute-start.13 = (bf16[128,4096]{1,0:T(8,128)(2,1)S(1)}, bf16[128,4096]{1,0:T(8,128)(2,1)S(1)}, u32[]{:S(2)}, u32[]{:S(2)}) collective-permute-start(bf16[128,4096]{1,0:T(8,128)(2,1)S(1)} %get-tuple-element.83), channel_id=1, source_target_pairs={{0,2},{1,3},{2,0},{3,1},{4,6},{5,7},{6,4},{7,5},{8,10},{9,11},{10,... | collective-permute-start | bytes 3145736 | tf_op jit(solution)/shard_map/ppermute | solution.py:47
  63.5 1.5 %collective-permute-start.11 = (bf16[128,640]{1,0:T(8,128)(2,1)S(1)}, bf16[128,640]{1,0:T(8,128)(2,1)S(1)}, u32[]{:S(2)}, u32[]{:S(2)}) collective-permute-start(bf16[128,640]{1,0:T(8,128)(2,1)S(1)} %bring_home.1.own), channel_id=1, source_target_pairs={{0,1},{1,0},{2,3},{3,2},{4,5},{5,4},{6,7},{7,6},{8,9},{9,8},{10,11... | collective-permute-start | bytes 491528 | tf_op jit(solution)/shard_map/ppermute | solution.py:47
  65.7 11.3 %collective-permute-start.12 = (bf16[128,1408]{1,0:T(8,128)(2,1)S(1)}, bf16[128,1408]{1,0:T(8,128)(2,1)S(1)}, u32[]{:S(2)}, u32[]{:S(2)}) collective-permute-start(bf16[128,1408]{1,0:T(8,128)(2,1)S(1)} %spread_far.1), channel_id=1, source_target_pairs={{0,2},{1,3},{2,0},{3,1},{4,6},{5,7},{6,4},{7,5},{8,10},{9,11},{10,... | collective-permute-start | bytes 1081352 | tf_op jit(solution)/shard_map/ppermute | solution.py:47
  66.8 10.2 %copy-start.7 = (bf16[128,2048]{1,0:T(8,128)(2,1)S(1)}, bf16[128,2048]{1,0:T(8,128)(2,1)}, u32[]{:S(2)}) copy-start(bf16[128,2048]{1,0:T(8,128)(2,1)} %inputs.5) | copy-start | bytes 1572868
  68.0 2.2 %collective-permute-start.14 = (bf16[128,512]{1,0:T(8,128)(2,1)S(1)}, bf16[128,512]{1,0:T(8,128)(2,1)S(1)}, u32[]{:S(2)}, u32[]{:S(2)}) collective-permute-start(bf16[128,512]{1,0:T(8,128)(2,1)S(1)} %get-tuple-element.88), channel_id=1, source_target_pairs={{0,1},{1,0},{2,3},{3,2},{4,5},{5,4},{6,7},{7,6},{8,9},{9,8},{10,11... | collective-permute-start | bytes 393224 | tf_op jit(solution)/shard_map/ppermute | solution.py:47
  68.1 13.7 %collective-permute-start.18 = (bf16[128,1024]{1,0:T(8,128)(2,1)S(1)}, bf16[128,1024]{1,0:T(8,128)(2,1)S(1)}, u32[]{:S(2)}, u32[]{:S(2)}) collective-permute-start(bf16[128,1024]{1,0:T(8,128)(2,1)S(1)} %spread_rest.1), channel_id=1, source_target_pairs={{0,2},{1,3},{2,0},{3,1},{4,6},{5,7},{6,4},{7,5},{8,10},{9,11},{10,... | collective-permute-start | bytes 786440 | tf_op jit(solution)/shard_map/ppermute | solution.py:47
  69.7 1.3 %collective-permute-start.15 = (bf16[128,512]{1,0:T(8,128)(2,1)S(1)}, bf16[128,512]{1,0:T(8,128)(2,1)S(1)}, u32[]{:S(2)}, u32[]{:S(2)}) collective-permute-start(bf16[128,512]{1,0:T(8,128)(2,1)S(1)} %get-tuple-element.89), channel_id=1, source_target_pairs={{0,1},{1,0},{2,3},{3,2},{4,5},{5,4},{6,7},{7,6},{8,9},{9,8},{10,11... | collective-permute-start | bytes 393224 | tf_op jit(solution)/shard_map/ppermute | solution.py:47
  69.9 1.4 %collective-permute-start.16 = (bf16[128,512]{1,0:T(8,128)(2,1)S(1)}, bf16[128,512]{1,0:T(8,128)(2,1)S(1)}, u32[]{:S(2)}, u32[]{:S(2)}) collective-permute-start(bf16[128,512]{1,0:T(8,128)(2,1)S(1)} %get-tuple-element.90), channel_id=1, source_target_pairs={{0,1},{1,0},{2,3},{3,2},{4,5},{5,4},{6,7},{7,6},{8,9},{9,8},{10,11... | collective-permute-start | bytes 393224 | tf_op jit(solution)/shard_map/ppermute | solution.py:47
  70.2 1.3 %collective-permute-start.17 = (bf16[128,512]{1,0:T(8,128)(2,1)S(1)}, bf16[128,512]{1,0:T(8,128)(2,1)S(1)}, u32[]{:S(2)}, u32[]{:S(2)}) collective-permute-start(bf16[128,512]{1,0:T(8,128)(2,1)S(1)} %get-tuple-element.91), channel_id=1, source_target_pairs={{0,1},{1,0},{2,3},{3,2},{4,5},{5,4},{6,7},{7,6},{8,9},{9,8},{10,11... | collective-permute-start | bytes 393224 | tf_op jit(solution)/shard_map/ppermute | solution.py:47
  (8 other events, 9.4 us)

commit v7 on v5

--- a/solution.py
+++ b/solution.py
@@ -16,6 +16,7 @@
 VMEM = pl.BlockSpec(memory_space=pltpu.VMEM)
 SMEM = pl.BlockSpec(memory_space=pltpu.SMEM)
 TILE = 512
+EXTRA = 3 * HEAD_DIM
 
 
 def dot(left, right, dims=(((1,), (0,)), ((), ()))):
@@ -68,16 +69,20 @@
     near_turned,
     output_turned,
     own_here,
-    near_here,
     far_output,
     send_out,
     receive_out,
     segments_out,
 ):
-    width = near_here.shape[1]
-    far_left, far_right = far_output.at[:, :width], far_output.at[:, width:]
-    for slot, target in enumerate((own_here, near_here, far_left, far_right)):
-        target[...] = w_output[:, pl.ds(block_start(order, slot, width), width)]
+    width = own_here.shape[1]
+    blocks = [w_output[:, pl.ds(block_start(order, slot, width), width)] for slot in range(4)]
+    own_here[...] = blocks[0]
+    for target, left, right in (
+        (far_output, blocks[2], blocks[3]),
+        (near_turned.at[3 * HEAD_DIM :, :], blocks[1], blocks[3]),
+    ):
+        target[:, :width] = left
+        target[:, width:] = right
     for start in range(0, w_output.shape[1], TILE):
         output_turned[start : start + TILE, :] = w_output[:, start : start + TILE].T
     for source, target in ((send, send_out), (receive, receive_out), (segments, segments_out)):
@@ -100,9 +105,8 @@
         "prepare",
         [
             shape(low, 3 * heads, 2 * width),
-            shape(low, 3 * heads, 2 * width),
+            shape(low, 4 * heads, 2 * width),
             shape(low, w_output.shape[1], heads),
-            shape(low, heads, width),
             shape(low, heads, width),
             shape(low, heads, 2 * width),
             shape(jnp.int32, *send.shape),
@@ -259,91 +263,114 @@
     return call(bring_home_kernel, "bring_home", out, (moved, send, home), first=VMEM)
 
 
-def spread_into(own, near, weights, near_weights, first, out, place, held, total, sem):
-    span = held.shape[1]
-    copy = pltpu.make_async_copy(near_weights.at[:, pl.ds(first, span)], held, sem)
-    copy.start()
-    own_grads = own[:, : 3 * HEAD_DIM]
-    near_grads = near[:, : 3 * HEAD_DIM]
-    for start in range(0, span, TILE):
-        columns = slice(first + start, first + start + TILE)
-        total[:, start : start + TILE] = dot(own_grads, weights[:, columns])
-    copy.wait()
-    for start in range(0, span, TILE):
-        tile = slice(start, start + TILE)
-        result = total[:, tile] + dot(near_grads, held[:, tile])
-        out[:, place + start : place + start + TILE] = result.astype(out.dtype)
-
-
-def spread_far_kernel(own, near, weights, near_weights, out, *scratch):
-    width = weights.shape[1] // 2
-    write_parts(
-        read_parts(own[:, 4 * HEAD_DIM :]) + read_parts(near[:, 4 * HEAD_DIM :]),
-        out.at[:, :HEAD_DIM],
-    )
-    attended = slice(3 * HEAD_DIM, 4 * HEAD_DIM)
-    out[:, HEAD_DIM : 2 * HEAD_DIM] = own[:, attended]
-    out[:, 2 * HEAD_DIM : 3 * HEAD_DIM] = near[:, attended]
-    spread_into(own, near, weights, near_weights, width, out, 3 * HEAD_DIM, *scratch)
-
-
-def spread_rest_kernel(own, near, weights, near_weights, out, *scratch):
-    width = weights.shape[1] // 2
-    spread_into(own, near, weights, near_weights, width + width // 2, out, 0, *scratch)
-
-
-def spread_own_kernel(own, near, weights, near_weights, out, *scratch):
-    spread_into(own, near, weights, near_weights, 0, out, 0, *scratch)
-
-
-def spread(kernel, name, out, span, operands):
-    rows, depth = operands[0].shape[0], operands[2].shape[0]
+def spread_kernel(first, place):
+    def kernel(own, near, weights, near_weights, out, held, total, sems):
+        depth, span = held.shape
+        copies = []
+        for index, start in enumerate(range(0, span, TILE)):
+            source = near_weights.at[pl.ds(0, depth), pl.ds(first + start, TILE)]
+            target = held.at[:, pl.ds(start, TILE)]
+            copies.append(pltpu.make_async_copy(source, target, sems.at[index]))
+            copies[-1].start()
+        if place:
+            attended = slice(depth, depth + HEAD_DIM)
+            out[:, :HEAD_DIM] = own[:, attended]
+            out[:, HEAD_DIM : 2 * HEAD_DIM] = near[:, attended]
+            row_dot = read_parts(own[:, depth + HEAD_DIM :]) + read_parts(near[:, depth + HEAD_DIM :])
+            write_parts(row_dot, out.at[:, 2 * HEAD_DIM : place])
+        own_rows, near_rows = own[:, :depth], near[:, :depth]
+        for start in range(0, span, TILE):
+            columns = slice(first + start, first + start + TILE)
+            total[:, start : start + TILE] = dot(own_rows, weights[:, columns])
+        for index, start in enumerate(range(0, span, TILE)):
+            copies[index].wait()
+            result = total[:, start : start + TILE] + dot(near_rows, held[:, start : start + TILE])
+            out[:, place + start : place + start + TILE] = result.astype(out.dtype)
+
+    return kernel
+
+
+def spread(name, first, span, place, dtype, own, near, weights, near_weights):
+    rows, depth = own.shape[0], weights.shape[0]
     return pl.pallas_call(
-        kernel,
-        out_shape=out,
+        spread_kernel(first, place),
+        out_shape=shape(dtype, rows, place + span),
         in_specs=[VMEM] * 3 + [pl.BlockSpec(memory_space=pl.ANY)],
         out_specs=VMEM,
         scratch_shapes=[
             pltpu.VMEM((depth, span), jnp.bfloat16),
             pltpu.VMEM((rows, span), jnp.float32),
-            pltpu.SemaphoreType.DMA,
+            pltpu.SemaphoreType.DMA((span // TILE,)),
         ],
         compiler_params=pltpu.CompilerParams(vmem_limit_bytes=VMEM_LIMIT),
         cost_estimate=pl.CostEstimate(flops=1000, bytes_accessed=1000, transcendentals=0),
         name=name,
-    )(*operands)
-
-
-def finish_out_kernel(inputs, own, near, far, w_own, w_near, w_far, w_last, out):
+    )(own, near, weights, near_weights)
+
+
+def finish_out_kernel(
+    near_weights, inputs, own, near, far, w_own, w_far, w_last, out, w_near, sem
+):
     width = inputs.shape[1]
-    attended = slice(3 * HEAD_DIM, 4 * HEAD_DIM)
-    rows = jnp.concatenate(
-        [own[:, attended], near[:, attended], far[:, HEAD_DIM : 3 * HEAD_DIM]], axis=1
-    )
+    rows = pl.ds(3 * HEAD_DIM, HEAD_DIM)
+    copy = pltpu.make_async_copy(near_weights.at[rows, pl.ds(0, width)], w_near, sem)
+    copy.start()
+    there = slice(3 * HEAD_DIM, 4 * HEAD_DIM)
+    attended = [own[:, there], near[:, there], far[:, : 2 * HEAD_DIM]]
+    attended = jnp.concatenate(attended, axis=1)
+    copy.wait()
     for start in range(0, width, TILE):
         tile = slice(start, start + TILE)
         second = slice(width + start, width + start + TILE)
         stacked = [w_own[:, tile], w_near[:, tile], w_far[:, tile], w_last[:, second]]
-        total = dot(rows, jnp.concatenate(stacked, axis=0))
+        total = dot(attended, jnp.concatenate(stacked, axis=0))
         out[:, tile] = (inputs[:, tile].astype(jnp.float32) + total).astype(jnp.bfloat16)
 
 
-def finish_grad_kernel(inputs, cotangent, gain, inverse, own, near, grad_own, far, rest, out):
-    width = inputs.shape[1]
-    row_dot = read_parts(own[:, 4 * HEAD_DIM :]) + read_parts(near[:, 4 * HEAD_DIM :])
-    mean_dot = (row_dot + read_parts(far[:, :HEAD_DIM])) / (4 * width)
+def finish_grad_kernel(first, count, *refs):
+    inputs, cotangent, gain, inverse, own, near, grad_own, far = refs[:8]
+    got, (out, held, sem) = refs[8 : 8 + count], refs[-3:]
+    row_dot = read_parts(far[:, 2 * HEAD_DIM : EXTRA])
+    row_dot = row_dot + read_parts(own[:, 4 * HEAD_DIM :]) + read_parts(near[:, 4 * HEAD_DIM :])
+    mean_dot = row_dot / (4 * inputs.shape[1])
     inverse_rms = inverse[...]
-    for start in range(0, width, TILE):
-        tile = slice(start, start + TILE)
-        if start < width // 2:
-            got = far[:, 3 * HEAD_DIM + start : 3 * HEAD_DIM + start + TILE]
-        else:
-            got = rest[:, start - width // 2 : start - width // 2 + TILE]
-        grad_normed = grad_own[:, tile] + got.astype(jnp.float32)
-        grad_hat = grad_normed * gain[:, tile].astype(jnp.float32)
-        scaled = inputs[:, tile].astype(jnp.float32) * inverse_rms
-        change = inverse_rms * (grad_hat - scaled * mean_dot)
-        out[:, tile] = (cotangent[:, tile].astype(jnp.float32) + change).astype(jnp.bfloat16)
+    place = 0
+    if not first:
+        got = (far.at[:, EXTRA:], *got)
+    for piece in got:
+        for start in range(0, piece.shape[1], TILE):
+            tile = slice(first + place, first + place + TILE)
+            grad_normed = grad_own[:, tile] + piece[:, start : start + TILE].astype(jnp.float32)
+            grad_hat = grad_normed * gain[:, tile].astype(jnp.float32)
+            scaled = inputs[:, tile].astype(jnp.float32) * inverse_rms
+            change = inverse_rms * (grad_hat - scaled * mean_dot)
+            result = cotangent[:, tile].astype(jnp.float32) + change
+            held[:, place : place + TILE] = result.astype(jnp.bfloat16)
+            place += TILE
+    copy = pltpu.make_async_copy(held, out.at[:, pl.ds(first, held.shape[1])], sem)
+    copy.start()
+    copy.wait()
+
+
+def finish_grad(name, first, fixed, got, before):
+    rows, width = fixed[0].shape
+    span = sum(piece.shape[1] for piece in got)
+    if not first:
+        span += fixed[-1].shape[1] - EXTRA
+    count = len(got)
+    operands = (*fixed, *got, *before)
+    hbm = pl.BlockSpec(memory_space=pltpu.HBM)
+    return pl.pallas_call(
+        lambda *refs: finish_grad_kernel(first, count, *refs),
+        out_shape=shape(jnp.bfloat16, rows, width),
+        in_specs=[VMEM] * (len(fixed) + count) + [hbm] * len(before),
+        out_specs=hbm,
+        scratch_shapes=[pltpu.VMEM((rows, span), jnp.bfloat16), pltpu.SemaphoreType.DMA],
+        input_output_aliases={len(operands) - 1: 0} if before else {},
+        compiler_params=pltpu.CompilerParams(vmem_limit_bytes=VMEM_LIMIT),
+        cost_estimate=pl.CostEstimate(flops=1000, bytes_accessed=1000, transcendentals=0),
+        name=name,
+    )(*operands)
 
 
 def move(bucket):
@@ -378,7 +405,7 @@
     x1 = swap(inputs, 1, tensor)
     c1 = swap(cotangent, 1, tensor)
     weights = (w_query, w_key, w_value)
-    (own_turned, near_turned, output_turned, own_here, near_here, far_output, *indices) = prepare(
+    (own_turned, near_turned, output_turned, own_here, far_output, *indices) = prepare(
         order,
         *weights,
         w_output,
@@ -412,34 +439,32 @@
     own = bring_home(move(back), send, home)
 
     near = swap(own, 1, tensor)
-    sides = (own, near, own_turned, near_turned)
-    half = width // 2
-    far_shape = shape(low, rows, 3 * HEAD_DIM + half)
-    far_part = spread(spread_far_kernel, "spread_far", far_shape, half, sides)
-    far = swap(far_part, 2, tensor)
-    sides = (after(own, far_part), *sides[1:])
-    rest_part = spread(spread_rest_kernel, "spread_rest", shape(low, rows, half), half, sides)
-    rest = swap(rest_part, 2, tensor)
-    sides = (after(own, rest_part), *sides[1:])
-    own_shape = shape(jnp.float32, rows, width)
-    grad_own = spread(spread_own_kernel, "spread_own", own_shape, width, sides)
-    near_here = swap(after(near_here, home), 1, tensor)
     last_output = swap(after(far_output, near), 1, tensor)
+    quarter = width // 4
+    turn, got = own, []
+    for first, span in ((0, 2 * quarter), (2 * quarter, quarter), (3 * quarter, quarter)):
+        place = 0 if first else EXTRA
+        part = spread(
+            "spread_far", width + first, span, place, low, turn, near, own_turned, near_turned
+        )
+        got.append(swap(part, 2, tensor))
+        turn = after(own, part)
+    grad_own = spread(
+        "spread_own", 0, width, 0, jnp.float32, turn, near, own_turned, near_turned
+    )
+    far, middle, rest = got
     layer_out = call(
         finish_out_kernel,
         "finish_out",
         shape(low, rows, width),
-        (inputs, own, near, far, own_here, near_here, far_output, last_output),
-        first=VMEM,
-    )
-    rest = after(rest, layer_out)
-    input_grad = call(
-        finish_grad_kernel,
-        "finish_grad",
-        shape(low, rows, width),
-        (inputs, cotangent, gain, inverse_rms, own, near, grad_own, far, rest),
-        first=VMEM,
-    )
+        (near_turned, inputs, own, near, far, own_here, far_output, last_output),
+        scratch=[pltpu.VMEM((HEAD_DIM, width), low), pltpu.SemaphoreType.DMA],
+        first=pl.BlockSpec(memory_space=pl.ANY),
+    )
+    middle = after(middle, layer_out)
+    fixed = (inputs, cotangent, gain, inverse_rms, own, near, grad_own, far)
+    begun = finish_grad("finish_most", 0, fixed, (middle,), ())
+    input_grad = finish_grad("finish_rest", 3 * quarter, fixed, (rest,), (begun,))
     return (layer_out, input_grad)
 
 

time: 79.5 us -> 79 us (level)
  waiting for transfers between devices: 22.4 us -> 20.1 us
  Pallas kernels: 13.3 us -> 14.9 us
    pallas_call x3 -> x6, Pallas kernels: 2.35 us -> 5.15 us  [the longest x4 3.08 us: spread(): pl.pallas_call(spread_kernel(first, place), out_shape=shape(dtype, rows,...]
    ppermute x15, waiting for transfers between devices: 22.4 us -> 20.1 us  [swap(): return lax.ppermute(array, 'tensor', [(i, i ^ mask) for i in range(count)])]
    pallas_call x8 -> x7, Pallas kernels: 10.9 us -> 9.73 us  [call(): pl.pallas_call(kernel, out_shape=shapes, in_specs=[first] + [rest] * (len...]
  transfers between devices with their start and end apart: 15 -> 15, of which waited for: 5 -> 6; matrix products, arithmetic and copies ran while one was open for 1% -> 1% of each run, Pallas kernels for 12% -> 15%
where the time goes in v7:
time: 79 us; the launch traced here: 78.6 us
  blocking collectives  22.7 us (29%)
  waiting for transfers between devices  20.1 us (25%)
  Pallas kernels  14.9 us (19%)
  starting transfers between devices  11.1 us (14%)
  local copies, waits for them, and re-layouts  9.04 us (11%)
  between operations  0.81 us (1%)
    all_to_all x2, blocking collectives, move(): return lax.all_to_all(bucket, 'dp', split_axis=0, concat_axis=0, tiled=True)  22.7 us
    ppermute x15, waiting for transfers between devices, swap(): return lax.ppermute(array, 'tensor', [(i, i ^ mask) for i in range(count)])  20.1 us
    ppermute x15, starting transfers between devices, swap(): return lax.ppermute(array, 'tensor', [(i, i ^ mask) for i in range(count)])  11.1 us
    pallas_call x7, Pallas kernels, call(): pl.pallas_call(kernel, out_shape=shapes, in_specs=[first] + [rest] * (len...  9.73 us
    unnamed x22, local copies, waits for them, and re-layouts  8.34 us
    pallas_call x4, Pallas kernels, spread(): pl.pallas_call(spread_kernel(first, place), out_shape=shape(dtype, rows,...  3.08 us
    pallas_call x2, Pallas kernels, finish_grad(): pl.pallas_call(lambda *refs: finish_grad_kernel(first, count, *refs), out...  2.06 us
  transfers between devices with their start and end apart: 15, of which 6 were waited for; matrix products, arithmetic and copies ran while one was open for 1% of the time, Pallas kernels for 15%

profile of v7, /device:TPU:0, one launch (start us, length us, event | category | flops | bytes accessed | tf_op | source)
XLA Modules:
  0.0 78.6 jit_solution(11234717646506906954)
XLA Ops:
  1.2 2.9 %collective-permute-start.1 = (bf16[128,2048]{1,0:T(8,128)(2,1)}, bf16[128,2048]{1,0:T(8,128)(2,1)S(1)}, u32[]{:S(2)}, u32[]{:S(2)}) collective-permute-start(bf16[128,2048]{1,0:T(8,128)(2,1)} %refs_0_.3), channel_id=1, source_target_pairs={{0,2},{1,3},{2,0},{3,1},{4,6},{5,7},{6,4},{7,5},{8,10},{9,11},{10,... | collective-permute-start | bytes 1572872 | tf_op jit(solution)/shard_map/ppermute | solution.py:47
  4.9 2.0 %collective-permute-start.3 = (bf16[1,2048]{1,0:T(2,128)(2,1)S(1)}, bf16[1,2048]{1,0:T(2,128)(2,1)S(1)}, u32[]{:S(2)}, u32[]{:S(2)}) collective-permute-start(bf16[1,2048]{1,0:T(2,128)(2,1)S(1)} %reshape.19.refs_2_), channel_id=1, source_target_pairs={{0,2},{1,3},{2,0},{3,1},{4,6},{5,7},{6,4},{7,5},{8,10},{9,11},{10,... | collective-permute-start | bytes 12296 | tf_op jit(solution)/shard_map/ppermute | solution.py:47
  6.9 1.6 %copy-done.1 = bf16[8192,128]{1,0:T(8,128)(2,1)S(1)} copy-done((bf16[8192,128]{1,0:T(8,128)(2,1)S(1)}, bf16[8192,128]{1,0:T(8,128)(2,1)}, u32[]{:S(2)}) %copy-start.1) | copy-done | bytes 2097176
  8.5 1.6 %copy-done.2 = bf16[8192,128]{1,0:T(8,128)(2,1)S(1)} copy-done((bf16[8192,128]{1,0:T(8,128)(2,1)S(1)}, bf16[8192,128]{1,0:T(8,128)(2,1)}, u32[]{:S(2)}) %copy-start.2) | copy-done | bytes 2097176
  10.1 1.6 %copy-done.4 = bf16[8192,128]{1,0:T(8,128)(2,1)S(1)} copy-done((bf16[8192,128]{1,0:T(8,128)(2,1)S(1)}, bf16[8192,128]{1,0:T(8,128)(2,1)}, u32[]{:S(2)}) %copy-start.4) | copy-done | bytes 2097176
  11.7 1.6 %copy-done.7 = bf16[128,8192]{1,0:T(8,128)(2,1)S(1)} copy-done((bf16[128,8192]{1,0:T(8,128)(2,1)S(1)}, bf16[128,8192]{1,0:T(8,128)(2,1)}, u32[]{:S(2)}) %copy-start.7) | copy-done | bytes 2097176
  15.2 2.9 %prepare.1 = (bf16[384,4096]{1,0:T(8,128)(2,1)S(1)}, bf16[512,4096]{1,0:T(8,128)(2,1)S(1)}, bf16[8192,128]{1,0:T(8,128)(2,1)S(1)}, bf16[128,2048]{1,0:T(8,128)(2...) custom-call(s32[4]{0:T(128)S(1)} %iota_xor_fusion.order, ...), custom_call_target="tpu_custom_call" | custom-call | flops 1000 | bytes 1000 | tf_op jit(solution)/shard_map/prepare/pallas_call | solution.py:29
  18.2 1.1 %begin.1 = (f32[128,1]{1,0:T(8,128)S(1)}, f32[128,128]{1,0:T(8,128)S(1)}) custom-call(s32[4]{0:T(128)S(1)} %iota_xor_fusion.order, bf16[128,2048]{1,0:T(8,128)(2,1)S(1)} %copy-done, bf16[128,2048]{1,0:T(8,128)(2,1)S(1)} %collective-permute-done.x1, bf16[128,2048]{1,0:T(8,128)(2,1)S(1)} %copy-done.6, bf16[128,2048]{1,0:T(8,128)(2,1)S(1)} %collective-permute-done.4.c1, ...), custom_call_target="tpu_custom_call" | custom-call | flops 1000 | bytes 1000 | tf_op jit(solution)/shard_map/begin/pallas_call | solution.py:29
  19.3 8.7 %collective-permute-done.3 = bf16[1,2048]{1,0:T(2,128)(2,1)S(1)} collective-permute-done((bf16[1,2048]{1,0:T(2,128)(2,1)S(1)}, bf16[1,2048]{1,0:T(2,128)(2,1)S(1)}, u32[]{:S(2)}, u32[]{:S(2)}) %collective-permute-start.3) | collective-permute-done | bytes 4128 | tf_op jit(solution)/shard_map/ppermute | solution.py:47
  29.5 1.1 %collective-permute-done.7.gain_near = bf16[2,2048]{1,0:T(2,128)(2,1)S(1)} collective-permute-done((bf16[2,2048]{1,0:T(2,128)(2,1)S(1)}, bf16[2,2048]{1,0:T(2,128)(2,1)S(1)}, u32[]{:S(2)}, u32[]{:S(2)}) %collective-permute-start.7) | collective-permute-done | bytes 8224 | tf_op jit(solution)/shard_map/ppermute | solution.py:47
  30.7 2.3 %project.1 = (bf16[128,384]{1,0:T(8,128)(2,1)S(1)}, f32[128,1]{1,0:T(8,128)S(1)}, bf16[128,512]{1,0:T(8,128)(2,1)S(1)}) custom-call(s32[4]{0:T(128)S(1)} %iota_xor_fusion.order, bf16[128,2048]{1,0:T(8,128)(2,1)S(1)} %copy-done, bf16[128,2048]{1,0:T(8,128)(2,1)S(1)} %collective-permute-done.x1, bf16[128,2048]{1,0:T(8,128)(2,1)S(1)} %collective-permute-done.1.x2, ...), custom_call_target="tpu_custom_call" | custom-call | flops 1000 | bytes 1000 | tf_op jit(solution)/shard_map/project/pallas_call | solution.py:29
  33.1 1.8 %collective-permute-start.11 = (bf16[128,4096]{1,0:T(8,128)(2,1)S(1)}, bf16[128,4096]{1,0:T(8,128)(2,1)S(1)}, u32[]{:S(2)}, u32[]{:S(2)}) collective-permute-start(bf16[128,4096]{1,0:T(8,128)(2,1)S(1)} %get-tuple-element.49), channel_id=1, source_target_pairs={{0,2},{1,3},{2,0},{3,1},{4,6},{5,7},{6,4},{7,5},{8,10},{9,11},{10,... | collective-permute-start | bytes 3145736 | tf_op jit(solution)/shard_map/ppermute | solution.py:47
  34.9 12.9 %all_to_all.22 = bf16[8,16,512]{2,1,0:T(8,128)(2,1)S(1)} all-to-all(bf16[8,16,512]{2,1,0:T(8,128)(2,1)S(1)} %bitcast.9), channel_id=1, replica_groups=mesh['dp'=8,'tensor'=4] {'dp'}, dimensions={0} | all-to-all | bytes 262144 | tf_op jit(solution)/shard_map/all_to_all | solution.py:377
  47.8 1.1 %attend.1 = bf16[128,512]{1,0:T(8,128)(2,1)S(1)} custom-call(bf16[128,512]{1,0:T(8,128)(2,1)S(1)} %bitcast.6, s32[1,128]{1,0:T(1,128)S(1)} %get-tuple-element.44.receive, s32[1,128]{1,0:T(1,128)S(1)} %get-tuple-element.45.segments), custom_call_target="tpu_custom_call" | custom-call | flops 1000 | bytes 1000 | tf_op jit(solution)/shard_map/attend/pallas_call | solution.py:29
  48.9 9.7 %all_to_all.23 = bf16[8,16,512]{2,1,0:T(8,128)(2,1)S(1)} all-to-all(bf16[8,16,512]{2,1,0:T(8,128)(2,1)S(1)} %bitcast.7), channel_id=1, replica_groups=mesh['dp'=8,'tensor'=4] {'dp'}, dimensions={0} | all-to-all | bytes 262144 | tf_op jit(solution)/shard_map/all_to_all | solution.py:377
  59.0 1.4 %collective-permute-done.9.near.refs_5_ = bf16[128,640]{1,0:T(8,128)(2,1)S(1)} collective-permute-done((bf16[128,640]{1,0:T(8,128)(2,1)S(1)}, bf16[128,640]{1,0:T(8,128)(2,1)S(1)}, u32[]{:S(2)}, u32[]{:S(2)}) %collective-permute-start.9) | collective-permute-done | bytes 163872 | tf_op jit(solution)/shard_map/ppermute | solution.py:47
  62.3 1.6 %collective-permute-start.14 = (bf16[128,512]{1,0:T(8,128)(2,1)S(1)}, bf16[128,512]{1,0:T(8,128)(2,1)S(1)}, u32[]{:S(2)}, u32[]{:S(2)}) collective-permute-start(bf16[128,512]{1,0:T(8,128)(2,1)S(1)} %spread_far.4), channel_id=1, source_target_pairs={{0,2},{1,3},{2,0},{3,1},{4,6},{5,7},{6,4},{7,5},{8,10},{9,11},{10,... | collective-permute-start | bytes 393224 | tf_op jit(solution)/shard_map/ppermute | solution.py:47
  64.9 1.5 %spread_own.1.refs_6_ = f32[128,2048]{1,0:T(8,128)S(1)} custom-call(bf16[128,640]{1,0:T(8,128)(2,1)S(1)} %bring_home.1.own.refs_4_, bf16[128,640]{1,0:T(8,128)(2,1)S(1)} %collective-permute-done.9.near.refs_5_, bf16[384,4096]{1,0:T(8,128)(2,1)S(1)} %get-tuple-element.46.weights, bf16[512,4096]{1,0:T(8,128)(2,1)S(1)} %collective-permute-done.8.near_weights), custom_call_target="tpu_custom_call" | custom-call | flops 1000 | bytes 1000 | tf_op jit(solution)/shard_map/spread_own/pallas_call | solution.py:295
  66.4 6.2 %collective-permute-done.10.far.refs_7_ = bf16[128,1408]{1,0:T(8,128)(2,1)S(1)} collective-permute-done((bf16[128,1408]{1,0:T(8,128)(2,1)S(1)}, bf16[128,1408]{1,0:T(8,128)(2,1)S(1)}, u32[]{:S(2)}, u32[]{:S(2)}) %collective-permute-start.10) | collective-permute-done | bytes 360480 | tf_op jit(solution)/shard_map/ppermute | solution.py:47
  72.7 1.3 %finish_out.1 = bf16[128,2048]{1,0:T(8,128)(2,1)} custom-call(bf16[512,4096]{1,0:T(8,128)(2,1)S(1)} %collective-permute-done.8.near_weights, bf16[128,2048]{1,0:T(8,128)(2,1)S(1)} %copy-done, bf16[128,640]{1,0:T(8,128)(2,1)S(1)} %bring_home.1.own.refs_4_, bf16[128,640]{1,0:T(8,128)(2,1)S(1)} %collective-permute-done.9.near.refs_5_, ...), custom_call_target="tpu_custom_call" | custom-call | flops 1000 | bytes 1000 | tf_op jit(solution)/shard_map/finish_out/pallas_call | solution.py:29
  74.0 1.5 %collective-permute-done.14.refs_8_ = bf16[128,512]{1,0:T(8,128)(2,1)S(1)} collective-permute-done((bf16[128,512]{1,0:T(8,128)(2,1)S(1)}, bf16[128,512]{1,0:T(8,128)(2,1)S(1)}, u32[]{:S(2)}, u32[]{:S(2)}) %collective-permute-start.14) | collective-permute-done | bytes 131104 | tf_op jit(solution)/shard_map/ppermute | solution.py:47
  75.5 1.2 %finish_most.1.refs_9_ = bf16[128,2048]{1,0:T(8,128)(2,1)} custom-call(bf16[128,2048]{1,0:T(8,128)(2,1)S(1)} %copy-done, bf16[128,2048]{1,0:T(8,128)(2,1)S(1)} %copy-done.6, bf16[1,2048]{1,0:T(2,128)(2,1)S(1)} %reshape.19.refs_2_, f32[128,1]{1,0:T(8,128)S(1)} %get-tuple-element.51.refs_3_, bf16[128,640]{1,0:T(8,128)(2,1)S(1)} %bring_home.1.own.refs_4_, ...), custom_call_target="tpu_custom_call" | custom-call | flops 1000 | bytes 1000 | tf_op jit(solution)/shard_map/finish_most/pallas_call | solution.py:363
  76.6 1.1 %collective-permute-done.13.refs_8_ = bf16[128,512]{1,0:T(8,128)(2,1)S(1)} collective-permute-done((bf16[128,512]{1,0:T(8,128)(2,1)S(1)}, bf16[128,512]{1,0:T(8,128)(2,1)S(1)}, u32[]{:S(2)}, u32[]{:S(2)}) %collective-permute-start.13) | collective-permute-done | bytes 131104 | tf_op jit(solution)/shard_map/ppermute | solution.py:47
  77.7 0.9 %finish_rest.1 = bf16[128,2048]{1,0:T(8,128)(2,1)} custom-call(bf16[128,2048]{1,0:T(8,128)(2,1)S(1)} %copy-done, bf16[128,2048]{1,0:T(8,128)(2,1)S(1)} %copy-done.6, bf16[1,2048]{1,0:T(2,128)(2,1)S(1)} %reshape.19.refs_2_, f32[128,1]{1,0:T(8,128)S(1)} %get-tuple-element.51.refs_3_, ...), custom_call_target="tpu_custom_call", output_to_operand_aliasing={{}: (9, {})} | custom-call | flops 1000 | bytes 1000 | tf_op jit(solution)/shard_map/finish_rest/pallas_call | solution.py:363
  (46 shorter events, 8.3 us)
Async XLA Ops:
  0.6 17.5 %collective-permute-start = (bf16[128,2048]{1,0:T(8,128)(2,1)}, bf16[128,2048]{1,0:T(8,128)(2,1)S(1)}, u32[]{:S(2)}, u32[]{:S(2)}) collective-permute-start(bf16[128,2048]{1,0:T(8,128)(2,1)} %refs_0_.3), channel_id=1, source_target_pairs={{0,1},{1,0},{2,3},{3,2},{4,5},{5,4},{6,7},{7,6},{8,9},{9,8},{10,11... | collective-permute-start | bytes 1572872 | tf_op jit(solution)/shard_map/ppermute | solution.py:47
  1.1 17.0 %collective-permute-start.4 = (bf16[128,2048]{1,0:T(8,128)(2,1)}, bf16[128,2048]{1,0:T(8,128)(2,1)S(1)}, u32[]{:S(2)}, u32[]{:S(2)}) collective-permute-start(bf16[128,2048]{1,0:T(8,128)(2,1)} %refs_1_.3), channel_id=1, source_target_pairs={{0,1},{1,0},{2,3},{3,2},{4,5},{5,4},{6,7},{7,6},{8,9},{9,8},{10,11... | collective-permute-start | bytes 1572872 | tf_op jit(solution)/shard_map/ppermute | solution.py:47
  1.2 26.7 %collective-permute-start.1 = (bf16[128,2048]{1,0:T(8,128)(2,1)}, bf16[128,2048]{1,0:T(8,128)(2,1)S(1)}, u32[]{:S(2)}, u32[]{:S(2)}) collective-permute-start(bf16[128,2048]{1,0:T(8,128)(2,1)} %refs_0_.3), channel_id=1, source_target_pairs={{0,2},{1,3},{2,0},{3,1},{4,6},{5,7},{6,4},{7,5},{8,10},{9,11},{10,... | collective-permute-start | bytes 1572872 | tf_op jit(solution)/shard_map/ppermute | solution.py:47
  4.2 23.8 %collective-permute-start.2 = (bf16[128,2048]{1,0:T(8,128)(2,1)}, bf16[128,2048]{1,0:T(8,128)(2,1)S(1)}, u32[]{:S(2)}, u32[]{:S(2)}) collective-permute-start(bf16[128,2048]{1,0:T(8,128)(2,1)} %refs_1_.3), channel_id=1, source_target_pairs={{0,2},{1,3},{2,0},{3,1},{4,6},{5,7},{6,4},{7,5},{8,10},{9,11},{10,... | collective-permute-start | bytes 1572872 | tf_op jit(solution)/shard_map/ppermute | solution.py:47
  4.9 23.1 %collective-permute-start.3 = (bf16[1,2048]{1,0:T(2,128)(2,1)S(1)}, bf16[1,2048]{1,0:T(2,128)(2,1)S(1)}, u32[]{:S(2)}, u32[]{:S(2)}) collective-permute-start(bf16[1,2048]{1,0:T(2,128)(2,1)S(1)} %reshape.19.refs_2_), channel_id=1, source_target_pairs={{0,2},{1,3},{2,0},{3,1},{4,6},{5,7},{6,4},{7,5},{8,10},{9,11},{10,... | collective-permute-start | bytes 12296 | tf_op jit(solution)/shard_map/ppermute | solution.py:47
  6.9 1.6 %copy-start.1 = (bf16[8192,128]{1,0:T(8,128)(2,1)S(1)}, bf16[8192,128]{1,0:T(8,128)(2,1)}, u32[]{:S(2)}) copy-start(bf16[8192,128]{1,0:T(8,128)(2,1)} %w_query.3) | copy-start | bytes 6291460
  8.5 1.6 %copy-start.2 = (bf16[8192,128]{1,0:T(8,128)(2,1)S(1)}, bf16[8192,128]{1,0:T(8,128)(2,1)}, u32[]{:S(2)}) copy-start(bf16[8192,128]{1,0:T(8,128)(2,1)} %w_key.3) | copy-start | bytes 6291460
  10.1 1.6 %copy-start.4 = (bf16[8192,128]{1,0:T(8,128)(2,1)S(1)}, bf16[8192,128]{1,0:T(8,128)(2,1)}, u32[]{:S(2)}) copy-start(bf16[8192,128]{1,0:T(8,128)(2,1)} %w_value.3) | copy-start | bytes 6291460
  11.7 1.6 %copy-start.7 = (bf16[128,8192]{1,0:T(8,128)(2,1)S(1)}, bf16[128,8192]{1,0:T(8,128)(2,1)}, u32[]{:S(2)}) copy-start(bf16[128,8192]{1,0:T(8,128)(2,1)} %w_output.1) | copy-start | bytes 6291460
  13.3 0.7 copy-start.8
  15.2 2.9 %copy-start = (bf16[128,2048]{1,0:T(8,128)(2,1)S(1)}, bf16[128,2048]{1,0:T(8,128)(2,1)}, u32[]{:S(2)}) copy-start(bf16[128,2048]{1,0:T(8,128)(2,1)} %refs_0_.3) | copy-start | bytes 1572868
  15.2 2.9 %copy-start.6 = (bf16[128,2048]{1,0:T(8,128)(2,1)S(1)}, bf16[128,2048]{1,0:T(8,128)(2,1)}, u32[]{:S(2)}) copy-start(bf16[128,2048]{1,0:T(8,128)(2,1)} %refs_1_.3) | copy-start | bytes 1572868
  18.1 12.5 %copy-start.5 = (bf16[8192,128]{1,0:T(8,128)(2,1)S(1)}, bf16[8192,128]{1,0:T(8,128)(2,1)}, u32[]{:S(2)}) copy-start(bf16[8192,128]{1,0:T(8,128)(2,1)} %w_value.3) | copy-start | bytes 6291460
  19.3 11.4 %copy-start.3 = (bf16[8192,128]{1,0:T(8,128)(2,1)S(1)}, bf16[8192,128]{1,0:T(8,128)(2,1)}, u32[]{:S(2)}) copy-start(bf16[8192,128]{1,0:T(8,128)(2,1)} %w_key.3) | copy-start | bytes 6291460
  28.0 2.7 %collective-permute-start.5 = (bf16[128,2048]{1,0:T(8,128)(2,1)S(1)}, bf16[128,2048]{1,0:T(8,128)(2,1)S(1)}, u32[]{:S(2)}, u32[]{:S(2)}) collective-permute-start(bf16[128,2048]{1,0:T(8,128)(2,1)S(1)} %collective-permute-done.1.x2), channel_id=1, source_target_pairs={{0,1},{1,0},{2,3},{3,2},{4,5},{5,4},{6,7},{7,6},{8,9},{9,8},{10,11... | collective-permute-start | bytes 1572872 | tf_op jit(solution)/shard_map/ppermute | solution.py:47
  28.0 2.7 %collective-permute-start.6 = (bf16[128,2048]{1,0:T(8,128)(2,1)S(1)}, bf16[128,2048]{1,0:T(8,128)(2,1)S(1)}, u32[]{:S(2)}, u32[]{:S(2)}) collective-permute-start(bf16[128,2048]{1,0:T(8,128)(2,1)S(1)} %collective-permute-done.2.c2), channel_id=1, source_target_pairs={{0,1},{1,0},{2,3},{3,2},{4,5},{5,4},{6,7},{7,6},{8,9},{9,8},{10,11... | collective-permute-start | bytes 1572872 | tf_op jit(solution)/shard_map/ppermute | solution.py:47
  28.5 2.1 %collective-permute-start.7 = (bf16[2,2048]{1,0:T(2,128)(2,1)S(1)}, bf16[2,2048]{1,0:T(2,128)(2,1)S(1)}, u32[]{:S(2)}, u32[]{:S(2)}) collective-permute-start(bf16[2,2048]{1,0:T(2,128)(2,1)S(1)} %pad_maximum_fusion.gain_own), channel_id=1, source_target_pairs={{0,1},{1,0},{2,3},{3,2},{4,5},{5,4},{6,7},{7,6},{8,9},{9,8},{10,11... | collective-permute-start | bytes 24584 | tf_op jit(solution)/shard_map/ppermute | solution.py:47
  32.9 27.6 %collective-permute-start.8 = (bf16[512,4096]{1,0:T(8,128)(2,1)S(1)}, bf16[512,4096]{1,0:T(8,128)(2,1)S(1)}, u32[]{:S(2)}, u32[]{:S(2)}) collective-permute-start(bf16[512,4096]{1,0:T(8,128)(2,1)S(1)} %get-tuple-element.42), channel_id=1, source_target_pairs={{0,1},{1,0},{2,3},{3,2},{4,5},{5,4},{6,7},{7,6},{8,9},{9,8},{10,11... | collective-permute-start | bytes 12582920 | tf_op jit(solution)/shard_map/ppermute | solution.py:47
  33.1 27.3 %collective-permute-start.11 = (bf16[128,4096]{1,0:T(8,128)(2,1)S(1)}, bf16[128,4096]{1,0:T(8,128)(2,1)S(1)}, u32[]{:S(2)}, u32[]{:S(2)}) collective-permute-start(bf16[128,4096]{1,0:T(8,128)(2,1)S(1)} %get-tuple-element.49), channel_id=1, source_target_pairs={{0,2},{1,3},{2,0},{3,1},{4,6},{5,7},{6,4},{7,5},{8,10},{9,11},{10,... | collective-permute-start | bytes 3145736 | tf_op jit(solution)/shard_map/ppermute | solution.py:47
  58.9 1.5 %collective-permute-start.9 = (bf16[128,640]{1,0:T(8,128)(2,1)S(1)}, bf16[128,640]{1,0:T(8,128)(2,1)S(1)}, u32[]{:S(2)}, u32[]{:S(2)}) collective-permute-start(bf16[128,640]{1,0:T(8,128)(2,1)S(1)} %bring_home.1.own.refs_4_), channel_id=1, source_target_pairs={{0,1},{1,0},{2,3},{3,2},{4,5},{5,4},{6,7},{7,6},{8,9},{9,8},{10,11... | collective-permute-start | bytes 491528 | tf_op jit(solution)/shard_map/ppermute | solution.py:47
  60.4 6.0 %collective-permute-start.12 = (bf16[128,4096]{1,0:T(8,128)(2,1)S(1)}, bf16[128,4096]{1,0:T(8,128)(2,1)S(1)}, u32[]{:S(2)}, u32[]{:S(2)}) collective-permute-start(bf16[128,4096]{1,0:T(8,128)(2,1)S(1)} %collective-permute-done.11.w_far), channel_id=1, source_target_pairs={{0,1},{1,0},{2,3},{3,2},{4,5},{5,4},{6,7},{7,6},{8,9},{9,8},{10,11... | collective-permute-start | bytes 3145736 | tf_op jit(solution)/shard_map/ppermute | solution.py:47
  61.3 11.3 %collective-permute-start.10 = (bf16[128,1408]{1,0:T(8,128)(2,1)S(1)}, bf16[128,1408]{1,0:T(8,128)(2,1)S(1)}, u32[]{:S(2)}, u32[]{:S(2)}) collective-permute-start(bf16[128,1408]{1,0:T(8,128)(2,1)S(1)} %spread_far.3), channel_id=1, source_target_pairs={{0,2},{1,3},{2,0},{3,1},{4,6},{5,7},{6,4},{7,5},{8,10},{9,11},{10,... | collective-permute-start | bytes 1081352 | tf_op jit(solution)/shard_map/ppermute | solution.py:47
  62.3 13.1 %collective-permute-start.14 = (bf16[128,512]{1,0:T(8,128)(2,1)S(1)}, bf16[128,512]{1,0:T(8,128)(2,1)S(1)}, u32[]{:S(2)}, u32[]{:S(2)}) collective-permute-start(bf16[128,512]{1,0:T(8,128)(2,1)S(1)} %spread_far.4), channel_id=1, source_target_pairs={{0,2},{1,3},{2,0},{3,1},{4,6},{5,7},{6,4},{7,5},{8,10},{9,11},{10,... | collective-permute-start | bytes 393224 | tf_op jit(solution)/shard_map/ppermute | solution.py:47
  64.3 13.4 %collective-permute-start.13 = (bf16[128,512]{1,0:T(8,128)(2,1)S(1)}, bf16[128,512]{1,0:T(8,128)(2,1)S(1)}, u32[]{:S(2)}, u32[]{:S(2)}) collective-permute-start(bf16[128,512]{1,0:T(8,128)(2,1)S(1)} %spread_far.5), channel_id=1, source_target_pairs={{0,2},{1,3},{2,0},{3,1},{4,6},{5,7},{6,4},{7,5},{8,10},{9,11},{10,... | collective-permute-start | bytes 393224 | tf_op jit(solution)/shard_map/ppermute | solution.py:47
  (2 other events, 1.3 us)

commit v8 on v7

v8 whole, which is shorter than its diff:
```python
import math

import jax
import jax.numpy as jnp
from jax import lax
from jax.experimental import pallas as pl
from jax.experimental.pallas import tpu as pltpu
from jax.sharding import PartitionSpec as P

HEAD_DIM = 128
EPSILON = 1e-05
SCALING = 1.0 / math.sqrt(HEAD_DIM)
CONTRACT_LAST = (((1,), (1,)), ((), ()))
CONTRACT_FIRST = (((0,), (0,)), ((), ()))
VMEM_LIMIT = 12 * 1024 * 1024
VMEM = pl.BlockSpec(memory_space=pltpu.VMEM)
SMEM = pl.BlockSpec(memory_space=pltpu.SMEM)
TILE = 512


def dot(left, right, dims=(((1,), (0,)), ((), ()))):
    return lax.dot_general(left, right, dims, preferred_element_type=jnp.float32)


def call(kernel, name, out_shape, operands, scratch=(), first=SMEM, rest=VMEM):
    single = not isinstance(out_shape, (list, tuple))
    shapes = [out_shape] if single else list(out_shape)
    results = pl.pallas_call(
        kernel,
        out_shape=shapes,
        in_specs=[first] + [rest] * (len(operands) - 1),
        out_specs=[VMEM] * len(shapes),
        scratch_shapes=list(scratch),
        compiler_params=pltpu.CompilerParams(vmem_limit_bytes=VMEM_LIMIT),
        cost_estimate=pl.CostEstimate(flops=1000, bytes_accessed=1000, transcendentals=0),
        name=name,
    )(*operands)
    return results[0] if single else results


def shape(dtype, *sizes):
    return jax.ShapeDtypeStruct(sizes, dtype)


def swap(array, mask, count):
    return lax.ppermute(array, "tensor", [(i, i ^ mask) for i in range(count)])


def block_start(order, slot, width):
    return pl.multiple_of(order[slot] * width, width)


def one_hot(places, rows):
    row = lax.broadcasted_iota(jnp.int32, (rows, places.shape[1]), 0)
    return jnp.where(places == row, 1.0, 0.0).astype(jnp.bfloat16)


def prepare_kernel(
    order,
    w_query,
    w_key,
    w_value,
    w_output,
    near_output,
    send,
    receive,
    segments,
    own_turned,
    near_turned,
    here,
    there,
    here_turned,
    there_turned,
    send_out,
    receive_out,
    segments_out,
):
    heads, width = w_output.shape[0], here.shape[1]
    for slot, out, turned in ((0, here, here_turned), (2, there, there_turned)):
        columns = pl.ds(block_start(order, slot, width), width)
        for part, weight in enumerate((w_output, near_output)):
            rows = slice(part * heads, (part + 1) * heads)
            block = weight[:, columns]
            out[rows, :] = block
            turned[:, rows] = block.T
    for source, target in ((send, send_out), (receive, receive_out), (segments, segments_out)):
        target[...] = source[...]
    for out, slots in ((own_turned, (0, 2)), (near_turned, (1, 3))):
        for part, slot in enumerate(slots):
            first = block_start(order, slot, width)
            for start in range(0, width, TILE):
                columns = slice(part * width + start, part * width + start + TILE)
                for place, weight in enumerate((w_query, w_key, w_value)):
                    rows = slice(place * HEAD_DIM, (place + 1) * HEAD_DIM)
                    out[rows, columns] = weight[pl.ds(first + start, TILE), :].T


def prepare(order, w_query, w_key, w_value, w_output, near_output, send, receive, segments, width):
    heads = w_query.shape[1]
    low = jnp.bfloat16
    return call(
        prepare_kernel,
        "prepare",
        [
            *[shape(low, 3 * heads, 2 * width)] * 2,
            *[shape(low, 2 * heads, width)] * 2,
            *[shape(low, width, 2 * heads)] * 2,
            shape(jnp.int32, *send.shape),
            shape(jnp.int32, *receive.shape),
            shape(jnp.int32, *segments.shape),
        ],
        (order, w_query, w_key, w_value, w_output, near_output, send, receive, segments),
    )


def sum_squares(block):
    wide = block[...].astype(jnp.float32)
    return jnp.sum(wide * wide, axis=-1, keepdims=True)


def begin_kernel(x0, x1, c0, here_turned, squares, part):
    squares[...] = sum_squares(x0) + sum_squares(x1)
    part[...] = dot(c0[...], here_turned[...])


def begin(x0, x1, c0, here_turned):
    rows, columns = x0.shape[0], here_turned.shape[1]
    shapes = [shape(jnp.float32, rows, 1), shape(jnp.float32, rows, columns)]
    return call(begin_kernel, "begin", shapes, (x0, x1, c0, here_turned), first=VMEM)


def add_grad_kernel(c2, there_turned, part, own_part, near_part):
    total = part[...] + dot(c2[...], there_turned[...])
    heads = own_part.shape[1]
    own_part[...] = total[:, :heads]
    near_part[...] = total[:, heads:]


def add_grad(c2, there_turned, part):
    shapes = [shape(jnp.float32, part.shape[0], part.shape[1] // 2)] * 2
    return call(add_grad_kernel, "add_grad", shapes, (c2, there_turned, part), first=VMEM)


def add_squares_kernel(x2, squares_in, squares):
    squares[...] = squares_in[...] + sum_squares(x2)


def add_squares(x2, squares):
    out = shape(jnp.float32, *squares.shape)
    return call(add_squares_kernel, "add_squares", out, (x2, squares), first=VMEM)


def project_kernel(
    order,
    x0,
    x1,
    x2,
    x3,
    gain_own,
    gain_near,
    w_query,
    w_key,
    w_value,
    squares,
    own_part,
    got_part,
    send,
    home,
    inverse,
    bucket,
    total,
):
    blocks = (x0, x1, x2, x3)
    width = x0.shape[1]
    mean = (squares[...] + sum_squares(x3)) / (width * len(blocks))
    inverse_rms = lax.rsqrt(mean + EPSILON)
    inverse[...] = inverse_rms
    head_grad = (own_part[...] + got_part[...]).astype(jnp.bfloat16)
    for index, block in enumerate(blocks):
        gain = (gain_own, gain_near)[index % 2][index // 2 : index // 2 + 1, :]
        scaled = block[...].astype(jnp.float32) * inverse_rms
        normed = (scaled * gain.astype(jnp.float32)).astype(jnp.bfloat16)
        here = pl.ds(block_start(order, index, width), width)
        weights = jnp.concatenate([w_query[here, :], w_key[here, :], w_value[here, :]], axis=1)
        product = dot(normed, weights)
        total[...] = total[...] + product if index else product
    rounded = total[...].astype(jnp.bfloat16)
    home[...] = rounded
    chosen = one_hot(send[...], rounded.shape[0])
    split = rounded.shape[1]
    bucket[:, :split] = dot(chosen, rounded, CONTRACT_FIRST).astype(jnp.bfloat16)
    bucket[:, split:] = dot(chosen, head_grad, CONTRACT_FIRST).astype(jnp.bfloat16)


def project(order, blocks, gains, weights, squares, own_part, got_part, send):
    rows = blocks[0].shape[0]
    columns = 3 * HEAD_DIM
    return call(
        project_kernel,
        "project",
        [
            shape(jnp.bfloat16, rows, columns),
            shape(jnp.float32, rows, 1),
            shape(jnp.bfloat16, send.shape[1], columns + HEAD_DIM),
        ],
        (order, *blocks, *gains, *weights, squares, own_part, got_part, send),
        scratch=[pltpu.VMEM((rows, columns), jnp.float32)],
    )


def attend_kernel(moved, receive, segments, back):
    place = one_hot(receive[...], moved.shape[0])
    rows = dot(place, moved[...], CONTRACT_FIRST).astype(jnp.bfloat16)
    queries, key_rows, value_rows, head_grad = (
        rows[:, index * HEAD_DIM : (index + 1) * HEAD_DIM] for index in range(4)
    )
    count = rows.shape[0]
    down = lax.broadcasted_iota(jnp.int32, (count, count), 0)
    across = lax.broadcasted_iota(jnp.int32, (count, count), 1)
    stays = segments[...]
    own_stay = jnp.sum(jnp.where(down == across, stays, 0), axis=1, keepdims=True)
    allowed = (own_stay == stays) & (across <= down)
    scores = jnp.where(allowed, dot(queries, key_rows, CONTRACT_LAST) * SCALING, -1e30)
    raised = jnp.exp(scores - jnp.max(scores, axis=-1, keepdims=True))
    softmax_out = raised / jnp.sum(raised, axis=-1, keepdims=True)
    low_weights = softmax_out.astype(jnp.bfloat16)
    attended = dot(low_weights, value_rows).astype(jnp.bfloat16)
    grad_value = dot(low_weights, head_grad, CONTRACT_FIRST).astype(jnp.bfloat16)
    grad_probs = dot(head_grad, value_rows, CONTRACT_LAST)
    inner = jnp.sum(softmax_out * grad_probs, axis=-1, keepdims=True)
    grad_scores = (softmax_out * (grad_probs - inner) * SCALING).astype(jnp.bfloat16)
    grad_query = dot(grad_scores, key_rows).astype(jnp.bfloat16)
    grad_key = dot(grad_scores, queries, CONTRACT_FIRST).astype(jnp.bfloat16)
    results = jnp.concatenate([grad_query, grad_key, grad_value, attended], axis=1)
    back[...] = dot(place, results).astype(jnp.bfloat16)


def attend(moved, receive, segments):
    out = shape(jnp.bfloat16, *moved.shape)
    return call(attend_kernel, "attend", out, (moved, receive, segments), first=VMEM)


def write_parts(value, out):
    out[...] = jnp.zeros_like(out)
    for place in range(3):
        low = value.astype(jnp.bfloat16)
        out[:, place : place + 1] = low
        value = value - low.astype(jnp.float32)


def read_parts(parts):
    return sum(parts[:, place : place + 1].astype(jnp.float32) for place in (2, 1, 0))


def bring_home_kernel(moved, send, home, grads, extras):
    chosen = one_hot(send[...], grads.shape[0])
    rows = dot(chosen, moved[...])
    split = 3 * HEAD_DIM
    grads[...] = rows[:, :split].astype(jnp.bfloat16)
    extras[:, :HEAD_DIM] = rows[:, split:].astype(jnp.bfloat16)
    product = rows[:, :split] * home[...].astype(jnp.float32)
    row_dot = jnp.sum(product, axis=-1, keepdims=True)
    write_parts(row_dot, extras.at[:, HEAD_DIM:])


def bring_home(moved, send, home):
    rows = home.shape[0]
    shapes = [shape(jnp.bfloat16, rows, 3 * HEAD_DIM), shape(jnp.bfloat16, rows, 2 * HEAD_DIM)]
    return call(bring_home_kernel, "bring_home", shapes, (moved, send, home), first=VMEM)


def spread_kernel(first):
    def kernel(own, near, weights, near_weights, out, held, total, sems):
        span = held.shape[1]
        copies = []
        for index, start in enumerate(range(0, span, TILE)):
            source = near_weights.at[:, pl.ds(first + start, TILE)]
            target = held.at[:, pl.ds(start, TILE)]
            copies.append(pltpu.make_async_copy(source, target, sems.at[index]))
            copies[-1].start()
        own_rows, near_rows = own[...], near[...]
        for start in range(0, span, TILE):
            columns = slice(first + start, first + start + TILE)
            total[:, start : start + TILE] = dot(own_rows, weights[:, columns])
        for index, start in enumerate(range(0, span, TILE)):
            copies[index].wait()
            tile = slice(start, start + TILE)
            result = total[:, tile] + dot(near_rows, held[:, tile])
            out[:, tile] = result.astype(out.dtype)

    return kernel


def spread(name, first, span, dtype, own, near, weights, near_weights):
    rows, depth = own.shape
    return pl.pallas_call(
        spread_kernel(first),
        out_shape=shape(dtype, rows, span),
        in_specs=[VMEM] * 3 + [pl.BlockSpec(memory_space=pl.ANY)],
        out_specs=VMEM,
        scratch_shapes=[
            pltpu.VMEM((depth, span), jnp.bfloat16),
            pltpu.VMEM((rows, span), jnp.float32),
            pltpu.SemaphoreType.DMA((span // TILE,)),
        ],
        compiler_params=pltpu.CompilerParams(vmem_limit_bytes=VMEM_LIMIT),
        cost_estimate=pl.CostEstimate(flops=1000, bytes_accessed=1000, transcendentals=0),
        name=name,
    )(own, near, weights, near_weights)


def finish_out_kernel(inputs, own, near, far, last, here, there, out):
    width = inputs.shape[1]
    chip = jnp.concatenate([own[:, :HEAD_DIM], near[:, :HEAD_DIM]], axis=1)
    other = jnp.concatenate([far[:, :HEAD_DIM], last[:, :HEAD_DIM]], axis=1)
    for start in range(0, width, TILE):
        tile = slice(start, start + TILE)
        total = dot(chip, here[:, tile]) + dot(other, there[:, tile])
        out[:, tile] = (inputs[:, tile].astype(jnp.float32) + total).astype(jnp.bfloat16)


def finish_most_kernel(
    inputs, cotangent, gain, inverse, own, near, far, last, grad_own, got, middle, *outs
):
    out, left, held, sem = outs
    row_dot = sum(read_parts(extras[:, HEAD_DIM:]) for extras in (own, near, far, last))
    mean_dot = row_dot / (4 * inputs.shape[1])
    inverse_rms = inverse[...]
    most = held.shape[1]
    for start in range(0, inputs.shape[1], TILE):
        tile = slice(start, start + TILE)
        grad_normed = grad_own[:, tile]
        if start < got.shape[1]:
            grad_normed = grad_normed + got[:, tile].astype(jnp.float32)
        elif start < most:
            part = slice(start - got.shape[1], start - got.shape[1] + TILE)
            grad_normed = grad_normed + middle[:, part].astype(jnp.float32)
        grad_hat = grad_normed * gain[:, tile].astype(jnp.float32)
        scaled = inputs[:, tile].astype(jnp.float32) * inverse_rms
        change = inverse_rms * (grad_hat - scaled * mean_dot)
        result = cotangent[:, tile].astype(jnp.float32) + change
        if start < most:
            held[:, tile] = result.astype(jnp.bfloat16)
        else:
            left[:, start - most : start - most + TILE] = result
    copy = pltpu.make_async_copy(held, out.at[:, pl.ds(0, most)], sem)
    copy.start()
    copy.wait()


def finish_rest_kernel(gain, inverse, left, rest, before, out, held, sem):
    span = rest.shape[1]
    first = out.shape[1] - span
    for start in range(0, span, TILE):
        tile = slice(start, start + TILE)
        columns = slice(first + start, first + start + TILE)
        grad_hat = rest[:, tile].astype(jnp.float32) * gain[:, columns].astype(jnp.float32)
        held[:, tile] = (left[:, tile] + inverse[...] * grad_hat).astype(jnp.bfloat16)
    copy = pltpu.make_async_copy(held, out.at[:, pl.ds(first, span)], sem)
    copy.start()
    copy.wait()


def finish_grad(inputs, cotangent, gain, inverse, extras, grad_own, got, middle, rest):
    rows, width = inputs.shape
    span = rest.shape[1]
    hbm = pl.BlockSpec(memory_space=pltpu.HBM)
    options = dict(
        compiler_params=pltpu.CompilerParams(vmem_limit_bytes=VMEM_LIMIT),
        cost_estimate=pl.CostEstimate(flops=1000, bytes_accessed=1000, transcendentals=0),
    )
    begun, left = pl.pallas_call(
        finish_most_kernel,
        out_shape=[shape(jnp.bfloat16, rows, width), shape(jnp.float32, rows, span)],
        in_specs=[VMEM] * 11,
        out_specs=[hbm, VMEM],
        scratch_shapes=[pltpu.VMEM((rows, width - span), jnp.bfloat16), pltpu.SemaphoreType.DMA],
        name="finish_most",
        **options,
    )(inputs, cotangent, gain, inverse, *extras, grad_own, got, middle)
    return pl.pallas_call(
        finish_rest_kernel,
        out_shape=shape(jnp.bfloat16, rows, width),
        in_specs=[VMEM] * 4 + [hbm],
        out_specs=hbm,
        scratch_shapes=[pltpu.VMEM((rows, span), jnp.bfloat16), pltpu.SemaphoreType.DMA],
        input_output_aliases={4: 0},
        name="finish_rest",
        **options,
    )(gain, inverse, left, rest, begun)


def move(bucket):
    return lax.all_to_all(bucket, "dp", split_axis=0, concat_axis=0, tiled=True)


def after(array, *others):
    return lax.optimization_barrier((array, *others))[0]


def on_device(
    inputs,
    cotangent,
    norm_gain,
    w_query,
    w_key,
    w_value,
    w_output,
    send_rows,
    receive_slots,
    owner_segments,
):
    rows, width = inputs.shape
    tensor = lax.axis_size("tensor")
    low = jnp.bfloat16
    order = lax.axis_index("tensor").astype(jnp.int32) ^ jnp.arange(4, dtype=jnp.int32)
    gain = norm_gain.reshape(1, width)

    x2 = swap(inputs, 2, tensor)
    c2 = swap(cotangent, 2, tensor)
    gain2 = swap(gain, 2, tensor)
    x1 = swap(inputs, 1, tensor)
    near_output = swap(w_output, 1, tensor)
    weights = (w_query, w_key, w_value)
    own_turned, near_turned, here, there, here_turned, there_turned, *indices = prepare(
        order,
        *weights,
        w_output,
        near_output,
        send_rows,
        receive_slots.reshape(1, rows),
        owner_segments.reshape(1, rows),
        width,
    )
    send, receive, segments = indices
    squares, part = begin(inputs, x1, cotangent, here_turned)

    x2, c2, gain2, squares, part = lax.optimization_barrier((x2, c2, gain2, squares, part))
    x3 = swap(x2, 1, tensor)
    gain_own = jnp.concatenate([gain, gain2], axis=0)
    gain_near = swap(gain_own, 1, tensor)
    own_part, near_part = add_grad(c2, there_turned, part)
    got_part = swap(near_part, 1, tensor)
    squares = add_squares(x2, squares)
    home, inverse_rms, bucket = project(
        order,
        (inputs, x1, x2, x3),
        (gain_own, gain_near),
        weights,
        squares,
        own_part,
        got_part,
        send,
    )
    near_turned = swap(after(near_turned, home), 1, tensor)
    there = swap(after(there, home), 2, tensor)
    back = attend(move(bucket), receive, segments)
    own, own_extras = bring_home(move(back), send, home)

    near = swap(own, 1, tensor)
    far_extras = swap(own_extras, 2, tensor)
    quarter = width // 4
    turn, got = own, []
    for first, span in ((0, 2 * quarter), (2 * quarter, quarter), (3 * quarter, quarter)):
        part = spread("spread_far", width + first, span, low, turn, near, own_turned, near_turned)
        got.append(swap(part if first else after(part, far_extras), 2, tensor))
        turn = after(own, part)
    grad_own = spread("spread_own", 0, width, jnp.float32, turn, near, own_turned, near_turned)
    extras = (own_extras, swap(own_extras, 1, tensor), far_extras, swap(far_extras, 1, tensor))
    layer_out = call(
        finish_out_kernel,
        "finish_out",
        shape(low, rows, width),
        (inputs, *extras, here, there),
        first=VMEM,
    )
    got[1] = after(got[1], layer_out)
    input_grad = finish_grad(inputs, cotangent, gain, inverse_rms, extras, grad_own, *got)
    return (layer_out, input_grad)


def solution(mesh):
    return jax.shard_map(
        on_device,
        mesh=mesh,
        in_specs=(
            P("dp", "tensor"),
            P("dp", "tensor"),
            P("tensor"),
            P(None, "tensor"),
            P(None, "tensor"),
            P(None, "tensor"),
            P("tensor", None),
            P("dp", None),
            P("dp"),
            P("dp"),
        ),
        out_specs=(P("dp", "tensor"), P("dp", "tensor")),
        check_vma=False,
    )
```

time: 79 us -> 78.7 us (level)
    ppermute x15 -> x17, starting transfers between devices: 11.1 us -> 11.5 us  [swap(): return lax.ppermute(array, 'tensor', [(i, i ^ mask) for i in range(count)])]
    ppermute x15 -> x17, waiting for transfers between devices: 20.1 us -> 19.7 us  [swap(): return lax.ppermute(array, 'tensor', [(i, i ^ mask) for i in range(count)])]
    pallas_call x7 -> x8, Pallas kernels: 9.73 us -> 9.61 us  [call(): pl.pallas_call(kernel, out_shape=shapes, in_specs=[first] + [rest] * (len...]
  transfers between devices with their start and end apart: 15 -> 17, of which waited for: 6 -> 7; matrix products, arithmetic and copies ran while one was open for 1% -> 1% of each run, Pallas kernels for 15% -> 15%
where the time goes in v8:
time: 78.7 us; the launch traced here: 78.3 us
  blocking collectives  22.7 us (29%)
  waiting for transfers between devices  19.7 us (25%)
  Pallas kernels  14.6 us (19%)
  starting transfers between devices  11.5 us (15%)
  local copies, waits for them, and re-layouts  9.04 us (11%)
  between operations  0.8 us (1%)
    all_to_all x2, blocking collectives, move(): return lax.all_to_all(bucket, 'dp', split_axis=0, concat_axis=0, tiled=True)  22.7 us
    ppermute x17, waiting for transfers between devices, swap(): return lax.ppermute(array, 'tensor', [(i, i ^ mask) for i in range(count)])  19.7 us
    ppermute x17, starting transfers between devices, swap(): return lax.ppermute(array, 'tensor', [(i, i ^ mask) for i in range(count)])  11.5 us
    pallas_call x8, Pallas kernels, call(): pl.pallas_call(kernel, out_shape=shapes, in_specs=[first] + [rest] * (len...  9.61 us
    unnamed x22, local copies, waits for them, and re-layouts  8.35 us
    pallas_call x4, Pallas kernels, spread(): pl.pallas_call(spread_kernel(first), out_shape=shape(dtype, rows, span),...  2.94 us
  transfers between devices with their start and end apart: 17, of which 7 were waited for; matrix products, arithmetic and copies ran while one was open for 1% of the time, Pallas kernels for 15%

profile of v8, /device:TPU:0, one launch (start us, length us, event | category | flops | bytes accessed | tf_op | source)
XLA Modules:
  0.0 78.3 jit_solution(7268425277385130965)
XLA Ops:
  1.2 2.9 %collective-permute-start.1 = (bf16[128,2048]{1,0:T(8,128)(2,1)}, bf16[128,2048]{1,0:T(8,128)(2,1)S(1)}, u32[]{:S(2)}, u32[]{:S(2)}) collective-permute-start(bf16[128,2048]{1,0:T(8,128)(2,1)} %inputs.3), channel_id=1, source_target_pairs={{0,2},{1,3},{2,0},{3,1},{4,6},{5,7},{6,4},{7,5},{8,10},{9,11},{10,... | collective-permute-start | bytes 1572872 | tf_op jit(solution)/shard_map/ppermute | solution.py:46
  4.9 2.0 %collective-permute-start.3 = (bf16[1,2048]{1,0:T(2,128)(2,1)S(1)}, bf16[1,2048]{1,0:T(2,128)(2,1)S(1)}, u32[]{:S(2)}, u32[]{:S(2)}) collective-permute-start(bf16[1,2048]{1,0:T(2,128)(2,1)S(1)} %reshape.17.gain), channel_id=1, source_target_pairs={{0,2},{1,3},{2,0},{3,1},{4,6},{5,7},{6,4},{7,5},{8,10},{9,11},{10,... | collective-permute-start | bytes 12296 | tf_op jit(solution)/shard_map/ppermute | solution.py:46
  6.9 1.6 %copy-done = bf16[8192,128]{1,0:T(8,128)(2,1)S(1)} copy-done((bf16[8192,128]{1,0:T(8,128)(2,1)S(1)}, bf16[8192,128]{1,0:T(8,128)(2,1)}, u32[]{:S(2)}) %copy-start) | copy-done | bytes 2097176
  8.5 1.6 %copy-done.2 = bf16[8192,128]{1,0:T(8,128)(2,1)S(1)} copy-done((bf16[8192,128]{1,0:T(8,128)(2,1)S(1)}, bf16[8192,128]{1,0:T(8,128)(2,1)}, u32[]{:S(2)}) %copy-start.2) | copy-done | bytes 2097176
  10.1 1.6 %copy-done.4 = bf16[8192,128]{1,0:T(8,128)(2,1)S(1)} copy-done((bf16[8192,128]{1,0:T(8,128)(2,1)S(1)}, bf16[8192,128]{1,0:T(8,128)(2,1)}, u32[]{:S(2)}) %copy-start.4) | copy-done | bytes 2097176
  11.7 1.6 %copy-done.7 = bf16[128,8192]{1,0:T(8,128)(2,1)S(1)} copy-done((bf16[128,8192]{1,0:T(8,128)(2,1)S(1)}, bf16[128,8192]{1,0:T(8,128)(2,1)}, u32[]{:S(2)}) %copy-start.7) | copy-done | bytes 2097176
  15.2 2.8 %prepare.1 = (bf16[384,4096]{1,0:T(8,128)(2,1)S(1)}, bf16[384,4096]{1,0:T(8,128)(2,1)S(1)}, bf16[256,2048]{1,0:T(8,128)(2,1)S(1)}, bf16[256,2048]{1,0:T(8,128)(2...) custom-call(s32[4]{0:T(128)S(1)} %iota_xor_fusion.order, ...), custom_call_target="tpu_custom_call" | custom-call | flops 1000 | bytes 1000 | tf_op jit(solution)/shard_map/prepare/pallas_call | solution.py:28
  18.5 9.5 %collective-permute-done.3 = bf16[1,2048]{1,0:T(2,128)(2,1)S(1)} collective-permute-done((bf16[1,2048]{1,0:T(2,128)(2,1)S(1)}, bf16[1,2048]{1,0:T(2,128)(2,1)S(1)}, u32[]{:S(2)}, u32[]{:S(2)}) %collective-permute-start.3) | collective-permute-done | bytes 4128 | tf_op jit(solution)/shard_map/ppermute | solution.py:46
  28.0 1.4 %add_grad.1 = (f32[128,128]{1,0:T(8,128)S(1)}, f32[128,128]{1,0:T(8,128)S(1)}) custom-call(bf16[128,2048]{1,0:T(8,128)(2,1)} %collective-permute-done.2.c2, bf16[2048,256]{1,0:T(8,128)(2,1)S(1)} %get-tuple-element.41.there_turned, f32[128,256]{1,0:T(8,128)S(1)} %get-tuple-element.42.part), custom_call_target="tpu_custom_call" | custom-call | flops 1000 | bytes 1000 | tf_op jit(solution)/shard_map/add_grad/pallas_call | solution.py:28
  30.2 1.0 %collective-permute-done.6.gain_near = bf16[2,2048]{1,0:T(2,128)(2,1)S(1)} collective-permute-done((bf16[2,2048]{1,0:T(2,128)(2,1)S(1)}, bf16[2,2048]{1,0:T(2,128)(2,1)S(1)}, u32[]{:S(2)}, u32[]{:S(2)}) %collective-permute-start.6) | collective-permute-done | bytes 8224 | tf_op jit(solution)/shard_map/ppermute | solution.py:46
  31.2 2.2 %project.1 = (bf16[128,384]{1,0:T(8,128)(2,1)S(1)}, f32[128,1]{1,0:T(8,128)S(1)}, bf16[128,512]{1,0:T(8,128)(2,1)S(1)}) custom-call(s32[4]{0:T(128)S(1)} %iota_xor_fusion.order, bf16[128,2048]{1,0:T(8,128)(2,1)S(1)} %copy-done.5, bf16[128,2048]{1,0:T(8,128)(2,1)S(1)} %collective-permute-done.x1, bf16[128,2048]{1,0:T(8,128)(2,1)S(1)} %collective-permute-done.1.x2, ...), custom_call_target="tpu_custom_call" | custom-call | flops 1000 | bytes 1000 | tf_op jit(solution)/shard_map/project/pallas_call | solution.py:28
  33.7 1.7 %collective-permute-start.11 = (bf16[256,2048]{1,0:T(8,128)(2,1)S(1)}, bf16[256,2048]{1,0:T(8,128)(2,1)S(1)}, u32[]{:S(2)}, u32[]{:S(2)}) collective-permute-start(bf16[256,2048]{1,0:T(8,128)(2,1)S(1)} %get-tuple-element.53), channel_id=1, source_target_pairs={{0,2},{1,3},{2,0},{3,1},{4,6},{5,7},{6,4},{7,5},{8,10},{9,11},{10,... | collective-permute-start | bytes 3145736 | tf_op jit(solution)/shard_map/ppermute | solution.py:46
  35.4 12.9 %all_to_all.22 = bf16[8,16,512]{2,1,0:T(8,128)(2,1)S(1)} all-to-all(bf16[8,16,512]{2,1,0:T(8,128)(2,1)S(1)} %bitcast.9), channel_id=1, replica_groups=mesh['dp'=8,'tensor'=4] {'dp'}, dimensions={0} | all-to-all | bytes 262144 | tf_op jit(solution)/shard_map/all_to_all | solution.py:394
  48.4 1.1 %attend.1 = bf16[128,512]{1,0:T(8,128)(2,1)S(1)} custom-call(bf16[128,512]{1,0:T(8,128)(2,1)S(1)} %bitcast.7, s32[1,128]{1,0:T(1,128)S(1)} %get-tuple-element.47.receive, s32[1,128]{1,0:T(1,128)S(1)} %get-tuple-element.48.segments), custom_call_target="tpu_custom_call" | custom-call | flops 1000 | bytes 1000 | tf_op jit(solution)/shard_map/attend/pallas_call | solution.py:28
  49.5 9.7 %all_to_all.23 = bf16[8,16,512]{2,1,0:T(8,128)(2,1)S(1)} all-to-all(bf16[8,16,512]{2,1,0:T(8,128)(2,1)S(1)} %bitcast.8), channel_id=1, replica_groups=mesh['dp'=8,'tensor'=4] {'dp'}, dimensions={0} | all-to-all | bytes 262144 | tf_op jit(solution)/shard_map/all_to_all | solution.py:394
  60.8 0.8 spread_far.3
  61.6 2.5 %collective-permute-done.9.far = bf16[128,256]{1,0:T(8,128)(2,1)S(1)} collective-permute-done((bf16[128,256]{1,0:T(8,128)(2,1)S(1)}, bf16[128,256]{1,0:T(8,128)(2,1)S(1)}, u32[]{:S(2)}, u32[]{:S(2)}) %collective-permute-start.9) | collective-permute-done | bytes 65568 | tf_op jit(solution)/shard_map/ppermute | solution.py:46
  65.0 1.6 %collective-permute-start.15 = (bf16[128,512]{1,0:T(8,128)(2,1)S(1)}, bf16[128,512]{1,0:T(8,128)(2,1)S(1)}, u32[]{:S(2)}, u32[]{:S(2)}) collective-permute-start(bf16[128,512]{1,0:T(8,128)(2,1)S(1)} %spread_far.4), channel_id=1, source_target_pairs={{0,2},{1,3},{2,0},{3,1},{4,6},{5,7},{6,4},{7,5},{8,10},{9,11},{10,... | collective-permute-start | bytes 393224 | tf_op jit(solution)/shard_map/ppermute | solution.py:46
  67.5 1.3 %collective-permute-done.10.last = bf16[128,256]{1,0:T(8,128)(2,1)S(1)} collective-permute-done((bf16[128,256]{1,0:T(8,128)(2,1)S(1)}, bf16[128,256]{1,0:T(8,128)(2,1)S(1)}, u32[]{:S(2)}, u32[]{:S(2)}) %collective-permute-start.10) | collective-permute-done | bytes 65568 | tf_op jit(solution)/shard_map/ppermute | solution.py:46
  68.8 1.3 %finish_out.1 = bf16[128,2048]{1,0:T(8,128)(2,1)} custom-call(bf16[128,2048]{1,0:T(8,128)(2,1)S(1)} %copy-done.5, bf16[128,256]{1,0:T(8,128)(2,1)S(1)} %get-tuple-element.50.own, bf16[128,256]{1,0:T(8,128)(2,1)S(1)} %collective-permute-done.8.near, bf16[128,256]{1,0:T(8,128)(2,1)S(1)} %collective-permute-done.9.far, ...), custom_call_target="tpu_custom_call" | custom-call | flops 1000 | bytes 1000 | tf_op jit(solution)/shard_map/finish_out/pallas_call | solution.py:28
  70.1 1.4 %spread_own.1.grad_own = f32[128,2048]{1,0:T(8,128)S(1)} custom-call(bf16[128,384]{1,0:T(8,128)(2,1)S(1)} %get-tuple-element.61.own, bf16[128,384]{1,0:T(8,128)(2,1)S(1)} %collective-permute-done.12.near, bf16[384,4096]{1,0:T(8,128)(2,1)S(1)} %get-tuple-element.56.weights, bf16[384,4096]{1,0:T(8,128)(2,1)S(1)} %collective-permute-done.13.near_weights), custom_call_target="tpu_custom_call" | custom-call | flops 1000 | bytes 1000 | tf_op jit(solution)/shard_map/spread_own/pallas_call | solution.py:296
  71.5 4.6 %collective-permute-done.15.middle = bf16[128,512]{1,0:T(8,128)(2,1)S(1)} collective-permute-done((bf16[128,512]{1,0:T(8,128)(2,1)S(1)}, bf16[128,512]{1,0:T(8,128)(2,1)S(1)}, u32[]{:S(2)}, u32[]{:S(2)}) %collective-permute-start.15) | collective-permute-done | bytes 131104 | tf_op jit(solution)/shard_map/ppermute | solution.py:46
  76.1 1.3 %finish_most.1 = (bf16[128,2048]{1,0:T(8,128)(2,1)}, f32[128,512]{1,0:T(8,128)S(1)}) custom-call(bf16[128,2048]{1,0:T(8,128)(2,1)S(1)} %copy-done.5, bf16[128,2048]{1,0:T(8,128)(2,1)S(1)} %copy-done.6, bf16[1,2048]{1,0:T(2,128)(2,1)S(1)} %reshape.17.gain, f32[128,1]{1,0:T(8,128)S(1)} %get-tuple-element.54.inverse, ...), custom_call_target="tpu_custom_call" | custom-call | flops 1000 | bytes 1000 | tf_op jit(solution)/shard_map/finish_most/pallas_call | solution.py:372
  77.5 0.8 finish_rest.1
  (51 shorter events, 8.6 us)
Async XLA Ops:
  0.6 6.3 %collective-permute-start.4 = (bf16[128,8192]{1,0:T(8,128)(2,1)}, bf16[128,8192]{1,0:T(8,128)(2,1)S(1)}, u32[]{:S(2)}, u32[]{:S(2)}) collective-permute-start(bf16[128,8192]{1,0:T(8,128)(2,1)} %w_output.1), channel_id=1, source_target_pairs={{0,1},{1,0},{2,3},{3,2},{4,5},{5,4},{6,7},{7,6},{8,9},{9,8},{10,11... | collective-permute-start | bytes 6291464 | tf_op jit(solution)/shard_map/ppermute | solution.py:46
  1.1 16.9 %collective-permute-start = (bf16[128,2048]{1,0:T(8,128)(2,1)}, bf16[128,2048]{1,0:T(8,128)(2,1)S(1)}, u32[]{:S(2)}, u32[]{:S(2)}) collective-permute-start(bf16[128,2048]{1,0:T(8,128)(2,1)} %inputs.3), channel_id=1, source_target_pairs={{0,1},{1,0},{2,3},{3,2},{4,5},{5,4},{6,7},{7,6},{8,9},{9,8},{10,11... | collective-permute-start | bytes 1572872 | tf_op jit(solution)/shard_map/ppermute | solution.py:46
  1.2 26.8 %collective-permute-start.1 = (bf16[128,2048]{1,0:T(8,128)(2,1)}, bf16[128,2048]{1,0:T(8,128)(2,1)S(1)}, u32[]{:S(2)}, u32[]{:S(2)}) collective-permute-start(bf16[128,2048]{1,0:T(8,128)(2,1)} %inputs.3), channel_id=1, source_target_pairs={{0,2},{1,3},{2,0},{3,1},{4,6},{5,7},{6,4},{7,5},{8,10},{9,11},{10,... | collective-permute-start | bytes 1572872 | tf_op jit(solution)/shard_map/ppermute | solution.py:46
  4.2 23.8 %collective-permute-start.2 = (bf16[128,2048]{1,0:T(8,128)(2,1)}, bf16[128,2048]{1,0:T(8,128)(2,1)}, u32[]{:S(2)}, u32[]{:S(2)}) collective-permute-start(bf16[128,2048]{1,0:T(8,128)(2,1)} %cotangent.1), channel_id=1, source_target_pairs={{0,2},{1,3},{2,0},{3,1},{4,6},{5,7},{6,4},{7,5},{8,10},{9,11},{10,... | collective-permute-start | bytes 1572872 | tf_op jit(solution)/shard_map/ppermute | solution.py:46
  4.9 23.1 %collective-permute-start.3 = (bf16[1,2048]{1,0:T(2,128)(2,1)S(1)}, bf16[1,2048]{1,0:T(2,128)(2,1)S(1)}, u32[]{:S(2)}, u32[]{:S(2)}) collective-permute-start(bf16[1,2048]{1,0:T(2,128)(2,1)S(1)} %reshape.17.gain), channel_id=1, source_target_pairs={{0,2},{1,3},{2,0},{3,1},{4,6},{5,7},{6,4},{7,5},{8,10},{9,11},{10,... | collective-permute-start | bytes 12296 | tf_op jit(solution)/shard_map/ppermute | solution.py:46
  6.9 1.6 %copy-start = (bf16[8192,128]{1,0:T(8,128)(2,1)S(1)}, bf16[8192,128]{1,0:T(8,128)(2,1)}, u32[]{:S(2)}) copy-start(bf16[8192,128]{1,0:T(8,128)(2,1)} %w_query.3) | copy-start | bytes 6291460
  8.5 1.6 %copy-start.2 = (bf16[8192,128]{1,0:T(8,128)(2,1)S(1)}, bf16[8192,128]{1,0:T(8,128)(2,1)}, u32[]{:S(2)}) copy-start(bf16[8192,128]{1,0:T(8,128)(2,1)} %w_key.3) | copy-start | bytes 6291460
  10.1 1.6 %copy-start.4 = (bf16[8192,128]{1,0:T(8,128)(2,1)S(1)}, bf16[8192,128]{1,0:T(8,128)(2,1)}, u32[]{:S(2)}) copy-start(bf16[8192,128]{1,0:T(8,128)(2,1)} %w_value.3) | copy-start | bytes 6291460
  15.2 2.8 %copy-start.5 = (bf16[128,2048]{1,0:T(8,128)(2,1)S(1)}, bf16[128,2048]{1,0:T(8,128)(2,1)}, u32[]{:S(2)}) copy-start(bf16[128,2048]{1,0:T(8,128)(2,1)} %inputs.3) | copy-start | bytes 1572868
  15.2 2.8 %copy-start.6 = (bf16[128,2048]{1,0:T(8,128)(2,1)S(1)}, bf16[128,2048]{1,0:T(8,128)(2,1)}, u32[]{:S(2)}) copy-start(bf16[128,2048]{1,0:T(8,128)(2,1)} %cotangent.1) | copy-start | bytes 1572868
  18.1 13.1 %copy-start.1 = (bf16[8192,128]{1,0:T(8,128)(2,1)S(1)}, bf16[8192,128]{1,0:T(8,128)(2,1)}, u32[]{:S(2)}) copy-start(bf16[8192,128]{1,0:T(8,128)(2,1)} %w_query.3) | copy-start | bytes 6291460
  18.1 13.1 %copy-start.3 = (bf16[8192,128]{1,0:T(8,128)(2,1)S(1)}, bf16[8192,128]{1,0:T(8,128)(2,1)}, u32[]{:S(2)}) copy-start(bf16[8192,128]{1,0:T(8,128)(2,1)} %w_key.3) | copy-start | bytes 6291460
  28.0 3.2 %collective-permute-start.5 = (bf16[128,2048]{1,0:T(8,128)(2,1)S(1)}, bf16[128,2048]{1,0:T(8,128)(2,1)S(1)}, u32[]{:S(2)}, u32[]{:S(2)}) collective-permute-start(bf16[128,2048]{1,0:T(8,128)(2,1)S(1)} %collective-permute-done.1.x2), channel_id=1, source_target_pairs={{0,1},{1,0},{2,3},{3,2},{4,5},{5,4},{6,7},{7,6},{8,9},{9,8},{10,11... | collective-permute-start | bytes 1572872 | tf_op jit(solution)/shard_map/ppermute | solution.py:46
  29.4 1.8 %collective-permute-start.7 = (f32[128,128]{1,0:T(8,128)S(1)}, f32[128,128]{1,0:T(8,128)S(1)}, u32[]{:S(2)}, u32[]{:S(2)}) collective-permute-start(f32[128,128]{1,0:T(8,128)S(1)} %get-tuple-element.44), channel_id=1, source_target_pairs={{0,1},{1,0},{2,3},{3,2},{4,5},{5,4},{6,7},{7,6},{8,9},{9,8},{10,11... | collective-permute-start | bytes 196616 | tf_op jit(solution)/shard_map/ppermute | solution.py:46
  29.9 1.2 %collective-permute-start.6 = (bf16[2,2048]{1,0:T(2,128)(2,1)S(1)}, bf16[2,2048]{1,0:T(2,128)(2,1)S(1)}, u32[]{:S(2)}, u32[]{:S(2)}) collective-permute-start(bf16[2,2048]{1,0:T(2,128)(2,1)S(1)} %pad_maximum_fusion.gain_own), channel_id=1, source_target_pairs={{0,1},{1,0},{2,3},{3,2},{4,5},{5,4},{6,7},{7,6},{8,9},{9,8},{10,11... | collective-permute-start | bytes 24584 | tf_op jit(solution)/shard_map/ppermute | solution.py:46
  33.5 27.4 %collective-permute-start.13 = (bf16[384,4096]{1,0:T(8,128)(2,1)S(1)}, bf16[384,4096]{1,0:T(8,128)(2,1)S(1)}, u32[]{:S(2)}, u32[]{:S(2)}) collective-permute-start(bf16[384,4096]{1,0:T(8,128)(2,1)S(1)} %get-tuple-element.58), channel_id=1, source_target_pairs={{0,1},{1,0},{2,3},{3,2},{4,5},{5,4},{6,7},{7,6},{8,9},{9,8},{10,11... | collective-permute-start | bytes 9437192 | tf_op jit(solution)/shard_map/ppermute | solution.py:46
  33.7 35.1 %collective-permute-start.11 = (bf16[256,2048]{1,0:T(8,128)(2,1)S(1)}, bf16[256,2048]{1,0:T(8,128)(2,1)S(1)}, u32[]{:S(2)}, u32[]{:S(2)}) collective-permute-start(bf16[256,2048]{1,0:T(8,128)(2,1)S(1)} %get-tuple-element.53), channel_id=1, source_target_pairs={{0,2},{1,3},{2,0},{3,1},{4,6},{5,7},{6,4},{7,5},{8,10},{9,11},{10,... | collective-permute-start | bytes 3145736 | tf_op jit(solution)/shard_map/ppermute | solution.py:46
  59.5 1.4 %collective-permute-start.12 = (bf16[128,384]{1,0:T(8,128)(2,1)S(1)}, bf16[128,384]{1,0:T(8,128)(2,1)S(1)}, u32[]{:S(2)}, u32[]{:S(2)}) collective-permute-start(bf16[128,384]{1,0:T(8,128)(2,1)S(1)} %get-tuple-element.61.own), channel_id=1, source_target_pairs={{0,1},{1,0},{2,3},{3,2},{4,5},{5,4},{6,7},{7,6},{8,9},{9,8},{10,11... | collective-permute-start | bytes 294920 | tf_op jit(solution)/shard_map/ppermute | solution.py:46
  59.5 4.5 %collective-permute-start.9 = (bf16[128,256]{1,0:T(8,128)(2,1)S(1)}, bf16[128,256]{1,0:T(8,128)(2,1)S(1)}, u32[]{:S(2)}, u32[]{:S(2)}) collective-permute-start(bf16[128,256]{1,0:T(8,128)(2,1)S(1)} %get-tuple-element.50.own), channel_id=1, source_target_pairs={{0,2},{1,3},{2,0},{3,1},{4,6},{5,7},{6,4},{7,5},{8,10},{9,11},{10,... | collective-permute-start | bytes 196616 | tf_op jit(solution)/shard_map/ppermute | solution.py:46
  64.0 12.0 %collective-permute-start.14 = (bf16[128,1024]{1,0:T(8,128)(2,1)S(1)}, bf16[128,1024]{1,0:T(8,128)(2,1)S(1)}, u32[]{:S(2)}, u32[]{:S(2)}) collective-permute-start(bf16[128,1024]{1,0:T(8,128)(2,1)S(1)} %spread_far.3), channel_id=1, source_target_pairs={{0,2},{1,3},{2,0},{3,1},{4,6},{5,7},{6,4},{7,5},{8,10},{9,11},{10,... | collective-permute-start | bytes 786440 | tf_op jit(solution)/shard_map/ppermute | solution.py:46
  64.6 3.0 %collective-permute-start.8 = (bf16[128,256]{1,0:T(8,128)(2,1)S(1)}, bf16[128,256]{1,0:T(8,128)(2,1)S(1)}, u32[]{:S(2)}, u32[]{:S(2)}) collective-permute-start(bf16[128,256]{1,0:T(8,128)(2,1)S(1)} %get-tuple-element.50.own), channel_id=1, source_target_pairs={{0,1},{1,0},{2,3},{3,2},{4,5},{5,4},{6,7},{7,6},{8,9},{9,8},{10,11... | collective-permute-start | bytes 196616 | tf_op jit(solution)/shard_map/ppermute | solution.py:46
  65.0 11.1 %collective-permute-start.15 = (bf16[128,512]{1,0:T(8,128)(2,1)S(1)}, bf16[128,512]{1,0:T(8,128)(2,1)S(1)}, u32[]{:S(2)}, u32[]{:S(2)}) collective-permute-start(bf16[128,512]{1,0:T(8,128)(2,1)S(1)} %spread_far.4), channel_id=1, source_target_pairs={{0,2},{1,3},{2,0},{3,1},{4,6},{5,7},{6,4},{7,5},{8,10},{9,11},{10,... | collective-permute-start | bytes 393224 | tf_op jit(solution)/shard_map/ppermute | solution.py:46
  66.9 10.6 %collective-permute-start.16 = (bf16[128,512]{1,0:T(8,128)(2,1)S(1)}, bf16[128,512]{1,0:T(8,128)(2,1)S(1)}, u32[]{:S(2)}, u32[]{:S(2)}) collective-permute-start(bf16[128,512]{1,0:T(8,128)(2,1)S(1)} %spread_far.5), channel_id=1, source_target_pairs={{0,2},{1,3},{2,0},{3,1},{4,6},{5,7},{6,4},{7,5},{8,10},{9,11},{10,... | collective-permute-start | bytes 393224 | tf_op jit(solution)/shard_map/ppermute | solution.py:46
  67.5 1.3 %collective-permute-start.10 = (bf16[128,256]{1,0:T(8,128)(2,1)S(1)}, bf16[128,256]{1,0:T(8,128)(2,1)S(1)}, u32[]{:S(2)}, u32[]{:S(2)}) collective-permute-start(bf16[128,256]{1,0:T(8,128)(2,1)S(1)} %collective-permute-done.9.far), channel_id=1, source_target_pairs={{0,1},{1,0},{2,3},{3,2},{4,5},{5,4},{6,7},{7,6},{8,9},{9,8},{10,11... | collective-permute-start | bytes 196616 | tf_op jit(solution)/shard_map/ppermute | solution.py:46
  (4 other events, 3.6 us)

commit v9 on v8

--- a/solution.py
+++ b/solution.py
@@ -12,7 +12,7 @@
 SCALING = 1.0 / math.sqrt(HEAD_DIM)
 CONTRACT_LAST = (((1,), (1,)), ((), ()))
 CONTRACT_FIRST = (((0,), (0,)), ((), ()))
-VMEM_LIMIT = 12 * 1024 * 1024
+VMEM_LIMIT = 6 * 1024 * 1024
 VMEM = pl.BlockSpec(memory_space=pltpu.VMEM)
 SMEM = pl.BlockSpec(memory_space=pltpu.SMEM)
 TILE = 512
@@ -291,7 +291,7 @@
     return kernel
 
 
-def spread(name, first, span, dtype, own, near, weights, near_weights):
+def spread(name, first, span, dtype, own, near, weights, near_weights, flops=1000):
     rows, depth = own.shape
     return pl.pallas_call(
         spread_kernel(first),
@@ -304,7 +304,7 @@
             pltpu.SemaphoreType.DMA((span // TILE,)),
         ],
         compiler_params=pltpu.CompilerParams(vmem_limit_bytes=VMEM_LIMIT),
-        cost_estimate=pl.CostEstimate(flops=1000, bytes_accessed=1000, transcendentals=0),
+        cost_estimate=pl.CostEstimate(flops=flops, bytes_accessed=1000, transcendentals=0),
         name=name,
     )(own, near, weights, near_weights)
 
@@ -348,17 +348,23 @@
     copy.wait()
 
 
-def finish_rest_kernel(gain, inverse, left, rest, before, out, held, sem):
+def finish_rest_kernel(gain, inverse, left, rest, before, out, held, sems):
     span = rest.shape[1]
     first = out.shape[1] - span
-    for start in range(0, span, TILE):
-        tile = slice(start, start + TILE)
-        columns = slice(first + start, first + start + TILE)
+    half = span // 2
+    copies = []
+    for index, start in enumerate(range(0, span, half)):
+        tile = slice(start, start + half)
+        columns = slice(first + start, first + start + half)
         grad_hat = rest[:, tile].astype(jnp.float32) * gain[:, columns].astype(jnp.float32)
         held[:, tile] = (left[:, tile] + inverse[...] * grad_hat).astype(jnp.bfloat16)
-    copy = pltpu.make_async_copy(held, out.at[:, pl.ds(first, span)], sem)
-    copy.start()
-    copy.wait()
+        target = out.at[:, pl.ds(first + start, half)]
+        copies.append(
+            pltpu.make_async_copy(held.at[:, pl.ds(start, half)], target, sems.at[index])
+        )
+        copies[-1].start()
+    for copy in copies:
+        copy.wait()
 
 
 def finish_grad(inputs, cotangent, gain, inverse, extras, grad_own, got, middle, rest):
@@ -383,7 +389,7 @@
         out_shape=shape(jnp.bfloat16, rows, width),
         in_specs=[VMEM] * 4 + [hbm],
         out_specs=hbm,
-        scratch_shapes=[pltpu.VMEM((rows, span), jnp.bfloat16), pltpu.SemaphoreType.DMA],
+        scratch_shapes=[pltpu.VMEM((rows, span), jnp.bfloat16), pltpu.SemaphoreType.DMA((2,))],
         input_output_aliases={4: 0},
         name="finish_rest",
         **options,
@@ -462,9 +468,11 @@
     quarter = width // 4
     turn, got = own, []
     for first, span in ((0, 2 * quarter), (2 * quarter, quarter), (3 * quarter, quarter)):
-        part = spread("spread_far", width + first, span, low, turn, near, own_turned, near_turned)
-        got.append(swap(part if first else after(part, far_extras), 2, tensor))
-        turn = after(own, part)
+        flops = 4 * rows * span * width if first else 1000
+        sides = (turn, near, own_turned, near_turned)
+        part = spread("spread_far", width + first, span, low, *sides, flops=flops)
+        got.append(swap(part, 2, tensor))
+        turn = after(own, part, far_extras)
     grad_own = spread("spread_own", 0, width, jnp.float32, turn, near, own_turned, near_turned)
     extras = (own_extras, swap(own_extras, 1, tensor), far_extras, swap(far_extras, 1, tensor))
     layer_out = call(

time: 78.7 us -> 76.8 us (0.976)
  waiting for transfers between devices: 19.7 us -> 17.4 us
    ppermute x17, waiting for transfers between devices: 19.7 us -> 17.4 us  [swap(): return lax.ppermute(array, 'tensor', [(i, i ^ mask) for i in range(count)])]
    unnamed x22 -> x24, local copies, waits for them, and re-layouts: 8.35 us -> 8.35 us
where the time goes in v9:
time: 76.8 us; the launch traced here: 76.4 us
  blocking collectives  22.7 us (30%)
  waiting for transfers between devices  17.4 us (23%)
  Pallas kernels  14.5 us (19%)
  starting transfers between devices  11.9 us (15%)
  local copies, waits for them, and re-layouts  9.04 us (12%)
  between operations  0.81 us (1%)
    all_to_all x2, blocking collectives, move(): return lax.all_to_all(bucket, 'dp', split_axis=0, concat_axis=0, tiled=True)  22.7 us
    ppermute x17, waiting for transfers between devices, swap(): return lax.ppermute(array, 'tensor', [(i, i ^ mask) for i in range(count)])  17.4 us
    ppermute x17, starting transfers between devices, swap(): return lax.ppermute(array, 'tensor', [(i, i ^ mask) for i in range(count)])  11.9 us
    pallas_call x8, Pallas kernels, call(): pl.pallas_call(kernel, out_shape=shapes, in_specs=[first] + [rest] * (len...  9.6 us
    unnamed x24, local copies, waits for them, and re-layouts  8.35 us
    pallas_call x4, Pallas kernels, spread(): pl.pallas_call(spread_kernel(first), out_shape=shape(dtype, rows, span),...  2.94 us
  transfers between devices with their start and end apart: 17, of which 7 were waited for; matrix products, arithmetic and copies ran while one was open for 1% of the time, Pallas kernels for 15%

profile of v9, /device:TPU:0, one launch (start us, length us, event | category | flops | bytes accessed | tf_op | source)
XLA Modules:
  0.0 76.4 jit_solution(4002642482594377821)
XLA Ops:
  1.2 2.9 %collective-permute-start.1 = (bf16[128,2048]{1,0:T(8,128)(2,1)}, bf16[128,2048]{1,0:T(8,128)(2,1)S(1)}, u32[]{:S(2)}, u32[]{:S(2)}) collective-permute-start(bf16[128,2048]{1,0:T(8,128)(2,1)} %inputs.3), channel_id=1, source_target_pairs={{0,2},{1,3},{2,0},{3,1},{4,6},{5,7},{6,4},{7,5},{8,10},{9,11},{10,... | collective-permute-start | bytes 1572872 | tf_op jit(solution)/shard_map/ppermute | solution.py:46
  4.9 2.0 %collective-permute-start.3 = (bf16[1,2048]{1,0:T(2,128)(2,1)S(1)}, bf16[1,2048]{1,0:T(2,128)(2,1)S(1)}, u32[]{:S(2)}, u32[]{:S(2)}) collective-permute-start(bf16[1,2048]{1,0:T(2,128)(2,1)S(1)} %reshape.17.gain), channel_id=1, source_target_pairs={{0,2},{1,3},{2,0},{3,1},{4,6},{5,7},{6,4},{7,5},{8,10},{9,11},{10,... | collective-permute-start | bytes 12296 | tf_op jit(solution)/shard_map/ppermute | solution.py:46
  6.9 1.6 %copy-done = bf16[8192,128]{1,0:T(8,128)(2,1)S(1)} copy-done((bf16[8192,128]{1,0:T(8,128)(2,1)S(1)}, bf16[8192,128]{1,0:T(8,128)(2,1)}, u32[]{:S(2)}) %copy-start) | copy-done | bytes 2097176
  8.5 1.6 %copy-done.2 = bf16[8192,128]{1,0:T(8,128)(2,1)S(1)} copy-done((bf16[8192,128]{1,0:T(8,128)(2,1)S(1)}, bf16[8192,128]{1,0:T(8,128)(2,1)}, u32[]{:S(2)}) %copy-start.2) | copy-done | bytes 2097176
  10.1 1.6 %copy-done.4 = bf16[8192,128]{1,0:T(8,128)(2,1)S(1)} copy-done((bf16[8192,128]{1,0:T(8,128)(2,1)S(1)}, bf16[8192,128]{1,0:T(8,128)(2,1)}, u32[]{:S(2)}) %copy-start.4) | copy-done | bytes 2097176
  11.7 1.6 %copy-done.8 = bf16[128,8192]{1,0:T(8,128)(2,1)S(1)} copy-done((bf16[128,8192]{1,0:T(8,128)(2,1)S(1)}, bf16[128,8192]{1,0:T(8,128)(2,1)}, u32[]{:S(2)}) %copy-start.8) | copy-done | bytes 2097176
  15.2 2.8 %prepare.1 = (bf16[384,4096]{1,0:T(8,128)(2,1)S(1)}, bf16[384,4096]{1,0:T(8,128)(2,1)S(1)}, bf16[256,2048]{1,0:T(8,128)(2,1)S(1)}, bf16[256,2048]{1,0:T(8,128)(2...) custom-call(s32[4]{0:T(128)S(1)} %iota_xor_fusion.order, ...), custom_call_target="tpu_custom_call" | custom-call | flops 1000 | bytes 1000 | tf_op jit(solution)/shard_map/prepare/pallas_call | solution.py:28
  18.5 9.5 %collective-permute-done.3 = bf16[1,2048]{1,0:T(2,128)(2,1)S(1)} collective-permute-done((bf16[1,2048]{1,0:T(2,128)(2,1)S(1)}, bf16[1,2048]{1,0:T(2,128)(2,1)S(1)}, u32[]{:S(2)}, u32[]{:S(2)}) %collective-permute-start.3) | collective-permute-done | bytes 4128 | tf_op jit(solution)/shard_map/ppermute | solution.py:46
  28.0 1.4 %add_grad.1 = (f32[128,128]{1,0:T(8,128)S(1)}, f32[128,128]{1,0:T(8,128)S(1)}) custom-call(bf16[128,2048]{1,0:T(8,128)(2,1)} %collective-permute-done.2.c2, bf16[2048,256]{1,0:T(8,128)(2,1)S(1)} %get-tuple-element.40.there_turned, f32[128,256]{1,0:T(8,128)S(1)} %get-tuple-element.41.part), custom_call_target="tpu_custom_call" | custom-call | flops 1000 | bytes 1000 | tf_op jit(solution)/shard_map/add_grad/pallas_call | solution.py:28
  30.2 1.0 %collective-permute-done.6.gain_near = bf16[2,2048]{1,0:T(2,128)(2,1)S(1)} collective-permute-done((bf16[2,2048]{1,0:T(2,128)(2,1)S(1)}, bf16[2,2048]{1,0:T(2,128)(2,1)S(1)}, u32[]{:S(2)}, u32[]{:S(2)}) %collective-permute-start.6) | collective-permute-done | bytes 8224 | tf_op jit(solution)/shard_map/ppermute | solution.py:46
  31.2 2.2 %project.1 = (bf16[128,384]{1,0:T(8,128)(2,1)S(1)}, f32[128,1]{1,0:T(8,128)S(1)}, bf16[128,512]{1,0:T(8,128)(2,1)S(1)}) custom-call(s32[4]{0:T(128)S(1)} %iota_xor_fusion.order, bf16[128,2048]{1,0:T(8,128)(2,1)S(1)} %copy-done.6, bf16[128,2048]{1,0:T(8,128)(2,1)S(1)} %collective-permute-done.x1, bf16[128,2048]{1,0:T(8,128)(2,1)S(1)} %collective-permute-done.1.x2, ...), custom_call_target="tpu_custom_call" | custom-call | flops 1000 | bytes 1000 | tf_op jit(solution)/shard_map/project/pallas_call | solution.py:28
  33.7 1.7 %collective-permute-start.11 = (bf16[256,2048]{1,0:T(8,128)(2,1)S(1)}, bf16[256,2048]{1,0:T(8,128)(2,1)S(1)}, u32[]{:S(2)}, u32[]{:S(2)}) collective-permute-start(bf16[256,2048]{1,0:T(8,128)(2,1)S(1)} %get-tuple-element.52), channel_id=1, source_target_pairs={{0,2},{1,3},{2,0},{3,1},{4,6},{5,7},{6,4},{7,5},{8,10},{9,11},{10,... | collective-permute-start | bytes 3145736 | tf_op jit(solution)/shard_map/ppermute | solution.py:46
  35.4 12.9 %all_to_all.22 = bf16[8,16,512]{2,1,0:T(8,128)(2,1)S(1)} all-to-all(bf16[8,16,512]{2,1,0:T(8,128)(2,1)S(1)} %bitcast.9), channel_id=1, replica_groups=mesh['dp'=8,'tensor'=4] {'dp'}, dimensions={0} | all-to-all | bytes 262144 | tf_op jit(solution)/shard_map/all_to_all | solution.py:400
  48.4 1.1 %attend.1 = bf16[128,512]{1,0:T(8,128)(2,1)S(1)} custom-call(bf16[128,512]{1,0:T(8,128)(2,1)S(1)} %bitcast.7, s32[1,128]{1,0:T(1,128)S(1)} %get-tuple-element.46.receive, s32[1,128]{1,0:T(1,128)S(1)} %get-tuple-element.47.segments), custom_call_target="tpu_custom_call" | custom-call | flops 1000 | bytes 1000 | tf_op jit(solution)/shard_map/attend/pallas_call | solution.py:28
  49.5 9.7 %all_to_all.23 = bf16[8,16,512]{2,1,0:T(8,128)(2,1)S(1)} all-to-all(bf16[8,16,512]{2,1,0:T(8,128)(2,1)S(1)} %bitcast.8), channel_id=1, replica_groups=mesh['dp'=8,'tensor'=4] {'dp'}, dimensions={0} | all-to-all | bytes 262144 | tf_op jit(solution)/shard_map/all_to_all | solution.py:400
  61.6 0.9 %collective-permute-start.14 = (bf16[128,1024]{1,0:T(8,128)(2,1)S(1)}, bf16[128,1024]{1,0:T(8,128)(2,1)S(1)}, u32[]{:S(2)}, u32[]{:S(2)}) collective-permute-start(bf16[128,1024]{1,0:T(8,128)(2,1)S(1)} %spread_far.3), channel_id=1, source_target_pairs={{0,2},{1,3},{2,0},{3,1},{4,6},{5,7},{6,4},{7,5},{8,10},{9,11},{10,... | collective-permute-start | bytes 786440 | tf_op jit(solution)/shard_map/ppermute | solution.py:46
  62.5 1.6 %collective-permute-done.9.far = bf16[128,256]{1,0:T(8,128)(2,1)S(1)} collective-permute-done((bf16[128,256]{1,0:T(8,128)(2,1)S(1)}, bf16[128,256]{1,0:T(8,128)(2,1)S(1)}, u32[]{:S(2)}, u32[]{:S(2)}) %collective-permute-start.9) | collective-permute-done | bytes 65568 | tf_op jit(solution)/shard_map/ppermute | solution.py:46
  65.4 1.6 %collective-permute-start.16 = (bf16[128,512]{1,0:T(8,128)(2,1)S(1)}, bf16[128,512]{1,0:T(8,128)(2,1)S(1)}, u32[]{:S(2)}, u32[]{:S(2)}) collective-permute-start(bf16[128,512]{1,0:T(8,128)(2,1)S(1)} %spread_far.5), channel_id=1, source_target_pairs={{0,2},{1,3},{2,0},{3,1},{4,6},{5,7},{6,4},{7,5},{8,10},{9,11},{10,... | collective-permute-start | bytes 393224 | tf_op jit(solution)/shard_map/ppermute | solution.py:46
  67.0 1.3 %collective-permute-done.10.last = bf16[128,256]{1,0:T(8,128)(2,1)S(1)} collective-permute-done((bf16[128,256]{1,0:T(8,128)(2,1)S(1)}, bf16[128,256]{1,0:T(8,128)(2,1)S(1)}, u32[]{:S(2)}, u32[]{:S(2)}) %collective-permute-start.10) | collective-permute-done | bytes 65568 | tf_op jit(solution)/shard_map/ppermute | solution.py:46
  68.3 1.3 %finish_out.1 = bf16[128,2048]{1,0:T(8,128)(2,1)} custom-call(bf16[128,2048]{1,0:T(8,128)(2,1)S(1)} %copy-done.6, bf16[128,256]{1,0:T(8,128)(2,1)S(1)} %get-tuple-element.49.own, bf16[128,256]{1,0:T(8,128)(2,1)S(1)} %collective-permute-done.8.near, bf16[128,256]{1,0:T(8,128)(2,1)S(1)} %collective-permute-done.9.far, ...), custom_call_target="tpu_custom_call" | custom-call | flops 1000 | bytes 1000 | tf_op jit(solution)/shard_map/finish_out/pallas_call | solution.py:28
  69.5 1.4 %spread_own.1.grad_own = f32[128,2048]{1,0:T(8,128)S(1)} custom-call(bf16[128,384]{1,0:T(8,128)(2,1)S(1)} %get-tuple-element.60.own, bf16[128,384]{1,0:T(8,128)(2,1)S(1)} %collective-permute-done.12.near, bf16[384,4096]{1,0:T(8,128)(2,1)S(1)} %get-tuple-element.55.weights, bf16[384,4096]{1,0:T(8,128)(2,1)S(1)} %collective-permute-done.13.near_weights), custom_call_target="tpu_custom_call" | custom-call | flops 1000 | bytes 1000 | tf_op jit(solution)/shard_map/spread_own/pallas_call | solution.py:296
  71.0 2.7 %collective-permute-done.15.middle = bf16[128,512]{1,0:T(8,128)(2,1)S(1)} collective-permute-done((bf16[128,512]{1,0:T(8,128)(2,1)S(1)}, bf16[128,512]{1,0:T(8,128)(2,1)S(1)}, u32[]{:S(2)}, u32[]{:S(2)}) %collective-permute-start.15) | collective-permute-done | bytes 131104 | tf_op jit(solution)/shard_map/ppermute | solution.py:46
  73.6 1.3 %finish_most.1 = (bf16[128,2048]{1,0:T(8,128)(2,1)}, f32[128,512]{1,0:T(8,128)S(1)}) custom-call(bf16[128,2048]{1,0:T(8,128)(2,1)S(1)} %copy-done.6, bf16[128,2048]{1,0:T(8,128)(2,1)S(1)} %copy-done.7, bf16[1,2048]{1,0:T(2,128)(2,1)S(1)} %reshape.17.gain, f32[128,1]{1,0:T(8,128)S(1)} %get-tuple-element.53.inverse, ...), custom_call_target="tpu_custom_call" | custom-call | flops 1000 | bytes 1000 | tf_op jit(solution)/shard_map/finish_most/pallas_call | solution.py:378
  74.9 0.8 collective-permute-done.16.rest
  (53 shorter events, 9.4 us)
Async XLA Ops:
  0.6 6.3 %collective-permute-start.4 = (bf16[128,8192]{1,0:T(8,128)(2,1)}, bf16[128,8192]{1,0:T(8,128)(2,1)S(1)}, u32[]{:S(2)}, u32[]{:S(2)}) collective-permute-start(bf16[128,8192]{1,0:T(8,128)(2,1)} %w_output.1), channel_id=1, source_target_pairs={{0,1},{1,0},{2,3},{3,2},{4,5},{5,4},{6,7},{7,6},{8,9},{9,8},{10,11... | collective-permute-start | bytes 6291464 | tf_op jit(solution)/shard_map/ppermute | solution.py:46
  1.1 16.9 %collective-permute-start = (bf16[128,2048]{1,0:T(8,128)(2,1)}, bf16[128,2048]{1,0:T(8,128)(2,1)S(1)}, u32[]{:S(2)}, u32[]{:S(2)}) collective-permute-start(bf16[128,2048]{1,0:T(8,128)(2,1)} %inputs.3), channel_id=1, source_target_pairs={{0,1},{1,0},{2,3},{3,2},{4,5},{5,4},{6,7},{7,6},{8,9},{9,8},{10,11... | collective-permute-start | bytes 1572872 | tf_op jit(solution)/shard_map/ppermute | solution.py:46
  1.2 26.8 %collective-permute-start.1 = (bf16[128,2048]{1,0:T(8,128)(2,1)}, bf16[128,2048]{1,0:T(8,128)(2,1)S(1)}, u32[]{:S(2)}, u32[]{:S(2)}) collective-permute-start(bf16[128,2048]{1,0:T(8,128)(2,1)} %inputs.3), channel_id=1, source_target_pairs={{0,2},{1,3},{2,0},{3,1},{4,6},{5,7},{6,4},{7,5},{8,10},{9,11},{10,... | collective-permute-start | bytes 1572872 | tf_op jit(solution)/shard_map/ppermute | solution.py:46
  4.2 23.8 %collective-permute-start.2 = (bf16[128,2048]{1,0:T(8,128)(2,1)}, bf16[128,2048]{1,0:T(8,128)(2,1)}, u32[]{:S(2)}, u32[]{:S(2)}) collective-permute-start(bf16[128,2048]{1,0:T(8,128)(2,1)} %cotangent.1), channel_id=1, source_target_pairs={{0,2},{1,3},{2,0},{3,1},{4,6},{5,7},{6,4},{7,5},{8,10},{9,11},{10,... | collective-permute-start | bytes 1572872 | tf_op jit(solution)/shard_map/ppermute | solution.py:46
  4.9 23.1 %collective-permute-start.3 = (bf16[1,2048]{1,0:T(2,128)(2,1)S(1)}, bf16[1,2048]{1,0:T(2,128)(2,1)S(1)}, u32[]{:S(2)}, u32[]{:S(2)}) collective-permute-start(bf16[1,2048]{1,0:T(2,128)(2,1)S(1)} %reshape.17.gain), channel_id=1, source_target_pairs={{0,2},{1,3},{2,0},{3,1},{4,6},{5,7},{6,4},{7,5},{8,10},{9,11},{10,... | collective-permute-start | bytes 12296 | tf_op jit(solution)/shard_map/ppermute | solution.py:46
  6.9 1.6 %copy-start = (bf16[8192,128]{1,0:T(8,128)(2,1)S(1)}, bf16[8192,128]{1,0:T(8,128)(2,1)}, u32[]{:S(2)}) copy-start(bf16[8192,128]{1,0:T(8,128)(2,1)} %w_query.3) | copy-start | bytes 6291460
  8.5 1.6 %copy-start.2 = (bf16[8192,128]{1,0:T(8,128)(2,1)S(1)}, bf16[8192,128]{1,0:T(8,128)(2,1)}, u32[]{:S(2)}) copy-start(bf16[8192,128]{1,0:T(8,128)(2,1)} %w_key.3) | copy-start | bytes 6291460
  15.2 2.8 %copy-start.6 = (bf16[128,2048]{1,0:T(8,128)(2,1)S(1)}, bf16[128,2048]{1,0:T(8,128)(2,1)}, u32[]{:S(2)}) copy-start(bf16[128,2048]{1,0:T(8,128)(2,1)} %inputs.3) | copy-start | bytes 1572868
  15.2 2.8 %copy-start.7 = (bf16[128,2048]{1,0:T(8,128)(2,1)S(1)}, bf16[128,2048]{1,0:T(8,128)(2,1)}, u32[]{:S(2)}) copy-start(bf16[128,2048]{1,0:T(8,128)(2,1)} %cotangent.1) | copy-start | bytes 1572868
  15.2 16.0 %copy-start.5 = (bf16[8192,128]{1,0:T(8,128)(2,1)S(1)}, bf16[8192,128]{1,0:T(8,128)(2,1)}, u32[]{:S(2)}) copy-start(bf16[8192,128]{1,0:T(8,128)(2,1)} %w_value.3) | copy-start | bytes 6291460
  18.1 13.1 %copy-start.1 = (bf16[8192,128]{1,0:T(8,128)(2,1)S(1)}, bf16[8192,128]{1,0:T(8,128)(2,1)}, u32[]{:S(2)}) copy-start(bf16[8192,128]{1,0:T(8,128)(2,1)} %w_query.3) | copy-start | bytes 6291460
  18.1 13.1 %copy-start.3 = (bf16[8192,128]{1,0:T(8,128)(2,1)S(1)}, bf16[8192,128]{1,0:T(8,128)(2,1)}, u32[]{:S(2)}) copy-start(bf16[8192,128]{1,0:T(8,128)(2,1)} %w_key.3) | copy-start | bytes 6291460
  28.0 3.2 %collective-permute-start.5 = (bf16[128,2048]{1,0:T(8,128)(2,1)S(1)}, bf16[128,2048]{1,0:T(8,128)(2,1)S(1)}, u32[]{:S(2)}, u32[]{:S(2)}) collective-permute-start(bf16[128,2048]{1,0:T(8,128)(2,1)S(1)} %collective-permute-done.1.x2), channel_id=1, source_target_pairs={{0,1},{1,0},{2,3},{3,2},{4,5},{5,4},{6,7},{7,6},{8,9},{9,8},{10,11... | collective-permute-start | bytes 1572872 | tf_op jit(solution)/shard_map/ppermute | solution.py:46
  29.4 1.8 %collective-permute-start.7 = (f32[128,128]{1,0:T(8,128)S(1)}, f32[128,128]{1,0:T(8,128)S(1)}, u32[]{:S(2)}, u32[]{:S(2)}) collective-permute-start(f32[128,128]{1,0:T(8,128)S(1)} %get-tuple-element.43), channel_id=1, source_target_pairs={{0,1},{1,0},{2,3},{3,2},{4,5},{5,4},{6,7},{7,6},{8,9},{9,8},{10,11... | collective-permute-start | bytes 196616 | tf_op jit(solution)/shard_map/ppermute | solution.py:46
  29.9 1.2 %collective-permute-start.6 = (bf16[2,2048]{1,0:T(2,128)(2,1)S(1)}, bf16[2,2048]{1,0:T(2,128)(2,1)S(1)}, u32[]{:S(2)}, u32[]{:S(2)}) collective-permute-start(bf16[2,2048]{1,0:T(2,128)(2,1)S(1)} %pad_maximum_fusion.gain_own), channel_id=1, source_target_pairs={{0,1},{1,0},{2,3},{3,2},{4,5},{5,4},{6,7},{7,6},{8,9},{9,8},{10,11... | collective-permute-start | bytes 24584 | tf_op jit(solution)/shard_map/ppermute | solution.py:46
  33.5 27.4 %collective-permute-start.13 = (bf16[384,4096]{1,0:T(8,128)(2,1)S(1)}, bf16[384,4096]{1,0:T(8,128)(2,1)S(1)}, u32[]{:S(2)}, u32[]{:S(2)}) collective-permute-start(bf16[384,4096]{1,0:T(8,128)(2,1)S(1)} %get-tuple-element.57), channel_id=1, source_target_pairs={{0,1},{1,0},{2,3},{3,2},{4,5},{5,4},{6,7},{7,6},{8,9},{9,8},{10,11... | collective-permute-start | bytes 9437192 | tf_op jit(solution)/shard_map/ppermute | solution.py:46
  33.7 34.6 %collective-permute-start.11 = (bf16[256,2048]{1,0:T(8,128)(2,1)S(1)}, bf16[256,2048]{1,0:T(8,128)(2,1)S(1)}, u32[]{:S(2)}, u32[]{:S(2)}) collective-permute-start(bf16[256,2048]{1,0:T(8,128)(2,1)S(1)} %get-tuple-element.52), channel_id=1, source_target_pairs={{0,2},{1,3},{2,0},{3,1},{4,6},{5,7},{6,4},{7,5},{8,10},{9,11},{10,... | collective-permute-start | bytes 3145736 | tf_op jit(solution)/shard_map/ppermute | solution.py:46
  59.5 1.4 %collective-permute-start.12 = (bf16[128,384]{1,0:T(8,128)(2,1)S(1)}, bf16[128,384]{1,0:T(8,128)(2,1)S(1)}, u32[]{:S(2)}, u32[]{:S(2)}) collective-permute-start(bf16[128,384]{1,0:T(8,128)(2,1)S(1)} %get-tuple-element.60.own), channel_id=1, source_target_pairs={{0,1},{1,0},{2,3},{3,2},{4,5},{5,4},{6,7},{7,6},{8,9},{9,8},{10,11... | collective-permute-start | bytes 294920 | tf_op jit(solution)/shard_map/ppermute | solution.py:46
  59.5 4.5 %collective-permute-start.9 = (bf16[128,256]{1,0:T(8,128)(2,1)S(1)}, bf16[128,256]{1,0:T(8,128)(2,1)S(1)}, u32[]{:S(2)}, u32[]{:S(2)}) collective-permute-start(bf16[128,256]{1,0:T(8,128)(2,1)S(1)} %get-tuple-element.49.own), channel_id=1, source_target_pairs={{0,2},{1,3},{2,0},{3,1},{4,6},{5,7},{6,4},{7,5},{8,10},{9,11},{10,... | collective-permute-start | bytes 196616 | tf_op jit(solution)/shard_map/ppermute | solution.py:46
  61.6 12.0 %collective-permute-start.14 = (bf16[128,1024]{1,0:T(8,128)(2,1)S(1)}, bf16[128,1024]{1,0:T(8,128)(2,1)S(1)}, u32[]{:S(2)}, u32[]{:S(2)}) collective-permute-start(bf16[128,1024]{1,0:T(8,128)(2,1)S(1)} %spread_far.3), channel_id=1, source_target_pairs={{0,2},{1,3},{2,0},{3,1},{4,6},{5,7},{6,4},{7,5},{8,10},{9,11},{10,... | collective-permute-start | bytes 786440 | tf_op jit(solution)/shard_map/ppermute | solution.py:46
  62.5 4.5 %collective-permute-start.8 = (bf16[128,256]{1,0:T(8,128)(2,1)S(1)}, bf16[128,256]{1,0:T(8,128)(2,1)S(1)}, u32[]{:S(2)}, u32[]{:S(2)}) collective-permute-start(bf16[128,256]{1,0:T(8,128)(2,1)S(1)} %get-tuple-element.49.own), channel_id=1, source_target_pairs={{0,1},{1,0},{2,3},{3,2},{4,5},{5,4},{6,7},{7,6},{8,9},{9,8},{10,11... | collective-permute-start | bytes 196616 | tf_op jit(solution)/shard_map/ppermute | solution.py:46
  64.4 9.2 %collective-permute-start.15 = (bf16[128,512]{1,0:T(8,128)(2,1)S(1)}, bf16[128,512]{1,0:T(8,128)(2,1)S(1)}, u32[]{:S(2)}, u32[]{:S(2)}) collective-permute-start(bf16[128,512]{1,0:T(8,128)(2,1)S(1)} %spread_far.4), channel_id=1, source_target_pairs={{0,2},{1,3},{2,0},{3,1},{4,6},{5,7},{6,4},{7,5},{8,10},{9,11},{10,... | collective-permute-start | bytes 393224 | tf_op jit(solution)/shard_map/ppermute | solution.py:46
  65.4 10.2 %collective-permute-start.16 = (bf16[128,512]{1,0:T(8,128)(2,1)S(1)}, bf16[128,512]{1,0:T(8,128)(2,1)S(1)}, u32[]{:S(2)}, u32[]{:S(2)}) collective-permute-start(bf16[128,512]{1,0:T(8,128)(2,1)S(1)} %spread_far.5), channel_id=1, source_target_pairs={{0,2},{1,3},{2,0},{3,1},{4,6},{5,7},{6,4},{7,5},{8,10},{9,11},{10,... | collective-permute-start | bytes 393224 | tf_op jit(solution)/shard_map/ppermute | solution.py:46
  67.0 1.3 %collective-permute-start.10 = (bf16[128,256]{1,0:T(8,128)(2,1)S(1)}, bf16[128,256]{1,0:T(8,128)(2,1)S(1)}, u32[]{:S(2)}, u32[]{:S(2)}) collective-permute-start(bf16[128,256]{1,0:T(8,128)(2,1)S(1)} %collective-permute-done.9.far), channel_id=1, source_target_pairs={{0,1},{1,0},{2,3},{3,2},{4,5},{5,4},{6,7},{7,6},{8,9},{9,8},{10,11... | collective-permute-start | bytes 196616 | tf_op jit(solution)/shard_map/ppermute | solution.py:46
  (5 other events, 5.1 us)

commit v10 on v9

--- a/solution.py
+++ b/solution.py
@@ -129,16 +129,32 @@
     return call(begin_kernel, "begin", shapes, (x0, x1, c0, here_turned), first=VMEM)
 
 
-def add_grad_kernel(c2, there_turned, part, own_part, near_part):
-    total = part[...] + dot(c2[...], there_turned[...])
+def add_grad_kernel(c2, there_turned, part, own_part, near_part, held, sems):
+    copies = []
+    for index, start in enumerate(range(0, held.shape[1], TILE)):
+        tile = pl.ds(start, TILE)
+        copies.append(pltpu.make_async_copy(c2.at[:, tile], held.at[:, tile], sems.at[index]))
+        copies[-1].start()
+    total = part[...]
+    for index, copy in enumerate(copies):
+        tile = slice(index * TILE, (index + 1) * TILE)
+        copy.wait()
+        total = total + dot(held[:, tile], there_turned[tile, :])
     heads = own_part.shape[1]
     own_part[...] = total[:, :heads]
     near_part[...] = total[:, heads:]
 
 
 def add_grad(c2, there_turned, part):
-    shapes = [shape(jnp.float32, part.shape[0], part.shape[1] // 2)] * 2
-    return call(add_grad_kernel, "add_grad", shapes, (c2, there_turned, part), first=VMEM)
+    rows, width = c2.shape
+    return call(
+        add_grad_kernel,
+        "add_grad",
+        [shape(jnp.float32, rows, part.shape[1] // 2)] * 2,
+        (c2, there_turned, part),
+        scratch=[pltpu.VMEM((rows, width), c2.dtype), pltpu.SemaphoreType.DMA((width // TILE,))],
+        first=pl.BlockSpec(memory_space=pl.ANY),
+    )
 
 
 def add_squares_kernel(x2, squares_in, squares):
@@ -270,39 +286,22 @@
 
 
 def spread_kernel(first):
-    def kernel(own, near, weights, near_weights, out, held, total, sems):
-        span = held.shape[1]
-        copies = []
-        for index, start in enumerate(range(0, span, TILE)):
-            source = near_weights.at[:, pl.ds(first + start, TILE)]
-            target = held.at[:, pl.ds(start, TILE)]
-            copies.append(pltpu.make_async_copy(source, target, sems.at[index]))
-            copies[-1].start()
+    def kernel(own, near, weights, near_weights, out):
         own_rows, near_rows = own[...], near[...]
-        for start in range(0, span, TILE):
+        for start in range(0, out.shape[1], TILE):
             columns = slice(first + start, first + start + TILE)
-            total[:, start : start + TILE] = dot(own_rows, weights[:, columns])
-        for index, start in enumerate(range(0, span, TILE)):
-            copies[index].wait()
-            tile = slice(start, start + TILE)
-            result = total[:, tile] + dot(near_rows, held[:, tile])
-            out[:, tile] = result.astype(out.dtype)
+            total = dot(own_rows, weights[:, columns]) + dot(near_rows, near_weights[:, columns])
+            out[:, start : start + TILE] = total.astype(out.dtype)
 
     return kernel
 
 
 def spread(name, first, span, dtype, own, near, weights, near_weights, flops=1000):
-    rows, depth = own.shape
     return pl.pallas_call(
         spread_kernel(first),
-        out_shape=shape(dtype, rows, span),
-        in_specs=[VMEM] * 3 + [pl.BlockSpec(memory_space=pl.ANY)],
+        out_shape=shape(dtype, own.shape[0], span),
+        in_specs=[VMEM] * 4,
         out_specs=VMEM,
-        scratch_shapes=[
-            pltpu.VMEM((depth, span), jnp.bfloat16),
-            pltpu.VMEM((rows, span), jnp.float32),
-            pltpu.SemaphoreType.DMA((span // TILE,)),
-        ],
         compiler_params=pltpu.CompilerParams(vmem_limit_bytes=VMEM_LIMIT),
         cost_estimate=pl.CostEstimate(flops=flops, bytes_accessed=1000, transcendentals=0),
         name=name,
@@ -320,9 +319,14 @@
 
 
 def finish_most_kernel(
-    inputs, cotangent, gain, inverse, own, near, far, last, grad_own, got, middle, *outs
+    inputs, cotangent, gain, inverse, own, near, far, last, grad_own, *pieces
 ):
-    out, left, held, sem = outs
+    *pieces, out, left, held, sem = pieces
+    tiles = [
+        piece.at[:, start : start + TILE]
+        for piece in pieces
+        for start in range(0, piece.shape[1], TILE)
+    ]
     row_dot = sum(read_parts(extras[:, HEAD_DIM:]) for extras in (own, near, far, last))
     mean_dot = row_dot / (4 * inputs.shape[1])
     inverse_rms = inverse[...]
@@ -330,11 +334,8 @@
     for start in range(0, inputs.shape[1], TILE):
         tile = slice(start, start + TILE)
         grad_normed = grad_own[:, tile]
-        if start < got.shape[1]:
-            grad_normed = grad_normed + got[:, tile].astype(jnp.float32)
-        elif start < most:
-            part = slice(start - got.shape[1], start - got.shape[1] + TILE)
-            grad_normed = grad_normed + middle[:, part].astype(jnp.float32)
+        if start < most:
+            grad_normed = grad_normed + tiles[start // TILE][...].astype(jnp.float32)
         grad_hat = grad_normed * gain[:, tile].astype(jnp.float32)
         scaled = inputs[:, tile].astype(jnp.float32) * inverse_rms
         change = inverse_rms * (grad_hat - scaled * mean_dot)
@@ -367,8 +368,9 @@
         copy.wait()
 
 
-def finish_grad(inputs, cotangent, gain, inverse, extras, grad_own, got, middle, rest):
+def finish_grad(inputs, cotangent, gain, inverse, extras, grad_own, pieces):
     rows, width = inputs.shape
+    *pieces, rest = pieces
     span = rest.shape[1]
     hbm = pl.BlockSpec(memory_space=pltpu.HBM)
     options = dict(
@@ -378,12 +380,12 @@
     begun, left = pl.pallas_call(
         finish_most_kernel,
         out_shape=[shape(jnp.bfloat16, rows, width), shape(jnp.float32, rows, span)],
-        in_specs=[VMEM] * 11,
+        in_specs=[VMEM] * (9 + len(pieces)),
         out_specs=[hbm, VMEM],
         scratch_shapes=[pltpu.VMEM((rows, width - span), jnp.bfloat16), pltpu.SemaphoreType.DMA],
         name="finish_most",
         **options,
-    )(inputs, cotangent, gain, inverse, *extras, grad_own, got, middle)
+    )(inputs, cotangent, gain, inverse, *extras, grad_own, *pieces)
     return pl.pallas_call(
         finish_rest_kernel,
         out_shape=shape(jnp.bfloat16, rows, width),
@@ -483,7 +485,7 @@
         first=VMEM,
     )
     got[1] = after(got[1], layer_out)
-    input_grad = finish_grad(inputs, cotangent, gain, inverse_rms, extras, grad_own, *got)
+    input_grad = finish_grad(inputs, cotangent, gain, inverse_rms, extras, grad_own, got)
     return (layer_out, input_grad)
 
 

time: 76.8 us -> 76.7 us (level)
  waiting for transfers between devices: 17.4 us -> 18.3 us
  Pallas kernels: 14.5 us -> 13.6 us
    pallas_call x4, Pallas kernels: 2.94 us -> 1.77 us  [spread(): pl.pallas_call(spread_kernel(first), out_shape=shape(dtype, own.shape[0],...]
    ppermute x17, waiting for transfers between devices: 17.4 us -> 18.3 us  [swap(): return lax.ppermute(array, 'tensor', [(i, i ^ mask) for i in range(count)])]
  transfers between devices with their start and end apart: 17 -> 17, of which waited for: 7 -> 7; matrix products, arithmetic and copies ran while one was open for 1% -> 1% of each run, Pallas kernels for 15% -> 14%
where the time goes in v10:
time: 76.7 us; the launch traced here: 76.3 us
  blocking collectives  22.7 us (30%)
  waiting for transfers between devices  18.3 us (24%)
  Pallas kernels  13.6 us (18%)
  starting transfers between devices  11.8 us (15%)
  local copies, waits for them, and re-layouts  9.04 us (12%)
  between operations  0.81 us (1%)
    all_to_all x2, blocking collectives, move(): return lax.all_to_all(bucket, 'dp', split_axis=0, concat_axis=0, tiled=True)  22.7 us
    ppermute x17, waiting for transfers between devices, swap(): return lax.ppermute(array, 'tensor', [(i, i ^ mask) for i in range(count)])  18.3 us
    ppermute x17, starting transfers between devices, swap(): return lax.ppermute(array, 'tensor', [(i, i ^ mask) for i in range(count)])  11.8 us
    pallas_call x8, Pallas kernels, call(): pl.pallas_call(kernel, out_shape=shapes, in_specs=[first] + [rest] * (len...  9.83 us
    unnamed x24, local copies, waits for them, and re-layouts  8.35 us
    pallas_call x4, Pallas kernels, spread(): pl.pallas_call(spread_kernel(first), out_shape=shape(dtype, own.shape[0],...  1.77 us
  transfers between devices with their start and end apart: 17, of which 7 were waited for; matrix products, arithmetic and copies ran while one was open for 1% of the time, Pallas kernels for 14%

profile of v10, /device:TPU:0, one launch (start us, length us, event | category | flops | bytes accessed | tf_op | source)
XLA Modules:
  0.0 76.3 jit_solution(9769844924965028912)
XLA Ops:
  1.2 2.9 %collective-permute-start.1 = (bf16[128,2048]{1,0:T(8,128)(2,1)}, bf16[128,2048]{1,0:T(8,128)(2,1)S(1)}, u32[]{:S(2)}, u32[]{:S(2)}) collective-permute-start(bf16[128,2048]{1,0:T(8,128)(2,1)} %inputs.3), channel_id=1, source_target_pairs={{0,2},{1,3},{2,0},{3,1},{4,6},{5,7},{6,4},{7,5},{8,10},{9,11},{10,... | collective-permute-start | bytes 1572872 | tf_op jit(solution)/shard_map/ppermute | solution.py:46
  4.9 2.0 %collective-permute-start.3 = (bf16[1,2048]{1,0:T(2,128)(2,1)S(1)}, bf16[1,2048]{1,0:T(2,128)(2,1)S(1)}, u32[]{:S(2)}, u32[]{:S(2)}) collective-permute-start(bf16[1,2048]{1,0:T(2,128)(2,1)S(1)} %reshape.17.gain), channel_id=1, source_target_pairs={{0,2},{1,3},{2,0},{3,1},{4,6},{5,7},{6,4},{7,5},{8,10},{9,11},{10,... | collective-permute-start | bytes 12296 | tf_op jit(solution)/shard_map/ppermute | solution.py:46
  6.9 1.6 %copy-done = bf16[8192,128]{1,0:T(8,128)(2,1)S(1)} copy-done((bf16[8192,128]{1,0:T(8,128)(2,1)S(1)}, bf16[8192,128]{1,0:T(8,128)(2,1)}, u32[]{:S(2)}) %copy-start) | copy-done | bytes 2097176
  8.5 1.6 %copy-done.2 = bf16[8192,128]{1,0:T(8,128)(2,1)S(1)} copy-done((bf16[8192,128]{1,0:T(8,128)(2,1)S(1)}, bf16[8192,128]{1,0:T(8,128)(2,1)}, u32[]{:S(2)}) %copy-start.2) | copy-done | bytes 2097176
  10.1 1.6 %copy-done.4 = bf16[8192,128]{1,0:T(8,128)(2,1)S(1)} copy-done((bf16[8192,128]{1,0:T(8,128)(2,1)S(1)}, bf16[8192,128]{1,0:T(8,128)(2,1)}, u32[]{:S(2)}) %copy-start.4) | copy-done | bytes 2097176
  11.7 1.6 %copy-done.8 = bf16[128,8192]{1,0:T(8,128)(2,1)S(1)} copy-done((bf16[128,8192]{1,0:T(8,128)(2,1)S(1)}, bf16[128,8192]{1,0:T(8,128)(2,1)}, u32[]{:S(2)}) %copy-start.8) | copy-done | bytes 2097176
  15.2 2.8 %prepare.1 = (bf16[384,4096]{1,0:T(8,128)(2,1)S(1)}, bf16[384,4096]{1,0:T(8,128)(2,1)S(1)}, bf16[256,2048]{1,0:T(8,128)(2,1)S(1)}, bf16[256,2048]{1,0:T(8,128)(2...) custom-call(s32[4]{0:T(128)S(1)} %iota_xor_fusion.order, ...), custom_call_target="tpu_custom_call" | custom-call | flops 1000 | bytes 1000 | tf_op jit(solution)/shard_map/prepare/pallas_call | solution.py:28
  18.5 9.5 %collective-permute-done.3 = bf16[1,2048]{1,0:T(2,128)(2,1)S(1)} collective-permute-done((bf16[1,2048]{1,0:T(2,128)(2,1)S(1)}, bf16[1,2048]{1,0:T(2,128)(2,1)S(1)}, u32[]{:S(2)}, u32[]{:S(2)}) %collective-permute-start.3) | collective-permute-done | bytes 4128 | tf_op jit(solution)/shard_map/ppermute | solution.py:46
  28.0 1.6 %add_grad.1 = (f32[128,128]{1,0:T(8,128)S(1)}, f32[128,128]{1,0:T(8,128)S(1)}) custom-call(bf16[128,2048]{1,0:T(8,128)(2,1)} %collective-permute-done.2.c2, bf16[2048,256]{1,0:T(8,128)(2,1)S(1)} %get-tuple-element.40.there_turned, f32[128,256]{1,0:T(8,128)S(1)} %get-tuple-element.41.part), custom_call_target="tpu_custom_call" | custom-call | flops 1000 | bytes 1000 | tf_op jit(solution)/shard_map/add_grad/pallas_call | solution.py:28
  30.4 1.0 %collective-permute-done.6.gain_near = bf16[2,2048]{1,0:T(2,128)(2,1)S(1)} collective-permute-done((bf16[2,2048]{1,0:T(2,128)(2,1)S(1)}, bf16[2,2048]{1,0:T(2,128)(2,1)S(1)}, u32[]{:S(2)}, u32[]{:S(2)}) %collective-permute-start.6) | collective-permute-done | bytes 8224 | tf_op jit(solution)/shard_map/ppermute | solution.py:46
  31.4 2.2 %project.1 = (bf16[128,384]{1,0:T(8,128)(2,1)S(1)}, f32[128,1]{1,0:T(8,128)S(1)}, bf16[128,512]{1,0:T(8,128)(2,1)S(1)}) custom-call(s32[4]{0:T(128)S(1)} %iota_xor_fusion.order, bf16[128,2048]{1,0:T(8,128)(2,1)S(1)} %copy-done.6, bf16[128,2048]{1,0:T(8,128)(2,1)S(1)} %collective-permute-done.x1, bf16[128,2048]{1,0:T(8,128)(2,1)S(1)} %collective-permute-done.1.x2, ...), custom_call_target="tpu_custom_call" | custom-call | flops 1000 | bytes 1000 | tf_op jit(solution)/shard_map/project/pallas_call | solution.py:28
  33.9 1.7 %collective-permute-start.11 = (bf16[256,2048]{1,0:T(8,128)(2,1)S(1)}, bf16[256,2048]{1,0:T(8,128)(2,1)S(1)}, u32[]{:S(2)}, u32[]{:S(2)}) collective-permute-start(bf16[256,2048]{1,0:T(8,128)(2,1)S(1)} %get-tuple-element.52), channel_id=1, source_target_pairs={{0,2},{1,3},{2,0},{3,1},{4,6},{5,7},{6,4},{7,5},{8,10},{9,11},{10,... | collective-permute-start | bytes 3145736 | tf_op jit(solution)/shard_map/ppermute | solution.py:46
  35.7 12.9 %all_to_all.22 = bf16[8,16,512]{2,1,0:T(8,128)(2,1)S(1)} all-to-all(bf16[8,16,512]{2,1,0:T(8,128)(2,1)S(1)} %bitcast.9), channel_id=1, replica_groups=mesh['dp'=8,'tensor'=4] {'dp'}, dimensions={0} | all-to-all | bytes 262144 | tf_op jit(solution)/shard_map/all_to_all | solution.py:402
  48.6 1.1 %attend.1 = bf16[128,512]{1,0:T(8,128)(2,1)S(1)} custom-call(bf16[128,512]{1,0:T(8,128)(2,1)S(1)} %bitcast.7, s32[1,128]{1,0:T(1,128)S(1)} %get-tuple-element.46.receive, s32[1,128]{1,0:T(1,128)S(1)} %get-tuple-element.47.segments), custom_call_target="tpu_custom_call" | custom-call | flops 1000 | bytes 1000 | tf_op jit(solution)/shard_map/attend/pallas_call | solution.py:28
  49.7 9.7 %all_to_all.23 = bf16[8,16,512]{2,1,0:T(8,128)(2,1)S(1)} all-to-all(bf16[8,16,512]{2,1,0:T(8,128)(2,1)S(1)} %bitcast.8), channel_id=1, replica_groups=mesh['dp'=8,'tensor'=4] {'dp'}, dimensions={0} | all-to-all | bytes 262144 | tf_op jit(solution)/shard_map/all_to_all | solution.py:402
  61.5 0.9 %collective-permute-start.14 = (bf16[128,1024]{1,0:T(8,128)(2,1)S(1)}, bf16[128,1024]{1,0:T(8,128)(2,1)S(1)}, u32[]{:S(2)}, u32[]{:S(2)}) collective-permute-start(bf16[128,1024]{1,0:T(8,128)(2,1)S(1)} %spread_far.3), channel_id=1, source_target_pairs={{0,2},{1,3},{2,0},{3,1},{4,6},{5,7},{6,4},{7,5},{8,10},{9,11},{10,... | collective-permute-start | bytes 786440 | tf_op jit(solution)/shard_map/ppermute | solution.py:46
  62.4 1.9 %collective-permute-done.9.far = bf16[128,256]{1,0:T(8,128)(2,1)S(1)} collective-permute-done((bf16[128,256]{1,0:T(8,128)(2,1)S(1)}, bf16[128,256]{1,0:T(8,128)(2,1)S(1)}, u32[]{:S(2)}, u32[]{:S(2)}) %collective-permute-start.9) | collective-permute-done | bytes 65568 | tf_op jit(solution)/shard_map/ppermute | solution.py:46
  65.5 1.6 %collective-permute-start.16 = (bf16[128,512]{1,0:T(8,128)(2,1)S(1)}, bf16[128,512]{1,0:T(8,128)(2,1)S(1)}, u32[]{:S(2)}, u32[]{:S(2)}) collective-permute-start(bf16[128,512]{1,0:T(8,128)(2,1)S(1)} %spread_far.5), channel_id=1, source_target_pairs={{0,2},{1,3},{2,0},{3,1},{4,6},{5,7},{6,4},{7,5},{8,10},{9,11},{10,... | collective-permute-start | bytes 393224 | tf_op jit(solution)/shard_map/ppermute | solution.py:46
  67.1 1.3 %collective-permute-done.10.last = bf16[128,256]{1,0:T(8,128)(2,1)S(1)} collective-permute-done((bf16[128,256]{1,0:T(8,128)(2,1)S(1)}, bf16[128,256]{1,0:T(8,128)(2,1)S(1)}, u32[]{:S(2)}, u32[]{:S(2)}) %collective-permute-start.10) | collective-permute-done | bytes 65568 | tf_op jit(solution)/shard_map/ppermute | solution.py:46
  68.3 1.3 %finish_out.1 = bf16[128,2048]{1,0:T(8,128)(2,1)} custom-call(bf16[128,2048]{1,0:T(8,128)(2,1)S(1)} %copy-done.6, bf16[128,256]{1,0:T(8,128)(2,1)S(1)} %get-tuple-element.49.own, bf16[128,256]{1,0:T(8,128)(2,1)S(1)} %collective-permute-done.8.near, bf16[128,256]{1,0:T(8,128)(2,1)S(1)} %collective-permute-done.9.far, ...), custom_call_target="tpu_custom_call" | custom-call | flops 1000 | bytes 1000 | tf_op jit(solution)/shard_map/finish_out/pallas_call | solution.py:28
  70.3 3.2 %collective-permute-done.15.pieces_1_ = bf16[128,512]{1,0:T(8,128)(2,1)S(1)} collective-permute-done((bf16[128,512]{1,0:T(8,128)(2,1)S(1)}, bf16[128,512]{1,0:T(8,128)(2,1)S(1)}, u32[]{:S(2)}, u32[]{:S(2)}) %collective-permute-start.15) | collective-permute-done | bytes 131104 | tf_op jit(solution)/shard_map/ppermute | solution.py:46
  73.6 1.3 %finish_most.1 = (bf16[128,2048]{1,0:T(8,128)(2,1)}, f32[128,512]{1,0:T(8,128)S(1)}) custom-call(bf16[128,2048]{1,0:T(8,128)(2,1)S(1)} %copy-done.6, bf16[128,2048]{1,0:T(8,128)(2,1)S(1)} %copy-done.7, bf16[1,2048]{1,0:T(2,128)(2,1)S(1)} %reshape.17.gain, f32[128,1]{1,0:T(8,128)S(1)} %get-tuple-element.53.inverse, ...), custom_call_target="tpu_custom_call" | custom-call | flops 1000 | bytes 1000 | tf_op jit(solution)/shard_map/finish_most/pallas_call | solution.py:380
  74.8 0.7 collective-permute-done.16.rest
  75.6 0.8 finish_rest.1
  (53 shorter events, 8.8 us)
Async XLA Ops:
  0.6 6.3 %collective-permute-start.4 = (bf16[128,8192]{1,0:T(8,128)(2,1)}, bf16[128,8192]{1,0:T(8,128)(2,1)S(1)}, u32[]{:S(2)}, u32[]{:S(2)}) collective-permute-start(bf16[128,8192]{1,0:T(8,128)(2,1)} %w_output.1), channel_id=1, source_target_pairs={{0,1},{1,0},{2,3},{3,2},{4,5},{5,4},{6,7},{7,6},{8,9},{9,8},{10,11... | collective-permute-start | bytes 6291464 | tf_op jit(solution)/shard_map/ppermute | solution.py:46
  1.1 16.9 %collective-permute-start = (bf16[128,2048]{1,0:T(8,128)(2,1)}, bf16[128,2048]{1,0:T(8,128)(2,1)S(1)}, u32[]{:S(2)}, u32[]{:S(2)}) collective-permute-start(bf16[128,2048]{1,0:T(8,128)(2,1)} %inputs.3), channel_id=1, source_target_pairs={{0,1},{1,0},{2,3},{3,2},{4,5},{5,4},{6,7},{7,6},{8,9},{9,8},{10,11... | collective-permute-start | bytes 1572872 | tf_op jit(solution)/shard_map/ppermute | solution.py:46
  1.2 26.8 %collective-permute-start.1 = (bf16[128,2048]{1,0:T(8,128)(2,1)}, bf16[128,2048]{1,0:T(8,128)(2,1)S(1)}, u32[]{:S(2)}, u32[]{:S(2)}) collective-permute-start(bf16[128,2048]{1,0:T(8,128)(2,1)} %inputs.3), channel_id=1, source_target_pairs={{0,2},{1,3},{2,0},{3,1},{4,6},{5,7},{6,4},{7,5},{8,10},{9,11},{10,... | collective-permute-start | bytes 1572872 | tf_op jit(solution)/shard_map/ppermute | solution.py:46
  4.2 23.8 %collective-permute-start.2 = (bf16[128,2048]{1,0:T(8,128)(2,1)}, bf16[128,2048]{1,0:T(8,128)(2,1)}, u32[]{:S(2)}, u32[]{:S(2)}) collective-permute-start(bf16[128,2048]{1,0:T(8,128)(2,1)} %cotangent.1), channel_id=1, source_target_pairs={{0,2},{1,3},{2,0},{3,1},{4,6},{5,7},{6,4},{7,5},{8,10},{9,11},{10,... | collective-permute-start | bytes 1572872 | tf_op jit(solution)/shard_map/ppermute | solution.py:46
  4.9 23.1 %collective-permute-start.3 = (bf16[1,2048]{1,0:T(2,128)(2,1)S(1)}, bf16[1,2048]{1,0:T(2,128)(2,1)S(1)}, u32[]{:S(2)}, u32[]{:S(2)}) collective-permute-start(bf16[1,2048]{1,0:T(2,128)(2,1)S(1)} %reshape.17.gain), channel_id=1, source_target_pairs={{0,2},{1,3},{2,0},{3,1},{4,6},{5,7},{6,4},{7,5},{8,10},{9,11},{10,... | collective-permute-start | bytes 12296 | tf_op jit(solution)/shard_map/ppermute | solution.py:46
  6.9 1.6 %copy-start = (bf16[8192,128]{1,0:T(8,128)(2,1)S(1)}, bf16[8192,128]{1,0:T(8,128)(2,1)}, u32[]{:S(2)}) copy-start(bf16[8192,128]{1,0:T(8,128)(2,1)} %w_query.3) | copy-start | bytes 6291460
  8.5 1.6 %copy-start.2 = (bf16[8192,128]{1,0:T(8,128)(2,1)S(1)}, bf16[8192,128]{1,0:T(8,128)(2,1)}, u32[]{:S(2)}) copy-start(bf16[8192,128]{1,0:T(8,128)(2,1)} %w_key.3) | copy-start | bytes 6291460
  15.2 2.8 %copy-start.6 = (bf16[128,2048]{1,0:T(8,128)(2,1)S(1)}, bf16[128,2048]{1,0:T(8,128)(2,1)}, u32[]{:S(2)}) copy-start(bf16[128,2048]{1,0:T(8,128)(2,1)} %inputs.3) | copy-start | bytes 1572868
  15.2 2.8 %copy-start.7 = (bf16[128,2048]{1,0:T(8,128)(2,1)S(1)}, bf16[128,2048]{1,0:T(8,128)(2,1)}, u32[]{:S(2)}) copy-start(bf16[128,2048]{1,0:T(8,128)(2,1)} %cotangent.1) | copy-start | bytes 1572868
  15.2 16.2 %copy-start.5 = (bf16[8192,128]{1,0:T(8,128)(2,1)S(1)}, bf16[8192,128]{1,0:T(8,128)(2,1)}, u32[]{:S(2)}) copy-start(bf16[8192,128]{1,0:T(8,128)(2,1)} %w_value.3) | copy-start | bytes 6291460
  18.1 13.4 %copy-start.1 = (bf16[8192,128]{1,0:T(8,128)(2,1)S(1)}, bf16[8192,128]{1,0:T(8,128)(2,1)}, u32[]{:S(2)}) copy-start(bf16[8192,128]{1,0:T(8,128)(2,1)} %w_query.3) | copy-start | bytes 6291460
  18.1 13.4 %copy-start.3 = (bf16[8192,128]{1,0:T(8,128)(2,1)S(1)}, bf16[8192,128]{1,0:T(8,128)(2,1)}, u32[]{:S(2)}) copy-start(bf16[8192,128]{1,0:T(8,128)(2,1)} %w_key.3) | copy-start | bytes 6291460
  28.0 3.4 %collective-permute-start.5 = (bf16[128,2048]{1,0:T(8,128)(2,1)S(1)}, bf16[128,2048]{1,0:T(8,128)(2,1)S(1)}, u32[]{:S(2)}, u32[]{:S(2)}) collective-permute-start(bf16[128,2048]{1,0:T(8,128)(2,1)S(1)} %collective-permute-done.1.x2), channel_id=1, source_target_pairs={{0,1},{1,0},{2,3},{3,2},{4,5},{5,4},{6,7},{7,6},{8,9},{9,8},{10,11... | collective-permute-start | bytes 1572872 | tf_op jit(solution)/shard_map/ppermute | solution.py:46
  29.6 1.8 %collective-permute-start.7 = (f32[128,128]{1,0:T(8,128)S(1)}, f32[128,128]{1,0:T(8,128)S(1)}, u32[]{:S(2)}, u32[]{:S(2)}) collective-permute-start(f32[128,128]{1,0:T(8,128)S(1)} %get-tuple-element.43), channel_id=1, source_target_pairs={{0,1},{1,0},{2,3},{3,2},{4,5},{5,4},{6,7},{7,6},{8,9},{9,8},{10,11... | collective-permute-start | bytes 196616 | tf_op jit(solution)/shard_map/ppermute | solution.py:46
  30.2 1.2 %collective-permute-start.6 = (bf16[2,2048]{1,0:T(2,128)(2,1)S(1)}, bf16[2,2048]{1,0:T(2,128)(2,1)S(1)}, u32[]{:S(2)}, u32[]{:S(2)}) collective-permute-start(bf16[2,2048]{1,0:T(2,128)(2,1)S(1)} %pad_maximum_fusion.gain_own), channel_id=1, source_target_pairs={{0,1},{1,0},{2,3},{3,2},{4,5},{5,4},{6,7},{7,6},{8,9},{9,8},{10,11... | collective-permute-start | bytes 24584 | tf_op jit(solution)/shard_map/ppermute | solution.py:46
  33.7 27.4 %collective-permute-start.13 = (bf16[384,4096]{1,0:T(8,128)(2,1)S(1)}, bf16[384,4096]{1,0:T(8,128)(2,1)S(1)}, u32[]{:S(2)}, u32[]{:S(2)}) collective-permute-start(bf16[384,4096]{1,0:T(8,128)(2,1)S(1)} %get-tuple-element.57), channel_id=1, source_target_pairs={{0,1},{1,0},{2,3},{3,2},{4,5},{5,4},{6,7},{7,6},{8,9},{9,8},{10,11... | collective-permute-start | bytes 9437192 | tf_op jit(solution)/shard_map/ppermute | solution.py:46
  33.9 34.4 %collective-permute-start.11 = (bf16[256,2048]{1,0:T(8,128)(2,1)S(1)}, bf16[256,2048]{1,0:T(8,128)(2,1)S(1)}, u32[]{:S(2)}, u32[]{:S(2)}) collective-permute-start(bf16[256,2048]{1,0:T(8,128)(2,1)S(1)} %get-tuple-element.52), channel_id=1, source_target_pairs={{0,2},{1,3},{2,0},{3,1},{4,6},{5,7},{6,4},{7,5},{8,10},{9,11},{10,... | collective-permute-start | bytes 3145736 | tf_op jit(solution)/shard_map/ppermute | solution.py:46
  59.7 1.4 %collective-permute-start.12 = (bf16[128,384]{1,0:T(8,128)(2,1)S(1)}, bf16[128,384]{1,0:T(8,128)(2,1)S(1)}, u32[]{:S(2)}, u32[]{:S(2)}) collective-permute-start(bf16[128,384]{1,0:T(8,128)(2,1)S(1)} %get-tuple-element.60.own), channel_id=1, source_target_pairs={{0,1},{1,0},{2,3},{3,2},{4,5},{5,4},{6,7},{7,6},{8,9},{9,8},{10,11... | collective-permute-start | bytes 294920 | tf_op jit(solution)/shard_map/ppermute | solution.py:46
  59.8 4.5 %collective-permute-start.9 = (bf16[128,256]{1,0:T(8,128)(2,1)S(1)}, bf16[128,256]{1,0:T(8,128)(2,1)S(1)}, u32[]{:S(2)}, u32[]{:S(2)}) collective-permute-start(bf16[128,256]{1,0:T(8,128)(2,1)S(1)} %get-tuple-element.49.own), channel_id=1, source_target_pairs={{0,2},{1,3},{2,0},{3,1},{4,6},{5,7},{6,4},{7,5},{8,10},{9,11},{10,... | collective-permute-start | bytes 196616 | tf_op jit(solution)/shard_map/ppermute | solution.py:46
  61.5 12.0 %collective-permute-start.14 = (bf16[128,1024]{1,0:T(8,128)(2,1)S(1)}, bf16[128,1024]{1,0:T(8,128)(2,1)S(1)}, u32[]{:S(2)}, u32[]{:S(2)}) collective-permute-start(bf16[128,1024]{1,0:T(8,128)(2,1)S(1)} %spread_far.3), channel_id=1, source_target_pairs={{0,2},{1,3},{2,0},{3,1},{4,6},{5,7},{6,4},{7,5},{8,10},{9,11},{10,... | collective-permute-start | bytes 786440 | tf_op jit(solution)/shard_map/ppermute | solution.py:46
  62.4 4.7 %collective-permute-start.8 = (bf16[128,256]{1,0:T(8,128)(2,1)S(1)}, bf16[128,256]{1,0:T(8,128)(2,1)S(1)}, u32[]{:S(2)}, u32[]{:S(2)}) collective-permute-start(bf16[128,256]{1,0:T(8,128)(2,1)S(1)} %get-tuple-element.49.own), channel_id=1, source_target_pairs={{0,1},{1,0},{2,3},{3,2},{4,5},{5,4},{6,7},{7,6},{8,9},{9,8},{10,11... | collective-permute-start | bytes 196616 | tf_op jit(solution)/shard_map/ppermute | solution.py:46
  64.6 9.0 %collective-permute-start.15 = (bf16[128,512]{1,0:T(8,128)(2,1)S(1)}, bf16[128,512]{1,0:T(8,128)(2,1)S(1)}, u32[]{:S(2)}, u32[]{:S(2)}) collective-permute-start(bf16[128,512]{1,0:T(8,128)(2,1)S(1)} %spread_far.4), channel_id=1, source_target_pairs={{0,2},{1,3},{2,0},{3,1},{4,6},{5,7},{6,4},{7,5},{8,10},{9,11},{10,... | collective-permute-start | bytes 393224 | tf_op jit(solution)/shard_map/ppermute | solution.py:46
  65.5 10.1 %collective-permute-start.16 = (bf16[128,512]{1,0:T(8,128)(2,1)S(1)}, bf16[128,512]{1,0:T(8,128)(2,1)S(1)}, u32[]{:S(2)}, u32[]{:S(2)}) collective-permute-start(bf16[128,512]{1,0:T(8,128)(2,1)S(1)} %spread_far.5), channel_id=1, source_target_pairs={{0,2},{1,3},{2,0},{3,1},{4,6},{5,7},{6,4},{7,5},{8,10},{9,11},{10,... | collective-permute-start | bytes 393224 | tf_op jit(solution)/shard_map/ppermute | solution.py:46
  67.1 1.3 %collective-permute-start.10 = (bf16[128,256]{1,0:T(8,128)(2,1)S(1)}, bf16[128,256]{1,0:T(8,128)(2,1)S(1)}, u32[]{:S(2)}, u32[]{:S(2)}) collective-permute-start(bf16[128,256]{1,0:T(8,128)(2,1)S(1)} %collective-permute-done.9.far), channel_id=1, source_target_pairs={{0,1},{1,0},{2,3},{3,2},{4,5},{5,4},{6,7},{7,6},{8,9},{9,8},{10,11... | collective-permute-start | bytes 196616 | tf_op jit(solution)/shard_map/ppermute | solution.py:46
  (5 other events, 5.1 us)

commit v11 on v10

--- a/solution.py
+++ b/solution.py
@@ -16,13 +16,15 @@
 VMEM = pl.BlockSpec(memory_space=pltpu.VMEM)
 SMEM = pl.BlockSpec(memory_space=pltpu.SMEM)
 TILE = 512
+SQUARES_FLOPS = 10000000000
+HOME_FLOPS = 80000000000
 
 
 def dot(left, right, dims=(((1,), (0,)), ((), ()))):
     return lax.dot_general(left, right, dims, preferred_element_type=jnp.float32)
 
 
-def call(kernel, name, out_shape, operands, scratch=(), first=SMEM, rest=VMEM):
+def call(kernel, name, out_shape, operands, scratch=(), first=SMEM, rest=VMEM, flops=1000):
     single = not isinstance(out_shape, (list, tuple))
     shapes = [out_shape] if single else list(out_shape)
     results = pl.pallas_call(
@@ -32,7 +34,7 @@
         out_specs=[VMEM] * len(shapes),
         scratch_shapes=list(scratch),
         compiler_params=pltpu.CompilerParams(vmem_limit_bytes=VMEM_LIMIT),
-        cost_estimate=pl.CostEstimate(flops=1000, bytes_accessed=1000, transcendentals=0),
+        cost_estimate=pl.CostEstimate(flops=flops, bytes_accessed=1000, transcendentals=0),
         name=name,
     )(*operands)
     return results[0] if single else results
@@ -163,7 +165,10 @@
 
 def add_squares(x2, squares):
     out = shape(jnp.float32, *squares.shape)
-    return call(add_squares_kernel, "add_squares", out, (x2, squares), first=VMEM)
+    operands = (x2, squares)
+    return call(
+        add_squares_kernel, "add_squares", out, operands, first=VMEM, flops=SQUARES_FLOPS
+    )
 
 
 def project_kernel(
@@ -178,12 +183,8 @@
     w_key,
     w_value,
     squares,
-    own_part,
-    got_part,
-    send,
     home,
     inverse,
-    bucket,
     total,
 ):
     blocks = (x0, x1, x2, x3)
@@ -191,7 +192,6 @@
     mean = (squares[...] + sum_squares(x3)) / (width * len(blocks))
     inverse_rms = lax.rsqrt(mean + EPSILON)
     inverse[...] = inverse_rms
-    head_grad = (own_part[...] + got_part[...]).astype(jnp.bfloat16)
     for index, block in enumerate(blocks):
         gain = (gain_own, gain_near)[index % 2][index // 2 : index // 2 + 1, :]
         scaled = block[...].astype(jnp.float32) * inverse_rms
@@ -200,28 +200,31 @@
         weights = jnp.concatenate([w_query[here, :], w_key[here, :], w_value[here, :]], axis=1)
         product = dot(normed, weights)
         total[...] = total[...] + product if index else product
-    rounded = total[...].astype(jnp.bfloat16)
-    home[...] = rounded
-    chosen = one_hot(send[...], rounded.shape[0])
-    split = rounded.shape[1]
-    bucket[:, :split] = dot(chosen, rounded, CONTRACT_FIRST).astype(jnp.bfloat16)
-    bucket[:, split:] = dot(chosen, head_grad, CONTRACT_FIRST).astype(jnp.bfloat16)
-
-
-def project(order, blocks, gains, weights, squares, own_part, got_part, send):
+    home[...] = total[...].astype(jnp.bfloat16)
+
+
+def project(order, blocks, gains, weights, squares):
     rows = blocks[0].shape[0]
     columns = 3 * HEAD_DIM
     return call(
         project_kernel,
         "project",
-        [
-            shape(jnp.bfloat16, rows, columns),
-            shape(jnp.float32, rows, 1),
-            shape(jnp.bfloat16, send.shape[1], columns + HEAD_DIM),
-        ],
-        (order, *blocks, *gains, *weights, squares, own_part, got_part, send),
+        [shape(jnp.bfloat16, rows, columns), shape(jnp.float32, rows, 1)],
+        (order, *blocks, *gains, *weights, squares),
         scratch=[pltpu.VMEM((rows, columns), jnp.float32)],
     )
+
+
+def fill_kernel(home, own_part, got_part, send, bucket):
+    head_grad = (own_part[...] + got_part[...]).astype(jnp.bfloat16)
+    rows = jnp.concatenate([home[...], head_grad], axis=1)
+    chosen = one_hot(send[...], rows.shape[0])
+    bucket[...] = dot(chosen, rows, CONTRACT_FIRST).astype(jnp.bfloat16)
+
+
+def fill(home, own_part, got_part, send):
+    out = shape(jnp.bfloat16, send.shape[1], 4 * HEAD_DIM)
+    return call(fill_kernel, "fill", out, (home, own_part, got_part, send), first=VMEM)
 
 
 def attend_kernel(moved, receive, segments, back):
@@ -282,7 +285,8 @@
 def bring_home(moved, send, home):
     rows = home.shape[0]
     shapes = [shape(jnp.bfloat16, rows, 3 * HEAD_DIM), shape(jnp.bfloat16, rows, 2 * HEAD_DIM)]
-    return call(bring_home_kernel, "bring_home", shapes, (moved, send, home), first=VMEM)
+    operands = (moved, send, home)
+    return call(bring_home_kernel, "bring_home", shapes, operands, first=VMEM, flops=HOME_FLOPS)
 
 
 def spread_kernel(first):
@@ -449,21 +453,16 @@
     gain_near = swap(gain_own, 1, tensor)
     own_part, near_part = add_grad(c2, there_turned, part)
     got_part = swap(near_part, 1, tensor)
-    squares = add_squares(x2, squares)
-    home, inverse_rms, bucket = project(
-        order,
-        (inputs, x1, x2, x3),
-        (gain_own, gain_near),
-        weights,
-        squares,
-        own_part,
-        got_part,
-        send,
-    )
+    squares = add_squares(x2, after(squares, near_part))
+    home, inverse_rms = project(
+        order, (inputs, x1, x2, x3), (gain_own, gain_near), weights, squares
+    )
+    bucket = fill(home, own_part, got_part, send)
     near_turned = swap(after(near_turned, home), 1, tensor)
-    there = swap(after(there, home), 2, tensor)
+    there = swap(after(there, near_part), 2, tensor)
     back = attend(move(bucket), receive, segments)
-    own, own_extras = bring_home(move(back), send, home)
+    moved, there = lax.optimization_barrier((move(back), there))
+    own, own_extras = bring_home(moved, send, home)
 
     near = swap(own, 1, tensor)
     far_extras = swap(own_extras, 2, tensor)

time: 76.7 us -> 83.6 us (1.090)
  Pallas kernels: 13.6 us -> 27.2 us
  blocking collectives: 22.7 us -> 13.4 us
  waiting for transfers between devices: 18.3 us -> 10.8 us
  starting transfers between devices: 11.8 us -> 17 us
  local copies, waits for them, and re-layouts: 9.04 us -> 13.6 us
    ppermute x17, waiting for transfers between devices: 18.3 us -> 3.63 us  [swap(): return lax.ppermute(array, 'tensor', [(i, i ^ mask) for i in range(count)])]
    all_to_all x2 -> x1, blocking collectives: 22.7 us -> 13.4 us  [move(): return lax.all_to_all(bucket, 'dp', split_axis=0, concat_axis=0, tiled=True)]
    pallas_call x4, Pallas kernels: 1.77 us -> 9.41 us  [spread(): pl.pallas_call(spread_kernel(first), out_shape=shape(dtype, own.shape[0],...]
    all_to_all x0 -> x1, waiting for transfers between devices: none -> 7.2 us  [move(): return lax.all_to_all(bucket, 'dp', split_axis=0, concat_axis=0, tiled=True)]
    pallas_call x8 -> x9, Pallas kernels: 9.83 us -> 15.8 us  [call(): pl.pallas_call(kernel, out_shape=shapes, in_specs=[first] + [rest] * (len...]
    unnamed x24 -> x38, local copies, waits for them, and re-layouts: 8.35 us -> 13 us
    all_to_all x0 -> x1, starting transfers between devices: none -> 3.37 us  [move(): return lax.all_to_all(bucket, 'dp', split_axis=0, concat_axis=0, tiled=True)]
    ppermute x17, starting transfers between devices: 11.8 us -> 13.6 us  [swap(): return lax.ppermute(array, 'tensor', [(i, i ^ mask) for i in range(count)])]
  transfers between devices with their start and end apart: 17 -> 18, of which waited for: 7 -> 4; matrix products, arithmetic and copies ran while one was open for 1% -> 1% of each run, Pallas kernels for 14% -> 30%
where the time goes in v11:
time: 83.6 us; the launch traced here: 82.9 us
  Pallas kernels  27.2 us (33%)
  starting transfers between devices  17 us (20%)
  local copies, waits for them, and re-layouts  13.6 us (16%)
  blocking collectives  13.4 us (16%)
  waiting for transfers between devices  10.8 us (13%)
  between operations  0.86 us (1%)
    pallas_call x9, Pallas kernels, call(): pl.pallas_call(kernel, out_shape=shapes, in_specs=[first] + [rest] * (len...  15.8 us
    ppermute x17, starting transfers between devices, swap(): return lax.ppermute(array, 'tensor', [(i, i ^ mask) for i in range(count)])  13.6 us
    all_to_all x1, blocking collectives, move(): return lax.all_to_all(bucket, 'dp', split_axis=0, concat_axis=0, tiled=True)  13.4 us
    unnamed x38, local copies, waits for them, and re-layouts  13 us
    pallas_call x4, Pallas kernels, spread(): pl.pallas_call(spread_kernel(first), out_shape=shape(dtype, own.shape[0],...  9.41 us
    all_to_all x1, waiting for transfers between devices, move(): return lax.all_to_all(bucket, 'dp', split_axis=0, concat_axis=0, tiled=True)  7.2 us
    ppermute x17, waiting for transfers between devices, swap(): return lax.ppermute(array, 'tensor', [(i, i ^ mask) for i in range(count)])  3.63 us
    all_to_all x1, starting transfers between devices, move(): return lax.all_to_all(bucket, 'dp', split_axis=0, concat_axis=0, tiled=True)  3.37 us
  transfers between devices with their start and end apart: 18, of which 4 were waited for; matrix products, arithmetic and copies ran while one was open for 1% of the time, Pallas kernels for 30%

profile of v11, /device:TPU:0, one launch (start us, length us, event | category | flops | bytes accessed | tf_op | source)
XLA Modules:
  0.0 82.9 jit_solution(11858300915190730349)
XLA Ops:
  1.2 2.9 %collective-permute-start.1 = (bf16[128,2048]{1,0:T(8,128)(2,1)}, bf16[128,2048]{1,0:T(8,128)(2,1)}, u32[]{:S(2)}, u32[]{:S(2)}) collective-permute-start(bf16[128,2048]{1,0:T(8,128)(2,1)} %inputs.3), channel_id=1, source_target_pairs={{0,2},{1,3},{2,0},{3,1},{4,6},{5,7},{6,4},{7,5},{8,10},{9,11},{10,... | collective-permute-start | bytes 1572872 | tf_op jit(solution)/shard_map/ppermute | solution.py:48
  4.9 2.0 %collective-permute-start.3 = (bf16[1,2048]{1,0:T(2,128)(2,1)S(1)}, bf16[1,2048]{1,0:T(2,128)(2,1)S(1)}, u32[]{:S(2)}, u32[]{:S(2)}) collective-permute-start(bf16[1,2048]{1,0:T(2,128)(2,1)S(1)} %reshape.17.gain), channel_id=1, source_target_pairs={{0,2},{1,3},{2,0},{3,1},{4,6},{5,7},{6,4},{7,5},{8,10},{9,11},{10,... | collective-permute-start | bytes 12296 | tf_op jit(solution)/shard_map/ppermute | solution.py:48
  8.3 1.6 %copy-done.2 = bf16[8192,128]{1,0:T(8,128)(2,1)S(1)} copy-done((bf16[8192,128]{1,0:T(8,128)(2,1)S(1)}, bf16[8192,128]{1,0:T(8,128)(2,1)}, u32[]{:S(2)}) %copy-start.2) | copy-done | bytes 2097176
  9.9 1.6 %copy-done.4 = bf16[8192,128]{1,0:T(8,128)(2,1)S(1)} copy-done((bf16[8192,128]{1,0:T(8,128)(2,1)S(1)}, bf16[8192,128]{1,0:T(8,128)(2,1)}, u32[]{:S(2)}) %copy-start.4) | copy-done | bytes 2097176
  11.4 1.6 %copy-done.6 = bf16[8192,128]{1,0:T(8,128)(2,1)S(1)} copy-done((bf16[8192,128]{1,0:T(8,128)(2,1)S(1)}, bf16[8192,128]{1,0:T(8,128)(2,1)}, u32[]{:S(2)}) %copy-start.6) | copy-done | bytes 2097176
  13.0 1.6 %copy-done.10 = bf16[128,8192]{1,0:T(8,128)(2,1)S(1)} copy-done((bf16[128,8192]{1,0:T(8,128)(2,1)S(1)}, bf16[128,8192]{1,0:T(8,128)(2,1)}, u32[]{:S(2)}) %copy-start.10) | copy-done | bytes 2097176
  14.6 1.6 %copy-done.12 = bf16[128,8192]{1,0:T(8,128)(2,1)S(1)} copy-done((bf16[128,8192]{1,0:T(8,128)(2,1)S(1)}, bf16[128,8192]{1,0:T(8,128)(2,1)}, u32[]{:S(2)}) %copy-start.12) | copy-done | bytes 2097176
  18.2 3.6 %prepare.1 = (bf16[384,4096]{1,0:T(8,128)(2,1)S(1)}, bf16[384,4096]{1,0:T(8,128)(2,1)S(1)}, bf16[256,2048]{1,0:T(8,128)(2,1)S(1)}, bf16[256,2048]{1,0:T(8,128)(2...) custom-call(s32[4]{0:T(128)S(1)} %iota_xor_fusion.order, ...), custom_call_target="tpu_custom_call" | custom-call | flops 1000 | bytes 1000 | tf_op jit(solution)/shard_map/prepare/pallas_call | solution.py:30
  21.8 1.6 %copy-done.18 = bf16[384,4096]{1,0:T(8,128)(2,1)} copy-done((bf16[384,4096]{1,0:T(8,128)(2,1)}, bf16[384,4096]{1,0:T(8,128)(2,1)S(1)}, u32[]{:S(2)}) %copy-start.18) | copy-done | bytes 3145752
  23.4 1.8 %begin.1 = (f32[128,1]{1,0:T(8,128)S(1)}, f32[128,256]{1,0:T(8,128)S(1)}) custom-call(bf16[128,2048]{1,0:T(8,128)(2,1)S(1)} %copy-done, bf16[128,2048]{1,0:T(8,128)(2,1)} %collective-permute-done.x1, bf16[128,2048]{1,0:T(8,128)(2,1)S(1)} %copy-done.8, bf16[2048,256]{1,0:T(8,128)(2,1)S(1)} %get-tuple-element.35.here_turned), custom_call_target="tpu_custom_call" | custom-call | flops 1000 | bytes 1000 | tf_op jit(solution)/shard_map/begin/pallas_call | solution.py:30
  25.3 2.7 %collective-permute-done.3 = bf16[1,2048]{1,0:T(2,128)(2,1)S(1)} collective-permute-done((bf16[1,2048]{1,0:T(2,128)(2,1)S(1)}, bf16[1,2048]{1,0:T(2,128)(2,1)S(1)}, u32[]{:S(2)}, u32[]{:S(2)}) %collective-permute-start.3) | collective-permute-done | bytes 4128 | tf_op jit(solution)/shard_map/ppermute | solution.py:48
  28.0 1.6 %add_grad.1 = (f32[128,128]{1,0:T(8,128)S(1)}, f32[128,128]{1,0:T(8,128)S(1)}) custom-call(bf16[128,2048]{1,0:T(8,128)(2,1)} %collective-permute-done.2.c2, bf16[2048,256]{1,0:T(8,128)(2,1)S(1)} %get-tuple-element.42.there_turned, f32[128,256]{1,0:T(8,128)S(1)} %get-tuple-element.43.part), custom_call_target="tpu_custom_call" | custom-call | flops 1000 | bytes 1000 | tf_op jit(solution)/shard_map/add_grad/pallas_call | solution.py:30
  30.3 1.8 %collective-permute-start.8 = (bf16[256,2048]{1,0:T(8,128)(2,1)}, bf16[256,2048]{1,0:T(8,128)(2,1)}, u32[]{:S(2)}, u32[]{:S(2)}) collective-permute-start(bf16[256,2048]{1,0:T(8,128)(2,1)} %get-tuple-element.52), channel_id=1, source_target_pairs={{0,2},{1,3},{2,0},{3,1},{4,6},{5,7},{6,4},{7,5},{8,10},{9,11},{10,... | collective-permute-start | bytes 3145736 | tf_op jit(solution)/shard_map/ppermute | solution.py:48
  33.5 2.7 %project.1 = (bf16[128,384]{1,0:T(8,128)(2,1)S(1)}, f32[128,1]{1,0:T(8,128)S(1)}) custom-call(s32[4]{0:T(128)S(1)} %iota_xor_fusion.order, bf16[128,2048]{1,0:T(8,128)(2,1)S(1)} %copy-done, bf16[128,2048]{1,0:T(8,128)(2,1)} %collective-permute-done.x1, bf16[128,2048]{1,0:T(8,128)(2,1)} %collective-permute-done.1.x2, ...), custom_call_target="tpu_custom_call" | custom-call | flops 1000 | bytes 1000 | tf_op jit(solution)/shard_map/project/pallas_call | solution.py:30
  36.4 13.4 %all_to_all.23 = bf16[8,16,512]{2,1,0:T(8,128)(2,1)S(1)} all-to-all(bf16[8,16,512]{2,1,0:T(8,128)(2,1)S(1)} %bitcast.7), channel_id=1, replica_groups=mesh['dp'=8,'tensor'=4] {'dp'}, dimensions={0} | all-to-all | bytes 262144 | tf_op jit(solution)/shard_map/all_to_all | solution.py:406
  49.8 1.7 %attend.1 = bf16[128,512]{1,0:T(8,128)(2,1)} custom-call(bf16[128,512]{1,0:T(8,128)(2,1)S(1)} %bitcast.6, s32[1,128]{1,0:T(1,128)S(1)} %get-tuple-element.49.receive, s32[1,128]{1,0:T(1,128)S(1)} %get-tuple-element.50.segments), custom_call_target="tpu_custom_call" | custom-call | flops 1000 | bytes 1000 | tf_op jit(solution)/shard_map/attend/pallas_call | solution.py:30
  51.5 3.4 %all-to-all-start.1 = ((bf16[8,16,512]{2,1,0:T(8,128)(2,1)}), bf16[8,16,512]{2,1,0:T(8,128)(2,1)S(1)}, u32[]{:S(2)}, u32[]{:S(2)}) async-start(bf16[8,16,512]{2,1,0:T(8,128)(2,1)} %bitcast.4), calls=%async_computation.1 | async-start | bytes 262144 | tf_op jit(solution)/shard_map/all_to_all | solution.py:406
  55.0 7.2 %all-to-all-done.1 = bf16[8,16,512]{2,1,0:T(8,128)(2,1)S(1)} async-done(((bf16[8,16,512]{2,1,0:T(8,128)(2,1)}), bf16[8,16,512]{2,1,0:T(8,128)(2,1)S(1)}, u32[]{:S(2)}, u32[]{:S(2)}) %all-to-all-start.1) | async-done | bytes 131104 | tf_op jit(solution)/shard_map/all_to_all | solution.py:406
  62.5 1.5 %collective-permute-start.10 = (bf16[128,256]{1,0:T(8,128)(2,1)S(1)}, bf16[128,256]{1,0:T(8,128)(2,1)S(1)}, u32[]{:S(2)}, u32[]{:S(2)}) collective-permute-start(bf16[128,256]{1,0:T(8,128)(2,1)S(1)} %get-tuple-element.54.own), channel_id=1, source_target_pairs={{0,2},{1,3},{2,0},{3,1},{4,6},{5,7},{6,4},{7,5},{8,10},{9,11},{10,... | collective-permute-start | bytes 196616 | tf_op jit(solution)/shard_map/ppermute | solution.py:48
  64.0 2.4 %spread_far.3 = bf16[128,1024]{1,0:T(8,128)(2,1)S(1)} custom-call(bf16[128,384]{1,0:T(8,128)(2,1)S(1)} %get-tuple-element.64.own, bf16[128,384]{1,0:T(8,128)(2,1)S(1)} %collective-permute-done.12.near, bf16[384,4096]{1,0:T(8,128)(2,1)S(1)} %get-tuple-element.59.weights, bf16[384,4096]{1,0:T(8,128)(2,1)} %collective-permute-done.13.near_weights), custom_call_target="tpu_custom_call" | custom-call | flops 1000 | bytes 1000 | tf_op jit(solution)/shard_map/spread_far/pallas_call | solution.py:304
  67.7 2.2 %spread_far.4 = bf16[128,512]{1,0:T(8,128)(2,1)S(1)} custom-call(bf16[128,384]{1,0:T(8,128)(2,1)S(1)} %get-tuple-element.64.own, bf16[128,384]{1,0:T(8,128)(2,1)S(1)} %collective-permute-done.12.near, bf16[384,4096]{1,0:T(8,128)(2,1)S(1)} %get-tuple-element.59.weights, bf16[384,4096]{1,0:T(8,128)(2,1)} %collective-permute-done.13.near_weights), custom_call_target="tpu_custom_call" | custom-call | flops 536870912 | bytes 1000 | tf_op jit(solution)/shard_map/spread_far/pallas_call | solution.py:304
  70.8 2.2 %spread_far.5 = bf16[128,512]{1,0:T(8,128)(2,1)S(1)} custom-call(bf16[128,384]{1,0:T(8,128)(2,1)S(1)} %get-tuple-element.64.own, bf16[128,384]{1,0:T(8,128)(2,1)S(1)} %collective-permute-done.12.near, bf16[384,4096]{1,0:T(8,128)(2,1)S(1)} %get-tuple-element.59.weights, bf16[384,4096]{1,0:T(8,128)(2,1)} %collective-permute-done.13.near_weights), custom_call_target="tpu_custom_call" | custom-call | flops 536870912 | bytes 1000 | tf_op jit(solution)/shard_map/spread_far/pallas_call | solution.py:304
  75.7 2.5 %finish_out.1 = bf16[128,2048]{1,0:T(8,128)(2,1)} custom-call(bf16[128,2048]{1,0:T(8,128)(2,1)S(1)} %copy-done.1, bf16[128,256]{1,0:T(8,128)(2,1)S(1)} %get-tuple-element.54.own, bf16[128,256]{1,0:T(8,128)(2,1)S(1)} %collective-permute-done.9.near, bf16[128,256]{1,0:T(8,128)(2,1)S(1)} %collective-permute-done.10.far, ...), custom_call_target="tpu_custom_call" | custom-call | flops 1000 | bytes 1000 | tf_op jit(solution)/shard_map/finish_out/pallas_call | solution.py:30
  78.2 2.7 %spread_own.1.grad_own = f32[128,2048]{1,0:T(8,128)S(1)} custom-call(bf16[128,384]{1,0:T(8,128)(2,1)S(1)} %get-tuple-element.64.own, bf16[128,384]{1,0:T(8,128)(2,1)S(1)} %collective-permute-done.12.near, bf16[384,4096]{1,0:T(8,128)(2,1)S(1)} %get-tuple-element.59.weights, bf16[384,4096]{1,0:T(8,128)(2,1)} %collective-permute-done.13.near_weights), custom_call_target="tpu_custom_call" | custom-call | flops 1000 | bytes 1000 | tf_op jit(solution)/shard_map/spread_own/pallas_call | solution.py:304
  (69 shorter events, 14.2 us)
Async XLA Ops:
  0.6 6.3 %collective-permute-start.4 = (bf16[128,8192]{1,0:T(8,128)(2,1)}, bf16[128,8192]{1,0:T(8,128)(2,1)S(1)}, u32[]{:S(2)}, u32[]{:S(2)}) collective-permute-start(bf16[128,8192]{1,0:T(8,128)(2,1)} %w_output.1), channel_id=1, source_target_pairs={{0,1},{1,0},{2,3},{3,2},{4,5},{5,4},{6,7},{7,6},{8,9},{9,8},{10,11... | collective-permute-start | bytes 6291464 | tf_op jit(solution)/shard_map/ppermute | solution.py:48
  1.1 22.3 %collective-permute-start = (bf16[128,2048]{1,0:T(8,128)(2,1)}, bf16[128,2048]{1,0:T(8,128)(2,1)}, u32[]{:S(2)}, u32[]{:S(2)}) collective-permute-start(bf16[128,2048]{1,0:T(8,128)(2,1)} %inputs.3), channel_id=1, source_target_pairs={{0,1},{1,0},{2,3},{3,2},{4,5},{5,4},{6,7},{7,6},{8,9},{9,8},{10,11... | collective-permute-start | bytes 1572872 | tf_op jit(solution)/shard_map/ppermute | solution.py:48
  1.2 26.8 %collective-permute-start.1 = (bf16[128,2048]{1,0:T(8,128)(2,1)}, bf16[128,2048]{1,0:T(8,128)(2,1)}, u32[]{:S(2)}, u32[]{:S(2)}) collective-permute-start(bf16[128,2048]{1,0:T(8,128)(2,1)} %inputs.3), channel_id=1, source_target_pairs={{0,2},{1,3},{2,0},{3,1},{4,6},{5,7},{6,4},{7,5},{8,10},{9,11},{10,... | collective-permute-start | bytes 1572872 | tf_op jit(solution)/shard_map/ppermute | solution.py:48
  4.2 23.8 %collective-permute-start.2 = (bf16[128,2048]{1,0:T(8,128)(2,1)}, bf16[128,2048]{1,0:T(8,128)(2,1)}, u32[]{:S(2)}, u32[]{:S(2)}) collective-permute-start(bf16[128,2048]{1,0:T(8,128)(2,1)} %cotangent.1), channel_id=1, source_target_pairs={{0,2},{1,3},{2,0},{3,1},{4,6},{5,7},{6,4},{7,5},{8,10},{9,11},{10,... | collective-permute-start | bytes 1572872 | tf_op jit(solution)/shard_map/ppermute | solution.py:48
  4.9 23.1 %collective-permute-start.3 = (bf16[1,2048]{1,0:T(2,128)(2,1)S(1)}, bf16[1,2048]{1,0:T(2,128)(2,1)S(1)}, u32[]{:S(2)}, u32[]{:S(2)}) collective-permute-start(bf16[1,2048]{1,0:T(2,128)(2,1)S(1)} %reshape.17.gain), channel_id=1, source_target_pairs={{0,2},{1,3},{2,0},{3,1},{4,6},{5,7},{6,4},{7,5},{8,10},{9,11},{10,... | collective-permute-start | bytes 12296 | tf_op jit(solution)/shard_map/ppermute | solution.py:48
  18.2 5.2 %copy-start = (bf16[128,2048]{1,0:T(8,128)(2,1)S(1)}, bf16[128,2048]{1,0:T(8,128)(2,1)}, u32[]{:S(2)}) copy-start(bf16[128,2048]{1,0:T(8,128)(2,1)} %inputs.3) | copy-start | bytes 1572868
  18.2 5.2 %copy-start.8 = (bf16[128,2048]{1,0:T(8,128)(2,1)S(1)}, bf16[128,2048]{1,0:T(8,128)(2,1)}, u32[]{:S(2)}) copy-start(bf16[128,2048]{1,0:T(8,128)(2,1)} %cotangent.1) | copy-start | bytes 1572868
  23.4 6.2 %copy-start.13 = (bf16[256,2048]{1,0:T(8,128)(2,1)}, bf16[256,2048]{1,0:T(8,128)(2,1)S(1)}, u32[]{:S(2)}) copy-start(bf16[256,2048]{1,0:T(8,128)(2,1)S(1)} %get-tuple-element.55.here) | copy-start | bytes 3145732
  29.6 6.6 %collective-permute-start.7 = (f32[128,128]{1,0:T(8,128)S(1)}, f32[128,128]{1,0:T(8,128)S(1)}, u32[]{:S(2)}, u32[]{:S(2)}) collective-permute-start(f32[128,128]{1,0:T(8,128)S(1)} %get-tuple-element.44), channel_id=1, source_target_pairs={{0,1},{1,0},{2,3},{3,2},{4,5},{5,4},{6,7},{7,6},{8,9},{9,8},{10,11... | collective-permute-start | bytes 196616 | tf_op jit(solution)/shard_map/ppermute | solution.py:48
  29.7 3.7 %collective-permute-start.6 = (bf16[2,2048]{1,0:T(2,128)(2,1)S(1)}, bf16[2,2048]{1,0:T(2,128)(2,1)S(1)}, u32[]{:S(2)}, u32[]{:S(2)}) collective-permute-start(bf16[2,2048]{1,0:T(2,128)(2,1)S(1)} %pad_maximum_fusion.gain_own), channel_id=1, source_target_pairs={{0,1},{1,0},{2,3},{3,2},{4,5},{5,4},{6,7},{7,6},{8,9},{9,8},{10,11... | collective-permute-start | bytes 24584 | tf_op jit(solution)/shard_map/ppermute | solution.py:48
  30.3 3.2 %collective-permute-start.5 = (bf16[128,2048]{1,0:T(8,128)(2,1)}, bf16[128,2048]{1,0:T(8,128)(2,1)S(1)}, u32[]{:S(2)}, u32[]{:S(2)}) collective-permute-start(bf16[128,2048]{1,0:T(8,128)(2,1)} %collective-permute-done.1.x2), channel_id=1, source_target_pairs={{0,1},{1,0},{2,3},{3,2},{4,5},{5,4},{6,7},{7,6},{8,9},{9,8},{10,11... | collective-permute-start | bytes 1572872 | tf_op jit(solution)/shard_map/ppermute | solution.py:48
  30.3 3.1 %copy-start.7 = (bf16[8192,128]{1,0:T(8,128)(2,1)S(1)}, bf16[8192,128]{1,0:T(8,128)(2,1)}, u32[]{:S(2)}) copy-start(bf16[8192,128]{1,0:T(8,128)(2,1)} %w_value.3) | copy-start | bytes 6291460
  30.3 31.9 %collective-permute-start.8 = (bf16[256,2048]{1,0:T(8,128)(2,1)}, bf16[256,2048]{1,0:T(8,128)(2,1)}, u32[]{:S(2)}, u32[]{:S(2)}) collective-permute-start(bf16[256,2048]{1,0:T(8,128)(2,1)} %get-tuple-element.52), channel_id=1, source_target_pairs={{0,2},{1,3},{2,0},{3,1},{4,6},{5,7},{6,4},{7,5},{8,10},{9,11},{10,... | collective-permute-start | bytes 3145736 | tf_op jit(solution)/shard_map/ppermute | solution.py:48
  51.5 10.7 %all-to-all-start.1 = ((bf16[8,16,512]{2,1,0:T(8,128)(2,1)}), bf16[8,16,512]{2,1,0:T(8,128)(2,1)S(1)}, u32[]{:S(2)}, u32[]{:S(2)}) async-start(bf16[8,16,512]{2,1,0:T(8,128)(2,1)} %bitcast.4), calls=%async_computation.1 | async-start | bytes 262144 | tf_op jit(solution)/shard_map/all_to_all | solution.py:406
  54.9 9.1 %collective-permute-start.13 = (bf16[384,4096]{1,0:T(8,128)(2,1)}, bf16[384,4096]{1,0:T(8,128)(2,1)}, u32[]{:S(2)}, u32[]{:S(2)}) collective-permute-start(bf16[384,4096]{1,0:T(8,128)(2,1)} %copy-done.18), channel_id=1, source_target_pairs={{0,1},{1,0},{2,3},{3,2},{4,5},{5,4},{6,7},{7,6},{8,9},{9,8},{10,11... | collective-permute-start | bytes 9437192 | tf_op jit(solution)/shard_map/ppermute | solution.py:48
  62.5 1.6 %collective-permute-start.12 = (bf16[128,384]{1,0:T(8,128)(2,1)S(1)}, bf16[128,384]{1,0:T(8,128)(2,1)S(1)}, u32[]{:S(2)}, u32[]{:S(2)}) collective-permute-start(bf16[128,384]{1,0:T(8,128)(2,1)S(1)} %get-tuple-element.64.own), channel_id=1, source_target_pairs={{0,1},{1,0},{2,3},{3,2},{4,5},{5,4},{6,7},{7,6},{8,9},{9,8},{10,11... | collective-permute-start | bytes 294920 | tf_op jit(solution)/shard_map/ppermute | solution.py:48
  62.5 5.1 %collective-permute-start.10 = (bf16[128,256]{1,0:T(8,128)(2,1)S(1)}, bf16[128,256]{1,0:T(8,128)(2,1)S(1)}, u32[]{:S(2)}, u32[]{:S(2)}) collective-permute-start(bf16[128,256]{1,0:T(8,128)(2,1)S(1)} %get-tuple-element.54.own), channel_id=1, source_target_pairs={{0,2},{1,3},{2,0},{3,1},{4,6},{5,7},{6,4},{7,5},{8,10},{9,11},{10,... | collective-permute-start | bytes 196616 | tf_op jit(solution)/shard_map/ppermute | solution.py:48
  66.4 14.5 %collective-permute-start.14 = (bf16[128,1024]{1,0:T(8,128)(2,1)S(1)}, bf16[128,1024]{1,0:T(8,128)(2,1)S(1)}, u32[]{:S(2)}, u32[]{:S(2)}) collective-permute-start(bf16[128,1024]{1,0:T(8,128)(2,1)S(1)} %spread_far.3), channel_id=1, source_target_pairs={{0,2},{1,3},{2,0},{3,1},{4,6},{5,7},{6,4},{7,5},{8,10},{9,11},{10,... | collective-permute-start | bytes 786440 | tf_op jit(solution)/shard_map/ppermute | solution.py:48
  69.9 5.8 %copy-start.1 = (bf16[128,2048]{1,0:T(8,128)(2,1)S(1)}, bf16[128,2048]{1,0:T(8,128)(2,1)}, u32[]{:S(2)}) copy-start(bf16[128,2048]{1,0:T(8,128)(2,1)} %inputs.3) | copy-start | bytes 1572868
  69.9 5.8 %copy-start.14 = (bf16[256,2048]{1,0:T(8,128)(2,1)S(1)}, bf16[256,2048]{1,0:T(8,128)(2,1)}, u32[]{:S(2)}) copy-start(bf16[256,2048]{1,0:T(8,128)(2,1)} %copy-done.13) | copy-start | bytes 3145732
  69.9 11.0 %collective-permute-start.15 = (bf16[128,512]{1,0:T(8,128)(2,1)S(1)}, bf16[128,512]{1,0:T(8,128)(2,1)S(1)}, u32[]{:S(2)}, u32[]{:S(2)}) collective-permute-start(bf16[128,512]{1,0:T(8,128)(2,1)S(1)} %spread_far.4), channel_id=1, source_target_pairs={{0,2},{1,3},{2,0},{3,1},{4,6},{5,7},{6,4},{7,5},{8,10},{9,11},{10,... | collective-permute-start | bytes 393224 | tf_op jit(solution)/shard_map/ppermute | solution.py:48
  73.0 9.2 %collective-permute-start.16 = (bf16[128,512]{1,0:T(8,128)(2,1)S(1)}, bf16[128,512]{1,0:T(8,128)(2,1)S(1)}, u32[]{:S(2)}, u32[]{:S(2)}) collective-permute-start(bf16[128,512]{1,0:T(8,128)(2,1)S(1)} %spread_far.5), channel_id=1, source_target_pairs={{0,2},{1,3},{2,0},{3,1},{4,6},{5,7},{6,4},{7,5},{8,10},{9,11},{10,... | collective-permute-start | bytes 393224 | tf_op jit(solution)/shard_map/ppermute | solution.py:48
  74.3 1.3 %collective-permute-start.9 = (bf16[128,256]{1,0:T(8,128)(2,1)S(1)}, bf16[128,256]{1,0:T(8,128)(2,1)S(1)}, u32[]{:S(2)}, u32[]{:S(2)}) collective-permute-start(bf16[128,256]{1,0:T(8,128)(2,1)S(1)} %get-tuple-element.54.own), channel_id=1, source_target_pairs={{0,1},{1,0},{2,3},{3,2},{4,5},{5,4},{6,7},{7,6},{8,9},{9,8},{10,11... | collective-permute-start | bytes 196616 | tf_op jit(solution)/shard_map/ppermute | solution.py:48
  74.3 1.4 %collective-permute-start.11 = (bf16[128,256]{1,0:T(8,128)(2,1)S(1)}, bf16[128,256]{1,0:T(8,128)(2,1)S(1)}, u32[]{:S(2)}, u32[]{:S(2)}) collective-permute-start(bf16[128,256]{1,0:T(8,128)(2,1)S(1)} %collective-permute-done.10.far), channel_id=1, source_target_pairs={{0,1},{1,0},{2,3},{3,2},{4,5},{5,4},{6,7},{7,6},{8,9},{9,8},{10,11... | collective-permute-start | bytes 196616 | tf_op jit(solution)/shard_map/ppermute | solution.py:48
  (13 other events, 21.8 us)

commit v12 on v11

--- a/solution.py
+++ b/solution.py
@@ -17,7 +17,7 @@
 SMEM = pl.BlockSpec(memory_space=pltpu.SMEM)
 TILE = 512
 SQUARES_FLOPS = 10000000000
-HOME_FLOPS = 80000000000
+HOME_FLOPS = 30000000000
 
 
 def dot(left, right, dims=(((1,), (0,)), ((), ()))):

time: 83.6 us -> 83 us (level)
  blocking collectives: 13.4 us -> 9.86 us
  starting transfers between devices: 17 us -> 19.7 us
    all_to_all x1, blocking collectives: 13.4 us -> 9.86 us  [move(): return lax.all_to_all(bucket, 'dp', split_axis=0, concat_axis=0, tiled=True)]
    all_to_all x1, starting transfers between devices: 3.37 us -> 6.03 us  [move(): return lax.all_to_all(bucket, 'dp', split_axis=0, concat_axis=0, tiled=True)]
where the time goes in v12:
time: 83 us; the launch traced here: 82.3 us
  Pallas kernels  27.2 us (33%)
  starting transfers between devices  19.7 us (24%)
  local copies, waits for them, and re-layouts  13.6 us (16%)
  waiting for transfers between devices  11.1 us (13%)
  blocking collectives  9.86 us (12%)
  between operations  0.84 us (1%)
    pallas_call x9, Pallas kernels, call(): pl.pallas_call(kernel, out_shape=shapes, in_specs=[first] + [rest] * (len...  15.8 us
    ppermute x17, starting transfers between devices, swap(): return lax.ppermute(array, 'tensor', [(i, i ^ mask) for i in range(count)])  13.7 us
    unnamed x38, local copies, waits for them, and re-layouts  13 us
    all_to_all x1, blocking collectives, move(): return lax.all_to_all(bucket, 'dp', split_axis=0, concat_axis=0, tiled=True)  9.86 us
    pallas_call x4, Pallas kernels, spread(): pl.pallas_call(spread_kernel(first), out_shape=shape(dtype, own.shape[0],...  9.39 us
    all_to_all x1, waiting for transfers between devices, move(): return lax.all_to_all(bucket, 'dp', split_axis=0, concat_axis=0, tiled=True)  7.43 us
    all_to_all x1, starting transfers between devices, move(): return lax.all_to_all(bucket, 'dp', split_axis=0, concat_axis=0, tiled=True)  6.03 us
    ppermute x17, waiting for transfers between devices, swap(): return lax.ppermute(array, 'tensor', [(i, i ^ mask) for i in range(count)])  3.64 us
  transfers between devices with their start and end apart: 18, of which 4 were waited for; matrix products, arithmetic and copies ran while one was open for 1% of the time, Pallas kernels for 30%

profile of v12, /device:TPU:0, one launch (start us, length us, event | category | flops | bytes accessed | tf_op | source)
XLA Modules:
  0.0 82.3 jit_solution(13858681400224627869)
XLA Ops:
  1.2 2.9 %collective-permute-start.1 = (bf16[128,2048]{1,0:T(8,128)(2,1)}, bf16[128,2048]{1,0:T(8,128)(2,1)}, u32[]{:S(2)}, u32[]{:S(2)}) collective-permute-start(bf16[128,2048]{1,0:T(8,128)(2,1)} %inputs.3), channel_id=1, source_target_pairs={{0,2},{1,3},{2,0},{3,1},{4,6},{5,7},{6,4},{7,5},{8,10},{9,11},{10,... | collective-permute-start | bytes 1572872 | tf_op jit(solution)/shard_map/ppermute | solution.py:48
  4.9 2.0 %collective-permute-start.3 = (bf16[1,2048]{1,0:T(2,128)(2,1)S(1)}, bf16[1,2048]{1,0:T(2,128)(2,1)S(1)}, u32[]{:S(2)}, u32[]{:S(2)}) collective-permute-start(bf16[1,2048]{1,0:T(2,128)(2,1)S(1)} %reshape.17.gain), channel_id=1, source_target_pairs={{0,2},{1,3},{2,0},{3,1},{4,6},{5,7},{6,4},{7,5},{8,10},{9,11},{10,... | collective-permute-start | bytes 12296 | tf_op jit(solution)/shard_map/ppermute | solution.py:48
  6.9 1.4 %copy-done.11 = bf16[128,8192]{1,0:T(8,128)(2,1)} copy-done((bf16[128,8192]{1,0:T(8,128)(2,1)}, bf16[128,8192]{1,0:T(8,128)(2,1)S(1)}, u32[]{:S(2)}) %copy-start.11) | copy-done | bytes 2097176
  8.3 1.6 %copy-done.2 = bf16[8192,128]{1,0:T(8,128)(2,1)S(1)} copy-done((bf16[8192,128]{1,0:T(8,128)(2,1)S(1)}, bf16[8192,128]{1,0:T(8,128)(2,1)}, u32[]{:S(2)}) %copy-start.2) | copy-done | bytes 2097176
  9.9 1.6 %copy-done.4 = bf16[8192,128]{1,0:T(8,128)(2,1)S(1)} copy-done((bf16[8192,128]{1,0:T(8,128)(2,1)S(1)}, bf16[8192,128]{1,0:T(8,128)(2,1)}, u32[]{:S(2)}) %copy-start.4) | copy-done | bytes 2097176
  11.4 1.6 %copy-done.6 = bf16[8192,128]{1,0:T(8,128)(2,1)S(1)} copy-done((bf16[8192,128]{1,0:T(8,128)(2,1)S(1)}, bf16[8192,128]{1,0:T(8,128)(2,1)}, u32[]{:S(2)}) %copy-start.6) | copy-done | bytes 2097176
  13.0 1.6 %copy-done.10 = bf16[128,8192]{1,0:T(8,128)(2,1)S(1)} copy-done((bf16[128,8192]{1,0:T(8,128)(2,1)S(1)}, bf16[128,8192]{1,0:T(8,128)(2,1)}, u32[]{:S(2)}) %copy-start.10) | copy-done | bytes 2097176
  14.6 1.6 %copy-done.12 = bf16[128,8192]{1,0:T(8,128)(2,1)S(1)} copy-done((bf16[128,8192]{1,0:T(8,128)(2,1)S(1)}, bf16[128,8192]{1,0:T(8,128)(2,1)}, u32[]{:S(2)}) %copy-start.12) | copy-done | bytes 2097176
  18.2 3.6 %prepare.1 = (bf16[384,4096]{1,0:T(8,128)(2,1)S(1)}, bf16[384,4096]{1,0:T(8,128)(2,1)S(1)}, bf16[256,2048]{1,0:T(8,128)(2,1)S(1)}, bf16[256,2048]{1,0:T(8,128)(2...) custom-call(s32[4]{0:T(128)S(1)} %iota_xor_fusion.order, ...), custom_call_target="tpu_custom_call" | custom-call | flops 1000 | bytes 1000 | tf_op jit(solution)/shard_map/prepare/pallas_call | solution.py:30
  21.8 1.6 %copy-done.18 = bf16[384,4096]{1,0:T(8,128)(2,1)} copy-done((bf16[384,4096]{1,0:T(8,128)(2,1)}, bf16[384,4096]{1,0:T(8,128)(2,1)S(1)}, u32[]{:S(2)}) %copy-start.18) | copy-done | bytes 3145752
  23.4 1.9 %begin.1 = (f32[128,1]{1,0:T(8,128)S(1)}, f32[128,256]{1,0:T(8,128)S(1)}) custom-call(bf16[128,2048]{1,0:T(8,128)(2,1)S(1)} %copy-done, bf16[128,2048]{1,0:T(8,128)(2,1)} %collective-permute-done.x1, bf16[128,2048]{1,0:T(8,128)(2,1)S(1)} %copy-done.8, bf16[2048,256]{1,0:T(8,128)(2,1)S(1)} %get-tuple-element.35.here_turned), custom_call_target="tpu_custom_call" | custom-call | flops 1000 | bytes 1000 | tf_op jit(solution)/shard_map/begin/pallas_call | solution.py:30
  25.3 2.7 %collective-permute-done.3 = bf16[1,2048]{1,0:T(2,128)(2,1)S(1)} collective-permute-done((bf16[1,2048]{1,0:T(2,128)(2,1)S(1)}, bf16[1,2048]{1,0:T(2,128)(2,1)S(1)}, u32[]{:S(2)}, u32[]{:S(2)}) %collective-permute-start.3) | collective-permute-done | bytes 4128 | tf_op jit(solution)/shard_map/ppermute | solution.py:48
  28.0 1.6 %add_grad.1 = (f32[128,128]{1,0:T(8,128)S(1)}, f32[128,128]{1,0:T(8,128)S(1)}) custom-call(bf16[128,2048]{1,0:T(8,128)(2,1)} %collective-permute-done.2.c2, bf16[2048,256]{1,0:T(8,128)(2,1)S(1)} %get-tuple-element.42.there_turned, f32[128,256]{1,0:T(8,128)S(1)} %get-tuple-element.43.part), custom_call_target="tpu_custom_call" | custom-call | flops 1000 | bytes 1000 | tf_op jit(solution)/shard_map/add_grad/pallas_call | solution.py:30
  30.3 1.8 %collective-permute-start.8 = (bf16[256,2048]{1,0:T(8,128)(2,1)}, bf16[256,2048]{1,0:T(8,128)(2,1)}, u32[]{:S(2)}, u32[]{:S(2)}) collective-permute-start(bf16[256,2048]{1,0:T(8,128)(2,1)} %get-tuple-element.52), channel_id=1, source_target_pairs={{0,2},{1,3},{2,0},{3,1},{4,6},{5,7},{6,4},{7,5},{8,10},{9,11},{10,... | collective-permute-start | bytes 3145736 | tf_op jit(solution)/shard_map/ppermute | solution.py:48
  33.5 2.7 %project.1 = (bf16[128,384]{1,0:T(8,128)(2,1)S(1)}, f32[128,1]{1,0:T(8,128)S(1)}) custom-call(s32[4]{0:T(128)S(1)} %iota_xor_fusion.order, bf16[128,2048]{1,0:T(8,128)(2,1)S(1)} %copy-done, bf16[128,2048]{1,0:T(8,128)(2,1)} %collective-permute-done.x1, bf16[128,2048]{1,0:T(8,128)(2,1)} %collective-permute-done.1.x2, ...), custom_call_target="tpu_custom_call" | custom-call | flops 1000 | bytes 1000 | tf_op jit(solution)/shard_map/project/pallas_call | solution.py:30
  37.1 6.0 %all-to-all-start = ((bf16[8,16,512]{2,1,0:T(8,128)(2,1)}), bf16[8,16,512]{2,1,0:T(8,128)(2,1)S(1)}, u32[]{:S(2)}, u32[]{:S(2)}) async-start(bf16[8,16,512]{2,1,0:T(8,128)(2,1)} %bitcast.2), calls=%async_computation | async-start | bytes 262144 | tf_op jit(solution)/shard_map/all_to_all | solution.py:406
  43.2 7.4 %all-to-all-done = bf16[8,16,512]{2,1,0:T(8,128)(2,1)S(1)} async-done(((bf16[8,16,512]{2,1,0:T(8,128)(2,1)}), bf16[8,16,512]{2,1,0:T(8,128)(2,1)S(1)}, u32[]{:S(2)}, u32[]{:S(2)}) %all-to-all-start) | async-done | bytes 131104 | tf_op jit(solution)/shard_map/all_to_all | solution.py:406
  51.8 9.9 %all_to_all.23 = bf16[8,16,512]{2,1,0:T(8,128)(2,1)S(1)} all-to-all(bf16[8,16,512]{2,1,0:T(8,128)(2,1)S(1)} %bitcast.7), channel_id=1, replica_groups=mesh['dp'=8,'tensor'=4] {'dp'}, dimensions={0} | all-to-all | bytes 262144 | tf_op jit(solution)/shard_map/all_to_all | solution.py:406
  62.0 1.5 %collective-permute-start.10 = (bf16[128,256]{1,0:T(8,128)(2,1)S(1)}, bf16[128,256]{1,0:T(8,128)(2,1)S(1)}, u32[]{:S(2)}, u32[]{:S(2)}) collective-permute-start(bf16[128,256]{1,0:T(8,128)(2,1)S(1)} %get-tuple-element.54.own), channel_id=1, source_target_pairs={{0,2},{1,3},{2,0},{3,1},{4,6},{5,7},{6,4},{7,5},{8,10},{9,11},{10,... | collective-permute-start | bytes 196616 | tf_op jit(solution)/shard_map/ppermute | solution.py:48
  63.4 2.3 %spread_far.3 = bf16[128,1024]{1,0:T(8,128)(2,1)S(1)} custom-call(bf16[128,384]{1,0:T(8,128)(2,1)S(1)} %get-tuple-element.64.own, bf16[128,384]{1,0:T(8,128)(2,1)S(1)} %collective-permute-done.12.near, bf16[384,4096]{1,0:T(8,128)(2,1)S(1)} %get-tuple-element.59.weights, bf16[384,4096]{1,0:T(8,128)(2,1)} %collective-permute-done.13.near_weights), custom_call_target="tpu_custom_call" | custom-call | flops 1000 | bytes 1000 | tf_op jit(solution)/shard_map/spread_far/pallas_call | solution.py:304
  67.1 2.2 %spread_far.4 = bf16[128,512]{1,0:T(8,128)(2,1)S(1)} custom-call(bf16[128,384]{1,0:T(8,128)(2,1)S(1)} %get-tuple-element.64.own, bf16[128,384]{1,0:T(8,128)(2,1)S(1)} %collective-permute-done.12.near, bf16[384,4096]{1,0:T(8,128)(2,1)S(1)} %get-tuple-element.59.weights, bf16[384,4096]{1,0:T(8,128)(2,1)} %collective-permute-done.13.near_weights), custom_call_target="tpu_custom_call" | custom-call | flops 536870912 | bytes 1000 | tf_op jit(solution)/shard_map/spread_far/pallas_call | solution.py:304
  70.2 2.2 %spread_far.5 = bf16[128,512]{1,0:T(8,128)(2,1)S(1)} custom-call(bf16[128,384]{1,0:T(8,128)(2,1)S(1)} %get-tuple-element.64.own, bf16[128,384]{1,0:T(8,128)(2,1)S(1)} %collective-permute-done.12.near, bf16[384,4096]{1,0:T(8,128)(2,1)S(1)} %get-tuple-element.59.weights, bf16[384,4096]{1,0:T(8,128)(2,1)} %collective-permute-done.13.near_weights), custom_call_target="tpu_custom_call" | custom-call | flops 536870912 | bytes 1000 | tf_op jit(solution)/shard_map/spread_far/pallas_call | solution.py:304
  75.1 2.5 %finish_out.1 = bf16[128,2048]{1,0:T(8,128)(2,1)} custom-call(bf16[128,2048]{1,0:T(8,128)(2,1)S(1)} %copy-done.1, bf16[128,256]{1,0:T(8,128)(2,1)S(1)} %get-tuple-element.54.own, bf16[128,256]{1,0:T(8,128)(2,1)S(1)} %collective-permute-done.9.near, bf16[128,256]{1,0:T(8,128)(2,1)S(1)} %collective-permute-done.10.far, ...), custom_call_target="tpu_custom_call" | custom-call | flops 1000 | bytes 1000 | tf_op jit(solution)/shard_map/finish_out/pallas_call | solution.py:30
  77.6 2.7 %spread_own.1.grad_own = f32[128,2048]{1,0:T(8,128)S(1)} custom-call(bf16[128,384]{1,0:T(8,128)(2,1)S(1)} %get-tuple-element.64.own, bf16[128,384]{1,0:T(8,128)(2,1)S(1)} %collective-permute-done.12.near, bf16[384,4096]{1,0:T(8,128)(2,1)S(1)} %get-tuple-element.59.weights, bf16[384,4096]{1,0:T(8,128)(2,1)} %collective-permute-done.13.near_weights), custom_call_target="tpu_custom_call" | custom-call | flops 1000 | bytes 1000 | tf_op jit(solution)/shard_map/spread_own/pallas_call | solution.py:304
  (69 shorter events, 14.7 us)
Async XLA Ops:
  0.6 6.3 %collective-permute-start.4 = (bf16[128,8192]{1,0:T(8,128)(2,1)}, bf16[128,8192]{1,0:T(8,128)(2,1)S(1)}, u32[]{:S(2)}, u32[]{:S(2)}) collective-permute-start(bf16[128,8192]{1,0:T(8,128)(2,1)} %w_output.1), channel_id=1, source_target_pairs={{0,1},{1,0},{2,3},{3,2},{4,5},{5,4},{6,7},{7,6},{8,9},{9,8},{10,11... | collective-permute-start | bytes 6291464 | tf_op jit(solution)/shard_map/ppermute | solution.py:48
  1.1 22.3 %collective-permute-start = (bf16[128,2048]{1,0:T(8,128)(2,1)}, bf16[128,2048]{1,0:T(8,128)(2,1)}, u32[]{:S(2)}, u32[]{:S(2)}) collective-permute-start(bf16[128,2048]{1,0:T(8,128)(2,1)} %inputs.3), channel_id=1, source_target_pairs={{0,1},{1,0},{2,3},{3,2},{4,5},{5,4},{6,7},{7,6},{8,9},{9,8},{10,11... | collective-permute-start | bytes 1572872 | tf_op jit(solution)/shard_map/ppermute | solution.py:48
  1.2 26.8 %collective-permute-start.1 = (bf16[128,2048]{1,0:T(8,128)(2,1)}, bf16[128,2048]{1,0:T(8,128)(2,1)}, u32[]{:S(2)}, u32[]{:S(2)}) collective-permute-start(bf16[128,2048]{1,0:T(8,128)(2,1)} %inputs.3), channel_id=1, source_target_pairs={{0,2},{1,3},{2,0},{3,1},{4,6},{5,7},{6,4},{7,5},{8,10},{9,11},{10,... | collective-permute-start | bytes 1572872 | tf_op jit(solution)/shard_map/ppermute | solution.py:48
  4.2 23.8 %collective-permute-start.2 = (bf16[128,2048]{1,0:T(8,128)(2,1)}, bf16[128,2048]{1,0:T(8,128)(2,1)}, u32[]{:S(2)}, u32[]{:S(2)}) collective-permute-start(bf16[128,2048]{1,0:T(8,128)(2,1)} %cotangent.1), channel_id=1, source_target_pairs={{0,2},{1,3},{2,0},{3,1},{4,6},{5,7},{6,4},{7,5},{8,10},{9,11},{10,... | collective-permute-start | bytes 1572872 | tf_op jit(solution)/shard_map/ppermute | solution.py:48
  4.9 23.1 %collective-permute-start.3 = (bf16[1,2048]{1,0:T(2,128)(2,1)S(1)}, bf16[1,2048]{1,0:T(2,128)(2,1)S(1)}, u32[]{:S(2)}, u32[]{:S(2)}) collective-permute-start(bf16[1,2048]{1,0:T(2,128)(2,1)S(1)} %reshape.17.gain), channel_id=1, source_target_pairs={{0,2},{1,3},{2,0},{3,1},{4,6},{5,7},{6,4},{7,5},{8,10},{9,11},{10,... | collective-permute-start | bytes 12296 | tf_op jit(solution)/shard_map/ppermute | solution.py:48
  18.2 5.2 %copy-start = (bf16[128,2048]{1,0:T(8,128)(2,1)S(1)}, bf16[128,2048]{1,0:T(8,128)(2,1)}, u32[]{:S(2)}) copy-start(bf16[128,2048]{1,0:T(8,128)(2,1)} %inputs.3) | copy-start | bytes 1572868
  18.2 5.2 %copy-start.8 = (bf16[128,2048]{1,0:T(8,128)(2,1)S(1)}, bf16[128,2048]{1,0:T(8,128)(2,1)}, u32[]{:S(2)}) copy-start(bf16[128,2048]{1,0:T(8,128)(2,1)} %cotangent.1) | copy-start | bytes 1572868
  23.4 6.2 %copy-start.13 = (bf16[256,2048]{1,0:T(8,128)(2,1)}, bf16[256,2048]{1,0:T(8,128)(2,1)S(1)}, u32[]{:S(2)}) copy-start(bf16[256,2048]{1,0:T(8,128)(2,1)S(1)} %get-tuple-element.55.here) | copy-start | bytes 3145732
  29.6 6.6 %collective-permute-start.7 = (f32[128,128]{1,0:T(8,128)S(1)}, f32[128,128]{1,0:T(8,128)S(1)}, u32[]{:S(2)}, u32[]{:S(2)}) collective-permute-start(f32[128,128]{1,0:T(8,128)S(1)} %get-tuple-element.44), channel_id=1, source_target_pairs={{0,1},{1,0},{2,3},{3,2},{4,5},{5,4},{6,7},{7,6},{8,9},{9,8},{10,11... | collective-permute-start | bytes 196616 | tf_op jit(solution)/shard_map/ppermute | solution.py:48
  29.7 3.7 %collective-permute-start.6 = (bf16[2,2048]{1,0:T(2,128)(2,1)S(1)}, bf16[2,2048]{1,0:T(2,128)(2,1)S(1)}, u32[]{:S(2)}, u32[]{:S(2)}) collective-permute-start(bf16[2,2048]{1,0:T(2,128)(2,1)S(1)} %pad_maximum_fusion.gain_own), channel_id=1, source_target_pairs={{0,1},{1,0},{2,3},{3,2},{4,5},{5,4},{6,7},{7,6},{8,9},{9,8},{10,11... | collective-permute-start | bytes 24584 | tf_op jit(solution)/shard_map/ppermute | solution.py:48
  30.3 3.2 %collective-permute-start.5 = (bf16[128,2048]{1,0:T(8,128)(2,1)}, bf16[128,2048]{1,0:T(8,128)(2,1)S(1)}, u32[]{:S(2)}, u32[]{:S(2)}) collective-permute-start(bf16[128,2048]{1,0:T(8,128)(2,1)} %collective-permute-done.1.x2), channel_id=1, source_target_pairs={{0,1},{1,0},{2,3},{3,2},{4,5},{5,4},{6,7},{7,6},{8,9},{9,8},{10,11... | collective-permute-start | bytes 1572872 | tf_op jit(solution)/shard_map/ppermute | solution.py:48
  30.3 3.1 %copy-start.7 = (bf16[8192,128]{1,0:T(8,128)(2,1)S(1)}, bf16[8192,128]{1,0:T(8,128)(2,1)}, u32[]{:S(2)}) copy-start(bf16[8192,128]{1,0:T(8,128)(2,1)} %w_value.3) | copy-start | bytes 6291460
  30.3 31.3 %collective-permute-start.8 = (bf16[256,2048]{1,0:T(8,128)(2,1)}, bf16[256,2048]{1,0:T(8,128)(2,1)}, u32[]{:S(2)}, u32[]{:S(2)}) collective-permute-start(bf16[256,2048]{1,0:T(8,128)(2,1)} %get-tuple-element.52), channel_id=1, source_target_pairs={{0,2},{1,3},{2,0},{3,1},{4,6},{5,7},{6,4},{7,5},{8,10},{9,11},{10,... | collective-permute-start | bytes 3145736 | tf_op jit(solution)/shard_map/ppermute | solution.py:48
  37.1 13.6 %all-to-all-start = ((bf16[8,16,512]{2,1,0:T(8,128)(2,1)}), bf16[8,16,512]{2,1,0:T(8,128)(2,1)S(1)}, u32[]{:S(2)}, u32[]{:S(2)}) async-start(bf16[8,16,512]{2,1,0:T(8,128)(2,1)} %bitcast.2), calls=%async_computation | async-start | bytes 262144 | tf_op jit(solution)/shard_map/all_to_all | solution.py:406
  43.1 20.4 %collective-permute-start.13 = (bf16[384,4096]{1,0:T(8,128)(2,1)}, bf16[384,4096]{1,0:T(8,128)(2,1)}, u32[]{:S(2)}, u32[]{:S(2)}) collective-permute-start(bf16[384,4096]{1,0:T(8,128)(2,1)} %copy-done.18), channel_id=1, source_target_pairs={{0,1},{1,0},{2,3},{3,2},{4,5},{5,4},{6,7},{7,6},{8,9},{9,8},{10,11... | collective-permute-start | bytes 9437192 | tf_op jit(solution)/shard_map/ppermute | solution.py:48
  61.9 1.6 %collective-permute-start.12 = (bf16[128,384]{1,0:T(8,128)(2,1)S(1)}, bf16[128,384]{1,0:T(8,128)(2,1)S(1)}, u32[]{:S(2)}, u32[]{:S(2)}) collective-permute-start(bf16[128,384]{1,0:T(8,128)(2,1)S(1)} %get-tuple-element.64.own), channel_id=1, source_target_pairs={{0,1},{1,0},{2,3},{3,2},{4,5},{5,4},{6,7},{7,6},{8,9},{9,8},{10,11... | collective-permute-start | bytes 294920 | tf_op jit(solution)/shard_map/ppermute | solution.py:48
  62.0 5.1 %collective-permute-start.10 = (bf16[128,256]{1,0:T(8,128)(2,1)S(1)}, bf16[128,256]{1,0:T(8,128)(2,1)S(1)}, u32[]{:S(2)}, u32[]{:S(2)}) collective-permute-start(bf16[128,256]{1,0:T(8,128)(2,1)S(1)} %get-tuple-element.54.own), channel_id=1, source_target_pairs={{0,2},{1,3},{2,0},{3,1},{4,6},{5,7},{6,4},{7,5},{8,10},{9,11},{10,... | collective-permute-start | bytes 196616 | tf_op jit(solution)/shard_map/ppermute | solution.py:48
  65.8 14.5 %collective-permute-start.14 = (bf16[128,1024]{1,0:T(8,128)(2,1)S(1)}, bf16[128,1024]{1,0:T(8,128)(2,1)S(1)}, u32[]{:S(2)}, u32[]{:S(2)}) collective-permute-start(bf16[128,1024]{1,0:T(8,128)(2,1)S(1)} %spread_far.3), channel_id=1, source_target_pairs={{0,2},{1,3},{2,0},{3,1},{4,6},{5,7},{6,4},{7,5},{8,10},{9,11},{10,... | collective-permute-start | bytes 786440 | tf_op jit(solution)/shard_map/ppermute | solution.py:48
  69.3 5.8 %copy-start.1 = (bf16[128,2048]{1,0:T(8,128)(2,1)S(1)}, bf16[128,2048]{1,0:T(8,128)(2,1)}, u32[]{:S(2)}) copy-start(bf16[128,2048]{1,0:T(8,128)(2,1)} %inputs.3) | copy-start | bytes 1572868
  69.3 5.8 %copy-start.14 = (bf16[256,2048]{1,0:T(8,128)(2,1)S(1)}, bf16[256,2048]{1,0:T(8,128)(2,1)}, u32[]{:S(2)}) copy-start(bf16[256,2048]{1,0:T(8,128)(2,1)} %copy-done.13) | copy-start | bytes 3145732
  69.3 11.0 %collective-permute-start.15 = (bf16[128,512]{1,0:T(8,128)(2,1)S(1)}, bf16[128,512]{1,0:T(8,128)(2,1)S(1)}, u32[]{:S(2)}, u32[]{:S(2)}) collective-permute-start(bf16[128,512]{1,0:T(8,128)(2,1)S(1)} %spread_far.4), channel_id=1, source_target_pairs={{0,2},{1,3},{2,0},{3,1},{4,6},{5,7},{6,4},{7,5},{8,10},{9,11},{10,... | collective-permute-start | bytes 393224 | tf_op jit(solution)/shard_map/ppermute | solution.py:48
  72.4 9.2 %collective-permute-start.16 = (bf16[128,512]{1,0:T(8,128)(2,1)S(1)}, bf16[128,512]{1,0:T(8,128)(2,1)S(1)}, u32[]{:S(2)}, u32[]{:S(2)}) collective-permute-start(bf16[128,512]{1,0:T(8,128)(2,1)S(1)} %spread_far.5), channel_id=1, source_target_pairs={{0,2},{1,3},{2,0},{3,1},{4,6},{5,7},{6,4},{7,5},{8,10},{9,11},{10,... | collective-permute-start | bytes 393224 | tf_op jit(solution)/shard_map/ppermute | solution.py:48
  73.7 1.3 %collective-permute-start.9 = (bf16[128,256]{1,0:T(8,128)(2,1)S(1)}, bf16[128,256]{1,0:T(8,128)(2,1)S(1)}, u32[]{:S(2)}, u32[]{:S(2)}) collective-permute-start(bf16[128,256]{1,0:T(8,128)(2,1)S(1)} %get-tuple-element.54.own), channel_id=1, source_target_pairs={{0,1},{1,0},{2,3},{3,2},{4,5},{5,4},{6,7},{7,6},{8,9},{9,8},{10,11... | collective-permute-start | bytes 196616 | tf_op jit(solution)/shard_map/ppermute | solution.py:48
  73.7 1.4 %collective-permute-start.11 = (bf16[128,256]{1,0:T(8,128)(2,1)S(1)}, bf16[128,256]{1,0:T(8,128)(2,1)S(1)}, u32[]{:S(2)}, u32[]{:S(2)}) collective-permute-start(bf16[128,256]{1,0:T(8,128)(2,1)S(1)} %collective-permute-done.10.far), channel_id=1, source_target_pairs={{0,1},{1,0},{2,3},{3,2},{4,5},{5,4},{6,7},{7,6},{8,9},{9,8},{10,11... | collective-permute-start | bytes 196616 | tf_op jit(solution)/shard_map/ppermute | solution.py:48
  (13 other events, 21.8 us)

commit v13 on v10

--- a/solution.py
+++ b/solution.py
@@ -16,13 +16,15 @@
 VMEM = pl.BlockSpec(memory_space=pltpu.VMEM)
 SMEM = pl.BlockSpec(memory_space=pltpu.SMEM)
 TILE = 512
+SQUARES_FLOPS = 10000000000
+HOME_FLOPS = 24000000000
 
 
 def dot(left, right, dims=(((1,), (0,)), ((), ()))):
     return lax.dot_general(left, right, dims, preferred_element_type=jnp.float32)
 
 
-def call(kernel, name, out_shape, operands, scratch=(), first=SMEM, rest=VMEM):
+def call(kernel, name, out_shape, operands, scratch=(), first=SMEM, rest=VMEM, flops=1000):
     single = not isinstance(out_shape, (list, tuple))
     shapes = [out_shape] if single else list(out_shape)
     results = pl.pallas_call(
@@ -32,7 +34,7 @@
         out_specs=[VMEM] * len(shapes),
         scratch_shapes=list(scratch),
         compiler_params=pltpu.CompilerParams(vmem_limit_bytes=VMEM_LIMIT),
-        cost_estimate=pl.CostEstimate(flops=1000, bytes_accessed=1000, transcendentals=0),
+        cost_estimate=pl.CostEstimate(flops=flops, bytes_accessed=1000, transcendentals=0),
         name=name,
     )(*operands)
     return results[0] if single else results
@@ -163,7 +165,10 @@
 
 def add_squares(x2, squares):
     out = shape(jnp.float32, *squares.shape)
-    return call(add_squares_kernel, "add_squares", out, (x2, squares), first=VMEM)
+    operands = (x2, squares)
+    return call(
+        add_squares_kernel, "add_squares", out, operands, first=VMEM, flops=SQUARES_FLOPS
+    )
 
 
 def project_kernel(
@@ -282,7 +287,8 @@
 def bring_home(moved, send, home):
     rows = home.shape[0]
     shapes = [shape(jnp.bfloat16, rows, 3 * HEAD_DIM), shape(jnp.bfloat16, rows, 2 * HEAD_DIM)]
-    return call(bring_home_kernel, "bring_home", shapes, (moved, send, home), first=VMEM)
+    operands = (moved, send, home)
+    return call(bring_home_kernel, "bring_home", shapes, operands, first=VMEM, flops=HOME_FLOPS)
 
 
 def spread_kernel(first):
@@ -449,7 +455,7 @@
     gain_near = swap(gain_own, 1, tensor)
     own_part, near_part = add_grad(c2, there_turned, part)
     got_part = swap(near_part, 1, tensor)
-    squares = add_squares(x2, squares)
+    squares = add_squares(x2, after(squares, near_part))
     home, inverse_rms, bucket = project(
         order,
         (inputs, x1, x2, x3),
@@ -461,9 +467,10 @@
         send,
     )
     near_turned = swap(after(near_turned, home), 1, tensor)
-    there = swap(after(there, home), 2, tensor)
+    there = swap(after(there, near_part), 2, tensor)
     back = attend(move(bucket), receive, segments)
-    own, own_extras = bring_home(move(back), send, home)
+    moved, there = lax.optimization_barrier((move(back), there))
+    own, own_extras = bring_home(moved, send, home)
 
     near = swap(own, 1, tensor)
     far_extras = swap(own_extras, 2, tensor)

time: 76.7 us -> 77.5 us (1.010)
  waiting for transfers between devices: 18.3 us -> 15.7 us
  starting transfers between devices: 11.8 us -> 14.1 us
  local copies, waits for them, and re-layouts: 9.04 us -> 9.92 us
    ppermute x17, waiting for transfers between devices: 18.3 us -> 15.7 us  [swap(): return lax.ppermute(array, 'tensor', [(i, i ^ mask) for i in range(count)])]
    ppermute x17, starting transfers between devices: 11.8 us -> 14.1 us  [swap(): return lax.ppermute(array, 'tensor', [(i, i ^ mask) for i in range(count)])]
    unnamed x24, local copies, waits for them, and re-layouts: 8.35 us -> 9.23 us
  transfers between devices with their start and end apart: 17 -> 17, of which waited for: 7 -> 6; matrix products, arithmetic and copies ran while one was open for 1% -> 1% of each run, Pallas kernels for 14% -> 15%
where the time goes in v13:
time: 77.5 us; the launch traced here: 77.1 us
  blocking collectives  22.9 us (30%)
  waiting for transfers between devices  15.7 us (20%)
  starting transfers between devices  14.1 us (18%)
  Pallas kernels  13.6 us (18%)
  local copies, waits for them, and re-layouts  9.92 us (13%)
  between operations  0.79 us (1%)
    all_to_all x2, blocking collectives, move(): return lax.all_to_all(bucket, 'dp', split_axis=0, concat_axis=0, tiled=True)  22.9 us
    ppermute x17, waiting for transfers between devices, swap(): return lax.ppermute(array, 'tensor', [(i, i ^ mask) for i in range(count)])  15.7 us
    ppermute x17, starting transfers between devices, swap(): return lax.ppermute(array, 'tensor', [(i, i ^ mask) for i in range(count)])  14.1 us
    pallas_call x8, Pallas kernels, call(): pl.pallas_call(kernel, out_shape=shapes, in_specs=[first] + [rest] * (len...  9.78 us
    unnamed x24, local copies, waits for them, and re-layouts  9.23 us
    pallas_call x4, Pallas kernels, spread(): pl.pallas_call(spread_kernel(first), out_shape=shape(dtype, own.shape[0],...  1.77 us
  transfers between devices with their start and end apart: 17, of which 6 were waited for; matrix products, arithmetic and copies ran while one was open for 1% of the time, Pallas kernels for 15%

profile of v13, /device:TPU:0, one launch (start us, length us, event | category | flops | bytes accessed | tf_op | source)
XLA Modules:
  0.0 77.1 jit_solution(13038706726485630136)
XLA Ops:
  1.2 2.9 %collective-permute-start.1 = (bf16[128,2048]{1,0:T(8,128)(2,1)}, bf16[128,2048]{1,0:T(8,128)(2,1)S(1)}, u32[]{:S(2)}, u32[]{:S(2)}) collective-permute-start(bf16[128,2048]{1,0:T(8,128)(2,1)} %inputs.3), channel_id=1, source_target_pairs={{0,2},{1,3},{2,0},{3,1},{4,6},{5,7},{6,4},{7,5},{8,10},{9,11},{10,... | collective-permute-start | bytes 1572872 | tf_op jit(solution)/shard_map/ppermute | solution.py:48
  4.9 2.0 %collective-permute-start.3 = (bf16[1,2048]{1,0:T(2,128)(2,1)S(1)}, bf16[1,2048]{1,0:T(2,128)(2,1)S(1)}, u32[]{:S(2)}, u32[]{:S(2)}) collective-permute-start(bf16[1,2048]{1,0:T(2,128)(2,1)S(1)} %reshape.17.gain), channel_id=1, source_target_pairs={{0,2},{1,3},{2,0},{3,1},{4,6},{5,7},{6,4},{7,5},{8,10},{9,11},{10,... | collective-permute-start | bytes 12296 | tf_op jit(solution)/shard_map/ppermute | solution.py:48
  6.9 1.6 %copy-done = bf16[8192,128]{1,0:T(8,128)(2,1)S(1)} copy-done((bf16[8192,128]{1,0:T(8,128)(2,1)S(1)}, bf16[8192,128]{1,0:T(8,128)(2,1)}, u32[]{:S(2)}) %copy-start) | copy-done | bytes 2097176
  8.5 1.6 %copy-done.2 = bf16[8192,128]{1,0:T(8,128)(2,1)S(1)} copy-done((bf16[8192,128]{1,0:T(8,128)(2,1)S(1)}, bf16[8192,128]{1,0:T(8,128)(2,1)}, u32[]{:S(2)}) %copy-start.2) | copy-done | bytes 2097176
  10.1 1.6 %copy-done.4 = bf16[8192,128]{1,0:T(8,128)(2,1)S(1)} copy-done((bf16[8192,128]{1,0:T(8,128)(2,1)S(1)}, bf16[8192,128]{1,0:T(8,128)(2,1)}, u32[]{:S(2)}) %copy-start.4) | copy-done | bytes 2097176
  11.7 1.6 %copy-done.8 = bf16[128,8192]{1,0:T(8,128)(2,1)S(1)} copy-done((bf16[128,8192]{1,0:T(8,128)(2,1)S(1)}, bf16[128,8192]{1,0:T(8,128)(2,1)}, u32[]{:S(2)}) %copy-start.8) | copy-done | bytes 2097176
  15.2 2.8 %prepare.1 = (bf16[384,4096]{1,0:T(8,128)(2,1)S(1)}, bf16[384,4096]{1,0:T(8,128)(2,1)S(1)}, bf16[256,2048]{1,0:T(8,128)(2,1)S(1)}, bf16[256,2048]{1,0:T(8,128)(2...) custom-call(s32[4]{0:T(128)S(1)} %iota_xor_fusion.order, ...), custom_call_target="tpu_custom_call" | custom-call | flops 1000 | bytes 1000 | tf_op jit(solution)/shard_map/prepare/pallas_call | solution.py:30
  18.5 9.5 %collective-permute-done.3 = bf16[1,2048]{1,0:T(2,128)(2,1)S(1)} collective-permute-done((bf16[1,2048]{1,0:T(2,128)(2,1)S(1)}, bf16[1,2048]{1,0:T(2,128)(2,1)S(1)}, u32[]{:S(2)}, u32[]{:S(2)}) %collective-permute-start.3) | collective-permute-done | bytes 4128 | tf_op jit(solution)/shard_map/ppermute | solution.py:48
  28.0 1.6 %add_grad.1 = (f32[128,128]{1,0:T(8,128)S(1)}, f32[128,128]{1,0:T(8,128)S(1)}) custom-call(bf16[128,2048]{1,0:T(8,128)(2,1)} %collective-permute-done.2.c2, bf16[2048,256]{1,0:T(8,128)(2,1)S(1)} %get-tuple-element.43.there_turned, f32[128,256]{1,0:T(8,128)S(1)} %get-tuple-element.44.part), custom_call_target="tpu_custom_call" | custom-call | flops 1000 | bytes 1000 | tf_op jit(solution)/shard_map/add_grad/pallas_call | solution.py:30
  30.3 1.8 %collective-permute-start.8 = (bf16[256,2048]{1,0:T(8,128)(2,1)S(1)}, bf16[256,2048]{1,0:T(8,128)(2,1)S(1)}, u32[]{:S(2)}, u32[]{:S(2)}) collective-permute-start(bf16[256,2048]{1,0:T(8,128)(2,1)S(1)} %get-tuple-element.53), channel_id=1, source_target_pairs={{0,2},{1,3},{2,0},{3,1},{4,6},{5,7},{6,4},{7,5},{8,10},{9,11},{10,... | collective-permute-start | bytes 3145736 | tf_op jit(solution)/shard_map/ppermute | solution.py:48
  33.2 2.2 %project.1 = (bf16[128,384]{1,0:T(8,128)(2,1)S(1)}, f32[128,1]{1,0:T(8,128)S(1)}, bf16[128,512]{1,0:T(8,128)(2,1)S(1)}) custom-call(s32[4]{0:T(128)S(1)} %iota_xor_fusion.order, bf16[128,2048]{1,0:T(8,128)(2,1)S(1)} %copy-done.6, bf16[128,2048]{1,0:T(8,128)(2,1)S(1)} %collective-permute-done.x1, bf16[128,2048]{1,0:T(8,128)(2,1)S(1)} %collective-permute-done.1.x2, ...), custom_call_target="tpu_custom_call" | custom-call | flops 1000 | bytes 1000 | tf_op jit(solution)/shard_map/project/pallas_call | solution.py:30
  35.9 13.2 %all_to_all.23 = bf16[8,16,512]{2,1,0:T(8,128)(2,1)S(1)} all-to-all(bf16[8,16,512]{2,1,0:T(8,128)(2,1)S(1)} %bitcast.8), channel_id=1, replica_groups=mesh['dp'=8,'tensor'=4] {'dp'}, dimensions={0} | all-to-all | bytes 262144 | tf_op jit(solution)/shard_map/all_to_all | solution.py:408
  49.1 1.1 %attend.1 = bf16[128,512]{1,0:T(8,128)(2,1)S(1)} custom-call(bf16[128,512]{1,0:T(8,128)(2,1)S(1)} %bitcast.6, s32[1,128]{1,0:T(1,128)S(1)} %get-tuple-element.50.receive, s32[1,128]{1,0:T(1,128)S(1)} %get-tuple-element.51.segments), custom_call_target="tpu_custom_call" | custom-call | flops 1000 | bytes 1000 | tf_op jit(solution)/shard_map/attend/pallas_call | solution.py:30
  50.1 9.7 %all_to_all.24 = bf16[8,16,512]{2,1,0:T(8,128)(2,1)S(1)} all-to-all(bf16[8,16,512]{2,1,0:T(8,128)(2,1)S(1)} %bitcast.7), channel_id=1, replica_groups=mesh['dp'=8,'tensor'=4] {'dp'}, dimensions={0} | all-to-all | bytes 262144 | tf_op jit(solution)/shard_map/all_to_all | solution.py:408
  60.2 1.6 %collective-permute-start.10 = (bf16[128,256]{1,0:T(8,128)(2,1)S(1)}, bf16[128,256]{1,0:T(8,128)(2,1)S(1)}, u32[]{:S(2)}, u32[]{:S(2)}) collective-permute-start(bf16[128,256]{1,0:T(8,128)(2,1)S(1)} %get-tuple-element.56.own), channel_id=1, source_target_pairs={{0,2},{1,3},{2,0},{3,1},{4,6},{5,7},{6,4},{7,5},{8,10},{9,11},{10,... | collective-permute-start | bytes 196616 | tf_op jit(solution)/shard_map/ppermute | solution.py:48
  62.3 1.3 %collective-permute-start.14 = (bf16[128,1024]{1,0:T(8,128)(2,1)S(1)}, bf16[128,1024]{1,0:T(8,128)(2,1)S(1)}, u32[]{:S(2)}, u32[]{:S(2)}) collective-permute-start(bf16[128,1024]{1,0:T(8,128)(2,1)S(1)} %spread_far.3), channel_id=1, source_target_pairs={{0,2},{1,3},{2,0},{3,1},{4,6},{5,7},{6,4},{7,5},{8,10},{9,11},{10,... | collective-permute-start | bytes 786440 | tf_op jit(solution)/shard_map/ppermute | solution.py:48
  63.6 1.2 %collective-permute-done.10.far = bf16[128,256]{1,0:T(8,128)(2,1)S(1)} collective-permute-done((bf16[128,256]{1,0:T(8,128)(2,1)S(1)}, bf16[128,256]{1,0:T(8,128)(2,1)S(1)}, u32[]{:S(2)}, u32[]{:S(2)}) %collective-permute-start.10) | collective-permute-done | bytes 65568 | tf_op jit(solution)/shard_map/ppermute | solution.py:48
  65.1 1.6 %collective-permute-start.15 = (bf16[128,512]{1,0:T(8,128)(2,1)S(1)}, bf16[128,512]{1,0:T(8,128)(2,1)S(1)}, u32[]{:S(2)}, u32[]{:S(2)}) collective-permute-start(bf16[128,512]{1,0:T(8,128)(2,1)S(1)} %spread_far.4), channel_id=1, source_target_pairs={{0,2},{1,3},{2,0},{3,1},{4,6},{5,7},{6,4},{7,5},{8,10},{9,11},{10,... | collective-permute-start | bytes 393224 | tf_op jit(solution)/shard_map/ppermute | solution.py:48
  68.0 0.7 collective-permute-done.9.near
  68.9 1.3 %finish_out.1 = bf16[128,2048]{1,0:T(8,128)(2,1)} custom-call(bf16[128,2048]{1,0:T(8,128)(2,1)S(1)} %copy-done.6, bf16[128,256]{1,0:T(8,128)(2,1)S(1)} %get-tuple-element.56.own, bf16[128,256]{1,0:T(8,128)(2,1)S(1)} %collective-permute-done.9.near, bf16[128,256]{1,0:T(8,128)(2,1)S(1)} %collective-permute-done.10.far, ...), custom_call_target="tpu_custom_call" | custom-call | flops 1000 | bytes 1000 | tf_op jit(solution)/shard_map/finish_out/pallas_call | solution.py:30
  70.9 3.4 %collective-permute-done.15.pieces_1_ = bf16[128,512]{1,0:T(8,128)(2,1)S(1)} collective-permute-done((bf16[128,512]{1,0:T(8,128)(2,1)S(1)}, bf16[128,512]{1,0:T(8,128)(2,1)S(1)}, u32[]{:S(2)}, u32[]{:S(2)}) %collective-permute-start.15) | collective-permute-done | bytes 131104 | tf_op jit(solution)/shard_map/ppermute | solution.py:48
  74.3 1.3 %finish_most.1 = (bf16[128,2048]{1,0:T(8,128)(2,1)}, f32[128,512]{1,0:T(8,128)S(1)}) custom-call(bf16[128,2048]{1,0:T(8,128)(2,1)S(1)} %copy-done.6, bf16[128,2048]{1,0:T(8,128)(2,1)S(1)} %copy-done.7, bf16[1,2048]{1,0:T(2,128)(2,1)S(1)} %reshape.17.gain, f32[128,1]{1,0:T(8,128)S(1)} %get-tuple-element.59.inverse, ...), custom_call_target="tpu_custom_call" | custom-call | flops 1000 | bytes 1000 | tf_op jit(solution)/shard_map/finish_most/pallas_call | solution.py:386
  75.6 0.8 collective-permute-done.16.rest
  76.3 0.8 finish_rest.1
  (53 shorter events, 9.4 us)
Async XLA Ops:
  0.6 6.3 %collective-permute-start.4 = (bf16[128,8192]{1,0:T(8,128)(2,1)}, bf16[128,8192]{1,0:T(8,128)(2,1)S(1)}, u32[]{:S(2)}, u32[]{:S(2)}) collective-permute-start(bf16[128,8192]{1,0:T(8,128)(2,1)} %w_output.1), channel_id=1, source_target_pairs={{0,1},{1,0},{2,3},{3,2},{4,5},{5,4},{6,7},{7,6},{8,9},{9,8},{10,11... | collective-permute-start | bytes 6291464 | tf_op jit(solution)/shard_map/ppermute | solution.py:48
  1.1 16.9 %collective-permute-start = (bf16[128,2048]{1,0:T(8,128)(2,1)}, bf16[128,2048]{1,0:T(8,128)(2,1)S(1)}, u32[]{:S(2)}, u32[]{:S(2)}) collective-permute-start(bf16[128,2048]{1,0:T(8,128)(2,1)} %inputs.3), channel_id=1, source_target_pairs={{0,1},{1,0},{2,3},{3,2},{4,5},{5,4},{6,7},{7,6},{8,9},{9,8},{10,11... | collective-permute-start | bytes 1572872 | tf_op jit(solution)/shard_map/ppermute | solution.py:48
  1.2 26.8 %collective-permute-start.1 = (bf16[128,2048]{1,0:T(8,128)(2,1)}, bf16[128,2048]{1,0:T(8,128)(2,1)S(1)}, u32[]{:S(2)}, u32[]{:S(2)}) collective-permute-start(bf16[128,2048]{1,0:T(8,128)(2,1)} %inputs.3), channel_id=1, source_target_pairs={{0,2},{1,3},{2,0},{3,1},{4,6},{5,7},{6,4},{7,5},{8,10},{9,11},{10,... | collective-permute-start | bytes 1572872 | tf_op jit(solution)/shard_map/ppermute | solution.py:48
  4.2 23.8 %collective-permute-start.2 = (bf16[128,2048]{1,0:T(8,128)(2,1)}, bf16[128,2048]{1,0:T(8,128)(2,1)}, u32[]{:S(2)}, u32[]{:S(2)}) collective-permute-start(bf16[128,2048]{1,0:T(8,128)(2,1)} %cotangent.1), channel_id=1, source_target_pairs={{0,2},{1,3},{2,0},{3,1},{4,6},{5,7},{6,4},{7,5},{8,10},{9,11},{10,... | collective-permute-start | bytes 1572872 | tf_op jit(solution)/shard_map/ppermute | solution.py:48
  4.9 23.1 %collective-permute-start.3 = (bf16[1,2048]{1,0:T(2,128)(2,1)S(1)}, bf16[1,2048]{1,0:T(2,128)(2,1)S(1)}, u32[]{:S(2)}, u32[]{:S(2)}) collective-permute-start(bf16[1,2048]{1,0:T(2,128)(2,1)S(1)} %reshape.17.gain), channel_id=1, source_target_pairs={{0,2},{1,3},{2,0},{3,1},{4,6},{5,7},{6,4},{7,5},{8,10},{9,11},{10,... | collective-permute-start | bytes 12296 | tf_op jit(solution)/shard_map/ppermute | solution.py:48
  6.9 1.6 %copy-start = (bf16[8192,128]{1,0:T(8,128)(2,1)S(1)}, bf16[8192,128]{1,0:T(8,128)(2,1)}, u32[]{:S(2)}) copy-start(bf16[8192,128]{1,0:T(8,128)(2,1)} %w_query.3) | copy-start | bytes 6291460
  8.5 1.6 %copy-start.2 = (bf16[8192,128]{1,0:T(8,128)(2,1)S(1)}, bf16[8192,128]{1,0:T(8,128)(2,1)}, u32[]{:S(2)}) copy-start(bf16[8192,128]{1,0:T(8,128)(2,1)} %w_key.3) | copy-start | bytes 6291460
  15.2 2.8 %copy-start.6 = (bf16[128,2048]{1,0:T(8,128)(2,1)S(1)}, bf16[128,2048]{1,0:T(8,128)(2,1)}, u32[]{:S(2)}) copy-start(bf16[128,2048]{1,0:T(8,128)(2,1)} %inputs.3) | copy-start | bytes 1572868
  15.2 2.8 %copy-start.7 = (bf16[128,2048]{1,0:T(8,128)(2,1)S(1)}, bf16[128,2048]{1,0:T(8,128)(2,1)}, u32[]{:S(2)}) copy-start(bf16[128,2048]{1,0:T(8,128)(2,1)} %cotangent.1) | copy-start | bytes 1572868
  29.6 2.7 %collective-permute-start.7 = (f32[128,128]{1,0:T(8,128)S(1)}, f32[128,128]{1,0:T(8,128)S(1)}, u32[]{:S(2)}, u32[]{:S(2)}) collective-permute-start(f32[128,128]{1,0:T(8,128)S(1)} %get-tuple-element.45), channel_id=1, source_target_pairs={{0,1},{1,0},{2,3},{3,2},{4,5},{5,4},{6,7},{7,6},{8,9},{9,8},{10,11... | collective-permute-start | bytes 196616 | tf_op jit(solution)/shard_map/ppermute | solution.py:48
  29.7 2.6 %collective-permute-start.6 = (bf16[2,2048]{1,0:T(2,128)(2,1)S(1)}, bf16[2,2048]{1,0:T(2,128)(2,1)S(1)}, u32[]{:S(2)}, u32[]{:S(2)}) collective-permute-start(bf16[2,2048]{1,0:T(2,128)(2,1)S(1)} %pad_maximum_fusion.gain_own), channel_id=1, source_target_pairs={{0,1},{1,0},{2,3},{3,2},{4,5},{5,4},{6,7},{7,6},{8,9},{9,8},{10,11... | collective-permute-start | bytes 24584 | tf_op jit(solution)/shard_map/ppermute | solution.py:48
  30.2 2.0 %collective-permute-start.5 = (bf16[128,2048]{1,0:T(8,128)(2,1)S(1)}, bf16[128,2048]{1,0:T(8,128)(2,1)S(1)}, u32[]{:S(2)}, u32[]{:S(2)}) collective-permute-start(bf16[128,2048]{1,0:T(8,128)(2,1)S(1)} %collective-permute-done.1.x2), channel_id=1, source_target_pairs={{0,1},{1,0},{2,3},{3,2},{4,5},{5,4},{6,7},{7,6},{8,9},{9,8},{10,11... | collective-permute-start | bytes 1572872 | tf_op jit(solution)/shard_map/ppermute | solution.py:48
  30.3 2.0 %copy-start.1 = (bf16[8192,128]{1,0:T(8,128)(2,1)S(1)}, bf16[8192,128]{1,0:T(8,128)(2,1)}, u32[]{:S(2)}) copy-start(bf16[8192,128]{1,0:T(8,128)(2,1)} %w_query.3) | copy-start | bytes 6291460
  30.3 2.2 %copy-start.3 = (bf16[8192,128]{1,0:T(8,128)(2,1)S(1)}, bf16[8192,128]{1,0:T(8,128)(2,1)}, u32[]{:S(2)}) copy-start(bf16[8192,128]{1,0:T(8,128)(2,1)} %w_key.3) | copy-start | bytes 6291460
  30.3 2.9 %copy-start.5 = (bf16[8192,128]{1,0:T(8,128)(2,1)S(1)}, bf16[8192,128]{1,0:T(8,128)(2,1)}, u32[]{:S(2)}) copy-start(bf16[8192,128]{1,0:T(8,128)(2,1)} %w_value.3) | copy-start | bytes 6291460
  30.3 29.6 %collective-permute-start.8 = (bf16[256,2048]{1,0:T(8,128)(2,1)S(1)}, bf16[256,2048]{1,0:T(8,128)(2,1)S(1)}, u32[]{:S(2)}, u32[]{:S(2)}) collective-permute-start(bf16[256,2048]{1,0:T(8,128)(2,1)S(1)} %get-tuple-element.53), channel_id=1, source_target_pairs={{0,2},{1,3},{2,0},{3,1},{4,6},{5,7},{6,4},{7,5},{8,10},{9,11},{10,... | collective-permute-start | bytes 3145736 | tf_op jit(solution)/shard_map/ppermute | solution.py:48
  35.4 26.4 %collective-permute-start.13 = (bf16[384,4096]{1,0:T(8,128)(2,1)S(1)}, bf16[384,4096]{1,0:T(8,128)(2,1)S(1)}, u32[]{:S(2)}, u32[]{:S(2)}) collective-permute-start(bf16[384,4096]{1,0:T(8,128)(2,1)S(1)} %get-tuple-element.63), channel_id=1, source_target_pairs={{0,1},{1,0},{2,3},{3,2},{4,5},{5,4},{6,7},{7,6},{8,9},{9,8},{10,11... | collective-permute-start | bytes 9437192 | tf_op jit(solution)/shard_map/ppermute | solution.py:48
  60.1 1.7 %collective-permute-start.12 = (bf16[128,384]{1,0:T(8,128)(2,1)S(1)}, bf16[128,384]{1,0:T(8,128)(2,1)S(1)}, u32[]{:S(2)}, u32[]{:S(2)}) collective-permute-start(bf16[128,384]{1,0:T(8,128)(2,1)S(1)} %get-tuple-element.66.own), channel_id=1, source_target_pairs={{0,1},{1,0},{2,3},{3,2},{4,5},{5,4},{6,7},{7,6},{8,9},{9,8},{10,11... | collective-permute-start | bytes 294920 | tf_op jit(solution)/shard_map/ppermute | solution.py:48
  60.2 4.5 %collective-permute-start.10 = (bf16[128,256]{1,0:T(8,128)(2,1)S(1)}, bf16[128,256]{1,0:T(8,128)(2,1)S(1)}, u32[]{:S(2)}, u32[]{:S(2)}) collective-permute-start(bf16[128,256]{1,0:T(8,128)(2,1)S(1)} %get-tuple-element.56.own), channel_id=1, source_target_pairs={{0,2},{1,3},{2,0},{3,1},{4,6},{5,7},{6,4},{7,5},{8,10},{9,11},{10,... | collective-permute-start | bytes 196616 | tf_op jit(solution)/shard_map/ppermute | solution.py:48
  62.3 12.0 %collective-permute-start.14 = (bf16[128,1024]{1,0:T(8,128)(2,1)S(1)}, bf16[128,1024]{1,0:T(8,128)(2,1)S(1)}, u32[]{:S(2)}, u32[]{:S(2)}) collective-permute-start(bf16[128,1024]{1,0:T(8,128)(2,1)S(1)} %spread_far.3), channel_id=1, source_target_pairs={{0,2},{1,3},{2,0},{3,1},{4,6},{5,7},{6,4},{7,5},{8,10},{9,11},{10,... | collective-permute-start | bytes 786440 | tf_op jit(solution)/shard_map/ppermute | solution.py:48
  65.1 9.2 %collective-permute-start.15 = (bf16[128,512]{1,0:T(8,128)(2,1)S(1)}, bf16[128,512]{1,0:T(8,128)(2,1)S(1)}, u32[]{:S(2)}, u32[]{:S(2)}) collective-permute-start(bf16[128,512]{1,0:T(8,128)(2,1)S(1)} %spread_far.4), channel_id=1, source_target_pairs={{0,2},{1,3},{2,0},{3,1},{4,6},{5,7},{6,4},{7,5},{8,10},{9,11},{10,... | collective-permute-start | bytes 393224 | tf_op jit(solution)/shard_map/ppermute | solution.py:48
  67.0 9.4 %collective-permute-start.16 = (bf16[128,512]{1,0:T(8,128)(2,1)S(1)}, bf16[128,512]{1,0:T(8,128)(2,1)S(1)}, u32[]{:S(2)}, u32[]{:S(2)}) collective-permute-start(bf16[128,512]{1,0:T(8,128)(2,1)S(1)} %spread_far.5), channel_id=1, source_target_pairs={{0,2},{1,3},{2,0},{3,1},{4,6},{5,7},{6,4},{7,5},{8,10},{9,11},{10,... | collective-permute-start | bytes 393224 | tf_op jit(solution)/shard_map/ppermute | solution.py:48
  67.5 1.3 %collective-permute-start.9 = (bf16[128,256]{1,0:T(8,128)(2,1)S(1)}, bf16[128,256]{1,0:T(8,128)(2,1)S(1)}, u32[]{:S(2)}, u32[]{:S(2)}) collective-permute-start(bf16[128,256]{1,0:T(8,128)(2,1)S(1)} %get-tuple-element.56.own), channel_id=1, source_target_pairs={{0,1},{1,0},{2,3},{3,2},{4,5},{5,4},{6,7},{7,6},{8,9},{9,8},{10,11... | collective-permute-start | bytes 196616 | tf_op jit(solution)/shard_map/ppermute | solution.py:48
  67.5 1.4 %collective-permute-start.11 = (bf16[128,256]{1,0:T(8,128)(2,1)S(1)}, bf16[128,256]{1,0:T(8,128)(2,1)S(1)}, u32[]{:S(2)}, u32[]{:S(2)}) collective-permute-start(bf16[128,256]{1,0:T(8,128)(2,1)S(1)} %collective-permute-done.10.far), channel_id=1, source_target_pairs={{0,1},{1,0},{2,3},{3,2},{4,5},{5,4},{6,7},{7,6},{8,9},{9,8},{10,11... | collective-permute-start | bytes 196616 | tf_op jit(solution)/shard_map/ppermute | solution.py:48
  (5 other events, 5.1 us)

commit v14 on v10

--- a/solution.py
+++ b/solution.py
@@ -12,7 +12,7 @@
 SCALING = 1.0 / math.sqrt(HEAD_DIM)
 CONTRACT_LAST = (((1,), (1,)), ((), ()))
 CONTRACT_FIRST = (((0,), (0,)), ((), ()))
-VMEM_LIMIT = 6 * 1024 * 1024
+VMEM_LIMIT = 3 * 1024 * 1024
 VMEM = pl.BlockSpec(memory_space=pltpu.VMEM)
 SMEM = pl.BlockSpec(memory_space=pltpu.SMEM)
 TILE = 512
@@ -69,20 +69,20 @@
     near_turned,
     here,
     there,
-    here_turned,
     there_turned,
     send_out,
     receive_out,
     segments_out,
 ):
     heads, width = w_output.shape[0], here.shape[1]
-    for slot, out, turned in ((0, here, here_turned), (2, there, there_turned)):
+    for slot, out, turned in ((0, here, None), (2, there, there_turned)):
         columns = pl.ds(block_start(order, slot, width), width)
         for part, weight in enumerate((w_output, near_output)):
             rows = slice(part * heads, (part + 1) * heads)
             block = weight[:, columns]
             out[rows, :] = block
-            turned[:, rows] = block.T
+            if turned is not None:
+                turned[:, rows] = block.T
     for source, target in ((send, send_out), (receive, receive_out), (segments, segments_out)):
         target[...] = source[...]
     for out, slots in ((own_turned, (0, 2)), (near_turned, (1, 3))):
@@ -104,7 +104,7 @@
         [
             *[shape(low, 3 * heads, 2 * width)] * 2,
             *[shape(low, 2 * heads, width)] * 2,
-            *[shape(low, width, 2 * heads)] * 2,
+            shape(low, width, 2 * heads),
             shape(jnp.int32, *send.shape),
             shape(jnp.int32, *receive.shape),
             shape(jnp.int32, *segments.shape),
@@ -118,43 +118,27 @@
     return jnp.sum(wide * wide, axis=-1, keepdims=True)
 
 
-def begin_kernel(x0, x1, c0, here_turned, squares, part):
+def begin_kernel(x0, x1, c0, here, squares, part):
     squares[...] = sum_squares(x0) + sum_squares(x1)
-    part[...] = dot(c0[...], here_turned[...])
-
-
-def begin(x0, x1, c0, here_turned):
-    rows, columns = x0.shape[0], here_turned.shape[1]
+    part[...] = dot(c0[...], here[...], CONTRACT_LAST)
+
+
+def begin(x0, x1, c0, here):
+    rows, columns = x0.shape[0], here.shape[0]
     shapes = [shape(jnp.float32, rows, 1), shape(jnp.float32, rows, columns)]
-    return call(begin_kernel, "begin", shapes, (x0, x1, c0, here_turned), first=VMEM)
-
-
-def add_grad_kernel(c2, there_turned, part, own_part, near_part, held, sems):
-    copies = []
-    for index, start in enumerate(range(0, held.shape[1], TILE)):
-        tile = pl.ds(start, TILE)
-        copies.append(pltpu.make_async_copy(c2.at[:, tile], held.at[:, tile], sems.at[index]))
-        copies[-1].start()
-    total = part[...]
-    for index, copy in enumerate(copies):
-        tile = slice(index * TILE, (index + 1) * TILE)
-        copy.wait()
-        total = total + dot(held[:, tile], there_turned[tile, :])
+    return call(begin_kernel, "begin", shapes, (x0, x1, c0, here), first=VMEM)
+
+
+def add_grad_kernel(c2, there_turned, part, own_part, near_part):
+    total = part[...] + dot(c2[...], there_turned[...])
     heads = own_part.shape[1]
     own_part[...] = total[:, :heads]
     near_part[...] = total[:, heads:]
 
 
 def add_grad(c2, there_turned, part):
-    rows, width = c2.shape
-    return call(
-        add_grad_kernel,
-        "add_grad",
-        [shape(jnp.float32, rows, part.shape[1] // 2)] * 2,
-        (c2, there_turned, part),
-        scratch=[pltpu.VMEM((rows, width), c2.dtype), pltpu.SemaphoreType.DMA((width // TILE,))],
-        first=pl.BlockSpec(memory_space=pl.ANY),
-    )
+    shapes = [shape(jnp.float32, part.shape[0], part.shape[1] // 2)] * 2
+    return call(add_grad_kernel, "add_grad", shapes, (c2, there_turned, part), first=VMEM)
 
 
 def add_squares_kernel(x2, squares_in, squares):
@@ -430,7 +414,7 @@
     x1 = swap(inputs, 1, tensor)
     near_output = swap(w_output, 1, tensor)
     weights = (w_query, w_key, w_value)
-    own_turned, near_turned, here, there, here_turned, there_turned, *indices = prepare(
+    own_turned, near_turned, here, there, there_turned, *indices = prepare(
         order,
         *weights,
         w_output,
@@ -441,7 +425,7 @@
         width,
     )
     send, receive, segments = indices
-    squares, part = begin(inputs, x1, cotangent, here_turned)
+    squares, part = begin(inputs, x1, cotangent, here)
 
     x2, c2, gain2, squares, part = lax.optimization_barrier((x2, c2, gain2, squares, part))
     x3 = swap(x2, 1, tensor)

time: 76.7 us -> 76.5 us (level)
  transfers between devices with their start and end apart: 17 -> 17, of which waited for: 7 -> 7; matrix products, arithmetic and copies ran while one was open for 1% -> 1% of each run, Pallas kernels for 14% -> 13%
where the time goes in v14:
time: 76.5 us; the launch traced here: 76.1 us
  blocking collectives  22.7 us (30%)
  waiting for transfers between devices  18.4 us (24%)
  Pallas kernels  13.2 us (17%)
  starting transfers between devices  11.9 us (16%)
  local copies, waits for them, and re-layouts  9.04 us (12%)
  between operations  0.81 us (1%)
    all_to_all x2, blocking collectives, move(): return lax.all_to_all(bucket, 'dp', split_axis=0, concat_axis=0, tiled=True)  22.7 us
    ppermute x17, waiting for transfers between devices, swap(): return lax.ppermute(array, 'tensor', [(i, i ^ mask) for i in range(count)])  18.4 us
    ppermute x17, starting transfers between devices, swap(): return lax.ppermute(array, 'tensor', [(i, i ^ mask) for i in range(count)])  11.9 us
    pallas_call x8, Pallas kernels, call(): pl.pallas_call(kernel, out_shape=shapes, in_specs=[first] + [rest] * (len...  9.45 us
    unnamed x24, local copies, waits for them, and re-layouts  8.35 us
    pallas_call x4, Pallas kernels, spread(): pl.pallas_call(spread_kernel(first), out_shape=shape(dtype, own.shape[0],...  1.77 us
  transfers between devices with their start and end apart: 17, of which 7 were waited for; matrix products, arithmetic and copies ran while one was open for 1% of the time, Pallas kernels for 13%

profile of v14, /device:TPU:0, one launch (start us, length us, event | category | flops | bytes accessed | tf_op | source)
XLA Modules:
  0.0 76.1 jit_solution(15477200176516911450)
XLA Ops:
  1.2 2.9 %collective-permute-start.1 = (bf16[128,2048]{1,0:T(8,128)(2,1)}, bf16[128,2048]{1,0:T(8,128)(2,1)S(1)}, u32[]{:S(2)}, u32[]{:S(2)}) collective-permute-start(bf16[128,2048]{1,0:T(8,128)(2,1)} %inputs.3), channel_id=1, source_target_pairs={{0,2},{1,3},{2,0},{3,1},{4,6},{5,7},{6,4},{7,5},{8,10},{9,11},{10,... | collective-permute-start | bytes 1572872 | tf_op jit(solution)/shard_map/ppermute | solution.py:46
  4.9 2.0 %collective-permute-start.3 = (bf16[1,2048]{1,0:T(2,128)(2,1)S(1)}, bf16[1,2048]{1,0:T(2,128)(2,1)S(1)}, u32[]{:S(2)}, u32[]{:S(2)}) collective-permute-start(bf16[1,2048]{1,0:T(2,128)(2,1)S(1)} %reshape.17.gain), channel_id=1, source_target_pairs={{0,2},{1,3},{2,0},{3,1},{4,6},{5,7},{6,4},{7,5},{8,10},{9,11},{10,... | collective-permute-start | bytes 12296 | tf_op jit(solution)/shard_map/ppermute | solution.py:46
  6.9 1.6 %copy-done = bf16[8192,128]{1,0:T(8,128)(2,1)S(1)} copy-done((bf16[8192,128]{1,0:T(8,128)(2,1)S(1)}, bf16[8192,128]{1,0:T(8,128)(2,1)}, u32[]{:S(2)}) %copy-start) | copy-done | bytes 2097176
  8.5 1.6 %copy-done.2 = bf16[8192,128]{1,0:T(8,128)(2,1)S(1)} copy-done((bf16[8192,128]{1,0:T(8,128)(2,1)S(1)}, bf16[8192,128]{1,0:T(8,128)(2,1)}, u32[]{:S(2)}) %copy-start.2) | copy-done | bytes 2097176
  10.1 1.6 %copy-done.4 = bf16[8192,128]{1,0:T(8,128)(2,1)S(1)} copy-done((bf16[8192,128]{1,0:T(8,128)(2,1)S(1)}, bf16[8192,128]{1,0:T(8,128)(2,1)}, u32[]{:S(2)}) %copy-start.4) | copy-done | bytes 2097176
  11.7 1.6 %copy-done.8 = bf16[128,8192]{1,0:T(8,128)(2,1)S(1)} copy-done((bf16[128,8192]{1,0:T(8,128)(2,1)S(1)}, bf16[128,8192]{1,0:T(8,128)(2,1)}, u32[]{:S(2)}) %copy-start.8) | copy-done | bytes 2097176
  15.2 2.5 %prepare.1 = (bf16[384,4096]{1,0:T(8,128)(2,1)S(1)}, bf16[384,4096]{1,0:T(8,128)(2,1)S(1)}, bf16[256,2048]{1,0:T(8,128)(2,1)S(1)}, bf16[256,2048]{1,0:T(8,128)(2...) custom-call(s32[4]{0:T(128)S(1)} %iota_xor_fusion.order, ...), custom_call_target="tpu_custom_call" | custom-call | flops 1000 | bytes 1000 | tf_op jit(solution)/shard_map/prepare/pallas_call | solution.py:28
  18.4 9.6 %collective-permute-done.3 = bf16[1,2048]{1,0:T(2,128)(2,1)S(1)} collective-permute-done((bf16[1,2048]{1,0:T(2,128)(2,1)S(1)}, bf16[1,2048]{1,0:T(2,128)(2,1)S(1)}, u32[]{:S(2)}, u32[]{:S(2)}) %collective-permute-start.3) | collective-permute-done | bytes 4128 | tf_op jit(solution)/shard_map/ppermute | solution.py:46
  28.0 1.4 %add_grad.1 = (f32[128,128]{1,0:T(8,128)S(1)}, f32[128,128]{1,0:T(8,128)S(1)}) custom-call(bf16[128,2048]{1,0:T(8,128)(2,1)} %collective-permute-done.2.c2, bf16[2048,256]{1,0:T(8,128)(2,1)S(1)} %get-tuple-element.39.there_turned, f32[128,256]{1,0:T(8,128)S(1)} %get-tuple-element.40.part), custom_call_target="tpu_custom_call" | custom-call | flops 1000 | bytes 1000 | tf_op jit(solution)/shard_map/add_grad/pallas_call | solution.py:28
  30.2 1.0 %collective-permute-done.6.gain_near = bf16[2,2048]{1,0:T(2,128)(2,1)S(1)} collective-permute-done((bf16[2,2048]{1,0:T(2,128)(2,1)S(1)}, bf16[2,2048]{1,0:T(2,128)(2,1)S(1)}, u32[]{:S(2)}, u32[]{:S(2)}) %collective-permute-start.6) | collective-permute-done | bytes 8224 | tf_op jit(solution)/shard_map/ppermute | solution.py:46
  31.2 2.2 %project.1 = (bf16[128,384]{1,0:T(8,128)(2,1)S(1)}, f32[128,1]{1,0:T(8,128)S(1)}, bf16[128,512]{1,0:T(8,128)(2,1)S(1)}) custom-call(s32[4]{0:T(128)S(1)} %iota_xor_fusion.order, bf16[128,2048]{1,0:T(8,128)(2,1)S(1)} %copy-done.6, bf16[128,2048]{1,0:T(8,128)(2,1)S(1)} %collective-permute-done.x1, bf16[128,2048]{1,0:T(8,128)(2,1)S(1)} %collective-permute-done.1.x2, ...), custom_call_target="tpu_custom_call" | custom-call | flops 1000 | bytes 1000 | tf_op jit(solution)/shard_map/project/pallas_call | solution.py:28
  33.7 1.7 %collective-permute-start.11 = (bf16[256,2048]{1,0:T(8,128)(2,1)S(1)}, bf16[256,2048]{1,0:T(8,128)(2,1)S(1)}, u32[]{:S(2)}, u32[]{:S(2)}) collective-permute-start(bf16[256,2048]{1,0:T(8,128)(2,1)S(1)} %get-tuple-element.50), channel_id=1, source_target_pairs={{0,2},{1,3},{2,0},{3,1},{4,6},{5,7},{6,4},{7,5},{8,10},{9,11},{10,... | collective-permute-start | bytes 3145736 | tf_op jit(solution)/shard_map/ppermute | solution.py:46
  35.4 12.9 %all_to_all.22 = bf16[8,16,512]{2,1,0:T(8,128)(2,1)S(1)} all-to-all(bf16[8,16,512]{2,1,0:T(8,128)(2,1)S(1)} %bitcast.9), channel_id=1, replica_groups=mesh['dp'=8,'tensor'=4] {'dp'}, dimensions={0} | all-to-all | bytes 262144 | tf_op jit(solution)/shard_map/all_to_all | solution.py:386
  48.4 1.1 %attend.1 = bf16[128,512]{1,0:T(8,128)(2,1)S(1)} custom-call(bf16[128,512]{1,0:T(8,128)(2,1)S(1)} %bitcast.7, s32[1,128]{1,0:T(1,128)S(1)} %get-tuple-element.45.receive, s32[1,128]{1,0:T(1,128)S(1)} %get-tuple-element.46.segments), custom_call_target="tpu_custom_call" | custom-call | flops 1000 | bytes 1000 | tf_op jit(solution)/shard_map/attend/pallas_call | solution.py:28
  49.5 9.7 %all_to_all.23 = bf16[8,16,512]{2,1,0:T(8,128)(2,1)S(1)} all-to-all(bf16[8,16,512]{2,1,0:T(8,128)(2,1)S(1)} %bitcast.8), channel_id=1, replica_groups=mesh['dp'=8,'tensor'=4] {'dp'}, dimensions={0} | all-to-all | bytes 262144 | tf_op jit(solution)/shard_map/all_to_all | solution.py:386
  61.3 0.9 %collective-permute-start.14 = (bf16[128,1024]{1,0:T(8,128)(2,1)S(1)}, bf16[128,1024]{1,0:T(8,128)(2,1)S(1)}, u32[]{:S(2)}, u32[]{:S(2)}) collective-permute-start(bf16[128,1024]{1,0:T(8,128)(2,1)S(1)} %spread_far.3), channel_id=1, source_target_pairs={{0,2},{1,3},{2,0},{3,1},{4,6},{5,7},{6,4},{7,5},{8,10},{9,11},{10,... | collective-permute-start | bytes 786440 | tf_op jit(solution)/shard_map/ppermute | solution.py:46
  62.1 1.9 %collective-permute-done.9.far = bf16[128,256]{1,0:T(8,128)(2,1)S(1)} collective-permute-done((bf16[128,256]{1,0:T(8,128)(2,1)S(1)}, bf16[128,256]{1,0:T(8,128)(2,1)S(1)}, u32[]{:S(2)}, u32[]{:S(2)}) %collective-permute-start.9) | collective-permute-done | bytes 65568 | tf_op jit(solution)/shard_map/ppermute | solution.py:46
  65.2 1.6 %collective-permute-start.16 = (bf16[128,512]{1,0:T(8,128)(2,1)S(1)}, bf16[128,512]{1,0:T(8,128)(2,1)S(1)}, u32[]{:S(2)}, u32[]{:S(2)}) collective-permute-start(bf16[128,512]{1,0:T(8,128)(2,1)S(1)} %spread_far.5), channel_id=1, source_target_pairs={{0,2},{1,3},{2,0},{3,1},{4,6},{5,7},{6,4},{7,5},{8,10},{9,11},{10,... | collective-permute-start | bytes 393224 | tf_op jit(solution)/shard_map/ppermute | solution.py:46
  66.8 1.3 %collective-permute-done.10.last = bf16[128,256]{1,0:T(8,128)(2,1)S(1)} collective-permute-done((bf16[128,256]{1,0:T(8,128)(2,1)S(1)}, bf16[128,256]{1,0:T(8,128)(2,1)S(1)}, u32[]{:S(2)}, u32[]{:S(2)}) %collective-permute-start.10) | collective-permute-done | bytes 65568 | tf_op jit(solution)/shard_map/ppermute | solution.py:46
  68.1 1.3 %finish_out.1 = bf16[128,2048]{1,0:T(8,128)(2,1)} custom-call(bf16[128,2048]{1,0:T(8,128)(2,1)S(1)} %copy-done.6, bf16[128,256]{1,0:T(8,128)(2,1)S(1)} %get-tuple-element.48.own, bf16[128,256]{1,0:T(8,128)(2,1)S(1)} %collective-permute-done.8.near, bf16[128,256]{1,0:T(8,128)(2,1)S(1)} %collective-permute-done.9.far, ...), custom_call_target="tpu_custom_call" | custom-call | flops 1000 | bytes 1000 | tf_op jit(solution)/shard_map/finish_out/pallas_call | solution.py:28
  70.1 3.2 %collective-permute-done.15.pieces_1_ = bf16[128,512]{1,0:T(8,128)(2,1)S(1)} collective-permute-done((bf16[128,512]{1,0:T(8,128)(2,1)S(1)}, bf16[128,512]{1,0:T(8,128)(2,1)S(1)}, u32[]{:S(2)}, u32[]{:S(2)}) %collective-permute-start.15) | collective-permute-done | bytes 131104 | tf_op jit(solution)/shard_map/ppermute | solution.py:46
  73.3 1.3 %finish_most.1 = (bf16[128,2048]{1,0:T(8,128)(2,1)}, f32[128,512]{1,0:T(8,128)S(1)}) custom-call(bf16[128,2048]{1,0:T(8,128)(2,1)S(1)} %copy-done.6, bf16[128,2048]{1,0:T(8,128)(2,1)S(1)} %copy-done.7, bf16[1,2048]{1,0:T(2,128)(2,1)S(1)} %reshape.17.gain, f32[128,1]{1,0:T(8,128)S(1)} %get-tuple-element.51.inverse, ...), custom_call_target="tpu_custom_call" | custom-call | flops 1000 | bytes 1000 | tf_op jit(solution)/shard_map/finish_most/pallas_call | solution.py:364
  74.6 0.7 collective-permute-done.16.rest
  75.3 0.8 finish_rest.1
  (53 shorter events, 9.0 us)
Async XLA Ops:
  0.6 6.3 %collective-permute-start.4 = (bf16[128,8192]{1,0:T(8,128)(2,1)}, bf16[128,8192]{1,0:T(8,128)(2,1)S(1)}, u32[]{:S(2)}, u32[]{:S(2)}) collective-permute-start(bf16[128,8192]{1,0:T(8,128)(2,1)} %w_output.1), channel_id=1, source_target_pairs={{0,1},{1,0},{2,3},{3,2},{4,5},{5,4},{6,7},{7,6},{8,9},{9,8},{10,11... | collective-permute-start | bytes 6291464 | tf_op jit(solution)/shard_map/ppermute | solution.py:46
  1.1 16.6 %collective-permute-start = (bf16[128,2048]{1,0:T(8,128)(2,1)}, bf16[128,2048]{1,0:T(8,128)(2,1)S(1)}, u32[]{:S(2)}, u32[]{:S(2)}) collective-permute-start(bf16[128,2048]{1,0:T(8,128)(2,1)} %inputs.3), channel_id=1, source_target_pairs={{0,1},{1,0},{2,3},{3,2},{4,5},{5,4},{6,7},{7,6},{8,9},{9,8},{10,11... | collective-permute-start | bytes 1572872 | tf_op jit(solution)/shard_map/ppermute | solution.py:46
  1.2 26.8 %collective-permute-start.1 = (bf16[128,2048]{1,0:T(8,128)(2,1)}, bf16[128,2048]{1,0:T(8,128)(2,1)S(1)}, u32[]{:S(2)}, u32[]{:S(2)}) collective-permute-start(bf16[128,2048]{1,0:T(8,128)(2,1)} %inputs.3), channel_id=1, source_target_pairs={{0,2},{1,3},{2,0},{3,1},{4,6},{5,7},{6,4},{7,5},{8,10},{9,11},{10,... | collective-permute-start | bytes 1572872 | tf_op jit(solution)/shard_map/ppermute | solution.py:46
  4.2 23.8 %collective-permute-start.2 = (bf16[128,2048]{1,0:T(8,128)(2,1)}, bf16[128,2048]{1,0:T(8,128)(2,1)}, u32[]{:S(2)}, u32[]{:S(2)}) collective-permute-start(bf16[128,2048]{1,0:T(8,128)(2,1)} %cotangent.1), channel_id=1, source_target_pairs={{0,2},{1,3},{2,0},{3,1},{4,6},{5,7},{6,4},{7,5},{8,10},{9,11},{10,... | collective-permute-start | bytes 1572872 | tf_op jit(solution)/shard_map/ppermute | solution.py:46
  4.9 23.1 %collective-permute-start.3 = (bf16[1,2048]{1,0:T(2,128)(2,1)S(1)}, bf16[1,2048]{1,0:T(2,128)(2,1)S(1)}, u32[]{:S(2)}, u32[]{:S(2)}) collective-permute-start(bf16[1,2048]{1,0:T(2,128)(2,1)S(1)} %reshape.17.gain), channel_id=1, source_target_pairs={{0,2},{1,3},{2,0},{3,1},{4,6},{5,7},{6,4},{7,5},{8,10},{9,11},{10,... | collective-permute-start | bytes 12296 | tf_op jit(solution)/shard_map/ppermute | solution.py:46
  6.9 1.6 %copy-start = (bf16[8192,128]{1,0:T(8,128)(2,1)S(1)}, bf16[8192,128]{1,0:T(8,128)(2,1)}, u32[]{:S(2)}) copy-start(bf16[8192,128]{1,0:T(8,128)(2,1)} %w_query.3) | copy-start | bytes 6291460
  8.5 1.6 %copy-start.2 = (bf16[8192,128]{1,0:T(8,128)(2,1)S(1)}, bf16[8192,128]{1,0:T(8,128)(2,1)}, u32[]{:S(2)}) copy-start(bf16[8192,128]{1,0:T(8,128)(2,1)} %w_key.3) | copy-start | bytes 6291460
  15.2 2.5 %copy-start.6 = (bf16[128,2048]{1,0:T(8,128)(2,1)S(1)}, bf16[128,2048]{1,0:T(8,128)(2,1)}, u32[]{:S(2)}) copy-start(bf16[128,2048]{1,0:T(8,128)(2,1)} %inputs.3) | copy-start | bytes 1572868
  15.2 2.5 %copy-start.7 = (bf16[128,2048]{1,0:T(8,128)(2,1)S(1)}, bf16[128,2048]{1,0:T(8,128)(2,1)}, u32[]{:S(2)}) copy-start(bf16[128,2048]{1,0:T(8,128)(2,1)} %cotangent.1) | copy-start | bytes 1572868
  15.2 16.0 %copy-start.5 = (bf16[8192,128]{1,0:T(8,128)(2,1)S(1)}, bf16[8192,128]{1,0:T(8,128)(2,1)}, u32[]{:S(2)}) copy-start(bf16[8192,128]{1,0:T(8,128)(2,1)} %w_value.3) | copy-start | bytes 6291460
  17.8 13.4 %copy-start.1 = (bf16[8192,128]{1,0:T(8,128)(2,1)S(1)}, bf16[8192,128]{1,0:T(8,128)(2,1)}, u32[]{:S(2)}) copy-start(bf16[8192,128]{1,0:T(8,128)(2,1)} %w_query.3) | copy-start | bytes 6291460
  17.8 13.4 %copy-start.3 = (bf16[8192,128]{1,0:T(8,128)(2,1)S(1)}, bf16[8192,128]{1,0:T(8,128)(2,1)}, u32[]{:S(2)}) copy-start(bf16[8192,128]{1,0:T(8,128)(2,1)} %w_key.3) | copy-start | bytes 6291460
  28.0 3.2 %collective-permute-start.5 = (bf16[128,2048]{1,0:T(8,128)(2,1)S(1)}, bf16[128,2048]{1,0:T(8,128)(2,1)S(1)}, u32[]{:S(2)}, u32[]{:S(2)}) collective-permute-start(bf16[128,2048]{1,0:T(8,128)(2,1)S(1)} %collective-permute-done.1.x2), channel_id=1, source_target_pairs={{0,1},{1,0},{2,3},{3,2},{4,5},{5,4},{6,7},{7,6},{8,9},{9,8},{10,11... | collective-permute-start | bytes 1572872 | tf_op jit(solution)/shard_map/ppermute | solution.py:46
  29.4 1.8 %collective-permute-start.7 = (f32[128,128]{1,0:T(8,128)S(1)}, f32[128,128]{1,0:T(8,128)S(1)}, u32[]{:S(2)}, u32[]{:S(2)}) collective-permute-start(f32[128,128]{1,0:T(8,128)S(1)} %get-tuple-element.42), channel_id=1, source_target_pairs={{0,1},{1,0},{2,3},{3,2},{4,5},{5,4},{6,7},{7,6},{8,9},{9,8},{10,11... | collective-permute-start | bytes 196616 | tf_op jit(solution)/shard_map/ppermute | solution.py:46
  29.9 1.2 %collective-permute-start.6 = (bf16[2,2048]{1,0:T(2,128)(2,1)S(1)}, bf16[2,2048]{1,0:T(2,128)(2,1)S(1)}, u32[]{:S(2)}, u32[]{:S(2)}) collective-permute-start(bf16[2,2048]{1,0:T(2,128)(2,1)S(1)} %pad_maximum_fusion.gain_own), channel_id=1, source_target_pairs={{0,1},{1,0},{2,3},{3,2},{4,5},{5,4},{6,7},{7,6},{8,9},{9,8},{10,11... | collective-permute-start | bytes 24584 | tf_op jit(solution)/shard_map/ppermute | solution.py:46
  33.5 27.4 %collective-permute-start.13 = (bf16[384,4096]{1,0:T(8,128)(2,1)S(1)}, bf16[384,4096]{1,0:T(8,128)(2,1)S(1)}, u32[]{:S(2)}, u32[]{:S(2)}) collective-permute-start(bf16[384,4096]{1,0:T(8,128)(2,1)S(1)} %get-tuple-element.55), channel_id=1, source_target_pairs={{0,1},{1,0},{2,3},{3,2},{4,5},{5,4},{6,7},{7,6},{8,9},{9,8},{10,11... | collective-permute-start | bytes 9437192 | tf_op jit(solution)/shard_map/ppermute | solution.py:46
  33.7 34.4 %collective-permute-start.11 = (bf16[256,2048]{1,0:T(8,128)(2,1)S(1)}, bf16[256,2048]{1,0:T(8,128)(2,1)S(1)}, u32[]{:S(2)}, u32[]{:S(2)}) collective-permute-start(bf16[256,2048]{1,0:T(8,128)(2,1)S(1)} %get-tuple-element.50), channel_id=1, source_target_pairs={{0,2},{1,3},{2,0},{3,1},{4,6},{5,7},{6,4},{7,5},{8,10},{9,11},{10,... | collective-permute-start | bytes 3145736 | tf_op jit(solution)/shard_map/ppermute | solution.py:46
  59.4 1.4 %collective-permute-start.12 = (bf16[128,384]{1,0:T(8,128)(2,1)S(1)}, bf16[128,384]{1,0:T(8,128)(2,1)S(1)}, u32[]{:S(2)}, u32[]{:S(2)}) collective-permute-start(bf16[128,384]{1,0:T(8,128)(2,1)S(1)} %get-tuple-element.58.own), channel_id=1, source_target_pairs={{0,1},{1,0},{2,3},{3,2},{4,5},{5,4},{6,7},{7,6},{8,9},{9,8},{10,11... | collective-permute-start | bytes 294920 | tf_op jit(solution)/shard_map/ppermute | solution.py:46
  59.5 4.5 %collective-permute-start.9 = (bf16[128,256]{1,0:T(8,128)(2,1)S(1)}, bf16[128,256]{1,0:T(8,128)(2,1)S(1)}, u32[]{:S(2)}, u32[]{:S(2)}) collective-permute-start(bf16[128,256]{1,0:T(8,128)(2,1)S(1)} %get-tuple-element.48.own), channel_id=1, source_target_pairs={{0,2},{1,3},{2,0},{3,1},{4,6},{5,7},{6,4},{7,5},{8,10},{9,11},{10,... | collective-permute-start | bytes 196616 | tf_op jit(solution)/shard_map/ppermute | solution.py:46
  61.3 12.0 %collective-permute-start.14 = (bf16[128,1024]{1,0:T(8,128)(2,1)S(1)}, bf16[128,1024]{1,0:T(8,128)(2,1)S(1)}, u32[]{:S(2)}, u32[]{:S(2)}) collective-permute-start(bf16[128,1024]{1,0:T(8,128)(2,1)S(1)} %spread_far.3), channel_id=1, source_target_pairs={{0,2},{1,3},{2,0},{3,1},{4,6},{5,7},{6,4},{7,5},{8,10},{9,11},{10,... | collective-permute-start | bytes 786440 | tf_op jit(solution)/shard_map/ppermute | solution.py:46
  62.1 4.7 %collective-permute-start.8 = (bf16[128,256]{1,0:T(8,128)(2,1)S(1)}, bf16[128,256]{1,0:T(8,128)(2,1)S(1)}, u32[]{:S(2)}, u32[]{:S(2)}) collective-permute-start(bf16[128,256]{1,0:T(8,128)(2,1)S(1)} %get-tuple-element.48.own), channel_id=1, source_target_pairs={{0,1},{1,0},{2,3},{3,2},{4,5},{5,4},{6,7},{7,6},{8,9},{9,8},{10,11... | collective-permute-start | bytes 196616 | tf_op jit(solution)/shard_map/ppermute | solution.py:46
  64.4 8.9 %collective-permute-start.15 = (bf16[128,512]{1,0:T(8,128)(2,1)S(1)}, bf16[128,512]{1,0:T(8,128)(2,1)S(1)}, u32[]{:S(2)}, u32[]{:S(2)}) collective-permute-start(bf16[128,512]{1,0:T(8,128)(2,1)S(1)} %spread_far.4), channel_id=1, source_target_pairs={{0,2},{1,3},{2,0},{3,1},{4,6},{5,7},{6,4},{7,5},{8,10},{9,11},{10,... | collective-permute-start | bytes 393224 | tf_op jit(solution)/shard_map/ppermute | solution.py:46
  65.2 10.1 %collective-permute-start.16 = (bf16[128,512]{1,0:T(8,128)(2,1)S(1)}, bf16[128,512]{1,0:T(8,128)(2,1)S(1)}, u32[]{:S(2)}, u32[]{:S(2)}) collective-permute-start(bf16[128,512]{1,0:T(8,128)(2,1)S(1)} %spread_far.5), channel_id=1, source_target_pairs={{0,2},{1,3},{2,0},{3,1},{4,6},{5,7},{6,4},{7,5},{8,10},{9,11},{10,... | collective-permute-start | bytes 393224 | tf_op jit(solution)/shard_map/ppermute | solution.py:46
  66.8 1.3 %collective-permute-start.10 = (bf16[128,256]{1,0:T(8,128)(2,1)S(1)}, bf16[128,256]{1,0:T(8,128)(2,1)S(1)}, u32[]{:S(2)}, u32[]{:S(2)}) collective-permute-start(bf16[128,256]{1,0:T(8,128)(2,1)S(1)} %collective-permute-done.9.far), channel_id=1, source_target_pairs={{0,1},{1,0},{2,3},{3,2},{4,5},{5,4},{6,7},{7,6},{8,9},{9,8},{10,11... | collective-permute-start | bytes 196616 | tf_op jit(solution)/shard_map/ppermute | solution.py:46
  (5 other events, 5.1 us)

commit v15 on v14

--- a/solution.py
+++ b/solution.py
@@ -129,16 +129,18 @@
     return call(begin_kernel, "begin", shapes, (x0, x1, c0, here), first=VMEM)
 
 
-def add_grad_kernel(c2, there_turned, part, own_part, near_part):
-    total = part[...] + dot(c2[...], there_turned[...])
-    heads = own_part.shape[1]
-    own_part[...] = total[:, :heads]
-    near_part[...] = total[:, heads:]
-
-
-def add_grad(c2, there_turned, part):
-    shapes = [shape(jnp.float32, part.shape[0], part.shape[1] // 2)] * 2
-    return call(add_grad_kernel, "add_grad", shapes, (c2, there_turned, part), first=VMEM)
+def add_grad_kernel(half):
+    def kernel(c2, there_turned, part, total):
+        heads = total.shape[1]
+        columns = slice(half * heads, (half + 1) * heads)
+        total[...] = part[:, columns] + dot(c2[...], there_turned[:, columns])
+
+    return kernel
+
+
+def add_grad(half, c2, there_turned, part):
+    out = shape(jnp.float32, part.shape[0], part.shape[1] // 2)
+    return call(add_grad_kernel(half), "add_grad", out, (c2, there_turned, part), first=VMEM)
 
 
 def add_squares_kernel(x2, squares_in, squares):
@@ -156,8 +158,8 @@
     x1,
     x2,
     x3,
-    gain_own,
-    gain_near,
+    gain_chip,
+    gain_far,
     w_query,
     w_key,
     w_value,
@@ -177,7 +179,7 @@
     inverse[...] = inverse_rms
     head_grad = (own_part[...] + got_part[...]).astype(jnp.bfloat16)
     for index, block in enumerate(blocks):
-        gain = (gain_own, gain_near)[index % 2][index // 2 : index // 2 + 1, :]
+        gain = (gain_chip, gain_far)[index // 2][index % 2 : index % 2 + 1, :]
         scaled = block[...].astype(jnp.float32) * inverse_rms
         normed = (scaled * gain.astype(jnp.float32)).astype(jnp.bfloat16)
         here = pl.ds(block_start(order, index, width), width)
@@ -410,7 +412,8 @@
 
     x2 = swap(inputs, 2, tensor)
     c2 = swap(cotangent, 2, tensor)
-    gain2 = swap(gain, 2, tensor)
+    gain_chip = jnp.concatenate([gain, swap(gain, 1, tensor)], axis=0)
+    gain_far = swap(gain_chip, 2, tensor)
     x1 = swap(inputs, 1, tensor)
     near_output = swap(w_output, 1, tensor)
     weights = (w_query, w_key, w_value)
@@ -427,17 +430,16 @@
     send, receive, segments = indices
     squares, part = begin(inputs, x1, cotangent, here)
 
-    x2, c2, gain2, squares, part = lax.optimization_barrier((x2, c2, gain2, squares, part))
+    x2, c2, gain_far, squares, part = lax.optimization_barrier((x2, c2, gain_far, squares, part))
     x3 = swap(x2, 1, tensor)
-    gain_own = jnp.concatenate([gain, gain2], axis=0)
-    gain_near = swap(gain_own, 1, tensor)
-    own_part, near_part = add_grad(c2, there_turned, part)
+    near_part = add_grad(1, c2, there_turned, part)
     got_part = swap(near_part, 1, tensor)
+    own_part = add_grad(0, c2, there_turned, after(part, near_part))
     squares = add_squares(x2, squares)
     home, inverse_rms, bucket = project(
         order,
         (inputs, x1, x2, x3),
-        (gain_own, gain_near),
+        (gain_chip, gain_far),
         weights,
         squares,
         own_part,

time: 76.5 us -> 75.8 us (level)
  waiting for transfers between devices: 18.4 us -> 16.4 us
  starting transfers between devices: 11.9 us -> 12.7 us
    ppermute x17, waiting for transfers between devices: 18.4 us -> 16.4 us  [swap(): return lax.ppermute(array, 'tensor', [(i, i ^ mask) for i in range(count)])]
    ppermute x17, starting transfers between devices: 11.9 us -> 12.7 us  [swap(): return lax.ppermute(array, 'tensor', [(i, i ^ mask) for i in range(count)])]
    pallas_call x8 -> x9, Pallas kernels: 9.45 us -> 9.84 us  [call(): pl.pallas_call(kernel, out_shape=shapes, in_specs=[first] + [rest] * (len...]
    unnamed x24 -> x22, local copies, waits for them, and re-layouts: 8.35 us -> 8.57 us
  transfers between devices with their start and end apart: 17 -> 17, of which waited for: 7 -> 8; matrix products, arithmetic and copies ran while one was open for 1% -> 1% of each run, Pallas kernels for 13% -> 14%
where the time goes in v15:
time: 75.8 us; the launch traced here: 75.4 us
  blocking collectives  22.7 us (30%)
  waiting for transfers between devices  16.4 us (22%)
  Pallas kernels  13.6 us (18%)
  starting transfers between devices  12.7 us (17%)
  local copies, waits for them, and re-layouts  9.26 us (12%)
  between operations  0.8 us (1%)
    all_to_all x2, blocking collectives, move(): return lax.all_to_all(bucket, 'dp', split_axis=0, concat_axis=0, tiled=True)  22.7 us
    ppermute x17, waiting for transfers between devices, swap(): return lax.ppermute(array, 'tensor', [(i, i ^ mask) for i in range(count)])  16.4 us
    ppermute x17, starting transfers between devices, swap(): return lax.ppermute(array, 'tensor', [(i, i ^ mask) for i in range(count)])  12.7 us
    pallas_call x9, Pallas kernels, call(): pl.pallas_call(kernel, out_shape=shapes, in_specs=[first] + [rest] * (len...  9.84 us
    unnamed x22, local copies, waits for them, and re-layouts  8.57 us
    pallas_call x4, Pallas kernels, spread(): pl.pallas_call(spread_kernel(first), out_shape=shape(dtype, own.shape[0],...  1.76 us
  transfers between devices with their start and end apart: 17, of which 8 were waited for; matrix products, arithmetic and copies ran while one was open for 1% of the time, Pallas kernels for 14%

profile of v15, /device:TPU:0, one launch (start us, length us, event | category | flops | bytes accessed | tf_op | source)
XLA Modules:
  0.0 75.4 jit_solution(16656971855039774267)
XLA Ops:
  1.2 2.9 %collective-permute-start.1 = (bf16[128,2048]{1,0:T(8,128)(2,1)}, bf16[128,2048]{1,0:T(8,128)(2,1)S(1)}, u32[]{:S(2)}, u32[]{:S(2)}) collective-permute-start(bf16[128,2048]{1,0:T(8,128)(2,1)} %inputs.3), channel_id=1, source_target_pairs={{0,2},{1,3},{2,0},{3,1},{4,6},{5,7},{6,4},{7,5},{8,10},{9,11},{10,... | collective-permute-start | bytes 1572872 | tf_op jit(solution)/shard_map/ppermute | solution.py:46
  4.9 1.2 %collective-permute-done.3 = bf16[1,2048]{1,0:T(2,128)(2,1)S(1)} collective-permute-done((bf16[1,2048]{1,0:T(2,128)(2,1)S(1)}, bf16[1,2048]{1,0:T(2,128)(2,1)S(1)}, u32[]{:S(2)}, u32[]{:S(2)}) %collective-permute-start.3) | collective-permute-done | bytes 4128 | tf_op jit(solution)/shard_map/ppermute | solution.py:46
  6.1 2.6 %collective-permute-start.4 = (bf16[2,2048]{1,0:T(2,128)(2,1)S(1)}, bf16[2,2048]{1,0:T(2,128)(2,1)S(1)}, u32[]{:S(2)}, u32[]{:S(2)}) collective-permute-start(bf16[2,2048]{1,0:T(2,128)(2,1)S(1)} %pad_maximum_fusion.gain_chip), channel_id=1, source_target_pairs={{0,2},{1,3},{2,0},{3,1},{4,6},{5,7},{6,4},{7,5},{8,10},{9,11},{10,... | collective-permute-start | bytes 24584 | tf_op jit(solution)/shard_map/ppermute | solution.py:46
  8.7 1.6 %copy-done = bf16[8192,128]{1,0:T(8,128)(2,1)S(1)} copy-done((bf16[8192,128]{1,0:T(8,128)(2,1)S(1)}, bf16[8192,128]{1,0:T(8,128)(2,1)}, u32[]{:S(2)}) %copy-start) | copy-done | bytes 2097176
  10.3 1.6 %copy-done.2 = bf16[8192,128]{1,0:T(8,128)(2,1)S(1)} copy-done((bf16[8192,128]{1,0:T(8,128)(2,1)S(1)}, bf16[8192,128]{1,0:T(8,128)(2,1)}, u32[]{:S(2)}) %copy-start.2) | copy-done | bytes 2097176
  11.9 1.6 %copy-done.4 = bf16[8192,128]{1,0:T(8,128)(2,1)S(1)} copy-done((bf16[8192,128]{1,0:T(8,128)(2,1)S(1)}, bf16[8192,128]{1,0:T(8,128)(2,1)}, u32[]{:S(2)}) %copy-start.4) | copy-done | bytes 2097176
  13.5 1.6 %copy-done.7 = bf16[128,8192]{1,0:T(8,128)(2,1)S(1)} copy-done((bf16[128,8192]{1,0:T(8,128)(2,1)S(1)}, bf16[128,8192]{1,0:T(8,128)(2,1)}, u32[]{:S(2)}) %copy-start.7) | copy-done | bytes 2097176
  17.0 3.7 %prepare.1 = (bf16[384,4096]{1,0:T(8,128)(2,1)S(1)}, bf16[384,4096]{1,0:T(8,128)(2,1)S(1)}, bf16[256,2048]{1,0:T(8,128)(2,1)S(1)}, bf16[256,2048]{1,0:T(8,128)(2...) custom-call(s32[4]{0:T(128)S(1)} %iota_xor_fusion.order, ...), custom_call_target="tpu_custom_call" | custom-call | flops 1000 | bytes 1000 | tf_op jit(solution)/shard_map/prepare/pallas_call | solution.py:28
  21.3 6.7 %collective-permute-done.4.gain_far = bf16[2,2048]{1,0:T(2,128)(2,1)S(1)} collective-permute-done((bf16[2,2048]{1,0:T(2,128)(2,1)S(1)}, bf16[2,2048]{1,0:T(2,128)(2,1)S(1)}, u32[]{:S(2)}, u32[]{:S(2)}) %collective-permute-start.4) | collective-permute-done | bytes 8224 | tf_op jit(solution)/shard_map/ppermute | solution.py:46
  30.2 2.2 %project.1 = (bf16[128,384]{1,0:T(8,128)(2,1)S(1)}, f32[128,1]{1,0:T(8,128)S(1)}, bf16[128,512]{1,0:T(8,128)(2,1)S(1)}) custom-call(s32[4]{0:T(128)S(1)} %iota_xor_fusion.order, bf16[128,2048]{1,0:T(8,128)(2,1)S(1)} %copy-done.5, bf16[128,2048]{1,0:T(8,128)(2,1)S(1)} %collective-permute-done.x1, bf16[128,2048]{1,0:T(8,128)(2,1)S(1)} %collective-permute-done.1.x2, ...), custom_call_target="tpu_custom_call" | custom-call | flops 1000 | bytes 1000 | tf_op jit(solution)/shard_map/project/pallas_call | solution.py:28
  33.0 1.7 %collective-permute-start.11 = (bf16[256,2048]{1,0:T(8,128)(2,1)S(1)}, bf16[256,2048]{1,0:T(8,128)(2,1)S(1)}, u32[]{:S(2)}, u32[]{:S(2)}) collective-permute-start(bf16[256,2048]{1,0:T(8,128)(2,1)S(1)} %get-tuple-element.48), channel_id=1, source_target_pairs={{0,2},{1,3},{2,0},{3,1},{4,6},{5,7},{6,4},{7,5},{8,10},{9,11},{10,... | collective-permute-start | bytes 3145736 | tf_op jit(solution)/shard_map/ppermute | solution.py:46
  34.8 12.9 %all_to_all.22 = bf16[8,16,512]{2,1,0:T(8,128)(2,1)S(1)} all-to-all(bf16[8,16,512]{2,1,0:T(8,128)(2,1)S(1)} %bitcast.9), channel_id=1, replica_groups=mesh['dp'=8,'tensor'=4] {'dp'}, dimensions={0} | all-to-all | bytes 262144 | tf_op jit(solution)/shard_map/all_to_all | solution.py:388
  47.7 1.1 %attend.1 = bf16[128,512]{1,0:T(8,128)(2,1)S(1)} custom-call(bf16[128,512]{1,0:T(8,128)(2,1)S(1)} %bitcast.7, s32[1,128]{1,0:T(1,128)S(1)} %get-tuple-element.43.receive, s32[1,128]{1,0:T(1,128)S(1)} %get-tuple-element.44.segments), custom_call_target="tpu_custom_call" | custom-call | flops 1000 | bytes 1000 | tf_op jit(solution)/shard_map/attend/pallas_call | solution.py:28
  48.8 9.7 %all_to_all.23 = bf16[8,16,512]{2,1,0:T(8,128)(2,1)S(1)} all-to-all(bf16[8,16,512]{2,1,0:T(8,128)(2,1)S(1)} %bitcast.8), channel_id=1, replica_groups=mesh['dp'=8,'tensor'=4] {'dp'}, dimensions={0} | all-to-all | bytes 262144 | tf_op jit(solution)/shard_map/all_to_all | solution.py:388
  59.4 0.7 collective-permute-done.12.near
  60.6 0.9 %collective-permute-start.14 = (bf16[128,1024]{1,0:T(8,128)(2,1)S(1)}, bf16[128,1024]{1,0:T(8,128)(2,1)S(1)}, u32[]{:S(2)}, u32[]{:S(2)}) collective-permute-start(bf16[128,1024]{1,0:T(8,128)(2,1)S(1)} %spread_far.3), channel_id=1, source_target_pairs={{0,2},{1,3},{2,0},{3,1},{4,6},{5,7},{6,4},{7,5},{8,10},{9,11},{10,... | collective-permute-start | bytes 786440 | tf_op jit(solution)/shard_map/ppermute | solution.py:46
  61.5 1.9 %collective-permute-done.9.far = bf16[128,256]{1,0:T(8,128)(2,1)S(1)} collective-permute-done((bf16[128,256]{1,0:T(8,128)(2,1)S(1)}, bf16[128,256]{1,0:T(8,128)(2,1)S(1)}, u32[]{:S(2)}, u32[]{:S(2)}) %collective-permute-start.9) | collective-permute-done | bytes 65568 | tf_op jit(solution)/shard_map/ppermute | solution.py:46
  64.6 1.6 %collective-permute-start.16 = (bf16[128,512]{1,0:T(8,128)(2,1)S(1)}, bf16[128,512]{1,0:T(8,128)(2,1)S(1)}, u32[]{:S(2)}, u32[]{:S(2)}) collective-permute-start(bf16[128,512]{1,0:T(8,128)(2,1)S(1)} %spread_far.5), channel_id=1, source_target_pairs={{0,2},{1,3},{2,0},{3,1},{4,6},{5,7},{6,4},{7,5},{8,10},{9,11},{10,... | collective-permute-start | bytes 393224 | tf_op jit(solution)/shard_map/ppermute | solution.py:46
  66.2 1.3 %collective-permute-done.10.last = bf16[128,256]{1,0:T(8,128)(2,1)S(1)} collective-permute-done((bf16[128,256]{1,0:T(8,128)(2,1)S(1)}, bf16[128,256]{1,0:T(8,128)(2,1)S(1)}, u32[]{:S(2)}, u32[]{:S(2)}) %collective-permute-start.10) | collective-permute-done | bytes 65568 | tf_op jit(solution)/shard_map/ppermute | solution.py:46
  67.4 1.3 %finish_out.1 = bf16[128,2048]{1,0:T(8,128)(2,1)} custom-call(bf16[128,2048]{1,0:T(8,128)(2,1)S(1)} %copy-done.5, bf16[128,256]{1,0:T(8,128)(2,1)S(1)} %get-tuple-element.46.own, bf16[128,256]{1,0:T(8,128)(2,1)S(1)} %collective-permute-done.8.near, bf16[128,256]{1,0:T(8,128)(2,1)S(1)} %collective-permute-done.9.far, ...), custom_call_target="tpu_custom_call" | custom-call | flops 1000 | bytes 1000 | tf_op jit(solution)/shard_map/finish_out/pallas_call | solution.py:28
  69.4 3.2 %collective-permute-done.15.pieces_1_ = bf16[128,512]{1,0:T(8,128)(2,1)S(1)} collective-permute-done((bf16[128,512]{1,0:T(8,128)(2,1)S(1)}, bf16[128,512]{1,0:T(8,128)(2,1)S(1)}, u32[]{:S(2)}, u32[]{:S(2)}) %collective-permute-start.15) | collective-permute-done | bytes 131104 | tf_op jit(solution)/shard_map/ppermute | solution.py:46
  72.6 1.3 %finish_most.1 = (bf16[128,2048]{1,0:T(8,128)(2,1)}, f32[128,512]{1,0:T(8,128)S(1)}) custom-call(bf16[128,2048]{1,0:T(8,128)(2,1)S(1)} %copy-done.5, bf16[128,2048]{1,0:T(8,128)(2,1)S(1)} %copy-done.6, bf16[1,2048]{1,0:T(2,128)(2,1)S(1)} %reshape.17.gain, f32[128,1]{1,0:T(8,128)S(1)} %get-tuple-element.49.inverse, ...), custom_call_target="tpu_custom_call" | custom-call | flops 1000 | bytes 1000 | tf_op jit(solution)/shard_map/finish_most/pallas_call | solution.py:366
  73.9 0.8 collective-permute-done.16.rest
  74.6 0.8 %finish_rest.1 = bf16[128,2048]{1,0:T(8,128)(2,1)} custom-call(bf16[1,2048]{1,0:T(2,128)(2,1)S(1)} %reshape.17.gain, f32[128,1]{1,0:T(8,128)S(1)} %get-tuple-element.49.inverse, f32[128,512]{1,0:T(8,128)S(1)} %get-tuple-element.58.left, bf16[128,512]{1,0:T(8,128)(2,1)S(1)} %collective-permute-done.16.rest, ...), custom_call_target="tpu_custom_call", output_to_operand_aliasing={{}: (4, {})} | custom-call | flops 1000 | bytes 1000 | tf_op jit(solution)/shard_map/finish_rest/pallas_call | solution.py:375
  (52 shorter events, 9.9 us)
Async XLA Ops:
  0.6 8.1 %collective-permute-start.5 = (bf16[128,8192]{1,0:T(8,128)(2,1)}, bf16[128,8192]{1,0:T(8,128)(2,1)}, u32[]{:S(2)}, u32[]{:S(2)}) collective-permute-start(bf16[128,8192]{1,0:T(8,128)(2,1)} %w_output.1), channel_id=1, source_target_pairs={{0,1},{1,0},{2,3},{3,2},{4,5},{5,4},{6,7},{7,6},{8,9},{9,8},{10,11... | collective-permute-start | bytes 6291464 | tf_op jit(solution)/shard_map/ppermute | solution.py:46
  1.1 19.5 %collective-permute-start = (bf16[128,2048]{1,0:T(8,128)(2,1)}, bf16[128,2048]{1,0:T(8,128)(2,1)S(1)}, u32[]{:S(2)}, u32[]{:S(2)}) collective-permute-start(bf16[128,2048]{1,0:T(8,128)(2,1)} %inputs.3), channel_id=1, source_target_pairs={{0,1},{1,0},{2,3},{3,2},{4,5},{5,4},{6,7},{7,6},{8,9},{9,8},{10,11... | collective-permute-start | bytes 1572872 | tf_op jit(solution)/shard_map/ppermute | solution.py:46
  1.2 26.7 %collective-permute-start.1 = (bf16[128,2048]{1,0:T(8,128)(2,1)}, bf16[128,2048]{1,0:T(8,128)(2,1)S(1)}, u32[]{:S(2)}, u32[]{:S(2)}) collective-permute-start(bf16[128,2048]{1,0:T(8,128)(2,1)} %inputs.3), channel_id=1, source_target_pairs={{0,2},{1,3},{2,0},{3,1},{4,6},{5,7},{6,4},{7,5},{8,10},{9,11},{10,... | collective-permute-start | bytes 1572872 | tf_op jit(solution)/shard_map/ppermute | solution.py:46
  4.2 23.8 %collective-permute-start.2 = (bf16[128,2048]{1,0:T(8,128)(2,1)}, bf16[128,2048]{1,0:T(8,128)(2,1)S(1)}, u32[]{:S(2)}, u32[]{:S(2)}) collective-permute-start(bf16[128,2048]{1,0:T(8,128)(2,1)} %cotangent.1), channel_id=1, source_target_pairs={{0,2},{1,3},{2,0},{3,1},{4,6},{5,7},{6,4},{7,5},{8,10},{9,11},{10,... | collective-permute-start | bytes 1572872 | tf_op jit(solution)/shard_map/ppermute | solution.py:46
  4.9 1.2 %collective-permute-start.3 = (bf16[1,2048]{1,0:T(2,128)(2,1)S(1)}, bf16[1,2048]{1,0:T(2,128)(2,1)S(1)}, u32[]{:S(2)}, u32[]{:S(2)}) collective-permute-start(bf16[1,2048]{1,0:T(2,128)(2,1)S(1)} %reshape.17.gain), channel_id=1, source_target_pairs={{0,1},{1,0},{2,3},{3,2},{4,5},{5,4},{6,7},{7,6},{8,9},{9,8},{10,11... | collective-permute-start | bytes 12296 | tf_op jit(solution)/shard_map/ppermute | solution.py:46
  6.1 21.9 %collective-permute-start.4 = (bf16[2,2048]{1,0:T(2,128)(2,1)S(1)}, bf16[2,2048]{1,0:T(2,128)(2,1)S(1)}, u32[]{:S(2)}, u32[]{:S(2)}) collective-permute-start(bf16[2,2048]{1,0:T(2,128)(2,1)S(1)} %pad_maximum_fusion.gain_chip), channel_id=1, source_target_pairs={{0,2},{1,3},{2,0},{3,1},{4,6},{5,7},{6,4},{7,5},{8,10},{9,11},{10,... | collective-permute-start | bytes 24584 | tf_op jit(solution)/shard_map/ppermute | solution.py:46
  8.7 1.6 %copy-start = (bf16[8192,128]{1,0:T(8,128)(2,1)S(1)}, bf16[8192,128]{1,0:T(8,128)(2,1)}, u32[]{:S(2)}) copy-start(bf16[8192,128]{1,0:T(8,128)(2,1)} %w_query.3) | copy-start | bytes 6291460
  10.3 1.6 %copy-start.2 = (bf16[8192,128]{1,0:T(8,128)(2,1)S(1)}, bf16[8192,128]{1,0:T(8,128)(2,1)}, u32[]{:S(2)}) copy-start(bf16[8192,128]{1,0:T(8,128)(2,1)} %w_key.3) | copy-start | bytes 6291460
  11.9 1.6 %copy-start.4 = (bf16[8192,128]{1,0:T(8,128)(2,1)S(1)}, bf16[8192,128]{1,0:T(8,128)(2,1)}, u32[]{:S(2)}) copy-start(bf16[8192,128]{1,0:T(8,128)(2,1)} %w_value.3) | copy-start | bytes 6291460
  17.0 3.7 %copy-start.5 = (bf16[128,2048]{1,0:T(8,128)(2,1)S(1)}, bf16[128,2048]{1,0:T(8,128)(2,1)}, u32[]{:S(2)}) copy-start(bf16[128,2048]{1,0:T(8,128)(2,1)} %inputs.3) | copy-start | bytes 1572868
  17.0 3.7 %copy-start.6 = (bf16[128,2048]{1,0:T(8,128)(2,1)S(1)}, bf16[128,2048]{1,0:T(8,128)(2,1)}, u32[]{:S(2)}) copy-start(bf16[128,2048]{1,0:T(8,128)(2,1)} %cotangent.1) | copy-start | bytes 1572868
  28.0 2.0 %collective-permute-start.6 = (bf16[128,2048]{1,0:T(8,128)(2,1)S(1)}, bf16[128,2048]{1,0:T(8,128)(2,1)S(1)}, u32[]{:S(2)}, u32[]{:S(2)}) collective-permute-start(bf16[128,2048]{1,0:T(8,128)(2,1)S(1)} %collective-permute-done.1.x2), channel_id=1, source_target_pairs={{0,1},{1,0},{2,3},{3,2},{4,5},{5,4},{6,7},{7,6},{8,9},{9,8},{10,11... | collective-permute-start | bytes 1572872 | tf_op jit(solution)/shard_map/ppermute | solution.py:46
  28.0 2.0 %copy-start.1 = (bf16[8192,128]{1,0:T(8,128)(2,1)S(1)}, bf16[8192,128]{1,0:T(8,128)(2,1)}, u32[]{:S(2)}) copy-start(bf16[8192,128]{1,0:T(8,128)(2,1)} %w_query.3) | copy-start | bytes 6291460
  28.0 2.2 %copy-start.3 = (bf16[8192,128]{1,0:T(8,128)(2,1)S(1)}, bf16[8192,128]{1,0:T(8,128)(2,1)}, u32[]{:S(2)}) copy-start(bf16[8192,128]{1,0:T(8,128)(2,1)} %w_key.3) | copy-start | bytes 6291460
  28.3 1.7 %collective-permute-start.7 = (f32[128,128]{1,0:T(8,128)S(1)}, f32[128,128]{1,0:T(8,128)S(1)}, u32[]{:S(2)}, u32[]{:S(2)}) collective-permute-start(f32[128,128]{1,0:T(8,128)S(1)} %add_grad.2), channel_id=1, source_target_pairs={{0,1},{1,0},{2,3},{3,2},{4,5},{5,4},{6,7},{7,6},{8,9},{9,8},{10,11... | collective-permute-start | bytes 196616 | tf_op jit(solution)/shard_map/ppermute | solution.py:46
  32.4 27.7 %collective-permute-start.13 = (bf16[384,4096]{1,0:T(8,128)(2,1)S(1)}, bf16[384,4096]{1,0:T(8,128)(2,1)S(1)}, u32[]{:S(2)}, u32[]{:S(2)}) collective-permute-start(bf16[384,4096]{1,0:T(8,128)(2,1)S(1)} %get-tuple-element.53), channel_id=1, source_target_pairs={{0,1},{1,0},{2,3},{3,2},{4,5},{5,4},{6,7},{7,6},{8,9},{9,8},{10,11... | collective-permute-start | bytes 9437192 | tf_op jit(solution)/shard_map/ppermute | solution.py:46
  33.0 34.4 %collective-permute-start.11 = (bf16[256,2048]{1,0:T(8,128)(2,1)S(1)}, bf16[256,2048]{1,0:T(8,128)(2,1)S(1)}, u32[]{:S(2)}, u32[]{:S(2)}) collective-permute-start(bf16[256,2048]{1,0:T(8,128)(2,1)S(1)} %get-tuple-element.48), channel_id=1, source_target_pairs={{0,2},{1,3},{2,0},{3,1},{4,6},{5,7},{6,4},{7,5},{8,10},{9,11},{10,... | collective-permute-start | bytes 3145736 | tf_op jit(solution)/shard_map/ppermute | solution.py:46
  58.8 1.4 %collective-permute-start.12 = (bf16[128,384]{1,0:T(8,128)(2,1)S(1)}, bf16[128,384]{1,0:T(8,128)(2,1)S(1)}, u32[]{:S(2)}, u32[]{:S(2)}) collective-permute-start(bf16[128,384]{1,0:T(8,128)(2,1)S(1)} %get-tuple-element.56.own), channel_id=1, source_target_pairs={{0,1},{1,0},{2,3},{3,2},{4,5},{5,4},{6,7},{7,6},{8,9},{9,8},{10,11... | collective-permute-start | bytes 294920 | tf_op jit(solution)/shard_map/ppermute | solution.py:46
  58.9 4.5 %collective-permute-start.9 = (bf16[128,256]{1,0:T(8,128)(2,1)S(1)}, bf16[128,256]{1,0:T(8,128)(2,1)S(1)}, u32[]{:S(2)}, u32[]{:S(2)}) collective-permute-start(bf16[128,256]{1,0:T(8,128)(2,1)S(1)} %get-tuple-element.46.own), channel_id=1, source_target_pairs={{0,2},{1,3},{2,0},{3,1},{4,6},{5,7},{6,4},{7,5},{8,10},{9,11},{10,... | collective-permute-start | bytes 196616 | tf_op jit(solution)/shard_map/ppermute | solution.py:46
  60.6 12.0 %collective-permute-start.14 = (bf16[128,1024]{1,0:T(8,128)(2,1)S(1)}, bf16[128,1024]{1,0:T(8,128)(2,1)S(1)}, u32[]{:S(2)}, u32[]{:S(2)}) collective-permute-start(bf16[128,1024]{1,0:T(8,128)(2,1)S(1)} %spread_far.3), channel_id=1, source_target_pairs={{0,2},{1,3},{2,0},{3,1},{4,6},{5,7},{6,4},{7,5},{8,10},{9,11},{10,... | collective-permute-start | bytes 786440 | tf_op jit(solution)/shard_map/ppermute | solution.py:46
  61.5 4.7 %collective-permute-start.8 = (bf16[128,256]{1,0:T(8,128)(2,1)S(1)}, bf16[128,256]{1,0:T(8,128)(2,1)S(1)}, u32[]{:S(2)}, u32[]{:S(2)}) collective-permute-start(bf16[128,256]{1,0:T(8,128)(2,1)S(1)} %get-tuple-element.46.own), channel_id=1, source_target_pairs={{0,1},{1,0},{2,3},{3,2},{4,5},{5,4},{6,7},{7,6},{8,9},{9,8},{10,11... | collective-permute-start | bytes 196616 | tf_op jit(solution)/shard_map/ppermute | solution.py:46
  63.7 8.9 %collective-permute-start.15 = (bf16[128,512]{1,0:T(8,128)(2,1)S(1)}, bf16[128,512]{1,0:T(8,128)(2,1)S(1)}, u32[]{:S(2)}, u32[]{:S(2)}) collective-permute-start(bf16[128,512]{1,0:T(8,128)(2,1)S(1)} %spread_far.4), channel_id=1, source_target_pairs={{0,2},{1,3},{2,0},{3,1},{4,6},{5,7},{6,4},{7,5},{8,10},{9,11},{10,... | collective-permute-start | bytes 393224 | tf_op jit(solution)/shard_map/ppermute | solution.py:46
  64.6 10.1 %collective-permute-start.16 = (bf16[128,512]{1,0:T(8,128)(2,1)S(1)}, bf16[128,512]{1,0:T(8,128)(2,1)S(1)}, u32[]{:S(2)}, u32[]{:S(2)}) collective-permute-start(bf16[128,512]{1,0:T(8,128)(2,1)S(1)} %spread_far.5), channel_id=1, source_target_pairs={{0,2},{1,3},{2,0},{3,1},{4,6},{5,7},{6,4},{7,5},{8,10},{9,11},{10,... | collective-permute-start | bytes 393224 | tf_op jit(solution)/shard_map/ppermute | solution.py:46
  66.2 1.3 %collective-permute-start.10 = (bf16[128,256]{1,0:T(8,128)(2,1)S(1)}, bf16[128,256]{1,0:T(8,128)(2,1)S(1)}, u32[]{:S(2)}, u32[]{:S(2)}) collective-permute-start(bf16[128,256]{1,0:T(8,128)(2,1)S(1)} %collective-permute-done.9.far), channel_id=1, source_target_pairs={{0,1},{1,0},{2,3},{3,2},{4,5},{5,4},{6,7},{7,6},{8,9},{9,8},{10,11... | collective-permute-start | bytes 196616 | tf_op jit(solution)/shard_map/ppermute | solution.py:46
  (4 other events, 3.6 us)

commit v16 on v15

--- a/solution.py
+++ b/solution.py
@@ -16,13 +16,15 @@
 VMEM = pl.BlockSpec(memory_space=pltpu.VMEM)
 SMEM = pl.BlockSpec(memory_space=pltpu.SMEM)
 TILE = 512
+SQUARES_FLOPS = 4000000000
+HOME_FLOPS = 24000000000
 
 
 def dot(left, right, dims=(((1,), (0,)), ((), ()))):
     return lax.dot_general(left, right, dims, preferred_element_type=jnp.float32)
 
 
-def call(kernel, name, out_shape, operands, scratch=(), first=SMEM, rest=VMEM):
+def call(kernel, name, out_shape, operands, scratch=(), first=SMEM, rest=VMEM, flops=1000):
     single = not isinstance(out_shape, (list, tuple))
     shapes = [out_shape] if single else list(out_shape)
     results = pl.pallas_call(
@@ -32,7 +34,7 @@
         out_specs=[VMEM] * len(shapes),
         scratch_shapes=list(scratch),
         compiler_params=pltpu.CompilerParams(vmem_limit_bytes=VMEM_LIMIT),
-        cost_estimate=pl.CostEstimate(flops=1000, bytes_accessed=1000, transcendentals=0),
+        cost_estimate=pl.CostEstimate(flops=flops, bytes_accessed=1000, transcendentals=0),
         name=name,
     )(*operands)
     return results[0] if single else results
@@ -149,7 +151,10 @@
 
 def add_squares(x2, squares):
     out = shape(jnp.float32, *squares.shape)
-    return call(add_squares_kernel, "add_squares", out, (x2, squares), first=VMEM)
+    operands = (x2, squares)
+    return call(
+        add_squares_kernel, "add_squares", out, operands, first=VMEM, flops=SQUARES_FLOPS
+    )
 
 
 def project_kernel(
@@ -268,7 +273,8 @@
 def bring_home(moved, send, home):
     rows = home.shape[0]
     shapes = [shape(jnp.bfloat16, rows, 3 * HEAD_DIM), shape(jnp.bfloat16, rows, 2 * HEAD_DIM)]
-    return call(bring_home_kernel, "bring_home", shapes, (moved, send, home), first=VMEM)
+    operands = (moved, send, home)
+    return call(bring_home_kernel, "bring_home", shapes, operands, first=VMEM, flops=HOME_FLOPS)
 
 
 def spread_kernel(first):
@@ -435,7 +441,7 @@
     near_part = add_grad(1, c2, there_turned, part)
     got_part = swap(near_part, 1, tensor)
     own_part = add_grad(0, c2, there_turned, after(part, near_part))
-    squares = add_squares(x2, squares)
+    squares = add_squares(x2, after(squares, near_part, own_part))
     home, inverse_rms, bucket = project(
         order,
         (inputs, x1, x2, x3),
@@ -447,9 +453,10 @@
         send,
     )
     near_turned = swap(after(near_turned, home), 1, tensor)
-    there = swap(after(there, home), 2, tensor)
+    there = swap(after(there, near_part), 2, tensor)
     back = attend(move(bucket), receive, segments)
-    own, own_extras = bring_home(move(back), send, home)
+    moved, there = lax.optimization_barrier((move(back), there))
+    own, own_extras = bring_home(moved, send, home)
 
     near = swap(own, 1, tensor)
     far_extras = swap(own_extras, 2, tensor)

time: 75.8 us -> 76.6 us (1.011)
  starting transfers between devices: 12.7 us -> 13.6 us
  waiting for transfers between devices: 16.4 us -> 15.5 us
    ppermute x17, starting transfers between devices: 12.7 us -> 13.6 us  [swap(): return lax.ppermute(array, 'tensor', [(i, i ^ mask) for i in range(count)])]
    ppermute x17, waiting for transfers between devices: 16.4 us -> 15.5 us  [swap(): return lax.ppermute(array, 'tensor', [(i, i ^ mask) for i in range(count)])]
  transfers between devices with their start and end apart: 17 -> 17, of which waited for: 8 -> 8; matrix products, arithmetic and copies ran while one was open for 1% -> 1% of each run, Pallas kernels for 14% -> 17%
where the time goes in v16:
time: 76.6 us; the launch traced here: 76.1 us
  blocking collectives  23.1 us (30%)
  waiting for transfers between devices  15.5 us (20%)
  Pallas kernels  14 us (18%)
  starting transfers between devices  13.6 us (18%)
  local copies, waits for them, and re-layouts  9.04 us (12%)
  between operations  0.82 us (1%)
    all_to_all x2, blocking collectives, move(): return lax.all_to_all(bucket, 'dp', split_axis=0, concat_axis=0, tiled=True)  23.1 us
    ppermute x17, waiting for transfers between devices, swap(): return lax.ppermute(array, 'tensor', [(i, i ^ mask) for i in range(count)])  15.5 us
    ppermute x17, starting transfers between devices, swap(): return lax.ppermute(array, 'tensor', [(i, i ^ mask) for i in range(count)])  13.6 us
    pallas_call x9, Pallas kernels, call(): pl.pallas_call(kernel, out_shape=shapes, in_specs=[first] + [rest] * (len...  10.2 us
    unnamed x22, local copies, waits for them, and re-layouts  8.35 us
    pallas_call x4, Pallas kernels, spread(): pl.pallas_call(spread_kernel(first), out_shape=shape(dtype, own.shape[0],...  1.77 us
  transfers between devices with their start and end apart: 17, of which 8 were waited for; matrix products, arithmetic and copies ran while one was open for 1% of the time, Pallas kernels for 17%

profile of v16, /device:TPU:0, one launch (start us, length us, event | category | flops | bytes accessed | tf_op | source)
XLA Modules:
  0.0 76.1 jit_solution(14427268738406523036)
XLA Ops:
  1.2 2.9 %collective-permute-start.1 = (bf16[128,2048]{1,0:T(8,128)(2,1)}, bf16[128,2048]{1,0:T(8,128)(2,1)}, u32[]{:S(2)}, u32[]{:S(2)}) collective-permute-start(bf16[128,2048]{1,0:T(8,128)(2,1)} %inputs.3), channel_id=1, source_target_pairs={{0,2},{1,3},{2,0},{3,1},{4,6},{5,7},{6,4},{7,5},{8,10},{9,11},{10,... | collective-permute-start | bytes 1572872 | tf_op jit(solution)/shard_map/ppermute | solution.py:48
  4.9 1.2 %collective-permute-done.3 = bf16[1,2048]{1,0:T(2,128)(2,1)S(1)} collective-permute-done((bf16[1,2048]{1,0:T(2,128)(2,1)S(1)}, bf16[1,2048]{1,0:T(2,128)(2,1)S(1)}, u32[]{:S(2)}, u32[]{:S(2)}) %collective-permute-start.3) | collective-permute-done | bytes 4128 | tf_op jit(solution)/shard_map/ppermute | solution.py:48
  6.1 2.6 %collective-permute-start.4 = (bf16[2,2048]{1,0:T(2,128)(2,1)S(1)}, bf16[2,2048]{1,0:T(2,128)(2,1)S(1)}, u32[]{:S(2)}, u32[]{:S(2)}) collective-permute-start(bf16[2,2048]{1,0:T(2,128)(2,1)S(1)} %pad_maximum_fusion.gain_chip), channel_id=1, source_target_pairs={{0,2},{1,3},{2,0},{3,1},{4,6},{5,7},{6,4},{7,5},{8,10},{9,11},{10,... | collective-permute-start | bytes 24584 | tf_op jit(solution)/shard_map/ppermute | solution.py:48
  8.7 1.6 %copy-done = bf16[8192,128]{1,0:T(8,128)(2,1)S(1)} copy-done((bf16[8192,128]{1,0:T(8,128)(2,1)S(1)}, bf16[8192,128]{1,0:T(8,128)(2,1)}, u32[]{:S(2)}) %copy-start) | copy-done | bytes 2097176
  10.3 1.6 %copy-done.2 = bf16[8192,128]{1,0:T(8,128)(2,1)S(1)} copy-done((bf16[8192,128]{1,0:T(8,128)(2,1)S(1)}, bf16[8192,128]{1,0:T(8,128)(2,1)}, u32[]{:S(2)}) %copy-start.2) | copy-done | bytes 2097176
  11.9 1.6 %copy-done.4 = bf16[8192,128]{1,0:T(8,128)(2,1)S(1)} copy-done((bf16[8192,128]{1,0:T(8,128)(2,1)S(1)}, bf16[8192,128]{1,0:T(8,128)(2,1)}, u32[]{:S(2)}) %copy-start.4) | copy-done | bytes 2097176
  13.5 1.6 %copy-done.7 = bf16[128,8192]{1,0:T(8,128)(2,1)S(1)} copy-done((bf16[128,8192]{1,0:T(8,128)(2,1)S(1)}, bf16[128,8192]{1,0:T(8,128)(2,1)}, u32[]{:S(2)}) %copy-start.7) | copy-done | bytes 2097176
  17.0 2.5 %prepare.1 = (bf16[384,4096]{1,0:T(8,128)(2,1)S(1)}, bf16[384,4096]{1,0:T(8,128)(2,1)S(1)}, bf16[256,2048]{1,0:T(8,128)(2,1)S(1)}, bf16[256,2048]{1,0:T(8,128)(2...) custom-call(s32[4]{0:T(128)S(1)} %iota_xor_fusion.order, ...), custom_call_target="tpu_custom_call" | custom-call | flops 1000 | bytes 1000 | tf_op jit(solution)/shard_map/prepare/pallas_call | solution.py:30
  20.1 7.8 %collective-permute-done.4.gain_far = bf16[2,2048]{1,0:T(2,128)(2,1)S(1)} collective-permute-done((bf16[2,2048]{1,0:T(2,128)(2,1)S(1)}, bf16[2,2048]{1,0:T(2,128)(2,1)S(1)}, u32[]{:S(2)}, u32[]{:S(2)}) %collective-permute-start.4) | collective-permute-done | bytes 8224 | tf_op jit(solution)/shard_map/ppermute | solution.py:48
  29.1 1.8 %collective-permute-start.8 = (bf16[256,2048]{1,0:T(8,128)(2,1)S(1)}, bf16[256,2048]{1,0:T(8,128)(2,1)S(1)}, u32[]{:S(2)}, u32[]{:S(2)}) collective-permute-start(bf16[256,2048]{1,0:T(8,128)(2,1)S(1)} %get-tuple-element.50), channel_id=1, source_target_pairs={{0,2},{1,3},{2,0},{3,1},{4,6},{5,7},{6,4},{7,5},{8,10},{9,11},{10,... | collective-permute-start | bytes 3145736 | tf_op jit(solution)/shard_map/ppermute | solution.py:48
  31.0 1.2 %add_squares.1.squares = f32[128,1]{1,0:T(8,128)S(1)} custom-call(bf16[128,2048]{1,0:T(8,128)(2,1)} %collective-permute-done.1.x2, f32[128,1]{1,0:T(8,128)S(1)} %get-tuple-element.44.squares_in), custom_call_target="tpu_custom_call" | custom-call | flops 4000000000 | bytes 1000 | tf_op jit(solution)/shard_map/add_squares/pallas_call | solution.py:30
  32.2 2.8 %project.1 = (bf16[128,384]{1,0:T(8,128)(2,1)S(1)}, f32[128,1]{1,0:T(8,128)S(1)}, bf16[128,512]{1,0:T(8,128)(2,1)S(1)}) custom-call(s32[4]{0:T(128)S(1)} %iota_xor_fusion.order, bf16[128,2048]{1,0:T(8,128)(2,1)S(1)} %copy-done.5, bf16[128,2048]{1,0:T(8,128)(2,1)S(1)} %collective-permute-done.x1, bf16[128,2048]{1,0:T(8,128)(2,1)} %collective-permute-done.1.x2, ...), custom_call_target="tpu_custom_call" | custom-call | flops 1000 | bytes 1000 | tf_op jit(solution)/shard_map/project/pallas_call | solution.py:30
  35.0 13.2 %all_to_all.23 = bf16[8,16,512]{2,1,0:T(8,128)(2,1)S(1)} all-to-all(bf16[8,16,512]{2,1,0:T(8,128)(2,1)S(1)} %bitcast.8), channel_id=1, replica_groups=mesh['dp'=8,'tensor'=4] {'dp'}, dimensions={0} | all-to-all | bytes 262144 | tf_op jit(solution)/shard_map/all_to_all | solution.py:394
  48.3 1.1 %attend.1 = bf16[128,512]{1,0:T(8,128)(2,1)S(1)} custom-call(bf16[128,512]{1,0:T(8,128)(2,1)S(1)} %bitcast.6, s32[1,128]{1,0:T(1,128)S(1)} %get-tuple-element.47.receive, s32[1,128]{1,0:T(1,128)S(1)} %get-tuple-element.48.segments), custom_call_target="tpu_custom_call" | custom-call | flops 1000 | bytes 1000 | tf_op jit(solution)/shard_map/attend/pallas_call | solution.py:30
  49.4 9.9 %all_to_all.24 = bf16[8,16,512]{2,1,0:T(8,128)(2,1)S(1)} all-to-all(bf16[8,16,512]{2,1,0:T(8,128)(2,1)S(1)} %bitcast.7), channel_id=1, replica_groups=mesh['dp'=8,'tensor'=4] {'dp'}, dimensions={0} | all-to-all | bytes 262144 | tf_op jit(solution)/shard_map/all_to_all | solution.py:394
  59.6 1.1 %collective-permute-start.10 = (bf16[128,256]{1,0:T(8,128)(2,1)S(1)}, bf16[128,256]{1,0:T(8,128)(2,1)S(1)}, u32[]{:S(2)}, u32[]{:S(2)}) collective-permute-start(bf16[128,256]{1,0:T(8,128)(2,1)S(1)} %get-tuple-element.53.own), channel_id=1, source_target_pairs={{0,2},{1,3},{2,0},{3,1},{4,6},{5,7},{6,4},{7,5},{8,10},{9,11},{10,... | collective-permute-start | bytes 196616 | tf_op jit(solution)/shard_map/ppermute | solution.py:48
  61.3 1.1 %collective-permute-start.14 = (bf16[128,1024]{1,0:T(8,128)(2,1)S(1)}, bf16[128,1024]{1,0:T(8,128)(2,1)S(1)}, u32[]{:S(2)}, u32[]{:S(2)}) collective-permute-start(bf16[128,1024]{1,0:T(8,128)(2,1)S(1)} %spread_far.3), channel_id=1, source_target_pairs={{0,2},{1,3},{2,0},{3,1},{4,6},{5,7},{6,4},{7,5},{8,10},{9,11},{10,... | collective-permute-start | bytes 786440 | tf_op jit(solution)/shard_map/ppermute | solution.py:48
  62.4 1.6 %collective-permute-done.10.far = bf16[128,256]{1,0:T(8,128)(2,1)S(1)} collective-permute-done((bf16[128,256]{1,0:T(8,128)(2,1)S(1)}, bf16[128,256]{1,0:T(8,128)(2,1)S(1)}, u32[]{:S(2)}, u32[]{:S(2)}) %collective-permute-start.10) | collective-permute-done | bytes 65568 | tf_op jit(solution)/shard_map/ppermute | solution.py:48
  64.4 1.1 %collective-permute-start.15 = (bf16[128,512]{1,0:T(8,128)(2,1)S(1)}, bf16[128,512]{1,0:T(8,128)(2,1)S(1)}, u32[]{:S(2)}, u32[]{:S(2)}) collective-permute-start(bf16[128,512]{1,0:T(8,128)(2,1)S(1)} %spread_far.4), channel_id=1, source_target_pairs={{0,2},{1,3},{2,0},{3,1},{4,6},{5,7},{6,4},{7,5},{8,10},{9,11},{10,... | collective-permute-start | bytes 393224 | tf_op jit(solution)/shard_map/ppermute | solution.py:48
  65.8 1.0 %collective-permute-start.16 = (bf16[128,512]{1,0:T(8,128)(2,1)S(1)}, bf16[128,512]{1,0:T(8,128)(2,1)S(1)}, u32[]{:S(2)}, u32[]{:S(2)}) collective-permute-start(bf16[128,512]{1,0:T(8,128)(2,1)S(1)} %spread_far.5), channel_id=1, source_target_pairs={{0,2},{1,3},{2,0},{3,1},{4,6},{5,7},{6,4},{7,5},{8,10},{9,11},{10,... | collective-permute-start | bytes 393224 | tf_op jit(solution)/shard_map/ppermute | solution.py:48
  68.3 1.3 %finish_out.1 = bf16[128,2048]{1,0:T(8,128)(2,1)} custom-call(bf16[128,2048]{1,0:T(8,128)(2,1)S(1)} %copy-done.5, bf16[128,256]{1,0:T(8,128)(2,1)S(1)} %get-tuple-element.53.own, bf16[128,256]{1,0:T(8,128)(2,1)S(1)} %collective-permute-done.9.near, bf16[128,256]{1,0:T(8,128)(2,1)S(1)} %collective-permute-done.10.far, ...), custom_call_target="tpu_custom_call" | custom-call | flops 1000 | bytes 1000 | tf_op jit(solution)/shard_map/finish_out/pallas_call | solution.py:30
  70.3 3.1 %collective-permute-done.15.pieces_1_ = bf16[128,512]{1,0:T(8,128)(2,1)S(1)} collective-permute-done((bf16[128,512]{1,0:T(8,128)(2,1)S(1)}, bf16[128,512]{1,0:T(8,128)(2,1)S(1)}, u32[]{:S(2)}, u32[]{:S(2)}) %collective-permute-start.15) | collective-permute-done | bytes 131104 | tf_op jit(solution)/shard_map/ppermute | solution.py:48
  73.3 1.3 %finish_most.1 = (bf16[128,2048]{1,0:T(8,128)(2,1)}, f32[128,512]{1,0:T(8,128)S(1)}) custom-call(bf16[128,2048]{1,0:T(8,128)(2,1)S(1)} %copy-done.5, bf16[128,2048]{1,0:T(8,128)(2,1)S(1)} %copy-done.6, bf16[1,2048]{1,0:T(2,128)(2,1)S(1)} %reshape.17.gain, f32[128,1]{1,0:T(8,128)S(1)} %get-tuple-element.55.inverse, ...), custom_call_target="tpu_custom_call" | custom-call | flops 1000 | bytes 1000 | tf_op jit(solution)/shard_map/finish_most/pallas_call | solution.py:372
  75.4 0.8 finish_rest.1
  (52 shorter events, 9.6 us)
Async XLA Ops:
  0.6 8.1 %collective-permute-start.5 = (bf16[128,8192]{1,0:T(8,128)(2,1)}, bf16[128,8192]{1,0:T(8,128)(2,1)S(1)}, u32[]{:S(2)}, u32[]{:S(2)}) collective-permute-start(bf16[128,8192]{1,0:T(8,128)(2,1)} %w_output.1), channel_id=1, source_target_pairs={{0,1},{1,0},{2,3},{3,2},{4,5},{5,4},{6,7},{7,6},{8,9},{9,8},{10,11... | collective-permute-start | bytes 6291464 | tf_op jit(solution)/shard_map/ppermute | solution.py:48
  1.1 18.4 %collective-permute-start = (bf16[128,2048]{1,0:T(8,128)(2,1)}, bf16[128,2048]{1,0:T(8,128)(2,1)S(1)}, u32[]{:S(2)}, u32[]{:S(2)}) collective-permute-start(bf16[128,2048]{1,0:T(8,128)(2,1)} %inputs.3), channel_id=1, source_target_pairs={{0,1},{1,0},{2,3},{3,2},{4,5},{5,4},{6,7},{7,6},{8,9},{9,8},{10,11... | collective-permute-start | bytes 1572872 | tf_op jit(solution)/shard_map/ppermute | solution.py:48
  1.2 26.7 %collective-permute-start.1 = (bf16[128,2048]{1,0:T(8,128)(2,1)}, bf16[128,2048]{1,0:T(8,128)(2,1)}, u32[]{:S(2)}, u32[]{:S(2)}) collective-permute-start(bf16[128,2048]{1,0:T(8,128)(2,1)} %inputs.3), channel_id=1, source_target_pairs={{0,2},{1,3},{2,0},{3,1},{4,6},{5,7},{6,4},{7,5},{8,10},{9,11},{10,... | collective-permute-start | bytes 1572872 | tf_op jit(solution)/shard_map/ppermute | solution.py:48
  4.2 23.8 %collective-permute-start.2 = (bf16[128,2048]{1,0:T(8,128)(2,1)}, bf16[128,2048]{1,0:T(8,128)(2,1)S(1)}, u32[]{:S(2)}, u32[]{:S(2)}) collective-permute-start(bf16[128,2048]{1,0:T(8,128)(2,1)} %cotangent.1), channel_id=1, source_target_pairs={{0,2},{1,3},{2,0},{3,1},{4,6},{5,7},{6,4},{7,5},{8,10},{9,11},{10,... | collective-permute-start | bytes 1572872 | tf_op jit(solution)/shard_map/ppermute | solution.py:48
  4.9 1.2 %collective-permute-start.3 = (bf16[1,2048]{1,0:T(2,128)(2,1)S(1)}, bf16[1,2048]{1,0:T(2,128)(2,1)S(1)}, u32[]{:S(2)}, u32[]{:S(2)}) collective-permute-start(bf16[1,2048]{1,0:T(2,128)(2,1)S(1)} %reshape.17.gain), channel_id=1, source_target_pairs={{0,1},{1,0},{2,3},{3,2},{4,5},{5,4},{6,7},{7,6},{8,9},{9,8},{10,11... | collective-permute-start | bytes 12296 | tf_op jit(solution)/shard_map/ppermute | solution.py:48
  6.1 21.9 %collective-permute-start.4 = (bf16[2,2048]{1,0:T(2,128)(2,1)S(1)}, bf16[2,2048]{1,0:T(2,128)(2,1)S(1)}, u32[]{:S(2)}, u32[]{:S(2)}) collective-permute-start(bf16[2,2048]{1,0:T(2,128)(2,1)S(1)} %pad_maximum_fusion.gain_chip), channel_id=1, source_target_pairs={{0,2},{1,3},{2,0},{3,1},{4,6},{5,7},{6,4},{7,5},{8,10},{9,11},{10,... | collective-permute-start | bytes 24584 | tf_op jit(solution)/shard_map/ppermute | solution.py:48
  8.7 1.6 %copy-start = (bf16[8192,128]{1,0:T(8,128)(2,1)S(1)}, bf16[8192,128]{1,0:T(8,128)(2,1)}, u32[]{:S(2)}) copy-start(bf16[8192,128]{1,0:T(8,128)(2,1)} %w_query.3) | copy-start | bytes 6291460
  10.3 1.6 %copy-start.2 = (bf16[8192,128]{1,0:T(8,128)(2,1)S(1)}, bf16[8192,128]{1,0:T(8,128)(2,1)}, u32[]{:S(2)}) copy-start(bf16[8192,128]{1,0:T(8,128)(2,1)} %w_key.3) | copy-start | bytes 6291460
  13.5 1.6 %copy-start.7 = (bf16[128,8192]{1,0:T(8,128)(2,1)S(1)}, bf16[128,8192]{1,0:T(8,128)(2,1)}, u32[]{:S(2)}) copy-start(bf16[128,8192]{1,0:T(8,128)(2,1)} %w_output.1) | copy-start | bytes 6291460
  17.0 2.5 %copy-start.5 = (bf16[128,2048]{1,0:T(8,128)(2,1)S(1)}, bf16[128,2048]{1,0:T(8,128)(2,1)}, u32[]{:S(2)}) copy-start(bf16[128,2048]{1,0:T(8,128)(2,1)} %inputs.3) | copy-start | bytes 1572868
  17.0 2.5 %copy-start.6 = (bf16[128,2048]{1,0:T(8,128)(2,1)S(1)}, bf16[128,2048]{1,0:T(8,128)(2,1)}, u32[]{:S(2)}) copy-start(bf16[128,2048]{1,0:T(8,128)(2,1)} %cotangent.1) | copy-start | bytes 1572868
  28.0 4.2 %collective-permute-start.6 = (bf16[128,2048]{1,0:T(8,128)(2,1)}, bf16[128,2048]{1,0:T(8,128)(2,1)S(1)}, u32[]{:S(2)}, u32[]{:S(2)}) collective-permute-start(bf16[128,2048]{1,0:T(8,128)(2,1)} %collective-permute-done.1.x2), channel_id=1, source_target_pairs={{0,1},{1,0},{2,3},{3,2},{4,5},{5,4},{6,7},{7,6},{8,9},{9,8},{10,11... | collective-permute-start | bytes 1572872 | tf_op jit(solution)/shard_map/ppermute | solution.py:48
  28.3 3.9 %collective-permute-start.7 = (f32[128,128]{1,0:T(8,128)S(1)}, f32[128,128]{1,0:T(8,128)S(1)}, u32[]{:S(2)}, u32[]{:S(2)}) collective-permute-start(f32[128,128]{1,0:T(8,128)S(1)} %add_grad.2), channel_id=1, source_target_pairs={{0,1},{1,0},{2,3},{3,2},{4,5},{5,4},{6,7},{7,6},{8,9},{9,8},{10,11... | collective-permute-start | bytes 196616 | tf_op jit(solution)/shard_map/ppermute | solution.py:48
  29.1 3.1 %copy-start.1 = (bf16[8192,128]{1,0:T(8,128)(2,1)S(1)}, bf16[8192,128]{1,0:T(8,128)(2,1)}, u32[]{:S(2)}) copy-start(bf16[8192,128]{1,0:T(8,128)(2,1)} %w_query.3) | copy-start | bytes 6291460
  29.1 3.1 %copy-start.3 = (bf16[8192,128]{1,0:T(8,128)(2,1)S(1)}, bf16[8192,128]{1,0:T(8,128)(2,1)}, u32[]{:S(2)}) copy-start(bf16[8192,128]{1,0:T(8,128)(2,1)} %w_key.3) | copy-start | bytes 6291460
  29.1 30.1 %collective-permute-start.8 = (bf16[256,2048]{1,0:T(8,128)(2,1)S(1)}, bf16[256,2048]{1,0:T(8,128)(2,1)S(1)}, u32[]{:S(2)}, u32[]{:S(2)}) collective-permute-start(bf16[256,2048]{1,0:T(8,128)(2,1)S(1)} %get-tuple-element.50), channel_id=1, source_target_pairs={{0,2},{1,3},{2,0},{3,1},{4,6},{5,7},{6,4},{7,5},{8,10},{9,11},{10,... | collective-permute-start | bytes 3145736 | tf_op jit(solution)/shard_map/ppermute | solution.py:48
  35.0 25.9 %collective-permute-start.13 = (bf16[384,4096]{1,0:T(8,128)(2,1)S(1)}, bf16[384,4096]{1,0:T(8,128)(2,1)S(1)}, u32[]{:S(2)}, u32[]{:S(2)}) collective-permute-start(bf16[384,4096]{1,0:T(8,128)(2,1)S(1)} %get-tuple-element.59), channel_id=1, source_target_pairs={{0,1},{1,0},{2,3},{3,2},{4,5},{5,4},{6,7},{7,6},{8,9},{9,8},{10,11... | collective-permute-start | bytes 9437192 | tf_op jit(solution)/shard_map/ppermute | solution.py:48
  59.5 1.4 %collective-permute-start.12 = (bf16[128,384]{1,0:T(8,128)(2,1)S(1)}, bf16[128,384]{1,0:T(8,128)(2,1)S(1)}, u32[]{:S(2)}, u32[]{:S(2)}) collective-permute-start(bf16[128,384]{1,0:T(8,128)(2,1)S(1)} %get-tuple-element.62.own), channel_id=1, source_target_pairs={{0,1},{1,0},{2,3},{3,2},{4,5},{5,4},{6,7},{7,6},{8,9},{9,8},{10,11... | collective-permute-start | bytes 294920 | tf_op jit(solution)/shard_map/ppermute | solution.py:48
  59.6 4.5 %collective-permute-start.10 = (bf16[128,256]{1,0:T(8,128)(2,1)S(1)}, bf16[128,256]{1,0:T(8,128)(2,1)S(1)}, u32[]{:S(2)}, u32[]{:S(2)}) collective-permute-start(bf16[128,256]{1,0:T(8,128)(2,1)S(1)} %get-tuple-element.53.own), channel_id=1, source_target_pairs={{0,2},{1,3},{2,0},{3,1},{4,6},{5,7},{6,4},{7,5},{8,10},{9,11},{10,... | collective-permute-start | bytes 196616 | tf_op jit(solution)/shard_map/ppermute | solution.py:48
  61.3 12.0 %collective-permute-start.14 = (bf16[128,1024]{1,0:T(8,128)(2,1)S(1)}, bf16[128,1024]{1,0:T(8,128)(2,1)S(1)}, u32[]{:S(2)}, u32[]{:S(2)}) collective-permute-start(bf16[128,1024]{1,0:T(8,128)(2,1)S(1)} %spread_far.3), channel_id=1, source_target_pairs={{0,2},{1,3},{2,0},{3,1},{4,6},{5,7},{6,4},{7,5},{8,10},{9,11},{10,... | collective-permute-start | bytes 786440 | tf_op jit(solution)/shard_map/ppermute | solution.py:48
  64.4 8.9 %collective-permute-start.15 = (bf16[128,512]{1,0:T(8,128)(2,1)S(1)}, bf16[128,512]{1,0:T(8,128)(2,1)S(1)}, u32[]{:S(2)}, u32[]{:S(2)}) collective-permute-start(bf16[128,512]{1,0:T(8,128)(2,1)S(1)} %spread_far.4), channel_id=1, source_target_pairs={{0,2},{1,3},{2,0},{3,1},{4,6},{5,7},{6,4},{7,5},{8,10},{9,11},{10,... | collective-permute-start | bytes 393224 | tf_op jit(solution)/shard_map/ppermute | solution.py:48
  65.8 9.5 %collective-permute-start.16 = (bf16[128,512]{1,0:T(8,128)(2,1)S(1)}, bf16[128,512]{1,0:T(8,128)(2,1)S(1)}, u32[]{:S(2)}, u32[]{:S(2)}) collective-permute-start(bf16[128,512]{1,0:T(8,128)(2,1)S(1)} %spread_far.5), channel_id=1, source_target_pairs={{0,2},{1,3},{2,0},{3,1},{4,6},{5,7},{6,4},{7,5},{8,10},{9,11},{10,... | collective-permute-start | bytes 393224 | tf_op jit(solution)/shard_map/ppermute | solution.py:48
  66.9 1.3 %collective-permute-start.9 = (bf16[128,256]{1,0:T(8,128)(2,1)S(1)}, bf16[128,256]{1,0:T(8,128)(2,1)S(1)}, u32[]{:S(2)}, u32[]{:S(2)}) collective-permute-start(bf16[128,256]{1,0:T(8,128)(2,1)S(1)} %get-tuple-element.53.own), channel_id=1, source_target_pairs={{0,1},{1,0},{2,3},{3,2},{4,5},{5,4},{6,7},{7,6},{8,9},{9,8},{10,11... | collective-permute-start | bytes 196616 | tf_op jit(solution)/shard_map/ppermute | solution.py:48
  66.9 1.4 %collective-permute-start.11 = (bf16[128,256]{1,0:T(8,128)(2,1)S(1)}, bf16[128,256]{1,0:T(8,128)(2,1)S(1)}, u32[]{:S(2)}, u32[]{:S(2)}) collective-permute-start(bf16[128,256]{1,0:T(8,128)(2,1)S(1)} %collective-permute-done.10.far), channel_id=1, source_target_pairs={{0,1},{1,0},{2,3},{3,2},{4,5},{5,4},{6,7},{7,6},{8,9},{9,8},{10,11... | collective-permute-start | bytes 196616 | tf_op jit(solution)/shard_map/ppermute | solution.py:48
  (4 other events, 3.6 us)

commit v17 on v16

--- a/solution.py
+++ b/solution.py
@@ -16,7 +16,7 @@
 VMEM = pl.BlockSpec(memory_space=pltpu.VMEM)
 SMEM = pl.BlockSpec(memory_space=pltpu.SMEM)
 TILE = 512
-SQUARES_FLOPS = 4000000000
+OWN_FLOPS = 4000000000
 HOME_FLOPS = 24000000000
 
 
@@ -142,19 +142,9 @@
 
 def add_grad(half, c2, there_turned, part):
     out = shape(jnp.float32, part.shape[0], part.shape[1] // 2)
-    return call(add_grad_kernel(half), "add_grad", out, (c2, there_turned, part), first=VMEM)
-
-
-def add_squares_kernel(x2, squares_in, squares):
-    squares[...] = squares_in[...] + sum_squares(x2)
-
-
-def add_squares(x2, squares):
-    out = shape(jnp.float32, *squares.shape)
-    operands = (x2, squares)
-    return call(
-        add_squares_kernel, "add_squares", out, operands, first=VMEM, flops=SQUARES_FLOPS
-    )
+    flops = 1000 if half else OWN_FLOPS
+    operands = (c2, there_turned, part)
+    return call(add_grad_kernel(half), "add_grad", out, operands, first=VMEM, flops=flops)
 
 
 def project_kernel(
@@ -179,7 +169,7 @@
 ):
     blocks = (x0, x1, x2, x3)
     width = x0.shape[1]
-    mean = (squares[...] + sum_squares(x3)) / (width * len(blocks))
+    mean = (squares[...] + sum_squares(x2) + sum_squares(x3)) / (width * len(blocks))
     inverse_rms = lax.rsqrt(mean + EPSILON)
     inverse[...] = inverse_rms
     head_grad = (own_part[...] + got_part[...]).astype(jnp.bfloat16)
@@ -441,7 +431,7 @@
     near_part = add_grad(1, c2, there_turned, part)
     got_part = swap(near_part, 1, tensor)
     own_part = add_grad(0, c2, there_turned, after(part, near_part))
-    squares = add_squares(x2, after(squares, near_part, own_part))
+    squares = after(squares, own_part)
     home, inverse_rms, bucket = project(
         order,
         (inputs, x1, x2, x3),

time: 76.6 us -> 77 us (level)
    pallas_call x9 -> x8, Pallas kernels: 10.2 us -> 10.7 us  [call(): pl.pallas_call(kernel, out_shape=shapes, in_specs=[first] + [rest] * (len...]
  transfers between devices with their start and end apart: 17 -> 17, of which waited for: 8 -> 8; matrix products, arithmetic and copies ran while one was open for 1% -> 1% of each run, Pallas kernels for 17% -> 18%
where the time goes in v17:
time: 77 us; the launch traced here: 76.5 us
  blocking collectives  23.1 us (30%)
  waiting for transfers between devices  15.7 us (20%)
  Pallas kernels  14.5 us (19%)
  starting transfers between devices  13.4 us (17%)
  local copies, waits for them, and re-layouts  9.03 us (12%)
  between operations  0.82 us (1%)
    all_to_all x2, blocking collectives, move(): return lax.all_to_all(bucket, 'dp', split_axis=0, concat_axis=0, tiled=True)  23.1 us
    ppermute x17, waiting for transfers between devices, swap(): return lax.ppermute(array, 'tensor', [(i, i ^ mask) for i in range(count)])  15.7 us
    ppermute x17, starting transfers between devices, swap(): return lax.ppermute(array, 'tensor', [(i, i ^ mask) for i in range(count)])  13.4 us
    pallas_call x8, Pallas kernels, call(): pl.pallas_call(kernel, out_shape=shapes, in_specs=[first] + [rest] * (len...  10.7 us
    unnamed x22, local copies, waits for them, and re-layouts  8.34 us
    pallas_call x4, Pallas kernels, spread(): pl.pallas_call(spread_kernel(first), out_shape=shape(dtype, own.shape[0],...  1.76 us
  transfers between devices with their start and end apart: 17, of which 8 were waited for; matrix products, arithmetic and copies ran while one was open for 1% of the time, Pallas kernels for 18%

profile of v17, /device:TPU:0, one launch (start us, length us, event | category | flops | bytes accessed | tf_op | source)
XLA Modules:
  0.0 76.5 jit_solution(18428016823185693829)
XLA Ops:
  1.2 2.9 %collective-permute-start.1 = (bf16[128,2048]{1,0:T(8,128)(2,1)}, bf16[128,2048]{1,0:T(8,128)(2,1)S(1)}, u32[]{:S(2)}, u32[]{:S(2)}) collective-permute-start(bf16[128,2048]{1,0:T(8,128)(2,1)} %inputs.3), channel_id=1, source_target_pairs={{0,2},{1,3},{2,0},{3,1},{4,6},{5,7},{6,4},{7,5},{8,10},{9,11},{10,... | collective-permute-start | bytes 1572872 | tf_op jit(solution)/shard_map/ppermute | solution.py:48
  4.9 1.2 %collective-permute-done.3 = bf16[1,2048]{1,0:T(2,128)(2,1)S(1)} collective-permute-done((bf16[1,2048]{1,0:T(2,128)(2,1)S(1)}, bf16[1,2048]{1,0:T(2,128)(2,1)S(1)}, u32[]{:S(2)}, u32[]{:S(2)}) %collective-permute-start.3) | collective-permute-done | bytes 4128 | tf_op jit(solution)/shard_map/ppermute | solution.py:48
  6.1 2.6 %collective-permute-start.4 = (bf16[2,2048]{1,0:T(2,128)(2,1)S(1)}, bf16[2,2048]{1,0:T(2,128)(2,1)S(1)}, u32[]{:S(2)}, u32[]{:S(2)}) collective-permute-start(bf16[2,2048]{1,0:T(2,128)(2,1)S(1)} %pad_maximum_fusion.gain_chip), channel_id=1, source_target_pairs={{0,2},{1,3},{2,0},{3,1},{4,6},{5,7},{6,4},{7,5},{8,10},{9,11},{10,... | collective-permute-start | bytes 24584 | tf_op jit(solution)/shard_map/ppermute | solution.py:48
  8.7 1.6 %copy-done = bf16[8192,128]{1,0:T(8,128)(2,1)S(1)} copy-done((bf16[8192,128]{1,0:T(8,128)(2,1)S(1)}, bf16[8192,128]{1,0:T(8,128)(2,1)}, u32[]{:S(2)}) %copy-start) | copy-done | bytes 2097176
  10.3 1.6 %copy-done.2 = bf16[8192,128]{1,0:T(8,128)(2,1)S(1)} copy-done((bf16[8192,128]{1,0:T(8,128)(2,1)S(1)}, bf16[8192,128]{1,0:T(8,128)(2,1)}, u32[]{:S(2)}) %copy-start.2) | copy-done | bytes 2097176
  11.9 1.6 %copy-done.4 = bf16[8192,128]{1,0:T(8,128)(2,1)S(1)} copy-done((bf16[8192,128]{1,0:T(8,128)(2,1)S(1)}, bf16[8192,128]{1,0:T(8,128)(2,1)}, u32[]{:S(2)}) %copy-start.4) | copy-done | bytes 2097176
  13.5 1.6 %copy-done.7 = bf16[128,8192]{1,0:T(8,128)(2,1)S(1)} copy-done((bf16[128,8192]{1,0:T(8,128)(2,1)S(1)}, bf16[128,8192]{1,0:T(8,128)(2,1)}, u32[]{:S(2)}) %copy-start.7) | copy-done | bytes 2097176
  17.0 2.5 %prepare.1 = (bf16[384,4096]{1,0:T(8,128)(2,1)S(1)}, bf16[384,4096]{1,0:T(8,128)(2,1)S(1)}, bf16[256,2048]{1,0:T(8,128)(2,1)S(1)}, bf16[256,2048]{1,0:T(8,128)(2...) custom-call(s32[4]{0:T(128)S(1)} %iota_xor_fusion.order, ...), custom_call_target="tpu_custom_call" | custom-call | flops 1000 | bytes 1000 | tf_op jit(solution)/shard_map/prepare/pallas_call | solution.py:30
  20.1 7.8 %collective-permute-done.4.gain_far = bf16[2,2048]{1,0:T(2,128)(2,1)S(1)} collective-permute-done((bf16[2,2048]{1,0:T(2,128)(2,1)S(1)}, bf16[2,2048]{1,0:T(2,128)(2,1)S(1)}, u32[]{:S(2)}, u32[]{:S(2)}) %collective-permute-start.4) | collective-permute-done | bytes 8224 | tf_op jit(solution)/shard_map/ppermute | solution.py:48
  28.0 1.3 %add_grad.2 = f32[128,128]{1,0:T(8,128)S(1)} custom-call(bf16[128,2048]{1,0:T(8,128)(2,1)} %collective-permute-done.2.c2, bf16[2048,256]{1,0:T(8,128)(2,1)S(1)} %get-tuple-element.41.there_turned, f32[128,256]{1,0:T(8,128)S(1)} %get-tuple-element.43.part), custom_call_target="tpu_custom_call" | custom-call | flops 1000 | bytes 1000 | tf_op jit(solution)/shard_map/add_grad/pallas_call | solution.py:30
  29.9 1.7 %collective-permute-start.8 = (bf16[256,2048]{1,0:T(8,128)(2,1)S(1)}, bf16[256,2048]{1,0:T(8,128)(2,1)S(1)}, u32[]{:S(2)}, u32[]{:S(2)}) collective-permute-start(bf16[256,2048]{1,0:T(8,128)(2,1)S(1)} %get-tuple-element.50), channel_id=1, source_target_pairs={{0,2},{1,3},{2,0},{3,1},{4,6},{5,7},{6,4},{7,5},{8,10},{9,11},{10,... | collective-permute-start | bytes 3145736 | tf_op jit(solution)/shard_map/ppermute | solution.py:48
  31.6 1.3 %add_grad.3.own_part = f32[128,128]{1,0:T(8,128)S(1)} custom-call(bf16[128,2048]{1,0:T(8,128)(2,1)} %collective-permute-done.2.c2, bf16[2048,256]{1,0:T(8,128)(2,1)S(1)} %get-tuple-element.41.there_turned, f32[128,256]{1,0:T(8,128)S(1)} %get-tuple-element.43.part), custom_call_target="tpu_custom_call" | custom-call | flops 4000000000 | bytes 1000 | tf_op jit(solution)/shard_map/add_grad/pallas_call | solution.py:30
  33.0 2.3 %project.1 = (bf16[128,384]{1,0:T(8,128)(2,1)S(1)}, f32[128,1]{1,0:T(8,128)S(1)}, bf16[128,512]{1,0:T(8,128)(2,1)S(1)}) custom-call(s32[4]{0:T(128)S(1)} %iota_xor_fusion.order, bf16[128,2048]{1,0:T(8,128)(2,1)S(1)} %copy-done.5, bf16[128,2048]{1,0:T(8,128)(2,1)S(1)} %collective-permute-done.x1, bf16[128,2048]{1,0:T(8,128)(2,1)S(1)} %collective-permute-done.1.x2, ...), custom_call_target="tpu_custom_call" | custom-call | flops 1000 | bytes 1000 | tf_op jit(solution)/shard_map/project/pallas_call | solution.py:30
  35.4 13.2 %all_to_all.23 = bf16[8,16,512]{2,1,0:T(8,128)(2,1)S(1)} all-to-all(bf16[8,16,512]{2,1,0:T(8,128)(2,1)S(1)} %bitcast.8), channel_id=1, replica_groups=mesh['dp'=8,'tensor'=4] {'dp'}, dimensions={0} | all-to-all | bytes 262144 | tf_op jit(solution)/shard_map/all_to_all | solution.py:384
  48.7 1.1 %attend.1 = bf16[128,512]{1,0:T(8,128)(2,1)S(1)} custom-call(bf16[128,512]{1,0:T(8,128)(2,1)S(1)} %bitcast.6, s32[1,128]{1,0:T(1,128)S(1)} %get-tuple-element.47.receive, s32[1,128]{1,0:T(1,128)S(1)} %get-tuple-element.48.segments), custom_call_target="tpu_custom_call" | custom-call | flops 1000 | bytes 1000 | tf_op jit(solution)/shard_map/attend/pallas_call | solution.py:30
  49.8 9.9 %all_to_all.24 = bf16[8,16,512]{2,1,0:T(8,128)(2,1)S(1)} all-to-all(bf16[8,16,512]{2,1,0:T(8,128)(2,1)S(1)} %bitcast.7), channel_id=1, replica_groups=mesh['dp'=8,'tensor'=4] {'dp'}, dimensions={0} | all-to-all | bytes 262144 | tf_op jit(solution)/shard_map/all_to_all | solution.py:384
  60.0 1.1 %collective-permute-start.10 = (bf16[128,256]{1,0:T(8,128)(2,1)S(1)}, bf16[128,256]{1,0:T(8,128)(2,1)S(1)}, u32[]{:S(2)}, u32[]{:S(2)}) collective-permute-start(bf16[128,256]{1,0:T(8,128)(2,1)S(1)} %get-tuple-element.53.own), channel_id=1, source_target_pairs={{0,2},{1,3},{2,0},{3,1},{4,6},{5,7},{6,4},{7,5},{8,10},{9,11},{10,... | collective-permute-start | bytes 196616 | tf_op jit(solution)/shard_map/ppermute | solution.py:48
  61.7 1.1 %collective-permute-start.14 = (bf16[128,1024]{1,0:T(8,128)(2,1)S(1)}, bf16[128,1024]{1,0:T(8,128)(2,1)S(1)}, u32[]{:S(2)}, u32[]{:S(2)}) collective-permute-start(bf16[128,1024]{1,0:T(8,128)(2,1)S(1)} %spread_far.3), channel_id=1, source_target_pairs={{0,2},{1,3},{2,0},{3,1},{4,6},{5,7},{6,4},{7,5},{8,10},{9,11},{10,... | collective-permute-start | bytes 786440 | tf_op jit(solution)/shard_map/ppermute | solution.py:48
  62.8 1.7 %collective-permute-done.10.far = bf16[128,256]{1,0:T(8,128)(2,1)S(1)} collective-permute-done((bf16[128,256]{1,0:T(8,128)(2,1)S(1)}, bf16[128,256]{1,0:T(8,128)(2,1)S(1)}, u32[]{:S(2)}, u32[]{:S(2)}) %collective-permute-start.10) | collective-permute-done | bytes 65568 | tf_op jit(solution)/shard_map/ppermute | solution.py:48
  64.8 1.1 %collective-permute-start.15 = (bf16[128,512]{1,0:T(8,128)(2,1)S(1)}, bf16[128,512]{1,0:T(8,128)(2,1)S(1)}, u32[]{:S(2)}, u32[]{:S(2)}) collective-permute-start(bf16[128,512]{1,0:T(8,128)(2,1)S(1)} %spread_far.4), channel_id=1, source_target_pairs={{0,2},{1,3},{2,0},{3,1},{4,6},{5,7},{6,4},{7,5},{8,10},{9,11},{10,... | collective-permute-start | bytes 393224 | tf_op jit(solution)/shard_map/ppermute | solution.py:48
  66.2 1.1 %collective-permute-start.16 = (bf16[128,512]{1,0:T(8,128)(2,1)S(1)}, bf16[128,512]{1,0:T(8,128)(2,1)S(1)}, u32[]{:S(2)}, u32[]{:S(2)}) collective-permute-start(bf16[128,512]{1,0:T(8,128)(2,1)S(1)} %spread_far.5), channel_id=1, source_target_pairs={{0,2},{1,3},{2,0},{3,1},{4,6},{5,7},{6,4},{7,5},{8,10},{9,11},{10,... | collective-permute-start | bytes 393224 | tf_op jit(solution)/shard_map/ppermute | solution.py:48
  68.7 1.3 %finish_out.1 = bf16[128,2048]{1,0:T(8,128)(2,1)} custom-call(bf16[128,2048]{1,0:T(8,128)(2,1)S(1)} %copy-done.5, bf16[128,256]{1,0:T(8,128)(2,1)S(1)} %get-tuple-element.53.own, bf16[128,256]{1,0:T(8,128)(2,1)S(1)} %collective-permute-done.9.near, bf16[128,256]{1,0:T(8,128)(2,1)S(1)} %collective-permute-done.10.far, ...), custom_call_target="tpu_custom_call" | custom-call | flops 1000 | bytes 1000 | tf_op jit(solution)/shard_map/finish_out/pallas_call | solution.py:30
  70.6 3.1 %collective-permute-done.15.pieces_1_ = bf16[128,512]{1,0:T(8,128)(2,1)S(1)} collective-permute-done((bf16[128,512]{1,0:T(8,128)(2,1)S(1)}, bf16[128,512]{1,0:T(8,128)(2,1)S(1)}, u32[]{:S(2)}, u32[]{:S(2)}) %collective-permute-start.15) | collective-permute-done | bytes 131104 | tf_op jit(solution)/shard_map/ppermute | solution.py:48
  73.7 1.3 %finish_most.1 = (bf16[128,2048]{1,0:T(8,128)(2,1)}, f32[128,512]{1,0:T(8,128)S(1)}) custom-call(bf16[128,2048]{1,0:T(8,128)(2,1)S(1)} %copy-done.5, bf16[128,2048]{1,0:T(8,128)(2,1)S(1)} %copy-done.6, bf16[1,2048]{1,0:T(2,128)(2,1)S(1)} %reshape.17.gain, f32[128,1]{1,0:T(8,128)S(1)} %get-tuple-element.55.inverse, ...), custom_call_target="tpu_custom_call" | custom-call | flops 1000 | bytes 1000 | tf_op jit(solution)/shard_map/finish_most/pallas_call | solution.py:362
  (51 shorter events, 9.8 us)
Async XLA Ops:
  0.6 8.1 %collective-permute-start.5 = (bf16[128,8192]{1,0:T(8,128)(2,1)}, bf16[128,8192]{1,0:T(8,128)(2,1)S(1)}, u32[]{:S(2)}, u32[]{:S(2)}) collective-permute-start(bf16[128,8192]{1,0:T(8,128)(2,1)} %w_output.1), channel_id=1, source_target_pairs={{0,1},{1,0},{2,3},{3,2},{4,5},{5,4},{6,7},{7,6},{8,9},{9,8},{10,11... | collective-permute-start | bytes 6291464 | tf_op jit(solution)/shard_map/ppermute | solution.py:48
  1.1 18.4 %collective-permute-start = (bf16[128,2048]{1,0:T(8,128)(2,1)}, bf16[128,2048]{1,0:T(8,128)(2,1)S(1)}, u32[]{:S(2)}, u32[]{:S(2)}) collective-permute-start(bf16[128,2048]{1,0:T(8,128)(2,1)} %inputs.3), channel_id=1, source_target_pairs={{0,1},{1,0},{2,3},{3,2},{4,5},{5,4},{6,7},{7,6},{8,9},{9,8},{10,11... | collective-permute-start | bytes 1572872 | tf_op jit(solution)/shard_map/ppermute | solution.py:48
  1.2 26.8 %collective-permute-start.1 = (bf16[128,2048]{1,0:T(8,128)(2,1)}, bf16[128,2048]{1,0:T(8,128)(2,1)S(1)}, u32[]{:S(2)}, u32[]{:S(2)}) collective-permute-start(bf16[128,2048]{1,0:T(8,128)(2,1)} %inputs.3), channel_id=1, source_target_pairs={{0,2},{1,3},{2,0},{3,1},{4,6},{5,7},{6,4},{7,5},{8,10},{9,11},{10,... | collective-permute-start | bytes 1572872 | tf_op jit(solution)/shard_map/ppermute | solution.py:48
  4.2 23.8 %collective-permute-start.2 = (bf16[128,2048]{1,0:T(8,128)(2,1)}, bf16[128,2048]{1,0:T(8,128)(2,1)}, u32[]{:S(2)}, u32[]{:S(2)}) collective-permute-start(bf16[128,2048]{1,0:T(8,128)(2,1)} %cotangent.1), channel_id=1, source_target_pairs={{0,2},{1,3},{2,0},{3,1},{4,6},{5,7},{6,4},{7,5},{8,10},{9,11},{10,... | collective-permute-start | bytes 1572872 | tf_op jit(solution)/shard_map/ppermute | solution.py:48
  4.9 1.2 %collective-permute-start.3 = (bf16[1,2048]{1,0:T(2,128)(2,1)S(1)}, bf16[1,2048]{1,0:T(2,128)(2,1)S(1)}, u32[]{:S(2)}, u32[]{:S(2)}) collective-permute-start(bf16[1,2048]{1,0:T(2,128)(2,1)S(1)} %reshape.17.gain), channel_id=1, source_target_pairs={{0,1},{1,0},{2,3},{3,2},{4,5},{5,4},{6,7},{7,6},{8,9},{9,8},{10,11... | collective-permute-start | bytes 12296 | tf_op jit(solution)/shard_map/ppermute | solution.py:48
  6.1 21.9 %collective-permute-start.4 = (bf16[2,2048]{1,0:T(2,128)(2,1)S(1)}, bf16[2,2048]{1,0:T(2,128)(2,1)S(1)}, u32[]{:S(2)}, u32[]{:S(2)}) collective-permute-start(bf16[2,2048]{1,0:T(2,128)(2,1)S(1)} %pad_maximum_fusion.gain_chip), channel_id=1, source_target_pairs={{0,2},{1,3},{2,0},{3,1},{4,6},{5,7},{6,4},{7,5},{8,10},{9,11},{10,... | collective-permute-start | bytes 24584 | tf_op jit(solution)/shard_map/ppermute | solution.py:48
  8.7 1.6 %copy-start = (bf16[8192,128]{1,0:T(8,128)(2,1)S(1)}, bf16[8192,128]{1,0:T(8,128)(2,1)}, u32[]{:S(2)}) copy-start(bf16[8192,128]{1,0:T(8,128)(2,1)} %w_query.3) | copy-start | bytes 6291460
  10.3 1.6 %copy-start.2 = (bf16[8192,128]{1,0:T(8,128)(2,1)S(1)}, bf16[8192,128]{1,0:T(8,128)(2,1)}, u32[]{:S(2)}) copy-start(bf16[8192,128]{1,0:T(8,128)(2,1)} %w_key.3) | copy-start | bytes 6291460
  11.9 1.6 %copy-start.4 = (bf16[8192,128]{1,0:T(8,128)(2,1)S(1)}, bf16[8192,128]{1,0:T(8,128)(2,1)}, u32[]{:S(2)}) copy-start(bf16[8192,128]{1,0:T(8,128)(2,1)} %w_value.3) | copy-start | bytes 6291460
  17.0 2.5 %copy-start.5 = (bf16[128,2048]{1,0:T(8,128)(2,1)S(1)}, bf16[128,2048]{1,0:T(8,128)(2,1)}, u32[]{:S(2)}) copy-start(bf16[128,2048]{1,0:T(8,128)(2,1)} %inputs.3) | copy-start | bytes 1572868
  17.0 2.5 %copy-start.6 = (bf16[128,2048]{1,0:T(8,128)(2,1)S(1)}, bf16[128,2048]{1,0:T(8,128)(2,1)}, u32[]{:S(2)}) copy-start(bf16[128,2048]{1,0:T(8,128)(2,1)} %cotangent.1) | copy-start | bytes 1572868
  28.0 5.0 %collective-permute-start.6 = (bf16[128,2048]{1,0:T(8,128)(2,1)S(1)}, bf16[128,2048]{1,0:T(8,128)(2,1)S(1)}, u32[]{:S(2)}, u32[]{:S(2)}) collective-permute-start(bf16[128,2048]{1,0:T(8,128)(2,1)S(1)} %collective-permute-done.1.x2), channel_id=1, source_target_pairs={{0,1},{1,0},{2,3},{3,2},{4,5},{5,4},{6,7},{7,6},{8,9},{9,8},{10,11... | collective-permute-start | bytes 1572872 | tf_op jit(solution)/shard_map/ppermute | solution.py:48
  29.3 3.6 %collective-permute-start.7 = (f32[128,128]{1,0:T(8,128)S(1)}, f32[128,128]{1,0:T(8,128)S(1)}, u32[]{:S(2)}, u32[]{:S(2)}) collective-permute-start(f32[128,128]{1,0:T(8,128)S(1)} %add_grad.2), channel_id=1, source_target_pairs={{0,1},{1,0},{2,3},{3,2},{4,5},{5,4},{6,7},{7,6},{8,9},{9,8},{10,11... | collective-permute-start | bytes 196616 | tf_op jit(solution)/shard_map/ppermute | solution.py:48
  29.9 3.1 %copy-start.1 = (bf16[8192,128]{1,0:T(8,128)(2,1)S(1)}, bf16[8192,128]{1,0:T(8,128)(2,1)}, u32[]{:S(2)}) copy-start(bf16[8192,128]{1,0:T(8,128)(2,1)} %w_query.3) | copy-start | bytes 6291460
  29.9 3.1 %copy-start.3 = (bf16[8192,128]{1,0:T(8,128)(2,1)S(1)}, bf16[8192,128]{1,0:T(8,128)(2,1)}, u32[]{:S(2)}) copy-start(bf16[8192,128]{1,0:T(8,128)(2,1)} %w_key.3) | copy-start | bytes 6291460
  29.9 29.7 %collective-permute-start.8 = (bf16[256,2048]{1,0:T(8,128)(2,1)S(1)}, bf16[256,2048]{1,0:T(8,128)(2,1)S(1)}, u32[]{:S(2)}, u32[]{:S(2)}) collective-permute-start(bf16[256,2048]{1,0:T(8,128)(2,1)S(1)} %get-tuple-element.50), channel_id=1, source_target_pairs={{0,2},{1,3},{2,0},{3,1},{4,6},{5,7},{6,4},{7,5},{8,10},{9,11},{10,... | collective-permute-start | bytes 3145736 | tf_op jit(solution)/shard_map/ppermute | solution.py:48
  35.4 25.9 %collective-permute-start.13 = (bf16[384,4096]{1,0:T(8,128)(2,1)S(1)}, bf16[384,4096]{1,0:T(8,128)(2,1)S(1)}, u32[]{:S(2)}, u32[]{:S(2)}) collective-permute-start(bf16[384,4096]{1,0:T(8,128)(2,1)S(1)} %get-tuple-element.59), channel_id=1, source_target_pairs={{0,1},{1,0},{2,3},{3,2},{4,5},{5,4},{6,7},{7,6},{8,9},{9,8},{10,11... | collective-permute-start | bytes 9437192 | tf_op jit(solution)/shard_map/ppermute | solution.py:48
  59.9 1.4 %collective-permute-start.12 = (bf16[128,384]{1,0:T(8,128)(2,1)S(1)}, bf16[128,384]{1,0:T(8,128)(2,1)S(1)}, u32[]{:S(2)}, u32[]{:S(2)}) collective-permute-start(bf16[128,384]{1,0:T(8,128)(2,1)S(1)} %get-tuple-element.62.own), channel_id=1, source_target_pairs={{0,1},{1,0},{2,3},{3,2},{4,5},{5,4},{6,7},{7,6},{8,9},{9,8},{10,11... | collective-permute-start | bytes 294920 | tf_op jit(solution)/shard_map/ppermute | solution.py:48
  60.0 4.5 %collective-permute-start.10 = (bf16[128,256]{1,0:T(8,128)(2,1)S(1)}, bf16[128,256]{1,0:T(8,128)(2,1)S(1)}, u32[]{:S(2)}, u32[]{:S(2)}) collective-permute-start(bf16[128,256]{1,0:T(8,128)(2,1)S(1)} %get-tuple-element.53.own), channel_id=1, source_target_pairs={{0,2},{1,3},{2,0},{3,1},{4,6},{5,7},{6,4},{7,5},{8,10},{9,11},{10,... | collective-permute-start | bytes 196616 | tf_op jit(solution)/shard_map/ppermute | solution.py:48
  61.7 12.0 %collective-permute-start.14 = (bf16[128,1024]{1,0:T(8,128)(2,1)S(1)}, bf16[128,1024]{1,0:T(8,128)(2,1)S(1)}, u32[]{:S(2)}, u32[]{:S(2)}) collective-permute-start(bf16[128,1024]{1,0:T(8,128)(2,1)S(1)} %spread_far.3), channel_id=1, source_target_pairs={{0,2},{1,3},{2,0},{3,1},{4,6},{5,7},{6,4},{7,5},{8,10},{9,11},{10,... | collective-permute-start | bytes 786440 | tf_op jit(solution)/shard_map/ppermute | solution.py:48
  64.8 8.9 %collective-permute-start.15 = (bf16[128,512]{1,0:T(8,128)(2,1)S(1)}, bf16[128,512]{1,0:T(8,128)(2,1)S(1)}, u32[]{:S(2)}, u32[]{:S(2)}) collective-permute-start(bf16[128,512]{1,0:T(8,128)(2,1)S(1)} %spread_far.4), channel_id=1, source_target_pairs={{0,2},{1,3},{2,0},{3,1},{4,6},{5,7},{6,4},{7,5},{8,10},{9,11},{10,... | collective-permute-start | bytes 393224 | tf_op jit(solution)/shard_map/ppermute | solution.py:48
  66.2 9.6 %collective-permute-start.16 = (bf16[128,512]{1,0:T(8,128)(2,1)S(1)}, bf16[128,512]{1,0:T(8,128)(2,1)S(1)}, u32[]{:S(2)}, u32[]{:S(2)}) collective-permute-start(bf16[128,512]{1,0:T(8,128)(2,1)S(1)} %spread_far.5), channel_id=1, source_target_pairs={{0,2},{1,3},{2,0},{3,1},{4,6},{5,7},{6,4},{7,5},{8,10},{9,11},{10,... | collective-permute-start | bytes 393224 | tf_op jit(solution)/shard_map/ppermute | solution.py:48
  67.3 1.3 %collective-permute-start.9 = (bf16[128,256]{1,0:T(8,128)(2,1)S(1)}, bf16[128,256]{1,0:T(8,128)(2,1)S(1)}, u32[]{:S(2)}, u32[]{:S(2)}) collective-permute-start(bf16[128,256]{1,0:T(8,128)(2,1)S(1)} %get-tuple-element.53.own), channel_id=1, source_target_pairs={{0,1},{1,0},{2,3},{3,2},{4,5},{5,4},{6,7},{7,6},{8,9},{9,8},{10,11... | collective-permute-start | bytes 196616 | tf_op jit(solution)/shard_map/ppermute | solution.py:48
  67.3 1.4 %collective-permute-start.11 = (bf16[128,256]{1,0:T(8,128)(2,1)S(1)}, bf16[128,256]{1,0:T(8,128)(2,1)S(1)}, u32[]{:S(2)}, u32[]{:S(2)}) collective-permute-start(bf16[128,256]{1,0:T(8,128)(2,1)S(1)} %collective-permute-done.10.far), channel_id=1, source_target_pairs={{0,1},{1,0},{2,3},{3,2},{4,5},{5,4},{6,7},{7,6},{8,9},{9,8},{10,11... | collective-permute-start | bytes 196616 | tf_op jit(solution)/shard_map/ppermute | solution.py:48
  (4 other events, 3.6 us)

commit v18 on v16

--- a/solution.py
+++ b/solution.py
@@ -12,7 +12,7 @@
 SCALING = 1.0 / math.sqrt(HEAD_DIM)
 CONTRACT_LAST = (((1,), (1,)), ((), ()))
 CONTRACT_FIRST = (((0,), (0,)), ((), ()))
-VMEM_LIMIT = 3 * 1024 * 1024
+VMEM_LIMIT = 5 * 1024 * 1024
 VMEM = pl.BlockSpec(memory_space=pltpu.VMEM)
 SMEM = pl.BlockSpec(memory_space=pltpu.SMEM)
 TILE = 512

time: 76.6 us -> 76.6 us (level)
  no operation moved by 1% of the time
where the time goes in v18:
time: 76.6 us; the launch traced here: 76.1 us
  blocking collectives  23.1 us (30%)
  waiting for transfers between devices  15.5 us (20%)
  Pallas kernels  14 us (18%)
  starting transfers between devices  13.6 us (18%)
  local copies, waits for them, and re-layouts  9.04 us (12%)
  between operations  0.82 us (1%)
    all_to_all x2, blocking collectives, move(): return lax.all_to_all(bucket, 'dp', split_axis=0, concat_axis=0, tiled=True)  23.1 us
    ppermute x17, waiting for transfers between devices, swap(): return lax.ppermute(array, 'tensor', [(i, i ^ mask) for i in range(count)])  15.5 us
    ppermute x17, starting transfers between devices, swap(): return lax.ppermute(array, 'tensor', [(i, i ^ mask) for i in range(count)])  13.6 us
    pallas_call x9, Pallas kernels, call(): pl.pallas_call(kernel, out_shape=shapes, in_specs=[first] + [rest] * (len...  10.2 us
    unnamed x22, local copies, waits for them, and re-layouts  8.35 us
    pallas_call x4, Pallas kernels, spread(): pl.pallas_call(spread_kernel(first), out_shape=shape(dtype, own.shape[0],...  1.77 us
  transfers between devices with their start and end apart: 17, of which 8 were waited for; matrix products, arithmetic and copies ran while one was open for 1% of the time, Pallas kernels for 17%

profile of v18, /device:TPU:0, one launch (start us, length us, event | category | flops | bytes accessed | tf_op | source)
XLA Modules:
  0.0 76.1 jit_solution(3890938843134285634)
XLA Ops:
  1.2 2.9 %collective-permute-start.1 = (bf16[128,2048]{1,0:T(8,128)(2,1)}, bf16[128,2048]{1,0:T(8,128)(2,1)}, u32[]{:S(2)}, u32[]{:S(2)}) collective-permute-start(bf16[128,2048]{1,0:T(8,128)(2,1)} %inputs.3), channel_id=1, source_target_pairs={{0,2},{1,3},{2,0},{3,1},{4,6},{5,7},{6,4},{7,5},{8,10},{9,11},{10,... | collective-permute-start | bytes 1572872 | tf_op jit(solution)/shard_map/ppermute | solution.py:48
  4.9 1.2 %collective-permute-done.3 = bf16[1,2048]{1,0:T(2,128)(2,1)S(1)} collective-permute-done((bf16[1,2048]{1,0:T(2,128)(2,1)S(1)}, bf16[1,2048]{1,0:T(2,128)(2,1)S(1)}, u32[]{:S(2)}, u32[]{:S(2)}) %collective-permute-start.3) | collective-permute-done | bytes 4128 | tf_op jit(solution)/shard_map/ppermute | solution.py:48
  6.1 2.6 %collective-permute-start.4 = (bf16[2,2048]{1,0:T(2,128)(2,1)S(1)}, bf16[2,2048]{1,0:T(2,128)(2,1)S(1)}, u32[]{:S(2)}, u32[]{:S(2)}) collective-permute-start(bf16[2,2048]{1,0:T(2,128)(2,1)S(1)} %pad_maximum_fusion.gain_chip), channel_id=1, source_target_pairs={{0,2},{1,3},{2,0},{3,1},{4,6},{5,7},{6,4},{7,5},{8,10},{9,11},{10,... | collective-permute-start | bytes 24584 | tf_op jit(solution)/shard_map/ppermute | solution.py:48
  8.7 1.6 %copy-done = bf16[8192,128]{1,0:T(8,128)(2,1)S(1)} copy-done((bf16[8192,128]{1,0:T(8,128)(2,1)S(1)}, bf16[8192,128]{1,0:T(8,128)(2,1)}, u32[]{:S(2)}) %copy-start) | copy-done | bytes 2097176
  10.3 1.6 %copy-done.2 = bf16[8192,128]{1,0:T(8,128)(2,1)S(1)} copy-done((bf16[8192,128]{1,0:T(8,128)(2,1)S(1)}, bf16[8192,128]{1,0:T(8,128)(2,1)}, u32[]{:S(2)}) %copy-start.2) | copy-done | bytes 2097176
  11.9 1.6 %copy-done.4 = bf16[8192,128]{1,0:T(8,128)(2,1)S(1)} copy-done((bf16[8192,128]{1,0:T(8,128)(2,1)S(1)}, bf16[8192,128]{1,0:T(8,128)(2,1)}, u32[]{:S(2)}) %copy-start.4) | copy-done | bytes 2097176
  13.5 1.6 %copy-done.7 = bf16[128,8192]{1,0:T(8,128)(2,1)S(1)} copy-done((bf16[128,8192]{1,0:T(8,128)(2,1)S(1)}, bf16[128,8192]{1,0:T(8,128)(2,1)}, u32[]{:S(2)}) %copy-start.7) | copy-done | bytes 2097176
  17.0 2.5 %prepare.1 = (bf16[384,4096]{1,0:T(8,128)(2,1)S(1)}, bf16[384,4096]{1,0:T(8,128)(2,1)S(1)}, bf16[256,2048]{1,0:T(8,128)(2,1)S(1)}, bf16[256,2048]{1,0:T(8,128)(2...) custom-call(s32[4]{0:T(128)S(1)} %iota_xor_fusion.order, ...), custom_call_target="tpu_custom_call" | custom-call | flops 1000 | bytes 1000 | tf_op jit(solution)/shard_map/prepare/pallas_call | solution.py:30
  20.1 7.8 %collective-permute-done.4.gain_far = bf16[2,2048]{1,0:T(2,128)(2,1)S(1)} collective-permute-done((bf16[2,2048]{1,0:T(2,128)(2,1)S(1)}, bf16[2,2048]{1,0:T(2,128)(2,1)S(1)}, u32[]{:S(2)}, u32[]{:S(2)}) %collective-permute-start.4) | collective-permute-done | bytes 8224 | tf_op jit(solution)/shard_map/ppermute | solution.py:48
  29.1 1.8 %collective-permute-start.8 = (bf16[256,2048]{1,0:T(8,128)(2,1)S(1)}, bf16[256,2048]{1,0:T(8,128)(2,1)S(1)}, u32[]{:S(2)}, u32[]{:S(2)}) collective-permute-start(bf16[256,2048]{1,0:T(8,128)(2,1)S(1)} %get-tuple-element.50), channel_id=1, source_target_pairs={{0,2},{1,3},{2,0},{3,1},{4,6},{5,7},{6,4},{7,5},{8,10},{9,11},{10,... | collective-permute-start | bytes 3145736 | tf_op jit(solution)/shard_map/ppermute | solution.py:48
  31.0 1.2 %add_squares.1.squares = f32[128,1]{1,0:T(8,128)S(1)} custom-call(bf16[128,2048]{1,0:T(8,128)(2,1)} %collective-permute-done.1.x2, f32[128,1]{1,0:T(8,128)S(1)} %get-tuple-element.44.squares_in), custom_call_target="tpu_custom_call" | custom-call | flops 4000000000 | bytes 1000 | tf_op jit(solution)/shard_map/add_squares/pallas_call | solution.py:30
  32.2 2.8 %project.1 = (bf16[128,384]{1,0:T(8,128)(2,1)S(1)}, f32[128,1]{1,0:T(8,128)S(1)}, bf16[128,512]{1,0:T(8,128)(2,1)S(1)}) custom-call(s32[4]{0:T(128)S(1)} %iota_xor_fusion.order, bf16[128,2048]{1,0:T(8,128)(2,1)S(1)} %copy-done.5, bf16[128,2048]{1,0:T(8,128)(2,1)S(1)} %collective-permute-done.x1, bf16[128,2048]{1,0:T(8,128)(2,1)} %collective-permute-done.1.x2, ...), custom_call_target="tpu_custom_call" | custom-call | flops 1000 | bytes 1000 | tf_op jit(solution)/shard_map/project/pallas_call | solution.py:30
  35.0 13.2 %all_to_all.23 = bf16[8,16,512]{2,1,0:T(8,128)(2,1)S(1)} all-to-all(bf16[8,16,512]{2,1,0:T(8,128)(2,1)S(1)} %bitcast.8), channel_id=1, replica_groups=mesh['dp'=8,'tensor'=4] {'dp'}, dimensions={0} | all-to-all | bytes 262144 | tf_op jit(solution)/shard_map/all_to_all | solution.py:394
  48.3 1.1 %attend.1 = bf16[128,512]{1,0:T(8,128)(2,1)S(1)} custom-call(bf16[128,512]{1,0:T(8,128)(2,1)S(1)} %bitcast.6, s32[1,128]{1,0:T(1,128)S(1)} %get-tuple-element.47.receive, s32[1,128]{1,0:T(1,128)S(1)} %get-tuple-element.48.segments), custom_call_target="tpu_custom_call" | custom-call | flops 1000 | bytes 1000 | tf_op jit(solution)/shard_map/attend/pallas_call | solution.py:30
  49.4 9.9 %all_to_all.24 = bf16[8,16,512]{2,1,0:T(8,128)(2,1)S(1)} all-to-all(bf16[8,16,512]{2,1,0:T(8,128)(2,1)S(1)} %bitcast.7), channel_id=1, replica_groups=mesh['dp'=8,'tensor'=4] {'dp'}, dimensions={0} | all-to-all | bytes 262144 | tf_op jit(solution)/shard_map/all_to_all | solution.py:394
  59.6 1.1 %collective-permute-start.10 = (bf16[128,256]{1,0:T(8,128)(2,1)S(1)}, bf16[128,256]{1,0:T(8,128)(2,1)S(1)}, u32[]{:S(2)}, u32[]{:S(2)}) collective-permute-start(bf16[128,256]{1,0:T(8,128)(2,1)S(1)} %get-tuple-element.53.own), channel_id=1, source_target_pairs={{0,2},{1,3},{2,0},{3,1},{4,6},{5,7},{6,4},{7,5},{8,10},{9,11},{10,... | collective-permute-start | bytes 196616 | tf_op jit(solution)/shard_map/ppermute | solution.py:48
  61.3 1.1 %collective-permute-start.14 = (bf16[128,1024]{1,0:T(8,128)(2,1)S(1)}, bf16[128,1024]{1,0:T(8,128)(2,1)S(1)}, u32[]{:S(2)}, u32[]{:S(2)}) collective-permute-start(bf16[128,1024]{1,0:T(8,128)(2,1)S(1)} %spread_far.3), channel_id=1, source_target_pairs={{0,2},{1,3},{2,0},{3,1},{4,6},{5,7},{6,4},{7,5},{8,10},{9,11},{10,... | collective-permute-start | bytes 786440 | tf_op jit(solution)/shard_map/ppermute | solution.py:48
  62.4 1.6 %collective-permute-done.10.far = bf16[128,256]{1,0:T(8,128)(2,1)S(1)} collective-permute-done((bf16[128,256]{1,0:T(8,128)(2,1)S(1)}, bf16[128,256]{1,0:T(8,128)(2,1)S(1)}, u32[]{:S(2)}, u32[]{:S(2)}) %collective-permute-start.10) | collective-permute-done | bytes 65568 | tf_op jit(solution)/shard_map/ppermute | solution.py:48
  64.4 1.1 %collective-permute-start.15 = (bf16[128,512]{1,0:T(8,128)(2,1)S(1)}, bf16[128,512]{1,0:T(8,128)(2,1)S(1)}, u32[]{:S(2)}, u32[]{:S(2)}) collective-permute-start(bf16[128,512]{1,0:T(8,128)(2,1)S(1)} %spread_far.4), channel_id=1, source_target_pairs={{0,2},{1,3},{2,0},{3,1},{4,6},{5,7},{6,4},{7,5},{8,10},{9,11},{10,... | collective-permute-start | bytes 393224 | tf_op jit(solution)/shard_map/ppermute | solution.py:48
  65.8 1.0 %collective-permute-start.16 = (bf16[128,512]{1,0:T(8,128)(2,1)S(1)}, bf16[128,512]{1,0:T(8,128)(2,1)S(1)}, u32[]{:S(2)}, u32[]{:S(2)}) collective-permute-start(bf16[128,512]{1,0:T(8,128)(2,1)S(1)} %spread_far.5), channel_id=1, source_target_pairs={{0,2},{1,3},{2,0},{3,1},{4,6},{5,7},{6,4},{7,5},{8,10},{9,11},{10,... | collective-permute-start | bytes 393224 | tf_op jit(solution)/shard_map/ppermute | solution.py:48
  68.3 1.3 %finish_out.1 = bf16[128,2048]{1,0:T(8,128)(2,1)} custom-call(bf16[128,2048]{1,0:T(8,128)(2,1)S(1)} %copy-done.5, bf16[128,256]{1,0:T(8,128)(2,1)S(1)} %get-tuple-element.53.own, bf16[128,256]{1,0:T(8,128)(2,1)S(1)} %collective-permute-done.9.near, bf16[128,256]{1,0:T(8,128)(2,1)S(1)} %collective-permute-done.10.far, ...), custom_call_target="tpu_custom_call" | custom-call | flops 1000 | bytes 1000 | tf_op jit(solution)/shard_map/finish_out/pallas_call | solution.py:30
  70.3 3.1 %collective-permute-done.15.pieces_1_ = bf16[128,512]{1,0:T(8,128)(2,1)S(1)} collective-permute-done((bf16[128,512]{1,0:T(8,128)(2,1)S(1)}, bf16[128,512]{1,0:T(8,128)(2,1)S(1)}, u32[]{:S(2)}, u32[]{:S(2)}) %collective-permute-start.15) | collective-permute-done | bytes 131104 | tf_op jit(solution)/shard_map/ppermute | solution.py:48
  73.3 1.3 %finish_most.1 = (bf16[128,2048]{1,0:T(8,128)(2,1)}, f32[128,512]{1,0:T(8,128)S(1)}) custom-call(bf16[128,2048]{1,0:T(8,128)(2,1)S(1)} %copy-done.5, bf16[128,2048]{1,0:T(8,128)(2,1)S(1)} %copy-done.6, bf16[1,2048]{1,0:T(2,128)(2,1)S(1)} %reshape.17.gain, f32[128,1]{1,0:T(8,128)S(1)} %get-tuple-element.55.inverse, ...), custom_call_target="tpu_custom_call" | custom-call | flops 1000 | bytes 1000 | tf_op jit(solution)/shard_map/finish_most/pallas_call | solution.py:372
  75.4 0.8 finish_rest.1
  (52 shorter events, 9.6 us)
Async XLA Ops:
  0.6 8.1 %collective-permute-start.5 = (bf16[128,8192]{1,0:T(8,128)(2,1)}, bf16[128,8192]{1,0:T(8,128)(2,1)S(1)}, u32[]{:S(2)}, u32[]{:S(2)}) collective-permute-start(bf16[128,8192]{1,0:T(8,128)(2,1)} %w_output.1), channel_id=1, source_target_pairs={{0,1},{1,0},{2,3},{3,2},{4,5},{5,4},{6,7},{7,6},{8,9},{9,8},{10,11... | collective-permute-start | bytes 6291464 | tf_op jit(solution)/shard_map/ppermute | solution.py:48
  1.1 18.4 %collective-permute-start = (bf16[128,2048]{1,0:T(8,128)(2,1)}, bf16[128,2048]{1,0:T(8,128)(2,1)S(1)}, u32[]{:S(2)}, u32[]{:S(2)}) collective-permute-start(bf16[128,2048]{1,0:T(8,128)(2,1)} %inputs.3), channel_id=1, source_target_pairs={{0,1},{1,0},{2,3},{3,2},{4,5},{5,4},{6,7},{7,6},{8,9},{9,8},{10,11... | collective-permute-start | bytes 1572872 | tf_op jit(solution)/shard_map/ppermute | solution.py:48
  1.2 26.7 %collective-permute-start.1 = (bf16[128,2048]{1,0:T(8,128)(2,1)}, bf16[128,2048]{1,0:T(8,128)(2,1)}, u32[]{:S(2)}, u32[]{:S(2)}) collective-permute-start(bf16[128,2048]{1,0:T(8,128)(2,1)} %inputs.3), channel_id=1, source_target_pairs={{0,2},{1,3},{2,0},{3,1},{4,6},{5,7},{6,4},{7,5},{8,10},{9,11},{10,... | collective-permute-start | bytes 1572872 | tf_op jit(solution)/shard_map/ppermute | solution.py:48
  4.2 23.8 %collective-permute-start.2 = (bf16[128,2048]{1,0:T(8,128)(2,1)}, bf16[128,2048]{1,0:T(8,128)(2,1)S(1)}, u32[]{:S(2)}, u32[]{:S(2)}) collective-permute-start(bf16[128,2048]{1,0:T(8,128)(2,1)} %cotangent.1), channel_id=1, source_target_pairs={{0,2},{1,3},{2,0},{3,1},{4,6},{5,7},{6,4},{7,5},{8,10},{9,11},{10,... | collective-permute-start | bytes 1572872 | tf_op jit(solution)/shard_map/ppermute | solution.py:48
  4.9 1.2 %collective-permute-start.3 = (bf16[1,2048]{1,0:T(2,128)(2,1)S(1)}, bf16[1,2048]{1,0:T(2,128)(2,1)S(1)}, u32[]{:S(2)}, u32[]{:S(2)}) collective-permute-start(bf16[1,2048]{1,0:T(2,128)(2,1)S(1)} %reshape.17.gain), channel_id=1, source_target_pairs={{0,1},{1,0},{2,3},{3,2},{4,5},{5,4},{6,7},{7,6},{8,9},{9,8},{10,11... | collective-permute-start | bytes 12296 | tf_op jit(solution)/shard_map/ppermute | solution.py:48
  6.1 21.9 %collective-permute-start.4 = (bf16[2,2048]{1,0:T(2,128)(2,1)S(1)}, bf16[2,2048]{1,0:T(2,128)(2,1)S(1)}, u32[]{:S(2)}, u32[]{:S(2)}) collective-permute-start(bf16[2,2048]{1,0:T(2,128)(2,1)S(1)} %pad_maximum_fusion.gain_chip), channel_id=1, source_target_pairs={{0,2},{1,3},{2,0},{3,1},{4,6},{5,7},{6,4},{7,5},{8,10},{9,11},{10,... | collective-permute-start | bytes 24584 | tf_op jit(solution)/shard_map/ppermute | solution.py:48
  8.7 1.6 %copy-start = (bf16[8192,128]{1,0:T(8,128)(2,1)S(1)}, bf16[8192,128]{1,0:T(8,128)(2,1)}, u32[]{:S(2)}) copy-start(bf16[8192,128]{1,0:T(8,128)(2,1)} %w_query.3) | copy-start | bytes 6291460
  10.3 1.6 %copy-start.2 = (bf16[8192,128]{1,0:T(8,128)(2,1)S(1)}, bf16[8192,128]{1,0:T(8,128)(2,1)}, u32[]{:S(2)}) copy-start(bf16[8192,128]{1,0:T(8,128)(2,1)} %w_key.3) | copy-start | bytes 6291460
  13.5 1.6 %copy-start.7 = (bf16[128,8192]{1,0:T(8,128)(2,1)S(1)}, bf16[128,8192]{1,0:T(8,128)(2,1)}, u32[]{:S(2)}) copy-start(bf16[128,8192]{1,0:T(8,128)(2,1)} %w_output.1) | copy-start | bytes 6291460
  17.0 2.5 %copy-start.5 = (bf16[128,2048]{1,0:T(8,128)(2,1)S(1)}, bf16[128,2048]{1,0:T(8,128)(2,1)}, u32[]{:S(2)}) copy-start(bf16[128,2048]{1,0:T(8,128)(2,1)} %inputs.3) | copy-start | bytes 1572868
  17.0 2.5 %copy-start.6 = (bf16[128,2048]{1,0:T(8,128)(2,1)S(1)}, bf16[128,2048]{1,0:T(8,128)(2,1)}, u32[]{:S(2)}) copy-start(bf16[128,2048]{1,0:T(8,128)(2,1)} %cotangent.1) | copy-start | bytes 1572868
  28.0 4.2 %collective-permute-start.6 = (bf16[128,2048]{1,0:T(8,128)(2,1)}, bf16[128,2048]{1,0:T(8,128)(2,1)S(1)}, u32[]{:S(2)}, u32[]{:S(2)}) collective-permute-start(bf16[128,2048]{1,0:T(8,128)(2,1)} %collective-permute-done.1.x2), channel_id=1, source_target_pairs={{0,1},{1,0},{2,3},{3,2},{4,5},{5,4},{6,7},{7,6},{8,9},{9,8},{10,11... | collective-permute-start | bytes 1572872 | tf_op jit(solution)/shard_map/ppermute | solution.py:48
  28.3 3.9 %collective-permute-start.7 = (f32[128,128]{1,0:T(8,128)S(1)}, f32[128,128]{1,0:T(8,128)S(1)}, u32[]{:S(2)}, u32[]{:S(2)}) collective-permute-start(f32[128,128]{1,0:T(8,128)S(1)} %add_grad.2), channel_id=1, source_target_pairs={{0,1},{1,0},{2,3},{3,2},{4,5},{5,4},{6,7},{7,6},{8,9},{9,8},{10,11... | collective-permute-start | bytes 196616 | tf_op jit(solution)/shard_map/ppermute | solution.py:48
  29.1 3.1 %copy-start.1 = (bf16[8192,128]{1,0:T(8,128)(2,1)S(1)}, bf16[8192,128]{1,0:T(8,128)(2,1)}, u32[]{:S(2)}) copy-start(bf16[8192,128]{1,0:T(8,128)(2,1)} %w_query.3) | copy-start | bytes 6291460
  29.1 3.1 %copy-start.3 = (bf16[8192,128]{1,0:T(8,128)(2,1)S(1)}, bf16[8192,128]{1,0:T(8,128)(2,1)}, u32[]{:S(2)}) copy-start(bf16[8192,128]{1,0:T(8,128)(2,1)} %w_key.3) | copy-start | bytes 6291460
  29.1 30.1 %collective-permute-start.8 = (bf16[256,2048]{1,0:T(8,128)(2,1)S(1)}, bf16[256,2048]{1,0:T(8,128)(2,1)S(1)}, u32[]{:S(2)}, u32[]{:S(2)}) collective-permute-start(bf16[256,2048]{1,0:T(8,128)(2,1)S(1)} %get-tuple-element.50), channel_id=1, source_target_pairs={{0,2},{1,3},{2,0},{3,1},{4,6},{5,7},{6,4},{7,5},{8,10},{9,11},{10,... | collective-permute-start | bytes 3145736 | tf_op jit(solution)/shard_map/ppermute | solution.py:48
  35.0 25.9 %collective-permute-start.13 = (bf16[384,4096]{1,0:T(8,128)(2,1)S(1)}, bf16[384,4096]{1,0:T(8,128)(2,1)S(1)}, u32[]{:S(2)}, u32[]{:S(2)}) collective-permute-start(bf16[384,4096]{1,0:T(8,128)(2,1)S(1)} %get-tuple-element.59), channel_id=1, source_target_pairs={{0,1},{1,0},{2,3},{3,2},{4,5},{5,4},{6,7},{7,6},{8,9},{9,8},{10,11... | collective-permute-start | bytes 9437192 | tf_op jit(solution)/shard_map/ppermute | solution.py:48
  59.5 1.4 %collective-permute-start.12 = (bf16[128,384]{1,0:T(8,128)(2,1)S(1)}, bf16[128,384]{1,0:T(8,128)(2,1)S(1)}, u32[]{:S(2)}, u32[]{:S(2)}) collective-permute-start(bf16[128,384]{1,0:T(8,128)(2,1)S(1)} %get-tuple-element.62.own), channel_id=1, source_target_pairs={{0,1},{1,0},{2,3},{3,2},{4,5},{5,4},{6,7},{7,6},{8,9},{9,8},{10,11... | collective-permute-start | bytes 294920 | tf_op jit(solution)/shard_map/ppermute | solution.py:48
  59.6 4.5 %collective-permute-start.10 = (bf16[128,256]{1,0:T(8,128)(2,1)S(1)}, bf16[128,256]{1,0:T(8,128)(2,1)S(1)}, u32[]{:S(2)}, u32[]{:S(2)}) collective-permute-start(bf16[128,256]{1,0:T(8,128)(2,1)S(1)} %get-tuple-element.53.own), channel_id=1, source_target_pairs={{0,2},{1,3},{2,0},{3,1},{4,6},{5,7},{6,4},{7,5},{8,10},{9,11},{10,... | collective-permute-start | bytes 196616 | tf_op jit(solution)/shard_map/ppermute | solution.py:48
  61.3 12.0 %collective-permute-start.14 = (bf16[128,1024]{1,0:T(8,128)(2,1)S(1)}, bf16[128,1024]{1,0:T(8,128)(2,1)S(1)}, u32[]{:S(2)}, u32[]{:S(2)}) collective-permute-start(bf16[128,1024]{1,0:T(8,128)(2,1)S(1)} %spread_far.3), channel_id=1, source_target_pairs={{0,2},{1,3},{2,0},{3,1},{4,6},{5,7},{6,4},{7,5},{8,10},{9,11},{10,... | collective-permute-start | bytes 786440 | tf_op jit(solution)/shard_map/ppermute | solution.py:48
  64.4 8.9 %collective-permute-start.15 = (bf16[128,512]{1,0:T(8,128)(2,1)S(1)}, bf16[128,512]{1,0:T(8,128)(2,1)S(1)}, u32[]{:S(2)}, u32[]{:S(2)}) collective-permute-start(bf16[128,512]{1,0:T(8,128)(2,1)S(1)} %spread_far.4), channel_id=1, source_target_pairs={{0,2},{1,3},{2,0},{3,1},{4,6},{5,7},{6,4},{7,5},{8,10},{9,11},{10,... | collective-permute-start | bytes 393224 | tf_op jit(solution)/shard_map/ppermute | solution.py:48
  65.8 9.5 %collective-permute-start.16 = (bf16[128,512]{1,0:T(8,128)(2,1)S(1)}, bf16[128,512]{1,0:T(8,128)(2,1)S(1)}, u32[]{:S(2)}, u32[]{:S(2)}) collective-permute-start(bf16[128,512]{1,0:T(8,128)(2,1)S(1)} %spread_far.5), channel_id=1, source_target_pairs={{0,2},{1,3},{2,0},{3,1},{4,6},{5,7},{6,4},{7,5},{8,10},{9,11},{10,... | collective-permute-start | bytes 393224 | tf_op jit(solution)/shard_map/ppermute | solution.py:48
  66.9 1.3 %collective-permute-start.9 = (bf16[128,256]{1,0:T(8,128)(2,1)S(1)}, bf16[128,256]{1,0:T(8,128)(2,1)S(1)}, u32[]{:S(2)}, u32[]{:S(2)}) collective-permute-start(bf16[128,256]{1,0:T(8,128)(2,1)S(1)} %get-tuple-element.53.own), channel_id=1, source_target_pairs={{0,1},{1,0},{2,3},{3,2},{4,5},{5,4},{6,7},{7,6},{8,9},{9,8},{10,11... | collective-permute-start | bytes 196616 | tf_op jit(solution)/shard_map/ppermute | solution.py:48
  66.9 1.4 %collective-permute-start.11 = (bf16[128,256]{1,0:T(8,128)(2,1)S(1)}, bf16[128,256]{1,0:T(8,128)(2,1)S(1)}, u32[]{:S(2)}, u32[]{:S(2)}) collective-permute-start(bf16[128,256]{1,0:T(8,128)(2,1)S(1)} %collective-permute-done.10.far), channel_id=1, source_target_pairs={{0,1},{1,0},{2,3},{3,2},{4,5},{5,4},{6,7},{7,6},{8,9},{9,8},{10,11... | collective-permute-start | bytes 196616 | tf_op jit(solution)/shard_map/ppermute | solution.py:48
  (4 other events, 3.6 us)

commit v19 on v16

--- a/solution.py
+++ b/solution.py
@@ -120,14 +120,19 @@
     return jnp.sum(wide * wide, axis=-1, keepdims=True)
 
 
-def begin_kernel(x0, x1, c0, here, squares, part):
+def begin_kernel(x0, x1, c0, here, squares, part, x1_out):
+    x1_out[...] = x1[...]
     squares[...] = sum_squares(x0) + sum_squares(x1)
     part[...] = dot(c0[...], here[...], CONTRACT_LAST)
 
 
 def begin(x0, x1, c0, here):
     rows, columns = x0.shape[0], here.shape[0]
-    shapes = [shape(jnp.float32, rows, 1), shape(jnp.float32, rows, columns)]
+    shapes = [
+        shape(jnp.float32, rows, 1),
+        shape(jnp.float32, rows, columns),
+        shape(x1.dtype, *x1.shape),
+    ]
     return call(begin_kernel, "begin", shapes, (x0, x1, c0, here), first=VMEM)
 
 
@@ -434,7 +439,7 @@
         width,
     )
     send, receive, segments = indices
-    squares, part = begin(inputs, x1, cotangent, here)
+    squares, part, x1 = begin(inputs, x1, cotangent, here)
 
     x2, c2, gain_far, squares, part = lax.optimization_barrier((x2, c2, gain_far, squares, part))
     x3 = swap(x2, 1, tensor)

time: 76.6 us -> 75.7 us (0.988)
  waiting for transfers between devices: 15.5 us -> 14.2 us
    ppermute x17, waiting for transfers between devices: 15.5 us -> 14.2 us  [swap(): return lax.ppermute(array, 'tensor', [(i, i ^ mask) for i in range(count)])]
  transfers between devices with their start and end apart: 17 -> 17, of which waited for: 8 -> 7; matrix products, arithmetic and copies ran while one was open for 1% -> 1% of each run, Pallas kernels for 17% -> 17%
where the time goes in v19:
time: 75.7 us; the launch traced here: 75.3 us
  blocking collectives  23.3 us (31%)
  starting transfers between devices  14.2 us (19%)
  waiting for transfers between devices  14.2 us (19%)
  Pallas kernels  13.5 us (18%)
  local copies, waits for them, and re-layouts  9.23 us (12%)
  between operations  0.8 us (1%)
    all_to_all x2, blocking collectives, move(): return lax.all_to_all(bucket, 'dp', split_axis=0, concat_axis=0, tiled=True)  23.3 us
    ppermute x17, starting transfers between devices, swap(): return lax.ppermute(array, 'tensor', [(i, i ^ mask) for i in range(count)])  14.2 us
    ppermute x17, waiting for transfers between devices, swap(): return lax.ppermute(array, 'tensor', [(i, i ^ mask) for i in range(count)])  14.2 us
    pallas_call x9, Pallas kernels, call(): pl.pallas_call(kernel, out_shape=shapes, in_specs=[first] + [rest] * (len...  9.74 us
    unnamed x22, local copies, waits for them, and re-layouts  8.54 us
    pallas_call x4, Pallas kernels, spread(): pl.pallas_call(spread_kernel(first), out_shape=shape(dtype, own.shape[0],...  1.77 us
  transfers between devices with their start and end apart: 17, of which 7 were waited for; matrix products, arithmetic and copies ran while one was open for 1% of the time, Pallas kernels for 17%

profile of v19, /device:TPU:0, one launch (start us, length us, event | category | flops | bytes accessed | tf_op | source)
XLA Modules:
  0.0 75.3 jit_solution(5620277442981728894)
XLA Ops:
  1.2 2.9 %collective-permute-start.2 = (bf16[128,2048]{1,0:T(8,128)(2,1)}, bf16[128,2048]{1,0:T(8,128)(2,1)S(1)}, u32[]{:S(2)}, u32[]{:S(2)}) collective-permute-start(bf16[128,2048]{1,0:T(8,128)(2,1)} %inputs.3), channel_id=1, source_target_pairs={{0,2},{1,3},{2,0},{3,1},{4,6},{5,7},{6,4},{7,5},{8,10},{9,11},{10,... | collective-permute-start | bytes 1572872 | tf_op jit(solution)/shard_map/ppermute | solution.py:48
  4.9 1.2 %collective-permute-done.4 = bf16[1,2048]{1,0:T(2,128)(2,1)S(1)} collective-permute-done((bf16[1,2048]{1,0:T(2,128)(2,1)S(1)}, bf16[1,2048]{1,0:T(2,128)(2,1)S(1)}, u32[]{:S(2)}, u32[]{:S(2)}) %collective-permute-start.4) | collective-permute-done | bytes 4128 | tf_op jit(solution)/shard_map/ppermute | solution.py:48
  6.1 2.6 %collective-permute-start.5 = (bf16[2,2048]{1,0:T(2,128)(2,1)S(1)}, bf16[2,2048]{1,0:T(2,128)(2,1)S(1)}, u32[]{:S(2)}, u32[]{:S(2)}) collective-permute-start(bf16[2,2048]{1,0:T(2,128)(2,1)S(1)} %pad_maximum_fusion.gain_chip), channel_id=1, source_target_pairs={{0,2},{1,3},{2,0},{3,1},{4,6},{5,7},{6,4},{7,5},{8,10},{9,11},{10,... | collective-permute-start | bytes 24584 | tf_op jit(solution)/shard_map/ppermute | solution.py:48
  8.7 1.6 %copy-done = bf16[8192,128]{1,0:T(8,128)(2,1)S(1)} copy-done((bf16[8192,128]{1,0:T(8,128)(2,1)S(1)}, bf16[8192,128]{1,0:T(8,128)(2,1)}, u32[]{:S(2)}) %copy-start) | copy-done | bytes 2097176
  10.3 1.6 %copy-done.2 = bf16[8192,128]{1,0:T(8,128)(2,1)S(1)} copy-done((bf16[8192,128]{1,0:T(8,128)(2,1)S(1)}, bf16[8192,128]{1,0:T(8,128)(2,1)}, u32[]{:S(2)}) %copy-start.2) | copy-done | bytes 2097176
  11.9 1.6 %copy-done.4 = bf16[8192,128]{1,0:T(8,128)(2,1)S(1)} copy-done((bf16[8192,128]{1,0:T(8,128)(2,1)S(1)}, bf16[8192,128]{1,0:T(8,128)(2,1)}, u32[]{:S(2)}) %copy-start.4) | copy-done | bytes 2097176
  13.5 1.6 %copy-done.7 = bf16[128,8192]{1,0:T(8,128)(2,1)S(1)} copy-done((bf16[128,8192]{1,0:T(8,128)(2,1)S(1)}, bf16[128,8192]{1,0:T(8,128)(2,1)}, u32[]{:S(2)}) %copy-start.7) | copy-done | bytes 2097176
  17.0 2.5 %prepare.1 = (bf16[384,4096]{1,0:T(8,128)(2,1)S(1)}, bf16[384,4096]{1,0:T(8,128)(2,1)S(1)}, bf16[256,2048]{1,0:T(8,128)(2,1)S(1)}, bf16[256,2048]{1,0:T(8,128)(2...) custom-call(s32[4]{0:T(128)S(1)} %iota_xor_fusion.order, ...), custom_call_target="tpu_custom_call" | custom-call | flops 1000 | bytes 1000 | tf_op jit(solution)/shard_map/prepare/pallas_call | solution.py:30
  19.6 1.7 %begin.1 = (f32[128,1]{1,0:T(8,128)S(1)}, f32[128,256]{1,0:T(8,128)S(1)}, bf16[128,2048]{1,0:T(8,128)(2,1)S(1)}) custom-call(bf16[128,2048]{1,0:T(8,128)(2,1)S(1)} %copy-done.5, bf16[128,2048]{1,0:T(8,128)(2,1)} %collective-permute-done.x1, bf16[128,2048]{1,0:T(8,128)(2,1)S(1)} %copy-done.6, bf16[256,2048]{1,0:T(8,128)(2,1)S(1)} %get-tuple-element.35.here), custom_call_target="tpu_custom_call" | custom-call | flops 1000 | bytes 1000 | tf_op jit(solution)/shard_map/begin/pallas_call | solution.py:30
  21.2 6.7 %collective-permute-done.5.gain_far = bf16[2,2048]{1,0:T(2,128)(2,1)S(1)} collective-permute-done((bf16[2,2048]{1,0:T(2,128)(2,1)S(1)}, bf16[2,2048]{1,0:T(2,128)(2,1)S(1)}, u32[]{:S(2)}, u32[]{:S(2)}) %collective-permute-start.5) | collective-permute-done | bytes 8224 | tf_op jit(solution)/shard_map/ppermute | solution.py:48
  29.1 1.8 %collective-permute-start.8 = (bf16[256,2048]{1,0:T(8,128)(2,1)S(1)}, bf16[256,2048]{1,0:T(8,128)(2,1)S(1)}, u32[]{:S(2)}, u32[]{:S(2)}) collective-permute-start(bf16[256,2048]{1,0:T(8,128)(2,1)S(1)} %get-tuple-element.52), channel_id=1, source_target_pairs={{0,2},{1,3},{2,0},{3,1},{4,6},{5,7},{6,4},{7,5},{8,10},{9,11},{10,... | collective-permute-start | bytes 3145736 | tf_op jit(solution)/shard_map/ppermute | solution.py:48
  31.4 2.2 %project.1 = (bf16[128,384]{1,0:T(8,128)(2,1)S(1)}, f32[128,1]{1,0:T(8,128)S(1)}, bf16[128,512]{1,0:T(8,128)(2,1)S(1)}) custom-call(s32[4]{0:T(128)S(1)} %iota_xor_fusion.order, bf16[128,2048]{1,0:T(8,128)(2,1)S(1)} %copy-done.5, bf16[128,2048]{1,0:T(8,128)(2,1)S(1)} %get-tuple-element.36.x1, bf16[128,2048]{1,0:T(8,128)(2,1)S(1)} %collective-permute-done.2.x2, ...), custom_call_target="tpu_custom_call" | custom-call | flops 1000 | bytes 1000 | tf_op jit(solution)/shard_map/project/pallas_call | solution.py:30
  33.7 13.4 %all_to_all.23 = bf16[8,16,512]{2,1,0:T(8,128)(2,1)S(1)} all-to-all(bf16[8,16,512]{2,1,0:T(8,128)(2,1)S(1)} %bitcast.8), channel_id=1, replica_groups=mesh['dp'=8,'tensor'=4] {'dp'}, dimensions={0} | all-to-all | bytes 262144 | tf_op jit(solution)/shard_map/all_to_all | solution.py:399
  47.1 1.1 %attend.1 = bf16[128,512]{1,0:T(8,128)(2,1)S(1)} custom-call(bf16[128,512]{1,0:T(8,128)(2,1)S(1)} %bitcast.6, s32[1,128]{1,0:T(1,128)S(1)} %get-tuple-element.49.receive, s32[1,128]{1,0:T(1,128)S(1)} %get-tuple-element.50.segments), custom_call_target="tpu_custom_call" | custom-call | flops 1000 | bytes 1000 | tf_op jit(solution)/shard_map/attend/pallas_call | solution.py:30
  48.2 9.9 %all_to_all.24 = bf16[8,16,512]{2,1,0:T(8,128)(2,1)S(1)} all-to-all(bf16[8,16,512]{2,1,0:T(8,128)(2,1)S(1)} %bitcast.7), channel_id=1, replica_groups=mesh['dp'=8,'tensor'=4] {'dp'}, dimensions={0} | all-to-all | bytes 262144 | tf_op jit(solution)/shard_map/all_to_all | solution.py:399
  58.4 1.6 %collective-permute-start.10 = (bf16[128,256]{1,0:T(8,128)(2,1)S(1)}, bf16[128,256]{1,0:T(8,128)(2,1)S(1)}, u32[]{:S(2)}, u32[]{:S(2)}) collective-permute-start(bf16[128,256]{1,0:T(8,128)(2,1)S(1)} %get-tuple-element.55.own), channel_id=1, source_target_pairs={{0,2},{1,3},{2,0},{3,1},{4,6},{5,7},{6,4},{7,5},{8,10},{9,11},{10,... | collective-permute-start | bytes 196616 | tf_op jit(solution)/shard_map/ppermute | solution.py:48
  60.5 1.3 %collective-permute-start.14 = (bf16[128,1024]{1,0:T(8,128)(2,1)S(1)}, bf16[128,1024]{1,0:T(8,128)(2,1)S(1)}, u32[]{:S(2)}, u32[]{:S(2)}) collective-permute-start(bf16[128,1024]{1,0:T(8,128)(2,1)S(1)} %spread_far.3), channel_id=1, source_target_pairs={{0,2},{1,3},{2,0},{3,1},{4,6},{5,7},{6,4},{7,5},{8,10},{9,11},{10,... | collective-permute-start | bytes 786440 | tf_op jit(solution)/shard_map/ppermute | solution.py:48
  61.7 1.2 %collective-permute-done.10.far = bf16[128,256]{1,0:T(8,128)(2,1)S(1)} collective-permute-done((bf16[128,256]{1,0:T(8,128)(2,1)S(1)}, bf16[128,256]{1,0:T(8,128)(2,1)S(1)}, u32[]{:S(2)}, u32[]{:S(2)}) %collective-permute-start.10) | collective-permute-done | bytes 65568 | tf_op jit(solution)/shard_map/ppermute | solution.py:48
  63.2 1.6 %collective-permute-start.15 = (bf16[128,512]{1,0:T(8,128)(2,1)S(1)}, bf16[128,512]{1,0:T(8,128)(2,1)S(1)}, u32[]{:S(2)}, u32[]{:S(2)}) collective-permute-start(bf16[128,512]{1,0:T(8,128)(2,1)S(1)} %spread_far.4), channel_id=1, source_target_pairs={{0,2},{1,3},{2,0},{3,1},{4,6},{5,7},{6,4},{7,5},{8,10},{9,11},{10,... | collective-permute-start | bytes 393224 | tf_op jit(solution)/shard_map/ppermute | solution.py:48
  67.1 1.3 %finish_out.1 = bf16[128,2048]{1,0:T(8,128)(2,1)} custom-call(bf16[128,2048]{1,0:T(8,128)(2,1)S(1)} %copy-done.5, bf16[128,256]{1,0:T(8,128)(2,1)S(1)} %get-tuple-element.55.own, bf16[128,256]{1,0:T(8,128)(2,1)S(1)} %collective-permute-done.9.near, bf16[128,256]{1,0:T(8,128)(2,1)S(1)} %collective-permute-done.10.far, ...), custom_call_target="tpu_custom_call" | custom-call | flops 1000 | bytes 1000 | tf_op jit(solution)/shard_map/finish_out/pallas_call | solution.py:30
  69.1 3.4 %collective-permute-done.15.pieces_1_ = bf16[128,512]{1,0:T(8,128)(2,1)S(1)} collective-permute-done((bf16[128,512]{1,0:T(8,128)(2,1)S(1)}, bf16[128,512]{1,0:T(8,128)(2,1)S(1)}, u32[]{:S(2)}, u32[]{:S(2)}) %collective-permute-start.15) | collective-permute-done | bytes 131104 | tf_op jit(solution)/shard_map/ppermute | solution.py:48
  72.5 1.2 %finish_most.1 = (bf16[128,2048]{1,0:T(8,128)(2,1)}, f32[128,512]{1,0:T(8,128)S(1)}) custom-call(bf16[128,2048]{1,0:T(8,128)(2,1)S(1)} %copy-done.5, bf16[128,2048]{1,0:T(8,128)(2,1)S(1)} %copy-done.6, bf16[1,2048]{1,0:T(2,128)(2,1)S(1)} %reshape.19.gain, f32[128,1]{1,0:T(8,128)S(1)} %get-tuple-element.57.inverse, ...), custom_call_target="tpu_custom_call" | custom-call | flops 1000 | bytes 1000 | tf_op jit(solution)/shard_map/finish_most/pallas_call | solution.py:377
  73.7 0.8 %collective-permute-done.16.rest = bf16[128,512]{1,0:T(8,128)(2,1)S(1)} collective-permute-done((bf16[128,512]{1,0:T(8,128)(2,1)S(1)}, bf16[128,512]{1,0:T(8,128)(2,1)S(1)}, u32[]{:S(2)}, u32[]{:S(2)}) %collective-permute-start.16) | collective-permute-done | bytes 131104 | tf_op jit(solution)/shard_map/ppermute | solution.py:48
  74.5 0.8 %finish_rest.1 = bf16[128,2048]{1,0:T(8,128)(2,1)} custom-call(bf16[1,2048]{1,0:T(2,128)(2,1)S(1)} %reshape.19.gain, f32[128,1]{1,0:T(8,128)S(1)} %get-tuple-element.57.inverse, f32[128,512]{1,0:T(8,128)S(1)} %get-tuple-element.66.left, bf16[128,512]{1,0:T(8,128)(2,1)S(1)} %collective-permute-done.16.rest, ...), custom_call_target="tpu_custom_call", output_to_operand_aliasing={{}: (4, {})} | custom-call | flops 1000 | bytes 1000 | tf_op jit(solution)/shard_map/finish_rest/pallas_call | solution.py:386
  (52 shorter events, 9.1 us)
Async XLA Ops:
  0.6 8.1 %collective-permute-start.1 = (bf16[128,8192]{1,0:T(8,128)(2,1)}, bf16[128,8192]{1,0:T(8,128)(2,1)S(1)}, u32[]{:S(2)}, u32[]{:S(2)}) collective-permute-start(bf16[128,8192]{1,0:T(8,128)(2,1)} %w_output.1), channel_id=1, source_target_pairs={{0,1},{1,0},{2,3},{3,2},{4,5},{5,4},{6,7},{7,6},{8,9},{9,8},{10,11... | collective-permute-start | bytes 6291464 | tf_op jit(solution)/shard_map/ppermute | solution.py:48
  1.1 18.4 %collective-permute-start = (bf16[128,2048]{1,0:T(8,128)(2,1)}, bf16[128,2048]{1,0:T(8,128)(2,1)}, u32[]{:S(2)}, u32[]{:S(2)}) collective-permute-start(bf16[128,2048]{1,0:T(8,128)(2,1)} %inputs.3), channel_id=1, source_target_pairs={{0,1},{1,0},{2,3},{3,2},{4,5},{5,4},{6,7},{7,6},{8,9},{9,8},{10,11... | collective-permute-start | bytes 1572872 | tf_op jit(solution)/shard_map/ppermute | solution.py:48
  1.2 26.7 %collective-permute-start.2 = (bf16[128,2048]{1,0:T(8,128)(2,1)}, bf16[128,2048]{1,0:T(8,128)(2,1)S(1)}, u32[]{:S(2)}, u32[]{:S(2)}) collective-permute-start(bf16[128,2048]{1,0:T(8,128)(2,1)} %inputs.3), channel_id=1, source_target_pairs={{0,2},{1,3},{2,0},{3,1},{4,6},{5,7},{6,4},{7,5},{8,10},{9,11},{10,... | collective-permute-start | bytes 1572872 | tf_op jit(solution)/shard_map/ppermute | solution.py:48
  4.2 23.8 %collective-permute-start.3 = (bf16[128,2048]{1,0:T(8,128)(2,1)}, bf16[128,2048]{1,0:T(8,128)(2,1)S(1)}, u32[]{:S(2)}, u32[]{:S(2)}) collective-permute-start(bf16[128,2048]{1,0:T(8,128)(2,1)} %cotangent.1), channel_id=1, source_target_pairs={{0,2},{1,3},{2,0},{3,1},{4,6},{5,7},{6,4},{7,5},{8,10},{9,11},{10,... | collective-permute-start | bytes 1572872 | tf_op jit(solution)/shard_map/ppermute | solution.py:48
  4.9 1.2 %collective-permute-start.4 = (bf16[1,2048]{1,0:T(2,128)(2,1)S(1)}, bf16[1,2048]{1,0:T(2,128)(2,1)S(1)}, u32[]{:S(2)}, u32[]{:S(2)}) collective-permute-start(bf16[1,2048]{1,0:T(2,128)(2,1)S(1)} %reshape.19.gain), channel_id=1, source_target_pairs={{0,1},{1,0},{2,3},{3,2},{4,5},{5,4},{6,7},{7,6},{8,9},{9,8},{10,11... | collective-permute-start | bytes 12296 | tf_op jit(solution)/shard_map/ppermute | solution.py:48
  6.1 21.9 %collective-permute-start.5 = (bf16[2,2048]{1,0:T(2,128)(2,1)S(1)}, bf16[2,2048]{1,0:T(2,128)(2,1)S(1)}, u32[]{:S(2)}, u32[]{:S(2)}) collective-permute-start(bf16[2,2048]{1,0:T(2,128)(2,1)S(1)} %pad_maximum_fusion.gain_chip), channel_id=1, source_target_pairs={{0,2},{1,3},{2,0},{3,1},{4,6},{5,7},{6,4},{7,5},{8,10},{9,11},{10,... | collective-permute-start | bytes 24584 | tf_op jit(solution)/shard_map/ppermute | solution.py:48
  8.7 1.6 %copy-start = (bf16[8192,128]{1,0:T(8,128)(2,1)S(1)}, bf16[8192,128]{1,0:T(8,128)(2,1)}, u32[]{:S(2)}) copy-start(bf16[8192,128]{1,0:T(8,128)(2,1)} %w_query.3) | copy-start | bytes 6291460
  10.3 1.6 %copy-start.2 = (bf16[8192,128]{1,0:T(8,128)(2,1)S(1)}, bf16[8192,128]{1,0:T(8,128)(2,1)}, u32[]{:S(2)}) copy-start(bf16[8192,128]{1,0:T(8,128)(2,1)} %w_key.3) | copy-start | bytes 6291460
  11.9 1.6 %copy-start.4 = (bf16[8192,128]{1,0:T(8,128)(2,1)S(1)}, bf16[8192,128]{1,0:T(8,128)(2,1)}, u32[]{:S(2)}) copy-start(bf16[8192,128]{1,0:T(8,128)(2,1)} %w_value.3) | copy-start | bytes 6291460
  17.0 2.5 %copy-start.5 = (bf16[128,2048]{1,0:T(8,128)(2,1)S(1)}, bf16[128,2048]{1,0:T(8,128)(2,1)}, u32[]{:S(2)}) copy-start(bf16[128,2048]{1,0:T(8,128)(2,1)} %inputs.3) | copy-start | bytes 1572868
  17.0 2.5 %copy-start.6 = (bf16[128,2048]{1,0:T(8,128)(2,1)S(1)}, bf16[128,2048]{1,0:T(8,128)(2,1)}, u32[]{:S(2)}) copy-start(bf16[128,2048]{1,0:T(8,128)(2,1)} %cotangent.1) | copy-start | bytes 1572868
  28.0 3.2 %collective-permute-start.6 = (bf16[128,2048]{1,0:T(8,128)(2,1)S(1)}, bf16[128,2048]{1,0:T(8,128)(2,1)S(1)}, u32[]{:S(2)}, u32[]{:S(2)}) collective-permute-start(bf16[128,2048]{1,0:T(8,128)(2,1)S(1)} %collective-permute-done.2.x2), channel_id=1, source_target_pairs={{0,1},{1,0},{2,3},{3,2},{4,5},{5,4},{6,7},{7,6},{8,9},{9,8},{10,11... | collective-permute-start | bytes 1572872 | tf_op jit(solution)/shard_map/ppermute | solution.py:48
  28.3 2.9 %collective-permute-start.7 = (f32[128,128]{1,0:T(8,128)S(1)}, f32[128,128]{1,0:T(8,128)S(1)}, u32[]{:S(2)}, u32[]{:S(2)}) collective-permute-start(f32[128,128]{1,0:T(8,128)S(1)} %add_grad.2), channel_id=1, source_target_pairs={{0,1},{1,0},{2,3},{3,2},{4,5},{5,4},{6,7},{7,6},{8,9},{9,8},{10,11... | collective-permute-start | bytes 196616 | tf_op jit(solution)/shard_map/ppermute | solution.py:48
  29.1 2.0 %copy-start.1 = (bf16[8192,128]{1,0:T(8,128)(2,1)S(1)}, bf16[8192,128]{1,0:T(8,128)(2,1)}, u32[]{:S(2)}) copy-start(bf16[8192,128]{1,0:T(8,128)(2,1)} %w_query.3) | copy-start | bytes 6291460
  29.1 2.2 %copy-start.3 = (bf16[8192,128]{1,0:T(8,128)(2,1)S(1)}, bf16[8192,128]{1,0:T(8,128)(2,1)}, u32[]{:S(2)}) copy-start(bf16[8192,128]{1,0:T(8,128)(2,1)} %w_key.3) | copy-start | bytes 6291460
  29.1 28.9 %collective-permute-start.8 = (bf16[256,2048]{1,0:T(8,128)(2,1)S(1)}, bf16[256,2048]{1,0:T(8,128)(2,1)S(1)}, u32[]{:S(2)}, u32[]{:S(2)}) collective-permute-start(bf16[256,2048]{1,0:T(8,128)(2,1)S(1)} %get-tuple-element.52), channel_id=1, source_target_pairs={{0,2},{1,3},{2,0},{3,1},{4,6},{5,7},{6,4},{7,5},{8,10},{9,11},{10,... | collective-permute-start | bytes 3145736 | tf_op jit(solution)/shard_map/ppermute | solution.py:48
  33.6 26.4 %collective-permute-start.13 = (bf16[384,4096]{1,0:T(8,128)(2,1)S(1)}, bf16[384,4096]{1,0:T(8,128)(2,1)S(1)}, u32[]{:S(2)}, u32[]{:S(2)}) collective-permute-start(bf16[384,4096]{1,0:T(8,128)(2,1)S(1)} %get-tuple-element.61), channel_id=1, source_target_pairs={{0,1},{1,0},{2,3},{3,2},{4,5},{5,4},{6,7},{7,6},{8,9},{9,8},{10,11... | collective-permute-start | bytes 9437192 | tf_op jit(solution)/shard_map/ppermute | solution.py:48
  58.3 1.7 %collective-permute-start.12 = (bf16[128,384]{1,0:T(8,128)(2,1)S(1)}, bf16[128,384]{1,0:T(8,128)(2,1)S(1)}, u32[]{:S(2)}, u32[]{:S(2)}) collective-permute-start(bf16[128,384]{1,0:T(8,128)(2,1)S(1)} %get-tuple-element.64.own), channel_id=1, source_target_pairs={{0,1},{1,0},{2,3},{3,2},{4,5},{5,4},{6,7},{7,6},{8,9},{9,8},{10,11... | collective-permute-start | bytes 294920 | tf_op jit(solution)/shard_map/ppermute | solution.py:48
  58.4 4.5 %collective-permute-start.10 = (bf16[128,256]{1,0:T(8,128)(2,1)S(1)}, bf16[128,256]{1,0:T(8,128)(2,1)S(1)}, u32[]{:S(2)}, u32[]{:S(2)}) collective-permute-start(bf16[128,256]{1,0:T(8,128)(2,1)S(1)} %get-tuple-element.55.own), channel_id=1, source_target_pairs={{0,2},{1,3},{2,0},{3,1},{4,6},{5,7},{6,4},{7,5},{8,10},{9,11},{10,... | collective-permute-start | bytes 196616 | tf_op jit(solution)/shard_map/ppermute | solution.py:48
  60.5 12.0 %collective-permute-start.14 = (bf16[128,1024]{1,0:T(8,128)(2,1)S(1)}, bf16[128,1024]{1,0:T(8,128)(2,1)S(1)}, u32[]{:S(2)}, u32[]{:S(2)}) collective-permute-start(bf16[128,1024]{1,0:T(8,128)(2,1)S(1)} %spread_far.3), channel_id=1, source_target_pairs={{0,2},{1,3},{2,0},{3,1},{4,6},{5,7},{6,4},{7,5},{8,10},{9,11},{10,... | collective-permute-start | bytes 786440 | tf_op jit(solution)/shard_map/ppermute | solution.py:48
  63.2 9.2 %collective-permute-start.15 = (bf16[128,512]{1,0:T(8,128)(2,1)S(1)}, bf16[128,512]{1,0:T(8,128)(2,1)S(1)}, u32[]{:S(2)}, u32[]{:S(2)}) collective-permute-start(bf16[128,512]{1,0:T(8,128)(2,1)S(1)} %spread_far.4), channel_id=1, source_target_pairs={{0,2},{1,3},{2,0},{3,1},{4,6},{5,7},{6,4},{7,5},{8,10},{9,11},{10,... | collective-permute-start | bytes 393224 | tf_op jit(solution)/shard_map/ppermute | solution.py:48
  65.1 9.4 %collective-permute-start.16 = (bf16[128,512]{1,0:T(8,128)(2,1)S(1)}, bf16[128,512]{1,0:T(8,128)(2,1)S(1)}, u32[]{:S(2)}, u32[]{:S(2)}) collective-permute-start(bf16[128,512]{1,0:T(8,128)(2,1)S(1)} %spread_far.5), channel_id=1, source_target_pairs={{0,2},{1,3},{2,0},{3,1},{4,6},{5,7},{6,4},{7,5},{8,10},{9,11},{10,... | collective-permute-start | bytes 393224 | tf_op jit(solution)/shard_map/ppermute | solution.py:48
  65.7 1.3 %collective-permute-start.9 = (bf16[128,256]{1,0:T(8,128)(2,1)S(1)}, bf16[128,256]{1,0:T(8,128)(2,1)S(1)}, u32[]{:S(2)}, u32[]{:S(2)}) collective-permute-start(bf16[128,256]{1,0:T(8,128)(2,1)S(1)} %get-tuple-element.55.own), channel_id=1, source_target_pairs={{0,1},{1,0},{2,3},{3,2},{4,5},{5,4},{6,7},{7,6},{8,9},{9,8},{10,11... | collective-permute-start | bytes 196616 | tf_op jit(solution)/shard_map/ppermute | solution.py:48
  65.7 1.4 %collective-permute-start.11 = (bf16[128,256]{1,0:T(8,128)(2,1)S(1)}, bf16[128,256]{1,0:T(8,128)(2,1)S(1)}, u32[]{:S(2)}, u32[]{:S(2)}) collective-permute-start(bf16[128,256]{1,0:T(8,128)(2,1)S(1)} %collective-permute-done.10.far), channel_id=1, source_target_pairs={{0,1},{1,0},{2,3},{3,2},{4,5},{5,4},{6,7},{7,6},{8,9},{9,8},{10,11... | collective-permute-start | bytes 196616 | tf_op jit(solution)/shard_map/ppermute | solution.py:48
  (4 other events, 3.6 us)

commit v20 on v15

--- a/solution.py
+++ b/solution.py
@@ -53,6 +53,20 @@
 def one_hot(places, rows):
     row = lax.broadcasted_iota(jnp.int32, (rows, places.shape[1]), 0)
     return jnp.where(places == row, 1.0, 0.0).astype(jnp.bfloat16)
+
+
+def slot_mask(receive, stays, slots):
+    place = one_hot(receive, slots).astype(jnp.float32)
+    down = lax.broadcasted_iota(jnp.int32, (slots, slots), 0)
+    across = lax.broadcasted_iota(jnp.int32, (slots, slots), 1)
+    position = lax.broadcasted_iota(jnp.int32, receive.shape, 1)
+    both = []
+    for values in (stays, position):
+        column = jnp.sum(place * values.astype(jnp.float32), axis=1, keepdims=True)
+        both.append((column, jnp.sum(jnp.where(down == across, column, 0.0), axis=0, keepdims=True)))
+    (stay_down, stay_across), (place_down, place_across) = both
+    allowed = (stay_down == stay_across) & (place_across <= place_down)
+    return jnp.where(allowed, 1.0, 0.0)
 
 
 def prepare_kernel(
@@ -73,8 +87,10 @@
     send_out,
     receive_out,
     segments_out,
+    mask_out,
 ):
     heads, width = w_output.shape[0], here.shape[1]
+    mask_out[...] = slot_mask(receive[...], segments[...], mask_out.shape[0])
     for slot, out, turned in ((0, here, None), (2, there, there_turned)):
         columns = pl.ds(block_start(order, slot, width), width)
         for part, weight in enumerate((w_output, near_output)):
@@ -108,6 +124,7 @@
             shape(jnp.int32, *send.shape),
             shape(jnp.int32, *receive.shape),
             shape(jnp.int32, *segments.shape),
+            shape(jnp.float32, send.shape[1], send.shape[1]),
         ],
         (order, w_query, w_key, w_value, w_output, near_output, send, receive, segments),
     )
@@ -210,18 +227,26 @@
     )
 
 
-def attend_kernel(moved, receive, segments, back):
+def attend_kernel(moved, mask, back):
+    back[...] = attention(moved[...], mask[...] > 0.5)
+
+
+def attend_sparse_kernel(moved, receive, segments, back):
     place = one_hot(receive[...], moved.shape[0])
     rows = dot(place, moved[...], CONTRACT_FIRST).astype(jnp.bfloat16)
-    queries, key_rows, value_rows, head_grad = (
-        rows[:, index * HEAD_DIM : (index + 1) * HEAD_DIM] for index in range(4)
-    )
     count = rows.shape[0]
     down = lax.broadcasted_iota(jnp.int32, (count, count), 0)
     across = lax.broadcasted_iota(jnp.int32, (count, count), 1)
     stays = segments[...]
     own_stay = jnp.sum(jnp.where(down == across, stays, 0), axis=1, keepdims=True)
-    allowed = (own_stay == stays) & (across <= down)
+    results = attention(rows, (own_stay == stays) & (across <= down))
+    back[...] = dot(place, results).astype(jnp.bfloat16)
+
+
+def attention(rows, allowed):
+    queries, key_rows, value_rows, head_grad = (
+        rows[:, index * HEAD_DIM : (index + 1) * HEAD_DIM] for index in range(4)
+    )
     scores = jnp.where(allowed, dot(queries, key_rows, CONTRACT_LAST) * SCALING, -1e30)
     raised = jnp.exp(scores - jnp.max(scores, axis=-1, keepdims=True))
     softmax_out = raised / jnp.sum(raised, axis=-1, keepdims=True)
@@ -233,13 +258,14 @@
     grad_scores = (softmax_out * (grad_probs - inner) * SCALING).astype(jnp.bfloat16)
     grad_query = dot(grad_scores, key_rows).astype(jnp.bfloat16)
     grad_key = dot(grad_scores, queries, CONTRACT_FIRST).astype(jnp.bfloat16)
-    results = jnp.concatenate([grad_query, grad_key, grad_value, attended], axis=1)
-    back[...] = dot(place, results).astype(jnp.bfloat16)
-
-
-def attend(moved, receive, segments):
+    return jnp.concatenate([grad_query, grad_key, grad_value, attended], axis=1)
+
+
+def attend(moved, receive, segments, mask):
     out = shape(jnp.bfloat16, *moved.shape)
-    return call(attend_kernel, "attend", out, (moved, receive, segments), first=VMEM)
+    if moved.shape[0] == receive.shape[1]:
+        return call(attend_kernel, "attend", out, (moved, mask), first=VMEM)
+    return call(attend_sparse_kernel, "attend", out, (moved, receive, segments), first=VMEM)
 
 
 def write_parts(value, out):
@@ -427,7 +453,7 @@
         owner_segments.reshape(1, rows),
         width,
     )
-    send, receive, segments = indices
+    send, receive, segments, mask = indices
     squares, part = begin(inputs, x1, cotangent, here)
 
     x2, c2, gain_far, squares, part = lax.optimization_barrier((x2, c2, gain_far, squares, part))
@@ -448,7 +474,7 @@
     )
     near_turned = swap(after(near_turned, home), 1, tensor)
     there = swap(after(there, home), 2, tensor)
-    back = attend(move(bucket), receive, segments)
+    back = attend(move(bucket), receive, segments, mask)
     own, own_extras = bring_home(move(back), send, home)
 
     near = swap(own, 1, tensor)

time: 75.8 us -> 75.3 us (level)
  no operation moved by 1% of the time
where the time goes in v20:
time: 75.3 us; the launch traced here: 74.9 us
  blocking collectives  22.7 us (30%)
  waiting for transfers between devices  15.9 us (21%)
  Pallas kernels  13.6 us (18%)
  starting transfers between devices  12.7 us (17%)
  local copies, waits for them, and re-layouts  9.26 us (12%)
  between operations  0.78 us (1%)
    all_to_all x2, blocking collectives, move(): return lax.all_to_all(bucket, 'dp', split_axis=0, concat_axis=0, tiled=True)  22.7 us
    ppermute x17, waiting for transfers between devices, swap(): return lax.ppermute(array, 'tensor', [(i, i ^ mask) for i in range(count)])  15.9 us
    ppermute x17, starting transfers between devices, swap(): return lax.ppermute(array, 'tensor', [(i, i ^ mask) for i in range(count)])  12.7 us
    pallas_call x9, Pallas kernels, call(): pl.pallas_call(kernel, out_shape=shapes, in_specs=[first] + [rest] * (len...  9.81 us
    unnamed x22, local copies, waits for them, and re-layouts  8.57 us
    pallas_call x4, Pallas kernels, spread(): pl.pallas_call(spread_kernel(first), out_shape=shape(dtype, own.shape[0],...  1.76 us
  transfers between devices with their start and end apart: 17, of which 8 were waited for; matrix products, arithmetic and copies ran while one was open for 1% of the time, Pallas kernels for 14%

profile of v20, /device:TPU:0, one launch (start us, length us, event | category | flops | bytes accessed | tf_op | source)
XLA Modules:
  0.0 74.9 jit_solution(17819379796593654330)
XLA Ops:
  1.2 2.9 %collective-permute-start.1 = (bf16[128,2048]{1,0:T(8,128)(2,1)}, bf16[128,2048]{1,0:T(8,128)(2,1)S(1)}, u32[]{:S(2)}, u32[]{:S(2)}) collective-permute-start(bf16[128,2048]{1,0:T(8,128)(2,1)} %inputs.3), channel_id=1, source_target_pairs={{0,2},{1,3},{2,0},{3,1},{4,6},{5,7},{6,4},{7,5},{8,10},{9,11},{10,... | collective-permute-start | bytes 1572872 | tf_op jit(solution)/shard_map/ppermute | solution.py:46
  4.9 1.2 %collective-permute-done.3 = bf16[1,2048]{1,0:T(2,128)(2,1)S(1)} collective-permute-done((bf16[1,2048]{1,0:T(2,128)(2,1)S(1)}, bf16[1,2048]{1,0:T(2,128)(2,1)S(1)}, u32[]{:S(2)}, u32[]{:S(2)}) %collective-permute-start.3) | collective-permute-done | bytes 4128 | tf_op jit(solution)/shard_map/ppermute | solution.py:46
  6.1 2.6 %collective-permute-start.4 = (bf16[2,2048]{1,0:T(2,128)(2,1)S(1)}, bf16[2,2048]{1,0:T(2,128)(2,1)S(1)}, u32[]{:S(2)}, u32[]{:S(2)}) collective-permute-start(bf16[2,2048]{1,0:T(2,128)(2,1)S(1)} %pad_maximum_fusion.gain_chip), channel_id=1, source_target_pairs={{0,2},{1,3},{2,0},{3,1},{4,6},{5,7},{6,4},{7,5},{8,10},{9,11},{10,... | collective-permute-start | bytes 24584 | tf_op jit(solution)/shard_map/ppermute | solution.py:46
  8.7 1.6 %copy-done = bf16[8192,128]{1,0:T(8,128)(2,1)S(1)} copy-done((bf16[8192,128]{1,0:T(8,128)(2,1)S(1)}, bf16[8192,128]{1,0:T(8,128)(2,1)}, u32[]{:S(2)}) %copy-start) | copy-done | bytes 2097176
  10.3 1.6 %copy-done.2 = bf16[8192,128]{1,0:T(8,128)(2,1)S(1)} copy-done((bf16[8192,128]{1,0:T(8,128)(2,1)S(1)}, bf16[8192,128]{1,0:T(8,128)(2,1)}, u32[]{:S(2)}) %copy-start.2) | copy-done | bytes 2097176
  11.9 1.6 %copy-done.4 = bf16[8192,128]{1,0:T(8,128)(2,1)S(1)} copy-done((bf16[8192,128]{1,0:T(8,128)(2,1)S(1)}, bf16[8192,128]{1,0:T(8,128)(2,1)}, u32[]{:S(2)}) %copy-start.4) | copy-done | bytes 2097176
  13.5 1.6 %copy-done.7 = bf16[128,8192]{1,0:T(8,128)(2,1)S(1)} copy-done((bf16[128,8192]{1,0:T(8,128)(2,1)S(1)}, bf16[128,8192]{1,0:T(8,128)(2,1)}, u32[]{:S(2)}) %copy-start.7) | copy-done | bytes 2097176
  17.0 4.1 %prepare.1 = (bf16[384,4096]{1,0:T(8,128)(2,1)S(1)}, bf16[384,4096]{1,0:T(8,128)(2,1)S(1)}, bf16[256,2048]{1,0:T(8,128)(2,1)S(1)}, bf16[256,2048]{1,0:T(8,128)(2...) custom-call(s32[4]{0:T(128)S(1)} %iota_xor_fusion.order, ...), custom_call_target="tpu_custom_call" | custom-call | flops 1000 | bytes 1000 | tf_op jit(solution)/shard_map/prepare/pallas_call | solution.py:28
  21.7 6.2 %collective-permute-done.4.gain_far = bf16[2,2048]{1,0:T(2,128)(2,1)S(1)} collective-permute-done((bf16[2,2048]{1,0:T(2,128)(2,1)S(1)}, bf16[2,2048]{1,0:T(2,128)(2,1)S(1)}, u32[]{:S(2)}, u32[]{:S(2)}) %collective-permute-start.4) | collective-permute-done | bytes 8224 | tf_op jit(solution)/shard_map/ppermute | solution.py:46
  30.2 2.2 %project.1 = (bf16[128,384]{1,0:T(8,128)(2,1)S(1)}, f32[128,1]{1,0:T(8,128)S(1)}, bf16[128,512]{1,0:T(8,128)(2,1)S(1)}) custom-call(s32[4]{0:T(128)S(1)} %iota_xor_fusion.order, bf16[128,2048]{1,0:T(8,128)(2,1)S(1)} %copy-done.5, bf16[128,2048]{1,0:T(8,128)(2,1)S(1)} %collective-permute-done.x1, bf16[128,2048]{1,0:T(8,128)(2,1)S(1)} %collective-permute-done.1.x2, ...), custom_call_target="tpu_custom_call" | custom-call | flops 1000 | bytes 1000 | tf_op jit(solution)/shard_map/project/pallas_call | solution.py:28
  33.0 1.7 %collective-permute-start.11 = (bf16[256,2048]{1,0:T(8,128)(2,1)S(1)}, bf16[256,2048]{1,0:T(8,128)(2,1)S(1)}, u32[]{:S(2)}, u32[]{:S(2)}) collective-permute-start(bf16[256,2048]{1,0:T(8,128)(2,1)S(1)} %get-tuple-element.46), channel_id=1, source_target_pairs={{0,2},{1,3},{2,0},{3,1},{4,6},{5,7},{6,4},{7,5},{8,10},{9,11},{10,... | collective-permute-start | bytes 3145736 | tf_op jit(solution)/shard_map/ppermute | solution.py:46
  34.8 12.9 %all_to_all.22 = bf16[8,16,512]{2,1,0:T(8,128)(2,1)S(1)} all-to-all(bf16[8,16,512]{2,1,0:T(8,128)(2,1)S(1)} %bitcast.9), channel_id=1, replica_groups=mesh['dp'=8,'tensor'=4] {'dp'}, dimensions={0} | all-to-all | bytes 262144 | tf_op jit(solution)/shard_map/all_to_all | solution.py:414
  48.3 9.7 %all_to_all.23 = bf16[8,16,512]{2,1,0:T(8,128)(2,1)S(1)} all-to-all(bf16[8,16,512]{2,1,0:T(8,128)(2,1)S(1)} %bitcast.8), channel_id=1, replica_groups=mesh['dp'=8,'tensor'=4] {'dp'}, dimensions={0} | all-to-all | bytes 262144 | tf_op jit(solution)/shard_map/all_to_all | solution.py:414
  58.9 0.7 collective-permute-done.12.near
  60.1 0.9 %collective-permute-start.14 = (bf16[128,1024]{1,0:T(8,128)(2,1)S(1)}, bf16[128,1024]{1,0:T(8,128)(2,1)S(1)}, u32[]{:S(2)}, u32[]{:S(2)}) collective-permute-start(bf16[128,1024]{1,0:T(8,128)(2,1)S(1)} %spread_far.3), channel_id=1, source_target_pairs={{0,2},{1,3},{2,0},{3,1},{4,6},{5,7},{6,4},{7,5},{8,10},{9,11},{10,... | collective-permute-start | bytes 786440 | tf_op jit(solution)/shard_map/ppermute | solution.py:46
  61.0 1.9 %collective-permute-done.9.far = bf16[128,256]{1,0:T(8,128)(2,1)S(1)} collective-permute-done((bf16[128,256]{1,0:T(8,128)(2,1)S(1)}, bf16[128,256]{1,0:T(8,128)(2,1)S(1)}, u32[]{:S(2)}, u32[]{:S(2)}) %collective-permute-start.9) | collective-permute-done | bytes 65568 | tf_op jit(solution)/shard_map/ppermute | solution.py:46
  64.1 1.6 %collective-permute-start.16 = (bf16[128,512]{1,0:T(8,128)(2,1)S(1)}, bf16[128,512]{1,0:T(8,128)(2,1)S(1)}, u32[]{:S(2)}, u32[]{:S(2)}) collective-permute-start(bf16[128,512]{1,0:T(8,128)(2,1)S(1)} %spread_far.5), channel_id=1, source_target_pairs={{0,2},{1,3},{2,0},{3,1},{4,6},{5,7},{6,4},{7,5},{8,10},{9,11},{10,... | collective-permute-start | bytes 393224 | tf_op jit(solution)/shard_map/ppermute | solution.py:46
  65.7 1.3 %collective-permute-done.10.last = bf16[128,256]{1,0:T(8,128)(2,1)S(1)} collective-permute-done((bf16[128,256]{1,0:T(8,128)(2,1)S(1)}, bf16[128,256]{1,0:T(8,128)(2,1)S(1)}, u32[]{:S(2)}, u32[]{:S(2)}) %collective-permute-start.10) | collective-permute-done | bytes 65568 | tf_op jit(solution)/shard_map/ppermute | solution.py:46
  66.9 1.3 %finish_out.1 = bf16[128,2048]{1,0:T(8,128)(2,1)} custom-call(bf16[128,2048]{1,0:T(8,128)(2,1)S(1)} %copy-done.5, bf16[128,256]{1,0:T(8,128)(2,1)S(1)} %get-tuple-element.44.own, bf16[128,256]{1,0:T(8,128)(2,1)S(1)} %collective-permute-done.8.near, bf16[128,256]{1,0:T(8,128)(2,1)S(1)} %collective-permute-done.9.far, ...), custom_call_target="tpu_custom_call" | custom-call | flops 1000 | bytes 1000 | tf_op jit(solution)/shard_map/finish_out/pallas_call | solution.py:28
  68.2 0.7 spread_own.1.grad_own
  68.9 3.2 %collective-permute-done.15.pieces_1_ = bf16[128,512]{1,0:T(8,128)(2,1)S(1)} collective-permute-done((bf16[128,512]{1,0:T(8,128)(2,1)S(1)}, bf16[128,512]{1,0:T(8,128)(2,1)S(1)}, u32[]{:S(2)}, u32[]{:S(2)}) %collective-permute-start.15) | collective-permute-done | bytes 131104 | tf_op jit(solution)/shard_map/ppermute | solution.py:46
  72.1 1.3 %finish_most.1 = (bf16[128,2048]{1,0:T(8,128)(2,1)}, f32[128,512]{1,0:T(8,128)S(1)}) custom-call(bf16[128,2048]{1,0:T(8,128)(2,1)S(1)} %copy-done.5, bf16[128,2048]{1,0:T(8,128)(2,1)S(1)} %copy-done.6, bf16[1,2048]{1,0:T(2,128)(2,1)S(1)} %reshape.17.gain, f32[128,1]{1,0:T(8,128)S(1)} %get-tuple-element.47.inverse, ...), custom_call_target="tpu_custom_call" | custom-call | flops 1000 | bytes 1000 | tf_op jit(solution)/shard_map/finish_most/pallas_call | solution.py:392
  73.4 0.8 %collective-permute-done.16.rest = bf16[128,512]{1,0:T(8,128)(2,1)S(1)} collective-permute-done((bf16[128,512]{1,0:T(8,128)(2,1)S(1)}, bf16[128,512]{1,0:T(8,128)(2,1)S(1)}, u32[]{:S(2)}, u32[]{:S(2)}) %collective-permute-start.16) | collective-permute-done | bytes 131104 | tf_op jit(solution)/shard_map/ppermute | solution.py:46
  74.2 0.8 %finish_rest.1 = bf16[128,2048]{1,0:T(8,128)(2,1)} custom-call(bf16[1,2048]{1,0:T(2,128)(2,1)S(1)} %reshape.17.gain, f32[128,1]{1,0:T(8,128)S(1)} %get-tuple-element.47.inverse, f32[128,512]{1,0:T(8,128)S(1)} %get-tuple-element.56.left, bf16[128,512]{1,0:T(8,128)(2,1)S(1)} %collective-permute-done.16.rest, ...), custom_call_target="tpu_custom_call", output_to_operand_aliasing={{}: (4, {})} | custom-call | flops 1000 | bytes 1000 | tf_op jit(solution)/shard_map/finish_rest/pallas_call | solution.py:401
  (52 shorter events, 9.8 us)
Async XLA Ops:
  0.6 8.1 %collective-permute-start.5 = (bf16[128,8192]{1,0:T(8,128)(2,1)}, bf16[128,8192]{1,0:T(8,128)(2,1)}, u32[]{:S(2)}, u32[]{:S(2)}) collective-permute-start(bf16[128,8192]{1,0:T(8,128)(2,1)} %w_output.1), channel_id=1, source_target_pairs={{0,1},{1,0},{2,3},{3,2},{4,5},{5,4},{6,7},{7,6},{8,9},{9,8},{10,11... | collective-permute-start | bytes 6291464 | tf_op jit(solution)/shard_map/ppermute | solution.py:46
  1.1 20.0 %collective-permute-start = (bf16[128,2048]{1,0:T(8,128)(2,1)}, bf16[128,2048]{1,0:T(8,128)(2,1)S(1)}, u32[]{:S(2)}, u32[]{:S(2)}) collective-permute-start(bf16[128,2048]{1,0:T(8,128)(2,1)} %inputs.3), channel_id=1, source_target_pairs={{0,1},{1,0},{2,3},{3,2},{4,5},{5,4},{6,7},{7,6},{8,9},{9,8},{10,11... | collective-permute-start | bytes 1572872 | tf_op jit(solution)/shard_map/ppermute | solution.py:46
  1.2 26.7 %collective-permute-start.1 = (bf16[128,2048]{1,0:T(8,128)(2,1)}, bf16[128,2048]{1,0:T(8,128)(2,1)S(1)}, u32[]{:S(2)}, u32[]{:S(2)}) collective-permute-start(bf16[128,2048]{1,0:T(8,128)(2,1)} %inputs.3), channel_id=1, source_target_pairs={{0,2},{1,3},{2,0},{3,1},{4,6},{5,7},{6,4},{7,5},{8,10},{9,11},{10,... | collective-permute-start | bytes 1572872 | tf_op jit(solution)/shard_map/ppermute | solution.py:46
  4.2 23.8 %collective-permute-start.2 = (bf16[128,2048]{1,0:T(8,128)(2,1)}, bf16[128,2048]{1,0:T(8,128)(2,1)S(1)}, u32[]{:S(2)}, u32[]{:S(2)}) collective-permute-start(bf16[128,2048]{1,0:T(8,128)(2,1)} %cotangent.1), channel_id=1, source_target_pairs={{0,2},{1,3},{2,0},{3,1},{4,6},{5,7},{6,4},{7,5},{8,10},{9,11},{10,... | collective-permute-start | bytes 1572872 | tf_op jit(solution)/shard_map/ppermute | solution.py:46
  4.9 1.2 %collective-permute-start.3 = (bf16[1,2048]{1,0:T(2,128)(2,1)S(1)}, bf16[1,2048]{1,0:T(2,128)(2,1)S(1)}, u32[]{:S(2)}, u32[]{:S(2)}) collective-permute-start(bf16[1,2048]{1,0:T(2,128)(2,1)S(1)} %reshape.17.gain), channel_id=1, source_target_pairs={{0,1},{1,0},{2,3},{3,2},{4,5},{5,4},{6,7},{7,6},{8,9},{9,8},{10,11... | collective-permute-start | bytes 12296 | tf_op jit(solution)/shard_map/ppermute | solution.py:46
  6.1 21.9 %collective-permute-start.4 = (bf16[2,2048]{1,0:T(2,128)(2,1)S(1)}, bf16[2,2048]{1,0:T(2,128)(2,1)S(1)}, u32[]{:S(2)}, u32[]{:S(2)}) collective-permute-start(bf16[2,2048]{1,0:T(2,128)(2,1)S(1)} %pad_maximum_fusion.gain_chip), channel_id=1, source_target_pairs={{0,2},{1,3},{2,0},{3,1},{4,6},{5,7},{6,4},{7,5},{8,10},{9,11},{10,... | collective-permute-start | bytes 24584 | tf_op jit(solution)/shard_map/ppermute | solution.py:46
  8.7 1.6 %copy-start = (bf16[8192,128]{1,0:T(8,128)(2,1)S(1)}, bf16[8192,128]{1,0:T(8,128)(2,1)}, u32[]{:S(2)}) copy-start(bf16[8192,128]{1,0:T(8,128)(2,1)} %w_query.3) | copy-start | bytes 6291460
  10.3 1.6 %copy-start.2 = (bf16[8192,128]{1,0:T(8,128)(2,1)S(1)}, bf16[8192,128]{1,0:T(8,128)(2,1)}, u32[]{:S(2)}) copy-start(bf16[8192,128]{1,0:T(8,128)(2,1)} %w_key.3) | copy-start | bytes 6291460
  11.9 1.6 %copy-start.4 = (bf16[8192,128]{1,0:T(8,128)(2,1)S(1)}, bf16[8192,128]{1,0:T(8,128)(2,1)}, u32[]{:S(2)}) copy-start(bf16[8192,128]{1,0:T(8,128)(2,1)} %w_value.3) | copy-start | bytes 6291460
  17.0 4.1 %copy-start.5 = (bf16[128,2048]{1,0:T(8,128)(2,1)S(1)}, bf16[128,2048]{1,0:T(8,128)(2,1)}, u32[]{:S(2)}) copy-start(bf16[128,2048]{1,0:T(8,128)(2,1)} %inputs.3) | copy-start | bytes 1572868
  17.0 4.1 %copy-start.6 = (bf16[128,2048]{1,0:T(8,128)(2,1)S(1)}, bf16[128,2048]{1,0:T(8,128)(2,1)}, u32[]{:S(2)}) copy-start(bf16[128,2048]{1,0:T(8,128)(2,1)} %cotangent.1) | copy-start | bytes 1572868
  28.0 2.0 %collective-permute-start.6 = (bf16[128,2048]{1,0:T(8,128)(2,1)S(1)}, bf16[128,2048]{1,0:T(8,128)(2,1)S(1)}, u32[]{:S(2)}, u32[]{:S(2)}) collective-permute-start(bf16[128,2048]{1,0:T(8,128)(2,1)S(1)} %collective-permute-done.1.x2), channel_id=1, source_target_pairs={{0,1},{1,0},{2,3},{3,2},{4,5},{5,4},{6,7},{7,6},{8,9},{9,8},{10,11... | collective-permute-start | bytes 1572872 | tf_op jit(solution)/shard_map/ppermute | solution.py:46
  28.0 2.0 %copy-start.1 = (bf16[8192,128]{1,0:T(8,128)(2,1)S(1)}, bf16[8192,128]{1,0:T(8,128)(2,1)}, u32[]{:S(2)}) copy-start(bf16[8192,128]{1,0:T(8,128)(2,1)} %w_query.3) | copy-start | bytes 6291460
  28.0 2.2 %copy-start.3 = (bf16[8192,128]{1,0:T(8,128)(2,1)S(1)}, bf16[8192,128]{1,0:T(8,128)(2,1)}, u32[]{:S(2)}) copy-start(bf16[8192,128]{1,0:T(8,128)(2,1)} %w_key.3) | copy-start | bytes 6291460
  28.3 1.7 %collective-permute-start.7 = (f32[128,128]{1,0:T(8,128)S(1)}, f32[128,128]{1,0:T(8,128)S(1)}, u32[]{:S(2)}, u32[]{:S(2)}) collective-permute-start(f32[128,128]{1,0:T(8,128)S(1)} %add_grad.2), channel_id=1, source_target_pairs={{0,1},{1,0},{2,3},{3,2},{4,5},{5,4},{6,7},{7,6},{8,9},{9,8},{10,11... | collective-permute-start | bytes 196616 | tf_op jit(solution)/shard_map/ppermute | solution.py:46
  32.4 27.2 %collective-permute-start.13 = (bf16[384,4096]{1,0:T(8,128)(2,1)S(1)}, bf16[384,4096]{1,0:T(8,128)(2,1)S(1)}, u32[]{:S(2)}, u32[]{:S(2)}) collective-permute-start(bf16[384,4096]{1,0:T(8,128)(2,1)S(1)} %get-tuple-element.51), channel_id=1, source_target_pairs={{0,1},{1,0},{2,3},{3,2},{4,5},{5,4},{6,7},{7,6},{8,9},{9,8},{10,11... | collective-permute-start | bytes 9437192 | tf_op jit(solution)/shard_map/ppermute | solution.py:46
  33.0 33.9 %collective-permute-start.11 = (bf16[256,2048]{1,0:T(8,128)(2,1)S(1)}, bf16[256,2048]{1,0:T(8,128)(2,1)S(1)}, u32[]{:S(2)}, u32[]{:S(2)}) collective-permute-start(bf16[256,2048]{1,0:T(8,128)(2,1)S(1)} %get-tuple-element.46), channel_id=1, source_target_pairs={{0,2},{1,3},{2,0},{3,1},{4,6},{5,7},{6,4},{7,5},{8,10},{9,11},{10,... | collective-permute-start | bytes 3145736 | tf_op jit(solution)/shard_map/ppermute | solution.py:46
  58.3 1.4 %collective-permute-start.12 = (bf16[128,384]{1,0:T(8,128)(2,1)S(1)}, bf16[128,384]{1,0:T(8,128)(2,1)S(1)}, u32[]{:S(2)}, u32[]{:S(2)}) collective-permute-start(bf16[128,384]{1,0:T(8,128)(2,1)S(1)} %get-tuple-element.54.own), channel_id=1, source_target_pairs={{0,1},{1,0},{2,3},{3,2},{4,5},{5,4},{6,7},{7,6},{8,9},{9,8},{10,11... | collective-permute-start | bytes 294920 | tf_op jit(solution)/shard_map/ppermute | solution.py:46
  58.4 4.5 %collective-permute-start.9 = (bf16[128,256]{1,0:T(8,128)(2,1)S(1)}, bf16[128,256]{1,0:T(8,128)(2,1)S(1)}, u32[]{:S(2)}, u32[]{:S(2)}) collective-permute-start(bf16[128,256]{1,0:T(8,128)(2,1)S(1)} %get-tuple-element.44.own), channel_id=1, source_target_pairs={{0,2},{1,3},{2,0},{3,1},{4,6},{5,7},{6,4},{7,5},{8,10},{9,11},{10,... | collective-permute-start | bytes 196616 | tf_op jit(solution)/shard_map/ppermute | solution.py:46
  60.1 12.0 %collective-permute-start.14 = (bf16[128,1024]{1,0:T(8,128)(2,1)S(1)}, bf16[128,1024]{1,0:T(8,128)(2,1)S(1)}, u32[]{:S(2)}, u32[]{:S(2)}) collective-permute-start(bf16[128,1024]{1,0:T(8,128)(2,1)S(1)} %spread_far.3), channel_id=1, source_target_pairs={{0,2},{1,3},{2,0},{3,1},{4,6},{5,7},{6,4},{7,5},{8,10},{9,11},{10,... | collective-permute-start | bytes 786440 | tf_op jit(solution)/shard_map/ppermute | solution.py:46
  61.0 4.7 %collective-permute-start.8 = (bf16[128,256]{1,0:T(8,128)(2,1)S(1)}, bf16[128,256]{1,0:T(8,128)(2,1)S(1)}, u32[]{:S(2)}, u32[]{:S(2)}) collective-permute-start(bf16[128,256]{1,0:T(8,128)(2,1)S(1)} %get-tuple-element.44.own), channel_id=1, source_target_pairs={{0,1},{1,0},{2,3},{3,2},{4,5},{5,4},{6,7},{7,6},{8,9},{9,8},{10,11... | collective-permute-start | bytes 196616 | tf_op jit(solution)/shard_map/ppermute | solution.py:46
  63.2 8.9 %collective-permute-start.15 = (bf16[128,512]{1,0:T(8,128)(2,1)S(1)}, bf16[128,512]{1,0:T(8,128)(2,1)S(1)}, u32[]{:S(2)}, u32[]{:S(2)}) collective-permute-start(bf16[128,512]{1,0:T(8,128)(2,1)S(1)} %spread_far.4), channel_id=1, source_target_pairs={{0,2},{1,3},{2,0},{3,1},{4,6},{5,7},{6,4},{7,5},{8,10},{9,11},{10,... | collective-permute-start | bytes 393224 | tf_op jit(solution)/shard_map/ppermute | solution.py:46
  64.1 10.1 %collective-permute-start.16 = (bf16[128,512]{1,0:T(8,128)(2,1)S(1)}, bf16[128,512]{1,0:T(8,128)(2,1)S(1)}, u32[]{:S(2)}, u32[]{:S(2)}) collective-permute-start(bf16[128,512]{1,0:T(8,128)(2,1)S(1)} %spread_far.5), channel_id=1, source_target_pairs={{0,2},{1,3},{2,0},{3,1},{4,6},{5,7},{6,4},{7,5},{8,10},{9,11},{10,... | collective-permute-start | bytes 393224 | tf_op jit(solution)/shard_map/ppermute | solution.py:46
  65.7 1.3 %collective-permute-start.10 = (bf16[128,256]{1,0:T(8,128)(2,1)S(1)}, bf16[128,256]{1,0:T(8,128)(2,1)S(1)}, u32[]{:S(2)}, u32[]{:S(2)}) collective-permute-start(bf16[128,256]{1,0:T(8,128)(2,1)S(1)} %collective-permute-done.9.far), channel_id=1, source_target_pairs={{0,1},{1,0},{2,3},{3,2},{4,5},{5,4},{6,7},{7,6},{8,9},{9,8},{10,11... | collective-permute-start | bytes 196616 | tf_op jit(solution)/shard_map/ppermute | solution.py:46
  (4 other events, 3.6 us)

commit v21 on v20

--- a/solution.py
+++ b/solution.py
@@ -16,13 +16,15 @@
 VMEM = pl.BlockSpec(memory_space=pltpu.VMEM)
 SMEM = pl.BlockSpec(memory_space=pltpu.SMEM)
 TILE = 512
+SQUARES_FLOPS = 4000000000
+HOME_FLOPS = 24000000000
 
 
 def dot(left, right, dims=(((1,), (0,)), ((), ()))):
     return lax.dot_general(left, right, dims, preferred_element_type=jnp.float32)
 
 
-def call(kernel, name, out_shape, operands, scratch=(), first=SMEM, rest=VMEM):
+def call(kernel, name, out_shape, operands, scratch=(), first=SMEM, rest=VMEM, flops=1000):
     single = not isinstance(out_shape, (list, tuple))
     shapes = [out_shape] if single else list(out_shape)
     results = pl.pallas_call(
@@ -32,7 +34,7 @@
         out_specs=[VMEM] * len(shapes),
         scratch_shapes=list(scratch),
         compiler_params=pltpu.CompilerParams(vmem_limit_bytes=VMEM_LIMIT),
-        cost_estimate=pl.CostEstimate(flops=1000, bytes_accessed=1000, transcendentals=0),
+        cost_estimate=pl.CostEstimate(flops=flops, bytes_accessed=1000, transcendentals=0),
         name=name,
     )(*operands)
     return results[0] if single else results
@@ -135,14 +137,19 @@
     return jnp.sum(wide * wide, axis=-1, keepdims=True)
 
 
-def begin_kernel(x0, x1, c0, here, squares, part):
+def begin_kernel(x0, x1, c0, here, squares, part, x1_out):
+    x1_out[...] = x1[...]
     squares[...] = sum_squares(x0) + sum_squares(x1)
     part[...] = dot(c0[...], here[...], CONTRACT_LAST)
 
 
 def begin(x0, x1, c0, here):
     rows, columns = x0.shape[0], here.shape[0]
-    shapes = [shape(jnp.float32, rows, 1), shape(jnp.float32, rows, columns)]
+    shapes = [
+        shape(jnp.float32, rows, 1),
+        shape(jnp.float32, rows, columns),
+        shape(x1.dtype, *x1.shape),
+    ]
     return call(begin_kernel, "begin", shapes, (x0, x1, c0, here), first=VMEM)
 
 
@@ -166,7 +173,10 @@
 
 def add_squares(x2, squares):
     out = shape(jnp.float32, *squares.shape)
-    return call(add_squares_kernel, "add_squares", out, (x2, squares), first=VMEM)
+    operands = (x2, squares)
+    return call(
+        add_squares_kernel, "add_squares", out, operands, first=VMEM, flops=SQUARES_FLOPS
+    )
 
 
 def project_kernel(
@@ -294,7 +304,8 @@
 def bring_home(moved, send, home):
     rows = home.shape[0]
     shapes = [shape(jnp.bfloat16, rows, 3 * HEAD_DIM), shape(jnp.bfloat16, rows, 2 * HEAD_DIM)]
-    return call(bring_home_kernel, "bring_home", shapes, (moved, send, home), first=VMEM)
+    operands = (moved, send, home)
+    return call(bring_home_kernel, "bring_home", shapes, operands, first=VMEM, flops=HOME_FLOPS)
 
 
 def spread_kernel(first):
@@ -454,14 +465,14 @@
         width,
     )
     send, receive, segments, mask = indices
-    squares, part = begin(inputs, x1, cotangent, here)
+    squares, part, x1 = begin(inputs, x1, cotangent, here)
 
     x2, c2, gain_far, squares, part = lax.optimization_barrier((x2, c2, gain_far, squares, part))
     x3 = swap(x2, 1, tensor)
     near_part = add_grad(1, c2, there_turned, part)
     got_part = swap(near_part, 1, tensor)
     own_part = add_grad(0, c2, there_turned, after(part, near_part))
-    squares = add_squares(x2, squares)
+    squares = add_squares(x2, after(squares, near_part, own_part))
     home, inverse_rms, bucket = project(
         order,
         (inputs, x1, x2, x3),
@@ -473,9 +484,10 @@
         send,
     )
     near_turned = swap(after(near_turned, home), 1, tensor)
-    there = swap(after(there, home), 2, tensor)
+    there = swap(after(there, near_part), 2, tensor)
     back = attend(move(bucket), receive, segments, mask)
-    own, own_extras = bring_home(move(back), send, home)
+    moved, there = lax.optimization_barrier((move(back), there))
+    own, own_extras = bring_home(moved, send, home)
 
     near = swap(own, 1, tensor)
     far_extras = swap(own_extras, 2, tensor)

time: 75.3 us -> 75.2 us (level)
  waiting for transfers between devices: 15.9 us -> 13.7 us
  starting transfers between devices: 12.7 us -> 14.2 us
    ppermute x17, waiting for transfers between devices: 15.9 us -> 13.7 us  [swap(): return lax.ppermute(array, 'tensor', [(i, i ^ mask) for i in range(count)])]
    ppermute x17, starting transfers between devices: 12.7 us -> 14.2 us  [swap(): return lax.ppermute(array, 'tensor', [(i, i ^ mask) for i in range(count)])]
  transfers between devices with their start and end apart: 17 -> 17, of which waited for: 8 -> 7; matrix products, arithmetic and copies ran while one was open for 1% -> 1% of each run, Pallas kernels for 14% -> 17%
where the time goes in v21:
time: 75.2 us; the launch traced here: 74.8 us
  blocking collectives  23.3 us (31%)
  starting transfers between devices  14.2 us (19%)
  waiting for transfers between devices  13.7 us (18%)
  Pallas kernels  13.5 us (18%)
  local copies, waits for them, and re-layouts  9.23 us (12%)
  between operations  0.77 us (1%)
    all_to_all x2, blocking collectives, move(): return lax.all_to_all(bucket, 'dp', split_axis=0, concat_axis=0, tiled=True)  23.3 us
    ppermute x17, starting transfers between devices, swap(): return lax.ppermute(array, 'tensor', [(i, i ^ mask) for i in range(count)])  14.2 us
    ppermute x17, waiting for transfers between devices, swap(): return lax.ppermute(array, 'tensor', [(i, i ^ mask) for i in range(count)])  13.7 us
    pallas_call x9, Pallas kernels, call(): pl.pallas_call(kernel, out_shape=shapes, in_specs=[first] + [rest] * (len...  9.71 us
    unnamed x22, local copies, waits for them, and re-layouts  8.54 us
    pallas_call x4, Pallas kernels, spread(): pl.pallas_call(spread_kernel(first), out_shape=shape(dtype, own.shape[0],...  1.76 us
  transfers between devices with their start and end apart: 17, of which 7 were waited for; matrix products, arithmetic and copies ran while one was open for 1% of the time, Pallas kernels for 17%

profile of v21, /device:TPU:0, one launch (start us, length us, event | category | flops | bytes accessed | tf_op | source)
XLA Modules:
  0.0 74.8 jit_solution(14737018051280514852)
XLA Ops:
  1.2 2.9 %collective-permute-start.2 = (bf16[128,2048]{1,0:T(8,128)(2,1)}, bf16[128,2048]{1,0:T(8,128)(2,1)S(1)}, u32[]{:S(2)}, u32[]{:S(2)}) collective-permute-start(bf16[128,2048]{1,0:T(8,128)(2,1)} %inputs.3), channel_id=1, source_target_pairs={{0,2},{1,3},{2,0},{3,1},{4,6},{5,7},{6,4},{7,5},{8,10},{9,11},{10,... | collective-permute-start | bytes 1572872 | tf_op jit(solution)/shard_map/ppermute | solution.py:48
  4.9 1.2 %collective-permute-done.4 = bf16[1,2048]{1,0:T(2,128)(2,1)S(1)} collective-permute-done((bf16[1,2048]{1,0:T(2,128)(2,1)S(1)}, bf16[1,2048]{1,0:T(2,128)(2,1)S(1)}, u32[]{:S(2)}, u32[]{:S(2)}) %collective-permute-start.4) | collective-permute-done | bytes 4128 | tf_op jit(solution)/shard_map/ppermute | solution.py:48
  6.1 2.6 %collective-permute-start.5 = (bf16[2,2048]{1,0:T(2,128)(2,1)S(1)}, bf16[2,2048]{1,0:T(2,128)(2,1)S(1)}, u32[]{:S(2)}, u32[]{:S(2)}) collective-permute-start(bf16[2,2048]{1,0:T(2,128)(2,1)S(1)} %pad_maximum_fusion.gain_chip), channel_id=1, source_target_pairs={{0,2},{1,3},{2,0},{3,1},{4,6},{5,7},{6,4},{7,5},{8,10},{9,11},{10,... | collective-permute-start | bytes 24584 | tf_op jit(solution)/shard_map/ppermute | solution.py:48
  8.7 1.6 %copy-done = bf16[8192,128]{1,0:T(8,128)(2,1)S(1)} copy-done((bf16[8192,128]{1,0:T(8,128)(2,1)S(1)}, bf16[8192,128]{1,0:T(8,128)(2,1)}, u32[]{:S(2)}) %copy-start) | copy-done | bytes 2097176
  10.3 1.6 %copy-done.2 = bf16[8192,128]{1,0:T(8,128)(2,1)S(1)} copy-done((bf16[8192,128]{1,0:T(8,128)(2,1)S(1)}, bf16[8192,128]{1,0:T(8,128)(2,1)}, u32[]{:S(2)}) %copy-start.2) | copy-done | bytes 2097176
  11.9 1.6 %copy-done.4 = bf16[8192,128]{1,0:T(8,128)(2,1)S(1)} copy-done((bf16[8192,128]{1,0:T(8,128)(2,1)S(1)}, bf16[8192,128]{1,0:T(8,128)(2,1)}, u32[]{:S(2)}) %copy-start.4) | copy-done | bytes 2097176
  13.5 1.6 %copy-done.7 = bf16[128,8192]{1,0:T(8,128)(2,1)S(1)} copy-done((bf16[128,8192]{1,0:T(8,128)(2,1)S(1)}, bf16[128,8192]{1,0:T(8,128)(2,1)}, u32[]{:S(2)}) %copy-start.7) | copy-done | bytes 2097176
  17.0 3.0 %prepare.1 = (bf16[384,4096]{1,0:T(8,128)(2,1)S(1)}, bf16[384,4096]{1,0:T(8,128)(2,1)S(1)}, bf16[256,2048]{1,0:T(8,128)(2,1)S(1)}, bf16[256,2048]{1,0:T(8,128)(2...) custom-call(s32[4]{0:T(128)S(1)} %iota_xor_fusion.order, ...), custom_call_target="tpu_custom_call" | custom-call | flops 1000 | bytes 1000 | tf_op jit(solution)/shard_map/prepare/pallas_call | solution.py:30
  20.0 1.7 %begin.1 = (f32[128,1]{1,0:T(8,128)S(1)}, f32[128,256]{1,0:T(8,128)S(1)}, bf16[128,2048]{1,0:T(8,128)(2,1)S(1)}) custom-call(bf16[128,2048]{1,0:T(8,128)(2,1)S(1)} %copy-done.5, bf16[128,2048]{1,0:T(8,128)(2,1)} %collective-permute-done.x1, bf16[128,2048]{1,0:T(8,128)(2,1)S(1)} %copy-done.6, bf16[256,2048]{1,0:T(8,128)(2,1)S(1)} %get-tuple-element.34.here), custom_call_target="tpu_custom_call" | custom-call | flops 1000 | bytes 1000 | tf_op jit(solution)/shard_map/begin/pallas_call | solution.py:30
  21.7 6.3 %collective-permute-done.5.gain_far = bf16[2,2048]{1,0:T(2,128)(2,1)S(1)} collective-permute-done((bf16[2,2048]{1,0:T(2,128)(2,1)S(1)}, bf16[2,2048]{1,0:T(2,128)(2,1)S(1)}, u32[]{:S(2)}, u32[]{:S(2)}) %collective-permute-start.5) | collective-permute-done | bytes 8224 | tf_op jit(solution)/shard_map/ppermute | solution.py:48
  29.1 1.8 %collective-permute-start.8 = (bf16[256,2048]{1,0:T(8,128)(2,1)S(1)}, bf16[256,2048]{1,0:T(8,128)(2,1)S(1)}, u32[]{:S(2)}, u32[]{:S(2)}) collective-permute-start(bf16[256,2048]{1,0:T(8,128)(2,1)S(1)} %get-tuple-element.50), channel_id=1, source_target_pairs={{0,2},{1,3},{2,0},{3,1},{4,6},{5,7},{6,4},{7,5},{8,10},{9,11},{10,... | collective-permute-start | bytes 3145736 | tf_op jit(solution)/shard_map/ppermute | solution.py:48
  31.4 2.2 %project.1 = (bf16[128,384]{1,0:T(8,128)(2,1)S(1)}, f32[128,1]{1,0:T(8,128)S(1)}, bf16[128,512]{1,0:T(8,128)(2,1)S(1)}) custom-call(s32[4]{0:T(128)S(1)} %iota_xor_fusion.order, bf16[128,2048]{1,0:T(8,128)(2,1)S(1)} %copy-done.5, bf16[128,2048]{1,0:T(8,128)(2,1)S(1)} %get-tuple-element.35.x1, bf16[128,2048]{1,0:T(8,128)(2,1)S(1)} %collective-permute-done.2.x2, ...), custom_call_target="tpu_custom_call" | custom-call | flops 1000 | bytes 1000 | tf_op jit(solution)/shard_map/project/pallas_call | solution.py:30
  33.7 13.4 %all_to_all.23 = bf16[8,16,512]{2,1,0:T(8,128)(2,1)S(1)} all-to-all(bf16[8,16,512]{2,1,0:T(8,128)(2,1)S(1)} %bitcast.8), channel_id=1, replica_groups=mesh['dp'=8,'tensor'=4] {'dp'}, dimensions={0} | all-to-all | bytes 262144 | tf_op jit(solution)/shard_map/all_to_all | solution.py:425
  47.7 9.9 %all_to_all.24 = bf16[8,16,512]{2,1,0:T(8,128)(2,1)S(1)} all-to-all(bf16[8,16,512]{2,1,0:T(8,128)(2,1)S(1)} %bitcast.7), channel_id=1, replica_groups=mesh['dp'=8,'tensor'=4] {'dp'}, dimensions={0} | all-to-all | bytes 262144 | tf_op jit(solution)/shard_map/all_to_all | solution.py:425
  57.9 1.6 %collective-permute-start.10 = (bf16[128,256]{1,0:T(8,128)(2,1)S(1)}, bf16[128,256]{1,0:T(8,128)(2,1)S(1)}, u32[]{:S(2)}, u32[]{:S(2)}) collective-permute-start(bf16[128,256]{1,0:T(8,128)(2,1)S(1)} %get-tuple-element.53.own), channel_id=1, source_target_pairs={{0,2},{1,3},{2,0},{3,1},{4,6},{5,7},{6,4},{7,5},{8,10},{9,11},{10,... | collective-permute-start | bytes 196616 | tf_op jit(solution)/shard_map/ppermute | solution.py:48
  60.0 1.3 %collective-permute-start.14 = (bf16[128,1024]{1,0:T(8,128)(2,1)S(1)}, bf16[128,1024]{1,0:T(8,128)(2,1)S(1)}, u32[]{:S(2)}, u32[]{:S(2)}) collective-permute-start(bf16[128,1024]{1,0:T(8,128)(2,1)S(1)} %spread_far.3), channel_id=1, source_target_pairs={{0,2},{1,3},{2,0},{3,1},{4,6},{5,7},{6,4},{7,5},{8,10},{9,11},{10,... | collective-permute-start | bytes 786440 | tf_op jit(solution)/shard_map/ppermute | solution.py:48
  61.2 1.2 %collective-permute-done.10.far = bf16[128,256]{1,0:T(8,128)(2,1)S(1)} collective-permute-done((bf16[128,256]{1,0:T(8,128)(2,1)S(1)}, bf16[128,256]{1,0:T(8,128)(2,1)S(1)}, u32[]{:S(2)}, u32[]{:S(2)}) %collective-permute-start.10) | collective-permute-done | bytes 65568 | tf_op jit(solution)/shard_map/ppermute | solution.py:48
  62.7 1.6 %collective-permute-start.15 = (bf16[128,512]{1,0:T(8,128)(2,1)S(1)}, bf16[128,512]{1,0:T(8,128)(2,1)S(1)}, u32[]{:S(2)}, u32[]{:S(2)}) collective-permute-start(bf16[128,512]{1,0:T(8,128)(2,1)S(1)} %spread_far.4), channel_id=1, source_target_pairs={{0,2},{1,3},{2,0},{3,1},{4,6},{5,7},{6,4},{7,5},{8,10},{9,11},{10,... | collective-permute-start | bytes 393224 | tf_op jit(solution)/shard_map/ppermute | solution.py:48
  65.7 0.7 collective-permute-done.9.near
  66.6 1.3 %finish_out.1 = bf16[128,2048]{1,0:T(8,128)(2,1)} custom-call(bf16[128,2048]{1,0:T(8,128)(2,1)S(1)} %copy-done.5, bf16[128,256]{1,0:T(8,128)(2,1)S(1)} %get-tuple-element.53.own, bf16[128,256]{1,0:T(8,128)(2,1)S(1)} %collective-permute-done.9.near, bf16[128,256]{1,0:T(8,128)(2,1)S(1)} %collective-permute-done.10.far, ...), custom_call_target="tpu_custom_call" | custom-call | flops 1000 | bytes 1000 | tf_op jit(solution)/shard_map/finish_out/pallas_call | solution.py:30
  68.6 3.4 %collective-permute-done.15.pieces_1_ = bf16[128,512]{1,0:T(8,128)(2,1)S(1)} collective-permute-done((bf16[128,512]{1,0:T(8,128)(2,1)S(1)}, bf16[128,512]{1,0:T(8,128)(2,1)S(1)}, u32[]{:S(2)}, u32[]{:S(2)}) %collective-permute-start.15) | collective-permute-done | bytes 131104 | tf_op jit(solution)/shard_map/ppermute | solution.py:48
  72.0 1.2 %finish_most.1 = (bf16[128,2048]{1,0:T(8,128)(2,1)}, f32[128,512]{1,0:T(8,128)S(1)}) custom-call(bf16[128,2048]{1,0:T(8,128)(2,1)S(1)} %copy-done.5, bf16[128,2048]{1,0:T(8,128)(2,1)S(1)} %copy-done.6, bf16[1,2048]{1,0:T(2,128)(2,1)S(1)} %reshape.19.gain, f32[128,1]{1,0:T(8,128)S(1)} %get-tuple-element.55.inverse, ...), custom_call_target="tpu_custom_call" | custom-call | flops 1000 | bytes 1000 | tf_op jit(solution)/shard_map/finish_most/pallas_call | solution.py:403
  73.2 0.8 %collective-permute-done.16.rest = bf16[128,512]{1,0:T(8,128)(2,1)S(1)} collective-permute-done((bf16[128,512]{1,0:T(8,128)(2,1)S(1)}, bf16[128,512]{1,0:T(8,128)(2,1)S(1)}, u32[]{:S(2)}, u32[]{:S(2)}) %collective-permute-start.16) | collective-permute-done | bytes 131104 | tf_op jit(solution)/shard_map/ppermute | solution.py:48
  74.0 0.8 %finish_rest.1 = bf16[128,2048]{1,0:T(8,128)(2,1)} custom-call(bf16[1,2048]{1,0:T(2,128)(2,1)S(1)} %reshape.19.gain, f32[128,1]{1,0:T(8,128)S(1)} %get-tuple-element.55.inverse, f32[128,512]{1,0:T(8,128)S(1)} %get-tuple-element.64.left, bf16[128,512]{1,0:T(8,128)(2,1)S(1)} %collective-permute-done.16.rest, ...), custom_call_target="tpu_custom_call", output_to_operand_aliasing={{}: (4, {})} | custom-call | flops 1000 | bytes 1000 | tf_op jit(solution)/shard_map/finish_rest/pallas_call | solution.py:412
  (52 shorter events, 8.9 us)
Async XLA Ops:
  0.6 8.1 %collective-permute-start.1 = (bf16[128,8192]{1,0:T(8,128)(2,1)}, bf16[128,8192]{1,0:T(8,128)(2,1)S(1)}, u32[]{:S(2)}, u32[]{:S(2)}) collective-permute-start(bf16[128,8192]{1,0:T(8,128)(2,1)} %w_output.1), channel_id=1, source_target_pairs={{0,1},{1,0},{2,3},{3,2},{4,5},{5,4},{6,7},{7,6},{8,9},{9,8},{10,11... | collective-permute-start | bytes 6291464 | tf_op jit(solution)/shard_map/ppermute | solution.py:48
  1.1 18.9 %collective-permute-start = (bf16[128,2048]{1,0:T(8,128)(2,1)}, bf16[128,2048]{1,0:T(8,128)(2,1)}, u32[]{:S(2)}, u32[]{:S(2)}) collective-permute-start(bf16[128,2048]{1,0:T(8,128)(2,1)} %inputs.3), channel_id=1, source_target_pairs={{0,1},{1,0},{2,3},{3,2},{4,5},{5,4},{6,7},{7,6},{8,9},{9,8},{10,11... | collective-permute-start | bytes 1572872 | tf_op jit(solution)/shard_map/ppermute | solution.py:48
  1.2 26.7 %collective-permute-start.2 = (bf16[128,2048]{1,0:T(8,128)(2,1)}, bf16[128,2048]{1,0:T(8,128)(2,1)S(1)}, u32[]{:S(2)}, u32[]{:S(2)}) collective-permute-start(bf16[128,2048]{1,0:T(8,128)(2,1)} %inputs.3), channel_id=1, source_target_pairs={{0,2},{1,3},{2,0},{3,1},{4,6},{5,7},{6,4},{7,5},{8,10},{9,11},{10,... | collective-permute-start | bytes 1572872 | tf_op jit(solution)/shard_map/ppermute | solution.py:48
  4.2 23.8 %collective-permute-start.3 = (bf16[128,2048]{1,0:T(8,128)(2,1)}, bf16[128,2048]{1,0:T(8,128)(2,1)S(1)}, u32[]{:S(2)}, u32[]{:S(2)}) collective-permute-start(bf16[128,2048]{1,0:T(8,128)(2,1)} %cotangent.1), channel_id=1, source_target_pairs={{0,2},{1,3},{2,0},{3,1},{4,6},{5,7},{6,4},{7,5},{8,10},{9,11},{10,... | collective-permute-start | bytes 1572872 | tf_op jit(solution)/shard_map/ppermute | solution.py:48
  4.9 1.2 %collective-permute-start.4 = (bf16[1,2048]{1,0:T(2,128)(2,1)S(1)}, bf16[1,2048]{1,0:T(2,128)(2,1)S(1)}, u32[]{:S(2)}, u32[]{:S(2)}) collective-permute-start(bf16[1,2048]{1,0:T(2,128)(2,1)S(1)} %reshape.19.gain), channel_id=1, source_target_pairs={{0,1},{1,0},{2,3},{3,2},{4,5},{5,4},{6,7},{7,6},{8,9},{9,8},{10,11... | collective-permute-start | bytes 12296 | tf_op jit(solution)/shard_map/ppermute | solution.py:48
  6.1 21.9 %collective-permute-start.5 = (bf16[2,2048]{1,0:T(2,128)(2,1)S(1)}, bf16[2,2048]{1,0:T(2,128)(2,1)S(1)}, u32[]{:S(2)}, u32[]{:S(2)}) collective-permute-start(bf16[2,2048]{1,0:T(2,128)(2,1)S(1)} %pad_maximum_fusion.gain_chip), channel_id=1, source_target_pairs={{0,2},{1,3},{2,0},{3,1},{4,6},{5,7},{6,4},{7,5},{8,10},{9,11},{10,... | collective-permute-start | bytes 24584 | tf_op jit(solution)/shard_map/ppermute | solution.py:48
  8.7 1.6 %copy-start = (bf16[8192,128]{1,0:T(8,128)(2,1)S(1)}, bf16[8192,128]{1,0:T(8,128)(2,1)}, u32[]{:S(2)}) copy-start(bf16[8192,128]{1,0:T(8,128)(2,1)} %w_query.3) | copy-start | bytes 6291460
  10.3 1.6 %copy-start.2 = (bf16[8192,128]{1,0:T(8,128)(2,1)S(1)}, bf16[8192,128]{1,0:T(8,128)(2,1)}, u32[]{:S(2)}) copy-start(bf16[8192,128]{1,0:T(8,128)(2,1)} %w_key.3) | copy-start | bytes 6291460
  11.9 1.6 %copy-start.4 = (bf16[8192,128]{1,0:T(8,128)(2,1)S(1)}, bf16[8192,128]{1,0:T(8,128)(2,1)}, u32[]{:S(2)}) copy-start(bf16[8192,128]{1,0:T(8,128)(2,1)} %w_value.3) | copy-start | bytes 6291460
  17.0 3.0 %copy-start.5 = (bf16[128,2048]{1,0:T(8,128)(2,1)S(1)}, bf16[128,2048]{1,0:T(8,128)(2,1)}, u32[]{:S(2)}) copy-start(bf16[128,2048]{1,0:T(8,128)(2,1)} %inputs.3) | copy-start | bytes 1572868
  17.0 3.0 %copy-start.6 = (bf16[128,2048]{1,0:T(8,128)(2,1)S(1)}, bf16[128,2048]{1,0:T(8,128)(2,1)}, u32[]{:S(2)}) copy-start(bf16[128,2048]{1,0:T(8,128)(2,1)} %cotangent.1) | copy-start | bytes 1572868
  28.0 3.2 %collective-permute-start.6 = (bf16[128,2048]{1,0:T(8,128)(2,1)S(1)}, bf16[128,2048]{1,0:T(8,128)(2,1)S(1)}, u32[]{:S(2)}, u32[]{:S(2)}) collective-permute-start(bf16[128,2048]{1,0:T(8,128)(2,1)S(1)} %collective-permute-done.2.x2), channel_id=1, source_target_pairs={{0,1},{1,0},{2,3},{3,2},{4,5},{5,4},{6,7},{7,6},{8,9},{9,8},{10,11... | collective-permute-start | bytes 1572872 | tf_op jit(solution)/shard_map/ppermute | solution.py:48
  28.3 2.9 %collective-permute-start.7 = (f32[128,128]{1,0:T(8,128)S(1)}, f32[128,128]{1,0:T(8,128)S(1)}, u32[]{:S(2)}, u32[]{:S(2)}) collective-permute-start(f32[128,128]{1,0:T(8,128)S(1)} %add_grad.2), channel_id=1, source_target_pairs={{0,1},{1,0},{2,3},{3,2},{4,5},{5,4},{6,7},{7,6},{8,9},{9,8},{10,11... | collective-permute-start | bytes 196616 | tf_op jit(solution)/shard_map/ppermute | solution.py:48
  29.1 2.0 %copy-start.1 = (bf16[8192,128]{1,0:T(8,128)(2,1)S(1)}, bf16[8192,128]{1,0:T(8,128)(2,1)}, u32[]{:S(2)}) copy-start(bf16[8192,128]{1,0:T(8,128)(2,1)} %w_query.3) | copy-start | bytes 6291460
  29.1 2.2 %copy-start.3 = (bf16[8192,128]{1,0:T(8,128)(2,1)S(1)}, bf16[8192,128]{1,0:T(8,128)(2,1)}, u32[]{:S(2)}) copy-start(bf16[8192,128]{1,0:T(8,128)(2,1)} %w_key.3) | copy-start | bytes 6291460
  29.1 28.4 %collective-permute-start.8 = (bf16[256,2048]{1,0:T(8,128)(2,1)S(1)}, bf16[256,2048]{1,0:T(8,128)(2,1)S(1)}, u32[]{:S(2)}, u32[]{:S(2)}) collective-permute-start(bf16[256,2048]{1,0:T(8,128)(2,1)S(1)} %get-tuple-element.50), channel_id=1, source_target_pairs={{0,2},{1,3},{2,0},{3,1},{4,6},{5,7},{6,4},{7,5},{8,10},{9,11},{10,... | collective-permute-start | bytes 3145736 | tf_op jit(solution)/shard_map/ppermute | solution.py:48
  33.6 25.9 %collective-permute-start.13 = (bf16[384,4096]{1,0:T(8,128)(2,1)S(1)}, bf16[384,4096]{1,0:T(8,128)(2,1)S(1)}, u32[]{:S(2)}, u32[]{:S(2)}) collective-permute-start(bf16[384,4096]{1,0:T(8,128)(2,1)S(1)} %get-tuple-element.59), channel_id=1, source_target_pairs={{0,1},{1,0},{2,3},{3,2},{4,5},{5,4},{6,7},{7,6},{8,9},{9,8},{10,11... | collective-permute-start | bytes 9437192 | tf_op jit(solution)/shard_map/ppermute | solution.py:48
  57.8 1.7 %collective-permute-start.12 = (bf16[128,384]{1,0:T(8,128)(2,1)S(1)}, bf16[128,384]{1,0:T(8,128)(2,1)S(1)}, u32[]{:S(2)}, u32[]{:S(2)}) collective-permute-start(bf16[128,384]{1,0:T(8,128)(2,1)S(1)} %get-tuple-element.62.own), channel_id=1, source_target_pairs={{0,1},{1,0},{2,3},{3,2},{4,5},{5,4},{6,7},{7,6},{8,9},{9,8},{10,11... | collective-permute-start | bytes 294920 | tf_op jit(solution)/shard_map/ppermute | solution.py:48
  57.9 4.5 %collective-permute-start.10 = (bf16[128,256]{1,0:T(8,128)(2,1)S(1)}, bf16[128,256]{1,0:T(8,128)(2,1)S(1)}, u32[]{:S(2)}, u32[]{:S(2)}) collective-permute-start(bf16[128,256]{1,0:T(8,128)(2,1)S(1)} %get-tuple-element.53.own), channel_id=1, source_target_pairs={{0,2},{1,3},{2,0},{3,1},{4,6},{5,7},{6,4},{7,5},{8,10},{9,11},{10,... | collective-permute-start | bytes 196616 | tf_op jit(solution)/shard_map/ppermute | solution.py:48
  60.0 12.0 %collective-permute-start.14 = (bf16[128,1024]{1,0:T(8,128)(2,1)S(1)}, bf16[128,1024]{1,0:T(8,128)(2,1)S(1)}, u32[]{:S(2)}, u32[]{:S(2)}) collective-permute-start(bf16[128,1024]{1,0:T(8,128)(2,1)S(1)} %spread_far.3), channel_id=1, source_target_pairs={{0,2},{1,3},{2,0},{3,1},{4,6},{5,7},{6,4},{7,5},{8,10},{9,11},{10,... | collective-permute-start | bytes 786440 | tf_op jit(solution)/shard_map/ppermute | solution.py:48
  62.7 9.2 %collective-permute-start.15 = (bf16[128,512]{1,0:T(8,128)(2,1)S(1)}, bf16[128,512]{1,0:T(8,128)(2,1)S(1)}, u32[]{:S(2)}, u32[]{:S(2)}) collective-permute-start(bf16[128,512]{1,0:T(8,128)(2,1)S(1)} %spread_far.4), channel_id=1, source_target_pairs={{0,2},{1,3},{2,0},{3,1},{4,6},{5,7},{6,4},{7,5},{8,10},{9,11},{10,... | collective-permute-start | bytes 393224 | tf_op jit(solution)/shard_map/ppermute | solution.py:48
  64.6 9.4 %collective-permute-start.16 = (bf16[128,512]{1,0:T(8,128)(2,1)S(1)}, bf16[128,512]{1,0:T(8,128)(2,1)S(1)}, u32[]{:S(2)}, u32[]{:S(2)}) collective-permute-start(bf16[128,512]{1,0:T(8,128)(2,1)S(1)} %spread_far.5), channel_id=1, source_target_pairs={{0,2},{1,3},{2,0},{3,1},{4,6},{5,7},{6,4},{7,5},{8,10},{9,11},{10,... | collective-permute-start | bytes 393224 | tf_op jit(solution)/shard_map/ppermute | solution.py:48
  65.2 1.3 %collective-permute-start.9 = (bf16[128,256]{1,0:T(8,128)(2,1)S(1)}, bf16[128,256]{1,0:T(8,128)(2,1)S(1)}, u32[]{:S(2)}, u32[]{:S(2)}) collective-permute-start(bf16[128,256]{1,0:T(8,128)(2,1)S(1)} %get-tuple-element.53.own), channel_id=1, source_target_pairs={{0,1},{1,0},{2,3},{3,2},{4,5},{5,4},{6,7},{7,6},{8,9},{9,8},{10,11... | collective-permute-start | bytes 196616 | tf_op jit(solution)/shard_map/ppermute | solution.py:48
  65.2 1.4 %collective-permute-start.11 = (bf16[128,256]{1,0:T(8,128)(2,1)S(1)}, bf16[128,256]{1,0:T(8,128)(2,1)S(1)}, u32[]{:S(2)}, u32[]{:S(2)}) collective-permute-start(bf16[128,256]{1,0:T(8,128)(2,1)S(1)} %collective-permute-done.10.far), channel_id=1, source_target_pairs={{0,1},{1,0},{2,3},{3,2},{4,5},{5,4},{6,7},{7,6},{8,9},{9,8},{10,11... | collective-permute-start | bytes 196616 | tf_op jit(solution)/shard_map/ppermute | solution.py:48
  (4 other events, 3.6 us)

commit v22 on v20

--- a/solution.py
+++ b/solution.py
@@ -299,10 +299,11 @@
 
 def spread_kernel(first):
     def kernel(own, near, weights, near_weights, out):
-        own_rows, near_rows = own[...], near[...]
+        both_rows = jnp.concatenate([own[...], near[...]], axis=1)
         for start in range(0, out.shape[1], TILE):
             columns = slice(first + start, first + start + TILE)
-            total = dot(own_rows, weights[:, columns]) + dot(near_rows, near_weights[:, columns])
+            both = jnp.concatenate([weights[:, columns], near_weights[:, columns]], axis=0)
+            total = dot(both_rows, both)
             out[:, start : start + TILE] = total.astype(out.dtype)
 
     return kernel

time: 75.3 us -> 75.2 us (level)
  no operation moved by 1% of the time
where the time goes in v22:
time: 75.2 us; the launch traced here: 74.9 us
  blocking collectives  22.7 us (30%)
  waiting for transfers between devices  16.1 us (21%)
  Pallas kernels  13.4 us (18%)
  starting transfers between devices  12.7 us (17%)
  local copies, waits for them, and re-layouts  9.26 us (12%)
  between operations  0.77 us (1%)
    all_to_all x2, blocking collectives, move(): return lax.all_to_all(bucket, 'dp', split_axis=0, concat_axis=0, tiled=True)  22.7 us
    ppermute x17, waiting for transfers between devices, swap(): return lax.ppermute(array, 'tensor', [(i, i ^ mask) for i in range(count)])  16.1 us
    ppermute x17, starting transfers between devices, swap(): return lax.ppermute(array, 'tensor', [(i, i ^ mask) for i in range(count)])  12.7 us
    pallas_call x9, Pallas kernels, call(): pl.pallas_call(kernel, out_shape=shapes, in_specs=[first] + [rest] * (len...  9.81 us
    unnamed x22, local copies, waits for them, and re-layouts  8.57 us
    pallas_call x4, Pallas kernels, spread(): pl.pallas_call(spread_kernel(first), out_shape=shape(dtype, own.shape[0],...  1.55 us
  transfers between devices with their start and end apart: 17, of which 8 were waited for; matrix products, arithmetic and copies ran while one was open for 1% of the time, Pallas kernels for 14%

profile of v22, /device:TPU:0, one launch (start us, length us, event | category | flops | bytes accessed | tf_op | source)
XLA Modules:
  0.0 74.9 jit_solution(16928228877203424004)
XLA Ops:
  1.2 2.9 %collective-permute-start.1 = (bf16[128,2048]{1,0:T(8,128)(2,1)}, bf16[128,2048]{1,0:T(8,128)(2,1)S(1)}, u32[]{:S(2)}, u32[]{:S(2)}) collective-permute-start(bf16[128,2048]{1,0:T(8,128)(2,1)} %inputs.3), channel_id=1, source_target_pairs={{0,2},{1,3},{2,0},{3,1},{4,6},{5,7},{6,4},{7,5},{8,10},{9,11},{10,... | collective-permute-start | bytes 1572872 | tf_op jit(solution)/shard_map/ppermute | solution.py:46
  4.2 0.7 reshape.17.gain
  4.9 1.2 %collective-permute-done.3 = bf16[1,2048]{1,0:T(2,128)(2,1)S(1)} collective-permute-done((bf16[1,2048]{1,0:T(2,128)(2,1)S(1)}, bf16[1,2048]{1,0:T(2,128)(2,1)S(1)}, u32[]{:S(2)}, u32[]{:S(2)}) %collective-permute-start.3) | collective-permute-done | bytes 4128 | tf_op jit(solution)/shard_map/ppermute | solution.py:46
  6.1 2.6 %collective-permute-start.4 = (bf16[2,2048]{1,0:T(2,128)(2,1)S(1)}, bf16[2,2048]{1,0:T(2,128)(2,1)S(1)}, u32[]{:S(2)}, u32[]{:S(2)}) collective-permute-start(bf16[2,2048]{1,0:T(2,128)(2,1)S(1)} %pad_maximum_fusion.gain_chip), channel_id=1, source_target_pairs={{0,2},{1,3},{2,0},{3,1},{4,6},{5,7},{6,4},{7,5},{8,10},{9,11},{10,... | collective-permute-start | bytes 24584 | tf_op jit(solution)/shard_map/ppermute | solution.py:46
  8.7 1.6 %copy-done = bf16[8192,128]{1,0:T(8,128)(2,1)S(1)} copy-done((bf16[8192,128]{1,0:T(8,128)(2,1)S(1)}, bf16[8192,128]{1,0:T(8,128)(2,1)}, u32[]{:S(2)}) %copy-start) | copy-done | bytes 2097176
  10.3 1.6 %copy-done.2 = bf16[8192,128]{1,0:T(8,128)(2,1)S(1)} copy-done((bf16[8192,128]{1,0:T(8,128)(2,1)S(1)}, bf16[8192,128]{1,0:T(8,128)(2,1)}, u32[]{:S(2)}) %copy-start.2) | copy-done | bytes 2097176
  11.9 1.6 %copy-done.4 = bf16[8192,128]{1,0:T(8,128)(2,1)S(1)} copy-done((bf16[8192,128]{1,0:T(8,128)(2,1)S(1)}, bf16[8192,128]{1,0:T(8,128)(2,1)}, u32[]{:S(2)}) %copy-start.4) | copy-done | bytes 2097176
  13.5 1.6 %copy-done.7 = bf16[128,8192]{1,0:T(8,128)(2,1)S(1)} copy-done((bf16[128,8192]{1,0:T(8,128)(2,1)S(1)}, bf16[128,8192]{1,0:T(8,128)(2,1)}, u32[]{:S(2)}) %copy-start.7) | copy-done | bytes 2097176
  17.0 4.1 %prepare.1 = (bf16[384,4096]{1,0:T(8,128)(2,1)S(1)}, bf16[384,4096]{1,0:T(8,128)(2,1)S(1)}, bf16[256,2048]{1,0:T(8,128)(2,1)S(1)}, bf16[256,2048]{1,0:T(8,128)(2...) custom-call(s32[4]{0:T(128)S(1)} %iota_xor_fusion.order, ...), custom_call_target="tpu_custom_call" | custom-call | flops 1000 | bytes 1000 | tf_op jit(solution)/shard_map/prepare/pallas_call | solution.py:28
  21.7 6.2 %collective-permute-done.4.gain_far = bf16[2,2048]{1,0:T(2,128)(2,1)S(1)} collective-permute-done((bf16[2,2048]{1,0:T(2,128)(2,1)S(1)}, bf16[2,2048]{1,0:T(2,128)(2,1)S(1)}, u32[]{:S(2)}, u32[]{:S(2)}) %collective-permute-start.4) | collective-permute-done | bytes 8224 | tf_op jit(solution)/shard_map/ppermute | solution.py:46
  30.2 2.2 %project.1 = (bf16[128,384]{1,0:T(8,128)(2,1)S(1)}, f32[128,1]{1,0:T(8,128)S(1)}, bf16[128,512]{1,0:T(8,128)(2,1)S(1)}) custom-call(s32[4]{0:T(128)S(1)} %iota_xor_fusion.order, bf16[128,2048]{1,0:T(8,128)(2,1)S(1)} %copy-done.5, bf16[128,2048]{1,0:T(8,128)(2,1)S(1)} %collective-permute-done.x1, bf16[128,2048]{1,0:T(8,128)(2,1)S(1)} %collective-permute-done.1.x2, ...), custom_call_target="tpu_custom_call" | custom-call | flops 1000 | bytes 1000 | tf_op jit(solution)/shard_map/project/pallas_call | solution.py:28
  33.0 1.7 %collective-permute-start.11 = (bf16[256,2048]{1,0:T(8,128)(2,1)S(1)}, bf16[256,2048]{1,0:T(8,128)(2,1)S(1)}, u32[]{:S(2)}, u32[]{:S(2)}) collective-permute-start(bf16[256,2048]{1,0:T(8,128)(2,1)S(1)} %get-tuple-element.46), channel_id=1, source_target_pairs={{0,2},{1,3},{2,0},{3,1},{4,6},{5,7},{6,4},{7,5},{8,10},{9,11},{10,... | collective-permute-start | bytes 3145736 | tf_op jit(solution)/shard_map/ppermute | solution.py:46
  34.8 12.9 %all_to_all.22 = bf16[8,16,512]{2,1,0:T(8,128)(2,1)S(1)} all-to-all(bf16[8,16,512]{2,1,0:T(8,128)(2,1)S(1)} %bitcast.9), channel_id=1, replica_groups=mesh['dp'=8,'tensor'=4] {'dp'}, dimensions={0} | all-to-all | bytes 262144 | tf_op jit(solution)/shard_map/all_to_all | solution.py:415
  48.3 9.7 %all_to_all.23 = bf16[8,16,512]{2,1,0:T(8,128)(2,1)S(1)} all-to-all(bf16[8,16,512]{2,1,0:T(8,128)(2,1)S(1)} %bitcast.8), channel_id=1, replica_groups=mesh['dp'=8,'tensor'=4] {'dp'}, dimensions={0} | all-to-all | bytes 262144 | tf_op jit(solution)/shard_map/all_to_all | solution.py:415
  58.9 0.7 collective-permute-done.12.near
  60.1 0.9 %collective-permute-start.14 = (bf16[128,1024]{1,0:T(8,128)(2,1)S(1)}, bf16[128,1024]{1,0:T(8,128)(2,1)S(1)}, u32[]{:S(2)}, u32[]{:S(2)}) collective-permute-start(bf16[128,1024]{1,0:T(8,128)(2,1)S(1)} %spread_far.3), channel_id=1, source_target_pairs={{0,2},{1,3},{2,0},{3,1},{4,6},{5,7},{6,4},{7,5},{8,10},{9,11},{10,... | collective-permute-start | bytes 786440 | tf_op jit(solution)/shard_map/ppermute | solution.py:46
  60.9 2.0 %collective-permute-done.9.far = bf16[128,256]{1,0:T(8,128)(2,1)S(1)} collective-permute-done((bf16[128,256]{1,0:T(8,128)(2,1)S(1)}, bf16[128,256]{1,0:T(8,128)(2,1)S(1)}, u32[]{:S(2)}, u32[]{:S(2)}) %collective-permute-start.9) | collective-permute-done | bytes 65568 | tf_op jit(solution)/shard_map/ppermute | solution.py:46
  64.0 1.6 %collective-permute-start.16 = (bf16[128,512]{1,0:T(8,128)(2,1)S(1)}, bf16[128,512]{1,0:T(8,128)(2,1)S(1)}, u32[]{:S(2)}, u32[]{:S(2)}) collective-permute-start(bf16[128,512]{1,0:T(8,128)(2,1)S(1)} %spread_far.5), channel_id=1, source_target_pairs={{0,2},{1,3},{2,0},{3,1},{4,6},{5,7},{6,4},{7,5},{8,10},{9,11},{10,... | collective-permute-start | bytes 393224 | tf_op jit(solution)/shard_map/ppermute | solution.py:46
  65.6 1.3 %collective-permute-done.10.last = bf16[128,256]{1,0:T(8,128)(2,1)S(1)} collective-permute-done((bf16[128,256]{1,0:T(8,128)(2,1)S(1)}, bf16[128,256]{1,0:T(8,128)(2,1)S(1)}, u32[]{:S(2)}, u32[]{:S(2)}) %collective-permute-start.10) | collective-permute-done | bytes 65568 | tf_op jit(solution)/shard_map/ppermute | solution.py:46
  66.9 1.3 %finish_out.1 = bf16[128,2048]{1,0:T(8,128)(2,1)} custom-call(bf16[128,2048]{1,0:T(8,128)(2,1)S(1)} %copy-done.5, bf16[128,256]{1,0:T(8,128)(2,1)S(1)} %get-tuple-element.44.own, bf16[128,256]{1,0:T(8,128)(2,1)S(1)} %collective-permute-done.8.near, bf16[128,256]{1,0:T(8,128)(2,1)S(1)} %collective-permute-done.9.far, ...), custom_call_target="tpu_custom_call" | custom-call | flops 1000 | bytes 1000 | tf_op jit(solution)/shard_map/finish_out/pallas_call | solution.py:28
  68.8 3.3 %collective-permute-done.15.pieces_1_ = bf16[128,512]{1,0:T(8,128)(2,1)S(1)} collective-permute-done((bf16[128,512]{1,0:T(8,128)(2,1)S(1)}, bf16[128,512]{1,0:T(8,128)(2,1)S(1)}, u32[]{:S(2)}, u32[]{:S(2)}) %collective-permute-start.15) | collective-permute-done | bytes 131104 | tf_op jit(solution)/shard_map/ppermute | solution.py:46
  72.1 1.3 %finish_most.1 = (bf16[128,2048]{1,0:T(8,128)(2,1)}, f32[128,512]{1,0:T(8,128)S(1)}) custom-call(bf16[128,2048]{1,0:T(8,128)(2,1)S(1)} %copy-done.5, bf16[128,2048]{1,0:T(8,128)(2,1)S(1)} %copy-done.6, bf16[1,2048]{1,0:T(2,128)(2,1)S(1)} %reshape.17.gain, f32[128,1]{1,0:T(8,128)S(1)} %get-tuple-element.47.inverse, ...), custom_call_target="tpu_custom_call" | custom-call | flops 1000 | bytes 1000 | tf_op jit(solution)/shard_map/finish_most/pallas_call | solution.py:393
  73.4 0.8 %collective-permute-done.16.rest = bf16[128,512]{1,0:T(8,128)(2,1)S(1)} collective-permute-done((bf16[128,512]{1,0:T(8,128)(2,1)S(1)}, bf16[128,512]{1,0:T(8,128)(2,1)S(1)}, u32[]{:S(2)}, u32[]{:S(2)}) %collective-permute-start.16) | collective-permute-done | bytes 131104 | tf_op jit(solution)/shard_map/ppermute | solution.py:46
  74.1 0.8 %finish_rest.1 = bf16[128,2048]{1,0:T(8,128)(2,1)} custom-call(bf16[1,2048]{1,0:T(2,128)(2,1)S(1)} %reshape.17.gain, f32[128,1]{1,0:T(8,128)S(1)} %get-tuple-element.47.inverse, f32[128,512]{1,0:T(8,128)S(1)} %get-tuple-element.56.left, bf16[128,512]{1,0:T(8,128)(2,1)S(1)} %collective-permute-done.16.rest, ...), custom_call_target="tpu_custom_call", output_to_operand_aliasing={{}: (4, {})} | custom-call | flops 1000 | bytes 1000 | tf_op jit(solution)/shard_map/finish_rest/pallas_call | solution.py:402
  (52 shorter events, 9.6 us)
Async XLA Ops:
  0.6 8.1 %collective-permute-start.5 = (bf16[128,8192]{1,0:T(8,128)(2,1)}, bf16[128,8192]{1,0:T(8,128)(2,1)}, u32[]{:S(2)}, u32[]{:S(2)}) collective-permute-start(bf16[128,8192]{1,0:T(8,128)(2,1)} %w_output.1), channel_id=1, source_target_pairs={{0,1},{1,0},{2,3},{3,2},{4,5},{5,4},{6,7},{7,6},{8,9},{9,8},{10,11... | collective-permute-start | bytes 6291464 | tf_op jit(solution)/shard_map/ppermute | solution.py:46
  1.1 20.0 %collective-permute-start = (bf16[128,2048]{1,0:T(8,128)(2,1)}, bf16[128,2048]{1,0:T(8,128)(2,1)S(1)}, u32[]{:S(2)}, u32[]{:S(2)}) collective-permute-start(bf16[128,2048]{1,0:T(8,128)(2,1)} %inputs.3), channel_id=1, source_target_pairs={{0,1},{1,0},{2,3},{3,2},{4,5},{5,4},{6,7},{7,6},{8,9},{9,8},{10,11... | collective-permute-start | bytes 1572872 | tf_op jit(solution)/shard_map/ppermute | solution.py:46
  1.2 26.7 %collective-permute-start.1 = (bf16[128,2048]{1,0:T(8,128)(2,1)}, bf16[128,2048]{1,0:T(8,128)(2,1)S(1)}, u32[]{:S(2)}, u32[]{:S(2)}) collective-permute-start(bf16[128,2048]{1,0:T(8,128)(2,1)} %inputs.3), channel_id=1, source_target_pairs={{0,2},{1,3},{2,0},{3,1},{4,6},{5,7},{6,4},{7,5},{8,10},{9,11},{10,... | collective-permute-start | bytes 1572872 | tf_op jit(solution)/shard_map/ppermute | solution.py:46
  4.2 23.8 %collective-permute-start.2 = (bf16[128,2048]{1,0:T(8,128)(2,1)}, bf16[128,2048]{1,0:T(8,128)(2,1)S(1)}, u32[]{:S(2)}, u32[]{:S(2)}) collective-permute-start(bf16[128,2048]{1,0:T(8,128)(2,1)} %cotangent.1), channel_id=1, source_target_pairs={{0,2},{1,3},{2,0},{3,1},{4,6},{5,7},{6,4},{7,5},{8,10},{9,11},{10,... | collective-permute-start | bytes 1572872 | tf_op jit(solution)/shard_map/ppermute | solution.py:46
  4.9 1.2 %collective-permute-start.3 = (bf16[1,2048]{1,0:T(2,128)(2,1)S(1)}, bf16[1,2048]{1,0:T(2,128)(2,1)S(1)}, u32[]{:S(2)}, u32[]{:S(2)}) collective-permute-start(bf16[1,2048]{1,0:T(2,128)(2,1)S(1)} %reshape.17.gain), channel_id=1, source_target_pairs={{0,1},{1,0},{2,3},{3,2},{4,5},{5,4},{6,7},{7,6},{8,9},{9,8},{10,11... | collective-permute-start | bytes 12296 | tf_op jit(solution)/shard_map/ppermute | solution.py:46
  6.1 21.9 %collective-permute-start.4 = (bf16[2,2048]{1,0:T(2,128)(2,1)S(1)}, bf16[2,2048]{1,0:T(2,128)(2,1)S(1)}, u32[]{:S(2)}, u32[]{:S(2)}) collective-permute-start(bf16[2,2048]{1,0:T(2,128)(2,1)S(1)} %pad_maximum_fusion.gain_chip), channel_id=1, source_target_pairs={{0,2},{1,3},{2,0},{3,1},{4,6},{5,7},{6,4},{7,5},{8,10},{9,11},{10,... | collective-permute-start | bytes 24584 | tf_op jit(solution)/shard_map/ppermute | solution.py:46
  8.7 1.6 %copy-start = (bf16[8192,128]{1,0:T(8,128)(2,1)S(1)}, bf16[8192,128]{1,0:T(8,128)(2,1)}, u32[]{:S(2)}) copy-start(bf16[8192,128]{1,0:T(8,128)(2,1)} %w_query.3) | copy-start | bytes 6291460
  10.3 1.6 %copy-start.2 = (bf16[8192,128]{1,0:T(8,128)(2,1)S(1)}, bf16[8192,128]{1,0:T(8,128)(2,1)}, u32[]{:S(2)}) copy-start(bf16[8192,128]{1,0:T(8,128)(2,1)} %w_key.3) | copy-start | bytes 6291460
  11.9 1.6 %copy-start.4 = (bf16[8192,128]{1,0:T(8,128)(2,1)S(1)}, bf16[8192,128]{1,0:T(8,128)(2,1)}, u32[]{:S(2)}) copy-start(bf16[8192,128]{1,0:T(8,128)(2,1)} %w_value.3) | copy-start | bytes 6291460
  17.0 4.1 %copy-start.5 = (bf16[128,2048]{1,0:T(8,128)(2,1)S(1)}, bf16[128,2048]{1,0:T(8,128)(2,1)}, u32[]{:S(2)}) copy-start(bf16[128,2048]{1,0:T(8,128)(2,1)} %inputs.3) | copy-start | bytes 1572868
  17.0 4.1 %copy-start.6 = (bf16[128,2048]{1,0:T(8,128)(2,1)S(1)}, bf16[128,2048]{1,0:T(8,128)(2,1)}, u32[]{:S(2)}) copy-start(bf16[128,2048]{1,0:T(8,128)(2,1)} %cotangent.1) | copy-start | bytes 1572868
  28.0 2.0 %collective-permute-start.6 = (bf16[128,2048]{1,0:T(8,128)(2,1)S(1)}, bf16[128,2048]{1,0:T(8,128)(2,1)S(1)}, u32[]{:S(2)}, u32[]{:S(2)}) collective-permute-start(bf16[128,2048]{1,0:T(8,128)(2,1)S(1)} %collective-permute-done.1.x2), channel_id=1, source_target_pairs={{0,1},{1,0},{2,3},{3,2},{4,5},{5,4},{6,7},{7,6},{8,9},{9,8},{10,11... | collective-permute-start | bytes 1572872 | tf_op jit(solution)/shard_map/ppermute | solution.py:46
  28.0 2.0 %copy-start.1 = (bf16[8192,128]{1,0:T(8,128)(2,1)S(1)}, bf16[8192,128]{1,0:T(8,128)(2,1)}, u32[]{:S(2)}) copy-start(bf16[8192,128]{1,0:T(8,128)(2,1)} %w_query.3) | copy-start | bytes 6291460
  28.0 2.2 %copy-start.3 = (bf16[8192,128]{1,0:T(8,128)(2,1)S(1)}, bf16[8192,128]{1,0:T(8,128)(2,1)}, u32[]{:S(2)}) copy-start(bf16[8192,128]{1,0:T(8,128)(2,1)} %w_key.3) | copy-start | bytes 6291460
  28.3 1.7 %collective-permute-start.7 = (f32[128,128]{1,0:T(8,128)S(1)}, f32[128,128]{1,0:T(8,128)S(1)}, u32[]{:S(2)}, u32[]{:S(2)}) collective-permute-start(f32[128,128]{1,0:T(8,128)S(1)} %add_grad.2), channel_id=1, source_target_pairs={{0,1},{1,0},{2,3},{3,2},{4,5},{5,4},{6,7},{7,6},{8,9},{9,8},{10,11... | collective-permute-start | bytes 196616 | tf_op jit(solution)/shard_map/ppermute | solution.py:46
  32.4 27.2 %collective-permute-start.13 = (bf16[384,4096]{1,0:T(8,128)(2,1)S(1)}, bf16[384,4096]{1,0:T(8,128)(2,1)S(1)}, u32[]{:S(2)}, u32[]{:S(2)}) collective-permute-start(bf16[384,4096]{1,0:T(8,128)(2,1)S(1)} %get-tuple-element.51), channel_id=1, source_target_pairs={{0,1},{1,0},{2,3},{3,2},{4,5},{5,4},{6,7},{7,6},{8,9},{9,8},{10,11... | collective-permute-start | bytes 9437192 | tf_op jit(solution)/shard_map/ppermute | solution.py:46
  33.0 33.9 %collective-permute-start.11 = (bf16[256,2048]{1,0:T(8,128)(2,1)S(1)}, bf16[256,2048]{1,0:T(8,128)(2,1)S(1)}, u32[]{:S(2)}, u32[]{:S(2)}) collective-permute-start(bf16[256,2048]{1,0:T(8,128)(2,1)S(1)} %get-tuple-element.46), channel_id=1, source_target_pairs={{0,2},{1,3},{2,0},{3,1},{4,6},{5,7},{6,4},{7,5},{8,10},{9,11},{10,... | collective-permute-start | bytes 3145736 | tf_op jit(solution)/shard_map/ppermute | solution.py:46
  58.3 1.4 %collective-permute-start.12 = (bf16[128,384]{1,0:T(8,128)(2,1)S(1)}, bf16[128,384]{1,0:T(8,128)(2,1)S(1)}, u32[]{:S(2)}, u32[]{:S(2)}) collective-permute-start(bf16[128,384]{1,0:T(8,128)(2,1)S(1)} %get-tuple-element.54.own), channel_id=1, source_target_pairs={{0,1},{1,0},{2,3},{3,2},{4,5},{5,4},{6,7},{7,6},{8,9},{9,8},{10,11... | collective-permute-start | bytes 294920 | tf_op jit(solution)/shard_map/ppermute | solution.py:46
  58.4 4.5 %collective-permute-start.9 = (bf16[128,256]{1,0:T(8,128)(2,1)S(1)}, bf16[128,256]{1,0:T(8,128)(2,1)S(1)}, u32[]{:S(2)}, u32[]{:S(2)}) collective-permute-start(bf16[128,256]{1,0:T(8,128)(2,1)S(1)} %get-tuple-element.44.own), channel_id=1, source_target_pairs={{0,2},{1,3},{2,0},{3,1},{4,6},{5,7},{6,4},{7,5},{8,10},{9,11},{10,... | collective-permute-start | bytes 196616 | tf_op jit(solution)/shard_map/ppermute | solution.py:46
  60.1 12.0 %collective-permute-start.14 = (bf16[128,1024]{1,0:T(8,128)(2,1)S(1)}, bf16[128,1024]{1,0:T(8,128)(2,1)S(1)}, u32[]{:S(2)}, u32[]{:S(2)}) collective-permute-start(bf16[128,1024]{1,0:T(8,128)(2,1)S(1)} %spread_far.3), channel_id=1, source_target_pairs={{0,2},{1,3},{2,0},{3,1},{4,6},{5,7},{6,4},{7,5},{8,10},{9,11},{10,... | collective-permute-start | bytes 786440 | tf_op jit(solution)/shard_map/ppermute | solution.py:46
  60.9 4.7 %collective-permute-start.8 = (bf16[128,256]{1,0:T(8,128)(2,1)S(1)}, bf16[128,256]{1,0:T(8,128)(2,1)S(1)}, u32[]{:S(2)}, u32[]{:S(2)}) collective-permute-start(bf16[128,256]{1,0:T(8,128)(2,1)S(1)} %get-tuple-element.44.own), channel_id=1, source_target_pairs={{0,1},{1,0},{2,3},{3,2},{4,5},{5,4},{6,7},{7,6},{8,9},{9,8},{10,11... | collective-permute-start | bytes 196616 | tf_op jit(solution)/shard_map/ppermute | solution.py:46
  63.2 8.9 %collective-permute-start.15 = (bf16[128,512]{1,0:T(8,128)(2,1)S(1)}, bf16[128,512]{1,0:T(8,128)(2,1)S(1)}, u32[]{:S(2)}, u32[]{:S(2)}) collective-permute-start(bf16[128,512]{1,0:T(8,128)(2,1)S(1)} %spread_far.4), channel_id=1, source_target_pairs={{0,2},{1,3},{2,0},{3,1},{4,6},{5,7},{6,4},{7,5},{8,10},{9,11},{10,... | collective-permute-start | bytes 393224 | tf_op jit(solution)/shard_map/ppermute | solution.py:46
  64.0 10.1 %collective-permute-start.16 = (bf16[128,512]{1,0:T(8,128)(2,1)S(1)}, bf16[128,512]{1,0:T(8,128)(2,1)S(1)}, u32[]{:S(2)}, u32[]{:S(2)}) collective-permute-start(bf16[128,512]{1,0:T(8,128)(2,1)S(1)} %spread_far.5), channel_id=1, source_target_pairs={{0,2},{1,3},{2,0},{3,1},{4,6},{5,7},{6,4},{7,5},{8,10},{9,11},{10,... | collective-permute-start | bytes 393224 | tf_op jit(solution)/shard_map/ppermute | solution.py:46
  65.6 1.3 %collective-permute-start.10 = (bf16[128,256]{1,0:T(8,128)(2,1)S(1)}, bf16[128,256]{1,0:T(8,128)(2,1)S(1)}, u32[]{:S(2)}, u32[]{:S(2)}) collective-permute-start(bf16[128,256]{1,0:T(8,128)(2,1)S(1)} %collective-permute-done.9.far), channel_id=1, source_target_pairs={{0,1},{1,0},{2,3},{3,2},{4,5},{5,4},{6,7},{7,6},{8,9},{9,8},{10,11... | collective-permute-start | bytes 196616 | tf_op jit(solution)/shard_map/ppermute | solution.py:46
  (4 other events, 3.6 us)

commit v23 on v20

--- a/solution.py
+++ b/solution.py
@@ -481,7 +481,7 @@
     far_extras = swap(own_extras, 2, tensor)
     quarter = width // 4
     turn, got = own, []
-    for first, span in ((0, 2 * quarter), (2 * quarter, quarter), (3 * quarter, quarter)):
+    for first, span in ((0, 2 * quarter), (2 * quarter, 2 * quarter)):
         flops = 4 * rows * span * width if first else 1000
         sides = (turn, near, own_turned, near_turned)
         part = spread("spread_far", width + first, span, low, *sides, flops=flops)

time: 75.3 us -> 79.3 us (1.053)
  waiting for transfers between devices: 15.9 us -> 20.5 us
    ppermute x17 -> x16, waiting for transfers between devices: 15.9 us -> 20.5 us  [swap(): return lax.ppermute(array, 'tensor', [(i, i ^ mask) for i in range(count)])]
    ppermute x17 -> x16, starting transfers between devices: 12.7 us -> 12.3 us  [swap(): return lax.ppermute(array, 'tensor', [(i, i ^ mask) for i in range(count)])]
    pallas_call x4 -> x3, Pallas kernels: 1.76 us -> 1.6 us  [spread(): pl.pallas_call(spread_kernel(first), out_shape=shape(dtype, own.shape[0],...]
  transfers between devices with their start and end apart: 17 -> 16, of which waited for: 8 -> 9; matrix products, arithmetic and copies ran while one was open for 1% -> 1% of each run, Pallas kernels for 14% -> 12%
where the time goes in v23:
time: 79.3 us; the launch traced here: 78.9 us
  blocking collectives  22.7 us (29%)
  waiting for transfers between devices  20.5 us (26%)
  Pallas kernels  13.4 us (17%)
  starting transfers between devices  12.3 us (16%)
  local copies, waits for them, and re-layouts  9.26 us (12%)
    all_to_all x2, blocking collectives, move(): return lax.all_to_all(bucket, 'dp', split_axis=0, concat_axis=0, tiled=True)  22.7 us
    ppermute x16, waiting for transfers between devices, swap(): return lax.ppermute(array, 'tensor', [(i, i ^ mask) for i in range(count)])  20.5 us
    ppermute x16, starting transfers between devices, swap(): return lax.ppermute(array, 'tensor', [(i, i ^ mask) for i in range(count)])  12.3 us
    pallas_call x9, Pallas kernels, call(): pl.pallas_call(kernel, out_shape=shapes, in_specs=[first] + [rest] * (len...  9.8 us
    unnamed x22, local copies, waits for them, and re-layouts  8.57 us
    pallas_call x3, Pallas kernels, spread(): pl.pallas_call(spread_kernel(first), out_shape=shape(dtype, own.shape[0],...  1.6 us
  transfers between devices with their start and end apart: 16, of which 9 were waited for; matrix products, arithmetic and copies ran while one was open for 1% of the time, Pallas kernels for 12%

profile of v23, /device:TPU:0, one launch (start us, length us, event | category | flops | bytes accessed | tf_op | source)
XLA Modules:
  0.0 78.9 jit_solution(4782148326221496788)
XLA Ops:
  1.2 2.9 %collective-permute-start.1 = (bf16[128,2048]{1,0:T(8,128)(2,1)}, bf16[128,2048]{1,0:T(8,128)(2,1)S(1)}, u32[]{:S(2)}, u32[]{:S(2)}) collective-permute-start(bf16[128,2048]{1,0:T(8,128)(2,1)} %inputs.3), channel_id=1, source_target_pairs={{0,2},{1,3},{2,0},{3,1},{4,6},{5,7},{6,4},{7,5},{8,10},{9,11},{10,... | collective-permute-start | bytes 1572872 | tf_op jit(solution)/shard_map/ppermute | solution.py:46
  4.2 0.7 reshape.17.gain
  4.9 1.2 %collective-permute-done.3 = bf16[1,2048]{1,0:T(2,128)(2,1)S(1)} collective-permute-done((bf16[1,2048]{1,0:T(2,128)(2,1)S(1)}, bf16[1,2048]{1,0:T(2,128)(2,1)S(1)}, u32[]{:S(2)}, u32[]{:S(2)}) %collective-permute-start.3) | collective-permute-done | bytes 4128 | tf_op jit(solution)/shard_map/ppermute | solution.py:46
  6.1 2.6 %collective-permute-start.4 = (bf16[2,2048]{1,0:T(2,128)(2,1)S(1)}, bf16[2,2048]{1,0:T(2,128)(2,1)S(1)}, u32[]{:S(2)}, u32[]{:S(2)}) collective-permute-start(bf16[2,2048]{1,0:T(2,128)(2,1)S(1)} %pad_maximum_fusion.gain_chip), channel_id=1, source_target_pairs={{0,2},{1,3},{2,0},{3,1},{4,6},{5,7},{6,4},{7,5},{8,10},{9,11},{10,... | collective-permute-start | bytes 24584 | tf_op jit(solution)/shard_map/ppermute | solution.py:46
  8.7 1.6 %copy-done = bf16[8192,128]{1,0:T(8,128)(2,1)S(1)} copy-done((bf16[8192,128]{1,0:T(8,128)(2,1)S(1)}, bf16[8192,128]{1,0:T(8,128)(2,1)}, u32[]{:S(2)}) %copy-start) | copy-done | bytes 2097176
  10.3 1.6 %copy-done.2 = bf16[8192,128]{1,0:T(8,128)(2,1)S(1)} copy-done((bf16[8192,128]{1,0:T(8,128)(2,1)S(1)}, bf16[8192,128]{1,0:T(8,128)(2,1)}, u32[]{:S(2)}) %copy-start.2) | copy-done | bytes 2097176
  11.9 1.6 %copy-done.4 = bf16[8192,128]{1,0:T(8,128)(2,1)S(1)} copy-done((bf16[8192,128]{1,0:T(8,128)(2,1)S(1)}, bf16[8192,128]{1,0:T(8,128)(2,1)}, u32[]{:S(2)}) %copy-start.4) | copy-done | bytes 2097176
  13.5 1.6 %copy-done.7 = bf16[128,8192]{1,0:T(8,128)(2,1)S(1)} copy-done((bf16[128,8192]{1,0:T(8,128)(2,1)S(1)}, bf16[128,8192]{1,0:T(8,128)(2,1)}, u32[]{:S(2)}) %copy-start.7) | copy-done | bytes 2097176
  17.0 4.1 %prepare.1 = (bf16[384,4096]{1,0:T(8,128)(2,1)S(1)}, bf16[384,4096]{1,0:T(8,128)(2,1)S(1)}, bf16[256,2048]{1,0:T(8,128)(2,1)S(1)}, bf16[256,2048]{1,0:T(8,128)(2...) custom-call(s32[4]{0:T(128)S(1)} %iota_xor_fusion.order, ...), custom_call_target="tpu_custom_call" | custom-call | flops 1000 | bytes 1000 | tf_op jit(solution)/shard_map/prepare/pallas_call | solution.py:28
  21.7 6.2 %collective-permute-done.4.gain_far = bf16[2,2048]{1,0:T(2,128)(2,1)S(1)} collective-permute-done((bf16[2,2048]{1,0:T(2,128)(2,1)S(1)}, bf16[2,2048]{1,0:T(2,128)(2,1)S(1)}, u32[]{:S(2)}, u32[]{:S(2)}) %collective-permute-start.4) | collective-permute-done | bytes 8224 | tf_op jit(solution)/shard_map/ppermute | solution.py:46
  30.2 2.2 %project.1 = (bf16[128,384]{1,0:T(8,128)(2,1)S(1)}, f32[128,1]{1,0:T(8,128)S(1)}, bf16[128,512]{1,0:T(8,128)(2,1)S(1)}) custom-call(s32[4]{0:T(128)S(1)} %iota_xor_fusion.order, bf16[128,2048]{1,0:T(8,128)(2,1)S(1)} %copy-done.5, bf16[128,2048]{1,0:T(8,128)(2,1)S(1)} %collective-permute-done.x1, bf16[128,2048]{1,0:T(8,128)(2,1)S(1)} %collective-permute-done.1.x2, ...), custom_call_target="tpu_custom_call" | custom-call | flops 1000 | bytes 1000 | tf_op jit(solution)/shard_map/project/pallas_call | solution.py:28
  33.0 1.7 %collective-permute-start.11 = (bf16[256,2048]{1,0:T(8,128)(2,1)S(1)}, bf16[256,2048]{1,0:T(8,128)(2,1)S(1)}, u32[]{:S(2)}, u32[]{:S(2)}) collective-permute-start(bf16[256,2048]{1,0:T(8,128)(2,1)S(1)} %get-tuple-element.45), channel_id=1, source_target_pairs={{0,2},{1,3},{2,0},{3,1},{4,6},{5,7},{6,4},{7,5},{8,10},{9,11},{10,... | collective-permute-start | bytes 3145736 | tf_op jit(solution)/shard_map/ppermute | solution.py:46
  34.8 12.9 %all_to_all.22 = bf16[8,16,512]{2,1,0:T(8,128)(2,1)S(1)} all-to-all(bf16[8,16,512]{2,1,0:T(8,128)(2,1)S(1)} %bitcast.9), channel_id=1, replica_groups=mesh['dp'=8,'tensor'=4] {'dp'}, dimensions={0} | all-to-all | bytes 262144 | tf_op jit(solution)/shard_map/all_to_all | solution.py:414
  48.3 9.7 %all_to_all.23 = bf16[8,16,512]{2,1,0:T(8,128)(2,1)S(1)} all-to-all(bf16[8,16,512]{2,1,0:T(8,128)(2,1)S(1)} %bitcast.8), channel_id=1, replica_groups=mesh['dp'=8,'tensor'=4] {'dp'}, dimensions={0} | all-to-all | bytes 262144 | tf_op jit(solution)/shard_map/all_to_all | solution.py:414
  58.9 0.7 collective-permute-done.12.near
  60.1 2.8 %collective-permute-done.9.far = bf16[128,256]{1,0:T(8,128)(2,1)S(1)} collective-permute-done((bf16[128,256]{1,0:T(8,128)(2,1)S(1)}, bf16[128,256]{1,0:T(8,128)(2,1)S(1)}, u32[]{:S(2)}, u32[]{:S(2)}) %collective-permute-start.9) | collective-permute-done | bytes 65568 | tf_op jit(solution)/shard_map/ppermute | solution.py:46
  63.9 1.5 %collective-permute-start.14 = (bf16[128,1024]{1,0:T(8,128)(2,1)S(1)}, bf16[128,1024]{1,0:T(8,128)(2,1)S(1)}, u32[]{:S(2)}, u32[]{:S(2)}) collective-permute-start(bf16[128,1024]{1,0:T(8,128)(2,1)S(1)} %spread_far.2), channel_id=1, source_target_pairs={{0,2},{1,3},{2,0},{3,1},{4,6},{5,7},{6,4},{7,5},{8,10},{9,11},{10,... | collective-permute-start | bytes 786440 | tf_op jit(solution)/shard_map/ppermute | solution.py:46
  65.9 0.7 collective-permute-done.8.near
  66.8 1.3 %finish_out.1 = bf16[128,2048]{1,0:T(8,128)(2,1)} custom-call(bf16[128,2048]{1,0:T(8,128)(2,1)S(1)} %copy-done.5, bf16[128,256]{1,0:T(8,128)(2,1)S(1)} %get-tuple-element.43.own, bf16[128,256]{1,0:T(8,128)(2,1)S(1)} %collective-permute-done.8.near, bf16[128,256]{1,0:T(8,128)(2,1)S(1)} %collective-permute-done.9.far, ...), custom_call_target="tpu_custom_call" | custom-call | flops 1000 | bytes 1000 | tf_op jit(solution)/shard_map/finish_out/pallas_call | solution.py:28
  68.1 0.7 spread_own.1.grad_own
  68.8 3.8 %collective-permute-done.15.rest = bf16[128,1024]{1,0:T(8,128)(2,1)S(1)} collective-permute-done((bf16[128,1024]{1,0:T(8,128)(2,1)S(1)}, bf16[128,1024]{1,0:T(8,128)(2,1)S(1)}, u32[]{:S(2)}, u32[]{:S(2)}) %collective-permute-start.15) | collective-permute-done | bytes 262176 | tf_op jit(solution)/shard_map/ppermute | solution.py:46
  72.6 4.3 %collective-permute-done.14.pieces_0_ = bf16[128,1024]{1,0:T(8,128)(2,1)S(1)} collective-permute-done((bf16[128,1024]{1,0:T(8,128)(2,1)S(1)}, bf16[128,1024]{1,0:T(8,128)(2,1)S(1)}, u32[]{:S(2)}, u32[]{:S(2)}) %collective-permute-start.14) | collective-permute-done | bytes 262176 | tf_op jit(solution)/shard_map/ppermute | solution.py:46
  76.9 1.2 %finish_most.1 = (bf16[128,2048]{1,0:T(8,128)(2,1)}, f32[128,1024]{1,0:T(8,128)S(1)}) custom-call(bf16[128,2048]{1,0:T(8,128)(2,1)S(1)} %copy-done.5, bf16[128,2048]{1,0:T(8,128)(2,1)S(1)} %copy-done.6, bf16[1,2048]{1,0:T(2,128)(2,1)S(1)} %reshape.17.gain, f32[128,1]{1,0:T(8,128)S(1)} %get-tuple-element.46.inverse, ...), custom_call_target="tpu_custom_call" | custom-call | flops 1000 | bytes 1000 | tf_op jit(solution)/shard_map/finish_most/pallas_call | solution.py:392
  78.1 0.8 %finish_rest.1 = bf16[128,2048]{1,0:T(8,128)(2,1)} custom-call(bf16[1,2048]{1,0:T(2,128)(2,1)S(1)} %reshape.17.gain, f32[128,1]{1,0:T(8,128)S(1)} %get-tuple-element.46.inverse, f32[128,1024]{1,0:T(8,128)S(1)} %get-tuple-element.53.left, bf16[128,1024]{1,0:T(8,128)(2,1)S(1)} %collective-permute-done.15.rest, ...), custom_call_target="tpu_custom_call", output_to_operand_aliasing={{}: (4, {})} | custom-call | flops 1000 | bytes 1000 | tf_op jit(solution)/shard_map/finish_rest/pallas_call | solution.py:401
  (49 shorter events, 9.6 us)
Async XLA Ops:
  0.6 8.1 %collective-permute-start.5 = (bf16[128,8192]{1,0:T(8,128)(2,1)}, bf16[128,8192]{1,0:T(8,128)(2,1)}, u32[]{:S(2)}, u32[]{:S(2)}) collective-permute-start(bf16[128,8192]{1,0:T(8,128)(2,1)} %w_output.1), channel_id=1, source_target_pairs={{0,1},{1,0},{2,3},{3,2},{4,5},{5,4},{6,7},{7,6},{8,9},{9,8},{10,11... | collective-permute-start | bytes 6291464 | tf_op jit(solution)/shard_map/ppermute | solution.py:46
  1.1 20.0 %collective-permute-start = (bf16[128,2048]{1,0:T(8,128)(2,1)}, bf16[128,2048]{1,0:T(8,128)(2,1)S(1)}, u32[]{:S(2)}, u32[]{:S(2)}) collective-permute-start(bf16[128,2048]{1,0:T(8,128)(2,1)} %inputs.3), channel_id=1, source_target_pairs={{0,1},{1,0},{2,3},{3,2},{4,5},{5,4},{6,7},{7,6},{8,9},{9,8},{10,11... | collective-permute-start | bytes 1572872 | tf_op jit(solution)/shard_map/ppermute | solution.py:46
  1.2 26.7 %collective-permute-start.1 = (bf16[128,2048]{1,0:T(8,128)(2,1)}, bf16[128,2048]{1,0:T(8,128)(2,1)S(1)}, u32[]{:S(2)}, u32[]{:S(2)}) collective-permute-start(bf16[128,2048]{1,0:T(8,128)(2,1)} %inputs.3), channel_id=1, source_target_pairs={{0,2},{1,3},{2,0},{3,1},{4,6},{5,7},{6,4},{7,5},{8,10},{9,11},{10,... | collective-permute-start | bytes 1572872 | tf_op jit(solution)/shard_map/ppermute | solution.py:46
  4.2 23.8 %collective-permute-start.2 = (bf16[128,2048]{1,0:T(8,128)(2,1)}, bf16[128,2048]{1,0:T(8,128)(2,1)S(1)}, u32[]{:S(2)}, u32[]{:S(2)}) collective-permute-start(bf16[128,2048]{1,0:T(8,128)(2,1)} %cotangent.1), channel_id=1, source_target_pairs={{0,2},{1,3},{2,0},{3,1},{4,6},{5,7},{6,4},{7,5},{8,10},{9,11},{10,... | collective-permute-start | bytes 1572872 | tf_op jit(solution)/shard_map/ppermute | solution.py:46
  4.9 1.2 %collective-permute-start.3 = (bf16[1,2048]{1,0:T(2,128)(2,1)S(1)}, bf16[1,2048]{1,0:T(2,128)(2,1)S(1)}, u32[]{:S(2)}, u32[]{:S(2)}) collective-permute-start(bf16[1,2048]{1,0:T(2,128)(2,1)S(1)} %reshape.17.gain), channel_id=1, source_target_pairs={{0,1},{1,0},{2,3},{3,2},{4,5},{5,4},{6,7},{7,6},{8,9},{9,8},{10,11... | collective-permute-start | bytes 12296 | tf_op jit(solution)/shard_map/ppermute | solution.py:46
  6.1 21.9 %collective-permute-start.4 = (bf16[2,2048]{1,0:T(2,128)(2,1)S(1)}, bf16[2,2048]{1,0:T(2,128)(2,1)S(1)}, u32[]{:S(2)}, u32[]{:S(2)}) collective-permute-start(bf16[2,2048]{1,0:T(2,128)(2,1)S(1)} %pad_maximum_fusion.gain_chip), channel_id=1, source_target_pairs={{0,2},{1,3},{2,0},{3,1},{4,6},{5,7},{6,4},{7,5},{8,10},{9,11},{10,... | collective-permute-start | bytes 24584 | tf_op jit(solution)/shard_map/ppermute | solution.py:46
  8.7 1.6 %copy-start = (bf16[8192,128]{1,0:T(8,128)(2,1)S(1)}, bf16[8192,128]{1,0:T(8,128)(2,1)}, u32[]{:S(2)}) copy-start(bf16[8192,128]{1,0:T(8,128)(2,1)} %w_query.3) | copy-start | bytes 6291460
  10.3 1.6 %copy-start.2 = (bf16[8192,128]{1,0:T(8,128)(2,1)S(1)}, bf16[8192,128]{1,0:T(8,128)(2,1)}, u32[]{:S(2)}) copy-start(bf16[8192,128]{1,0:T(8,128)(2,1)} %w_key.3) | copy-start | bytes 6291460
  11.9 1.6 %copy-start.4 = (bf16[8192,128]{1,0:T(8,128)(2,1)S(1)}, bf16[8192,128]{1,0:T(8,128)(2,1)}, u32[]{:S(2)}) copy-start(bf16[8192,128]{1,0:T(8,128)(2,1)} %w_value.3) | copy-start | bytes 6291460
  13.5 1.6 %copy-start.7 = (bf16[128,8192]{1,0:T(8,128)(2,1)S(1)}, bf16[128,8192]{1,0:T(8,128)(2,1)}, u32[]{:S(2)}) copy-start(bf16[128,8192]{1,0:T(8,128)(2,1)} %w_output.1) | copy-start | bytes 6291460
  17.0 4.1 %copy-start.5 = (bf16[128,2048]{1,0:T(8,128)(2,1)S(1)}, bf16[128,2048]{1,0:T(8,128)(2,1)}, u32[]{:S(2)}) copy-start(bf16[128,2048]{1,0:T(8,128)(2,1)} %inputs.3) | copy-start | bytes 1572868
  17.0 4.1 %copy-start.6 = (bf16[128,2048]{1,0:T(8,128)(2,1)S(1)}, bf16[128,2048]{1,0:T(8,128)(2,1)}, u32[]{:S(2)}) copy-start(bf16[128,2048]{1,0:T(8,128)(2,1)} %cotangent.1) | copy-start | bytes 1572868
  28.0 2.0 %collective-permute-start.6 = (bf16[128,2048]{1,0:T(8,128)(2,1)S(1)}, bf16[128,2048]{1,0:T(8,128)(2,1)S(1)}, u32[]{:S(2)}, u32[]{:S(2)}) collective-permute-start(bf16[128,2048]{1,0:T(8,128)(2,1)S(1)} %collective-permute-done.1.x2), channel_id=1, source_target_pairs={{0,1},{1,0},{2,3},{3,2},{4,5},{5,4},{6,7},{7,6},{8,9},{9,8},{10,11... | collective-permute-start | bytes 1572872 | tf_op jit(solution)/shard_map/ppermute | solution.py:46
  28.0 2.0 %copy-start.1 = (bf16[8192,128]{1,0:T(8,128)(2,1)S(1)}, bf16[8192,128]{1,0:T(8,128)(2,1)}, u32[]{:S(2)}) copy-start(bf16[8192,128]{1,0:T(8,128)(2,1)} %w_query.3) | copy-start | bytes 6291460
  28.0 2.2 %copy-start.3 = (bf16[8192,128]{1,0:T(8,128)(2,1)S(1)}, bf16[8192,128]{1,0:T(8,128)(2,1)}, u32[]{:S(2)}) copy-start(bf16[8192,128]{1,0:T(8,128)(2,1)} %w_key.3) | copy-start | bytes 6291460
  28.3 1.7 %collective-permute-start.7 = (f32[128,128]{1,0:T(8,128)S(1)}, f32[128,128]{1,0:T(8,128)S(1)}, u32[]{:S(2)}, u32[]{:S(2)}) collective-permute-start(f32[128,128]{1,0:T(8,128)S(1)} %add_grad.2), channel_id=1, source_target_pairs={{0,1},{1,0},{2,3},{3,2},{4,5},{5,4},{6,7},{7,6},{8,9},{9,8},{10,11... | collective-permute-start | bytes 196616 | tf_op jit(solution)/shard_map/ppermute | solution.py:46
  32.4 27.2 %collective-permute-start.13 = (bf16[384,4096]{1,0:T(8,128)(2,1)S(1)}, bf16[384,4096]{1,0:T(8,128)(2,1)S(1)}, u32[]{:S(2)}, u32[]{:S(2)}) collective-permute-start(bf16[384,4096]{1,0:T(8,128)(2,1)S(1)} %get-tuple-element.50), channel_id=1, source_target_pairs={{0,1},{1,0},{2,3},{3,2},{4,5},{5,4},{6,7},{7,6},{8,9},{9,8},{10,11... | collective-permute-start | bytes 9437192 | tf_op jit(solution)/shard_map/ppermute | solution.py:46
  33.0 33.8 %collective-permute-start.11 = (bf16[256,2048]{1,0:T(8,128)(2,1)S(1)}, bf16[256,2048]{1,0:T(8,128)(2,1)S(1)}, u32[]{:S(2)}, u32[]{:S(2)}) collective-permute-start(bf16[256,2048]{1,0:T(8,128)(2,1)S(1)} %get-tuple-element.45), channel_id=1, source_target_pairs={{0,2},{1,3},{2,0},{3,1},{4,6},{5,7},{6,4},{7,5},{8,10},{9,11},{10,... | collective-permute-start | bytes 3145736 | tf_op jit(solution)/shard_map/ppermute | solution.py:46
  58.3 1.4 %collective-permute-start.12 = (bf16[128,384]{1,0:T(8,128)(2,1)S(1)}, bf16[128,384]{1,0:T(8,128)(2,1)S(1)}, u32[]{:S(2)}, u32[]{:S(2)}) collective-permute-start(bf16[128,384]{1,0:T(8,128)(2,1)S(1)} %get-tuple-element.52.own), channel_id=1, source_target_pairs={{0,1},{1,0},{2,3},{3,2},{4,5},{5,4},{6,7},{7,6},{8,9},{9,8},{10,11... | collective-permute-start | bytes 294920 | tf_op jit(solution)/shard_map/ppermute | solution.py:46
  58.4 4.5 %collective-permute-start.9 = (bf16[128,256]{1,0:T(8,128)(2,1)S(1)}, bf16[128,256]{1,0:T(8,128)(2,1)S(1)}, u32[]{:S(2)}, u32[]{:S(2)}) collective-permute-start(bf16[128,256]{1,0:T(8,128)(2,1)S(1)} %get-tuple-element.43.own), channel_id=1, source_target_pairs={{0,2},{1,3},{2,0},{3,1},{4,6},{5,7},{6,4},{7,5},{8,10},{9,11},{10,... | collective-permute-start | bytes 196616 | tf_op jit(solution)/shard_map/ppermute | solution.py:46
  63.3 9.3 %collective-permute-start.15 = (bf16[128,1024]{1,0:T(8,128)(2,1)S(1)}, bf16[128,1024]{1,0:T(8,128)(2,1)S(1)}, u32[]{:S(2)}, u32[]{:S(2)}) collective-permute-start(bf16[128,1024]{1,0:T(8,128)(2,1)S(1)} %spread_far.3), channel_id=1, source_target_pairs={{0,2},{1,3},{2,0},{3,1},{4,6},{5,7},{6,4},{7,5},{8,10},{9,11},{10,... | collective-permute-start | bytes 786440 | tf_op jit(solution)/shard_map/ppermute | solution.py:46
  63.9 13.0 %collective-permute-start.14 = (bf16[128,1024]{1,0:T(8,128)(2,1)S(1)}, bf16[128,1024]{1,0:T(8,128)(2,1)S(1)}, u32[]{:S(2)}, u32[]{:S(2)}) collective-permute-start(bf16[128,1024]{1,0:T(8,128)(2,1)S(1)} %spread_far.2), channel_id=1, source_target_pairs={{0,2},{1,3},{2,0},{3,1},{4,6},{5,7},{6,4},{7,5},{8,10},{9,11},{10,... | collective-permute-start | bytes 786440 | tf_op jit(solution)/shard_map/ppermute | solution.py:46
  65.4 1.3 %collective-permute-start.8 = (bf16[128,256]{1,0:T(8,128)(2,1)S(1)}, bf16[128,256]{1,0:T(8,128)(2,1)S(1)}, u32[]{:S(2)}, u32[]{:S(2)}) collective-permute-start(bf16[128,256]{1,0:T(8,128)(2,1)S(1)} %get-tuple-element.43.own), channel_id=1, source_target_pairs={{0,1},{1,0},{2,3},{3,2},{4,5},{5,4},{6,7},{7,6},{8,9},{9,8},{10,11... | collective-permute-start | bytes 196616 | tf_op jit(solution)/shard_map/ppermute | solution.py:46
  65.4 1.4 %collective-permute-start.10 = (bf16[128,256]{1,0:T(8,128)(2,1)S(1)}, bf16[128,256]{1,0:T(8,128)(2,1)S(1)}, u32[]{:S(2)}, u32[]{:S(2)}) collective-permute-start(bf16[128,256]{1,0:T(8,128)(2,1)S(1)} %collective-permute-done.9.far), channel_id=1, source_target_pairs={{0,1},{1,0},{2,3},{3,2},{4,5},{5,4},{6,7},{7,6},{8,9},{9,8},{10,11... | collective-permute-start | bytes 196616 | tf_op jit(solution)/shard_map/ppermute | solution.py:46
  (3 other events, 2.0 us)
